TPU v7x, 32 devices: a whole 2x2x4 slice. The times are simulated.
32 devices in a mesh: wide: 8 (over y, x, core), narrow: 4 (over z).
Axes of the slice: x: 2, y: 2, z: 4, core: 2. Of those that a mesh axis runs over, the one named last changes fastest.
Arguments:
- amplitudes: float32 [1024, 8192], P(('wide', 'narrow')), may hold values from -6 to 6
- integrals: float32 [8192, 8192], P('narrow', 'wide'), may hold values from -0.125 to 0.125
- bare_terms: float32 [1024, 8192], P('wide', 'narrow'), may hold values from -6 to 6
- pattern: int32 [8, 64], replicated, may hold values 0 or 1
- block_order: int32 [8], replicated, may hold values from 0 to 7, each once
- occ_gap: float32 [1024], P('wide'), may hold values from 0.3 to 3
- virt_gap: float32 [8192], P('narrow'), may hold values from 0.3 to 3
Outputs:
- update: float32 [1024, 8192], P('wide', 'narrow')
All inputs are finite; a program needn't handle non-finite values.
Results may differ from a plain program's by a relative error of at most 0.000054.
Values sent between devices are 32-bit elements; how exact they have to be, the bound alone decides.
No kernel may reach another device: no remote copies, remote signals or barrier semaphores. Data moves between devices by JAX's collectives and lax.ppermute only.
A program may use at most 192 MiB of HBM per device.

v0:
```python
import jax
import jax.numpy as jnp
from jax import lax
from jax.sharding import PartitionSpec as P

TILE = 128


def shards(amplitudes, integrals, bare_terms, pattern, block_order, occ_gap, virt_gap):
    rows_local, columns = amplitudes.shape
    tile_count = block_order.shape[0]
    vir_count = pattern.shape[1]
    narrow_count = lax.axis_size("narrow")
    position = lax.axis_index("wide") * narrow_count + lax.axis_index("narrow")
    row_ids = position * rows_local + jnp.arange(rows_local, dtype=jnp.int32)
    tile_ids = row_ids // TILE
    every_tile = jnp.arange(tile_count, dtype=jnp.int32)
    matches = tile_ids[:, None] == every_tile[None, :]
    block_ids = jnp.sum(jnp.where(matches, block_order[None, :], 0), axis=1)
    chooser = (block_ids[:, None] == every_tile[None, :]).astype(jnp.float32)
    row_pattern = jnp.dot(
        chooser,
        pattern.astype(jnp.float32),
        preferred_element_type=jnp.float32,
        precision=lax.Precision.HIGHEST,
    )
    screened = (amplitudes.reshape(rows_local, vir_count, TILE) * row_pattern[:, :, None]).reshape(
        rows_local, columns
    )
    transposed = lax.all_to_all(screened, "narrow", split_axis=1, concat_axis=0, tiled=True)
    stacked = jnp.dot(
        lax.all_gather(transposed, "wide", axis=0, tiled=True),
        integrals,
        preferred_element_type=jnp.float32,
        precision=lax.Precision.HIGHEST,
    )
    partial_value = lax.all_to_all(stacked, "wide", split_axis=0, concat_axis=1, tiled=True)
    ladder = lax.psum_scatter(partial_value, "narrow", scatter_dimension=1, tiled=True)
    denominator = occ_gap[:, None] + virt_gap[None, :]
    return -(bare_terms + ladder) / denominator


def solution(mesh):
    placed = (
        P(("wide", "narrow"), None),
        P("narrow", "wide"),
        P("wide", "narrow"),
        P(),
        P(),
        P("wide"),
        P("narrow"),
    )
    return jax.shard_map(
        shards, mesh=mesh, in_specs=placed, out_specs=P("wide", "narrow"), check_vma=False
    )
```

profile of v0, /device:TPU:0, one launch (start us, length us, event | category | flops | bytes accessed | tf_op | source)
XLA Modules:
  0.0 266.9 jit_solution(2291615169966468119)
XLA Ops:
  6.5 0.0 all-gather.2.cloned.1.call-start
  6.5 0.7 select_reduce_fusion
  7.3 0.9 fusion
  8.2 0.3 mul.19
  8.5 1.9 bitcast_multiply_fusion
  10.4 0.1 copy.21
  10.5 31.9 %all_to_all.38 = f32[32,4,2048]{2,0,1:T(8,128)} all-to-all(f32[32,4,2048]{2,0,1:T(8,128)S(1)} %bitcast.22), channel_id=1, replica_groups=mesh['wide'=8,'narrow'=4] {'narrow'}, dimensions={1} | all-to-all | bytes 2097152 | tf_op jit(solution)/shard_map/all_to_all | solution.py:30
  42.4 0.0 all-gather.2.cloned.1.call-update
  42.4 0.0 reduce-scatter.2.cloned.1.call-start
  42.5 53.6 %all-gather.2.cloned.1.call-done = f32[1024,2048]{1,0:T(8,128)} async-done(((f32[128,2048]{1,0:T(8,128)}), f32[1024,2048]{1,0:T(8,128)}) %all-gather.2.cloned.1.call-update) | async-done | bytes 8388624 | tf_op jit(solution)/shard_map/all_gather | solution.py:32
  96.1 31.5 %fusion.3 = f32[1024,1024]{1,0:T(8,128)S(1)} fusion(f32[1024,2048]{1,0:T(8,128)} %all-gather.2.cloned.1.call-done, f32[2048,1024]{1,0:T(8,128)} %param.8), kind=kOutput, calls=%fused_computation.13 | convolution fusion | flops 25769803776 | bytes 20971520 | tf_op jit(solution)/shard_map/dot_general | solution.py:31
  127.6 51.6 %all_to_all.39 = f32[8,128,1024]{2,1,0:T(8,128)S(1)} all-to-all(f32[8,128,1024]{2,1,0:T(8,128)S(1)} %bitcast.20), channel_id=1, replica_groups=mesh['wide'=8,'narrow'=4] {'wide'}, dimensions={0} | all-to-all | bytes 8388608 | tf_op jit(solution)/shard_map/all_to_all | solution.py:37
  179.2 0.0 copy-start
  179.2 0.0 copy-start.1
  179.2 0.0 copy-start.2
  179.2 2.2 copy.17
  181.5 0.0 reduce-scatter.2.cloned.1.call-update
  181.5 76.0 %reduce-scatter.2.cloned.1.call-done = f32[128,2048]{1,0:T(8,128)} async-done(((f32[128,8192]{1,0:T(8,128)}), f32[128,2048]{1,0:T(8,128)}) %reduce-scatter.2.cloned.1.call-update) | async-done | bytes 1048592 | tf_op jit(solution)/shard_map/reduce_scatter | solution.py:38
  257.5 0.0 copy-done
  257.5 0.0 copy-done.1
  257.5 0.0 copy-done.2
  257.5 2.5 add_divide_fusion
  (1 shorter events, 0.0 us)
Async XLA Ops:
  6.5 89.5 %all-gather.2.cloned.1.call-start = ((), (), s32[]{:S(2)}) async-start(), calls=%async_computation.3 | async-start | bytes 9437184 | tf_op jit(solution)/shard_map/all_gather | solution.py:32
  42.4 215.1 %reduce-scatter.2.cloned.1.call-start = ((), (), s32[]{:S(2)}) async-start(), calls=%async_computation.4 | async-start | bytes 5242880 | tf_op jit(solution)/shard_map/reduce_scatter | solution.py:38
  179.2 78.3 %copy-start = (f32[128,2048]{1,0:T(8,128)S(1)}, f32[128,2048]{1,0:T(8,128)}, u32[]{:S(2)}) copy-start(f32[128,2048]{1,0:T(8,128)} %param.9) | copy-start | bytes 3145732
  179.2 78.3 %copy-start.1 = (f32[2048]{0:T(1024)S(1)}, f32[2048]{0:T(1024)}, u32[]{:S(2)}) copy-start(f32[2048]{0:T(1024)} %param.13) | copy-start | bytes 24580
  179.2 78.3 %copy-start.2 = (f32[128]{0:T(128)S(1)}, f32[128]{0:T(128)}, u32[]{:S(2)}) copy-start(f32[128]{0:T(128)} %param.12) | copy-start | bytes 1540
Sparse Core Ops, SparseCore 0:
  42.5 53.4 all-gather.1
  181.6 75.8 reduce-scatter.1
where the time goes:
time: 267 us
  waiting for transfers between devices  130 us (49%)
  blocking collectives  83.6 us (31%)
  matrix products  32.4 us (12%)
  between operations  13.4 us (5%)
  other arithmetic  5.1 us (2%)
    reduce_scatter x1, waiting for transfers between devices, shards(): lax.psum_scatter(partial_value, 'narrow', scatter_dimension=1, tiled=True)  76 us
    all_gather x1, waiting for transfers between devices, shards(): lax.all_gather(transposed, 'wide', axis=0, tiled=True)  53.6 us
    all_to_all x1, blocking collectives, shards(): lax.all_to_all(stacked, 'wide', split_axis=0, concat_axis=1, tiled=True)  51.6 us
    all_to_all x1, blocking collectives, shards(): lax.all_to_all(screened, 'narrow', split_axis=1, concat_axis=0, tiled=True)  31.9 us
    dot_general x1, matrix products, shards(): jnp.dot(lax.all_gather(transposed, 'wide', axis=0, tiled=True), integrals...  31.5 us
  transfers between devices with their start and end apart: 2, of which 2 were waited for; matrix products, arithmetic and copies ran while one was open for 0% of the time, Pallas kernels for 0%

commit v1 on v0

v1 whole, which is shorter than its diff:
```python
import jax
import jax.numpy as jnp
from jax import lax
from jax.sharding import PartitionSpec as P

TILE = 128
CHUNKS = 4


def shards(amplitudes, integrals, bare_terms, pattern, block_order, occ_gap, virt_gap):
    rows_local, columns = amplitudes.shape
    vir_count = pattern.shape[1]
    wide_count = lax.axis_size("wide")
    narrow_count = lax.axis_size("narrow")
    position = lax.axis_index("wide") * narrow_count + lax.axis_index("narrow")
    tile = position * rows_local // TILE
    row_pattern = pattern[block_order[tile]].astype(jnp.float32)
    screened = (
        amplitudes.reshape(rows_local, vir_count, TILE) * row_pattern[None, :, None]
    ).reshape(rows_local, columns)
    part = rows_local // CHUNKS
    rows_out, columns_out = bare_terms.shape
    ladders = []
    for chunk in range(CHUNKS):
        piece = screened[chunk * part : (chunk + 1) * part]
        transposed = lax.all_to_all(piece, "narrow", split_axis=1, concat_axis=0, tiled=True)
        stacked = jnp.dot(
            lax.all_gather(transposed, "wide", axis=0, tiled=True),
            integrals,
            preferred_element_type=jnp.float32,
            precision=lax.Precision.HIGH,
        )
        partial_value = lax.all_to_all(stacked, "wide", split_axis=0, concat_axis=1, tiled=True)
        ladder = lax.psum_scatter(partial_value, "narrow", scatter_dimension=1, tiled=True)
        ladders.append(ladder.reshape(narrow_count, part, columns_out))
    ladder = jnp.stack(ladders, axis=1).reshape(rows_out, columns_out)
    denominator = occ_gap[:, None] + virt_gap[None, :]
    return -(bare_terms + ladder) / denominator


def solution(mesh):
    placed = (
        P(("wide", "narrow"), None),
        P("narrow", "wide"),
        P("wide", "narrow"),
        P(),
        P(),
        P("wide"),
        P("narrow"),
    )
    return jax.shard_map(
        shards, mesh=mesh, in_specs=placed, out_specs=P("wide", "narrow"), check_vma=False
    )
```

time: 267 us -> 286 us (1.071)
  blocking collectives: 83.6 us -> 128 us
  waiting for transfers between devices: 130 us -> 101 us
  local copies, waits for them, and re-layouts: 2.66 us -> 8.24 us
  matrix products: 32.4 us -> 28.7 us
    all_gather x1 -> x4, waiting for transfers between devices: 53.6 us -> 13.1 us  [shards(): lax.all_gather(transposed, 'wide', axis=0, tiled=True)]
    all_to_all x1 -> x4, blocking collectives: 51.6 us -> 79.8 us  [shards(): lax.all_to_all(stacked, 'wide', split_axis=0, concat_axis=1, tiled=True)]
    all_to_all x1 -> x4, blocking collectives: 31.9 us -> 48 us  [shards(): lax.all_to_all(piece, 'narrow', split_axis=1, concat_axis=0, tiled=True)]
    reduce_scatter x1 -> x4, waiting for transfers between devices: 76 us -> 87.6 us  [shards(): lax.psum_scatter(partial_value, 'narrow', scatter_dimension=1, tiled=True)]
    dot_general x1 -> x4, matrix products: 31.5 us -> 28.7 us  [shards(): jnp.dot(lax.all_gather(transposed, 'wide', axis=0, tiled=True), integrals...]
  transfers between devices with their start and end apart: 2 -> 8, of which waited for: 2 -> 6; matrix products, arithmetic and copies ran while one was open for 0% -> 12% of each run, Pallas kernels for 0% -> 0%
where the time goes in v1:
time: 286 us; the launch traced here: 285 us
  blocking collectives  128 us (45%)
  waiting for transfers between devices  101 us (35%)
  matrix products  28.7 us (10%)
  between operations  15.6 us (5%)
  local copies, waits for them, and re-layouts  8.24 us (3%)
  other arithmetic  3.52 us (1%)
    reduce_scatter x4, waiting for transfers between devices, shards(): lax.psum_scatter(partial_value, 'narrow', scatter_dimension=1, tiled=True)  87.6 us
    all_to_all x4, blocking collectives, shards(): lax.all_to_all(stacked, 'wide', split_axis=0, concat_axis=1, tiled=True)  79.8 us
    all_to_all x4, blocking collectives, shards(): lax.all_to_all(piece, 'narrow', split_axis=1, concat_axis=0, tiled=True)  48 us
    dot_general x4, matrix products, shards(): jnp.dot(lax.all_gather(transposed, 'wide', axis=0, tiled=True), integrals...  28.7 us
    all_gather x4, waiting for transfers between devices, shards(): lax.all_gather(transposed, 'wide', axis=0, tiled=True)  13.1 us
  transfers between devices with their start and end apart: 8, of which 6 were waited for; matrix products, arithmetic and copies ran while one was open for 12% of the time, Pallas kernels for 0%

profile of v1, /device:TPU:0, one launch (start us, length us, event | category | flops | bytes accessed | tf_op | source)
XLA Modules:
  0.0 285.0 jit_solution(221345022167437418)
XLA Ops:
  6.5 1.2 dynamic_slice.6
  9.1 1.4 copy.35
  11.1 0.7 convert_bitcast_fusion
  11.8 0.2 bitcast_multiply_fusion
  12.2 0.2 copy.22
  12.4 15.1 %all_to_all.152 = f32[8,4,2048]{2,0,1:T(8,128)} all-to-all(f32[8,4,2048]{2,0,1:T(8,128)S(1)} %copy.22), channel_id=1, replica_groups=mesh['wide'=8,'narrow'=4] {'narrow'}, dimensions={1} | all-to-all | bytes 524288 | tf_op jit(solution)/shard_map/all_to_all | solution.py:26
  27.6 0.2 copy.28
  27.8 11.0 %all_to_all.153 = f32[8,4,2048]{2,0,1:T(8,128)} all-to-all(f32[8,4,2048]{2,0,1:T(8,128)S(1)} %copy.28), channel_id=1, replica_groups=mesh['wide'=8,'narrow'=4] {'narrow'}, dimensions={1} | all-to-all | bytes 524288 | tf_op jit(solution)/shard_map/all_to_all | solution.py:26
  39.0 0.2 copy.26
  39.2 10.9 %all_to_all.154 = f32[8,4,2048]{2,0,1:T(8,128)} all-to-all(f32[8,4,2048]{2,0,1:T(8,128)S(1)} %copy.26), channel_id=1, replica_groups=mesh['wide'=8,'narrow'=4] {'narrow'}, dimensions={1} | all-to-all | bytes 524288 | tf_op jit(solution)/shard_map/all_to_all | solution.py:26
  50.3 0.2 copy.24
  50.5 10.9 %all_to_all.155 = f32[8,4,2048]{2,0,1:T(8,128)} all-to-all(f32[8,4,2048]{2,0,1:T(8,128)S(1)} %copy.24), channel_id=1, replica_groups=mesh['wide'=8,'narrow'=4] {'narrow'}, dimensions={1} | all-to-all | bytes 524288 | tf_op jit(solution)/shard_map/all_to_all | solution.py:26
  61.4 7.3 %fusion.3 = f32[256,1024]{1,0:T(8,128)S(1)} fusion(f32[256,2048]{1,0:T(8,128)} %all-gather.5.cloned.1.call-done, f32[2048,1024]{1,0:T(8,128)} %param.8), kind=kOutput, calls=%fused_computation.7 | convolution fusion | flops 3221225472 | bytes 11534336 | tf_op jit(solution)/shard_map/dot_general | solution.py:27
  68.8 24.5 %all_to_all.156 = f32[8,32,1024]{2,1,0:T(8,128)S(1)} all-to-all(f32[8,32,1024]{2,1,0:T(8,128)S(1)} %bitcast.60), channel_id=1, replica_groups=mesh['wide'=8,'narrow'=4] {'wide'}, dimensions={0} | all-to-all | bytes 2097152 | tf_op jit(solution)/shard_map/all_to_all | solution.py:33
  93.2 1.1 copy.31
  94.4 7.2 %fusion.6 = f32[256,1024]{1,0:T(8,128)S(1)} fusion(f32[256,2048]{1,0:T(8,128)} %all-gather.11.cloned.1.call-done, f32[2048,1024]{1,0:T(8,128)} %param.8), kind=kOutput, calls=%fused_computation.10 | convolution fusion | flops 3221225472 | bytes 11534336 | tf_op jit(solution)/shard_map/dot_general | solution.py:27
  101.6 17.8 %all_to_all.157 = f32[8,32,1024]{2,1,0:T(8,128)S(1)} all-to-all(f32[8,32,1024]{2,1,0:T(8,128)S(1)} %bitcast.61), channel_id=1, replica_groups=mesh['wide'=8,'narrow'=4] {'wide'}, dimensions={0} | all-to-all | bytes 2097152 | tf_op jit(solution)/shard_map/all_to_all | solution.py:33
  119.4 1.1 copy.34
  120.5 6.1 %all-gather.9.cloned.1.call-done = f32[256,2048]{1,0:T(8,128)} async-done(((f32[32,2048]{1,0:T(8,128)}), f32[256,2048]{1,0:T(8,128)}) %all-gather.9.cloned.1.call-update) | async-done | bytes 2097168 | tf_op jit(solution)/shard_map/all_gather | solution.py:28
  126.7 7.1 %fusion.5 = f32[256,1024]{1,0:T(8,128)S(1)} fusion(f32[256,2048]{1,0:T(8,128)} %all-gather.9.cloned.1.call-done, f32[2048,1024]{1,0:T(8,128)} %param.8), kind=kOutput, calls=%fused_computation.9 | convolution fusion | flops 3221225472 | bytes 11534336 | tf_op jit(solution)/shard_map/dot_general | solution.py:27
  133.8 19.7 %all_to_all.158 = f32[8,32,1024]{2,1,0:T(8,128)S(1)} all-to-all(f32[8,32,1024]{2,1,0:T(8,128)S(1)} %bitcast.62), channel_id=1, replica_groups=mesh['wide'=8,'narrow'=4] {'wide'}, dimensions={0} | all-to-all | bytes 2097152 | tf_op jit(solution)/shard_map/all_to_all | solution.py:33
  153.5 1.1 copy.33
  154.6 7.0 %all-gather.7.cloned.1.call-done = f32[256,2048]{1,0:T(8,128)} async-done(((f32[32,2048]{1,0:T(8,128)}), f32[256,2048]{1,0:T(8,128)}) %all-gather.7.cloned.1.call-update) | async-done | bytes 2097168 | tf_op jit(solution)/shard_map/all_gather | solution.py:28
  161.6 7.1 %fusion.4 = f32[256,1024]{1,0:T(8,128)S(1)} fusion(f32[256,2048]{1,0:T(8,128)} %all-gather.7.cloned.1.call-done, f32[2048,1024]{1,0:T(8,128)} %param.8), kind=kOutput, calls=%fused_computation.8 | convolution fusion | flops 3221225472 | bytes 11534336 | tf_op jit(solution)/shard_map/dot_general | solution.py:27
  168.8 17.9 %all_to_all.159 = f32[8,32,1024]{2,1,0:T(8,128)S(1)} all-to-all(f32[8,32,1024]{2,1,0:T(8,128)S(1)} %bitcast.63), channel_id=1, replica_groups=mesh['wide'=8,'narrow'=4] {'wide'}, dimensions={0} | all-to-all | bytes 2097152 | tf_op jit(solution)/shard_map/all_to_all | solution.py:33
  186.7 1.1 copy.32
  187.8 3.2 %reduce-scatter.5.cloned.1.call-done = f32[32,2048]{1,0:T(8,128)} async-done(((f32[32,8192]{1,0:T(8,128)}), f32[32,2048]{1,0:T(8,128)}) %reduce-scatter.5.cloned.1.call-update) | async-done | bytes 262160 | tf_op jit(solution)/shard_map/reduce_scatter | solution.py:34
  190.9 28.1 %reduce-scatter.11.cloned.1.call-done = f32[32,2048]{1,0:T(8,128)} async-done(((f32[32,8192]{1,0:T(8,128)}), f32[32,2048]{1,0:T(8,128)}) %reduce-scatter.11.cloned.1.call-update) | async-done | bytes 262160 | tf_op jit(solution)/shard_map/reduce_scatter | solution.py:34
  219.0 28.1 %reduce-scatter.9.cloned.1.call-done = f32[32,2048]{1,0:T(8,128)} async-done(((f32[32,8192]{1,0:T(8,128)}), f32[32,2048]{1,0:T(8,128)}) %reduce-scatter.9.cloned.1.call-update) | async-done | bytes 262160 | tf_op jit(solution)/shard_map/reduce_scatter | solution.py:34
  247.1 28.2 %reduce-scatter.7.cloned.1.call-done = f32[32,2048]{1,0:T(8,128)} async-done(((f32[32,8192]{1,0:T(8,128)}), f32[32,2048]{1,0:T(8,128)}) %reduce-scatter.7.cloned.1.call-update) | async-done | bytes 262160 | tf_op jit(solution)/shard_map/reduce_scatter | solution.py:34
  275.4 1.4 pad_maximum_fusion
  276.9 1.3 fusion.1
  (30 shorter events, 1.1 us)
Async XLA Ops:
  6.5 54.9 %all-gather.5.cloned.1.call-start = ((), (), s32[]{:S(2)}) async-start(), calls=%async_computation.12 | async-start | bytes 2359296 | tf_op jit(solution)/shard_map/all_gather | solution.py:28
  27.5 67.0 %all-gather.11.cloned.1.call-start = ((), (), s32[]{:S(2)}) async-start(), calls=%async_computation.18 | async-start | bytes 2359296 | tf_op jit(solution)/shard_map/all_gather | solution.py:28
  38.9 87.8 %all-gather.9.cloned.1.call-start = ((), (), s32[]{:S(2)}) async-start(), calls=%async_computation.16 | async-start | bytes 2359296 | tf_op jit(solution)/shard_map/all_gather | solution.py:28
  50.1 111.5 %all-gather.7.cloned.1.call-start = ((), (), s32[]{:S(2)}) async-start(), calls=%async_computation.14 | async-start | bytes 2359296 | tf_op jit(solution)/shard_map/all_gather | solution.py:28
  61.4 129.6 %reduce-scatter.5.cloned.1.call-start = ((), (), s32[]{:S(2)}) async-start(), calls=%async_computation.13 | async-start | bytes 1310720 | tf_op jit(solution)/shard_map/reduce_scatter | solution.py:34
  94.4 124.6 %reduce-scatter.11.cloned.1.call-start = ((), (), s32[]{:S(2)}) async-start(), calls=%async_computation.19 | async-start | bytes 1310720 | tf_op jit(solution)/shard_map/reduce_scatter | solution.py:34
  120.5 126.6 %reduce-scatter.9.cloned.1.call-start = ((), (), s32[]{:S(2)}) async-start(), calls=%async_computation.17 | async-start | bytes 1310720 | tf_op jit(solution)/shard_map/reduce_scatter | solution.py:34
  154.6 120.8 %reduce-scatter.7.cloned.1.call-start = ((), (), s32[]{:S(2)}) async-start(), calls=%async_computation.15 | async-start | bytes 1310720 | tf_op jit(solution)/shard_map/reduce_scatter | solution.py:34
  275.4 1.5 copy-start
  275.4 1.5 copy-start.1
  275.4 1.5 copy-start.2
Sparse Core Ops, SparseCore 0:
  27.6 26.9 all-gather.4
  56.5 36.2 all-gather.10
  94.7 31.9 all-gather.8
  128.4 33.1 all-gather.6
  163.8 27.1 reduce-scatter.4
  193.2 25.7 reduce-scatter.10
  221.3 25.7 reduce-scatter.8
  249.5 25.8 reduce-scatter.6

commit v2 on v1

v2 whole, which is shorter than its diff:
```python
import functools

import jax
import jax.numpy as jnp
from jax import lax
from jax.experimental import pallas as pl
from jax.experimental.pallas import tpu as pltpu
from jax.sharding import PartitionSpec as P

TILE = 128
CHUNKS = 4
CORES = 2


def split_kernel(whole_ref, high_ref, low_ref):
    whole = whole_ref[...]
    high = whole.astype(jnp.bfloat16)
    high_ref[...] = high
    low_ref[...] = (whole - high.astype(jnp.float32)).astype(jnp.bfloat16)


def split(whole):
    rows, columns = whole.shape
    block = pl.BlockSpec((256, columns), lambda i: (i, 0))
    half = jax.ShapeDtypeStruct((rows, columns), jnp.bfloat16)
    return pl.pallas_call(
        split_kernel,
        grid=(rows // 256,),
        in_specs=[block],
        out_specs=[block, block],
        out_shape=[half, half],
        cost_estimate=pl.CostEstimate(
            flops=rows * columns, bytes_accessed=8 * rows * columns, transcendentals=0
        ),
        compiler_params=pltpu.CompilerParams(vmem_limit_bytes=16 * 2**20),
        name="split",
    )(whole)


def product_kernel(count, steps, *refs):
    lefts = refs[:count]
    own_high, own_low, other_high, other_low = refs[count : count + 4]
    outs = refs[count + 4 : 2 * count + 4]
    left = refs[2 * count + 4]
    rows = lefts[0].shape[0]
    total = count * rows
    step = pl.program_id(0)

    @pl.when(step == 0)
    def _():
        for k in range(count):
            value = lefts[k][...]
            high = value.astype(jnp.bfloat16)
            left[k * rows : (k + 1) * rows, :] = high
            left[total + k * rows : total + (k + 1) * rows, :] = (
                value - high.astype(jnp.float32)
            ).astype(jnp.bfloat16)

    def multiply(high_ref, low_ref):
        both = jnp.dot(left[...], high_ref[...], preferred_element_type=jnp.float32)
        small = jnp.dot(left[:total, :], low_ref[...], preferred_element_type=jnp.float32)
        result = both[:total] + (both[total:] + small)
        for k in range(count):
            outs[k][...] = result[k * rows : (k + 1) * rows]

    @pl.when(step < steps)
    def _():
        multiply(own_high, own_low)

    @pl.when(step >= steps)
    def _():
        multiply(other_high, other_low)


def product(lefts, own, other):
    count = len(lefts)
    rows, depth = lefts[0].shape
    columns = own[0].shape[1]
    width = min(512, columns)
    steps = columns // width
    total = count * rows
    left_spec = pl.BlockSpec((rows, depth), lambda j: (0, 0))
    own_spec = pl.BlockSpec((depth, width), lambda j: (0, jnp.minimum(j, steps - 1)))
    other_spec = pl.BlockSpec((depth, width), lambda j: (0, jnp.maximum(j - steps, 0)))
    out_spec = pl.BlockSpec((rows, width), lambda j: (0, j))
    return pl.pallas_call(
        functools.partial(product_kernel, count, steps),
        grid=(2 * steps,),
        in_specs=[left_spec] * count + [own_spec] * 2 + [other_spec] * 2,
        out_specs=[out_spec] * count,
        out_shape=[jax.ShapeDtypeStruct((rows, 2 * columns), jnp.float32)] * count,
        scratch_shapes=[pltpu.VMEM((2 * total, depth), jnp.bfloat16)],
        cost_estimate=pl.CostEstimate(
            flops=6 * total * depth * 2 * columns,
            bytes_accessed=8 * depth * columns + 8 * total * depth,
            transcendentals=0,
        ),
        compiler_params=pltpu.CompilerParams(vmem_limit_bytes=40 * 2**20),
        name="product",
    )(*lefts, *own, *other)


def choose(index, arrays):
    chosen = arrays[0]
    for k in range(1, len(arrays)):
        chosen = jnp.where(index == k, arrays[k], chosen)
    return chosen


def shards(amplitudes, integrals, bare_terms, pattern, block_order, occ_gap, virt_gap):
    rows_local, columns = amplitudes.shape
    depth, columns_local = integrals.shape
    rows_out, columns_out = bare_terms.shape
    wide_count = lax.axis_size("wide")
    narrow_count = lax.axis_size("narrow")
    chips = wide_count // CORES
    wide = lax.axis_index("wide")
    z = lax.axis_index("narrow")
    chip = wide // CORES
    core = wide % CORES
    part = rows_local // CHUNKS
    group = chips // narrow_count

    def across(value, mask):
        return lax.ppermute(value, "wide", [(w, w ^ mask) for w in range(wide_count)])

    def across_chips(value, mask):
        return across(value, mask * CORES)

    def along(value, mask):
        return lax.ppermute(value, "narrow", [(n, n ^ mask) for n in range(narrow_count)])

    own = split(integrals)
    other = split(across(integrals, 1))

    tile = (wide * narrow_count + z) * rows_local // TILE
    row_pattern = pattern[block_order[tile]].astype(jnp.float32)
    screen = jnp.repeat(row_pattern, TILE)[None, :]

    def gather(chunk):
        piece = amplitudes[chunk * part : (chunk + 1) * part]

        def slice_for(n):
            return lax.dynamic_slice_in_dim(piece, n * depth, depth, 1) * lax.dynamic_slice_in_dim(
                screen, n * depth, depth, 1
            )

        blocks = [slice_for(z)]
        for mask in range(1, narrow_count):
            blocks.append(along(slice_for(z ^ mask), mask))
        mine = jnp.concatenate([choose(z ^ n, blocks) for n in range(narrow_count)], axis=0)
        lefts = [mine]
        if chips == 4:
            lefts.append(across_chips(mine, 1))
            lefts.append(across_chips(mine, 2))
            if chunk % 2 == 0:
                lefts.append(across_chips(lefts[1], 2))
            else:
                lefts.append(across_chips(lefts[2], 1))
        else:
            for mask in range(1, chips):
                lefts.append(across_chips(mine, mask))
        return lefts

    def reduce(partials):
        arrived = [partials[0]]
        for mask in range(1, chips):
            arrived.append(across_chips(partials[mask], mask))

        def share(n):
            return jnp.concatenate(
                [choose(chip ^ (n * group + j), arrived) for j in range(group)], axis=1
            )

        up = down = None
        for step in range(1, narrow_count):
            send_up = share(z + narrow_count - step)
            send_down = share(z - narrow_count + step)
            if step > 1:
                send_up = send_up + up
                send_down = send_down + down
            up = lax.ppermute(send_up, "narrow", [(n, n + 1) for n in range(step)])
            down = lax.ppermute(
                send_down,
                "narrow",
                [(narrow_count - 1 - n, narrow_count - 2 - n) for n in range(step)],
            )
        return share(z) + (up + down)

    ladders = []
    for chunk in range(CHUNKS):
        partials = product(gather(chunk), own, other)
        ladder = reduce(partials).reshape(narrow_count, part, -1, CORES, columns_local)
        ladder = jnp.where(core == 0, ladder, ladder[:, :, :, ::-1])
        ladders.append(ladder.reshape(narrow_count, part, columns_out))
    ladder = jnp.stack(ladders, axis=1).reshape(rows_out, columns_out)
    denominator = occ_gap[:, None] + virt_gap[None, :]
    return -(bare_terms + ladder) / denominator


def solution(mesh):
    placed = (
        P(("wide", "narrow"), None),
        P("narrow", "wide"),
        P("wide", "narrow"),
        P(),
        P(),
        P("wide"),
        P("narrow"),
    )
    return jax.shard_map(
        shards, mesh=mesh, in_specs=placed, out_specs=P("wide", "narrow"), check_vma=False
    )
```

time: 286 us -> 228 us (0.80)
  blocking collectives: 128 us -> 0 us
  starting transfers between devices: 0.3 us -> 119 us
  waiting for transfers between devices: 101 us -> 50.1 us
  Pallas kernels: 0 us -> 39.3 us
  matrix products: 28.7 us -> 0 us
  between operations: 15.6 us -> 2.79 us
    all_to_all x8 -> x0, blocking collectives: 128 us -> none  [the longest x4 79.8 us: shards(): lax.all_to_all(stacked, 'wide', split_axis=0, concat_axis=1, tiled=True)]
    ppermute x0 -> x61, starting transfers between devices: none -> 119 us  [the longest x12 63.5 us: reduce(): up = lax.ppermute(send_up, 'narrow', [(n, n + 1) for n in range(step)])]
    reduce_scatter x4 -> x0, waiting for transfers between devices: 87.6 us -> none  [shards(): lax.psum_scatter(partial_value, 'narrow', scatter_dimension=1, tiled=True)]
    ppermute x0 -> x61, waiting for transfers between devices: none -> 50.1 us  [the longest x12 26.4 us: reduce(): up = lax.ppermute(send_up, 'narrow', [(n, n + 1) for n in range(step)])]
    pallas_call x0 -> x6, Pallas kernels: none -> 39.3 us  [the longest x4 32.1 us: product(): pl.pallas_call(functools.partial(product_kernel, count, steps), grid=(2 *...]
    dot_general x4 -> x0, matrix products: 28.7 us -> none  [shards(): jnp.dot(lax.all_gather(transposed, 'wide', axis=0, tiled=True), integrals...]
    all_gather x4 -> x0, waiting for transfers between devices: 13.1 us -> none  [shards(): lax.all_gather(transposed, 'wide', axis=0, tiled=True)]
    unnamed x7 -> x12, local copies, waits for them, and re-layouts: 1.5 us -> 7.43 us
  transfers between devices with their start and end apart: 8 -> 61, of which waited for: 6 -> 16; matrix products, arithmetic and copies ran while one was open for 12% -> 2% of each run, Pallas kernels for 0% -> 17%
where the time goes in v2:
time: 228 us; the launch traced here: 225 us
  starting transfers between devices  119 us (52%)
  waiting for transfers between devices  50.1 us (22%)
  Pallas kernels  39.3 us (17%)
  local copies, waits for them, and re-layouts  10 us (4%)
  other arithmetic  4.11 us (2%)
  between operations  2.79 us (1%)
    ppermute x12, starting transfers between devices, reduce(): up = lax.ppermute(send_up, 'narrow', [(n, n + 1) for n in range(step)])  63.5 us
    pallas_call x4, Pallas kernels, product(): pl.pallas_call(functools.partial(product_kernel, count, steps), grid=(2 *...  32.1 us
    ppermute x25, starting transfers between devices, across(): lax.ppermute(value, 'wide', [(w, w ^ mask) for w in range(wide_count)])  27.5 us
    ppermute x12, waiting for transfers between devices, reduce(): up = lax.ppermute(send_up, 'narrow', [(n, n + 1) for n in range(step)])  26.4 us
    ppermute x12, starting transfers between devices, along(): lax.ppermute(value, 'narrow', [(n, n ^ mask) for n in range(narrow_count)])  17.2 us
    ppermute x25, waiting for transfers between devices, across(): lax.ppermute(value, 'wide', [(w, w ^ mask) for w in range(wide_count)])  16 us
    ppermute x12, starting transfers between devices, reduce(): lax.ppermute(send_down, 'narrow', [(narrow_count - 1 - n, narrow_count -...  10.7 us
    ppermute x12, waiting for transfers between devices, along(): lax.ppermute(value, 'narrow', [(n, n ^ mask) for n in range(narrow_count)])  7.57 us
  transfers between devices with their start and end apart: 61, of which 16 were waited for; matrix products, arithmetic and copies ran while one was open for 2% of the time, Pallas kernels for 17%

profile of v2, /device:TPU:0, one launch (start us, length us, event | category | flops | bytes accessed | tf_op | source)
XLA Modules:
  0.0 225.3 jit_solution(9659189929507059065)
XLA Ops:
  5.8 4.7 %collective-permute-start = (f32[8,2048]{1,0:T(8,128)S(1)}, f32[8,2048]{1,0:T(8,128)S(1)}, u32[]{:S(2)}, u32[]{:S(2)}) collective-permute-start(f32[8,2048]{1,0:T(8,128)S(1)} %get-tuple-element.89), channel_id=1, source_target_pairs={{0,3},{1,2},{2,1},{3,0},{4,7},{5,6},{6,5},{7,4},{8,11},{9,10},{10,... | collective-permute-start | bytes 196616 | tf_op jit(solution)/shard_map/ppermute | solution.py:131
  11.1 3.7 %collective-permute-start.16 = (f32[8,2048]{1,0:T(8,128)S(1)}, f32[8,2048]{1,0:T(8,128)S(1)}, u32[]{:S(2)}, u32[]{:S(2)}) collective-permute-start(f32[8,2048]{1,0:T(8,128)S(1)} %get-tuple-element.92), channel_id=1, source_target_pairs={{0,3},{1,2},{2,1},{3,0},{4,7},{5,6},{6,5},{7,4},{8,11},{9,10},{10,... | collective-permute-start | bytes 196616 | tf_op jit(solution)/shard_map/ppermute | solution.py:131
  14.9 3.4 %copy-done.2 = f32[2048,1024]{1,0:T(8,128)S(1)} copy-done((f32[2048,1024]{1,0:T(8,128)S(1)}, f32[2048,1024]{1,0:T(8,128)}, u32[]{:S(2)}) %copy-start.2) | copy-done | bytes 8388632
  20.2 3.7 %collective-permute-start.31 = (f32[8,2048]{1,0:T(8,128)S(1)}, f32[8,2048]{1,0:T(8,128)S(1)}, u32[]{:S(2)}, u32[]{:S(2)}) collective-permute-start(f32[8,2048]{1,0:T(8,128)S(1)} %get-tuple-element.95), channel_id=1, source_target_pairs={{0,3},{1,2},{2,1},{3,0},{4,7},{5,6},{6,5},{7,4},{8,11},{9,10},{10,... | collective-permute-start | bytes 196616 | tf_op jit(solution)/shard_map/ppermute | solution.py:131
  24.1 4.1 %collective-permute-done.17 = f32[8,2048]{1,0:T(8,128)S(1)} collective-permute-done((f32[8,2048]{1,0:T(8,128)S(1)}, f32[8,2048]{1,0:T(8,128)S(1)}, u32[]{:S(2)}, u32[]{:S(2)}) %collective-permute-start.17) | collective-permute-done | bytes 65568 | tf_op jit(solution)/shard_map/ppermute | solution.py:131
  28.5 3.3 %collective-permute-start.47 = (f32[8,2048]{1,0:T(8,128)S(1)}, f32[8,2048]{1,0:T(8,128)S(1)}, u32[]{:S(2)}, u32[]{:S(2)}) collective-permute-start(f32[8,2048]{1,0:T(8,128)S(1)} %get-tuple-element.83), channel_id=1, source_target_pairs={{0,2},{1,3},{2,0},{3,1},{4,6},{5,7},{6,4},{7,5},{8,10},{9,11},{10,... | collective-permute-start | bytes 196616 | tf_op jit(solution)/shard_map/ppermute | solution.py:131
  39.6 4.9 %collective-permute-done.3.refs_1_ = f32[32,2048]{1,0:T(8,128)S(1)} collective-permute-done((f32[32,2048]{1,0:T(8,128)S(1)}, f32[32,2048]{1,0:T(8,128)S(1)}, u32[]{:S(2)}, u32[]{:S(2)}) %collective-permute-start.3) | collective-permute-done | bytes 262176 | tf_op jit(solution)/shard_map/ppermute | solution.py:125
  47.7 6.0 %split.3 = (bf16[2048,1024]{1,0:T(8,128)(2,1)S(1)}, bf16[2048,1024]{1,0:T(8,128)(2,1)S(1)}) custom-call(f32[2048,1024]{1,0:T(8,128)} %collective-permute-done.6.whole_ref), custom_call_target="tpu_custom_call" | custom-call | flops 2097152 | bytes 16777216 | tf_op jit(solution)/shard_map/split/pallas_call | solution.py:26
  60.3 8.0 %product.4 = (f32[32,2048]{1,0:T(8,128)S(1)}, f32[32,2048]{1,0:T(8,128)S(1)}, f32[32,2048]{1,0:T(8,128)S(1)}, f32[32,2048]{1,0:T(8,128)S(1)}) custom-call(f32[32,2048]{1,0:T(8,128)S(1)} %pad_maximum_fusion.1.refs_0_, f32[32,2048]{1,0:T(8,128)S(1)} %collective-permute-done.3.refs_1_, f32[32,2048]{1,0:T(8,128)S(1)} %collective-permute-done.4.refs_2_, ...), custom_call_target="tpu_custom_call" | custom-call | flops 3221225472 | bytes 18874368 | tf_op jit(solution)/shard_map/product/pallas_call | solution.py:86
  73.4 8.0 %product.5 = (f32[32,2048]{1,0:T(8,128)S(1)}, f32[32,2048]{1,0:T(8,128)S(1)}, f32[32,2048]{1,0:T(8,128)S(1)}, f32[32,2048]{1,0:T(8,128)S(1)}) custom-call(f32[32,2048]{1,0:T(8,128)S(1)} %pad_maximum_fusion.2.refs_0_, f32[32,2048]{1,0:T(8,128)S(1)} %collective-permute-done.19.refs_1_, f32[32,2048]{1,0:T(8,128)S(1)} %collective-permute-done.20.refs_2_, ...), custom_call_target="tpu_custom_call" | custom-call | flops 3221225472 | bytes 18874368 | tf_op jit(solution)/shard_map/product/pallas_call | solution.py:86
  82.5 8.0 %product.6 = (f32[32,2048]{1,0:T(8,128)S(1)}, f32[32,2048]{1,0:T(8,128)S(1)}, f32[32,2048]{1,0:T(8,128)S(1)}, f32[32,2048]{1,0:T(8,128)S(1)}) custom-call(f32[32,2048]{1,0:T(8,128)S(1)} %pad_maximum_fusion.3.refs_0_, f32[32,2048]{1,0:T(8,128)S(1)} %collective-permute-done.34.refs_1_, f32[32,2048]{1,0:T(8,128)S(1)} %collective-permute-done.35.refs_2_, ...), custom_call_target="tpu_custom_call" | custom-call | flops 3221225472 | bytes 18874368 | tf_op jit(solution)/shard_map/product/pallas_call | solution.py:86
  93.6 8.0 %product.7 = (f32[32,2048]{1,0:T(8,128)S(1)}, f32[32,2048]{1,0:T(8,128)S(1)}, f32[32,2048]{1,0:T(8,128)S(1)}, f32[32,2048]{1,0:T(8,128)S(1)}) custom-call(f32[32,2048]{1,0:T(8,128)S(1)} %pad_maximum_fusion.4.refs_0_, f32[32,2048]{1,0:T(8,128)S(1)} %collective-permute-done.49.refs_1_, f32[32,2048]{1,0:T(8,128)S(1)} %collective-permute-done.50.refs_2_, ...), custom_call_target="tpu_custom_call" | custom-call | flops 3221225472 | bytes 18874368 | tf_op jit(solution)/shard_map/product/pallas_call | solution.py:86
  105.9 4.1 %collective-permute-done.23 = f32[32,2048]{1,0:T(8,128)S(1)} collective-permute-done((f32[32,2048]{1,0:T(8,128)S(1)}, f32[32,2048]{1,0:T(8,128)S(1)}, u32[]{:S(2)}, u32[]{:S(2)}) %collective-permute-start.23) | collective-permute-done | bytes 262176 | tf_op jit(solution)/shard_map/ppermute | solution.py:125
  112.5 3.1 %collective-permute-done.37 = f32[32,2048]{1,0:T(8,128)S(1)} collective-permute-done((f32[32,2048]{1,0:T(8,128)S(1)}, f32[32,2048]{1,0:T(8,128)S(1)}, u32[]{:S(2)}, u32[]{:S(2)}) %collective-permute-start.37) | collective-permute-done | bytes 262176 | tf_op jit(solution)/shard_map/ppermute | solution.py:125
  127.2 11.5 %collective-permute-start.10 = (f32[32,2048]{1,0:T(8,128)S(1)}, f32[32,2048]{1,0:T(8,128)S(1)}, u32[]{:S(2)}, u32[]{:S(2)}) collective-permute-start(f32[32,2048]{1,0:T(8,128)S(1)} %get-tuple-element.46), channel_id=1, source_target_pairs={{0,1},{4,5},{8,9},{12,13},{16,17},{20,21},{24,25},{28,29}} | collective-permute-start | bytes 786440 | tf_op jit(solution)/shard_map/ppermute | solution.py:182
  140.1 4.6 %collective-permute-start.25 = (f32[32,2048]{1,0:T(8,128)S(1)}, f32[32,2048]{1,0:T(8,128)S(1)}, u32[]{:S(2)}, u32[]{:S(2)}) collective-permute-start(f32[32,2048]{1,0:T(8,128)S(1)} %get-tuple-element.52), channel_id=1, source_target_pairs={{0,1},{4,5},{8,9},{12,13},{16,17},{20,21},{24,25},{28,29}} | collective-permute-start | bytes 786440 | tf_op jit(solution)/shard_map/ppermute | solution.py:182
  146.1 8.7 %collective-permute-start.40 = (f32[32,2048]{1,0:T(8,128)S(1)}, f32[32,2048]{1,0:T(8,128)S(1)}, u32[]{:S(2)}, u32[]{:S(2)}) collective-permute-start(f32[32,2048]{1,0:T(8,128)S(1)} %get-tuple-element.54), channel_id=1, source_target_pairs={{0,1},{4,5},{8,9},{12,13},{16,17},{20,21},{24,25},{28,29}} | collective-permute-start | bytes 786440 | tf_op jit(solution)/shard_map/ppermute | solution.py:182
  156.2 4.6 %collective-permute-start.55 = (f32[32,2048]{1,0:T(8,128)S(1)}, f32[32,2048]{1,0:T(8,128)S(1)}, u32[]{:S(2)}, u32[]{:S(2)}) collective-permute-start(f32[32,2048]{1,0:T(8,128)S(1)} %get-tuple-element.56), channel_id=1, source_target_pairs={{0,1},{4,5},{8,9},{12,13},{16,17},{20,21},{24,25},{28,29}} | collective-permute-start | bytes 786440 | tf_op jit(solution)/shard_map/ppermute | solution.py:182
  162.2 4.2 %collective-permute-done.55 = f32[32,2048]{1,0:T(8,128)S(1)} collective-permute-done((f32[32,2048]{1,0:T(8,128)S(1)}, f32[32,2048]{1,0:T(8,128)S(1)}, u32[]{:S(2)}, u32[]{:S(2)}) %collective-permute-start.55) | collective-permute-done | bytes 262176 | tf_op jit(solution)/shard_map/ppermute | solution.py:182
  166.5 4.4 %collective-permute-start.11 = (f32[32,2048]{1,0:T(8,128)S(1)}, f32[32,2048]{1,0:T(8,128)S(1)}, u32[]{:S(2)}, u32[]{:S(2)}) collective-permute-start(f32[32,2048]{1,0:T(8,128)S(1)} %select_add_fusion.14), channel_id=1, source_target_pairs={{0,1},{1,2},{4,5},{5,6},{8,9},{9,10},{12,13},{13,14},{16,17},{17,1... | collective-permute-start | bytes 786440 | tf_op jit(solution)/shard_map/ppermute | solution.py:182
  170.9 4.8 %collective-permute-done.11 = f32[32,2048]{1,0:T(8,128)S(1)} collective-permute-done((f32[32,2048]{1,0:T(8,128)S(1)}, f32[32,2048]{1,0:T(8,128)S(1)}, u32[]{:S(2)}, u32[]{:S(2)}) %collective-permute-start.11) | collective-permute-done | bytes 262176 | tf_op jit(solution)/shard_map/ppermute | solution.py:182
  175.7 4.4 %collective-permute-start.26 = (f32[32,2048]{1,0:T(8,128)S(1)}, f32[32,2048]{1,0:T(8,128)S(1)}, u32[]{:S(2)}, u32[]{:S(2)}) collective-permute-start(f32[32,2048]{1,0:T(8,128)S(1)} %select_add_fusion.10), channel_id=1, source_target_pairs={{0,1},{1,2},{4,5},{5,6},{8,9},{9,10},{12,13},{13,14},{16,17},{17,1... | collective-permute-start | bytes 786440 | tf_op jit(solution)/shard_map/ppermute | solution.py:182
  180.2 3.8 %collective-permute-done.26 = f32[32,2048]{1,0:T(8,128)S(1)} collective-permute-done((f32[32,2048]{1,0:T(8,128)S(1)}, f32[32,2048]{1,0:T(8,128)S(1)}, u32[]{:S(2)}, u32[]{:S(2)}) %collective-permute-start.26) | collective-permute-done | bytes 262176 | tf_op jit(solution)/shard_map/ppermute | solution.py:182
  184.0 4.9 %collective-permute-start.41 = (f32[32,2048]{1,0:T(8,128)S(1)}, f32[32,2048]{1,0:T(8,128)S(1)}, u32[]{:S(2)}, u32[]{:S(2)}) collective-permute-start(f32[32,2048]{1,0:T(8,128)S(1)} %select_add_fusion.6), channel_id=1, source_target_pairs={{0,1},{1,2},{4,5},{5,6},{8,9},{9,10},{12,13},{13,14},{16,17},{17,1... | collective-permute-start | bytes 786440 | tf_op jit(solution)/shard_map/ppermute | solution.py:182
  189.0 6.2 %collective-permute-done.41 = f32[32,2048]{1,0:T(8,128)S(1)} collective-permute-done((f32[32,2048]{1,0:T(8,128)S(1)}, f32[32,2048]{1,0:T(8,128)S(1)}, u32[]{:S(2)}, u32[]{:S(2)}) %collective-permute-start.41) | collective-permute-done | bytes 262176 | tf_op jit(solution)/shard_map/ppermute | solution.py:182
  195.2 4.4 %collective-permute-start.56 = (f32[32,2048]{1,0:T(8,128)S(1)}, f32[32,2048]{1,0:T(8,128)S(1)}, u32[]{:S(2)}, u32[]{:S(2)}) collective-permute-start(f32[32,2048]{1,0:T(8,128)S(1)} %select_add_fusion.2), channel_id=1, source_target_pairs={{0,1},{1,2},{4,5},{5,6},{8,9},{9,10},{12,13},{13,14},{16,17},{17,1... | collective-permute-start | bytes 786440 | tf_op jit(solution)/shard_map/ppermute | solution.py:182
  199.7 3.8 %collective-permute-done.56 = f32[32,2048]{1,0:T(8,128)S(1)} collective-permute-done((f32[32,2048]{1,0:T(8,128)S(1)}, f32[32,2048]{1,0:T(8,128)S(1)}, u32[]{:S(2)}, u32[]{:S(2)}) %collective-permute-start.56) | collective-permute-done | bytes 262176 | tf_op jit(solution)/shard_map/ppermute | solution.py:182
  203.4 4.4 %collective-permute-start.12 = (f32[32,2048]{1,0:T(8,128)S(1)}, f32[32,2048]{1,0:T(8,128)S(1)}, u32[]{:S(2)}, u32[]{:S(2)}) collective-permute-start(f32[32,2048]{1,0:T(8,128)S(1)} %select_add_fusion.15), channel_id=1, source_target_pairs={{0,1},{1,2},{2,3},{4,5},{5,6},{6,7},{8,9},{9,10},{10,11},{12,13},{... | collective-permute-start | bytes 786440 | tf_op jit(solution)/shard_map/ppermute | solution.py:182
  207.9 3.7 %collective-permute-start.27 = (f32[32,2048]{1,0:T(8,128)S(1)}, f32[32,2048]{1,0:T(8,128)S(1)}, u32[]{:S(2)}, u32[]{:S(2)}) collective-permute-start(f32[32,2048]{1,0:T(8,128)S(1)} %select_add_fusion.11), channel_id=1, source_target_pairs={{0,1},{1,2},{2,3},{4,5},{5,6},{6,7},{8,9},{9,10},{10,11},{12,13},{... | collective-permute-start | bytes 786440 | tf_op jit(solution)/shard_map/ppermute | solution.py:182
  211.7 4.4 %collective-permute-start.42 = (f32[32,2048]{1,0:T(8,128)S(1)}, f32[32,2048]{1,0:T(8,128)S(1)}, u32[]{:S(2)}, u32[]{:S(2)}) collective-permute-start(f32[32,2048]{1,0:T(8,128)S(1)} %select_add_fusion.7), channel_id=1, source_target_pairs={{0,1},{1,2},{2,3},{4,5},{5,6},{6,7},{8,9},{9,10},{10,11},{12,13},{... | collective-permute-start | bytes 786440 | tf_op jit(solution)/shard_map/ppermute | solution.py:182
  216.2 3.7 %collective-permute-start.57 = (f32[32,2048]{1,0:T(8,128)S(1)}, f32[32,2048]{1,0:T(8,128)S(1)}, u32[]{:S(2)}, u32[]{:S(2)}) collective-permute-start(f32[32,2048]{1,0:T(8,128)S(1)} %select_add_fusion.3), channel_id=1, source_target_pairs={{0,1},{1,2},{2,3},{4,5},{5,6},{6,7},{8,9},{9,10},{10,11},{12,13},{... | collective-permute-start | bytes 786440 | tf_op jit(solution)/shard_map/ppermute | solution.py:182
  220.2 3.5 %collective-permute-done.57 = f32[32,2048]{1,0:T(8,128)S(1)} collective-permute-done((f32[32,2048]{1,0:T(8,128)S(1)}, f32[32,2048]{1,0:T(8,128)S(1)}, u32[]{:S(2)}, u32[]{:S(2)}) %collective-permute-start.57) | collective-permute-done | bytes 262176 | tf_op jit(solution)/shard_map/ppermute | solution.py:182
  (150 shorter events, 59.5 us)
Async XLA Ops:
  0.0 46.1 %collective-permute-start.6 = (f32[2048,1024]{1,0:T(8,128)}, f32[2048,1024]{1,0:T(8,128)}, u32[]{:S(2)}, u32[]{:S(2)}) collective-permute-start(f32[2048,1024]{1,0:T(8,128)} %whole_ref.1), channel_id=1, source_target_pairs={{0,4},{4,0},{8,12},{12,8},{16,20},{20,16},{24,28},{28,24},{1,5},{5... | collective-permute-start | bytes 25165832 | tf_op jit(solution)/shard_map/ppermute | solution.py:125
  5.8 13.7 %collective-permute-start = (f32[8,2048]{1,0:T(8,128)S(1)}, f32[8,2048]{1,0:T(8,128)S(1)}, u32[]{:S(2)}, u32[]{:S(2)}) collective-permute-start(f32[8,2048]{1,0:T(8,128)S(1)} %get-tuple-element.89), channel_id=1, source_target_pairs={{0,3},{1,2},{2,1},{3,0},{4,7},{5,6},{6,5},{7,4},{8,11},{9,10},{10,... | collective-permute-start | bytes 196616 | tf_op jit(solution)/shard_map/ppermute | solution.py:131
  11.1 12.9 %collective-permute-start.16 = (f32[8,2048]{1,0:T(8,128)S(1)}, f32[8,2048]{1,0:T(8,128)S(1)}, u32[]{:S(2)}, u32[]{:S(2)}) collective-permute-start(f32[8,2048]{1,0:T(8,128)S(1)} %get-tuple-element.92), channel_id=1, source_target_pairs={{0,3},{1,2},{2,1},{3,0},{4,7},{5,6},{6,5},{7,4},{8,11},{9,10},{10,... | collective-permute-start | bytes 196616 | tf_op jit(solution)/shard_map/ppermute | solution.py:131
  37.0 20.8 %collective-permute-start.4 = (f32[32,2048]{1,0:T(8,128)S(1)}, f32[32,2048]{1,0:T(8,128)S(1)}, u32[]{:S(2)}, u32[]{:S(2)}) collective-permute-start(f32[32,2048]{1,0:T(8,128)S(1)} %pad_maximum_fusion.1.refs_0_), channel_id=1, source_target_pairs={{0,16},{4,20},{8,24},{12,28},{16,0},{20,4},{24,8},{28,12},{1,17},{... | collective-permute-start | bytes 786440 | tf_op jit(solution)/shard_map/ppermute | solution.py:125
  38.5 19.7 %collective-permute-start.20 = (f32[32,2048]{1,0:T(8,128)S(1)}, f32[32,2048]{1,0:T(8,128)S(1)}, u32[]{:S(2)}, u32[]{:S(2)}) collective-permute-start(f32[32,2048]{1,0:T(8,128)S(1)} %pad_maximum_fusion.2.refs_0_), channel_id=1, source_target_pairs={{0,16},{4,20},{8,24},{12,28},{16,0},{20,4},{24,8},{28,12},{1,17},{... | collective-permute-start | bytes 786440 | tf_op jit(solution)/shard_map/ppermute | solution.py:125
  39.1 29.3 %collective-permute-start.19 = (f32[32,2048]{1,0:T(8,128)S(1)}, f32[32,2048]{1,0:T(8,128)S(1)}, u32[]{:S(2)}, u32[]{:S(2)}) collective-permute-start(f32[32,2048]{1,0:T(8,128)S(1)} %pad_maximum_fusion.2.refs_0_), channel_id=1, source_target_pairs={{0,8},{4,12},{8,0},{12,4},{16,24},{20,28},{24,16},{28,20},{1,9},{5... | collective-permute-start | bytes 786440 | tf_op jit(solution)/shard_map/ppermute | solution.py:125
  44.5 15.2 %collective-permute-start.5 = (f32[32,2048]{1,0:T(8,128)S(1)}, f32[32,2048]{1,0:T(8,128)S(1)}, u32[]{:S(2)}, u32[]{:S(2)}) collective-permute-start(f32[32,2048]{1,0:T(8,128)S(1)} %collective-permute-done.3.refs_1_), channel_id=1, source_target_pairs={{0,16},{4,20},{8,24},{12,28},{16,0},{20,4},{24,8},{28,12},{1,17},{... | collective-permute-start | bytes 786440 | tf_op jit(solution)/shard_map/ppermute | solution.py:125
  46.1 23.8 %collective-permute-start.34 = (f32[32,2048]{1,0:T(8,128)S(1)}, f32[32,2048]{1,0:T(8,128)S(1)}, u32[]{:S(2)}, u32[]{:S(2)}) collective-permute-start(f32[32,2048]{1,0:T(8,128)S(1)} %pad_maximum_fusion.3.refs_0_), channel_id=1, source_target_pairs={{0,8},{4,12},{8,0},{12,4},{16,24},{20,28},{24,16},{28,20},{1,9},{5... | collective-permute-start | bytes 786440 | tf_op jit(solution)/shard_map/ppermute | solution.py:125
  57.7 23.7 %collective-permute-start.35 = (f32[32,2048]{1,0:T(8,128)S(1)}, f32[32,2048]{1,0:T(8,128)S(1)}, u32[]{:S(2)}, u32[]{:S(2)}) collective-permute-start(f32[32,2048]{1,0:T(8,128)S(1)} %pad_maximum_fusion.3.refs_0_), channel_id=1, source_target_pairs={{0,16},{4,20},{8,24},{12,28},{16,0},{20,4},{24,8},{28,12},{1,17},{... | collective-permute-start | bytes 786440 | tf_op jit(solution)/shard_map/ppermute | solution.py:125
  58.3 12.2 %collective-permute-start.50 = (f32[32,2048]{1,0:T(8,128)S(1)}, f32[32,2048]{1,0:T(8,128)S(1)}, u32[]{:S(2)}, u32[]{:S(2)}) collective-permute-start(f32[32,2048]{1,0:T(8,128)S(1)} %pad_maximum_fusion.4.refs_0_), channel_id=1, source_target_pairs={{0,16},{4,20},{8,24},{12,28},{16,0},{20,4},{24,8},{28,12},{1,17},{... | collective-permute-start | bytes 786440 | tf_op jit(solution)/shard_map/ppermute | solution.py:125
  68.3 22.2 %collective-permute-start.49 = (f32[32,2048]{1,0:T(8,128)S(1)}, f32[32,2048]{1,0:T(8,128)S(1)}, u32[]{:S(2)}, u32[]{:S(2)}) collective-permute-start(f32[32,2048]{1,0:T(8,128)S(1)} %pad_maximum_fusion.4.refs_0_), channel_id=1, source_target_pairs={{0,8},{4,12},{8,0},{12,4},{16,24},{20,28},{24,16},{28,20},{1,9},{5... | collective-permute-start | bytes 786440 | tf_op jit(solution)/shard_map/ppermute | solution.py:125
  69.9 12.1 %collective-permute-start.36 = (f32[32,2048]{1,0:T(8,128)S(1)}, f32[32,2048]{1,0:T(8,128)S(1)}, u32[]{:S(2)}, u32[]{:S(2)}) collective-permute-start(f32[32,2048]{1,0:T(8,128)S(1)} %collective-permute-done.34.refs_1_), channel_id=1, source_target_pairs={{0,16},{4,20},{8,24},{12,28},{16,0},{20,4},{24,8},{28,12},{1,17},{... | collective-permute-start | bytes 786440 | tf_op jit(solution)/shard_map/ppermute | solution.py:125
  70.4 22.7 %collective-permute-start.51 = (f32[32,2048]{1,0:T(8,128)S(1)}, f32[32,2048]{1,0:T(8,128)S(1)}, u32[]{:S(2)}, u32[]{:S(2)}) collective-permute-start(f32[32,2048]{1,0:T(8,128)S(1)} %collective-permute-done.50.refs_2_), channel_id=1, source_target_pairs={{0,8},{4,12},{8,0},{12,4},{16,24},{20,28},{24,16},{28,20},{1,9},{5... | collective-permute-start | bytes 786440 | tf_op jit(solution)/shard_map/ppermute | solution.py:125
  71.0 30.7 %collective-permute-start.7 = (f32[32,2048]{1,0:T(8,128)S(1)}, f32[32,2048]{1,0:T(8,128)S(1)}, u32[]{:S(2)}, u32[]{:S(2)}) collective-permute-start(f32[32,2048]{1,0:T(8,128)S(1)} %get-tuple-element.29), channel_id=1, source_target_pairs={{0,24},{4,28},{8,16},{12,20},{16,8},{20,12},{24,0},{28,4},{1,25},{... | collective-permute-start | bytes 786440 | tf_op jit(solution)/shard_map/ppermute | solution.py:125
  81.4 20.8 %collective-permute-start.8 = (f32[32,2048]{1,0:T(8,128)S(1)}, f32[32,2048]{1,0:T(8,128)S(1)}, u32[]{:S(2)}, u32[]{:S(2)}) collective-permute-start(f32[32,2048]{1,0:T(8,128)S(1)} %get-tuple-element.30), channel_id=1, source_target_pairs={{0,16},{4,20},{8,24},{12,28},{16,0},{20,4},{24,8},{28,12},{1,17},{... | collective-permute-start | bytes 786440 | tf_op jit(solution)/shard_map/ppermute | solution.py:125
  82.0 22.7 %collective-permute-start.9 = (f32[32,2048]{1,0:T(8,128)S(1)}, f32[32,2048]{1,0:T(8,128)S(1)}, u32[]{:S(2)}, u32[]{:S(2)}) collective-permute-start(f32[32,2048]{1,0:T(8,128)S(1)} %get-tuple-element.31), channel_id=1, source_target_pairs={{0,8},{4,12},{8,0},{12,4},{16,24},{20,28},{24,16},{28,20},{1,9},{5... | collective-permute-start | bytes 786440 | tf_op jit(solution)/shard_map/ppermute | solution.py:125
  90.6 14.7 %collective-permute-start.22 = (f32[32,2048]{1,0:T(8,128)S(1)}, f32[32,2048]{1,0:T(8,128)S(1)}, u32[]{:S(2)}, u32[]{:S(2)}) collective-permute-start(f32[32,2048]{1,0:T(8,128)S(1)} %get-tuple-element.33), channel_id=1, source_target_pairs={{0,24},{4,28},{8,16},{12,20},{16,8},{20,12},{24,0},{28,4},{1,25},{... | collective-permute-start | bytes 786440 | tf_op jit(solution)/shard_map/ppermute | solution.py:125
  93.1 16.9 %collective-permute-start.23 = (f32[32,2048]{1,0:T(8,128)S(1)}, f32[32,2048]{1,0:T(8,128)S(1)}, u32[]{:S(2)}, u32[]{:S(2)}) collective-permute-start(f32[32,2048]{1,0:T(8,128)S(1)} %get-tuple-element.34), channel_id=1, source_target_pairs={{0,16},{4,20},{8,24},{12,28},{16,0},{20,4},{24,8},{28,12},{1,17},{... | collective-permute-start | bytes 786440 | tf_op jit(solution)/shard_map/ppermute | solution.py:125
  102.2 13.4 %collective-permute-start.37 = (f32[32,2048]{1,0:T(8,128)S(1)}, f32[32,2048]{1,0:T(8,128)S(1)}, u32[]{:S(2)}, u32[]{:S(2)}) collective-permute-start(f32[32,2048]{1,0:T(8,128)S(1)} %get-tuple-element.37), channel_id=1, source_target_pairs={{0,24},{4,28},{8,16},{12,20},{16,8},{20,12},{24,0},{28,4},{1,25},{... | collective-permute-start | bytes 786440 | tf_op jit(solution)/shard_map/ppermute | solution.py:125
  104.7 12.4 %collective-permute-start.38 = (f32[32,2048]{1,0:T(8,128)S(1)}, f32[32,2048]{1,0:T(8,128)S(1)}, u32[]{:S(2)}, u32[]{:S(2)}) collective-permute-start(f32[32,2048]{1,0:T(8,128)S(1)} %get-tuple-element.38), channel_id=1, source_target_pairs={{0,16},{4,20},{8,24},{12,28},{16,0},{20,4},{24,8},{28,12},{1,17},{... | collective-permute-start | bytes 786440 | tf_op jit(solution)/shard_map/ppermute | solution.py:125
  105.3 12.5 %collective-permute-start.39 = (f32[32,2048]{1,0:T(8,128)S(1)}, f32[32,2048]{1,0:T(8,128)S(1)}, u32[]{:S(2)}, u32[]{:S(2)}) collective-permute-start(f32[32,2048]{1,0:T(8,128)S(1)} %get-tuple-element.39), channel_id=1, source_target_pairs={{0,8},{4,12},{8,0},{12,4},{16,24},{20,28},{24,16},{28,20},{1,9},{5... | collective-permute-start | bytes 786440 | tf_op jit(solution)/shard_map/ppermute | solution.py:125
  124.7 15.3 %collective-permute-start.29 = (f32[32,2048]{1,0:T(8,128)S(1)}, f32[32,2048]{1,0:T(8,128)S(1)}, u32[]{:S(2)}, u32[]{:S(2)}) collective-permute-start(f32[32,2048]{1,0:T(8,128)S(1)} %select_add_fusion.8), channel_id=1, source_target_pairs={{3,2},{2,1},{7,6},{6,5},{11,10},{10,9},{15,14},{14,13},{19,18},{18... | collective-permute-start | bytes 786440 | tf_op jit(solution)/shard_map/ppermute | solution.py:183
  125.6 19.0 %collective-permute-start.44 = (f32[32,2048]{1,0:T(8,128)S(1)}, f32[32,2048]{1,0:T(8,128)S(1)}, u32[]{:S(2)}, u32[]{:S(2)}) collective-permute-start(f32[32,2048]{1,0:T(8,128)S(1)} %select_add_fusion.4), channel_id=1, source_target_pairs={{3,2},{2,1},{7,6},{6,5},{11,10},{10,9},{15,14},{14,13},{19,18},{18... | collective-permute-start | bytes 786440 | tf_op jit(solution)/shard_map/ppermute | solution.py:183
  126.4 19.6 %collective-permute-start.59 = (f32[32,2048]{1,0:T(8,128)S(1)}, f32[32,2048]{1,0:T(8,128)S(1)}, u32[]{:S(2)}, u32[]{:S(2)}) collective-permute-start(f32[32,2048]{1,0:T(8,128)S(1)} %select_add_fusion), channel_id=1, source_target_pairs={{3,2},{2,1},{7,6},{6,5},{11,10},{10,9},{15,14},{14,13},{19,18},{18... | collective-permute-start | bytes 786440 | tf_op jit(solution)/shard_map/ppermute | solution.py:183
  127.2 27.6 %collective-permute-start.10 = (f32[32,2048]{1,0:T(8,128)S(1)}, f32[32,2048]{1,0:T(8,128)S(1)}, u32[]{:S(2)}, u32[]{:S(2)}) collective-permute-start(f32[32,2048]{1,0:T(8,128)S(1)} %get-tuple-element.46), channel_id=1, source_target_pairs={{0,1},{4,5},{8,9},{12,13},{16,17},{20,21},{24,25},{28,29}} | collective-permute-start | bytes 786440 | tf_op jit(solution)/shard_map/ppermute | solution.py:182
  138.7 69.2 %collective-permute-start.15 = (f32[32,2048]{1,0:T(8,128)S(1)}, f32[32,2048]{1,0:T(8,128)S(1)}, u32[]{:S(2)}, u32[]{:S(2)}) collective-permute-start(f32[32,2048]{1,0:T(8,128)S(1)} %get-tuple-element.45), channel_id=1, source_target_pairs={{3,2},{2,1},{1,0},{7,6},{6,5},{5,4},{11,10},{10,9},{9,8},{15,14},{... | collective-permute-start | bytes 786440 | tf_op jit(solution)/shard_map/ppermute | solution.py:183
  140.1 16.1 %collective-permute-start.25 = (f32[32,2048]{1,0:T(8,128)S(1)}, f32[32,2048]{1,0:T(8,128)S(1)}, u32[]{:S(2)}, u32[]{:S(2)}) collective-permute-start(f32[32,2048]{1,0:T(8,128)S(1)} %get-tuple-element.52), channel_id=1, source_target_pairs={{0,1},{4,5},{8,9},{12,13},{16,17},{20,21},{24,25},{28,29}} | collective-permute-start | bytes 786440 | tf_op jit(solution)/shard_map/ppermute | solution.py:182
  144.7 71.5 %collective-permute-start.30 = (f32[32,2048]{1,0:T(8,128)S(1)}, f32[32,2048]{1,0:T(8,128)S(1)}, u32[]{:S(2)}, u32[]{:S(2)}) collective-permute-start(f32[32,2048]{1,0:T(8,128)S(1)} %get-tuple-element.51), channel_id=1, source_target_pairs={{3,2},{2,1},{1,0},{7,6},{6,5},{5,4},{11,10},{10,9},{9,8},{15,14},{... | collective-permute-start | bytes 786440 | tf_op jit(solution)/shard_map/ppermute | solution.py:183
  146.1 14.8 %collective-permute-start.40 = (f32[32,2048]{1,0:T(8,128)S(1)}, f32[32,2048]{1,0:T(8,128)S(1)}, u32[]{:S(2)}, u32[]{:S(2)}) collective-permute-start(f32[32,2048]{1,0:T(8,128)S(1)} %get-tuple-element.54), channel_id=1, source_target_pairs={{0,1},{4,5},{8,9},{12,13},{16,17},{20,21},{24,25},{28,29}} | collective-permute-start | bytes 786440 | tf_op jit(solution)/shard_map/ppermute | solution.py:182
  154.8 65.2 %collective-permute-start.45 = (f32[32,2048]{1,0:T(8,128)S(1)}, f32[32,2048]{1,0:T(8,128)S(1)}, u32[]{:S(2)}, u32[]{:S(2)}) collective-permute-start(f32[32,2048]{1,0:T(8,128)S(1)} %get-tuple-element.53), channel_id=1, source_target_pairs={{3,2},{2,1},{1,0},{7,6},{6,5},{5,4},{11,10},{10,9},{9,8},{15,14},{... | collective-permute-start | bytes 786440 | tf_op jit(solution)/shard_map/ppermute | solution.py:183
  160.9 59.3 %collective-permute-start.60 = (f32[32,2048]{1,0:T(8,128)S(1)}, f32[32,2048]{1,0:T(8,128)S(1)}, u32[]{:S(2)}, u32[]{:S(2)}) collective-permute-start(f32[32,2048]{1,0:T(8,128)S(1)} %get-tuple-element.55), channel_id=1, source_target_pairs={{3,2},{2,1},{1,0},{7,6},{6,5},{5,4},{11,10},{10,9},{9,8},{15,14},{... | collective-permute-start | bytes 786440 | tf_op jit(solution)/shard_map/ppermute | solution.py:183
  207.9 12.0 %collective-permute-start.27 = (f32[32,2048]{1,0:T(8,128)S(1)}, f32[32,2048]{1,0:T(8,128)S(1)}, u32[]{:S(2)}, u32[]{:S(2)}) collective-permute-start(f32[32,2048]{1,0:T(8,128)S(1)} %select_add_fusion.11), channel_id=1, source_target_pairs={{0,1},{1,2},{2,3},{4,5},{5,6},{6,7},{8,9},{9,10},{10,11},{12,13},{... | collective-permute-start | bytes 786440 | tf_op jit(solution)/shard_map/ppermute | solution.py:182
  (35 other events, 260.4 us)

commit v3 on v1

v3 whole, which is shorter than its diff:
```python
import functools

import jax
import jax.numpy as jnp
from jax import lax
from jax.experimental import pallas as pl
from jax.experimental.pallas import tpu as pltpu
from jax.sharding import PartitionSpec as P

TILE = 128
CHUNKS = 4
CORES = 2
GROUPS = ((0,), (1,), (2, 3))
UNITS = ((0, (0,)), (0, (1,)), (1, (0, 1)), (2, (0, 1)), (3, (0,)), (3, (1,)))
LATENCY = 0.5

SMEM = pl.BlockSpec(memory_space=pltpu.SMEM)
VMEM = pl.BlockSpec(memory_space=pltpu.VMEM)
ANY = pl.BlockSpec(memory_space=pl.ANY)


def after(value, *others):
    return lax.optimization_barrier((value, *others))[0]


def cut_kernel(count, bounds, place_ref, whole_ref, *outs):
    z = place_ref[2]
    depth = outs[0].shape[1]
    for g, (low, high) in enumerate(bounds):
        for m in range(count):
            start = pl.multiple_of((z ^ m) * depth, depth)
            outs[g * count + m][...] = whole_ref[low:high, pl.ds(start, depth)]


def cut(whole, count, depth, part, place):
    bounds = [(group[0] * part, (group[-1] + 1) * part) for group in GROUPS]
    shapes = [
        jax.ShapeDtypeStruct((high - low, depth), whole.dtype)
        for low, high in bounds
        for _ in range(count)
    ]
    outs = pl.pallas_call(
        functools.partial(cut_kernel, count, bounds),
        in_specs=[SMEM, VMEM],
        out_specs=[VMEM] * len(shapes),
        out_shape=shapes,
        cost_estimate=pl.CostEstimate(flops=0, bytes_accessed=4 * whole.size, transcendentals=0),
        name="cut",
    )(place, whole)
    return [outs[g * count : (g + 1) * count] for g in range(len(bounds))]


def pack_kernel(count, part, *refs):
    for c, out in enumerate(refs[count:]):
        for m in range(count):
            out[m * part : (m + 1) * part, :] = refs[m][c * part : (c + 1) * part, :]


def pack(blocks, part):
    count = len(blocks)
    rows, depth = blocks[0].shape
    shape = jax.ShapeDtypeStruct((count * part, depth), blocks[0].dtype)
    return pl.pallas_call(
        functools.partial(pack_kernel, count, part),
        in_specs=[VMEM] * count,
        out_specs=[VMEM] * (rows // part),
        out_shape=[shape] * (rows // part),
        cost_estimate=pl.CostEstimate(flops=0, bytes_accessed=rows * depth, transcendentals=0),
        name="pack",
    )(*blocks)


def split_kernel(step, whole_ref, high_ref, low_ref, buffer, sems):
    count = whole_ref.shape[0] // step

    def copy(i):
        return pltpu.make_async_copy(
            whole_ref.at[pl.ds(i * step, step)], buffer.at[i % 2], sems.at[i % 2]
        )

    copy(0).start()
    for i in range(count):
        if i + 1 < count:
            copy(i + 1).start()
        copy(i).wait()
        whole = buffer[i % 2]
        high = whole.astype(jnp.bfloat16)
        here = slice(i * step, (i + 1) * step)
        high_ref[here, :] = high
        low_ref[here, :] = (whole - high.astype(jnp.float32)).astype(jnp.bfloat16)


def split(whole):
    rows, columns = whole.shape
    step = min(256, rows)
    half = jax.ShapeDtypeStruct((rows, columns), jnp.bfloat16)
    return pl.pallas_call(
        functools.partial(split_kernel, step),
        in_specs=[ANY],
        out_specs=[VMEM, VMEM],
        out_shape=[half, half],
        scratch_shapes=[
            pltpu.VMEM((2, step, columns), jnp.float32),
            pltpu.SemaphoreType.DMA((2,)),
        ],
        cost_estimate=pl.CostEstimate(
            flops=rows * columns, bytes_accessed=4 * rows * columns, transcendentals=0
        ),
        compiler_params=pltpu.CompilerParams(vmem_limit_bytes=8 * 2**20),
        name="split",
    )(whole)


def product_kernel(count, rows, layout, halves, place_ref, pattern_ref, order_ref, *refs):
    lefts = refs[: len(layout)]
    factors = refs[len(layout) : len(layout) + 2 * halves]
    outs = refs[len(layout) + 2 * halves : -1]
    left = refs[-1]
    depth = lefts[0].shape[1]
    total = count * rows
    chip, core, z = place_ref[0], place_ref[1], place_ref[2]
    tiles = depth // TILE
    for held, pieces in zip(lefts, layout):
        start = 0
        for k, first, size in pieces:
            kind = order_ref[(chip ^ k) * CORES + core]
            high_rows = slice(k * rows + first, k * rows + first + size)
            low_rows = slice(total + k * rows + first, total + k * rows + first + size)
            for t in range(tiles):
                kept = pattern_ref[kind, z * tiles + t].astype(jnp.float32)
                here = slice(t * TILE, (t + 1) * TILE)
                value = held[start : start + size, here] * kept
                high = value.astype(jnp.bfloat16)
                left[high_rows, here] = high
                left[low_rows, here] = (value - high.astype(jnp.float32)).astype(jnp.bfloat16)
            start += size
    columns = factors[0].shape[1]
    width = min(512, columns)
    for half in range(halves):
        high_ref, low_ref = factors[2 * half : 2 * half + 2]
        for j in range(columns // width):
            here = slice(j * width, (j + 1) * width)
            both = jnp.dot(left[...], high_ref[:, here], preferred_element_type=jnp.float32)
            small = jnp.dot(
                left[:total, :], low_ref[:, here], preferred_element_type=jnp.float32
            )
            result = both[:total] + (both[total:] + small)
            there = slice(half * columns + j * width, half * columns + (j + 1) * width)
            for k in range(count):
                outs[k][:, there] = result[k * rows : (k + 1) * rows]


def product(lefts, layout, factors, place, pattern, block_order):
    rows, depth = lefts[0].shape
    count = sum(held.shape[0] for held in lefts) // rows
    halves = len(factors)
    columns = factors[0][0].shape[1]
    total = count * rows
    return pl.pallas_call(
        functools.partial(product_kernel, count, rows, layout, halves),
        in_specs=[SMEM] * 3 + [VMEM] * (len(lefts) + 2 * halves),
        out_specs=[VMEM] * count,
        out_shape=[jax.ShapeDtypeStruct((rows, halves * columns), jnp.float32)] * count,
        scratch_shapes=[pltpu.VMEM((2 * total, depth), jnp.bfloat16)],
        cost_estimate=pl.CostEstimate(
            flops=6 * total * depth * halves * columns,
            bytes_accessed=8 * total * depth,
            transcendentals=0,
        ),
        compiler_params=pltpu.CompilerParams(vmem_limit_bytes=16 * 2**20),
        name="product",
    )(place, pattern, block_order, *lefts, *[part for pair in factors for part in pair])


def finish_kernel(spec, group, count, part, width, place_ref, bare_ref, occ_ref, virt_ref, *refs):
    out_ref = refs[-1]
    chip, core, z = place_ref[0], place_ref[1], place_ref[2]
    rows_local = CHUNKS * part
    for number, (chunk, halves, s) in enumerate(spec):
        kept, arrived = refs[2 * number], refs[2 * number + 1]
        for position, half in enumerate(halves):
            column = (((chip % group) ^ s) * CORES + (half ^ core)) * width
            columns = pl.ds(pl.multiple_of(column, width), width)
            here = slice(position * width, (position + 1) * width)
            for m in range(count):
                rows = pl.ds(pl.multiple_of((z ^ m) * rows_local + chunk * part, part), part)
                block = slice(m * part, (m + 1) * part)
                ladder = kept[block, here] + arrived[block, here]
                gap = occ_ref[rows, :] + virt_ref[:, columns]
                out_ref[rows, columns] = -(bare_ref[rows, columns] + ladder) / gap


def finish(spec, pairs, group, count, part, width, place, bare, occ, virt):
    return pl.pallas_call(
        functools.partial(finish_kernel, spec, group, count, part, width),
        in_specs=[SMEM] + [VMEM] * (3 + 2 * len(pairs)),
        out_specs=VMEM,
        out_shape=jax.ShapeDtypeStruct(bare.shape, bare.dtype),
        cost_estimate=pl.CostEstimate(
            flops=5 * bare.size, bytes_accessed=8 * bare.size, transcendentals=0
        ),
        compiler_params=pltpu.CompilerParams(vmem_limit_bytes=8 * 2**20),
        name="finish",
    )(place, bare, occ[:, None], virt[None, :], *[part_in for pair in pairs for part_in in pair])


def event_order(events):
    free = {}
    done = {}
    order = []
    waiting = dict(events)
    while waiting:
        best = None
        for rank, (name, (needs, uses, length)) in enumerate(waiting.items()):
            if any(need not in done for need in needs):
                continue
            start = max([done[need] for need in needs] + [free.get(r, 0.0) for r, _ in uses] + [0.0])
            if best is None or start < best[0] - 1e-9:
                best = (start, name)
        start, name = best
        needs, uses, length = waiting.pop(name)
        for resource, busy in uses:
            free[resource] = start + busy
        done[name] = start + length
        order.append(name)
    return order


def shards(amplitudes, integrals, bare_terms, pattern, block_order, occ_gap, virt_gap):
    rows_local, columns = amplitudes.shape
    depth, columns_local = integrals.shape
    wide_count = lax.axis_size("wide")
    narrow_count = lax.axis_size("narrow")
    chips = wide_count // CORES
    wide = lax.axis_index("wide")
    z = lax.axis_index("narrow")
    chip = wide // CORES
    core = wide % CORES
    part = rows_local // CHUNKS
    rows = narrow_count * part
    group = chips // narrow_count
    place = jnp.stack([chip, core, z]).astype(jnp.int32)
    chip_bits = [1 << b for b in range(chips.bit_length() - 1)]
    narrow_bits = [1 << b for b in range(narrow_count.bit_length() - 1)]
    lane = {bit: "x" if n < len(chip_bits) // 2 else "y" for n, bit in enumerate(chip_bits)}

    def across(value, mask):
        return lax.ppermute(value, "wide", [(w, w ^ mask) for w in range(wide_count)])

    def across_chips(value, mask):
        return across(value, mask * CORES)

    def along(value, mask):
        return lax.ppermute(value, "narrow", [(n, n ^ mask) for n in range(narrow_count)])

    last = []

    def ordered(value):
        if last:
            value = after(value, last[-1])
        last.append(value)
        return value

    swapped = across(integrals, 1)
    pieces = cut(amplitudes, narrow_count, depth, part, place)
    spread = {}
    mine = {}
    held = {}
    layouts = {}
    factors = {}
    state = {}

    def spread_step(g):
        blocks = [pieces[g][0]]
        for mask in range(1, narrow_count):
            blocks.append(along(ordered(pieces[g][mask]), mask))
        spread[g] = blocks

    def gather_step(chunk, number):
        g = [n for n, group_of in enumerate(GROUPS) if chunk in group_of][0]
        if number == 0:
            if GROUPS[g][0] == chunk:
                for c, packed in zip(GROUPS[g], pack(spread[g], part)):
                    mine[c] = packed
            held[chunk] = [mine[chunk]]
            layouts[chunk] = [[(0, 0, rows)]]
        direct = chunk == 0 and chips == 4
        if direct and number == 0:
            send = ordered(mine[chunk])
            held[chunk] += [across_chips(send, 1), across_chips(send, 2)]
            layouts[chunk] += [[(1, 0, rows)], [(2, 0, rows)]]
        elif direct:
            near, far = held[chunk][1], held[chunk][2]
            first = across_chips(ordered(near[: rows // 2]), 2)
            second = across_chips(ordered(far[rows // 2 :]), 1)
            held[chunk] += [first, second]
            layouts[chunk] += [[(3, 0, rows // 2)], [(3, rows // 2, rows // 2)]]
        else:
            bit = chip_bits[number]
            send = ordered(jnp.concatenate(held[chunk], axis=0))
            held[chunk].append(across_chips(send, bit))
            layouts[chunk].append([(k | bit, 0, rows) for k in range(bit)])

    def split_step(half):
        factors[half] = split(ordered(integrals if half == 0 else swapped))

    def multiply(unit):
        chunk, halves = UNITS[unit]
        lefts = list(held[chunk])
        lefts[0] = ordered(lefts[0])
        partials = product(
            lefts, layouts[chunk], [factors[half] for half in halves], place, pattern, block_order
        )
        state[unit] = {(k, 0): block for k, block in enumerate(partials)}

    def exchange_step(unit, bit):
        now = state[unit]
        keys = [key for key in now if key[0] & bit]
        send = ordered(jnp.concatenate([now[key] for key in keys], axis=0))
        arrived = across_chips(send, bit)
        state[unit] = {key: now[key] for key in now if not key[0] & bit}
        for n, (r, s) in enumerate(keys):
            state[unit][r ^ bit, s | bit] = arrived[n * rows : (n + 1) * rows]

    def reduce_step(unit, bit, narrow_bit):
        now = state[unit]
        same = ((chip // bit) & 1) == ((z // narrow_bit) & 1)
        keys = [key for key in now if not key[1] & bit]
        pairs = [(now[r, s], now[r, s | bit]) for r, s in keys]
        leaving = jnp.concatenate([jnp.where(same, b, a) for a, b in pairs], axis=0)
        width = leaving.shape[1]
        leaving = leaving.reshape(-1, 2, narrow_bit * part, width)[:, ::-1].reshape(-1, width)
        arrived = along(ordered(leaving), narrow_bit)
        state[unit] = {}
        for n, (key, (a, b)) in enumerate(zip(keys, pairs)):
            kept = jnp.where(same, a, b)
            came = arrived[n * rows : (n + 1) * rows]
            state[unit][key] = (kept, came) if narrow_bit == narrow_bits[-1] else kept + came

    events = {}
    actions = {}

    def event(name, action, needs, uses):
        length = max(busy for _, busy in uses)
        on_core = all(resource == "core" for resource, _ in uses)
        events[name] = (needs, uses, length if on_core else length + LATENCY)
        actions[name] = action

    for g, chunks in enumerate(GROUPS):
        event(
            ("spread", g),
            functools.partial(spread_step, g),
            [],
            [("mid", 1.0 * len(chunks)), ("end", 0.75 * len(chunks)), ("core", 0.7)],
        )
    for half in range(2):
        needs = [("gather", 0, 0)] if half == 0 else [("multiply", 0)]
        event(("split", half), functools.partial(split_step, half), needs, [("core", 0.8)])
    for unit, (chunk, halves) in enumerate(UNITS):
        if unit == 0 or UNITS[unit - 1][0] != chunk:
            for number, bit in enumerate(chip_bits):
                g = [n for n, group_of in enumerate(GROUPS) if chunk in group_of][0]
                needs = [("gather", chunk, number - 1)] if number else [("spread", g)]
                uses = [(lane[bit], 1.0 * bit)]
                if chunk == 0 and chips == 4:
                    uses = [("x", 1.0 / bit), ("y", 1.0 / bit)]
                event(
                    ("gather", chunk, number),
                    functools.partial(gather_step, chunk, number),
                    needs,
                    uses,
                )
        share = len(halves) / CORES
        before = ("multiply", unit)
        needs = [("gather", chunk, len(chip_bits) - 1)] + [("split", half) for half in halves]
        event(before, functools.partial(multiply, unit), needs, [("core", 0.8 * share)])
        length = 2.0 * share
        for bit in chip_bits:
            if bit < group:
                now = ("exchange", unit, bit)
                event(
                    now, functools.partial(exchange_step, unit, bit), [before], [(lane[bit], length)]
                )
                before = now
        for narrow_bit in narrow_bits:
            bit = group * narrow_bit
            now = ("exchange", unit, bit)
            event(
                now, functools.partial(exchange_step, unit, bit), [before], [(lane[bit], length)]
            )
            before = now
            now = ("reduce", unit, narrow_bit)
            uses = [("end", length), ("mid", length * (0 if narrow_bit == 1 else narrow_bit))]
            event(now, functools.partial(reduce_step, unit, bit, narrow_bit), [before], uses)
            before = now
            length /= 2.0

    for name in event_order(events):
        actions[name]()

    spec = [(*UNITS[unit], s) for unit in range(len(UNITS)) for s in range(group)]
    pairs = [state[unit][0, s] for unit in range(len(UNITS)) for s in range(group)]
    return finish(
        spec,
        pairs,
        group,
        narrow_count,
        part,
        columns_local,
        place,
        bare_terms,
        occ_gap,
        virt_gap,
    )


def solution(mesh):
    placed = (
        P(("wide", "narrow"), None),
        P("narrow", "wide"),
        P("wide", "narrow"),
        P(),
        P(),
        P("wide"),
        P("narrow"),
    )
    return jax.shard_map(
        shards, mesh=mesh, in_specs=placed, out_specs=P("wide", "narrow"), check_vma=False
    )
```

time: 286 us -> 203 us (0.71)
  blocking collectives: 128 us -> 0 us
  waiting for transfers between devices: 101 us -> 49.6 us
  starting transfers between devices: 0.3 us -> 50.4 us
  Pallas kernels: 0 us -> 35.1 us
  local copies, waits for them, and re-layouts: 8.24 us -> 41.3 us
  matrix products: 28.7 us -> 0 us
  other arithmetic: 3.52 us -> 25.2 us
  between operations: 15.6 us -> 0.56 us
    all_to_all x8 -> x0, blocking collectives: 128 us -> none  [the longest x4 79.8 us: shards(): lax.all_to_all(stacked, 'wide', split_axis=0, concat_axis=1, tiled=True)]
    reduce_scatter x4 -> x0, waiting for transfers between devices: 87.6 us -> none  [shards(): lax.psum_scatter(partial_value, 'narrow', scatter_dimension=1, tiled=True)]
    ppermute x0 -> x44, starting transfers between devices: none -> 50.4 us  [the longest x21 29 us: along(): lax.ppermute(value, 'narrow', [(n, n ^ mask) for n in range(narrow_count)])]
    ppermute x0 -> x44, waiting for transfers between devices: none -> 49.6 us  [the longest x21 31.4 us: along(): lax.ppermute(value, 'narrow', [(n, n ^ mask) for n in range(narrow_count)])]
    pallas_call x0 -> x13, Pallas kernels: none -> 35.1 us  [the longest x6 18.1 us: product(): pl.pallas_call(functools.partial(product_kernel, count, rows, layout, hal...]
    unnamed x7 -> x102, local copies, waits for them, and re-layouts: 1.5 us -> 31 us
    dot_general x4 -> x0, matrix products: 28.7 us -> none  [shards(): jnp.dot(lax.all_gather(transposed, 'wide', axis=0, tiled=True), integrals...]
    all_gather x4 -> x0, waiting for transfers between devices: 13.1 us -> none  [shards(): lax.all_gather(transposed, 'wide', axis=0, tiled=True)]
  transfers between devices with their start and end apart: 8 -> 44, of which waited for: 6 -> 18; matrix products, arithmetic and copies ran while one was open for 12% -> 18% of each run, Pallas kernels for 0% -> 16%
where the time goes in v3:
time: 203 us; the launch traced here: 202 us
  starting transfers between devices  50.4 us (25%)
  waiting for transfers between devices  49.6 us (24%)
  local copies, waits for them, and re-layouts  41.3 us (20%)
  Pallas kernels  35.1 us (17%)
  other arithmetic  25.2 us (12%)
    ppermute x21, waiting for transfers between devices, along(): lax.ppermute(value, 'narrow', [(n, n ^ mask) for n in range(narrow_count)])  31.4 us
    unnamed x102, local copies, waits for them, and re-layouts  31 us
    ppermute x21, starting transfers between devices, along(): lax.ppermute(value, 'narrow', [(n, n ^ mask) for n in range(narrow_count)])  29 us
    ppermute x23, starting transfers between devices, across(): lax.ppermute(value, 'wide', [(w, w ^ mask) for w in range(wide_count)])  21.4 us
    ppermute x23, waiting for transfers between devices, across(): lax.ppermute(value, 'wide', [(w, w ^ mask) for w in range(wide_count)])  18.2 us
    pallas_call x6, Pallas kernels, product(): pl.pallas_call(functools.partial(product_kernel, count, rows, layout, hal...  18.1 us
    select_n x11, other arithmetic, reduce_step(): leaving = jnp.concatenate([jnp.where(same, b, a) for a, b in pairs], axis=0)  11 us
    rev x12, local copies, waits for them, and re-layouts, reduce_step(): leaving.reshape(-1, 2, narrow_bit * part, width)[:, ::-1].reshape(-1, width)  9.53 us
  transfers between devices with their start and end apart: 44, of which 18 were waited for; matrix products, arithmetic and copies ran while one was open for 18% of the time, Pallas kernels for 16%

profile of v3, /device:TPU:0, one launch (start us, length us, event | category | flops | bytes accessed | tf_op | source)
XLA Modules:
  0.0 202.1 jit_solution(15305296076719760890)
XLA Ops:
  1.1 2.2 %cut.1 = (f32[8,2048]{1,0:T(8,128)}, f32[8,2048]{1,0:T(8,128)}, f32[8,2048]{1,0:T(8,128)}, f32[8,2048]{1,0:T(8,128)}, f32[8,2048]{1,0:T(8,128)}, /*index=5*/f32[...) custom-call(s32[3]{0:T(128)} %pad_add_fusion.place_ref, ...), custom_call_target="tpu_custom_call" | custom-call | bytes 1048576 | tf_op jit(solution)/shard_map/cut/pallas_call | solution.py:42
  3.3 2.6 %collective-permute-start = (f32[8,2048]{1,0:T(8,128)}, f32[8,2048]{1,0:T(8,128)S(1)}, u32[]{:S(2)}, u32[]{:S(2)}) collective-permute-start(f32[8,2048]{1,0:T(8,128)} %get-tuple-element.97), channel_id=1, source_target_pairs={{0,1},{1,0},{2,3},{3,2},{4,5},{5,4},{6,7},{7,6},{8,9},{9,8},{10,11... | collective-permute-start | bytes 196616 | tf_op jit(solution)/shard_map/ppermute | solution.py:254
  5.9 2.6 %collective-permute-start.1 = (f32[8,2048]{1,0:T(8,128)}, f32[8,2048]{1,0:T(8,128)S(1)}, u32[]{:S(2)}, u32[]{:S(2)}) collective-permute-start(f32[8,2048]{1,0:T(8,128)} %get-tuple-element.99), channel_id=1, source_target_pairs={{0,2},{1,3},{2,0},{3,1},{4,6},{5,7},{6,4},{7,5},{8,10},{9,11},{10,... | collective-permute-start | bytes 196616 | tf_op jit(solution)/shard_map/ppermute | solution.py:254
  8.8 4.2 %collective-permute-done.1.refs_2_ = f32[8,2048]{1,0:T(8,128)S(1)} collective-permute-done((f32[8,2048]{1,0:T(8,128)}, f32[8,2048]{1,0:T(8,128)S(1)}, u32[]{:S(2)}, u32[]{:S(2)}) %collective-permute-start.1) | collective-permute-done | bytes 65568 | tf_op jit(solution)/shard_map/ppermute | solution.py:254
  19.1 2.2 %collective-permute-start.4 = (f32[8,2048]{1,0:T(8,128)}, f32[8,2048]{1,0:T(8,128)S(1)}, u32[]{:S(2)}, u32[]{:S(2)}) collective-permute-start(f32[8,2048]{1,0:T(8,128)} %get-tuple-element.106), channel_id=1, source_target_pairs={{0,2},{1,3},{2,0},{3,1},{4,6},{5,7},{6,4},{7,5},{8,10},{9,11},{10,... | collective-permute-start | bytes 196616 | tf_op jit(solution)/shard_map/ppermute | solution.py:254
  24.4 2.4 %collective-permute-start.13 = (f32[16,2048]{1,0:T(8,128)}, f32[16,2048]{1,0:T(8,128)S(1)}, u32[]{:S(2)}, u32[]{:S(2)}) collective-permute-start(f32[16,2048]{1,0:T(8,128)} %get-tuple-element.114), channel_id=1, source_target_pairs={{0,2},{1,3},{2,0},{3,1},{4,6},{5,7},{6,4},{7,5},{8,10},{9,11},{10,... | collective-permute-start | bytes 393224 | tf_op jit(solution)/shard_map/ppermute | solution.py:254
  33.2 2.5 %collective-permute-start.14 = (f32[16,2048]{1,0:T(8,128)}, f32[16,2048]{1,0:T(8,128)S(1)}, u32[]{:S(2)}, u32[]{:S(2)}) collective-permute-start(f32[16,2048]{1,0:T(8,128)} %get-tuple-element.115), channel_id=1, source_target_pairs={{0,3},{1,2},{2,1},{3,0},{4,7},{5,6},{6,5},{7,4},{8,11},{9,10},{10,... | collective-permute-start | bytes 393224 | tf_op jit(solution)/shard_map/ppermute | solution.py:254
  36.5 3.4 %copy-done.16 = f32[2048,1024]{1,0:T(8,128)S(1)} copy-done((f32[2048,1024]{1,0:T(8,128)S(1)}, f32[2048,1024]{1,0:T(8,128)}, u32[]{:S(2)}) %copy-start.16) | copy-done | bytes 8388632
  56.5 2.2 %copy-done.1 = bf16[2048,1024]{1,0:T(8,128)(2,1)S(1)} copy-done((bf16[2048,1024]{1,0:T(8,128)(2,1)S(1)}, bf16[2048,1024]{1,0:T(8,128)(2,1)}, u32[]{:S(2)}) %copy-start.1) | copy-done | bytes 4194328
  58.7 2.2 %copy-done.6 = bf16[2048,1024]{1,0:T(8,128)(2,1)S(1)} copy-done((bf16[2048,1024]{1,0:T(8,128)(2,1)S(1)}, bf16[2048,1024]{1,0:T(8,128)(2,1)}, u32[]{:S(2)}) %copy-start.6) | copy-done | bytes 4194328
  60.9 2.4 %product.6 = (f32[32,1024]{1,0:T(8,128)S(1)}, f32[32,1024]{1,0:T(8,128)S(1)}, f32[32,1024]{1,0:T(8,128)S(1)}, f32[32,1024]{1,0:T(8,128)S(1)}) custom-call(s32[3]{0:T(128)S(1)} %copy-done.23, s32[8,64]{1,0:T(8,128)S(1)} %copy-done.22, s32[8]{0:T(128)S(1)} %copy-done.24, f32[32,2048]{1,0:T(8,128)S(1)} %copy-done.18, ...), custom_call_target="tpu_custom_call" | custom-call | flops 1610612736 | bytes 2097152 | tf_op jit(solution)/shard_map/product/pallas_call | solution.py:159
  65.8 5.8 %split.3 = (bf16[2048,1024]{1,0:T(8,128)(2,1)S(1)}, bf16[2048,1024]{1,0:T(8,128)(2,1)S(1)}) custom-call(f32[2048,1024]{1,0:T(8,128)} %collective-permute-done.11.whole_ref), custom_call_target="tpu_custom_call" | custom-call | flops 2097152 | bytes 8388608 | tf_op jit(solution)/shard_map/split/pallas_call | solution.py:97
  71.7 2.4 %product.7 = (f32[32,1024]{1,0:T(8,128)S(1)}, f32[32,1024]{1,0:T(8,128)S(1)}, f32[32,1024]{1,0:T(8,128)S(1)}, f32[32,1024]{1,0:T(8,128)S(1)}) custom-call(s32[3]{0:T(128)S(1)} %copy-done.23, s32[8,64]{1,0:T(8,128)S(1)} %copy-done.22, s32[8]{0:T(128)S(1)} %copy-done.24, f32[32,2048]{1,0:T(8,128)S(1)} %copy-done.18, ...), custom_call_target="tpu_custom_call" | custom-call | flops 1610612736 | bytes 2097152 | tf_op jit(solution)/shard_map/product/pallas_call | solution.py:159
  78.1 4.0 %product.8 = (f32[32,2048]{1,0:T(8,128)S(1)}, f32[32,2048]{1,0:T(8,128)S(1)}, f32[32,2048]{1,0:T(8,128)S(1)}, f32[32,2048]{1,0:T(8,128)S(1)}) custom-call(s32[3]{0:T(128)S(1)} %copy-done.23, s32[8,64]{1,0:T(8,128)S(1)} %copy-done.22, s32[8]{0:T(128)S(1)} %copy-done.24, f32[32,2048]{1,0:T(8,128)S(1)} %copy-done.17, ...), custom_call_target="tpu_custom_call" | custom-call | flops 3221225472 | bytes 2097152 | tf_op jit(solution)/shard_map/product/pallas_call | solution.py:159
  87.6 3.4 %collective-permute-done.17 = f32[64,1024]{1,0:T(8,128)S(1)} collective-permute-done((f32[64,1024]{1,0:T(8,128)}, f32[64,1024]{1,0:T(8,128)S(1)}, u32[]{:S(2)}, u32[]{:S(2)}) %collective-permute-start.17) | collective-permute-done | bytes 262176 | tf_op jit(solution)/shard_map/ppermute | solution.py:254
  92.3 2.2 %copy-done.3 = bf16[2048,1024]{1,0:T(8,128)(2,1)S(1)} copy-done((bf16[2048,1024]{1,0:T(8,128)(2,1)S(1)}, bf16[2048,1024]{1,0:T(8,128)(2,1)}, u32[]{:S(2)}) %copy-start.3) | copy-done | bytes 4194328
  94.5 2.2 %copy-done.8 = bf16[2048,1024]{1,0:T(8,128)(2,1)S(1)} copy-done((bf16[2048,1024]{1,0:T(8,128)(2,1)S(1)}, bf16[2048,1024]{1,0:T(8,128)(2,1)}, u32[]{:S(2)}) %copy-start.8) | copy-done | bytes 4194328
  96.7 2.2 %copy-done.11 = bf16[2048,1024]{1,0:T(8,128)(2,1)S(1)} copy-done((bf16[2048,1024]{1,0:T(8,128)(2,1)S(1)}, bf16[2048,1024]{1,0:T(8,128)(2,1)}, u32[]{:S(2)}) %copy-start.11) | copy-done | bytes 4194328
  98.9 2.2 %copy-done.14 = bf16[2048,1024]{1,0:T(8,128)(2,1)S(1)} copy-done((bf16[2048,1024]{1,0:T(8,128)(2,1)S(1)}, bf16[2048,1024]{1,0:T(8,128)(2,1)}, u32[]{:S(2)}) %copy-start.14) | copy-done | bytes 4194328
  101.1 4.3 %product.9 = (f32[32,2048]{1,0:T(8,128)S(1)}, f32[32,2048]{1,0:T(8,128)S(1)}, f32[32,2048]{1,0:T(8,128)S(1)}, f32[32,2048]{1,0:T(8,128)S(1)}) custom-call(s32[3]{0:T(128)S(1)} %copy-done.23, s32[8,64]{1,0:T(8,128)S(1)} %copy-done.22, s32[8]{0:T(128)S(1)} %copy-done.24, f32[32,2048]{1,0:T(8,128)S(1)} %copy-done.20, ...), custom_call_target="tpu_custom_call" | custom-call | flops 3221225472 | bytes 2097152 | tf_op jit(solution)/shard_map/product/pallas_call | solution.py:159
  119.7 3.7 %collective-permute-done.29.refs_1_ = f32[32,2048]{1,0:T(8,128)S(1)} collective-permute-done((f32[32,2048]{1,0:T(8,128)S(1)}, f32[32,2048]{1,0:T(8,128)S(1)}, u32[]{:S(2)}, u32[]{:S(2)}) %collective-permute-start.29) | collective-permute-done | bytes 262176 | tf_op jit(solution)/shard_map/ppermute | solution.py:248
  128.1 6.5 %collective-permute-done.27 = f32[64,2048]{1,0:T(8,128)} collective-permute-done((f32[64,2048]{1,0:T(8,128)}, f32[64,2048]{1,0:T(8,128)}, u32[]{:S(2)}, u32[]{:S(2)}) %collective-permute-start.27) | collective-permute-done | bytes 524320 | tf_op jit(solution)/shard_map/ppermute | solution.py:254
  136.8 2.2 %copy-done.4 = bf16[2048,1024]{1,0:T(8,128)(2,1)S(1)} copy-done((bf16[2048,1024]{1,0:T(8,128)(2,1)S(1)}, bf16[2048,1024]{1,0:T(8,128)(2,1)}, u32[]{:S(2)}) %copy-start.4) | copy-done | bytes 4194328
  139.0 2.2 %copy-done.9 = bf16[2048,1024]{1,0:T(8,128)(2,1)S(1)} copy-done((bf16[2048,1024]{1,0:T(8,128)(2,1)S(1)}, bf16[2048,1024]{1,0:T(8,128)(2,1)}, u32[]{:S(2)}) %copy-start.9) | copy-done | bytes 4194328
  141.2 2.4 %product.10 = (f32[32,1024]{1,0:T(8,128)S(1)}, f32[32,1024]{1,0:T(8,128)S(1)}, f32[32,1024]{1,0:T(8,128)S(1)}, f32[32,1024]{1,0:T(8,128)S(1)}) custom-call(s32[3]{0:T(128)S(1)} %copy-done.23, s32[8,64]{1,0:T(8,128)S(1)} %copy-done.22, s32[8]{0:T(128)S(1)} %copy-done.24, f32[32,2048]{1,0:T(8,128)S(1)} %copy-done.19, ...), custom_call_target="tpu_custom_call" | custom-call | flops 1610612736 | bytes 2097152 | tf_op jit(solution)/shard_map/product/pallas_call | solution.py:159
  147.4 2.4 %product.11 = (f32[32,1024]{1,0:T(8,128)S(1)}, f32[32,1024]{1,0:T(8,128)S(1)}, f32[32,1024]{1,0:T(8,128)S(1)}, f32[32,1024]{1,0:T(8,128)S(1)}) custom-call(s32[3]{0:T(128)S(1)} %copy-done.23, s32[8,64]{1,0:T(8,128)S(1)} %copy-done.22, s32[8]{0:T(128)S(1)} %copy-done.24, f32[32,2048]{1,0:T(8,128)S(1)} %copy-done.19, ...), custom_call_target="tpu_custom_call" | custom-call | flops 1610612736 | bytes 2097152 | tf_op jit(solution)/shard_map/product/pallas_call | solution.py:159
  158.3 2.4 %collective-permute-done.34 = f32[32,2048]{1,0:T(8,128)} collective-permute-done((f32[32,2048]{1,0:T(8,128)}, f32[32,2048]{1,0:T(8,128)}, u32[]{:S(2)}, u32[]{:S(2)}) %collective-permute-start.34) | collective-permute-done | bytes 262176 | tf_op jit(solution)/shard_map/ppermute | solution.py:248
  168.1 5.7 %collective-permute-done.37 = f32[64,1024]{1,0:T(8,128)} collective-permute-done((f32[64,1024]{1,0:T(8,128)}, f32[64,1024]{1,0:T(8,128)}, u32[]{:S(2)}, u32[]{:S(2)}) %collective-permute-start.37) | collective-permute-done | bytes 262176 | tf_op jit(solution)/shard_map/ppermute | solution.py:254
  178.8 2.9 %collective-permute-done.39 = f32[32,1024]{1,0:T(8,128)S(1)} collective-permute-done((f32[32,1024]{1,0:T(8,128)S(1)}, f32[32,1024]{1,0:T(8,128)S(1)}, u32[]{:S(2)}, u32[]{:S(2)}) %collective-permute-start.39) | collective-permute-done | bytes 131104 | tf_op jit(solution)/shard_map/ppermute | solution.py:248
  185.4 4.7 %collective-permute-done.42 = f32[32,1024]{1,0:T(8,128)S(1)} collective-permute-done((f32[32,1024]{1,0:T(8,128)}, f32[32,1024]{1,0:T(8,128)S(1)}, u32[]{:S(2)}, u32[]{:S(2)}) %collective-permute-start.42) | collective-permute-done | bytes 131104 | tf_op jit(solution)/shard_map/ppermute | solution.py:248
  194.7 2.6 %collective-permute-done.40.refs_9_ = f32[32,1024]{1,0:T(8,128)S(1)} collective-permute-done((f32[32,1024]{1,0:T(8,128)}, f32[32,1024]{1,0:T(8,128)S(1)}, u32[]{:S(2)}, u32[]{:S(2)}) %collective-permute-start.40) | collective-permute-done | bytes 131104 | tf_op jit(solution)/shard_map/ppermute | solution.py:254
  197.4 2.9 %collective-permute-done.43.refs_11_ = f32[32,1024]{1,0:T(8,128)S(1)} collective-permute-done((f32[32,1024]{1,0:T(8,128)}, f32[32,1024]{1,0:T(8,128)S(1)}, u32[]{:S(2)}, u32[]{:S(2)}) %collective-permute-start.43) | collective-permute-done | bytes 131104 | tf_op jit(solution)/shard_map/ppermute | solution.py:254
  (225 shorter events, 103.2 us)
Async XLA Ops:
  0.0 64.2 %collective-permute-start.11 = (f32[2048,1024]{1,0:T(8,128)}, f32[2048,1024]{1,0:T(8,128)}, u32[]{:S(2)}, u32[]{:S(2)}) collective-permute-start(f32[2048,1024]{1,0:T(8,128)} %whole_ref.2), channel_id=1, source_target_pairs={{0,4},{4,0},{8,12},{12,8},{16,20},{20,16},{24,28},{28,24},{1,5},{5... | collective-permute-start | bytes 25165832 | tf_op jit(solution)/shard_map/ppermute | solution.py:248
  17.1 14.4 %collective-permute-start.12 = (f32[16,2048]{1,0:T(8,128)}, f32[16,2048]{1,0:T(8,128)S(1)}, u32[]{:S(2)}, u32[]{:S(2)}) collective-permute-start(f32[16,2048]{1,0:T(8,128)} %get-tuple-element.113), channel_id=1, source_target_pairs={{0,1},{1,0},{2,3},{3,2},{4,5},{5,4},{6,7},{7,6},{8,9},{9,8},{10,11... | collective-permute-start | bytes 393224 | tf_op jit(solution)/shard_map/ppermute | solution.py:254
  19.1 7.7 %collective-permute-start.4 = (f32[8,2048]{1,0:T(8,128)}, f32[8,2048]{1,0:T(8,128)S(1)}, u32[]{:S(2)}, u32[]{:S(2)}) collective-permute-start(f32[8,2048]{1,0:T(8,128)} %get-tuple-element.106), channel_id=1, source_target_pairs={{0,2},{1,3},{2,0},{3,1},{4,6},{5,7},{6,4},{7,5},{8,10},{9,11},{10,... | collective-permute-start | bytes 196616 | tf_op jit(solution)/shard_map/ppermute | solution.py:254
  24.4 8.9 %collective-permute-start.13 = (f32[16,2048]{1,0:T(8,128)}, f32[16,2048]{1,0:T(8,128)S(1)}, u32[]{:S(2)}, u32[]{:S(2)}) collective-permute-start(f32[16,2048]{1,0:T(8,128)} %get-tuple-element.114), channel_id=1, source_target_pairs={{0,2},{1,3},{2,0},{3,1},{4,6},{5,7},{6,4},{7,5},{8,10},{9,11},{10,... | collective-permute-start | bytes 393224 | tf_op jit(solution)/shard_map/ppermute | solution.py:254
  26.8 21.7 %collective-permute-start.8 = (f32[32,2048]{1,0:T(8,128)}, f32[32,2048]{1,0:T(8,128)S(1)}, u32[]{:S(2)}, u32[]{:S(2)}) collective-permute-start(f32[32,2048]{1,0:T(8,128)} %pack.3.refs_0_), channel_id=1, source_target_pairs={{0,8},{4,12},{8,0},{12,4},{16,24},{20,28},{24,16},{28,20},{1,9},{5... | collective-permute-start | bytes 786440 | tf_op jit(solution)/shard_map/ppermute | solution.py:248
  28.3 21.8 %collective-permute-start.7 = (f32[32,2048]{1,0:T(8,128)}, f32[32,2048]{1,0:T(8,128)S(1)}, u32[]{:S(2)}, u32[]{:S(2)}) collective-permute-start(f32[32,2048]{1,0:T(8,128)} %pack.3.refs_0_), channel_id=1, source_target_pairs={{0,16},{4,20},{8,24},{12,28},{16,0},{20,4},{24,8},{28,12},{1,17},{... | collective-permute-start | bytes 786440 | tf_op jit(solution)/shard_map/ppermute | solution.py:248
  31.5 20.2 %collective-permute-start.6 = (f32[32,2048]{1,0:T(8,128)}, f32[32,2048]{1,0:T(8,128)S(1)}, u32[]{:S(2)}, u32[]{:S(2)}) collective-permute-start(f32[32,2048]{1,0:T(8,128)} %pack.4.refs_0_), channel_id=1, source_target_pairs={{0,8},{4,12},{8,0},{12,4},{16,24},{20,28},{24,16},{28,20},{1,9},{5... | collective-permute-start | bytes 786440 | tf_op jit(solution)/shard_map/ppermute | solution.py:248
  33.2 12.7 %collective-permute-start.14 = (f32[16,2048]{1,0:T(8,128)}, f32[16,2048]{1,0:T(8,128)S(1)}, u32[]{:S(2)}, u32[]{:S(2)}) collective-permute-start(f32[16,2048]{1,0:T(8,128)} %get-tuple-element.115), channel_id=1, source_target_pairs={{0,3},{1,2},{2,1},{3,0},{4,7},{5,6},{6,5},{7,4},{8,11},{9,10},{10,... | collective-permute-start | bytes 393224 | tf_op jit(solution)/shard_map/ppermute | solution.py:254
  51.7 23.1 %collective-permute-start.19 = (f32[64,2048]{1,0:T(8,128)S(1)}, f32[64,2048]{1,0:T(8,128)S(1)}, u32[]{:S(2)}, u32[]{:S(2)}) collective-permute-start(f32[64,2048]{1,0:T(8,128)S(1)} %pad_maximum_fusion), channel_id=1, source_target_pairs={{0,16},{4,20},{8,24},{12,28},{16,0},{20,4},{24,8},{28,12},{1,17},{... | collective-permute-start | bytes 1572872 | tf_op jit(solution)/shard_map/ppermute | solution.py:248
  52.3 11.0 %collective-permute-start.16 = (f32[32,2048]{1,0:T(8,128)}, f32[32,2048]{1,0:T(8,128)S(1)}, u32[]{:S(2)}, u32[]{:S(2)}) collective-permute-start(f32[32,2048]{1,0:T(8,128)} %get-tuple-element.149.refs_0_), channel_id=1, source_target_pairs={{0,8},{4,12},{8,0},{12,4},{16,24},{20,28},{24,16},{28,20},{1,9},{5... | collective-permute-start | bytes 786440 | tf_op jit(solution)/shard_map/ppermute | solution.py:248
  64.2 17.9 %collective-permute-start.15 = (f32[64,1024]{1,0:T(8,128)S(1)}, f32[64,1024]{1,0:T(8,128)S(1)}, u32[]{:S(2)}, u32[]{:S(2)}) collective-permute-start(f32[64,1024]{1,0:T(8,128)S(1)} %pad_maximum_fusion.7), channel_id=1, source_target_pairs={{0,8},{4,12},{8,0},{12,4},{16,24},{20,28},{24,16},{28,20},{1,9},{5... | collective-permute-start | bytes 786440 | tf_op jit(solution)/shard_map/ppermute | solution.py:248
  74.2 7.9 %collective-permute-start.18 = (f32[64,1024]{1,0:T(8,128)S(1)}, f32[64,1024]{1,0:T(8,128)S(1)}, u32[]{:S(2)}, u32[]{:S(2)}) collective-permute-start(f32[64,1024]{1,0:T(8,128)S(1)} %pad_maximum_fusion.9), channel_id=1, source_target_pairs={{0,8},{4,12},{8,0},{12,4},{16,24},{20,28},{24,16},{28,20},{1,9},{5... | collective-permute-start | bytes 786440 | tf_op jit(solution)/shard_map/ppermute | solution.py:248
  74.6 17.7 %collective-permute-start.24 = (f32[64,2048]{1,0:T(8,128)}, f32[64,2048]{1,0:T(8,128)S(1)}, u32[]{:S(2)}, u32[]{:S(2)}) collective-permute-start(f32[64,2048]{1,0:T(8,128)} %pad_maximum_fusion.1), channel_id=1, source_target_pairs={{0,16},{4,20},{8,24},{12,28},{16,0},{20,4},{24,8},{28,12},{1,17},{... | collective-permute-start | bytes 1572872 | tf_op jit(solution)/shard_map/ppermute | solution.py:248
  83.6 7.4 %collective-permute-start.17 = (f32[64,1024]{1,0:T(8,128)}, f32[64,1024]{1,0:T(8,128)S(1)}, u32[]{:S(2)}, u32[]{:S(2)}) collective-permute-start(f32[64,1024]{1,0:T(8,128)} %bitcast.6), channel_id=1, source_target_pairs={{0,1},{1,0},{2,3},{3,2},{4,5},{5,4},{6,7},{7,6},{8,9},{9,8},{10,11... | collective-permute-start | bytes 786440 | tf_op jit(solution)/shard_map/ppermute | solution.py:254
  85.2 28.9 %collective-permute-start.26 = (f32[64,2048]{1,0:T(8,128)}, f32[64,2048]{1,0:T(8,128)}, u32[]{:S(2)}, u32[]{:S(2)}) collective-permute-start(f32[64,2048]{1,0:T(8,128)} %pad_maximum_fusion.2), channel_id=1, source_target_pairs={{0,8},{4,12},{8,0},{12,4},{16,24},{20,28},{24,16},{28,20},{1,9},{5... | collective-permute-start | bytes 1572872 | tf_op jit(solution)/shard_map/ppermute | solution.py:248
  85.6 19.8 %collective-permute-start.22 = (f32[64,1024]{1,0:T(8,128)}, f32[64,1024]{1,0:T(8,128)S(1)}, u32[]{:S(2)}, u32[]{:S(2)}) collective-permute-start(f32[64,1024]{1,0:T(8,128)} %bitcast.8), channel_id=1, source_target_pairs={{0,1},{1,0},{2,3},{3,2},{4,5},{5,4},{6,7},{7,6},{8,9},{9,8},{10,11... | collective-permute-start | bytes 786440 | tf_op jit(solution)/shard_map/ppermute | solution.py:254
  92.0 13.4 %collective-permute-start.20 = (f32[32,1024]{1,0:T(8,128)S(1)}, f32[32,1024]{1,0:T(8,128)S(1)}, u32[]{:S(2)}, u32[]{:S(2)}) collective-permute-start(f32[32,1024]{1,0:T(8,128)S(1)} %slice_add_fusion.10), channel_id=1, source_target_pairs={{0,16},{4,20},{8,24},{12,28},{16,0},{20,4},{24,8},{28,12},{1,17},{... | collective-permute-start | bytes 393224 | tf_op jit(solution)/shard_map/ppermute | solution.py:248
  109.5 83.3 %collective-permute-start.21 = (f32[32,1024]{1,0:T(8,128)}, f32[32,1024]{1,0:T(8,128)S(1)}, u32[]{:S(2)}, u32[]{:S(2)}) collective-permute-start(f32[32,1024]{1,0:T(8,128)} %bitcast.10), channel_id=1, source_target_pairs={{0,2},{1,3},{2,0},{3,1},{4,6},{5,7},{6,4},{7,5},{8,10},{9,11},{10,... | collective-permute-start | bytes 393224 | tf_op jit(solution)/shard_map/ppermute | solution.py:254
  110.8 14.5 %collective-permute-start.28 = (f32[64,2048]{1,0:T(8,128)}, f32[64,2048]{1,0:T(8,128)S(1)}, u32[]{:S(2)}, u32[]{:S(2)}) collective-permute-start(f32[64,2048]{1,0:T(8,128)} %pad_maximum_fusion.3), channel_id=1, source_target_pairs={{0,8},{4,12},{8,0},{12,4},{16,24},{20,28},{24,16},{28,20},{1,9},{5... | collective-permute-start | bytes 1572872 | tf_op jit(solution)/shard_map/ppermute | solution.py:248
  117.2 77.5 %collective-permute-start.25 = (f32[32,1024]{1,0:T(8,128)}, f32[32,1024]{1,0:T(8,128)S(1)}, u32[]{:S(2)}, u32[]{:S(2)}) collective-permute-start(f32[32,1024]{1,0:T(8,128)} %bitcast.12), channel_id=1, source_target_pairs={{0,2},{1,3},{2,0},{3,1},{4,6},{5,7},{6,4},{7,5},{8,10},{9,11},{10,... | collective-permute-start | bytes 393224 | tf_op jit(solution)/shard_map/ppermute | solution.py:254
  119.3 15.3 %collective-permute-start.27 = (f32[64,2048]{1,0:T(8,128)}, f32[64,2048]{1,0:T(8,128)}, u32[]{:S(2)}, u32[]{:S(2)}) collective-permute-start(f32[64,2048]{1,0:T(8,128)} %bitcast.39), channel_id=1, source_target_pairs={{0,1},{1,0},{2,3},{3,2},{4,5},{5,4},{6,7},{7,6},{8,9},{9,8},{10,11... | collective-permute-start | bytes 1572872 | tf_op jit(solution)/shard_map/ppermute | solution.py:254
  124.2 12.6 %collective-permute-start.32 = (f32[64,2048]{1,0:T(8,128)}, f32[64,2048]{1,0:T(8,128)S(1)}, u32[]{:S(2)}, u32[]{:S(2)}) collective-permute-start(f32[64,2048]{1,0:T(8,128)} %pad_maximum_fusion.6), channel_id=1, source_target_pairs={{0,16},{4,20},{8,24},{12,28},{16,0},{20,4},{24,8},{28,12},{1,17},{... | collective-permute-start | bytes 1572872 | tf_op jit(solution)/shard_map/ppermute | solution.py:248
  127.0 25.2 %collective-permute-start.31 = (f32[64,2048]{1,0:T(8,128)}, f32[64,2048]{1,0:T(8,128)}, u32[]{:S(2)}, u32[]{:S(2)}) collective-permute-start(f32[64,2048]{1,0:T(8,128)} %bitcast.38), channel_id=1, source_target_pairs={{0,1},{1,0},{2,3},{3,2},{4,5},{5,4},{6,7},{7,6},{8,9},{9,8},{10,11... | collective-permute-start | bytes 1572872 | tf_op jit(solution)/shard_map/ppermute | solution.py:254
  135.8 9.7 %collective-permute-start.30 = (f32[32,2048]{1,0:T(8,128)S(1)}, f32[32,2048]{1,0:T(8,128)S(1)}, u32[]{:S(2)}, u32[]{:S(2)}) collective-permute-start(f32[32,2048]{1,0:T(8,128)S(1)} %slice_add_fusion.2), channel_id=1, source_target_pairs={{0,16},{4,20},{8,24},{12,28},{16,0},{20,4},{24,8},{28,12},{1,17},{... | collective-permute-start | bytes 786440 | tf_op jit(solution)/shard_map/ppermute | solution.py:248
  144.3 12.1 %collective-permute-start.36 = (f32[64,1024]{1,0:T(8,128)}, f32[64,1024]{1,0:T(8,128)S(1)}, u32[]{:S(2)}, u32[]{:S(2)}) collective-permute-start(f32[64,1024]{1,0:T(8,128)} %pad_maximum_fusion.11), channel_id=1, source_target_pairs={{0,8},{4,12},{8,0},{12,4},{16,24},{20,28},{24,16},{28,20},{1,9},{5... | collective-permute-start | bytes 786440 | tf_op jit(solution)/shard_map/ppermute | solution.py:248
  155.0 39.7 %collective-permute-start.33 = (f32[32,2048]{1,0:T(8,128)}, f32[32,2048]{1,0:T(8,128)S(1)}, u32[]{:S(2)}, u32[]{:S(2)}) collective-permute-start(f32[32,2048]{1,0:T(8,128)} %bitcast.18), channel_id=1, source_target_pairs={{0,2},{1,3},{2,0},{3,1},{4,6},{5,7},{6,4},{7,5},{8,10},{9,11},{10,... | collective-permute-start | bytes 786440 | tf_op jit(solution)/shard_map/ppermute | solution.py:254
  156.4 8.1 %collective-permute-start.38 = (f32[64,1024]{1,0:T(8,128)}, f32[64,1024]{1,0:T(8,128)}, u32[]{:S(2)}, u32[]{:S(2)}) collective-permute-start(f32[64,1024]{1,0:T(8,128)} %pad_maximum_fusion.12), channel_id=1, source_target_pairs={{0,8},{4,12},{8,0},{12,4},{16,24},{20,28},{24,16},{28,20},{1,9},{5... | collective-permute-start | bytes 786440 | tf_op jit(solution)/shard_map/ppermute | solution.py:248
  163.3 10.5 %collective-permute-start.37 = (f32[64,1024]{1,0:T(8,128)}, f32[64,1024]{1,0:T(8,128)}, u32[]{:S(2)}, u32[]{:S(2)}) collective-permute-start(f32[64,1024]{1,0:T(8,128)} %bitcast.45), channel_id=1, source_target_pairs={{0,1},{1,0},{2,3},{3,2},{4,5},{5,4},{6,7},{7,6},{8,9},{9,8},{10,11... | collective-permute-start | bytes 786440 | tf_op jit(solution)/shard_map/ppermute | solution.py:254
  166.3 10.5 %collective-permute-start.41 = (f32[64,1024]{1,0:T(8,128)}, f32[64,1024]{1,0:T(8,128)S(1)}, u32[]{:S(2)}, u32[]{:S(2)}) collective-permute-start(f32[64,1024]{1,0:T(8,128)} %bitcast.24), channel_id=1, source_target_pairs={{0,1},{1,0},{2,3},{3,2},{4,5},{5,4},{6,7},{7,6},{8,9},{9,8},{10,11... | collective-permute-start | bytes 786440 | tf_op jit(solution)/shard_map/ppermute | solution.py:254
  173.8 20.9 %collective-permute-start.35 = (f32[32,2048]{1,0:T(8,128)}, f32[32,2048]{1,0:T(8,128)S(1)}, u32[]{:S(2)}, u32[]{:S(2)}) collective-permute-start(f32[32,2048]{1,0:T(8,128)} %bitcast.44), channel_id=1, source_target_pairs={{0,2},{1,3},{2,0},{3,1},{4,6},{5,7},{6,4},{7,5},{8,10},{9,11},{10,... | collective-permute-start | bytes 786440 | tf_op jit(solution)/shard_map/ppermute | solution.py:254
  190.1 7.3 %collective-permute-start.40 = (f32[32,1024]{1,0:T(8,128)}, f32[32,1024]{1,0:T(8,128)S(1)}, u32[]{:S(2)}, u32[]{:S(2)}) collective-permute-start(f32[32,1024]{1,0:T(8,128)} %bitcast.26), channel_id=1, source_target_pairs={{0,2},{1,3},{2,0},{3,1},{4,6},{5,7},{6,4},{7,5},{8,10},{9,11},{10,... | collective-permute-start | bytes 393224 | tf_op jit(solution)/shard_map/ppermute | solution.py:254
  192.8 7.5 %collective-permute-start.43 = (f32[32,1024]{1,0:T(8,128)}, f32[32,1024]{1,0:T(8,128)S(1)}, u32[]{:S(2)}, u32[]{:S(2)}) collective-permute-start(f32[32,1024]{1,0:T(8,128)} %bitcast.46), channel_id=1, source_target_pairs={{0,2},{1,3},{2,0},{3,1},{4,6},{5,7},{6,4},{7,5},{8,10},{9,11},{10,... | collective-permute-start | bytes 393224 | tf_op jit(solution)/shard_map/ppermute | solution.py:254
  (63 other events, 429.0 us)

commit v4 on v3

--- a/solution.py
+++ b/solution.py
@@ -45,6 +45,7 @@
         out_specs=[VMEM] * len(shapes),
         out_shape=shapes,
         cost_estimate=pl.CostEstimate(flops=0, bytes_accessed=4 * whole.size, transcendentals=0),
+        compiler_params=pltpu.CompilerParams(vmem_limit_bytes=2**20),
         name="cut",
     )(place, whole)
     return [outs[g * count : (g + 1) * count] for g in range(len(bounds))]
@@ -66,6 +67,7 @@
         out_specs=[VMEM] * (rows // part),
         out_shape=[shape] * (rows // part),
         cost_estimate=pl.CostEstimate(flops=0, bytes_accessed=rows * depth, transcendentals=0),
+        compiler_params=pltpu.CompilerParams(vmem_limit_bytes=2**20),
         name="pack",
     )(*blocks)
 
@@ -106,7 +108,7 @@
         cost_estimate=pl.CostEstimate(
             flops=rows * columns, bytes_accessed=4 * rows * columns, transcendentals=0
         ),
-        compiler_params=pltpu.CompilerParams(vmem_limit_bytes=8 * 2**20),
+        compiler_params=pltpu.CompilerParams(vmem_limit_bytes=3 * 2**20),
         name="split",
     )(whole)
 
@@ -167,7 +169,7 @@
             bytes_accessed=8 * total * depth,
             transcendentals=0,
         ),
-        compiler_params=pltpu.CompilerParams(vmem_limit_bytes=16 * 2**20),
+        compiler_params=pltpu.CompilerParams(vmem_limit_bytes=8 * total * depth + 3 * 2**20),
         name="product",
     )(place, pattern, block_order, *lefts, *[part for pair in factors for part in pair])
 
@@ -199,31 +201,30 @@
         cost_estimate=pl.CostEstimate(
             flops=5 * bare.size, bytes_accessed=8 * bare.size, transcendentals=0
         ),
-        compiler_params=pltpu.CompilerParams(vmem_limit_bytes=8 * 2**20),
+        compiler_params=pltpu.CompilerParams(vmem_limit_bytes=2 * 2**20),
         name="finish",
     )(place, bare, occ[:, None], virt[None, :], *[part_in for pair in pairs for part_in in pair])
 
 
 def event_order(events):
-    free = {}
+    taken = {}
     done = {}
-    order = []
-    waiting = dict(events)
-    while waiting:
-        best = None
-        for rank, (name, (needs, uses, length)) in enumerate(waiting.items()):
-            if any(need not in done for need in needs):
-                continue
-            start = max([done[need] for need in needs] + [free.get(r, 0.0) for r, _ in uses] + [0.0])
-            if best is None or start < best[0] - 1e-9:
-                best = (start, name)
-        start, name = best
-        needs, uses, length = waiting.pop(name)
+    starts = {}
+    for name, (needs, uses, length) in events.items():
+        start = max([done[need] for need in needs] + [0.0])
+        moved = True
+        while moved:
+            moved = False
+            for resource, busy in uses:
+                for low, high in taken.get(resource, ()):
+                    if low < start + busy - 1e-6 and start < high - 1e-6:
+                        start = high
+                        moved = True
         for resource, busy in uses:
-            free[resource] = start + busy
+            taken.setdefault(resource, []).append((start, start + busy))
         done[name] = start + length
-        order.append(name)
-    return order
+        starts[name] = start
+    return sorted(events, key=lambda name: starts[name])
 
 
 def shards(amplitudes, integrals, bare_terms, pattern, block_order, occ_gap, virt_gap):
@@ -328,8 +329,11 @@
         keys = [key for key in now if not key[1] & bit]
         pairs = [(now[r, s], now[r, s | bit]) for r, s in keys]
         leaving = jnp.concatenate([jnp.where(same, b, a) for a, b in pairs], axis=0)
-        width = leaving.shape[1]
-        leaving = leaving.reshape(-1, 2, narrow_bit * part, width)[:, ::-1].reshape(-1, width)
+        size = narrow_bit * part
+        leaving = jnp.concatenate(
+            [leaving[n * size : (n + 1) * size] for m in range(0, leaving.shape[0] // size, 2) for n in (m + 1, m)],
+            axis=0,
+        )
         arrived = along(ordered(leaving), narrow_bit)
         state[unit] = {}
         for n, (key, (a, b)) in enumerate(zip(keys, pairs)):
@@ -353,9 +357,6 @@
             [],
             [("mid", 1.0 * len(chunks)), ("end", 0.75 * len(chunks)), ("core", 0.7)],
         )
-    for half in range(2):
-        needs = [("gather", 0, 0)] if half == 0 else [("multiply", 0)]
-        event(("split", half), functools.partial(split_step, half), needs, [("core", 0.8)])
     for unit, (chunk, halves) in enumerate(UNITS):
         if unit == 0 or UNITS[unit - 1][0] != chunk:
             for number, bit in enumerate(chip_bits):
@@ -370,6 +371,10 @@
                     needs,
                     uses,
                 )
+        for half in halves:
+            if ("split", half) not in events:
+                needs = [("multiply", unit - 1)] if unit else [("gather", 0, 0)]
+                event(("split", half), functools.partial(split_step, half), needs, [("core", 0.8)])
         share = len(halves) / CORES
         before = ("multiply", unit)
         needs = [("gather", chunk, len(chip_bits) - 1)] + [("split", half) for half in halves]

time: 203 us -> 179 us (0.88)
  waiting for transfers between devices: 49.6 us -> 93.7 us
  local copies, waits for them, and re-layouts: 41.3 us -> 5.91 us
  other arithmetic: 25.2 us -> 1.3 us
  Pallas kernels: 35.1 us -> 28.4 us
  starting transfers between devices: 50.4 us -> 48.3 us
    ppermute x23, waiting for transfers between devices: 18.2 us -> 55.4 us  [across(): lax.ppermute(value, 'wide', [(w, w ^ mask) for w in range(wide_count)])]
    unnamed x102 -> x64, local copies, waits for them, and re-layouts: 31 us -> 5.66 us
    select_n x11 -> x12, other arithmetic: 11 us -> 0.53 us  [reduce_step(): leaving = jnp.concatenate([jnp.where(same, b, a) for a, b in pairs], axis=0)]
    rev x12 -> x0, local copies, waits for them, and re-layouts: 9.53 us -> none  [reduce_step(): leaving.reshape(-1, 2, narrow_bit * part, width)[:, ::-1].reshape(-1, width)]
    ppermute x21, waiting for transfers between devices: 31.4 us -> 38.3 us  [along(): lax.ppermute(value, 'narrow', [(n, n ^ mask) for n in range(narrow_count)])]
    add x6, other arithmetic: 6.47 us -> 0.21 us  [reduce_step(): kept + came]
    pallas_call x3, Pallas kernels: 5.23 us -> 0.07 us  [pack(): pl.pallas_call(functools.partial(pack_kernel, count, part), in_specs=[VME...]
    concatenate x6, other arithmetic: 3.15 us -> 0.15 us  [exchange_step(): send = ordered(jnp.concatenate([now[key] for key in keys], axis=0))]
  transfers between devices with their start and end apart: 44 -> 44, of which waited for: 18 -> 27; matrix products, arithmetic and copies ran while one was open for 18% -> 1% of each run, Pallas kernels for 16% -> 10%
where the time goes in v4:
time: 179 us; the launch traced here: 178 us
  waiting for transfers between devices  93.7 us (52%)
  starting transfers between devices  48.3 us (27%)
  Pallas kernels  28.4 us (16%)
  local copies, waits for them, and re-layouts  5.91 us (3%)
    ppermute x23, waiting for transfers between devices, across(): lax.ppermute(value, 'wide', [(w, w ^ mask) for w in range(wide_count)])  55.4 us
    ppermute x21, waiting for transfers between devices, along(): lax.ppermute(value, 'narrow', [(n, n ^ mask) for n in range(narrow_count)])  38.3 us
    ppermute x21, starting transfers between devices, along(): lax.ppermute(value, 'narrow', [(n, n ^ mask) for n in range(narrow_count)])  28.8 us
    ppermute x23, starting transfers between devices, across(): lax.ppermute(value, 'wide', [(w, w ^ mask) for w in range(wide_count)])  19.5 us
    pallas_call x6, Pallas kernels, product(): pl.pallas_call(functools.partial(product_kernel, count, rows, layout, hal...  18.3 us
    pallas_call x2, Pallas kernels, split(): pl.pallas_call(functools.partial(split_kernel, step), in_specs=[ANY], out...  7.55 us
    unnamed x64, local copies, waits for them, and re-layouts  5.66 us
  transfers between devices with their start and end apart: 44, of which 27 were waited for; matrix products, arithmetic and copies ran while one was open for 1% of the time, Pallas kernels for 10%

profile of v4, /device:TPU:0, one launch (start us, length us, event | category | flops | bytes accessed | tf_op | source)
XLA Modules:
  0.0 178.4 jit_solution(1898317967391676885)
XLA Ops:
  2.4 4.7 %collective-permute-start.2 = (f32[8,2048]{1,0:T(8,128)S(1)}, f32[8,2048]{1,0:T(8,128)S(1)}, u32[]{:S(2)}, u32[]{:S(2)}) collective-permute-start(f32[8,2048]{1,0:T(8,128)S(1)} %get-tuple-element.101), channel_id=1, source_target_pairs={{0,3},{1,2},{2,1},{3,0},{4,7},{5,6},{6,5},{7,4},{8,11},{9,10},{10,... | collective-permute-start | bytes 196616 | tf_op jit(solution)/shard_map/ppermute | solution.py:255
  10.0 3.2 %collective-permute-done.1.refs_2_ = f32[8,2048]{1,0:T(8,128)S(1)} collective-permute-done((f32[8,2048]{1,0:T(8,128)S(1)}, f32[8,2048]{1,0:T(8,128)S(1)}, u32[]{:S(2)}, u32[]{:S(2)}) %collective-permute-start.1) | collective-permute-done | bytes 65568 | tf_op jit(solution)/shard_map/ppermute | solution.py:255
  16.3 4.9 %collective-permute-done.4.refs_1_ = f32[32,2048]{1,0:T(8,128)S(1)} collective-permute-done((f32[32,2048]{1,0:T(8,128)S(1)}, f32[32,2048]{1,0:T(8,128)S(1)}, u32[]{:S(2)}, u32[]{:S(2)}) %collective-permute-start.4) | collective-permute-done | bytes 262176 | tf_op jit(solution)/shard_map/ppermute | solution.py:249
  24.6 3.4 %copy-done.4 = f32[2048,1024]{1,0:T(8,128)S(1)} copy-done((f32[2048,1024]{1,0:T(8,128)S(1)}, f32[2048,1024]{1,0:T(8,128)}, u32[]{:S(2)}) %copy-start.4) | copy-done | bytes 8388632
  29.7 2.4 %product.6 = (f32[32,1024]{1,0:T(8,128)S(1)}, f32[32,1024]{1,0:T(8,128)S(1)}, f32[32,1024]{1,0:T(8,128)S(1)}, f32[32,1024]{1,0:T(8,128)S(1)}) custom-call(s32[3]{0:T(128)S(1)} %pad_add_fusion.place_ref, s32[8,64]{1,0:T(8,128)S(1)} %copy-done.7, s32[8]{0:T(128)S(1)} %copy-done.8, f32[32,2048]{1,0:T(8,128)S(1)} %pack.3.refs_0_, ...), custom_call_target="tpu_custom_call" | custom-call | flops 1610612736 | bytes 2097152 | tf_op jit(solution)/shard_map/product/pallas_call | solution.py:161
  34.5 2.5 %collective-permute-start.13 = (f32[8,2048]{1,0:T(8,128)S(1)}, f32[8,2048]{1,0:T(8,128)S(1)}, u32[]{:S(2)}, u32[]{:S(2)}) collective-permute-start(f32[8,2048]{1,0:T(8,128)S(1)} %get-tuple-element.107), channel_id=1, source_target_pairs={{0,3},{1,2},{2,1},{3,0},{4,7},{5,6},{6,5},{7,4},{8,11},{9,10},{10,... | collective-permute-start | bytes 196616 | tf_op jit(solution)/shard_map/ppermute | solution.py:255
  40.7 2.5 %collective-permute-start.17 = (f32[16,2048]{1,0:T(8,128)S(1)}, f32[16,2048]{1,0:T(8,128)S(1)}, u32[]{:S(2)}, u32[]{:S(2)}) collective-permute-start(f32[16,2048]{1,0:T(8,128)S(1)} %get-tuple-element.114), channel_id=1, source_target_pairs={{0,3},{1,2},{2,1},{3,0},{4,7},{5,6},{6,5},{7,4},{8,11},{9,10},{10,... | collective-permute-start | bytes 393224 | tf_op jit(solution)/shard_map/ppermute | solution.py:255
  43.2 2.5 %collective-permute-done.12.refs_2_ = f32[8,2048]{1,0:T(8,128)S(1)} collective-permute-done((f32[8,2048]{1,0:T(8,128)S(1)}, f32[8,2048]{1,0:T(8,128)S(1)}, u32[]{:S(2)}, u32[]{:S(2)}) %collective-permute-start.12) | collective-permute-done | bytes 65568 | tf_op jit(solution)/shard_map/ppermute | solution.py:255
  45.7 3.0 %collective-permute-start.15 = (f32[16,2048]{1,0:T(8,128)S(1)}, f32[16,2048]{1,0:T(8,128)S(1)}, u32[]{:S(2)}, u32[]{:S(2)}) collective-permute-start(f32[16,2048]{1,0:T(8,128)S(1)} %get-tuple-element.112), channel_id=1, source_target_pairs={{0,1},{1,0},{2,3},{3,2},{4,5},{5,4},{6,7},{7,6},{8,9},{9,8},{10,11... | collective-permute-start | bytes 393224 | tf_op jit(solution)/shard_map/ppermute | solution.py:255
  48.9 4.0 %collective-permute-done.16.refs_2_ = f32[16,2048]{1,0:T(8,128)S(1)} collective-permute-done((f32[16,2048]{1,0:T(8,128)S(1)}, f32[16,2048]{1,0:T(8,128)S(1)}, u32[]{:S(2)}, u32[]{:S(2)}) %collective-permute-start.16) | collective-permute-done | bytes 131104 | tf_op jit(solution)/shard_map/ppermute | solution.py:255
  53.3 5.8 %split.3 = (bf16[2048,1024]{1,0:T(8,128)(2,1)S(1)}, bf16[2048,1024]{1,0:T(8,128)(2,1)S(1)}) custom-call(f32[2048,1024]{1,0:T(8,128)} %collective-permute-done.8.whole_ref), custom_call_target="tpu_custom_call" | custom-call | flops 2097152 | bytes 8388608 | tf_op jit(solution)/shard_map/split/pallas_call | solution.py:99
  59.1 2.5 %product.7 = (f32[32,1024]{1,0:T(8,128)S(1)}, f32[32,1024]{1,0:T(8,128)S(1)}, f32[32,1024]{1,0:T(8,128)S(1)}, f32[32,1024]{1,0:T(8,128)S(1)}) custom-call(s32[3]{0:T(128)S(1)} %pad_add_fusion.place_ref, s32[8,64]{1,0:T(8,128)S(1)} %copy-done.7, s32[8]{0:T(128)S(1)} %copy-done.8, f32[32,2048]{1,0:T(8,128)S(1)} %pack.3.refs_0_, ...), custom_call_target="tpu_custom_call" | custom-call | flops 1610612736 | bytes 2097152 | tf_op jit(solution)/shard_map/product/pallas_call | solution.py:161
  64.4 6.6 %collective-permute-done.10 = f32[64,1024]{1,0:T(8,128)S(1)} collective-permute-done((f32[64,1024]{1,0:T(8,128)S(1)}, f32[64,1024]{1,0:T(8,128)S(1)}, u32[]{:S(2)}, u32[]{:S(2)}) %collective-permute-start.10) | collective-permute-done | bytes 262176 | tf_op jit(solution)/shard_map/ppermute | solution.py:249
  72.5 4.0 %collective-permute-done.21.refs_1_ = f32[32,2048]{1,0:T(8,128)S(1)} collective-permute-done((f32[32,2048]{1,0:T(8,128)S(1)}, f32[32,2048]{1,0:T(8,128)S(1)}, u32[]{:S(2)}, u32[]{:S(2)}) %collective-permute-start.21) | collective-permute-done | bytes 262176 | tf_op jit(solution)/shard_map/ppermute | solution.py:249
  77.7 2.8 %collective-permute-start.18 = (f32[32,1024]{1,0:T(8,128)S(1)}, f32[32,1024]{1,0:T(8,128)S(1)}, u32[]{:S(2)}, u32[]{:S(2)}) collective-permute-start(f32[32,1024]{1,0:T(8,128)S(1)} %pad_maximum_fusion.11), channel_id=1, source_target_pairs={{0,2},{1,3},{2,0},{3,1},{4,6},{5,7},{6,4},{7,5},{8,10},{9,11},{10,... | collective-permute-start | bytes 393224 | tf_op jit(solution)/shard_map/ppermute | solution.py:255
  83.2 3.8 %collective-permute-done.20 = f32[32,1024]{1,0:T(8,128)S(1)} collective-permute-done((f32[32,1024]{1,0:T(8,128)S(1)}, f32[32,1024]{1,0:T(8,128)S(1)}, u32[]{:S(2)}, u32[]{:S(2)}) %collective-permute-start.20) | collective-permute-done | bytes 131104 | tf_op jit(solution)/shard_map/ppermute | solution.py:249
  87.6 10.7 %collective-permute-done.24.refs_2_ = f32[64,2048]{1,0:T(8,128)S(1)} collective-permute-done((f32[64,2048]{1,0:T(8,128)S(1)}, f32[64,2048]{1,0:T(8,128)S(1)}, u32[]{:S(2)}, u32[]{:S(2)}) %collective-permute-start.24) | collective-permute-done | bytes 524320 | tf_op jit(solution)/shard_map/ppermute | solution.py:249
  98.3 4.1 %product.8 = (f32[32,2048]{1,0:T(8,128)S(1)}, f32[32,2048]{1,0:T(8,128)S(1)}, f32[32,2048]{1,0:T(8,128)S(1)}, f32[32,2048]{1,0:T(8,128)S(1)}) custom-call(s32[3]{0:T(128)S(1)} %pad_add_fusion.place_ref, s32[8,64]{1,0:T(8,128)S(1)} %copy-done.7, s32[8]{0:T(128)S(1)} %copy-done.8, f32[32,2048]{1,0:T(8,128)S(1)} %pack.4.refs_0_, ...), custom_call_target="tpu_custom_call" | custom-call | flops 3221225472 | bytes 2097152 | tf_op jit(solution)/shard_map/product/pallas_call | solution.py:161
  103.8 3.9 %collective-permute-done.27.refs_2_ = f32[64,2048]{1,0:T(8,128)S(1)} collective-permute-done((f32[64,2048]{1,0:T(8,128)S(1)}, f32[64,2048]{1,0:T(8,128)S(1)}, u32[]{:S(2)}, u32[]{:S(2)}) %collective-permute-start.27) | collective-permute-done | bytes 524320 | tf_op jit(solution)/shard_map/ppermute | solution.py:249
  107.7 4.3 %product.9 = (f32[32,2048]{1,0:T(8,128)S(1)}, f32[32,2048]{1,0:T(8,128)S(1)}, f32[32,2048]{1,0:T(8,128)S(1)}, f32[32,2048]{1,0:T(8,128)S(1)}) custom-call(s32[3]{0:T(128)S(1)} %pad_add_fusion.place_ref, s32[8,64]{1,0:T(8,128)S(1)} %copy-done.7, s32[8]{0:T(128)S(1)} %copy-done.8, f32[32,2048]{1,0:T(8,128)S(1)} %get-tuple-element.157.refs_0_, ...), custom_call_target="tpu_custom_call" | custom-call | flops 3221225472 | bytes 2097152 | tf_op jit(solution)/shard_map/product/pallas_call | solution.py:161
  112.4 2.4 %collective-permute-done.25 = f32[64,2048]{1,0:T(8,128)S(1)} collective-permute-done((f32[64,2048]{1,0:T(8,128)S(1)}, f32[64,2048]{1,0:T(8,128)S(1)}, u32[]{:S(2)}, u32[]{:S(2)}) %collective-permute-start.25) | collective-permute-done | bytes 524320 | tf_op jit(solution)/shard_map/ppermute | solution.py:249
  115.0 2.3 %collective-permute-start.28 = (f32[64,2048]{1,0:T(8,128)S(1)}, f32[64,2048]{1,0:T(8,128)S(1)}, u32[]{:S(2)}, u32[]{:S(2)}) collective-permute-start(f32[64,2048]{1,0:T(8,128)S(1)} %constant_dynamic-update-slice_fusion.16), channel_id=1, source_target_pairs={{0,1},{1,0},{2,3},{3,2},{4,5},{5,4},{6,7},{7,6},{8,9},{9,8},{10,11... | collective-permute-start | bytes 1572872 | tf_op jit(solution)/shard_map/ppermute | solution.py:255
  117.3 2.5 %product.10 = (f32[32,1024]{1,0:T(8,128)S(1)}, f32[32,1024]{1,0:T(8,128)S(1)}, f32[32,1024]{1,0:T(8,128)S(1)}, f32[32,1024]{1,0:T(8,128)S(1)}) custom-call(s32[3]{0:T(128)S(1)} %pad_add_fusion.place_ref, s32[8,64]{1,0:T(8,128)S(1)} %copy-done.7, s32[8]{0:T(128)S(1)} %copy-done.8, f32[32,2048]{1,0:T(8,128)S(1)} %get-tuple-element.167.refs_0_, ...), custom_call_target="tpu_custom_call" | custom-call | flops 1610612736 | bytes 2097152 | tf_op jit(solution)/shard_map/product/pallas_call | solution.py:161
  120.3 2.5 %product.11 = (f32[32,1024]{1,0:T(8,128)S(1)}, f32[32,1024]{1,0:T(8,128)S(1)}, f32[32,1024]{1,0:T(8,128)S(1)}, f32[32,1024]{1,0:T(8,128)S(1)}) custom-call(s32[3]{0:T(128)S(1)} %pad_add_fusion.place_ref, s32[8,64]{1,0:T(8,128)S(1)} %copy-done.7, s32[8]{0:T(128)S(1)} %copy-done.8, f32[32,2048]{1,0:T(8,128)S(1)} %get-tuple-element.167.refs_0_, ...), custom_call_target="tpu_custom_call" | custom-call | flops 1610612736 | bytes 2097152 | tf_op jit(solution)/shard_map/product/pallas_call | solution.py:161
  129.6 6.7 %collective-permute-done.33 = f32[64,2048]{1,0:T(8,128)S(1)} collective-permute-done((f32[64,2048]{1,0:T(8,128)S(1)}, f32[64,2048]{1,0:T(8,128)S(1)}, u32[]{:S(2)}, u32[]{:S(2)}) %collective-permute-start.33) | collective-permute-done | bytes 524320 | tf_op jit(solution)/shard_map/ppermute | solution.py:255
  139.0 4.9 %collective-permute-done.34 = f32[32,2048]{1,0:T(8,128)S(1)} collective-permute-done((f32[32,2048]{1,0:T(8,128)S(1)}, f32[32,2048]{1,0:T(8,128)S(1)}, u32[]{:S(2)}, u32[]{:S(2)}) %collective-permute-start.34) | collective-permute-done | bytes 262176 | tf_op jit(solution)/shard_map/ppermute | solution.py:249
  146.2 7.7 %collective-permute-done.37 = f32[64,1024]{1,0:T(8,128)S(1)} collective-permute-done((f32[64,1024]{1,0:T(8,128)S(1)}, f32[64,1024]{1,0:T(8,128)S(1)}, u32[]{:S(2)}, u32[]{:S(2)}) %collective-permute-start.37) | collective-permute-done | bytes 262176 | tf_op jit(solution)/shard_map/ppermute | solution.py:255
  154.1 2.6 %collective-permute-done.41 = f32[64,1024]{1,0:T(8,128)S(1)} collective-permute-done((f32[64,1024]{1,0:T(8,128)S(1)}, f32[64,1024]{1,0:T(8,128)S(1)}, u32[]{:S(2)}, u32[]{:S(2)}) %collective-permute-start.41) | collective-permute-done | bytes 262176 | tf_op jit(solution)/shard_map/ppermute | solution.py:255
  157.5 4.2 %collective-permute-done.39 = f32[32,1024]{1,0:T(8,128)S(1)} collective-permute-done((f32[32,1024]{1,0:T(8,128)S(1)}, f32[32,1024]{1,0:T(8,128)S(1)}, u32[]{:S(2)}, u32[]{:S(2)}) %collective-permute-start.39) | collective-permute-done | bytes 131104 | tf_op jit(solution)/shard_map/ppermute | solution.py:249
  162.6 4.2 %collective-permute-done.42 = f32[32,1024]{1,0:T(8,128)S(1)} collective-permute-done((f32[32,1024]{1,0:T(8,128)S(1)}, f32[32,1024]{1,0:T(8,128)S(1)}, u32[]{:S(2)}, u32[]{:S(2)}) %collective-permute-start.42) | collective-permute-done | bytes 131104 | tf_op jit(solution)/shard_map/ppermute | solution.py:249
  167.3 2.6 %collective-permute-start.43 = (f32[32,1024]{1,0:T(8,128)S(1)}, f32[32,1024]{1,0:T(8,128)S(1)}, u32[]{:S(2)}, u32[]{:S(2)}) collective-permute-start(f32[32,1024]{1,0:T(8,128)S(1)} %pad_maximum_fusion.14), channel_id=1, source_target_pairs={{0,2},{1,3},{2,0},{3,1},{4,6},{5,7},{6,4},{7,5},{8,10},{9,11},{10,... | collective-permute-start | bytes 393224 | tf_op jit(solution)/shard_map/ppermute | solution.py:255
  169.9 5.3 %collective-permute-done.40.refs_9_ = f32[32,1024]{1,0:T(8,128)S(1)} collective-permute-done((f32[32,1024]{1,0:T(8,128)S(1)}, f32[32,1024]{1,0:T(8,128)S(1)}, u32[]{:S(2)}, u32[]{:S(2)}) %collective-permute-start.40) | collective-permute-done | bytes 131104 | tf_op jit(solution)/shard_map/ppermute | solution.py:255
  (188 shorter events, 48.1 us)
Async XLA Ops:
  0.0 53.3 %collective-permute-start.8 = (f32[2048,1024]{1,0:T(8,128)}, f32[2048,1024]{1,0:T(8,128)}, u32[]{:S(2)}, u32[]{:S(2)}) collective-permute-start(f32[2048,1024]{1,0:T(8,128)} %whole_ref.2), channel_id=1, source_target_pairs={{0,4},{4,0},{8,12},{12,8},{16,20},{20,16},{24,28},{28,24},{1,5},{5... | collective-permute-start | bytes 25165832 | tf_op jit(solution)/shard_map/ppermute | solution.py:249
  2.4 7.6 %collective-permute-start.2 = (f32[8,2048]{1,0:T(8,128)S(1)}, f32[8,2048]{1,0:T(8,128)S(1)}, u32[]{:S(2)}, u32[]{:S(2)}) collective-permute-start(f32[8,2048]{1,0:T(8,128)S(1)} %get-tuple-element.101), channel_id=1, source_target_pairs={{0,3},{1,2},{2,1},{3,0},{4,7},{5,6},{6,5},{7,4},{8,11},{9,10},{10,... | collective-permute-start | bytes 196616 | tf_op jit(solution)/shard_map/ppermute | solution.py:255
  13.2 8.0 %collective-permute-start.4 = (f32[32,2048]{1,0:T(8,128)S(1)}, f32[32,2048]{1,0:T(8,128)S(1)}, u32[]{:S(2)}, u32[]{:S(2)}) collective-permute-start(f32[32,2048]{1,0:T(8,128)S(1)} %pack.3.refs_0_), channel_id=1, source_target_pairs={{0,8},{4,12},{8,0},{12,4},{16,24},{20,28},{24,16},{28,20},{1,9},{5... | collective-permute-start | bytes 786440 | tf_op jit(solution)/shard_map/ppermute | solution.py:249
  14.8 7.7 %collective-permute-start.3 = (f32[32,2048]{1,0:T(8,128)S(1)}, f32[32,2048]{1,0:T(8,128)S(1)}, u32[]{:S(2)}, u32[]{:S(2)}) collective-permute-start(f32[32,2048]{1,0:T(8,128)S(1)} %pack.3.refs_0_), channel_id=1, source_target_pairs={{0,16},{4,20},{8,24},{12,28},{16,0},{20,4},{24,8},{28,12},{1,17},{... | collective-permute-start | bytes 786440 | tf_op jit(solution)/shard_map/ppermute | solution.py:249
  22.4 7.2 %collective-permute-start.6 = (f32[16,2048]{1,0:T(8,128)S(1)}, f32[16,2048]{1,0:T(8,128)S(1)}, u32[]{:S(2)}, u32[]{:S(2)}) collective-permute-start(f32[16,2048]{1,0:T(8,128)S(1)} %slice.344), channel_id=1, source_target_pairs={{0,8},{4,12},{8,0},{12,4},{16,24},{20,28},{24,16},{28,20},{1,9},{5... | collective-permute-start | bytes 393224 | tf_op jit(solution)/shard_map/ppermute | solution.py:249
  33.0 20.2 %collective-permute-start.7 = (f32[64,1024]{1,0:T(8,128)S(1)}, f32[64,1024]{1,0:T(8,128)S(1)}, u32[]{:S(2)}, u32[]{:S(2)}) collective-permute-start(f32[64,1024]{1,0:T(8,128)S(1)} %pad_maximum_fusion.5), channel_id=1, source_target_pairs={{0,8},{4,12},{8,0},{12,4},{16,24},{20,28},{24,16},{28,20},{1,9},{5... | collective-permute-start | bytes 786440 | tf_op jit(solution)/shard_map/ppermute | solution.py:249
  37.0 8.7 %collective-permute-start.12 = (f32[8,2048]{1,0:T(8,128)S(1)}, f32[8,2048]{1,0:T(8,128)S(1)}, u32[]{:S(2)}, u32[]{:S(2)}) collective-permute-start(f32[8,2048]{1,0:T(8,128)S(1)} %get-tuple-element.106), channel_id=1, source_target_pairs={{0,2},{1,3},{2,0},{3,1},{4,6},{5,7},{6,4},{7,5},{8,10},{9,11},{10,... | collective-permute-start | bytes 196616 | tf_op jit(solution)/shard_map/ppermute | solution.py:255
  37.2 8.5 %collective-permute-start.11 = (f32[8,2048]{1,0:T(8,128)S(1)}, f32[8,2048]{1,0:T(8,128)S(1)}, u32[]{:S(2)}, u32[]{:S(2)}) collective-permute-start(f32[8,2048]{1,0:T(8,128)S(1)} %get-tuple-element.105), channel_id=1, source_target_pairs={{0,1},{1,0},{2,3},{3,2},{4,5},{5,4},{6,7},{7,6},{8,9},{9,8},{10,11... | collective-permute-start | bytes 196616 | tf_op jit(solution)/shard_map/ppermute | solution.py:255
  40.7 8.2 %collective-permute-start.17 = (f32[16,2048]{1,0:T(8,128)S(1)}, f32[16,2048]{1,0:T(8,128)S(1)}, u32[]{:S(2)}, u32[]{:S(2)}) collective-permute-start(f32[16,2048]{1,0:T(8,128)S(1)} %get-tuple-element.114), channel_id=1, source_target_pairs={{0,3},{1,2},{2,1},{3,0},{4,7},{5,6},{6,5},{7,4},{8,11},{9,10},{10,... | collective-permute-start | bytes 393224 | tf_op jit(solution)/shard_map/ppermute | solution.py:255
  45.7 7.4 %collective-permute-start.15 = (f32[16,2048]{1,0:T(8,128)S(1)}, f32[16,2048]{1,0:T(8,128)S(1)}, u32[]{:S(2)}, u32[]{:S(2)}) collective-permute-start(f32[16,2048]{1,0:T(8,128)S(1)} %get-tuple-element.112), channel_id=1, source_target_pairs={{0,1},{1,0},{2,3},{3,2},{4,5},{5,4},{6,7},{7,6},{8,9},{9,8},{10,11... | collective-permute-start | bytes 393224 | tf_op jit(solution)/shard_map/ppermute | solution.py:255
  61.7 9.3 %collective-permute-start.10 = (f32[64,1024]{1,0:T(8,128)S(1)}, f32[64,1024]{1,0:T(8,128)S(1)}, u32[]{:S(2)}, u32[]{:S(2)}) collective-permute-start(f32[64,1024]{1,0:T(8,128)S(1)} %pad_maximum_fusion.6), channel_id=1, source_target_pairs={{0,8},{4,12},{8,0},{12,4},{16,24},{20,28},{24,16},{28,20},{1,9},{5... | collective-permute-start | bytes 786440 | tf_op jit(solution)/shard_map/ppermute | solution.py:249
  62.4 9.4 %collective-permute-start.9 = (f32[64,1024]{1,0:T(8,128)S(1)}, f32[64,1024]{1,0:T(8,128)S(1)}, u32[]{:S(2)}, u32[]{:S(2)}) collective-permute-start(f32[64,1024]{1,0:T(8,128)S(1)} %constant_dynamic-update-slice_fusion), channel_id=1, source_target_pairs={{0,1},{1,0},{2,3},{3,2},{4,5},{5,4},{6,7},{7,6},{8,9},{9,8},{10,11... | collective-permute-start | bytes 786440 | tf_op jit(solution)/shard_map/ppermute | solution.py:255
  62.9 13.6 %collective-permute-start.21 = (f32[32,2048]{1,0:T(8,128)S(1)}, f32[32,2048]{1,0:T(8,128)S(1)}, u32[]{:S(2)}, u32[]{:S(2)}) collective-permute-start(f32[32,2048]{1,0:T(8,128)S(1)} %pack.4.refs_0_), channel_id=1, source_target_pairs={{0,8},{4,12},{8,0},{12,4},{16,24},{20,28},{24,16},{28,20},{1,9},{5... | collective-permute-start | bytes 786440 | tf_op jit(solution)/shard_map/ppermute | solution.py:249
  71.1 9.4 %collective-permute-start.19 = (f32[64,1024]{1,0:T(8,128)S(1)}, f32[64,1024]{1,0:T(8,128)S(1)}, u32[]{:S(2)}, u32[]{:S(2)}) collective-permute-start(f32[64,1024]{1,0:T(8,128)S(1)} %constant_dynamic-update-slice_fusion.8), channel_id=1, source_target_pairs={{0,1},{1,0},{2,3},{3,2},{4,5},{5,4},{6,7},{7,6},{8,9},{9,8},{10,11... | collective-permute-start | bytes 786440 | tf_op jit(solution)/shard_map/ppermute | solution.py:255
  71.8 11.4 %collective-permute-start.23 = (f32[32,2048]{1,0:T(8,128)S(1)}, f32[32,2048]{1,0:T(8,128)S(1)}, u32[]{:S(2)}, u32[]{:S(2)}) collective-permute-start(f32[32,2048]{1,0:T(8,128)S(1)} %get-tuple-element.157.refs_0_), channel_id=1, source_target_pairs={{0,8},{4,12},{8,0},{12,4},{16,24},{20,28},{24,16},{28,20},{1,9},{5... | collective-permute-start | bytes 786440 | tf_op jit(solution)/shard_map/ppermute | solution.py:249
  77.7 89.5 %collective-permute-start.18 = (f32[32,1024]{1,0:T(8,128)S(1)}, f32[32,1024]{1,0:T(8,128)S(1)}, u32[]{:S(2)}, u32[]{:S(2)}) collective-permute-start(f32[32,1024]{1,0:T(8,128)S(1)} %pad_maximum_fusion.11), channel_id=1, source_target_pairs={{0,2},{1,3},{2,0},{3,1},{4,6},{5,7},{6,4},{7,5},{8,10},{9,11},{10,... | collective-permute-start | bytes 393224 | tf_op jit(solution)/shard_map/ppermute | solution.py:255
  81.7 16.6 %collective-permute-start.24 = (f32[64,2048]{1,0:T(8,128)S(1)}, f32[64,2048]{1,0:T(8,128)S(1)}, u32[]{:S(2)}, u32[]{:S(2)}) collective-permute-start(f32[64,2048]{1,0:T(8,128)S(1)} %pad_maximum_fusion), channel_id=1, source_target_pairs={{0,16},{4,20},{8,24},{12,28},{16,0},{20,4},{24,8},{28,12},{1,17},{... | collective-permute-start | bytes 1572872 | tf_op jit(solution)/shard_map/ppermute | solution.py:249
  87.2 20.5 %collective-permute-start.27 = (f32[64,2048]{1,0:T(8,128)S(1)}, f32[64,2048]{1,0:T(8,128)S(1)}, u32[]{:S(2)}, u32[]{:S(2)}) collective-permute-start(f32[64,2048]{1,0:T(8,128)S(1)} %pad_maximum_fusion.1), channel_id=1, source_target_pairs={{0,16},{4,20},{8,24},{12,28},{16,0},{20,4},{24,8},{28,12},{1,17},{... | collective-permute-start | bytes 1572872 | tf_op jit(solution)/shard_map/ppermute | solution.py:249
  87.2 82.7 %collective-permute-start.22 = (f32[32,1024]{1,0:T(8,128)S(1)}, f32[32,1024]{1,0:T(8,128)S(1)}, u32[]{:S(2)}, u32[]{:S(2)}) collective-permute-start(f32[32,1024]{1,0:T(8,128)S(1)} %pad_maximum_fusion.12), channel_id=1, source_target_pairs={{0,2},{1,3},{2,0},{3,1},{4,6},{5,7},{6,4},{7,5},{8,10},{9,11},{10,... | collective-permute-start | bytes 393224 | tf_op jit(solution)/shard_map/ppermute | solution.py:255
  102.5 12.3 %collective-permute-start.25 = (f32[64,2048]{1,0:T(8,128)S(1)}, f32[64,2048]{1,0:T(8,128)S(1)}, u32[]{:S(2)}, u32[]{:S(2)}) collective-permute-start(f32[64,2048]{1,0:T(8,128)S(1)} %pad_maximum_fusion.2), channel_id=1, source_target_pairs={{0,8},{4,12},{8,0},{12,4},{16,24},{20,28},{24,16},{28,20},{1,9},{5... | collective-permute-start | bytes 1572872 | tf_op jit(solution)/shard_map/ppermute | solution.py:249
  103.1 14.2 %collective-permute-start.30 = (f32[64,2048]{1,0:T(8,128)S(1)}, f32[64,2048]{1,0:T(8,128)S(1)}, u32[]{:S(2)}, u32[]{:S(2)}) collective-permute-start(f32[64,2048]{1,0:T(8,128)S(1)} %pad_maximum_fusion.3), channel_id=1, source_target_pairs={{0,16},{4,20},{8,24},{12,28},{16,0},{20,4},{24,8},{28,12},{1,17},{... | collective-permute-start | bytes 1572872 | tf_op jit(solution)/shard_map/ppermute | solution.py:249
  112.1 11.8 %collective-permute-start.29 = (f32[64,2048]{1,0:T(8,128)S(1)}, f32[64,2048]{1,0:T(8,128)S(1)}, u32[]{:S(2)}, u32[]{:S(2)}) collective-permute-start(f32[64,2048]{1,0:T(8,128)S(1)} %pad_maximum_fusion.4), channel_id=1, source_target_pairs={{0,8},{4,12},{8,0},{12,4},{16,24},{20,28},{24,16},{28,20},{1,9},{5... | collective-permute-start | bytes 1572872 | tf_op jit(solution)/shard_map/ppermute | solution.py:249
  115.0 12.8 %collective-permute-start.28 = (f32[64,2048]{1,0:T(8,128)S(1)}, f32[64,2048]{1,0:T(8,128)S(1)}, u32[]{:S(2)}, u32[]{:S(2)}) collective-permute-start(f32[64,2048]{1,0:T(8,128)S(1)} %constant_dynamic-update-slice_fusion.16), channel_id=1, source_target_pairs={{0,1},{1,0},{2,3},{3,2},{4,5},{5,4},{6,7},{7,6},{8,9},{9,8},{10,11... | collective-permute-start | bytes 1572872 | tf_op jit(solution)/shard_map/ppermute | solution.py:255
  124.1 12.2 %collective-permute-start.33 = (f32[64,2048]{1,0:T(8,128)S(1)}, f32[64,2048]{1,0:T(8,128)S(1)}, u32[]{:S(2)}, u32[]{:S(2)}) collective-permute-start(f32[64,2048]{1,0:T(8,128)S(1)} %constant_dynamic-update-slice_fusion.24), channel_id=1, source_target_pairs={{0,1},{1,0},{2,3},{3,2},{4,5},{5,4},{6,7},{7,6},{8,9},{9,8},{10,11... | collective-permute-start | bytes 1572872 | tf_op jit(solution)/shard_map/ppermute | solution.py:255
  127.8 9.2 %collective-permute-start.31 = (f32[32,2048]{1,0:T(8,128)S(1)}, f32[32,2048]{1,0:T(8,128)S(1)}, u32[]{:S(2)}, u32[]{:S(2)}) collective-permute-start(f32[32,2048]{1,0:T(8,128)S(1)} %slice_add_fusion.2), channel_id=1, source_target_pairs={{0,16},{4,20},{8,24},{12,28},{16,0},{20,4},{24,8},{28,12},{1,17},{... | collective-permute-start | bytes 786440 | tf_op jit(solution)/shard_map/ppermute | solution.py:249
  128.5 7.8 %collective-permute-start.38 = (f32[64,1024]{1,0:T(8,128)S(1)}, f32[64,1024]{1,0:T(8,128)S(1)}, u32[]{:S(2)}, u32[]{:S(2)}) collective-permute-start(f32[64,1024]{1,0:T(8,128)S(1)} %pad_maximum_fusion.9), channel_id=1, source_target_pairs={{0,8},{4,12},{8,0},{12,4},{16,24},{20,28},{24,16},{28,20},{1,9},{5... | collective-permute-start | bytes 786440 | tf_op jit(solution)/shard_map/ppermute | solution.py:249
  137.2 32.7 %collective-permute-start.32 = (f32[32,2048]{1,0:T(8,128)S(1)}, f32[32,2048]{1,0:T(8,128)S(1)}, u32[]{:S(2)}, u32[]{:S(2)}) collective-permute-start(f32[32,2048]{1,0:T(8,128)S(1)} %pad_maximum_fusion.8), channel_id=1, source_target_pairs={{0,2},{1,3},{2,0},{3,1},{4,6},{5,7},{6,4},{7,5},{8,10},{9,11},{10,... | collective-permute-start | bytes 786440 | tf_op jit(solution)/shard_map/ppermute | solution.py:255
  144.1 9.8 %collective-permute-start.37 = (f32[64,1024]{1,0:T(8,128)S(1)}, f32[64,1024]{1,0:T(8,128)S(1)}, u32[]{:S(2)}, u32[]{:S(2)}) collective-permute-start(f32[64,1024]{1,0:T(8,128)S(1)} %constant_dynamic-update-slice_fusion.32), channel_id=1, source_target_pairs={{0,1},{1,0},{2,3},{3,2},{4,5},{5,4},{6,7},{7,6},{8,9},{9,8},{10,11... | collective-permute-start | bytes 786440 | tf_op jit(solution)/shard_map/ppermute | solution.py:255
  145.3 11.5 %collective-permute-start.41 = (f32[64,1024]{1,0:T(8,128)S(1)}, f32[64,1024]{1,0:T(8,128)S(1)}, u32[]{:S(2)}, u32[]{:S(2)}) collective-permute-start(f32[64,1024]{1,0:T(8,128)S(1)} %constant_dynamic-update-slice_fusion.40), channel_id=1, source_target_pairs={{0,1},{1,0},{2,3},{3,2},{4,5},{5,4},{6,7},{7,6},{8,9},{9,8},{10,11... | collective-permute-start | bytes 786440 | tf_op jit(solution)/shard_map/ppermute | solution.py:255
  153.9 16.0 %collective-permute-start.35 = (f32[32,2048]{1,0:T(8,128)S(1)}, f32[32,2048]{1,0:T(8,128)S(1)}, u32[]{:S(2)}, u32[]{:S(2)}) collective-permute-start(f32[32,2048]{1,0:T(8,128)S(1)} %pad_maximum_fusion.10), channel_id=1, source_target_pairs={{0,2},{1,3},{2,0},{3,1},{4,6},{5,7},{6,4},{7,5},{8,10},{9,11},{10,... | collective-permute-start | bytes 786440 | tf_op jit(solution)/shard_map/ppermute | solution.py:255
  166.8 8.4 %collective-permute-start.40 = (f32[32,1024]{1,0:T(8,128)S(1)}, f32[32,1024]{1,0:T(8,128)S(1)}, u32[]{:S(2)}, u32[]{:S(2)}) collective-permute-start(f32[32,1024]{1,0:T(8,128)S(1)} %pad_maximum_fusion.13), channel_id=1, source_target_pairs={{0,2},{1,3},{2,0},{3,1},{4,6},{5,7},{6,4},{7,5},{8,10},{9,11},{10,... | collective-permute-start | bytes 393224 | tf_op jit(solution)/shard_map/ppermute | solution.py:255
  167.3 9.3 %collective-permute-start.43 = (f32[32,1024]{1,0:T(8,128)S(1)}, f32[32,1024]{1,0:T(8,128)S(1)}, u32[]{:S(2)}, u32[]{:S(2)}) collective-permute-start(f32[32,1024]{1,0:T(8,128)S(1)} %pad_maximum_fusion.14), channel_id=1, source_target_pairs={{0,2},{1,3},{2,0},{3,1},{4,6},{5,7},{6,4},{7,5},{8,10},{9,11},{10,... | collective-permute-start | bytes 393224 | tf_op jit(solution)/shard_map/ppermute | solution.py:255
  (23 other events, 248.9 us)

commit v5 on v4

--- a/solution.py
+++ b/solution.py
@@ -13,10 +13,12 @@
 GROUPS = ((0,), (1,), (2, 3))
 UNITS = ((0, (0,)), (0, (1,)), (1, (0, 1)), (2, (0, 1)), (3, (0,)), (3, (1,)))
 LATENCY = 0.5
+SLACK = 0.3
 
 SMEM = pl.BlockSpec(memory_space=pltpu.SMEM)
 VMEM = pl.BlockSpec(memory_space=pltpu.VMEM)
 ANY = pl.BlockSpec(memory_space=pl.ANY)
+SMALL = pl.CostEstimate(flops=1, bytes_accessed=1, transcendentals=0)
 
 
 def after(value, *others):
@@ -44,7 +46,7 @@
         in_specs=[SMEM, VMEM],
         out_specs=[VMEM] * len(shapes),
         out_shape=shapes,
-        cost_estimate=pl.CostEstimate(flops=0, bytes_accessed=4 * whole.size, transcendentals=0),
+        cost_estimate=SMALL,
         compiler_params=pltpu.CompilerParams(vmem_limit_bytes=2**20),
         name="cut",
     )(place, whole)
@@ -66,7 +68,7 @@
         in_specs=[VMEM] * count,
         out_specs=[VMEM] * (rows // part),
         out_shape=[shape] * (rows // part),
-        cost_estimate=pl.CostEstimate(flops=0, bytes_accessed=rows * depth, transcendentals=0),
+        cost_estimate=SMALL,
         compiler_params=pltpu.CompilerParams(vmem_limit_bytes=2**20),
         name="pack",
     )(*blocks)
@@ -105,9 +107,7 @@
             pltpu.VMEM((2, step, columns), jnp.float32),
             pltpu.SemaphoreType.DMA((2,)),
         ],
-        cost_estimate=pl.CostEstimate(
-            flops=rows * columns, bytes_accessed=4 * rows * columns, transcendentals=0
-        ),
+        cost_estimate=SMALL,
         compiler_params=pltpu.CompilerParams(vmem_limit_bytes=3 * 2**20),
         name="split",
     )(whole)
@@ -164,14 +164,50 @@
         out_specs=[VMEM] * count,
         out_shape=[jax.ShapeDtypeStruct((rows, halves * columns), jnp.float32)] * count,
         scratch_shapes=[pltpu.VMEM((2 * total, depth), jnp.bfloat16)],
-        cost_estimate=pl.CostEstimate(
-            flops=6 * total * depth * halves * columns,
-            bytes_accessed=8 * total * depth,
-            transcendentals=0,
-        ),
+        cost_estimate=SMALL,
         compiler_params=pltpu.CompilerParams(vmem_limit_bytes=8 * total * depth + 3 * 2**20),
         name="product",
     )(place, pattern, block_order, *lefts, *[part for pair in factors for part in pair])
+
+
+def turn_kernel(count, bit, narrow_bit, part, place_ref, *refs):
+    mine, theirs = refs[:count], refs[count : 2 * count]
+    send, kept = refs[2 * count], refs[2 * count + 1 :]
+    same = ((place_ref[0] // bit) & 1) == ((place_ref[2] // narrow_bit) & 1)
+    rows = mine[0].shape[0]
+    size = narrow_bit * part
+
+    def fill(keep, leave):
+        for n in range(count):
+            kept[n][...] = keep[n][...]
+            for m in range(rows // size):
+                source = slice((m ^ 1) * size, ((m ^ 1) + 1) * size)
+                send[n * rows + m * size : n * rows + (m + 1) * size, :] = leave[n][source, :]
+
+    @pl.when(same)
+    def _():
+        fill(mine, theirs)
+
+    @pl.when(jnp.logical_not(same))
+    def _():
+        fill(theirs, mine)
+
+
+def turn(pairs, bit, narrow_bit, part, place):
+    count = len(pairs)
+    rows, width = pairs[0][0].shape
+    kept = jax.ShapeDtypeStruct((rows, width), jnp.float32)
+    send = jax.ShapeDtypeStruct((count * rows, width), jnp.float32)
+    send, *kept = pl.pallas_call(
+        functools.partial(turn_kernel, count, bit, narrow_bit, part),
+        in_specs=[SMEM] + [VMEM] * (2 * count),
+        out_specs=[VMEM] * (1 + count),
+        out_shape=[send] + [kept] * count,
+        cost_estimate=SMALL,
+        compiler_params=pltpu.CompilerParams(vmem_limit_bytes=2**20),
+        name="turn",
+    )(place, *[a for a, _ in pairs], *[b for _, b in pairs])
+    return send, kept
 
 
 def finish_kernel(spec, group, count, part, width, place_ref, bare_ref, occ_ref, virt_ref, *refs):
@@ -198,9 +234,7 @@
         in_specs=[SMEM] + [VMEM] * (3 + 2 * len(pairs)),
         out_specs=VMEM,
         out_shape=jax.ShapeDtypeStruct(bare.shape, bare.dtype),
-        cost_estimate=pl.CostEstimate(
-            flops=5 * bare.size, bytes_accessed=8 * bare.size, transcendentals=0
-        ),
+        cost_estimate=SMALL,
         compiler_params=pltpu.CompilerParams(vmem_limit_bytes=2 * 2**20),
         name="finish",
     )(place, bare, occ[:, None], virt[None, :], *[part_in for pair in pairs for part_in in pair])
@@ -217,14 +251,14 @@
             moved = False
             for resource, busy in uses:
                 for low, high in taken.get(resource, ()):
-                    if low < start + busy - 1e-6 and start < high - 1e-6:
+                    if low < start + busy - SLACK and start < high - 1e-6:
                         start = high
                         moved = True
         for resource, busy in uses:
             taken.setdefault(resource, []).append((start, start + busy))
         done[name] = start + length
         starts[name] = start
-    return sorted(events, key=lambda name: starts[name])
+    return [(starts[name], done[name], name) for name in sorted(events, key=starts.get)]
 
 
 def shards(amplitudes, integrals, bare_terms, pattern, block_order, occ_gap, virt_gap):
@@ -255,11 +289,13 @@
         return lax.ppermute(value, "narrow", [(n, n ^ mask) for n in range(narrow_count)])
 
     last = []
+    landed = []
 
     def ordered(value):
         if last:
-            value = after(value, last[-1])
-        last.append(value)
+            value = after(value, *last, *landed)
+        last[:] = [value]
+        landed.clear()
         return value
 
     swapped = across(integrals, 1)
@@ -325,21 +361,15 @@
 
     def reduce_step(unit, bit, narrow_bit):
         now = state[unit]
-        same = ((chip // bit) & 1) == ((z // narrow_bit) & 1)
         keys = [key for key in now if not key[1] & bit]
         pairs = [(now[r, s], now[r, s | bit]) for r, s in keys]
-        leaving = jnp.concatenate([jnp.where(same, b, a) for a, b in pairs], axis=0)
-        size = narrow_bit * part
-        leaving = jnp.concatenate(
-            [leaving[n * size : (n + 1) * size] for m in range(0, leaving.shape[0] // size, 2) for n in (m + 1, m)],
-            axis=0,
-        )
+        leaving, kept = turn(pairs, bit, narrow_bit, part, place)
         arrived = along(ordered(leaving), narrow_bit)
         state[unit] = {}
-        for n, (key, (a, b)) in enumerate(zip(keys, pairs)):
-            kept = jnp.where(same, a, b)
+        for n, key in enumerate(keys):
             came = arrived[n * rows : (n + 1) * rows]
-            state[unit][key] = (kept, came) if narrow_bit == narrow_bits[-1] else kept + came
+            final = narrow_bit == narrow_bits[-1]
+            state[unit][key] = (kept[n], came) if final else kept[n] + came
 
     events = {}
     actions = {}
@@ -400,8 +430,14 @@
             before = now
             length /= 2.0
 
-    for name in event_order(events):
+    flying = []
+    for start, end, name in event_order(events):
+        for flight in [flight for flight in flying if flight[0] <= start]:
+            flying.remove(flight)
+            landed.extend(part_in for _, part_in in state[flight[1]].values())
         actions[name]()
+        if name[0] == "reduce" and name[2] == narrow_bits[-1]:
+            flying.append((end, name[1]))
 
     spec = [(*UNITS[unit], s) for unit in range(len(UNITS)) for s in range(group)]
     pairs = [state[unit][0, s] for unit in range(len(UNITS)) for s in range(group)]

time: 179 us -> 168 us (0.939)
  waiting for transfers between devices: 93.7 us -> 72.1 us
  Pallas kernels: 28.4 us -> 35.5 us
  starting transfers between devices: 48.3 us -> 53.8 us
    ppermute x23, waiting for transfers between devices: 55.4 us -> 23.2 us  [across(): lax.ppermute(value, 'wide', [(w, w ^ mask) for w in range(wide_count)])]
    ppermute x21, waiting for transfers between devices: 38.3 us -> 48.9 us  [along(): lax.ppermute(value, 'narrow', [(n, n ^ mask) for n in range(narrow_count)])]
    pallas_call x0 -> x12, Pallas kernels: none -> 7.26 us  [turn(): pl.pallas_call(functools.partial(turn_kernel, count, bit, narrow_bit, par...]
    ppermute x21, starting transfers between devices: 28.8 us -> 31.7 us  [along(): lax.ppermute(value, 'narrow', [(n, n ^ mask) for n in range(narrow_count)])]
    ppermute x23, starting transfers between devices: 19.5 us -> 22.1 us  [across(): lax.ppermute(value, 'wide', [(w, w ^ mask) for w in range(wide_count)])]
    unnamed x64 -> x14, local copies, waits for them, and re-layouts: 5.66 us -> 4.64 us
  transfers between devices with their start and end apart: 44 -> 44, of which waited for: 27 -> 20; matrix products, arithmetic and copies ran while one was open for 1% -> 1% of each run, Pallas kernels for 10% -> 20%
where the time goes in v5:
time: 168 us; the launch traced here: 167 us
  waiting for transfers between devices  72.1 us (43%)
  starting transfers between devices  53.8 us (32%)
  Pallas kernels  35.5 us (21%)
  local copies, waits for them, and re-layouts  4.91 us (3%)
    ppermute x21, waiting for transfers between devices, along(): lax.ppermute(value, 'narrow', [(n, n ^ mask) for n in range(narrow_count)])  48.9 us
    ppermute x21, starting transfers between devices, along(): lax.ppermute(value, 'narrow', [(n, n ^ mask) for n in range(narrow_count)])  31.7 us
    ppermute x23, waiting for transfers between devices, across(): lax.ppermute(value, 'wide', [(w, w ^ mask) for w in range(wide_count)])  23.2 us
    ppermute x23, starting transfers between devices, across(): lax.ppermute(value, 'wide', [(w, w ^ mask) for w in range(wide_count)])  22.1 us
    pallas_call x6, Pallas kernels, product(): pl.pallas_call(functools.partial(product_kernel, count, rows, layout, hal...  18.2 us
    pallas_call x2, Pallas kernels, split(): pl.pallas_call(functools.partial(split_kernel, step), in_specs=[ANY], out...  7.55 us
    pallas_call x12, Pallas kernels, turn(): pl.pallas_call(functools.partial(turn_kernel, count, bit, narrow_bit, par...  7.26 us
    unnamed x14, local copies, waits for them, and re-layouts  4.64 us
  transfers between devices with their start and end apart: 44, of which 20 were waited for; matrix products, arithmetic and copies ran while one was open for 1% of the time, Pallas kernels for 20%

profile of v5, /device:TPU:0, one launch (start us, length us, event | category | flops | bytes accessed | tf_op | source)
XLA Modules:
  0.0 167.3 jit_solution(11672095066026579051)
XLA Ops:
  2.4 4.7 %collective-permute-start.2 = (f32[8,2048]{1,0:T(8,128)S(1)}, f32[8,2048]{1,0:T(8,128)S(1)}, u32[]{:S(2)}, u32[]{:S(2)}) collective-permute-start(f32[8,2048]{1,0:T(8,128)S(1)} %get-tuple-element.131), channel_id=1, source_target_pairs={{0,3},{1,2},{2,1},{3,0},{4,7},{5,6},{6,5},{7,4},{8,11},{9,10},{10,... | collective-permute-start | bytes 196616 | tf_op jit(solution)/shard_map/ppermute | solution.py:289
  7.7 2.3 %collective-permute-done.2.refs_3_ = f32[8,2048]{1,0:T(8,128)S(1)} collective-permute-done((f32[8,2048]{1,0:T(8,128)S(1)}, f32[8,2048]{1,0:T(8,128)S(1)}, u32[]{:S(2)}, u32[]{:S(2)}) %collective-permute-start.2) | collective-permute-done | bytes 65568 | tf_op jit(solution)/shard_map/ppermute | solution.py:289
  10.0 3.2 %collective-permute-done.1.refs_2_ = f32[8,2048]{1,0:T(8,128)S(1)} collective-permute-done((f32[8,2048]{1,0:T(8,128)S(1)}, f32[8,2048]{1,0:T(8,128)S(1)}, u32[]{:S(2)}, u32[]{:S(2)}) %collective-permute-start.1) | collective-permute-done | bytes 65568 | tf_op jit(solution)/shard_map/ppermute | solution.py:289
  16.3 2.5 %collective-permute-start.5 = (f32[8,2048]{1,0:T(8,128)S(1)}, f32[8,2048]{1,0:T(8,128)S(1)}, u32[]{:S(2)}, u32[]{:S(2)}) collective-permute-start(f32[8,2048]{1,0:T(8,128)S(1)} %get-tuple-element.138), channel_id=1, source_target_pairs={{0,3},{1,2},{2,1},{3,0},{4,7},{5,6},{6,5},{7,4},{8,11},{9,10},{10,... | collective-permute-start | bytes 196616 | tf_op jit(solution)/shard_map/ppermute | solution.py:289
  19.0 3.4 %collective-permute-done.5.refs_3_ = f32[8,2048]{1,0:T(8,128)S(1)} collective-permute-done((f32[8,2048]{1,0:T(8,128)S(1)}, f32[8,2048]{1,0:T(8,128)S(1)}, u32[]{:S(2)}, u32[]{:S(2)}) %collective-permute-start.5) | collective-permute-done | bytes 65568 | tf_op jit(solution)/shard_map/ppermute | solution.py:289
  22.3 2.2 %collective-permute-start.3 = (f32[8,2048]{1,0:T(8,128)S(1)}, f32[8,2048]{1,0:T(8,128)S(1)}, u32[]{:S(2)}, u32[]{:S(2)}) collective-permute-start(f32[8,2048]{1,0:T(8,128)S(1)} %get-tuple-element.134), channel_id=1, source_target_pairs={{0,1},{1,0},{2,3},{3,2},{4,5},{5,4},{6,7},{7,6},{8,9},{9,8},{10,11... | collective-permute-start | bytes 196616 | tf_op jit(solution)/shard_map/ppermute | solution.py:289
  24.9 1.9 %collective-permute-done.3.refs_1_ = f32[8,2048]{1,0:T(8,128)S(1)} collective-permute-done((f32[8,2048]{1,0:T(8,128)S(1)}, f32[8,2048]{1,0:T(8,128)S(1)}, u32[]{:S(2)}, u32[]{:S(2)}) %collective-permute-start.3) | collective-permute-done | bytes 65568 | tf_op jit(solution)/shard_map/ppermute | solution.py:289
  29.5 2.3 %collective-permute-start.17 = (f32[16,2048]{1,0:T(8,128)S(1)}, f32[16,2048]{1,0:T(8,128)S(1)}, u32[]{:S(2)}, u32[]{:S(2)}) collective-permute-start(f32[16,2048]{1,0:T(8,128)S(1)} %get-tuple-element.145), channel_id=1, source_target_pairs={{0,3},{1,2},{2,1},{3,0},{4,7},{5,6},{6,5},{7,4},{8,11},{9,10},{10,... | collective-permute-start | bytes 393224 | tf_op jit(solution)/shard_map/ppermute | solution.py:289
  31.8 3.4 %copy-done = f32[2048,1024]{1,0:T(8,128)S(1)} copy-done((f32[2048,1024]{1,0:T(8,128)S(1)}, f32[2048,1024]{1,0:T(8,128)}, u32[]{:S(2)}) %copy-start) | copy-done | bytes 8388632
  35.2 1.7 %split.2 = (bf16[2048,1024]{1,0:T(8,128)(2,1)S(1)}, bf16[2048,1024]{1,0:T(8,128)(2,1)S(1)}) custom-call(f32[2048,1024]{1,0:T(8,128)S(1)} %copy-done), custom_call_target="tpu_custom_call" | custom-call | flops 1 | bytes 1 | tf_op jit(solution)/shard_map/split/pallas_call | solution.py:101
  39.1 2.5 %product.6 = (f32[32,1024]{1,0:T(8,128)S(1)}, f32[32,1024]{1,0:T(8,128)S(1)}, f32[32,1024]{1,0:T(8,128)S(1)}, f32[32,1024]{1,0:T(8,128)S(1)}) custom-call(s32[3]{0:T(128)S(1)} %pad_add_fusion.place_ref, s32[8,64]{1,0:T(8,128)S(1)} %copy-done.3, s32[8]{0:T(128)S(1)} %copy-done.4, f32[32,2048]{1,0:T(8,128)S(1)} %pack.3.refs_0_, ...), custom_call_target="tpu_custom_call" | custom-call | flops 1 | bytes 1 | tf_op jit(solution)/shard_map/product/pallas_call | solution.py:161
  42.2 5.8 %split.3 = (bf16[2048,1024]{1,0:T(8,128)(2,1)S(1)}, bf16[2048,1024]{1,0:T(8,128)(2,1)S(1)}) custom-call(f32[2048,1024]{1,0:T(8,128)} %collective-permute-done.12.whole_ref), custom_call_target="tpu_custom_call" | custom-call | flops 1 | bytes 1 | tf_op jit(solution)/shard_map/split/pallas_call | solution.py:101
  48.1 2.5 %product.7 = (f32[32,1024]{1,0:T(8,128)S(1)}, f32[32,1024]{1,0:T(8,128)S(1)}, f32[32,1024]{1,0:T(8,128)S(1)}, f32[32,1024]{1,0:T(8,128)S(1)}) custom-call(s32[3]{0:T(128)S(1)} %pad_add_fusion.place_ref, s32[8,64]{1,0:T(8,128)S(1)} %copy-done.3, s32[8]{0:T(128)S(1)} %copy-done.4, f32[32,2048]{1,0:T(8,128)S(1)} %pack.3.refs_0_, ...), custom_call_target="tpu_custom_call" | custom-call | flops 1 | bytes 1 | tf_op jit(solution)/shard_map/product/pallas_call | solution.py:161
  58.8 2.1 %collective-permute-done.13 = f32[64,1024]{1,0:T(8,128)S(1)} collective-permute-done((f32[64,1024]{1,0:T(8,128)S(1)}, f32[64,1024]{1,0:T(8,128)S(1)}, u32[]{:S(2)}, u32[]{:S(2)}) %collective-permute-start.13) | collective-permute-done | bytes 262176 | tf_op jit(solution)/shard_map/ppermute | solution.py:289
  63.2 4.1 %product.8 = (f32[32,2048]{1,0:T(8,128)S(1)}, f32[32,2048]{1,0:T(8,128)S(1)}, f32[32,2048]{1,0:T(8,128)S(1)}, f32[32,2048]{1,0:T(8,128)S(1)}) custom-call(s32[3]{0:T(128)S(1)} %pad_add_fusion.place_ref, s32[8,64]{1,0:T(8,128)S(1)} %copy-done.3, s32[8]{0:T(128)S(1)} %copy-done.4, f32[32,2048]{1,0:T(8,128)S(1)} %pack.4.refs_0_, ...), custom_call_target="tpu_custom_call" | custom-call | flops 1 | bytes 1 | tf_op jit(solution)/shard_map/product/pallas_call | solution.py:161
  72.3 11.0 %collective-permute-done.23.refs_1_ = f32[32,2048]{1,0:T(8,128)S(1)} collective-permute-done((f32[32,2048]{1,0:T(8,128)S(1)}, f32[32,2048]{1,0:T(8,128)S(1)}, u32[]{:S(2)}, u32[]{:S(2)}) %collective-permute-start.23) | collective-permute-done | bytes 262176 | tf_op jit(solution)/shard_map/ppermute | solution.py:283
  87.5 4.2 %collective-permute-done.20.refs_1_ = f32[32,1024]{1,0:T(8,128)S(1)} collective-permute-done((f32[32,1024]{1,0:T(8,128)S(1)}, f32[32,1024]{1,0:T(8,128)S(1)}, u32[]{:S(2)}, u32[]{:S(2)}) %collective-permute-start.20) | collective-permute-done | bytes 131104 | tf_op jit(solution)/shard_map/ppermute | solution.py:289
  91.7 1.9 %collective-permute-start.24 = (f32[32,1024]{1,0:T(8,128)S(1)}, f32[32,1024]{1,0:T(8,128)S(1)}, u32[]{:S(2)}, u32[]{:S(2)}) collective-permute-start(f32[32,1024]{1,0:T(8,128)S(1)} %get-tuple-element.193), channel_id=1, source_target_pairs={{0,2},{1,3},{2,0},{3,1},{4,6},{5,7},{6,4},{7,5},{8,10},{9,11},{10,... | collective-permute-start | bytes 393224 | tf_op jit(solution)/shard_map/ppermute | solution.py:289
  93.7 6.1 %collective-permute-done.24.refs_3_ = f32[32,1024]{1,0:T(8,128)S(1)} collective-permute-done((f32[32,1024]{1,0:T(8,128)S(1)}, f32[32,1024]{1,0:T(8,128)S(1)}, u32[]{:S(2)}, u32[]{:S(2)}) %collective-permute-start.24) | collective-permute-done | bytes 131104 | tf_op jit(solution)/shard_map/ppermute | solution.py:289
  101.3 4.1 %product.9 = (f32[32,2048]{1,0:T(8,128)S(1)}, f32[32,2048]{1,0:T(8,128)S(1)}, f32[32,2048]{1,0:T(8,128)S(1)}, f32[32,2048]{1,0:T(8,128)S(1)}) custom-call(s32[3]{0:T(128)S(1)} %pad_add_fusion.place_ref, s32[8,64]{1,0:T(8,128)S(1)} %copy-done.3, s32[8]{0:T(128)S(1)} %copy-done.4, f32[32,2048]{1,0:T(8,128)S(1)} %get-tuple-element.201.refs_0_, ...), custom_call_target="tpu_custom_call" | custom-call | flops 1 | bytes 1 | tf_op jit(solution)/shard_map/product/pallas_call | solution.py:161
  106.7 2.3 %collective-permute-done.30.refs_2_ = f32[64,2048]{1,0:T(8,128)S(1)} collective-permute-done((f32[64,2048]{1,0:T(8,128)S(1)}, f32[64,2048]{1,0:T(8,128)S(1)}, u32[]{:S(2)}, u32[]{:S(2)}) %collective-permute-start.30) | collective-permute-done | bytes 524320 | tf_op jit(solution)/shard_map/ppermute | solution.py:283
  109.0 2.5 %product.10 = (f32[32,1024]{1,0:T(8,128)S(1)}, f32[32,1024]{1,0:T(8,128)S(1)}, f32[32,1024]{1,0:T(8,128)S(1)}, f32[32,1024]{1,0:T(8,128)S(1)}) custom-call(s32[3]{0:T(128)S(1)} %pad_add_fusion.place_ref, s32[8,64]{1,0:T(8,128)S(1)} %copy-done.3, s32[8]{0:T(128)S(1)} %copy-done.4, f32[32,2048]{1,0:T(8,128)S(1)} %get-tuple-element.211.refs_0_, ...), custom_call_target="tpu_custom_call" | custom-call | flops 1 | bytes 1 | tf_op jit(solution)/shard_map/product/pallas_call | solution.py:161
  112.0 5.6 %collective-permute-done.32 = f32[64,2048]{1,0:T(8,128)S(1)} collective-permute-done((f32[64,2048]{1,0:T(8,128)S(1)}, f32[64,2048]{1,0:T(8,128)S(1)}, u32[]{:S(2)}, u32[]{:S(2)}) %collective-permute-start.32) | collective-permute-done | bytes 524320 | tf_op jit(solution)/shard_map/ppermute | solution.py:283
  118.2 2.5 %product.11 = (f32[32,1024]{1,0:T(8,128)S(1)}, f32[32,1024]{1,0:T(8,128)S(1)}, f32[32,1024]{1,0:T(8,128)S(1)}, f32[32,1024]{1,0:T(8,128)S(1)}) custom-call(s32[3]{0:T(128)S(1)} %pad_add_fusion.place_ref, s32[8,64]{1,0:T(8,128)S(1)} %copy-done.3, s32[8]{0:T(128)S(1)} %copy-done.4, f32[32,2048]{1,0:T(8,128)S(1)} %get-tuple-element.211.refs_0_, ...), custom_call_target="tpu_custom_call" | custom-call | flops 1 | bytes 1 | tf_op jit(solution)/shard_map/product/pallas_call | solution.py:161
  121.4 2.5 %collective-permute-start.33 = (f32[64,2048]{1,0:T(8,128)S(1)}, f32[64,2048]{1,0:T(8,128)S(1)}, u32[]{:S(2)}, u32[]{:S(2)}) collective-permute-start(f32[64,2048]{1,0:T(8,128)S(1)} %get-tuple-element.221), channel_id=1, source_target_pairs={{0,1},{1,0},{2,3},{3,2},{4,5},{5,4},{6,7},{7,6},{8,9},{9,8},{10,11... | collective-permute-start | bytes 1572872 | tf_op jit(solution)/shard_map/ppermute | solution.py:289
  126.1 14.8 %collective-permute-done.31.refs_5_ = f32[32,2048]{1,0:T(8,128)S(1)} collective-permute-done((f32[32,2048]{1,0:T(8,128)S(1)}, f32[32,2048]{1,0:T(8,128)S(1)}, u32[]{:S(2)}, u32[]{:S(2)}) %collective-permute-start.31) | collective-permute-done | bytes 262176 | tf_op jit(solution)/shard_map/ppermute | solution.py:289
  143.8 3.5 %collective-permute-done.36 = f32[64,1024]{1,0:T(8,128)S(1)} collective-permute-done((f32[64,1024]{1,0:T(8,128)S(1)}, f32[64,1024]{1,0:T(8,128)S(1)}, u32[]{:S(2)}, u32[]{:S(2)}) %collective-permute-start.36) | collective-permute-done | bytes 262176 | tf_op jit(solution)/shard_map/ppermute | solution.py:289
  149.1 3.4 %collective-permute-start.38 = (f32[32,2048]{1,0:T(8,128)S(1)}, f32[32,2048]{1,0:T(8,128)S(1)}, u32[]{:S(2)}, u32[]{:S(2)}) collective-permute-start(f32[32,2048]{1,0:T(8,128)S(1)} %get-tuple-element.236), channel_id=1, source_target_pairs={{0,2},{1,3},{2,0},{3,1},{4,6},{5,7},{6,4},{7,5},{8,10},{9,11},{10,... | collective-permute-start | bytes 786440 | tf_op jit(solution)/shard_map/ppermute | solution.py:289
  154.1 2.2 %collective-permute-start.41 = (f32[32,1024]{1,0:T(8,128)S(1)}, f32[32,1024]{1,0:T(8,128)S(1)}, u32[]{:S(2)}, u32[]{:S(2)}) collective-permute-start(f32[32,1024]{1,0:T(8,128)S(1)} %get-tuple-element.242), channel_id=1, source_target_pairs={{0,2},{1,3},{2,0},{3,1},{4,6},{5,7},{6,4},{7,5},{8,10},{9,11},{10,... | collective-permute-start | bytes 393224 | tf_op jit(solution)/shard_map/ppermute | solution.py:289
  160.0 2.5 %collective-permute-done.41.refs_9_ = f32[32,1024]{1,0:T(8,128)S(1)} collective-permute-done((f32[32,1024]{1,0:T(8,128)S(1)}, f32[32,1024]{1,0:T(8,128)S(1)}, u32[]{:S(2)}, u32[]{:S(2)}) %collective-permute-start.41) | collective-permute-done | bytes 131104 | tf_op jit(solution)/shard_map/ppermute | solution.py:289
  162.5 3.1 %collective-permute-done.43.refs_11_ = f32[32,1024]{1,0:T(8,128)S(1)} collective-permute-done((f32[32,1024]{1,0:T(8,128)S(1)}, f32[32,1024]{1,0:T(8,128)S(1)}, u32[]{:S(2)}, u32[]{:S(2)}) %collective-permute-start.43) | collective-permute-done | bytes 131104 | tf_op jit(solution)/shard_map/ppermute | solution.py:289
  165.5 1.8 %finish.1 = f32[128,2048]{1,0:T(8,128)} custom-call(s32[3]{0:T(128)S(1)} %pad_add_fusion.place_ref, f32[128,2048]{1,0:T(8,128)S(1)} %copy-done.1, f32[128,1]{1,0:T(8,128)S(1)} %copy.8.occ_ref, f32[1,2048]{1,0:T(1,128)S(1)} %bitcast.5, f32[32,1024]{1,0:T(8,128)S(1)} %get-tuple-element.178.refs_0_, f32[32,1024]{1,0:T(8,128)S(1)} %collective-permute-done.20.refs_1_, ...), custom_call_target="tpu_custom_call" | custom-call | flops 1 | bytes 1 | tf_op jit(solution)/shard_map/finish/pallas_call | solution.py:232
  (120 shorter events, 48.3 us)
Async XLA Ops:
  0.0 42.2 %collective-permute-start.12 = (f32[2048,1024]{1,0:T(8,128)}, f32[2048,1024]{1,0:T(8,128)}, u32[]{:S(2)}, u32[]{:S(2)}) collective-permute-start(f32[2048,1024]{1,0:T(8,128)} %whole_ref.2), channel_id=1, source_target_pairs={{0,4},{4,0},{8,12},{12,8},{16,20},{20,16},{24,28},{28,24},{1,5},{5... | collective-permute-start | bytes 25165832 | tf_op jit(solution)/shard_map/ppermute | solution.py:283
  2.4 7.6 %collective-permute-start.2 = (f32[8,2048]{1,0:T(8,128)S(1)}, f32[8,2048]{1,0:T(8,128)S(1)}, u32[]{:S(2)}, u32[]{:S(2)}) collective-permute-start(f32[8,2048]{1,0:T(8,128)S(1)} %get-tuple-element.131), channel_id=1, source_target_pairs={{0,3},{1,2},{2,1},{3,0},{4,7},{5,6},{6,5},{7,4},{8,11},{9,10},{10,... | collective-permute-start | bytes 196616 | tf_op jit(solution)/shard_map/ppermute | solution.py:289
  13.2 13.6 %collective-permute-start.7 = (f32[32,2048]{1,0:T(8,128)S(1)}, f32[32,2048]{1,0:T(8,128)S(1)}, u32[]{:S(2)}, u32[]{:S(2)}) collective-permute-start(f32[32,2048]{1,0:T(8,128)S(1)} %pack.3.refs_0_), channel_id=1, source_target_pairs={{0,8},{4,12},{8,0},{12,4},{16,24},{20,28},{24,16},{28,20},{1,9},{5... | collective-permute-start | bytes 786440 | tf_op jit(solution)/shard_map/ppermute | solution.py:283
  14.8 12.1 %collective-permute-start.6 = (f32[32,2048]{1,0:T(8,128)S(1)}, f32[32,2048]{1,0:T(8,128)S(1)}, u32[]{:S(2)}, u32[]{:S(2)}) collective-permute-start(f32[32,2048]{1,0:T(8,128)S(1)} %pack.3.refs_0_), channel_id=1, source_target_pairs={{0,16},{4,20},{8,24},{12,28},{16,0},{20,4},{24,8},{28,12},{1,17},{... | collective-permute-start | bytes 786440 | tf_op jit(solution)/shard_map/ppermute | solution.py:283
  26.9 14.7 %collective-permute-start.11 = (f32[32,2048]{1,0:T(8,128)S(1)}, f32[32,2048]{1,0:T(8,128)S(1)}, u32[]{:S(2)}, u32[]{:S(2)}) collective-permute-start(f32[32,2048]{1,0:T(8,128)S(1)} %pack.4.refs_0_), channel_id=1, source_target_pairs={{0,8},{4,12},{8,0},{12,4},{16,24},{20,28},{24,16},{28,20},{1,9},{5... | collective-permute-start | bytes 786440 | tf_op jit(solution)/shard_map/ppermute | solution.py:283
  27.5 9.4 %collective-permute-start.9 = (f32[16,2048]{1,0:T(8,128)S(1)}, f32[16,2048]{1,0:T(8,128)S(1)}, u32[]{:S(2)}, u32[]{:S(2)}) collective-permute-start(f32[16,2048]{1,0:T(8,128)S(1)} %slice.104), channel_id=1, source_target_pairs={{0,8},{4,12},{8,0},{12,4},{16,24},{20,28},{24,16},{28,20},{1,9},{5... | collective-permute-start | bytes 393224 | tf_op jit(solution)/shard_map/ppermute | solution.py:283
  29.0 9.2 %collective-permute-start.8 = (f32[16,2048]{1,0:T(8,128)S(1)}, f32[16,2048]{1,0:T(8,128)S(1)}, u32[]{:S(2)}, u32[]{:S(2)}) collective-permute-start(f32[16,2048]{1,0:T(8,128)S(1)} %slice.105), channel_id=1, source_target_pairs={{0,16},{4,20},{8,24},{12,28},{16,0},{20,4},{24,8},{28,12},{1,17},{... | collective-permute-start | bytes 393224 | tf_op jit(solution)/shard_map/ppermute | solution.py:283
  29.5 24.8 %collective-permute-start.17 = (f32[16,2048]{1,0:T(8,128)S(1)}, f32[16,2048]{1,0:T(8,128)S(1)}, u32[]{:S(2)}, u32[]{:S(2)}) collective-permute-start(f32[16,2048]{1,0:T(8,128)S(1)} %get-tuple-element.145), channel_id=1, source_target_pairs={{0,3},{1,2},{2,1},{3,0},{4,7},{5,6},{6,5},{7,4},{8,11},{9,10},{10,... | collective-permute-start | bytes 393224 | tf_op jit(solution)/shard_map/ppermute | solution.py:289
  36.9 18.6 %collective-permute-start.16 = (f32[16,2048]{1,0:T(8,128)S(1)}, f32[16,2048]{1,0:T(8,128)S(1)}, u32[]{:S(2)}, u32[]{:S(2)}) collective-permute-start(f32[16,2048]{1,0:T(8,128)S(1)} %get-tuple-element.144), channel_id=1, source_target_pairs={{0,2},{1,3},{2,0},{3,1},{4,6},{5,7},{6,4},{7,5},{8,10},{9,11},{10,... | collective-permute-start | bytes 393224 | tf_op jit(solution)/shard_map/ppermute | solution.py:289
  38.2 17.3 %collective-permute-start.15 = (f32[16,2048]{1,0:T(8,128)S(1)}, f32[16,2048]{1,0:T(8,128)S(1)}, u32[]{:S(2)}, u32[]{:S(2)}) collective-permute-start(f32[16,2048]{1,0:T(8,128)S(1)} %get-tuple-element.143), channel_id=1, source_target_pairs={{0,1},{1,0},{2,3},{3,2},{4,5},{5,4},{6,7},{7,6},{8,9},{9,8},{10,11... | collective-permute-start | bytes 393224 | tf_op jit(solution)/shard_map/ppermute | solution.py:289
  41.6 10.6 %collective-permute-start.10 = (f32[64,1024]{1,0:T(8,128)S(1)}, f32[64,1024]{1,0:T(8,128)S(1)}, u32[]{:S(2)}, u32[]{:S(2)}) collective-permute-start(f32[64,1024]{1,0:T(8,128)S(1)} %pad_maximum_fusion.5), channel_id=1, source_target_pairs={{0,8},{4,12},{8,0},{12,4},{16,24},{20,28},{24,16},{28,20},{1,9},{5... | collective-permute-start | bytes 786440 | tf_op jit(solution)/shard_map/ppermute | solution.py:283
  52.2 11.1 %collective-permute-start.19 = (f32[64,2048]{1,0:T(8,128)S(1)}, f32[64,2048]{1,0:T(8,128)S(1)}, u32[]{:S(2)}, u32[]{:S(2)}) collective-permute-start(f32[64,2048]{1,0:T(8,128)S(1)} %pad_maximum_fusion), channel_id=1, source_target_pairs={{0,16},{4,20},{8,24},{12,28},{16,0},{20,4},{24,8},{28,12},{1,17},{... | collective-permute-start | bytes 1572872 | tf_op jit(solution)/shard_map/ppermute | solution.py:283
  57.6 13.2 %collective-permute-start.21 = (f32[64,1024]{1,0:T(8,128)S(1)}, f32[64,1024]{1,0:T(8,128)S(1)}, u32[]{:S(2)}, u32[]{:S(2)}) collective-permute-start(f32[64,1024]{1,0:T(8,128)S(1)} %get-tuple-element.176), channel_id=1, source_target_pairs={{0,1},{1,0},{2,3},{3,2},{4,5},{5,4},{6,7},{7,6},{8,9},{9,8},{10,11... | collective-permute-start | bytes 786440 | tf_op jit(solution)/shard_map/ppermute | solution.py:289
  61.0 9.3 %collective-permute-start.18 = (f32[32,1024]{1,0:T(8,128)S(1)}, f32[32,1024]{1,0:T(8,128)S(1)}, u32[]{:S(2)}, u32[]{:S(2)}) collective-permute-start(f32[32,1024]{1,0:T(8,128)S(1)} %get-tuple-element.177), channel_id=1, source_target_pairs={{0,16},{4,20},{8,24},{12,28},{16,0},{20,4},{24,8},{28,12},{1,17},{... | collective-permute-start | bytes 393224 | tf_op jit(solution)/shard_map/ppermute | solution.py:283
  67.4 19.2 %collective-permute-start.25 = (f32[64,2048]{1,0:T(8,128)S(1)}, f32[64,2048]{1,0:T(8,128)S(1)}, u32[]{:S(2)}, u32[]{:S(2)}) collective-permute-start(f32[64,2048]{1,0:T(8,128)S(1)} %pad_maximum_fusion.1), channel_id=1, source_target_pairs={{0,8},{4,12},{8,0},{12,4},{16,24},{20,28},{24,16},{28,20},{1,9},{5... | collective-permute-start | bytes 1572872 | tf_op jit(solution)/shard_map/ppermute | solution.py:283
  68.2 15.0 %collective-permute-start.23 = (f32[32,2048]{1,0:T(8,128)S(1)}, f32[32,2048]{1,0:T(8,128)S(1)}, u32[]{:S(2)}, u32[]{:S(2)}) collective-permute-start(f32[32,2048]{1,0:T(8,128)S(1)} %get-tuple-element.201.refs_0_), channel_id=1, source_target_pairs={{0,8},{4,12},{8,0},{12,4},{16,24},{20,28},{24,16},{28,20},{1,9},{5... | collective-permute-start | bytes 786440 | tf_op jit(solution)/shard_map/ppermute | solution.py:283
  69.5 24.1 %collective-permute-start.27 = (f32[32,2048]{1,0:T(8,128)S(1)}, f32[32,2048]{1,0:T(8,128)S(1)}, u32[]{:S(2)}, u32[]{:S(2)}) collective-permute-start(f32[32,2048]{1,0:T(8,128)S(1)} %get-tuple-element.211.refs_0_), channel_id=1, source_target_pairs={{0,8},{4,12},{8,0},{12,4},{16,24},{20,28},{24,16},{28,20},{1,9},{5... | collective-permute-start | bytes 786440 | tf_op jit(solution)/shard_map/ppermute | solution.py:283
  70.9 15.1 %collective-permute-start.22 = (f32[32,1024]{1,0:T(8,128)S(1)}, f32[32,1024]{1,0:T(8,128)S(1)}, u32[]{:S(2)}, u32[]{:S(2)}) collective-permute-start(f32[32,1024]{1,0:T(8,128)S(1)} %get-tuple-element.189), channel_id=1, source_target_pairs={{0,16},{4,20},{8,24},{12,28},{16,0},{20,4},{24,8},{28,12},{1,17},{... | collective-permute-start | bytes 393224 | tf_op jit(solution)/shard_map/ppermute | solution.py:283
  83.3 8.4 %collective-permute-start.20 = (f32[32,1024]{1,0:T(8,128)S(1)}, f32[32,1024]{1,0:T(8,128)S(1)}, u32[]{:S(2)}, u32[]{:S(2)}) collective-permute-start(f32[32,1024]{1,0:T(8,128)S(1)} %get-tuple-element.186), channel_id=1, source_target_pairs={{0,2},{1,3},{2,0},{3,1},{4,6},{5,7},{6,4},{7,5},{8,10},{9,11},{10,... | collective-permute-start | bytes 393224 | tf_op jit(solution)/shard_map/ppermute | solution.py:289
  84.5 16.8 %collective-permute-start.28 = (f32[64,2048]{1,0:T(8,128)S(1)}, f32[64,2048]{1,0:T(8,128)S(1)}, u32[]{:S(2)}, u32[]{:S(2)}) collective-permute-start(f32[64,2048]{1,0:T(8,128)S(1)} %pad_maximum_fusion.2), channel_id=1, source_target_pairs={{0,16},{4,20},{8,24},{12,28},{16,0},{20,4},{24,8},{28,12},{1,17},{... | collective-permute-start | bytes 1572872 | tf_op jit(solution)/shard_map/ppermute | solution.py:283
  91.7 14.4 %collective-permute-start.26 = (f32[64,2048]{1,0:T(8,128)S(1)}, f32[64,2048]{1,0:T(8,128)S(1)}, u32[]{:S(2)}, u32[]{:S(2)}) collective-permute-start(f32[64,2048]{1,0:T(8,128)S(1)} %get-tuple-element.198), channel_id=1, source_target_pairs={{0,1},{1,0},{2,3},{3,2},{4,5},{5,4},{6,7},{7,6},{8,9},{9,8},{10,11... | collective-permute-start | bytes 1572872 | tf_op jit(solution)/shard_map/ppermute | solution.py:289
  91.7 8.1 %collective-permute-start.24 = (f32[32,1024]{1,0:T(8,128)S(1)}, f32[32,1024]{1,0:T(8,128)S(1)}, u32[]{:S(2)}, u32[]{:S(2)}) collective-permute-start(f32[32,1024]{1,0:T(8,128)S(1)} %get-tuple-element.193), channel_id=1, source_target_pairs={{0,2},{1,3},{2,0},{3,1},{4,6},{5,7},{6,4},{7,5},{8,10},{9,11},{10,... | collective-permute-start | bytes 393224 | tf_op jit(solution)/shard_map/ppermute | solution.py:289
  99.8 9.2 %collective-permute-start.30 = (f32[64,2048]{1,0:T(8,128)S(1)}, f32[64,2048]{1,0:T(8,128)S(1)}, u32[]{:S(2)}, u32[]{:S(2)}) collective-permute-start(f32[64,2048]{1,0:T(8,128)S(1)} %pad_maximum_fusion.3), channel_id=1, source_target_pairs={{0,16},{4,20},{8,24},{12,28},{16,0},{20,4},{24,8},{28,12},{1,17},{... | collective-permute-start | bytes 1572872 | tf_op jit(solution)/shard_map/ppermute | solution.py:283
  105.5 12.1 %collective-permute-start.32 = (f32[64,2048]{1,0:T(8,128)S(1)}, f32[64,2048]{1,0:T(8,128)S(1)}, u32[]{:S(2)}, u32[]{:S(2)}) collective-permute-start(f32[64,2048]{1,0:T(8,128)S(1)} %pad_maximum_fusion.4), channel_id=1, source_target_pairs={{0,8},{4,12},{8,0},{12,4},{16,24},{20,28},{24,16},{28,20},{1,9},{5... | collective-permute-start | bytes 1572872 | tf_op jit(solution)/shard_map/ppermute | solution.py:283
  106.2 14.6 %collective-permute-start.29 = (f32[32,2048]{1,0:T(8,128)S(1)}, f32[32,2048]{1,0:T(8,128)S(1)}, u32[]{:S(2)}, u32[]{:S(2)}) collective-permute-start(f32[32,2048]{1,0:T(8,128)S(1)} %get-tuple-element.205), channel_id=1, source_target_pairs={{0,16},{4,20},{8,24},{12,28},{16,0},{20,4},{24,8},{28,12},{1,17},{... | collective-permute-start | bytes 786440 | tf_op jit(solution)/shard_map/ppermute | solution.py:283
  111.5 14.0 %collective-permute-start.34 = (f32[64,1024]{1,0:T(8,128)S(1)}, f32[64,1024]{1,0:T(8,128)S(1)}, u32[]{:S(2)}, u32[]{:S(2)}) collective-permute-start(f32[64,1024]{1,0:T(8,128)S(1)} %pad_maximum_fusion.7), channel_id=1, source_target_pairs={{0,8},{4,12},{8,0},{12,4},{16,24},{20,28},{24,16},{28,20},{1,9},{5... | collective-permute-start | bytes 786440 | tf_op jit(solution)/shard_map/ppermute | solution.py:283
  121.4 20.5 %collective-permute-start.33 = (f32[64,2048]{1,0:T(8,128)S(1)}, f32[64,2048]{1,0:T(8,128)S(1)}, u32[]{:S(2)}, u32[]{:S(2)}) collective-permute-start(f32[64,2048]{1,0:T(8,128)S(1)} %get-tuple-element.221), channel_id=1, source_target_pairs={{0,1},{1,0},{2,3},{3,2},{4,5},{5,4},{6,7},{7,6},{8,9},{9,8},{10,11... | collective-permute-start | bytes 1572872 | tf_op jit(solution)/shard_map/ppermute | solution.py:289
  123.9 17.1 %collective-permute-start.31 = (f32[32,2048]{1,0:T(8,128)S(1)}, f32[32,2048]{1,0:T(8,128)S(1)}, u32[]{:S(2)}, u32[]{:S(2)}) collective-permute-start(f32[32,2048]{1,0:T(8,128)S(1)} %get-tuple-element.213), channel_id=1, source_target_pairs={{0,2},{1,3},{2,0},{3,1},{4,6},{5,7},{6,4},{7,5},{8,10},{9,11},{10,... | collective-permute-start | bytes 786440 | tf_op jit(solution)/shard_map/ppermute | solution.py:289
  124.9 17.0 %collective-permute-start.37 = (f32[64,1024]{1,0:T(8,128)S(1)}, f32[64,1024]{1,0:T(8,128)S(1)}, u32[]{:S(2)}, u32[]{:S(2)}) collective-permute-start(f32[64,1024]{1,0:T(8,128)S(1)} %pad_maximum_fusion.8), channel_id=1, source_target_pairs={{0,8},{4,12},{8,0},{12,4},{16,24},{20,28},{24,16},{28,20},{1,9},{5... | collective-permute-start | bytes 786440 | tf_op jit(solution)/shard_map/ppermute | solution.py:283
  142.7 9.8 %collective-permute-start.40 = (f32[64,1024]{1,0:T(8,128)S(1)}, f32[64,1024]{1,0:T(8,128)S(1)}, u32[]{:S(2)}, u32[]{:S(2)}) collective-permute-start(f32[64,1024]{1,0:T(8,128)S(1)} %get-tuple-element.234), channel_id=1, source_target_pairs={{0,1},{1,0},{2,3},{3,2},{4,5},{5,4},{6,7},{7,6},{8,9},{9,8},{10,11... | collective-permute-start | bytes 786440 | tf_op jit(solution)/shard_map/ppermute | solution.py:289
  149.1 10.6 %collective-permute-start.38 = (f32[32,2048]{1,0:T(8,128)S(1)}, f32[32,2048]{1,0:T(8,128)S(1)}, u32[]{:S(2)}, u32[]{:S(2)}) collective-permute-start(f32[32,2048]{1,0:T(8,128)S(1)} %get-tuple-element.236), channel_id=1, source_target_pairs={{0,2},{1,3},{2,0},{3,1},{4,6},{5,7},{6,4},{7,5},{8,10},{9,11},{10,... | collective-permute-start | bytes 786440 | tf_op jit(solution)/shard_map/ppermute | solution.py:289
  154.1 8.4 %collective-permute-start.41 = (f32[32,1024]{1,0:T(8,128)S(1)}, f32[32,1024]{1,0:T(8,128)S(1)}, u32[]{:S(2)}, u32[]{:S(2)}) collective-permute-start(f32[32,1024]{1,0:T(8,128)S(1)} %get-tuple-element.242), channel_id=1, source_target_pairs={{0,2},{1,3},{2,0},{3,1},{4,6},{5,7},{6,4},{7,5},{8,10},{9,11},{10,... | collective-permute-start | bytes 393224 | tf_op jit(solution)/shard_map/ppermute | solution.py:289
  (19 other events, 229.5 us)

commit v6 on v4

v6 whole, which is shorter than its diff:
```python
import functools

import jax
import jax.numpy as jnp
from jax import lax
from jax.experimental import pallas as pl
from jax.experimental.pallas import tpu as pltpu
from jax.sharding import PartitionSpec as P

TILE = 128
CHUNKS = 4
CORES = 2
GROUPS = ((0,), (1,), (2, 3))
UNITS = tuple((chunk, (half,)) for chunk in range(CHUNKS) for half in range(CORES))

SMEM = pl.BlockSpec(memory_space=pltpu.SMEM)
VMEM = pl.BlockSpec(memory_space=pltpu.VMEM)
ANY = pl.BlockSpec(memory_space=pl.ANY)
SMALL = pl.CostEstimate(flops=1, bytes_accessed=1, transcendentals=0)


def after(value, *others):
    return lax.optimization_barrier((value, *others))[0]


def cut_kernel(count, bounds, place_ref, whole_ref, *outs):
    z = place_ref[2]
    depth = outs[0].shape[1]
    for g, (low, high) in enumerate(bounds):
        for m in range(count):
            start = pl.multiple_of((z ^ m) * depth, depth)
            outs[g * count + m][...] = whole_ref[low:high, pl.ds(start, depth)]


def cut(whole, count, depth, part, place):
    bounds = [(group[0] * part, (group[-1] + 1) * part) for group in GROUPS]
    shapes = [
        jax.ShapeDtypeStruct((high - low, depth), whole.dtype)
        for low, high in bounds
        for _ in range(count)
    ]
    outs = pl.pallas_call(
        functools.partial(cut_kernel, count, bounds),
        in_specs=[SMEM, VMEM],
        out_specs=[VMEM] * len(shapes),
        out_shape=shapes,
        cost_estimate=SMALL,
        compiler_params=pltpu.CompilerParams(vmem_limit_bytes=2**20),
        name="cut",
    )(place, whole)
    return [outs[g * count : (g + 1) * count] for g in range(len(bounds))]


def pack_kernel(count, part, place_ref, *refs):
    z = place_ref[2]
    for c, out in enumerate(refs[count:]):
        for m in range(count):
            rows = pl.ds(pl.multiple_of((z ^ m) * part, part), part)
            out[rows, :] = refs[m][c * part : (c + 1) * part, :]


def pack(blocks, part, place):
    count = len(blocks)
    rows, depth = blocks[0].shape
    shape = jax.ShapeDtypeStruct((count * part, depth), blocks[0].dtype)
    return pl.pallas_call(
        functools.partial(pack_kernel, count, part),
        in_specs=[SMEM] + [VMEM] * count,
        out_specs=[VMEM] * (rows // part),
        out_shape=[shape] * (rows // part),
        cost_estimate=SMALL,
        compiler_params=pltpu.CompilerParams(vmem_limit_bytes=2**20),
        name="pack",
    )(place, *blocks)


def split_kernel(step, whole_ref, high_ref, low_ref, buffer, sems):
    count = whole_ref.shape[0] // step

    def copy(i):
        return pltpu.make_async_copy(
            whole_ref.at[pl.ds(i * step, step)], buffer.at[i % 2], sems.at[i % 2]
        )

    copy(0).start()
    for i in range(count):
        if i + 1 < count:
            copy(i + 1).start()
        copy(i).wait()
        whole = buffer[i % 2]
        high = whole.astype(jnp.bfloat16)
        here = slice(i * step, (i + 1) * step)
        high_ref[here, :] = high
        low_ref[here, :] = (whole - high.astype(jnp.float32)).astype(jnp.bfloat16)


def split(whole):
    rows, columns = whole.shape
    step = min(256, rows)
    half = jax.ShapeDtypeStruct((rows, columns), jnp.bfloat16)
    return pl.pallas_call(
        functools.partial(split_kernel, step),
        in_specs=[ANY],
        out_specs=[VMEM, VMEM],
        out_shape=[half, half],
        scratch_shapes=[
            pltpu.VMEM((2, step, columns), jnp.float32),
            pltpu.SemaphoreType.DMA((2,)),
        ],
        cost_estimate=SMALL,
        compiler_params=pltpu.CompilerParams(vmem_limit_bytes=3 * 2**20),
        name="split",
    )(whole)


def product_kernel(count, rows, layout, targets, halves, place_ref, pattern_ref, order_ref, *refs):
    lefts = refs[: len(layout)]
    factors = refs[len(layout) : len(layout) + 2 * halves]
    outs = refs[len(layout) + 2 * halves : -1]
    left = refs[-1]
    depth = lefts[0].shape[1]
    total = count * rows
    chip, core, z = place_ref[0], place_ref[1], place_ref[2]
    tiles = depth // TILE
    for held, pieces in zip(lefts, layout):
        start = 0
        for k, first, size in pieces:
            kind = order_ref[(chip ^ k) * CORES + core]
            high_rows = slice(k * rows + first, k * rows + first + size)
            low_rows = slice(total + k * rows + first, total + k * rows + first + size)
            for t in range(tiles):
                kept = pattern_ref[kind, z * tiles + t].astype(jnp.float32)
                here = slice(t * TILE, (t + 1) * TILE)
                value = held[start : start + size, here] * kept
                high = value.astype(jnp.bfloat16)
                left[high_rows, here] = high
                left[low_rows, here] = (value - high.astype(jnp.float32)).astype(jnp.bfloat16)
            start += size
    columns = factors[0].shape[1]
    width = min(512, columns)
    for half in range(halves):
        high_ref, low_ref = factors[2 * half : 2 * half + 2]
        for j in range(columns // width):
            here = slice(j * width, (j + 1) * width)
            both = jnp.dot(left[...], high_ref[:, here], preferred_element_type=jnp.float32)
            small = jnp.dot(
                left[:total, :], low_ref[:, here], preferred_element_type=jnp.float32
            )
            result = both[:total] + (both[total:] + small)
            there = slice(half * columns + j * width, half * columns + (j + 1) * width)
            for out, blocks in zip(outs, targets):
                for n, k in enumerate(blocks):
                    out[n * rows : (n + 1) * rows, there] = result[k * rows : (k + 1) * rows]


def product(lefts, layout, targets, factors, place, pattern, block_order):
    rows, depth = lefts[0].shape
    count = sum(held.shape[0] for held in lefts) // rows
    halves = len(factors)
    columns = factors[0][0].shape[1]
    total = count * rows
    return pl.pallas_call(
        functools.partial(product_kernel, count, rows, layout, targets, halves),
        in_specs=[SMEM] * 3 + [VMEM] * (len(lefts) + 2 * halves),
        out_specs=[VMEM] * len(targets),
        out_shape=[
            jax.ShapeDtypeStruct((len(blocks) * rows, halves * columns), jnp.float32)
            for blocks in targets
        ],
        scratch_shapes=[pltpu.VMEM((2 * total, depth), jnp.bfloat16)],
        cost_estimate=SMALL,
        compiler_params=pltpu.CompilerParams(vmem_limit_bytes=8 * total * depth + 3 * 2**20),
        name="product",
    )(place, pattern, block_order, *lefts, *[part for pair in factors for part in pair])


def finish_kernel(spec, group, count, part, width, place_ref, bare_ref, occ_ref, virt_ref, *refs):
    out_ref = refs[-1]
    chip, core = place_ref[0], place_ref[1]
    rows_local = CHUNKS * part
    for number, (chunk, halves, s) in enumerate(spec):
        kept, arrived = refs[2 * number], refs[2 * number + 1]
        for position, half in enumerate(halves):
            column = (((chip % group) ^ s) * CORES + (half ^ core)) * width
            columns = pl.ds(pl.multiple_of(column, width), width)
            here = slice(position * width, (position + 1) * width)
            for m in range(count):
                rows = slice(m * rows_local + chunk * part, m * rows_local + (chunk + 1) * part)
                block = slice(m * part, (m + 1) * part)
                ladder = kept[block, here] + arrived[block, here]
                gap = occ_ref[rows, :] + virt_ref[:, columns]
                out_ref[rows, columns] = -(bare_ref[rows, columns] + ladder) / gap


def finish(spec, pairs, group, count, part, width, place, bare, occ, virt):
    return pl.pallas_call(
        functools.partial(finish_kernel, spec, group, count, part, width),
        in_specs=[SMEM] + [VMEM] * (3 + 2 * len(pairs)),
        out_specs=VMEM,
        out_shape=jax.ShapeDtypeStruct(bare.shape, bare.dtype),
        cost_estimate=SMALL,
        compiler_params=pltpu.CompilerParams(vmem_limit_bytes=2 * 2**20),
        name="finish",
    )(place, bare, occ[:, None], virt[None, :], *[part_in for pair in pairs for part_in in pair])


def shards(amplitudes, integrals, bare_terms, pattern, block_order, occ_gap, virt_gap):
    rows_local, columns = amplitudes.shape
    depth, columns_local = integrals.shape
    wide_count = lax.axis_size("wide")
    narrow_count = lax.axis_size("narrow")
    chips = wide_count // CORES
    wide = lax.axis_index("wide")
    z = lax.axis_index("narrow")
    chip = wide // CORES
    core = wide % CORES
    part = rows_local // CHUNKS
    rows = narrow_count * part
    group = chips // narrow_count
    place = jnp.stack([chip, core, z]).astype(jnp.int32)
    chip_bits = [1 << b for b in range(chips.bit_length() - 1)]
    narrow_bits = [1 << b for b in range(narrow_count.bit_length() - 1)]
    targets = [list(range(chips))]
    for bit in reversed(chip_bits):
        targets = [[k for k in targets[0] if not k & bit] + [k for k in targets[0] if k & bit]]
    targets = [targets[0][: chips // 2], targets[0][chips // 2 :]]

    def across(value, mask):
        return lax.ppermute(value, "wide", [(w, w ^ mask) for w in range(wide_count)])

    def across_chips(value, mask):
        return across(value, mask * CORES)

    def along(value, mask):
        return lax.ppermute(value, "narrow", [(n, n ^ mask) for n in range(narrow_count)])

    last = []

    def ordered(*values):
        return list(lax.optimization_barrier((*values, *last))[: len(values)])

    def mark(*values):
        last[:] = values

    swapped = across(integrals, 1)
    pieces = cut(amplitudes, narrow_count, depth, part, place)
    spread = {}
    mine = {}
    held = {}
    layouts = {}
    factors = {}
    state = {}

    def spread_step(g):
        sends = ordered(*pieces[g][1:])
        mark(*sends)
        spread[g] = [pieces[g][0]] + [along(send, n + 1) for n, send in enumerate(sends)]

    def pack_step(g):
        packed = pack(ordered(*spread[g]), part, place)
        mark(*packed)
        mine.update(zip(GROUPS[g], packed))

    def gather_step(chunk, number):
        if number == 0:
            held[chunk] = [mine[chunk]]
            layouts[chunk] = [[(0, 0, rows)]]
        direct = chunk == 0 and chips == 4
        if direct and number == 0:
            (send,) = ordered(mine[chunk])
            mark(send)
            held[chunk] += [across_chips(send, 1), across_chips(send, 2)]
            layouts[chunk] += [[(1, 0, rows)], [(2, 0, rows)]]
        elif direct:
            near, far = ordered(held[chunk][1], held[chunk][2])
            near, far = near[: rows // 2], far[rows // 2 :]
            mark(near, far)
            held[chunk] += [across_chips(near, 2), across_chips(far, 1)]
            layouts[chunk] += [[(3, 0, rows // 2)], [(3, rows // 2, rows // 2)]]
        else:
            bit = chip_bits[number]
            send = jnp.concatenate(ordered(*held[chunk]), axis=0)
            mark(send)
            held[chunk].append(across_chips(send, bit))
            layouts[chunk].append([(k | bit, 0, rows) for k in range(bit)])

    def split_step(half):
        factors[half] = split(*ordered(integrals if half == 0 else swapped))
        mark(*factors[half])

    def multiply(unit):
        chunk, halves = UNITS[unit]
        partials = product(
            ordered(*held[chunk]),
            layouts[chunk],
            targets,
            [factors[half] for half in halves],
            place,
            pattern,
            block_order,
        )
        mark(*partials)
        state[unit] = {0: partials}

    def exchange_step(unit, bit):
        names = list(state[unit])
        if bit == chip_bits[0]:
            keep, leave = [state[unit][0][0]], ordered(state[unit][0][1])
        else:
            values = ordered(*state[unit].values())
            half = values[0].shape[0] // 2
            keep = [value[:half] for value in values]
            leave = [value[half:] for value in values]
        send = jnp.concatenate(leave, axis=0)
        mark(send)
        arrived = across_chips(send, bit)
        half = keep[0].shape[0]
        state[unit] = dict(zip(names, keep))
        for n, s in enumerate(names):
            state[unit][s | bit] = arrived[n * half : (n + 1) * half]

    def reduce_step(unit, bit, narrow_bit):
        now = dict(zip(state[unit], ordered(*state[unit].values())))
        same = ((chip // bit) & 1) == ((z // narrow_bit) & 1)
        names = [s for s in now if not s & bit]
        send = jnp.concatenate([jnp.where(same, now[s | bit], now[s]) for s in names], axis=0)
        mark(send)
        arrived = along(send, narrow_bit)
        size = now[0].shape[0]
        final = narrow_bit == narrow_bits[-1]
        state[unit] = {}
        for n, s in enumerate(names):
            kept = jnp.where(same, now[s], now[s | bit])
            came = arrived[n * size : (n + 1) * size]
            state[unit][s] = (kept, came) if final else kept + came

    def land(unit):
        names = list(state[unit])
        values = ordered(*[value for name in names for value in state[unit][name]])
        mark(values[-1])
        state[unit] = {name: (values[2 * n], values[2 * n + 1]) for n, name in enumerate(names)}

    steps = []
    for bit in chip_bits:
        if bit < group:
            steps.append(functools.partial(exchange_step, bit=bit))
    for narrow_bit in narrow_bits:
        bit = group * narrow_bit
        steps.append(functools.partial(exchange_step, bit=bit))
        steps.append(functools.partial(reduce_step, bit=bit, narrow_bit=narrow_bit))
    steps.append(land)

    gathers = [(chunk, number) for chunk in range(1, CHUNKS) for number in range(len(chip_bits))]
    spread_step(0)
    spread_step(1)
    pack_step(0)
    gather_step(0, 0)
    pack_step(1)
    split_step(0)
    for number in range(1, len(chip_bits)):
        gather_step(0, number)
    spread_step(2)
    gather_step(*gathers.pop(0))
    for tick in range(len(UNITS) + len(steps) - 1):
        if tick < len(UNITS):
            multiply(tick)
            steps[0](tick)
            if tick == 0:
                split_step(1)
                pack_step(2)
            late = UNITS[tick + 1][0] if tick + 1 < len(UNITS) else 0
            while gathers and (gathers[0][0] <= late or tick % CORES == gathers[0][1] - 1):
                gather_step(*gathers.pop(0))
        for number in (*range(len(steps) - 1, 1, -1), 1):
            if 0 <= tick - number < len(UNITS):
                steps[number](tick - number)

    spec = [(*UNITS[unit], s) for unit in range(len(UNITS)) for s in range(group)]
    pairs = [state[unit][s] for unit in range(len(UNITS)) for s in range(group)]
    return finish(
        spec,
        pairs,
        group,
        narrow_count,
        part,
        columns_local,
        place,
        bare_terms,
        occ_gap,
        virt_gap,
    )


def solution(mesh):
    placed = (
        P(("wide", "narrow"), None),
        P("narrow", "wide"),
        P("wide", "narrow"),
        P(),
        P(),
        P("wide"),
        P("narrow"),
    )
    return jax.shard_map(
        shards, mesh=mesh, in_specs=placed, out_specs=P("wide", "narrow"), check_vma=False
    )
```

time: 179 us -> 172 us (0.961)
  waiting for transfers between devices: 93.7 us -> 66.7 us
  local copies, waits for them, and re-layouts: 5.91 us -> 16.5 us
  starting transfers between devices: 48.3 us -> 55.2 us
  Pallas kernels: 28.4 us -> 31.6 us
    ppermute x23 -> x27, waiting for transfers between devices: 55.4 us -> 19.8 us  [across(): lax.ppermute(value, 'wide', [(w, w ^ mask) for w in range(wide_count)])]
    unnamed x64 -> x43, local copies, waits for them, and re-layouts: 5.66 us -> 16.2 us
    ppermute x21 -> x25, waiting for transfers between devices: 38.3 us -> 46.9 us  [along(): lax.ppermute(value, 'narrow', [(n, n ^ mask) for n in range(narrow_count)])]
    ppermute x23 -> x27, starting transfers between devices: 19.5 us -> 25.6 us  [across(): lax.ppermute(value, 'wide', [(w, w ^ mask) for w in range(wide_count)])]
    pallas_call x9 -> x11, Pallas kernels: 18.4 us -> 21.6 us  [the longest x8 19.9 us: product(): pl.pallas_call(functools.partial(product_kernel, count, rows, layout, tar...]
    ppermute x21 -> x25, starting transfers between devices: 28.8 us -> 29.6 us  [along(): lax.ppermute(value, 'narrow', [(n, n ^ mask) for n in range(narrow_count)])]
  transfers between devices with their start and end apart: 44 -> 52, of which waited for: 27 -> 24; matrix products, arithmetic and copies ran while one was open for 1% -> 1% of each run, Pallas kernels for 10% -> 14%
where the time goes in v6:
time: 172 us
  waiting for transfers between devices  66.7 us (39%)
  starting transfers between devices  55.2 us (32%)
  Pallas kernels  31.6 us (18%)
  local copies, waits for them, and re-layouts  16.5 us (10%)
    ppermute x25, waiting for transfers between devices, along(): lax.ppermute(value, 'narrow', [(n, n ^ mask) for n in range(narrow_count)])  46.9 us
    ppermute x25, starting transfers between devices, along(): lax.ppermute(value, 'narrow', [(n, n ^ mask) for n in range(narrow_count)])  29.6 us
    ppermute x27, starting transfers between devices, across(): lax.ppermute(value, 'wide', [(w, w ^ mask) for w in range(wide_count)])  25.6 us
    pallas_call x8, Pallas kernels, product(): pl.pallas_call(functools.partial(product_kernel, count, rows, layout, tar...  19.9 us
    ppermute x27, waiting for transfers between devices, across(): lax.ppermute(value, 'wide', [(w, w ^ mask) for w in range(wide_count)])  19.8 us
    unnamed x43, local copies, waits for them, and re-layouts  16.2 us
    pallas_call x2, Pallas kernels, split(): pl.pallas_call(functools.partial(split_kernel, step), in_specs=[ANY], out...  7.54 us
  transfers between devices with their start and end apart: 52, of which 24 were waited for; matrix products, arithmetic and copies ran while one was open for 1% of the time, Pallas kernels for 14%

profile of v6, /device:TPU:0, one launch (start us, length us, event | category | flops | bytes accessed | tf_op | source)
XLA Modules:
  0.0 171.7 jit_solution(1526832397931626520)
XLA Ops:
  2.4 2.6 %collective-permute-start = (f32[8,2048]{1,0:T(8,128)S(1)}, f32[8,2048]{1,0:T(8,128)S(1)}, u32[]{:S(2)}, u32[]{:S(2)}) collective-permute-start(f32[8,2048]{1,0:T(8,128)S(1)} %get-tuple-element.170), channel_id=1, source_target_pairs={{0,1},{1,0},{2,3},{3,2},{4,5},{5,4},{6,7},{7,6},{8,9},{9,8},{10,11... | collective-permute-start | bytes 196616 | tf_op jit(solution)/shard_map/ppermute | solution.py:235
  5.0 2.6 %collective-permute-start.1 = (f32[8,2048]{1,0:T(8,128)S(1)}, f32[8,2048]{1,0:T(8,128)S(1)}, u32[]{:S(2)}, u32[]{:S(2)}) collective-permute-start(f32[8,2048]{1,0:T(8,128)S(1)} %get-tuple-element.171), channel_id=1, source_target_pairs={{0,2},{1,3},{2,0},{3,1},{4,6},{5,7},{6,4},{7,5},{8,10},{9,11},{10,... | collective-permute-start | bytes 196616 | tf_op jit(solution)/shard_map/ppermute | solution.py:235
  7.8 4.2 %collective-permute-done.1.refs_2_ = f32[8,2048]{1,0:T(8,128)S(1)} collective-permute-done((f32[8,2048]{1,0:T(8,128)S(1)}, f32[8,2048]{1,0:T(8,128)S(1)}, u32[]{:S(2)}, u32[]{:S(2)}) %collective-permute-start.1) | collective-permute-done | bytes 65568 | tf_op jit(solution)/shard_map/ppermute | solution.py:235
  21.7 2.9 %collective-permute-start.7 = (f32[8,2048]{1,0:T(8,128)S(1)}, f32[8,2048]{1,0:T(8,128)S(1)}, u32[]{:S(2)}, u32[]{:S(2)}) collective-permute-start(f32[8,2048]{1,0:T(8,128)S(1)} %get-tuple-element.178), channel_id=1, source_target_pairs={{0,3},{1,2},{2,1},{3,0},{4,7},{5,6},{6,5},{7,4},{8,11},{9,10},{10,... | collective-permute-start | bytes 196616 | tf_op jit(solution)/shard_map/ppermute | solution.py:235
  28.4 3.4 %copy-done.13 = f32[2048,1024]{1,0:T(8,128)S(1)} copy-done((f32[2048,1024]{1,0:T(8,128)S(1)}, f32[2048,1024]{1,0:T(8,128)}, u32[]{:S(2)}) %copy-start.13) | copy-done | bytes 8388632
  40.2 2.4 %collective-permute-done.8.refs_3_ = f32[16,2048]{1,0:T(8,128)S(1)} collective-permute-done((f32[16,2048]{1,0:T(8,128)S(1)}, f32[16,2048]{1,0:T(8,128)S(1)}, u32[]{:S(2)}, u32[]{:S(2)}) %collective-permute-start.8) | collective-permute-done | bytes 131104 | tf_op jit(solution)/shard_map/ppermute | solution.py:229
  43.6 2.4 %collective-permute-start.14 = (f32[16,2048]{1,0:T(8,128)S(1)}, f32[16,2048]{1,0:T(8,128)S(1)}, u32[]{:S(2)}, u32[]{:S(2)}) collective-permute-start(f32[16,2048]{1,0:T(8,128)S(1)} %get-tuple-element.199), channel_id=1, source_target_pairs={{0,3},{1,2},{2,1},{3,0},{4,7},{5,6},{6,5},{7,4},{8,11},{9,10},{10,... | collective-permute-start | bytes 393224 | tf_op jit(solution)/shard_map/ppermute | solution.py:235
  46.0 2.2 %copy-done.1 = bf16[2048,1024]{1,0:T(8,128)(2,1)S(1)} copy-done((bf16[2048,1024]{1,0:T(8,128)(2,1)S(1)}, bf16[2048,1024]{1,0:T(8,128)(2,1)}, u32[]{:S(2)}) %copy-start.1) | copy-done | bytes 4194328
  48.2 2.2 %copy-done.5 = bf16[2048,1024]{1,0:T(8,128)(2,1)S(1)} copy-done((bf16[2048,1024]{1,0:T(8,128)(2,1)S(1)}, bf16[2048,1024]{1,0:T(8,128)(2,1)}, u32[]{:S(2)}) %copy-start.5) | copy-done | bytes 4194328
  50.4 2.5 %product.8 = (f32[64,1024]{1,0:T(8,128)S(1)}, f32[64,1024]{1,0:T(8,128)S(1)}) custom-call(s32[3]{0:T(128)S(1)} %pad_add_fusion.place_ref, s32[8,64]{1,0:T(8,128)S(1)} %copy-done.16, s32[8]{0:T(128)S(1)} %copy-done.17, f32[32,2048]{1,0:T(8,128)S(1)} %pack.3.refs_0_, f32[32,2048]{1,0:T(8,128)S(1)} %collective-permute-done.3.refs_1_, ...), custom_call_target="tpu_custom_call" | custom-call | flops 1 | bytes 1 | tf_op jit(solution)/shard_map/product/pallas_call | solution.py:162
  53.5 5.8 %split.3 = (bf16[2048,1024]{1,0:T(8,128)(2,1)S(1)}, bf16[2048,1024]{1,0:T(8,128)(2,1)S(1)}) custom-call(f32[2048,1024]{1,0:T(8,128)} %collective-permute-done.15.whole_ref), custom_call_target="tpu_custom_call" | custom-call | flops 1 | bytes 1 | tf_op jit(solution)/shard_map/split/pallas_call | solution.py:101
  61.6 2.5 %product.9 = (f32[64,1024]{1,0:T(8,128)S(1)}, f32[64,1024]{1,0:T(8,128)S(1)}) custom-call(s32[3]{0:T(128)S(1)} %pad_add_fusion.place_ref, s32[8,64]{1,0:T(8,128)S(1)} %copy-done.16, s32[8]{0:T(128)S(1)} %copy-done.17, f32[32,2048]{1,0:T(8,128)S(1)} %pack.3.refs_0_, f32[32,2048]{1,0:T(8,128)S(1)} %collective-permute-done.3.refs_1_, ...), custom_call_target="tpu_custom_call" | custom-call | flops 1 | bytes 1 | tf_op jit(solution)/shard_map/product/pallas_call | solution.py:162
  65.8 4.8 %collective-permute-done.16 = f32[64,1024]{1,0:T(8,128)S(1)} collective-permute-done((f32[64,1024]{1,0:T(8,128)S(1)}, f32[64,1024]{1,0:T(8,128)S(1)}, u32[]{:S(2)}, u32[]{:S(2)}) %collective-permute-start.16) | collective-permute-done | bytes 262176 | tf_op jit(solution)/shard_map/ppermute | solution.py:235
  70.7 2.5 %product.10 = (f32[64,1024]{1,0:T(8,128)S(1)}, f32[64,1024]{1,0:T(8,128)S(1)}) custom-call(s32[3]{0:T(128)S(1)} %pad_add_fusion.place_ref, s32[8,64]{1,0:T(8,128)S(1)} %copy-done.16, s32[8]{0:T(128)S(1)} %copy-done.17, f32[32,2048]{1,0:T(8,128)S(1)} %pack.4.refs_0_, f32[32,2048]{1,0:T(8,128)S(1)} %collective-permute-done.11.refs_1_, ...), custom_call_target="tpu_custom_call" | custom-call | flops 1 | bytes 1 | tf_op jit(solution)/shard_map/product/pallas_call | solution.py:162
  73.2 2.5 %product.11 = (f32[64,1024]{1,0:T(8,128)S(1)}, f32[64,1024]{1,0:T(8,128)S(1)}) custom-call(s32[3]{0:T(128)S(1)} %pad_add_fusion.place_ref, s32[8,64]{1,0:T(8,128)S(1)} %copy-done.16, s32[8]{0:T(128)S(1)} %copy-done.17, f32[32,2048]{1,0:T(8,128)S(1)} %pack.4.refs_0_, f32[32,2048]{1,0:T(8,128)S(1)} %collective-permute-done.11.refs_1_, ...), custom_call_target="tpu_custom_call" | custom-call | flops 1 | bytes 1 | tf_op jit(solution)/shard_map/product/pallas_call | solution.py:162
  78.4 5.0 %collective-permute-done.20.refs_1_ = f32[32,2048]{1,0:T(8,128)S(1)} collective-permute-done((f32[32,2048]{1,0:T(8,128)S(1)}, f32[32,2048]{1,0:T(8,128)S(1)}, u32[]{:S(2)}, u32[]{:S(2)}) %collective-permute-start.20) | collective-permute-done | bytes 262176 | tf_op jit(solution)/shard_map/ppermute | solution.py:229
  84.0 2.6 %collective-permute-done.24 = f32[64,1024]{1,0:T(8,128)S(1)} collective-permute-done((f32[64,1024]{1,0:T(8,128)S(1)}, f32[64,1024]{1,0:T(8,128)S(1)}, u32[]{:S(2)}, u32[]{:S(2)}) %collective-permute-start.24) | collective-permute-done | bytes 262176 | tf_op jit(solution)/shard_map/ppermute | solution.py:235
  91.9 3.8 %collective-permute-done.28 = f32[64,1024]{1,0:T(8,128)S(1)} collective-permute-done((f32[64,1024]{1,0:T(8,128)S(1)}, f32[64,1024]{1,0:T(8,128)S(1)}, u32[]{:S(2)}, u32[]{:S(2)}) %collective-permute-start.28) | collective-permute-done | bytes 262176 | tf_op jit(solution)/shard_map/ppermute | solution.py:235
  95.7 2.2 %copy-done.7 = bf16[2048,1024]{1,0:T(8,128)(2,1)S(1)} copy-done((bf16[2048,1024]{1,0:T(8,128)(2,1)S(1)}, bf16[2048,1024]{1,0:T(8,128)(2,1)}, u32[]{:S(2)}) %copy-start.7) | copy-done | bytes 4194328
  97.9 2.5 %product.12 = (f32[64,1024]{1,0:T(8,128)S(1)}, f32[64,1024]{1,0:T(8,128)S(1)}) custom-call(s32[3]{0:T(128)S(1)} %pad_add_fusion.place_ref, s32[8,64]{1,0:T(8,128)S(1)} %copy-done.16, s32[8]{0:T(128)S(1)} %copy-done.17, f32[32,2048]{1,0:T(8,128)S(1)} %get-tuple-element.267.refs_0_, f32[32,2048]{1,0:T(8,128)S(1)} %collective-permute-done.20.refs_1_, ...), custom_call_target="tpu_custom_call" | custom-call | flops 1 | bytes 1 | tf_op jit(solution)/shard_map/product/pallas_call | solution.py:162
  101.4 2.7 %product.13 = (f32[64,1024]{1,0:T(8,128)S(1)}, f32[64,1024]{1,0:T(8,128)S(1)}) custom-call(s32[3]{0:T(128)S(1)} %pad_add_fusion.place_ref, s32[8,64]{1,0:T(8,128)S(1)} %copy-done.16, s32[8]{0:T(128)S(1)} %copy-done.17, f32[32,2048]{1,0:T(8,128)S(1)} %get-tuple-element.267.refs_0_, f32[32,2048]{1,0:T(8,128)S(1)} %collective-permute-done.20.refs_1_, ...), custom_call_target="tpu_custom_call" | custom-call | flops 1 | bytes 1 | tf_op jit(solution)/shard_map/product/pallas_call | solution.py:162
  107.7 4.3 %collective-permute-done.29.refs_1_ = f32[32,2048]{1,0:T(8,128)S(1)} collective-permute-done((f32[32,2048]{1,0:T(8,128)S(1)}, f32[32,2048]{1,0:T(8,128)S(1)}, u32[]{:S(2)}, u32[]{:S(2)}) %collective-permute-start.29) | collective-permute-done | bytes 262176 | tf_op jit(solution)/shard_map/ppermute | solution.py:229
  119.6 5.2 %collective-permute-done.38 = f32[64,1024]{1,0:T(8,128)S(1)} collective-permute-done((f32[64,1024]{1,0:T(8,128)S(1)}, f32[64,1024]{1,0:T(8,128)S(1)}, u32[]{:S(2)}, u32[]{:S(2)}) %collective-permute-start.38) | collective-permute-done | bytes 262176 | tf_op jit(solution)/shard_map/ppermute | solution.py:235
  124.9 2.5 %product.14 = (f32[64,1024]{1,0:T(8,128)S(1)}, f32[64,1024]{1,0:T(8,128)S(1)}) custom-call(s32[3]{0:T(128)S(1)} %pad_add_fusion.place_ref, s32[8,64]{1,0:T(8,128)S(1)} %copy-done.16, s32[8]{0:T(128)S(1)} %copy-done.17, f32[32,2048]{1,0:T(8,128)S(1)} %get-tuple-element.296.refs_0_, f32[32,2048]{1,0:T(8,128)S(1)} %collective-permute-done.29.refs_1_, ...), custom_call_target="tpu_custom_call" | custom-call | flops 1 | bytes 1 | tf_op jit(solution)/shard_map/product/pallas_call | solution.py:162
  132.3 2.5 %product.15 = (f32[64,1024]{1,0:T(8,128)S(1)}, f32[64,1024]{1,0:T(8,128)S(1)}) custom-call(s32[3]{0:T(128)S(1)} %pad_add_fusion.place_ref, s32[8,64]{1,0:T(8,128)S(1)} %copy-done.16, s32[8]{0:T(128)S(1)} %copy-done.17, f32[32,2048]{1,0:T(8,128)S(1)} %get-tuple-element.296.refs_0_, f32[32,2048]{1,0:T(8,128)S(1)} %collective-permute-done.29.refs_1_, ...), custom_call_target="tpu_custom_call" | custom-call | flops 1 | bytes 1 | tf_op jit(solution)/shard_map/product/pallas_call | solution.py:162
  136.2 3.1 %collective-permute-done.42 = f32[64,1024]{1,0:T(8,128)S(1)} collective-permute-done((f32[64,1024]{1,0:T(8,128)S(1)}, f32[64,1024]{1,0:T(8,128)S(1)}, u32[]{:S(2)}, u32[]{:S(2)}) %collective-permute-start.42) | collective-permute-done | bytes 262176 | tf_op jit(solution)/shard_map/ppermute | solution.py:235
  141.8 2.6 %collective-permute-done.43 = f32[32,1024]{1,0:T(8,128)S(1)} collective-permute-done((f32[32,1024]{1,0:T(8,128)S(1)}, f32[32,1024]{1,0:T(8,128)S(1)}, u32[]{:S(2)}, u32[]{:S(2)}) %collective-permute-start.43) | collective-permute-done | bytes 131104 | tf_op jit(solution)/shard_map/ppermute | solution.py:229
  146.0 2.3 %collective-permute-done.46 = f32[64,1024]{1,0:T(8,128)S(1)} collective-permute-done((f32[64,1024]{1,0:T(8,128)S(1)}, f32[64,1024]{1,0:T(8,128)S(1)}, u32[]{:S(2)}, u32[]{:S(2)}) %collective-permute-start.46) | collective-permute-done | bytes 262176 | tf_op jit(solution)/shard_map/ppermute | solution.py:235
  148.3 2.1 %collective-permute-start.47 = (f32[32,1024]{1,0:T(8,128)S(1)}, f32[32,1024]{1,0:T(8,128)S(1)}, u32[]{:S(2)}, u32[]{:S(2)}) collective-permute-start(f32[32,1024]{1,0:T(8,128)S(1)} %get-tuple-element.334), channel_id=1, source_target_pairs={{0,16},{4,20},{8,24},{12,28},{16,0},{20,4},{24,8},{28,12},{1,17},{... | collective-permute-start | bytes 393224 | tf_op jit(solution)/shard_map/ppermute | solution.py:229
  154.5 3.9 %collective-permute-done.49 = f32[64,1024]{1,0:T(8,128)S(1)} collective-permute-done((f32[64,1024]{1,0:T(8,128)S(1)}, f32[64,1024]{1,0:T(8,128)S(1)}, u32[]{:S(2)}, u32[]{:S(2)}) %collective-permute-start.49) | collective-permute-done | bytes 262176 | tf_op jit(solution)/shard_map/ppermute | solution.py:235
  160.6 2.8 %collective-permute-done.50 = f32[32,1024]{1,0:T(8,128)S(1)} collective-permute-done((f32[32,1024]{1,0:T(8,128)S(1)}, f32[32,1024]{1,0:T(8,128)S(1)}, u32[]{:S(2)}, u32[]{:S(2)}) %collective-permute-start.50) | collective-permute-done | bytes 131104 | tf_op jit(solution)/shard_map/ppermute | solution.py:229
  163.7 6.2 %collective-permute-done.51.refs_15_ = f32[32,1024]{1,0:T(8,128)S(1)} collective-permute-done((f32[32,1024]{1,0:T(8,128)S(1)}, f32[32,1024]{1,0:T(8,128)S(1)}, u32[]{:S(2)}, u32[]{:S(2)}) %collective-permute-start.51) | collective-permute-done | bytes 131104 | tf_op jit(solution)/shard_map/ppermute | solution.py:235
  (169 shorter events, 69.7 us)
Async XLA Ops:
  0.0 52.9 %collective-permute-start.15 = (f32[2048,1024]{1,0:T(8,128)}, f32[2048,1024]{1,0:T(8,128)}, u32[]{:S(2)}, u32[]{:S(2)}) collective-permute-start(f32[2048,1024]{1,0:T(8,128)} %whole_ref.2), channel_id=1, source_target_pairs={{0,4},{4,0},{8,12},{12,8},{16,20},{20,16},{24,28},{28,24},{1,5},{5... | collective-permute-start | bytes 25165832 | tf_op jit(solution)/shard_map/ppermute | solution.py:229
  14.3 23.2 %collective-permute-start.3 = (f32[32,2048]{1,0:T(8,128)S(1)}, f32[32,2048]{1,0:T(8,128)S(1)}, u32[]{:S(2)}, u32[]{:S(2)}) collective-permute-start(f32[32,2048]{1,0:T(8,128)S(1)} %pack.3.refs_0_), channel_id=1, source_target_pairs={{0,8},{4,12},{8,0},{12,4},{16,24},{20,28},{24,16},{28,20},{1,9},{5... | collective-permute-start | bytes 786440 | tf_op jit(solution)/shard_map/ppermute | solution.py:229
  15.9 21.7 %collective-permute-start.4 = (f32[32,2048]{1,0:T(8,128)S(1)}, f32[32,2048]{1,0:T(8,128)S(1)}, u32[]{:S(2)}, u32[]{:S(2)}) collective-permute-start(f32[32,2048]{1,0:T(8,128)S(1)} %pack.3.refs_0_), channel_id=1, source_target_pairs={{0,16},{4,20},{8,24},{12,28},{16,0},{20,4},{24,8},{28,12},{1,17},{... | collective-permute-start | bytes 786440 | tf_op jit(solution)/shard_map/ppermute | solution.py:229
  38.7 21.3 %collective-permute-start.11 = (f32[32,2048]{1,0:T(8,128)S(1)}, f32[32,2048]{1,0:T(8,128)S(1)}, u32[]{:S(2)}, u32[]{:S(2)}) collective-permute-start(f32[32,2048]{1,0:T(8,128)S(1)} %pack.4.refs_0_), channel_id=1, source_target_pairs={{0,8},{4,12},{8,0},{12,4},{16,24},{20,28},{24,16},{28,20},{1,9},{5... | collective-permute-start | bytes 786440 | tf_op jit(solution)/shard_map/ppermute | solution.py:229
  40.2 19.1 %collective-permute-start.12 = (f32[16,2048]{1,0:T(8,128)S(1)}, f32[16,2048]{1,0:T(8,128)S(1)}, u32[]{:S(2)}, u32[]{:S(2)}) collective-permute-start(f32[16,2048]{1,0:T(8,128)S(1)} %get-tuple-element.197), channel_id=1, source_target_pairs={{0,1},{1,0},{2,3},{3,2},{4,5},{5,4},{6,7},{7,6},{8,9},{9,8},{10,11... | collective-permute-start | bytes 393224 | tf_op jit(solution)/shard_map/ppermute | solution.py:235
  42.6 16.8 %collective-permute-start.13 = (f32[16,2048]{1,0:T(8,128)S(1)}, f32[16,2048]{1,0:T(8,128)S(1)}, u32[]{:S(2)}, u32[]{:S(2)}) collective-permute-start(f32[16,2048]{1,0:T(8,128)S(1)} %get-tuple-element.198), channel_id=1, source_target_pairs={{0,2},{1,3},{2,0},{3,1},{4,6},{5,7},{6,4},{7,5},{8,10},{9,11},{10,... | collective-permute-start | bytes 393224 | tf_op jit(solution)/shard_map/ppermute | solution.py:235
  43.6 15.7 %collective-permute-start.14 = (f32[16,2048]{1,0:T(8,128)S(1)}, f32[16,2048]{1,0:T(8,128)S(1)}, u32[]{:S(2)}, u32[]{:S(2)}) collective-permute-start(f32[16,2048]{1,0:T(8,128)S(1)} %get-tuple-element.199), channel_id=1, source_target_pairs={{0,3},{1,2},{2,1},{3,0},{4,7},{5,6},{6,5},{7,4},{8,11},{9,10},{10,... | collective-permute-start | bytes 393224 | tf_op jit(solution)/shard_map/ppermute | solution.py:235
  52.9 11.2 %collective-permute-start.10 = (f32[64,1024]{1,0:T(8,128)S(1)}, f32[64,1024]{1,0:T(8,128)S(1)}, u32[]{:S(2)}, u32[]{:S(2)}) collective-permute-start(f32[64,1024]{1,0:T(8,128)S(1)} %get-tuple-element.208), channel_id=1, source_target_pairs={{0,8},{4,12},{8,0},{12,4},{16,24},{20,28},{24,16},{28,20},{1,9},{5... | collective-permute-start | bytes 786440 | tf_op jit(solution)/shard_map/ppermute | solution.py:229
  60.0 10.6 %collective-permute-start.17 = (f32[64,2048]{1,0:T(8,128)S(1)}, f32[64,2048]{1,0:T(8,128)S(1)}, u32[]{:S(2)}, u32[]{:S(2)}) collective-permute-start(f32[64,2048]{1,0:T(8,128)S(1)} %constant_dynamic-update-slice_fusion), channel_id=1, source_target_pairs={{0,16},{4,20},{8,24},{12,28},{16,0},{20,4},{24,8},{28,12},{1,17},{... | collective-permute-start | bytes 1572872 | tf_op jit(solution)/shard_map/ppermute | solution.py:229
  64.2 8.9 %collective-permute-start.19 = (f32[64,1024]{1,0:T(8,128)S(1)}, f32[64,1024]{1,0:T(8,128)S(1)}, u32[]{:S(2)}, u32[]{:S(2)}) collective-permute-start(f32[64,1024]{1,0:T(8,128)S(1)} %get-tuple-element.228), channel_id=1, source_target_pairs={{0,8},{4,12},{8,0},{12,4},{16,24},{20,28},{24,16},{28,20},{1,9},{5... | collective-permute-start | bytes 786440 | tf_op jit(solution)/shard_map/ppermute | solution.py:229
  75.7 7.6 %collective-permute-start.20 = (f32[32,2048]{1,0:T(8,128)S(1)}, f32[32,2048]{1,0:T(8,128)S(1)}, u32[]{:S(2)}, u32[]{:S(2)}) collective-permute-start(f32[32,2048]{1,0:T(8,128)S(1)} %get-tuple-element.267.refs_0_), channel_id=1, source_target_pairs={{0,8},{4,12},{8,0},{12,4},{16,24},{20,28},{24,16},{28,20},{1,9},{5... | collective-permute-start | bytes 786440 | tf_op jit(solution)/shard_map/ppermute | solution.py:229
  77.3 9.3 %collective-permute-start.24 = (f32[64,1024]{1,0:T(8,128)S(1)}, f32[64,1024]{1,0:T(8,128)S(1)}, u32[]{:S(2)}, u32[]{:S(2)}) collective-permute-start(f32[64,1024]{1,0:T(8,128)S(1)} %broadcast_select_fusion.6), channel_id=1, source_target_pairs={{0,1},{1,0},{2,3},{3,2},{4,5},{5,4},{6,7},{7,6},{8,9},{9,8},{10,11... | collective-permute-start | bytes 786440 | tf_op jit(solution)/shard_map/ppermute | solution.py:235
  77.8 9.9 %collective-permute-start.23 = (f32[64,1024]{1,0:T(8,128)S(1)}, f32[64,1024]{1,0:T(8,128)S(1)}, u32[]{:S(2)}, u32[]{:S(2)}) collective-permute-start(f32[64,1024]{1,0:T(8,128)S(1)} %get-tuple-element.236), channel_id=1, source_target_pairs={{0,8},{4,12},{8,0},{12,4},{16,24},{20,28},{24,16},{28,20},{1,9},{5... | collective-permute-start | bytes 786440 | tf_op jit(solution)/shard_map/ppermute | solution.py:229
  83.4 12.3 %collective-permute-start.22 = (f32[64,2048]{1,0:T(8,128)S(1)}, f32[64,2048]{1,0:T(8,128)S(1)}, u32[]{:S(2)}, u32[]{:S(2)}) collective-permute-start(f32[64,2048]{1,0:T(8,128)S(1)} %constant_dynamic-update-slice_fusion.2), channel_id=1, source_target_pairs={{0,16},{4,20},{8,24},{12,28},{16,0},{20,4},{24,8},{28,12},{1,17},{... | collective-permute-start | bytes 1572872 | tf_op jit(solution)/shard_map/ppermute | solution.py:229
  87.8 7.8 %collective-permute-start.28 = (f32[64,1024]{1,0:T(8,128)S(1)}, f32[64,1024]{1,0:T(8,128)S(1)}, u32[]{:S(2)}, u32[]{:S(2)}) collective-permute-start(f32[64,1024]{1,0:T(8,128)S(1)} %broadcast_select_fusion.5), channel_id=1, source_target_pairs={{0,1},{1,0},{2,3},{3,2},{4,5},{5,4},{6,7},{7,6},{8,9},{9,8},{10,11... | collective-permute-start | bytes 786440 | tf_op jit(solution)/shard_map/ppermute | solution.py:235
  88.0 12.5 %collective-permute-start.27 = (f32[64,1024]{1,0:T(8,128)S(1)}, f32[64,1024]{1,0:T(8,128)S(1)}, u32[]{:S(2)}, u32[]{:S(2)}) collective-permute-start(f32[64,1024]{1,0:T(8,128)S(1)} %get-tuple-element.245), channel_id=1, source_target_pairs={{0,8},{4,12},{8,0},{12,4},{16,24},{20,28},{24,16},{28,20},{1,9},{5... | collective-permute-start | bytes 786440 | tf_op jit(solution)/shard_map/ppermute | solution.py:229
  89.4 11.0 %collective-permute-start.21 = (f32[32,1024]{1,0:T(8,128)S(1)}, f32[32,1024]{1,0:T(8,128)S(1)}, u32[]{:S(2)}, u32[]{:S(2)}) collective-permute-start(f32[32,1024]{1,0:T(8,128)S(1)} %get-tuple-element.355), channel_id=1, source_target_pairs={{0,2},{1,3},{2,0},{3,1},{4,6},{5,7},{6,4},{7,5},{8,10},{9,11},{10,... | collective-permute-start | bytes 393224 | tf_op jit(solution)/shard_map/ppermute | solution.py:235
  91.4 9.0 %collective-permute-start.25 = (f32[32,1024]{1,0:T(8,128)S(1)}, f32[32,1024]{1,0:T(8,128)S(1)}, u32[]{:S(2)}, u32[]{:S(2)}) collective-permute-start(f32[32,1024]{1,0:T(8,128)S(1)} %get-tuple-element.354), channel_id=1, source_target_pairs={{0,16},{4,20},{8,24},{12,28},{16,0},{20,4},{24,8},{28,12},{1,17},{... | collective-permute-start | bytes 393224 | tf_op jit(solution)/shard_map/ppermute | solution.py:229
  104.1 7.9 %collective-permute-start.29 = (f32[32,2048]{1,0:T(8,128)S(1)}, f32[32,2048]{1,0:T(8,128)S(1)}, u32[]{:S(2)}, u32[]{:S(2)}) collective-permute-start(f32[32,2048]{1,0:T(8,128)S(1)} %get-tuple-element.296.refs_0_), channel_id=1, source_target_pairs={{0,8},{4,12},{8,0},{12,4},{16,24},{20,28},{24,16},{28,20},{1,9},{5... | collective-permute-start | bytes 786440 | tf_op jit(solution)/shard_map/ppermute | solution.py:229
  105.6 9.1 %collective-permute-start.34 = (f32[64,1024]{1,0:T(8,128)S(1)}, f32[64,1024]{1,0:T(8,128)S(1)}, u32[]{:S(2)}, u32[]{:S(2)}) collective-permute-start(f32[64,1024]{1,0:T(8,128)S(1)} %broadcast_select_fusion.4), channel_id=1, source_target_pairs={{0,1},{1,0},{2,3},{3,2},{4,5},{5,4},{6,7},{7,6},{8,9},{9,8},{10,11... | collective-permute-start | bytes 786440 | tf_op jit(solution)/shard_map/ppermute | solution.py:235
  105.6 8.0 %collective-permute-start.26 = (f32[32,1024]{1,0:T(8,128)S(1)}, f32[32,1024]{1,0:T(8,128)S(1)}, u32[]{:S(2)}, u32[]{:S(2)}) collective-permute-start(f32[32,1024]{1,0:T(8,128)S(1)} %get-tuple-element.351), channel_id=1, source_target_pairs={{0,2},{1,3},{2,0},{3,1},{4,6},{5,7},{6,4},{7,5},{8,10},{9,11},{10,... | collective-permute-start | bytes 393224 | tf_op jit(solution)/shard_map/ppermute | solution.py:235
  112.1 12.8 %collective-permute-start.32 = (f32[64,2048]{1,0:T(8,128)S(1)}, f32[64,2048]{1,0:T(8,128)S(1)}, u32[]{:S(2)}, u32[]{:S(2)}) collective-permute-start(f32[64,2048]{1,0:T(8,128)S(1)} %constant_dynamic-update-slice_fusion.4), channel_id=1, source_target_pairs={{0,16},{4,20},{8,24},{12,28},{16,0},{20,4},{24,8},{28,12},{1,17},{... | collective-permute-start | bytes 1572872 | tf_op jit(solution)/shard_map/ppermute | solution.py:229
  114.9 9.9 %collective-permute-start.38 = (f32[64,1024]{1,0:T(8,128)S(1)}, f32[64,1024]{1,0:T(8,128)S(1)}, u32[]{:S(2)}, u32[]{:S(2)}) collective-permute-start(f32[64,1024]{1,0:T(8,128)S(1)} %broadcast_select_fusion.3), channel_id=1, source_target_pairs={{0,1},{1,0},{2,3},{3,2},{4,5},{5,4},{6,7},{7,6},{8,9},{9,8},{10,11... | collective-permute-start | bytes 786440 | tf_op jit(solution)/shard_map/ppermute | solution.py:235
  116.2 13.9 %collective-permute-start.37 = (f32[64,1024]{1,0:T(8,128)S(1)}, f32[64,1024]{1,0:T(8,128)S(1)}, u32[]{:S(2)}, u32[]{:S(2)}) collective-permute-start(f32[64,1024]{1,0:T(8,128)S(1)} %get-tuple-element.272), channel_id=1, source_target_pairs={{0,8},{4,12},{8,0},{12,4},{16,24},{20,28},{24,16},{28,20},{1,9},{5... | collective-permute-start | bytes 786440 | tf_op jit(solution)/shard_map/ppermute | solution.py:229
  117.6 9.8 %collective-permute-start.31 = (f32[32,1024]{1,0:T(8,128)S(1)}, f32[32,1024]{1,0:T(8,128)S(1)}, u32[]{:S(2)}, u32[]{:S(2)}) collective-permute-start(f32[32,1024]{1,0:T(8,128)S(1)} %get-tuple-element.347), channel_id=1, source_target_pairs={{0,2},{1,3},{2,0},{3,1},{4,6},{5,7},{6,4},{7,5},{8,10},{9,11},{10,... | collective-permute-start | bytes 393224 | tf_op jit(solution)/shard_map/ppermute | solution.py:235
  119.3 8.1 %collective-permute-start.35 = (f32[32,1024]{1,0:T(8,128)S(1)}, f32[32,1024]{1,0:T(8,128)S(1)}, u32[]{:S(2)}, u32[]{:S(2)}) collective-permute-start(f32[32,1024]{1,0:T(8,128)S(1)} %get-tuple-element.346), channel_id=1, source_target_pairs={{0,16},{4,20},{8,24},{12,28},{16,0},{20,4},{24,8},{28,12},{1,17},{... | collective-permute-start | bytes 393224 | tf_op jit(solution)/shard_map/ppermute | solution.py:229
  127.4 7.4 %collective-permute-start.36 = (f32[32,1024]{1,0:T(8,128)S(1)}, f32[32,1024]{1,0:T(8,128)S(1)}, u32[]{:S(2)}, u32[]{:S(2)}) collective-permute-start(f32[32,1024]{1,0:T(8,128)S(1)} %get-tuple-element.343), channel_id=1, source_target_pairs={{0,2},{1,3},{2,0},{3,1},{4,6},{5,7},{6,4},{7,5},{8,10},{9,11},{10,... | collective-permute-start | bytes 393224 | tf_op jit(solution)/shard_map/ppermute | solution.py:235
  130.1 9.2 %collective-permute-start.42 = (f32[64,1024]{1,0:T(8,128)S(1)}, f32[64,1024]{1,0:T(8,128)S(1)}, u32[]{:S(2)}, u32[]{:S(2)}) collective-permute-start(f32[64,1024]{1,0:T(8,128)S(1)} %broadcast_select_fusion.2), channel_id=1, source_target_pairs={{0,1},{1,0},{2,3},{3,2},{4,5},{5,4},{6,7},{7,6},{8,9},{9,8},{10,11... | collective-permute-start | bytes 786440 | tf_op jit(solution)/shard_map/ppermute | solution.py:235
  132.1 8.2 %collective-permute-start.41 = (f32[64,1024]{1,0:T(8,128)S(1)}, f32[64,1024]{1,0:T(8,128)S(1)}, u32[]{:S(2)}, u32[]{:S(2)}) collective-permute-start(f32[64,1024]{1,0:T(8,128)S(1)} %get-tuple-element.288), channel_id=1, source_target_pairs={{0,8},{4,12},{8,0},{12,4},{16,24},{20,28},{24,16},{28,20},{1,9},{5... | collective-permute-start | bytes 786440 | tf_op jit(solution)/shard_map/ppermute | solution.py:229
  140.4 7.8 %collective-permute-start.46 = (f32[64,1024]{1,0:T(8,128)S(1)}, f32[64,1024]{1,0:T(8,128)S(1)}, u32[]{:S(2)}, u32[]{:S(2)}) collective-permute-start(f32[64,1024]{1,0:T(8,128)S(1)} %broadcast_select_fusion.1), channel_id=1, source_target_pairs={{0,1},{1,0},{2,3},{3,2},{4,5},{5,4},{6,7},{7,6},{8,9},{9,8},{10,11... | collective-permute-start | bytes 786440 | tf_op jit(solution)/shard_map/ppermute | solution.py:235
  140.9 9.6 %collective-permute-start.45 = (f32[64,1024]{1,0:T(8,128)S(1)}, f32[64,1024]{1,0:T(8,128)S(1)}, u32[]{:S(2)}, u32[]{:S(2)}) collective-permute-start(f32[64,1024]{1,0:T(8,128)S(1)} %get-tuple-element.301), channel_id=1, source_target_pairs={{0,8},{4,12},{8,0},{12,4},{16,24},{20,28},{24,16},{28,20},{1,9},{5... | collective-permute-start | bytes 786440 | tf_op jit(solution)/shard_map/ppermute | solution.py:229
  150.5 7.9 %collective-permute-start.49 = (f32[64,1024]{1,0:T(8,128)S(1)}, f32[64,1024]{1,0:T(8,128)S(1)}, u32[]{:S(2)}, u32[]{:S(2)}) collective-permute-start(f32[64,1024]{1,0:T(8,128)S(1)} %broadcast_select_fusion), channel_id=1, source_target_pairs={{0,1},{1,0},{2,3},{3,2},{4,5},{5,4},{6,7},{7,6},{8,9},{9,8},{10,11... | collective-permute-start | bytes 786440 | tf_op jit(solution)/shard_map/ppermute | solution.py:235
  (40 other events, 358.9 us)

commit v7 on v6

--- a/solution.py
+++ b/solution.py
@@ -15,7 +15,7 @@
 
 SMEM = pl.BlockSpec(memory_space=pltpu.SMEM)
 VMEM = pl.BlockSpec(memory_space=pltpu.VMEM)
-ANY = pl.BlockSpec(memory_space=pl.ANY)
+HBM = pl.BlockSpec(memory_space=pltpu.HBM)
 SMALL = pl.CostEstimate(flops=1, bytes_accessed=1, transcendentals=0)
 
 
@@ -51,7 +51,8 @@
     return [outs[g * count : (g + 1) * count] for g in range(len(bounds))]
 
 
-def pack_kernel(count, part, place_ref, *refs):
+def pack_kernel(count, part, place_ref, token_ref, *refs):
+    del token_ref
     z = place_ref[2]
     for c, out in enumerate(refs[count:]):
         for m in range(count):
@@ -59,22 +60,22 @@
             out[rows, :] = refs[m][c * part : (c + 1) * part, :]
 
 
-def pack(blocks, part, place):
+def pack(blocks, part, place, token):
     count = len(blocks)
     rows, depth = blocks[0].shape
     shape = jax.ShapeDtypeStruct((count * part, depth), blocks[0].dtype)
     return pl.pallas_call(
         functools.partial(pack_kernel, count, part),
-        in_specs=[SMEM] + [VMEM] * count,
+        in_specs=[SMEM, HBM] + [VMEM] * count,
         out_specs=[VMEM] * (rows // part),
         out_shape=[shape] * (rows // part),
         cost_estimate=SMALL,
         compiler_params=pltpu.CompilerParams(vmem_limit_bytes=2**20),
         name="pack",
-    )(place, *blocks)
-
-
-def split_kernel(step, whole_ref, high_ref, low_ref, buffer, sems):
+    )(place, token, *blocks)
+
+
+def split_kernel(step, whole_ref, high_ref, low_ref, token_ref, buffer, sems):
     count = whole_ref.shape[0] // step
 
     def copy(i):
@@ -83,6 +84,7 @@
         )
 
     copy(0).start()
+    token_ref[...] = jnp.zeros_like(token_ref)
     for i in range(count):
         if i + 1 < count:
             copy(i + 1).start()
@@ -100,9 +102,9 @@
     half = jax.ShapeDtypeStruct((rows, columns), jnp.bfloat16)
     return pl.pallas_call(
         functools.partial(split_kernel, step),
-        in_specs=[ANY],
-        out_specs=[VMEM, VMEM],
-        out_shape=[half, half],
+        in_specs=[HBM],
+        out_specs=[VMEM, VMEM, VMEM],
+        out_shape=[half, half, jax.ShapeDtypeStruct((8, 128), jnp.float32)],
         scratch_shapes=[
             pltpu.VMEM((2, step, columns), jnp.float32),
             pltpu.SemaphoreType.DMA((2,)),
@@ -168,7 +170,9 @@
             for blocks in targets
         ],
         scratch_shapes=[pltpu.VMEM((2 * total, depth), jnp.bfloat16)],
-        cost_estimate=SMALL,
+        cost_estimate=pl.CostEstimate(
+            flops=12 * total * depth * halves * columns, bytes_accessed=1, transcendentals=0
+        ),
         compiler_params=pltpu.CompilerParams(vmem_limit_bytes=8 * total * depth + 3 * 2**20),
         name="product",
     )(place, pattern, block_order, *lefts, *[part for pair in factors for part in pair])
@@ -235,6 +239,7 @@
         return lax.ppermute(value, "narrow", [(n, n ^ mask) for n in range(narrow_count)])
 
     last = []
+    token = []
 
     def ordered(*values):
         return list(lax.optimization_barrier((*values, *last))[: len(values)])
@@ -257,7 +262,7 @@
         spread[g] = [pieces[g][0]] + [along(send, n + 1) for n, send in enumerate(sends)]
 
     def pack_step(g):
-        packed = pack(ordered(*spread[g]), part, place)
+        packed = pack(ordered(*spread[g]), part, place, token[-1])
         mark(*packed)
         mine.update(zip(GROUPS[g], packed))
 
@@ -285,8 +290,8 @@
             layouts[chunk].append([(k | bit, 0, rows) for k in range(bit)])
 
     def split_step(half):
-        factors[half] = split(*ordered(integrals if half == 0 else swapped))
-        mark(*factors[half])
+        *factors[half], done = split(*ordered(integrals if half == 0 else swapped))
+        token.append(done)
 
     def multiply(unit):
         chunk, halves = UNITS[unit]
@@ -353,19 +358,19 @@
     gathers = [(chunk, number) for chunk in range(1, CHUNKS) for number in range(len(chip_bits))]
     spread_step(0)
     spread_step(1)
+    split_step(0)
     pack_step(0)
     gather_step(0, 0)
-    pack_step(1)
-    split_step(0)
     for number in range(1, len(chip_bits)):
         gather_step(0, number)
-    spread_step(2)
-    gather_step(*gathers.pop(0))
     for tick in range(len(UNITS) + len(steps) - 1):
         if tick < len(UNITS):
             multiply(tick)
             steps[0](tick)
             if tick == 0:
+                pack_step(1)
+                gather_step(*gathers.pop(0))
+                spread_step(2)
                 split_step(1)
                 pack_step(2)
             late = UNITS[tick + 1][0] if tick + 1 < len(UNITS) else 0

time: 172 us -> 171 us (level)
  starting transfers between devices: 55.2 us -> 64 us
  local copies, waits for them, and re-layouts: 16.5 us -> 7.94 us
    unnamed x43 -> x39, local copies, waits for them, and re-layouts: 16.2 us -> 7.59 us
    ppermute x27, starting transfers between devices: 25.6 us -> 30.2 us  [across(): lax.ppermute(value, 'wide', [(w, w ^ mask) for w in range(wide_count)])]
    ppermute x25, starting transfers between devices: 29.6 us -> 33.8 us  [along(): lax.ppermute(value, 'narrow', [(n, n ^ mask) for n in range(narrow_count)])]
  transfers between devices with their start and end apart: 52 -> 52, of which waited for: 24 -> 28; matrix products, arithmetic and copies ran while one was open for 1% -> 1% of each run, Pallas kernels for 14% -> 14%
where the time goes in v7:
time: 171 us
  waiting for transfers between devices  66 us (39%)
  starting transfers between devices  64 us (37%)
  Pallas kernels  31.4 us (18%)
  local copies, waits for them, and re-layouts  7.94 us (5%)
    ppermute x25, waiting for transfers between devices, along(): lax.ppermute(value, 'narrow', [(n, n ^ mask) for n in range(narrow_count)])  47.5 us
    ppermute x25, starting transfers between devices, along(): lax.ppermute(value, 'narrow', [(n, n ^ mask) for n in range(narrow_count)])  33.8 us
    ppermute x27, starting transfers between devices, across(): lax.ppermute(value, 'wide', [(w, w ^ mask) for w in range(wide_count)])  30.2 us
    pallas_call x8, Pallas kernels, product(): pl.pallas_call(functools.partial(product_kernel, count, rows, layout, tar...  19.7 us
    ppermute x27, waiting for transfers between devices, across(): lax.ppermute(value, 'wide', [(w, w ^ mask) for w in range(wide_count)])  18.5 us
    unnamed x39, local copies, waits for them, and re-layouts  7.59 us
    pallas_call x2, Pallas kernels, split(): pl.pallas_call(functools.partial(split_kernel, step), in_specs=[HBM], out...  7.55 us
  transfers between devices with their start and end apart: 52, of which 28 were waited for; matrix products, arithmetic and copies ran while one was open for 1% of the time, Pallas kernels for 14%

profile of v7, /device:TPU:0, one launch (start us, length us, event | category | flops | bytes accessed | tf_op | source)
XLA Modules:
  0.0 171.0 jit_solution(5360557535298042056)
XLA Ops:
  2.4 2.6 %collective-permute-start = (f32[8,2048]{1,0:T(8,128)S(1)}, f32[8,2048]{1,0:T(8,128)S(1)}, u32[]{:S(2)}, u32[]{:S(2)}) collective-permute-start(f32[8,2048]{1,0:T(8,128)S(1)} %get-tuple-element.174), channel_id=1, source_target_pairs={{0,1},{1,0},{2,3},{3,2},{4,5},{5,4},{6,7},{7,6},{8,9},{9,8},{10,11... | collective-permute-start | bytes 196616 | tf_op jit(solution)/shard_map/ppermute | solution.py:239
  5.0 2.6 %collective-permute-start.1 = (f32[8,2048]{1,0:T(8,128)S(1)}, f32[8,2048]{1,0:T(8,128)S(1)}, u32[]{:S(2)}, u32[]{:S(2)}) collective-permute-start(f32[8,2048]{1,0:T(8,128)S(1)} %get-tuple-element.175), channel_id=1, source_target_pairs={{0,2},{1,3},{2,0},{3,1},{4,6},{5,7},{6,4},{7,5},{8,10},{9,11},{10,... | collective-permute-start | bytes 196616 | tf_op jit(solution)/shard_map/ppermute | solution.py:239
  7.6 3.4 %copy-done = f32[2048,1024]{1,0:T(8,128)S(1)} copy-done((f32[2048,1024]{1,0:T(8,128)S(1)}, f32[2048,1024]{1,0:T(8,128)}, u32[]{:S(2)}) %copy-start) | copy-done | bytes 8388632
  17.4 4.2 %collective-permute-done.3.refs_1_ = f32[32,2048]{1,0:T(8,128)S(1)} collective-permute-done((f32[32,2048]{1,0:T(8,128)S(1)}, f32[32,2048]{1,0:T(8,128)S(1)}, u32[]{:S(2)}, u32[]{:S(2)}) %collective-permute-start.3) | collective-permute-done | bytes 262176 | tf_op jit(solution)/shard_map/ppermute | solution.py:233
  25.0 3.5 %collective-permute-start.10 = (f32[8,2048]{1,0:T(8,128)S(1)}, f32[8,2048]{1,0:T(8,128)S(1)}, u32[]{:S(2)}, u32[]{:S(2)}) collective-permute-start(f32[8,2048]{1,0:T(8,128)S(1)} %get-tuple-element.179), channel_id=1, source_target_pairs={{0,3},{1,2},{2,1},{3,0},{4,7},{5,6},{6,5},{7,4},{8,11},{9,10},{10,... | collective-permute-start | bytes 196616 | tf_op jit(solution)/shard_map/ppermute | solution.py:239
  30.2 2.5 %product.8 = (f32[64,1024]{1,0:T(8,128)S(1)}, f32[64,1024]{1,0:T(8,128)S(1)}) custom-call(s32[3]{0:T(128)S(1)} %pad_add_fusion.place_ref, s32[8,64]{1,0:T(8,128)S(1)} %copy-done.15, s32[8]{0:T(128)S(1)} %copy-done.16, f32[32,2048]{1,0:T(8,128)S(1)} %pack.3.refs_0_, f32[32,2048]{1,0:T(8,128)S(1)} %collective-permute-done.3.refs_1_, ...), custom_call_target="tpu_custom_call" | custom-call | flops 3221225472 | bytes 1 | tf_op jit(solution)/shard_map/product/pallas_call | solution.py:164
  40.2 2.7 %collective-permute-done.13.refs_1_ = f32[16,2048]{1,0:T(8,128)S(1)} collective-permute-done((f32[16,2048]{1,0:T(8,128)S(1)}, f32[16,2048]{1,0:T(8,128)S(1)}, u32[]{:S(2)}, u32[]{:S(2)}) %collective-permute-start.13) | collective-permute-done | bytes 131104 | tf_op jit(solution)/shard_map/ppermute | solution.py:239
  43.2 4.2 %collective-permute-done.14.refs_2_ = f32[16,2048]{1,0:T(8,128)S(1)} collective-permute-done((f32[16,2048]{1,0:T(8,128)S(1)}, f32[16,2048]{1,0:T(8,128)S(1)}, u32[]{:S(2)}, u32[]{:S(2)}) %collective-permute-start.14) | collective-permute-done | bytes 131104 | tf_op jit(solution)/shard_map/ppermute | solution.py:239
  47.5 5.8 %split.3 = (bf16[2048,1024]{1,0:T(8,128)(2,1)S(1)}, bf16[2048,1024]{1,0:T(8,128)(2,1)S(1)}, f32[8,128]{1,0:T(8,128)S(1)}) custom-call(f32[2048,1024]{1,0:T(8,128)} %collective-permute-done.12.whole_ref), custom_call_target="tpu_custom_call" | custom-call | flops 1 | bytes 1 | tf_op jit(solution)/shard_map/split/pallas_call | solution.py:103
  54.6 2.5 %product.9 = (f32[64,1024]{1,0:T(8,128)S(1)}, f32[64,1024]{1,0:T(8,128)S(1)}) custom-call(s32[3]{0:T(128)S(1)} %pad_add_fusion.place_ref, s32[8,64]{1,0:T(8,128)S(1)} %copy-done.15, s32[8]{0:T(128)S(1)} %copy-done.16, f32[32,2048]{1,0:T(8,128)S(1)} %pack.3.refs_0_, f32[32,2048]{1,0:T(8,128)S(1)} %collective-permute-done.3.refs_1_, ...), custom_call_target="tpu_custom_call" | custom-call | flops 3221225472 | bytes 1 | tf_op jit(solution)/shard_map/product/pallas_call | solution.py:164
  59.7 3.8 %collective-permute-done.16 = f32[64,1024]{1,0:T(8,128)S(1)} collective-permute-done((f32[64,1024]{1,0:T(8,128)S(1)}, f32[64,1024]{1,0:T(8,128)S(1)}, u32[]{:S(2)}, u32[]{:S(2)}) %collective-permute-start.16) | collective-permute-done | bytes 262176 | tf_op jit(solution)/shard_map/ppermute | solution.py:239
  63.6 2.5 %product.10 = (f32[64,1024]{1,0:T(8,128)S(1)}, f32[64,1024]{1,0:T(8,128)S(1)}) custom-call(s32[3]{0:T(128)S(1)} %pad_add_fusion.place_ref, s32[8,64]{1,0:T(8,128)S(1)} %copy-done.15, s32[8]{0:T(128)S(1)} %copy-done.16, f32[32,2048]{1,0:T(8,128)S(1)} %pack.4.refs_0_, f32[32,2048]{1,0:T(8,128)S(1)} %collective-permute-done.11.refs_1_, ...), custom_call_target="tpu_custom_call" | custom-call | flops 3221225472 | bytes 1 | tf_op jit(solution)/shard_map/product/pallas_call | solution.py:164
  66.2 2.5 %product.11 = (f32[64,1024]{1,0:T(8,128)S(1)}, f32[64,1024]{1,0:T(8,128)S(1)}) custom-call(s32[3]{0:T(128)S(1)} %pad_add_fusion.place_ref, s32[8,64]{1,0:T(8,128)S(1)} %copy-done.15, s32[8]{0:T(128)S(1)} %copy-done.16, f32[32,2048]{1,0:T(8,128)S(1)} %pack.4.refs_0_, f32[32,2048]{1,0:T(8,128)S(1)} %collective-permute-done.11.refs_1_, ...), custom_call_target="tpu_custom_call" | custom-call | flops 3221225472 | bytes 1 | tf_op jit(solution)/shard_map/product/pallas_call | solution.py:164
  69.4 4.4 %collective-permute-start.24 = (f32[64,1024]{1,0:T(8,128)S(1)}, f32[64,1024]{1,0:T(8,128)S(1)}, u32[]{:S(2)}, u32[]{:S(2)}) collective-permute-start(f32[64,1024]{1,0:T(8,128)S(1)} %broadcast_select_fusion.6), channel_id=1, source_target_pairs={{0,1},{1,0},{2,3},{3,2},{4,5},{5,4},{6,7},{7,6},{8,9},{9,8},{10,11... | collective-permute-start | bytes 786440 | tf_op jit(solution)/shard_map/ppermute | solution.py:239
  80.7 4.4 %collective-permute-start.28 = (f32[64,1024]{1,0:T(8,128)S(1)}, f32[64,1024]{1,0:T(8,128)S(1)}, u32[]{:S(2)}, u32[]{:S(2)}) collective-permute-start(f32[64,1024]{1,0:T(8,128)S(1)} %broadcast_select_fusion.5), channel_id=1, source_target_pairs={{0,1},{1,0},{2,3},{3,2},{4,5},{5,4},{6,7},{7,6},{8,9},{9,8},{10,11... | collective-permute-start | bytes 786440 | tf_op jit(solution)/shard_map/ppermute | solution.py:239
  86.1 3.8 %collective-permute-done.28 = f32[64,1024]{1,0:T(8,128)S(1)} collective-permute-done((f32[64,1024]{1,0:T(8,128)S(1)}, f32[64,1024]{1,0:T(8,128)S(1)}, u32[]{:S(2)}, u32[]{:S(2)}) %collective-permute-start.28) | collective-permute-done | bytes 262176 | tf_op jit(solution)/shard_map/ppermute | solution.py:239
  90.0 2.2 %copy-done.9 = bf16[2048,1024]{1,0:T(8,128)(2,1)S(1)} copy-done((bf16[2048,1024]{1,0:T(8,128)(2,1)S(1)}, bf16[2048,1024]{1,0:T(8,128)(2,1)}, u32[]{:S(2)}) %copy-start.9) | copy-done | bytes 4194328
  92.1 2.4 %product.12 = (f32[64,1024]{1,0:T(8,128)S(1)}, f32[64,1024]{1,0:T(8,128)S(1)}) custom-call(s32[3]{0:T(128)S(1)} %pad_add_fusion.place_ref, s32[8,64]{1,0:T(8,128)S(1)} %copy-done.15, s32[8]{0:T(128)S(1)} %copy-done.16, f32[32,2048]{1,0:T(8,128)S(1)} %get-tuple-element.271.refs_0_, f32[32,2048]{1,0:T(8,128)S(1)} %collective-permute-done.20.refs_1_, ...), custom_call_target="tpu_custom_call" | custom-call | flops 3221225472 | bytes 1 | tf_op jit(solution)/shard_map/product/pallas_call | solution.py:164
  95.6 2.5 %product.13 = (f32[64,1024]{1,0:T(8,128)S(1)}, f32[64,1024]{1,0:T(8,128)S(1)}) custom-call(s32[3]{0:T(128)S(1)} %pad_add_fusion.place_ref, s32[8,64]{1,0:T(8,128)S(1)} %copy-done.15, s32[8]{0:T(128)S(1)} %copy-done.16, f32[32,2048]{1,0:T(8,128)S(1)} %get-tuple-element.271.refs_0_, f32[32,2048]{1,0:T(8,128)S(1)} %collective-permute-done.20.refs_1_, ...), custom_call_target="tpu_custom_call" | custom-call | flops 3221225472 | bytes 1 | tf_op jit(solution)/shard_map/product/pallas_call | solution.py:164
  106.0 3.8 %collective-permute-done.26.refs_3_ = f32[32,1024]{1,0:T(8,128)S(1)} collective-permute-done((f32[32,1024]{1,0:T(8,128)S(1)}, f32[32,1024]{1,0:T(8,128)S(1)}, u32[]{:S(2)}, u32[]{:S(2)}) %collective-permute-start.26) | collective-permute-done | bytes 131104 | tf_op jit(solution)/shard_map/ppermute | solution.py:239
  110.6 2.3 %collective-permute-start.38 = (f32[64,1024]{1,0:T(8,128)S(1)}, f32[64,1024]{1,0:T(8,128)S(1)}, u32[]{:S(2)}, u32[]{:S(2)}) collective-permute-start(f32[64,1024]{1,0:T(8,128)S(1)} %broadcast_select_fusion.3), channel_id=1, source_target_pairs={{0,1},{1,0},{2,3},{3,2},{4,5},{5,4},{6,7},{7,6},{8,9},{9,8},{10,11... | collective-permute-start | bytes 786440 | tf_op jit(solution)/shard_map/ppermute | solution.py:239
  118.1 2.5 %product.14 = (f32[64,1024]{1,0:T(8,128)S(1)}, f32[64,1024]{1,0:T(8,128)S(1)}) custom-call(s32[3]{0:T(128)S(1)} %pad_add_fusion.place_ref, s32[8,64]{1,0:T(8,128)S(1)} %copy-done.15, s32[8]{0:T(128)S(1)} %copy-done.16, f32[32,2048]{1,0:T(8,128)S(1)} %get-tuple-element.300.refs_0_, f32[32,2048]{1,0:T(8,128)S(1)} %collective-permute-done.29.refs_1_, ...), custom_call_target="tpu_custom_call" | custom-call | flops 3221225472 | bytes 1 | tf_op jit(solution)/shard_map/product/pallas_call | solution.py:164
  120.6 2.5 %collective-permute-start.41 = (f32[64,1024]{1,0:T(8,128)S(1)}, f32[64,1024]{1,0:T(8,128)S(1)}, u32[]{:S(2)}, u32[]{:S(2)}) collective-permute-start(f32[64,1024]{1,0:T(8,128)S(1)} %get-tuple-element.292), channel_id=1, source_target_pairs={{0,8},{4,12},{8,0},{12,4},{16,24},{20,28},{24,16},{28,20},{1,9},{5... | collective-permute-start | bytes 786440 | tf_op jit(solution)/shard_map/ppermute | solution.py:233
  124.4 3.0 %collective-permute-start.39 = (f32[32,1024]{1,0:T(8,128)S(1)}, f32[32,1024]{1,0:T(8,128)S(1)}, u32[]{:S(2)}, u32[]{:S(2)}) collective-permute-start(f32[32,1024]{1,0:T(8,128)S(1)} %get-tuple-element.346), channel_id=1, source_target_pairs={{0,16},{4,20},{8,24},{12,28},{16,0},{20,4},{24,8},{28,12},{1,17},{... | collective-permute-start | bytes 393224 | tf_op jit(solution)/shard_map/ppermute | solution.py:233
  127.7 2.5 %product.15 = (f32[64,1024]{1,0:T(8,128)S(1)}, f32[64,1024]{1,0:T(8,128)S(1)}) custom-call(s32[3]{0:T(128)S(1)} %pad_add_fusion.place_ref, s32[8,64]{1,0:T(8,128)S(1)} %copy-done.15, s32[8]{0:T(128)S(1)} %copy-done.16, f32[32,2048]{1,0:T(8,128)S(1)} %get-tuple-element.300.refs_0_, f32[32,2048]{1,0:T(8,128)S(1)} %collective-permute-done.29.refs_1_, ...), custom_call_target="tpu_custom_call" | custom-call | flops 3221225472 | bytes 1 | tf_op jit(solution)/shard_map/product/pallas_call | solution.py:164
  132.5 5.5 %collective-permute-done.42 = f32[64,1024]{1,0:T(8,128)S(1)} collective-permute-done((f32[64,1024]{1,0:T(8,128)S(1)}, f32[64,1024]{1,0:T(8,128)S(1)}, u32[]{:S(2)}, u32[]{:S(2)}) %collective-permute-start.42) | collective-permute-done | bytes 262176 | tf_op jit(solution)/shard_map/ppermute | solution.py:239
  140.1 3.0 %collective-permute-done.43 = f32[32,1024]{1,0:T(8,128)S(1)} collective-permute-done((f32[32,1024]{1,0:T(8,128)S(1)}, f32[32,1024]{1,0:T(8,128)S(1)}, u32[]{:S(2)}, u32[]{:S(2)}) %collective-permute-start.43) | collective-permute-done | bytes 131104 | tf_op jit(solution)/shard_map/ppermute | solution.py:233
  143.2 4.0 %collective-permute-done.46 = f32[64,1024]{1,0:T(8,128)S(1)} collective-permute-done((f32[64,1024]{1,0:T(8,128)S(1)}, f32[64,1024]{1,0:T(8,128)S(1)}, u32[]{:S(2)}, u32[]{:S(2)}) %collective-permute-start.46) | collective-permute-done | bytes 262176 | tf_op jit(solution)/shard_map/ppermute | solution.py:239
  147.2 2.3 %collective-permute-start.47 = (f32[32,1024]{1,0:T(8,128)S(1)}, f32[32,1024]{1,0:T(8,128)S(1)}, u32[]{:S(2)}, u32[]{:S(2)}) collective-permute-start(f32[32,1024]{1,0:T(8,128)S(1)} %get-tuple-element.338), channel_id=1, source_target_pairs={{0,16},{4,20},{8,24},{12,28},{16,0},{20,4},{24,8},{28,12},{1,17},{... | collective-permute-start | bytes 393224 | tf_op jit(solution)/shard_map/ppermute | solution.py:233
  154.6 3.0 %collective-permute-done.49 = f32[64,1024]{1,0:T(8,128)S(1)} collective-permute-done((f32[64,1024]{1,0:T(8,128)S(1)}, f32[64,1024]{1,0:T(8,128)S(1)}, u32[]{:S(2)}, u32[]{:S(2)}) %collective-permute-start.49) | collective-permute-done | bytes 262176 | tf_op jit(solution)/shard_map/ppermute | solution.py:239
  159.8 2.9 %collective-permute-done.50 = f32[32,1024]{1,0:T(8,128)S(1)} collective-permute-done((f32[32,1024]{1,0:T(8,128)S(1)}, f32[32,1024]{1,0:T(8,128)S(1)}, u32[]{:S(2)}, u32[]{:S(2)}) %collective-permute-start.50) | collective-permute-done | bytes 131104 | tf_op jit(solution)/shard_map/ppermute | solution.py:233
  162.9 6.3 %collective-permute-done.51.refs_15_ = f32[32,1024]{1,0:T(8,128)S(1)} collective-permute-done((f32[32,1024]{1,0:T(8,128)S(1)}, f32[32,1024]{1,0:T(8,128)S(1)}, u32[]{:S(2)}, u32[]{:S(2)}) %collective-permute-start.51) | collective-permute-done | bytes 131104 | tf_op jit(solution)/shard_map/ppermute | solution.py:239
  (165 shorter events, 64.5 us)
Async XLA Ops:
  0.0 47.5 %collective-permute-start.12 = (f32[2048,1024]{1,0:T(8,128)}, f32[2048,1024]{1,0:T(8,128)}, u32[]{:S(2)}, u32[]{:S(2)}) collective-permute-start(f32[2048,1024]{1,0:T(8,128)} %whole_ref.2), channel_id=1, source_target_pairs={{0,4},{4,0},{8,12},{12,8},{16,20},{20,16},{24,28},{28,24},{1,5},{5... | collective-permute-start | bytes 25165832 | tf_op jit(solution)/shard_map/ppermute | solution.py:233
  2.4 10.4 %collective-permute-start = (f32[8,2048]{1,0:T(8,128)S(1)}, f32[8,2048]{1,0:T(8,128)S(1)}, u32[]{:S(2)}, u32[]{:S(2)}) collective-permute-start(f32[8,2048]{1,0:T(8,128)S(1)} %get-tuple-element.174), channel_id=1, source_target_pairs={{0,1},{1,0},{2,3},{3,2},{4,5},{5,4},{6,7},{7,6},{8,9},{9,8},{10,11... | collective-permute-start | bytes 196616 | tf_op jit(solution)/shard_map/ppermute | solution.py:239
  5.0 7.7 %collective-permute-start.1 = (f32[8,2048]{1,0:T(8,128)S(1)}, f32[8,2048]{1,0:T(8,128)S(1)}, u32[]{:S(2)}, u32[]{:S(2)}) collective-permute-start(f32[8,2048]{1,0:T(8,128)S(1)} %get-tuple-element.175), channel_id=1, source_target_pairs={{0,2},{1,3},{2,0},{3,1},{4,6},{5,7},{6,4},{7,5},{8,10},{9,11},{10,... | collective-permute-start | bytes 196616 | tf_op jit(solution)/shard_map/ppermute | solution.py:239
  25.0 7.7 %collective-permute-start.10 = (f32[8,2048]{1,0:T(8,128)S(1)}, f32[8,2048]{1,0:T(8,128)S(1)}, u32[]{:S(2)}, u32[]{:S(2)}) collective-permute-start(f32[8,2048]{1,0:T(8,128)S(1)} %get-tuple-element.179), channel_id=1, source_target_pairs={{0,3},{1,2},{2,1},{3,0},{4,7},{5,6},{6,5},{7,4},{8,11},{9,10},{10,... | collective-permute-start | bytes 196616 | tf_op jit(solution)/shard_map/ppermute | solution.py:239
  34.3 19.7 %collective-permute-start.11 = (f32[32,2048]{1,0:T(8,128)S(1)}, f32[32,2048]{1,0:T(8,128)S(1)}, u32[]{:S(2)}, u32[]{:S(2)}) collective-permute-start(f32[32,2048]{1,0:T(8,128)S(1)} %pack.4.refs_0_), channel_id=1, source_target_pairs={{0,8},{4,12},{8,0},{12,4},{16,24},{20,28},{24,16},{28,20},{1,9},{5... | collective-permute-start | bytes 786440 | tf_op jit(solution)/shard_map/ppermute | solution.py:233
  37.8 9.6 %collective-permute-start.14 = (f32[16,2048]{1,0:T(8,128)S(1)}, f32[16,2048]{1,0:T(8,128)S(1)}, u32[]{:S(2)}, u32[]{:S(2)}) collective-permute-start(f32[16,2048]{1,0:T(8,128)S(1)} %get-tuple-element.210), channel_id=1, source_target_pairs={{0,2},{1,3},{2,0},{3,1},{4,6},{5,7},{6,4},{7,5},{8,10},{9,11},{10,... | collective-permute-start | bytes 393224 | tf_op jit(solution)/shard_map/ppermute | solution.py:239
  39.0 8.5 %collective-permute-start.15 = (f32[16,2048]{1,0:T(8,128)S(1)}, f32[16,2048]{1,0:T(8,128)S(1)}, u32[]{:S(2)}, u32[]{:S(2)}) collective-permute-start(f32[16,2048]{1,0:T(8,128)S(1)} %get-tuple-element.211), channel_id=1, source_target_pairs={{0,3},{1,2},{2,1},{3,0},{4,7},{5,6},{6,5},{7,4},{8,11},{9,10},{10,... | collective-permute-start | bytes 393224 | tf_op jit(solution)/shard_map/ppermute | solution.py:239
  42.9 14.2 %collective-permute-start.7 = (f32[64,1024]{1,0:T(8,128)S(1)}, f32[64,1024]{1,0:T(8,128)S(1)}, u32[]{:S(2)}, u32[]{:S(2)}) collective-permute-start(f32[64,1024]{1,0:T(8,128)S(1)} %get-tuple-element.199), channel_id=1, source_target_pairs={{0,8},{4,12},{8,0},{12,4},{16,24},{20,28},{24,16},{28,20},{1,9},{5... | collective-permute-start | bytes 786440 | tf_op jit(solution)/shard_map/ppermute | solution.py:233
  54.0 9.6 %collective-permute-start.17 = (f32[64,2048]{1,0:T(8,128)S(1)}, f32[64,2048]{1,0:T(8,128)S(1)}, u32[]{:S(2)}, u32[]{:S(2)}) collective-permute-start(f32[64,2048]{1,0:T(8,128)S(1)} %constant_dynamic-update-slice_fusion), channel_id=1, source_target_pairs={{0,16},{4,20},{8,24},{12,28},{16,0},{20,4},{24,8},{28,12},{1,17},{... | collective-permute-start | bytes 1572872 | tf_op jit(solution)/shard_map/ppermute | solution.py:233
  68.7 8.4 %collective-permute-start.20 = (f32[32,2048]{1,0:T(8,128)S(1)}, f32[32,2048]{1,0:T(8,128)S(1)}, u32[]{:S(2)}, u32[]{:S(2)}) collective-permute-start(f32[32,2048]{1,0:T(8,128)S(1)} %get-tuple-element.271.refs_0_), channel_id=1, source_target_pairs={{0,8},{4,12},{8,0},{12,4},{16,24},{20,28},{24,16},{28,20},{1,9},{5... | collective-permute-start | bytes 786440 | tf_op jit(solution)/shard_map/ppermute | solution.py:233
  69.4 10.9 %collective-permute-start.24 = (f32[64,1024]{1,0:T(8,128)S(1)}, f32[64,1024]{1,0:T(8,128)S(1)}, u32[]{:S(2)}, u32[]{:S(2)}) collective-permute-start(f32[64,1024]{1,0:T(8,128)S(1)} %broadcast_select_fusion.6), channel_id=1, source_target_pairs={{0,1},{1,0},{2,3},{3,2},{4,5},{5,4},{6,7},{7,6},{8,9},{9,8},{10,11... | collective-permute-start | bytes 786440 | tf_op jit(solution)/shard_map/ppermute | solution.py:239
  77.1 12.8 %collective-permute-start.22 = (f32[64,2048]{1,0:T(8,128)S(1)}, f32[64,2048]{1,0:T(8,128)S(1)}, u32[]{:S(2)}, u32[]{:S(2)}) collective-permute-start(f32[64,2048]{1,0:T(8,128)S(1)} %constant_dynamic-update-slice_fusion.2), channel_id=1, source_target_pairs={{0,16},{4,20},{8,24},{12,28},{16,0},{20,4},{24,8},{28,12},{1,17},{... | collective-permute-start | bytes 1572872 | tf_op jit(solution)/shard_map/ppermute | solution.py:233
  80.7 9.1 %collective-permute-start.28 = (f32[64,1024]{1,0:T(8,128)S(1)}, f32[64,1024]{1,0:T(8,128)S(1)}, u32[]{:S(2)}, u32[]{:S(2)}) collective-permute-start(f32[64,1024]{1,0:T(8,128)S(1)} %broadcast_select_fusion.5), channel_id=1, source_target_pairs={{0,1},{1,0},{2,3},{3,2},{4,5},{5,4},{6,7},{7,6},{8,9},{9,8},{10,11... | collective-permute-start | bytes 786440 | tf_op jit(solution)/shard_map/ppermute | solution.py:239
  85.2 9.7 %collective-permute-start.27 = (f32[64,1024]{1,0:T(8,128)S(1)}, f32[64,1024]{1,0:T(8,128)S(1)}, u32[]{:S(2)}, u32[]{:S(2)}) collective-permute-start(f32[64,1024]{1,0:T(8,128)S(1)} %get-tuple-element.249), channel_id=1, source_target_pairs={{0,8},{4,12},{8,0},{12,4},{16,24},{20,28},{24,16},{28,20},{1,9},{5... | collective-permute-start | bytes 786440 | tf_op jit(solution)/shard_map/ppermute | solution.py:233
  85.8 8.8 %collective-permute-start.21 = (f32[32,1024]{1,0:T(8,128)S(1)}, f32[32,1024]{1,0:T(8,128)S(1)}, u32[]{:S(2)}, u32[]{:S(2)}) collective-permute-start(f32[32,1024]{1,0:T(8,128)S(1)} %get-tuple-element.359), channel_id=1, source_target_pairs={{0,2},{1,3},{2,0},{3,1},{4,6},{5,7},{6,4},{7,5},{8,10},{9,11},{10,... | collective-permute-start | bytes 393224 | tf_op jit(solution)/shard_map/ppermute | solution.py:239
  85.8 8.8 %collective-permute-start.25 = (f32[32,1024]{1,0:T(8,128)S(1)}, f32[32,1024]{1,0:T(8,128)S(1)}, u32[]{:S(2)}, u32[]{:S(2)}) collective-permute-start(f32[32,1024]{1,0:T(8,128)S(1)} %get-tuple-element.358), channel_id=1, source_target_pairs={{0,16},{4,20},{8,24},{12,28},{16,0},{20,4},{24,8},{28,12},{1,17},{... | collective-permute-start | bytes 393224 | tf_op jit(solution)/shard_map/ppermute | solution.py:233
  99.1 10.7 %collective-permute-start.34 = (f32[64,1024]{1,0:T(8,128)S(1)}, f32[64,1024]{1,0:T(8,128)S(1)}, u32[]{:S(2)}, u32[]{:S(2)}) collective-permute-start(f32[64,1024]{1,0:T(8,128)S(1)} %broadcast_select_fusion.4), channel_id=1, source_target_pairs={{0,1},{1,0},{2,3},{3,2},{4,5},{5,4},{6,7},{7,6},{8,9},{9,8},{10,11... | collective-permute-start | bytes 786440 | tf_op jit(solution)/shard_map/ppermute | solution.py:239
  101.0 8.8 %collective-permute-start.26 = (f32[32,1024]{1,0:T(8,128)S(1)}, f32[32,1024]{1,0:T(8,128)S(1)}, u32[]{:S(2)}, u32[]{:S(2)}) collective-permute-start(f32[32,1024]{1,0:T(8,128)S(1)} %get-tuple-element.355), channel_id=1, source_target_pairs={{0,2},{1,3},{2,0},{3,1},{4,6},{5,7},{6,4},{7,5},{8,10},{9,11},{10,... | collective-permute-start | bytes 393224 | tf_op jit(solution)/shard_map/ppermute | solution.py:239
  101.0 8.8 %collective-permute-start.30 = (f32[32,1024]{1,0:T(8,128)S(1)}, f32[32,1024]{1,0:T(8,128)S(1)}, u32[]{:S(2)}, u32[]{:S(2)}) collective-permute-start(f32[32,1024]{1,0:T(8,128)S(1)} %get-tuple-element.354), channel_id=1, source_target_pairs={{0,16},{4,20},{8,24},{12,28},{16,0},{20,4},{24,8},{28,12},{1,17},{... | collective-permute-start | bytes 393224 | tf_op jit(solution)/shard_map/ppermute | solution.py:233
  101.7 8.9 %collective-permute-start.33 = (f32[64,1024]{1,0:T(8,128)S(1)}, f32[64,1024]{1,0:T(8,128)S(1)}, u32[]{:S(2)}, u32[]{:S(2)}) collective-permute-start(f32[64,1024]{1,0:T(8,128)S(1)} %get-tuple-element.263), channel_id=1, source_target_pairs={{0,8},{4,12},{8,0},{12,4},{16,24},{20,28},{24,16},{28,20},{1,9},{5... | collective-permute-start | bytes 786440 | tf_op jit(solution)/shard_map/ppermute | solution.py:233
  104.9 13.2 %collective-permute-start.32 = (f32[64,2048]{1,0:T(8,128)S(1)}, f32[64,2048]{1,0:T(8,128)S(1)}, u32[]{:S(2)}, u32[]{:S(2)}) collective-permute-start(f32[64,2048]{1,0:T(8,128)S(1)} %constant_dynamic-update-slice_fusion.4), channel_id=1, source_target_pairs={{0,16},{4,20},{8,24},{12,28},{16,0},{20,4},{24,8},{28,12},{1,17},{... | collective-permute-start | bytes 1572872 | tf_op jit(solution)/shard_map/ppermute | solution.py:233
  110.6 7.4 %collective-permute-start.38 = (f32[64,1024]{1,0:T(8,128)S(1)}, f32[64,1024]{1,0:T(8,128)S(1)}, u32[]{:S(2)}, u32[]{:S(2)}) collective-permute-start(f32[64,1024]{1,0:T(8,128)S(1)} %broadcast_select_fusion.3), channel_id=1, source_target_pairs={{0,1},{1,0},{2,3},{3,2},{4,5},{5,4},{6,7},{7,6},{8,9},{9,8},{10,11... | collective-permute-start | bytes 786440 | tf_op jit(solution)/shard_map/ppermute | solution.py:239
  112.9 14.4 %collective-permute-start.37 = (f32[64,1024]{1,0:T(8,128)S(1)}, f32[64,1024]{1,0:T(8,128)S(1)}, u32[]{:S(2)}, u32[]{:S(2)}) collective-permute-start(f32[64,1024]{1,0:T(8,128)S(1)} %get-tuple-element.276), channel_id=1, source_target_pairs={{0,8},{4,12},{8,0},{12,4},{16,24},{20,28},{24,16},{28,20},{1,9},{5... | collective-permute-start | bytes 786440 | tf_op jit(solution)/shard_map/ppermute | solution.py:233
  114.5 9.8 %collective-permute-start.31 = (f32[32,1024]{1,0:T(8,128)S(1)}, f32[32,1024]{1,0:T(8,128)S(1)}, u32[]{:S(2)}, u32[]{:S(2)}) collective-permute-start(f32[32,1024]{1,0:T(8,128)S(1)} %get-tuple-element.351), channel_id=1, source_target_pairs={{0,2},{1,3},{2,0},{3,1},{4,6},{5,7},{6,4},{7,5},{8,10},{9,11},{10,... | collective-permute-start | bytes 393224 | tf_op jit(solution)/shard_map/ppermute | solution.py:239
  114.5 9.8 %collective-permute-start.35 = (f32[32,1024]{1,0:T(8,128)S(1)}, f32[32,1024]{1,0:T(8,128)S(1)}, u32[]{:S(2)}, u32[]{:S(2)}) collective-permute-start(f32[32,1024]{1,0:T(8,128)S(1)} %get-tuple-element.350), channel_id=1, source_target_pairs={{0,16},{4,20},{8,24},{12,28},{16,0},{20,4},{24,8},{28,12},{1,17},{... | collective-permute-start | bytes 393224 | tf_op jit(solution)/shard_map/ppermute | solution.py:233
  120.6 18.1 %collective-permute-start.41 = (f32[64,1024]{1,0:T(8,128)S(1)}, f32[64,1024]{1,0:T(8,128)S(1)}, u32[]{:S(2)}, u32[]{:S(2)}) collective-permute-start(f32[64,1024]{1,0:T(8,128)S(1)} %get-tuple-element.292), channel_id=1, source_target_pairs={{0,8},{4,12},{8,0},{12,4},{16,24},{20,28},{24,16},{28,20},{1,9},{5... | collective-permute-start | bytes 786440 | tf_op jit(solution)/shard_map/ppermute | solution.py:233
  127.4 10.6 %collective-permute-start.42 = (f32[64,1024]{1,0:T(8,128)S(1)}, f32[64,1024]{1,0:T(8,128)S(1)}, u32[]{:S(2)}, u32[]{:S(2)}) collective-permute-start(f32[64,1024]{1,0:T(8,128)S(1)} %broadcast_select_fusion.2), channel_id=1, source_target_pairs={{0,1},{1,0},{2,3},{3,2},{4,5},{5,4},{6,7},{7,6},{8,9},{9,8},{10,11... | collective-permute-start | bytes 786440 | tf_op jit(solution)/shard_map/ppermute | solution.py:239
  131.6 8.5 %collective-permute-start.40 = (f32[32,1024]{1,0:T(8,128)S(1)}, f32[32,1024]{1,0:T(8,128)S(1)}, u32[]{:S(2)}, u32[]{:S(2)}) collective-permute-start(f32[32,1024]{1,0:T(8,128)S(1)} %get-tuple-element.343), channel_id=1, source_target_pairs={{0,2},{1,3},{2,0},{3,1},{4,6},{5,7},{6,4},{7,5},{8,10},{9,11},{10,... | collective-permute-start | bytes 393224 | tf_op jit(solution)/shard_map/ppermute | solution.py:239
  138.7 8.4 %collective-permute-start.46 = (f32[64,1024]{1,0:T(8,128)S(1)}, f32[64,1024]{1,0:T(8,128)S(1)}, u32[]{:S(2)}, u32[]{:S(2)}) collective-permute-start(f32[64,1024]{1,0:T(8,128)S(1)} %broadcast_select_fusion.1), channel_id=1, source_target_pairs={{0,1},{1,0},{2,3},{3,2},{4,5},{5,4},{6,7},{7,6},{8,9},{9,8},{10,11... | collective-permute-start | bytes 786440 | tf_op jit(solution)/shard_map/ppermute | solution.py:239
  139.0 10.5 %collective-permute-start.45 = (f32[64,1024]{1,0:T(8,128)S(1)}, f32[64,1024]{1,0:T(8,128)S(1)}, u32[]{:S(2)}, u32[]{:S(2)}) collective-permute-start(f32[64,1024]{1,0:T(8,128)S(1)} %get-tuple-element.305), channel_id=1, source_target_pairs={{0,8},{4,12},{8,0},{12,4},{16,24},{20,28},{24,16},{28,20},{1,9},{5... | collective-permute-start | bytes 786440 | tf_op jit(solution)/shard_map/ppermute | solution.py:233
  143.1 7.8 %collective-permute-start.44 = (f32[32,1024]{1,0:T(8,128)S(1)}, f32[32,1024]{1,0:T(8,128)S(1)}, u32[]{:S(2)}, u32[]{:S(2)}) collective-permute-start(f32[32,1024]{1,0:T(8,128)S(1)} %get-tuple-element.339), channel_id=1, source_target_pairs={{0,2},{1,3},{2,0},{3,1},{4,6},{5,7},{6,4},{7,5},{8,10},{9,11},{10,... | collective-permute-start | bytes 393224 | tf_op jit(solution)/shard_map/ppermute | solution.py:239
  149.6 8.1 %collective-permute-start.49 = (f32[64,1024]{1,0:T(8,128)S(1)}, f32[64,1024]{1,0:T(8,128)S(1)}, u32[]{:S(2)}, u32[]{:S(2)}) collective-permute-start(f32[64,1024]{1,0:T(8,128)S(1)} %broadcast_select_fusion), channel_id=1, source_target_pairs={{0,1},{1,0},{2,3},{3,2},{4,5},{5,4},{6,7},{7,6},{8,9},{9,8},{10,11... | collective-permute-start | bytes 786440 | tf_op jit(solution)/shard_map/ppermute | solution.py:239
  (38 other events, 407.4 us)

commit v8 on v7

--- a/solution.py
+++ b/solution.py
@@ -12,6 +12,13 @@
 CORES = 2
 GROUPS = ((0,), (1,), (2, 3))
 UNITS = tuple((chunk, (half,)) for chunk in range(CHUNKS) for half in range(CORES))
+
+ORDER = (
+    "s0", "f0", "s1", "p0", "g00", "s2", "g01", "p1", "g10", "e0", "f1", "g11", "p2", "e1",
+    "g20", "r0", "r1", "g30", "x0", "g21", "e3", "x1", "g31", "e2", "z0", "r3", "e5", "z1",
+    "r2", "l0", "e4", "x3", "r5", "l1", "e6", "z3", "x2", "r4", "e7", "x5", "z2", "r6", "l3",
+    "x4", "z5", "r7", "l2", "z4", "x6", "l5", "z6", "x7", "l4", "z7", "l6", "l7",
+)
 
 SMEM = pl.BlockSpec(memory_space=pltpu.SMEM)
 VMEM = pl.BlockSpec(memory_space=pltpu.VMEM)
@@ -355,30 +362,30 @@
         steps.append(functools.partial(reduce_step, bit=bit, narrow_bit=narrow_bit))
     steps.append(land)
 
-    gathers = [(chunk, number) for chunk in range(1, CHUNKS) for number in range(len(chip_bits))]
-    spread_step(0)
-    spread_step(1)
-    split_step(0)
-    pack_step(0)
-    gather_step(0, 0)
-    for number in range(1, len(chip_bits)):
-        gather_step(0, number)
-    for tick in range(len(UNITS) + len(steps) - 1):
-        if tick < len(UNITS):
-            multiply(tick)
-            steps[0](tick)
-            if tick == 0:
-                pack_step(1)
-                gather_step(*gathers.pop(0))
-                spread_step(2)
-                split_step(1)
-                pack_step(2)
-            late = UNITS[tick + 1][0] if tick + 1 < len(UNITS) else 0
-            while gathers and (gathers[0][0] <= late or tick % CORES == gathers[0][1] - 1):
-                gather_step(*gathers.pop(0))
-        for number in (*range(len(steps) - 1, 1, -1), 1):
-            if 0 <= tick - number < len(UNITS):
-                steps[number](tick - number)
+    def send_step(unit):
+        multiply(unit)
+        steps[0](unit)
+
+    if chips == 4 and narrow_count == 4:
+        actions = dict(s=spread_step, p=pack_step, f=split_step, g=gather_step, e=send_step)
+        actions.update(r=steps[1], x=steps[2], z=steps[3], l=steps[4])
+        for name in ORDER:
+            actions[name[0]](*[int(number) for number in name[1:]])
+    else:
+        for half in range(CORES):
+            split_step(half)
+        for g in range(len(GROUPS)):
+            spread_step(g)
+            pack_step(g)
+        for chunk in range(CHUNKS):
+            for number in range(len(chip_bits)):
+                gather_step(chunk, number)
+        for tick in range(len(UNITS) + len(steps) - 1):
+            if tick < len(UNITS):
+                send_step(tick)
+            for number in range(len(steps) - 1, 0, -1):
+                if 0 <= tick - number < len(UNITS):
+                    steps[number](tick - number)
 
     spec = [(*UNITS[unit], s) for unit in range(len(UNITS)) for s in range(group)]
     pairs = [state[unit][s] for unit in range(len(UNITS)) for s in range(group)]

time: 171 us -> 160 us (0.936)
  waiting for transfers between devices: 66 us -> 51.6 us
  local copies, waits for them, and re-layouts: 7.94 us -> 18.9 us
  starting transfers between devices: 64 us -> 55 us
    ppermute x25, waiting for transfers between devices: 47.5 us -> 27.4 us  [along(): lax.ppermute(value, 'narrow', [(n, n ^ mask) for n in range(narrow_count)])]
    unnamed x39 -> x43, local copies, waits for them, and re-layouts: 7.59 us -> 18.5 us
    ppermute x25, starting transfers between devices: 33.8 us -> 25.4 us  [along(): lax.ppermute(value, 'narrow', [(n, n ^ mask) for n in range(narrow_count)])]
    ppermute x27, waiting for transfers between devices: 18.5 us -> 24.3 us  [across(): lax.ppermute(value, 'wide', [(w, w ^ mask) for w in range(wide_count)])]
  transfers between devices with their start and end apart: 52 -> 52, of which waited for: 28 -> 21; matrix products, arithmetic and copies ran while one was open for 1% -> 1% of each run, Pallas kernels for 14% -> 19%
where the time goes in v8:
time: 160 us; the launch traced here: 159 us
  starting transfers between devices  55 us (34%)
  waiting for transfers between devices  51.6 us (32%)
  Pallas kernels  31.3 us (20%)
  local copies, waits for them, and re-layouts  18.9 us (12%)
  other arithmetic  1.84 us (1%)
    ppermute x27, starting transfers between devices, across(): lax.ppermute(value, 'wide', [(w, w ^ mask) for w in range(wide_count)])  29.5 us
    ppermute x25, waiting for transfers between devices, along(): lax.ppermute(value, 'narrow', [(n, n ^ mask) for n in range(narrow_count)])  27.4 us
    ppermute x25, starting transfers between devices, along(): lax.ppermute(value, 'narrow', [(n, n ^ mask) for n in range(narrow_count)])  25.4 us
    ppermute x27, waiting for transfers between devices, across(): lax.ppermute(value, 'wide', [(w, w ^ mask) for w in range(wide_count)])  24.3 us
    pallas_call x8, Pallas kernels, product(): pl.pallas_call(functools.partial(product_kernel, count, rows, layout, tar...  19.7 us
    unnamed x43, local copies, waits for them, and re-layouts  18.5 us
    pallas_call x2, Pallas kernels, split(): pl.pallas_call(functools.partial(split_kernel, step), in_specs=[HBM], out...  7.55 us
  transfers between devices with their start and end apart: 52, of which 21 were waited for; matrix products, arithmetic and copies ran while one was open for 1% of the time, Pallas kernels for 19%

profile of v8, /device:TPU:0, one launch (start us, length us, event | category | flops | bytes accessed | tf_op | source)
XLA Modules:
  0.0 159.3 jit_solution(15559336968618298656)
XLA Ops:
  2.4 2.6 %collective-permute-start = (f32[8,2048]{1,0:T(8,128)S(1)}, f32[8,2048]{1,0:T(8,128)S(1)}, u32[]{:S(2)}, u32[]{:S(2)}) collective-permute-start(f32[8,2048]{1,0:T(8,128)S(1)} %get-tuple-element.171), channel_id=1, source_target_pairs={{0,1},{1,0},{2,3},{3,2},{4,5},{5,4},{6,7},{7,6},{8,9},{9,8},{10,11... | collective-permute-start | bytes 196616 | tf_op jit(solution)/shard_map/ppermute | solution.py:246
  5.0 2.6 %collective-permute-start.1 = (f32[8,2048]{1,0:T(8,128)S(1)}, f32[8,2048]{1,0:T(8,128)S(1)}, u32[]{:S(2)}, u32[]{:S(2)}) collective-permute-start(f32[8,2048]{1,0:T(8,128)S(1)} %get-tuple-element.172), channel_id=1, source_target_pairs={{0,2},{1,3},{2,0},{3,1},{4,6},{5,7},{6,4},{7,5},{8,10},{9,11},{10,... | collective-permute-start | bytes 196616 | tf_op jit(solution)/shard_map/ppermute | solution.py:246
  7.6 3.4 %copy-done = f32[2048,1024]{1,0:T(8,128)S(1)} copy-done((f32[2048,1024]{1,0:T(8,128)S(1)}, f32[2048,1024]{1,0:T(8,128)}, u32[]{:S(2)}) %copy-start) | copy-done | bytes 8388632
  12.7 2.1 %copy-done.4 = bf16[2048,1024]{1,0:T(8,128)(2,1)} copy-done((bf16[2048,1024]{1,0:T(8,128)(2,1)}, bf16[2048,1024]{1,0:T(8,128)(2,1)S(1)}, u32[]{:S(2)}) %copy-start.4) | copy-done | bytes 4194328
  21.3 4.2 %collective-permute-done.3.refs_1_ = f32[32,2048]{1,0:T(8,128)S(1)} collective-permute-done((f32[32,2048]{1,0:T(8,128)S(1)}, f32[32,2048]{1,0:T(8,128)S(1)}, u32[]{:S(2)}, u32[]{:S(2)}) %collective-permute-start.3) | collective-permute-done | bytes 262176 | tf_op jit(solution)/shard_map/ppermute | solution.py:240
  32.6 3.1 %collective-permute-done.8.refs_2_ = f32[8,2048]{1,0:T(8,128)S(1)} collective-permute-done((f32[8,2048]{1,0:T(8,128)S(1)}, f32[8,2048]{1,0:T(8,128)S(1)}, u32[]{:S(2)}, u32[]{:S(2)}) %collective-permute-start.8) | collective-permute-done | bytes 65568 | tf_op jit(solution)/shard_map/ppermute | solution.py:246
  38.9 2.5 %collective-permute-start.14 = (f32[16,2048]{1,0:T(8,128)S(1)}, f32[16,2048]{1,0:T(8,128)S(1)}, u32[]{:S(2)}, u32[]{:S(2)}) collective-permute-start(f32[16,2048]{1,0:T(8,128)S(1)} %get-tuple-element.193), channel_id=1, source_target_pairs={{0,3},{1,2},{2,1},{3,0},{4,7},{5,6},{6,5},{7,4},{8,11},{9,10},{10,... | collective-permute-start | bytes 393224 | tf_op jit(solution)/shard_map/ppermute | solution.py:246
  42.9 2.2 %copy-done.5 = bf16[2048,1024]{1,0:T(8,128)(2,1)S(1)} copy-done((bf16[2048,1024]{1,0:T(8,128)(2,1)S(1)}, bf16[2048,1024]{1,0:T(8,128)(2,1)}, u32[]{:S(2)}) %copy-start.5) | copy-done | bytes 4194328
  45.1 2.2 %copy-done.8 = bf16[2048,1024]{1,0:T(8,128)(2,1)S(1)} copy-done((bf16[2048,1024]{1,0:T(8,128)(2,1)S(1)}, bf16[2048,1024]{1,0:T(8,128)(2,1)}, u32[]{:S(2)}) %copy-start.8) | copy-done | bytes 4194328
  47.3 2.5 %product.8 = (f32[64,1024]{1,0:T(8,128)S(1)}, f32[64,1024]{1,0:T(8,128)S(1)}) custom-call(s32[3]{0:T(128)S(1)} %pad_add_fusion.place_ref, s32[8,64]{1,0:T(8,128)S(1)} %copy-done.16, s32[8]{0:T(128)S(1)} %copy-done.17, f32[32,2048]{1,0:T(8,128)S(1)} %pack.3.refs_0_, f32[32,2048]{1,0:T(8,128)S(1)} %collective-permute-done.3.refs_1_, ...), custom_call_target="tpu_custom_call" | custom-call | flops 3221225472 | bytes 1 | tf_op jit(solution)/shard_map/product/pallas_call | solution.py:171
  51.2 5.8 %split.3 = (bf16[2048,1024]{1,0:T(8,128)(2,1)S(1)}, bf16[2048,1024]{1,0:T(8,128)(2,1)S(1)}, f32[8,128]{1,0:T(8,128)S(1)}) custom-call(f32[2048,1024]{1,0:T(8,128)} %collective-permute-done.11.whole_ref), custom_call_target="tpu_custom_call" | custom-call | flops 1 | bytes 1 | tf_op jit(solution)/shard_map/split/pallas_call | solution.py:110
  57.6 2.5 %product.9 = (f32[64,1024]{1,0:T(8,128)S(1)}, f32[64,1024]{1,0:T(8,128)S(1)}) custom-call(s32[3]{0:T(128)S(1)} %pad_add_fusion.place_ref, s32[8,64]{1,0:T(8,128)S(1)} %copy-done.16, s32[8]{0:T(128)S(1)} %copy-done.17, f32[32,2048]{1,0:T(8,128)S(1)} %pack.3.refs_0_, f32[32,2048]{1,0:T(8,128)S(1)} %collective-permute-done.3.refs_1_, ...), custom_call_target="tpu_custom_call" | custom-call | flops 3221225472 | bytes 1 | tf_op jit(solution)/shard_map/product/pallas_call | solution.py:171
  64.2 5.4 %collective-permute-done.17 = f32[64,1024]{1,0:T(8,128)S(1)} collective-permute-done((f32[64,1024]{1,0:T(8,128)S(1)}, f32[64,1024]{1,0:T(8,128)S(1)}, u32[]{:S(2)}, u32[]{:S(2)}) %collective-permute-start.17) | collective-permute-done | bytes 262176 | tf_op jit(solution)/shard_map/ppermute | solution.py:240
  74.7 3.4 %collective-permute-done.19.refs_2_ = f32[64,2048]{1,0:T(8,128)S(1)} collective-permute-done((f32[64,2048]{1,0:T(8,128)}, f32[64,2048]{1,0:T(8,128)S(1)}, u32[]{:S(2)}, u32[]{:S(2)}) %collective-permute-start.19) | collective-permute-done | bytes 524320 | tf_op jit(solution)/shard_map/ppermute | solution.py:240
  78.1 2.2 %copy-done.11 = bf16[2048,1024]{1,0:T(8,128)(2,1)S(1)} copy-done((bf16[2048,1024]{1,0:T(8,128)(2,1)S(1)}, bf16[2048,1024]{1,0:T(8,128)(2,1)}, u32[]{:S(2)}) %copy-start.11) | copy-done | bytes 4194328
  80.3 2.2 %copy-done.14 = bf16[2048,1024]{1,0:T(8,128)(2,1)S(1)} copy-done((bf16[2048,1024]{1,0:T(8,128)(2,1)S(1)}, bf16[2048,1024]{1,0:T(8,128)(2,1)}, u32[]{:S(2)}) %copy-start.14) | copy-done | bytes 4194328
  82.5 2.5 %product.10 = (f32[64,1024]{1,0:T(8,128)S(1)}, f32[64,1024]{1,0:T(8,128)S(1)}) custom-call(s32[3]{0:T(128)S(1)} %pad_add_fusion.place_ref, s32[8,64]{1,0:T(8,128)S(1)} %copy-done.16, s32[8]{0:T(128)S(1)} %copy-done.17, f32[32,2048]{1,0:T(8,128)S(1)} %pack.4.refs_0_, f32[32,2048]{1,0:T(8,128)S(1)} %collective-permute-done.15.refs_1_, ...), custom_call_target="tpu_custom_call" | custom-call | flops 3221225472 | bytes 1 | tf_op jit(solution)/shard_map/product/pallas_call | solution.py:171
  87.8 2.4 %product.11 = (f32[64,1024]{1,0:T(8,128)S(1)}, f32[64,1024]{1,0:T(8,128)S(1)}) custom-call(s32[3]{0:T(128)S(1)} %pad_add_fusion.place_ref, s32[8,64]{1,0:T(8,128)S(1)} %copy-done.16, s32[8]{0:T(128)S(1)} %copy-done.17, f32[32,2048]{1,0:T(8,128)S(1)} %pack.4.refs_0_, f32[32,2048]{1,0:T(8,128)S(1)} %collective-permute-done.15.refs_1_, ...), custom_call_target="tpu_custom_call" | custom-call | flops 3221225472 | bytes 1 | tf_op jit(solution)/shard_map/product/pallas_call | solution.py:171
  91.9 2.1 %collective-permute-done.27 = f32[64,1024]{1,0:T(8,128)S(1)} collective-permute-done((f32[64,1024]{1,0:T(8,128)S(1)}, f32[64,1024]{1,0:T(8,128)S(1)}, u32[]{:S(2)}, u32[]{:S(2)}) %collective-permute-start.27) | collective-permute-done | bytes 262176 | tf_op jit(solution)/shard_map/ppermute | solution.py:240
  95.5 2.6 %product.12 = (f32[64,1024]{1,0:T(8,128)S(1)}, f32[64,1024]{1,0:T(8,128)S(1)}) custom-call(s32[3]{0:T(128)S(1)} %pad_add_fusion.place_ref, s32[8,64]{1,0:T(8,128)S(1)} %copy-done.16, s32[8]{0:T(128)S(1)} %copy-done.17, f32[32,2048]{1,0:T(8,128)S(1)} %get-tuple-element.273.refs_0_, f32[32,2048]{1,0:T(8,128)S(1)} %collective-permute-done.22.refs_1_, ...), custom_call_target="tpu_custom_call" | custom-call | flops 3221225472 | bytes 1 | tf_op jit(solution)/shard_map/product/pallas_call | solution.py:171
  99.6 2.3 %collective-permute-start.28 = (f32[32,1024]{1,0:T(8,128)S(1)}, f32[32,1024]{1,0:T(8,128)S(1)}, u32[]{:S(2)}, u32[]{:S(2)}) collective-permute-start(f32[32,1024]{1,0:T(8,128)S(1)} %get-tuple-element.356), channel_id=1, source_target_pairs={{0,2},{1,3},{2,0},{3,1},{4,6},{5,7},{6,4},{7,5},{8,10},{9,11},{10,... | collective-permute-start | bytes 393224 | tf_op jit(solution)/shard_map/ppermute | solution.py:246
  102.3 2.4 %product.13 = (f32[64,1024]{1,0:T(8,128)S(1)}, f32[64,1024]{1,0:T(8,128)S(1)}) custom-call(s32[3]{0:T(128)S(1)} %pad_add_fusion.place_ref, s32[8,64]{1,0:T(8,128)S(1)} %copy-done.16, s32[8]{0:T(128)S(1)} %copy-done.17, f32[32,2048]{1,0:T(8,128)S(1)} %get-tuple-element.273.refs_0_, f32[32,2048]{1,0:T(8,128)S(1)} %collective-permute-done.22.refs_1_, ...), custom_call_target="tpu_custom_call" | custom-call | flops 3221225472 | bytes 1 | tf_op jit(solution)/shard_map/product/pallas_call | solution.py:171
  109.3 2.4 %product.14 = (f32[64,1024]{1,0:T(8,128)S(1)}, f32[64,1024]{1,0:T(8,128)S(1)}) custom-call(s32[3]{0:T(128)S(1)} %pad_add_fusion.place_ref, s32[8,64]{1,0:T(8,128)S(1)} %copy-done.16, s32[8]{0:T(128)S(1)} %copy-done.17, f32[32,2048]{1,0:T(8,128)S(1)} %get-tuple-element.295.refs_0_, f32[32,2048]{1,0:T(8,128)S(1)} %collective-permute-done.20.refs_1_, ...), custom_call_target="tpu_custom_call" | custom-call | flops 3221225472 | bytes 1 | tf_op jit(solution)/shard_map/product/pallas_call | solution.py:171
  116.2 2.4 %product.15 = (f32[64,1024]{1,0:T(8,128)S(1)}, f32[64,1024]{1,0:T(8,128)S(1)}) custom-call(s32[3]{0:T(128)S(1)} %pad_add_fusion.place_ref, s32[8,64]{1,0:T(8,128)S(1)} %copy-done.16, s32[8]{0:T(128)S(1)} %copy-done.17, f32[32,2048]{1,0:T(8,128)S(1)} %get-tuple-element.295.refs_0_, f32[32,2048]{1,0:T(8,128)S(1)} %collective-permute-done.20.refs_1_, ...), custom_call_target="tpu_custom_call" | custom-call | flops 3221225472 | bytes 1 | tf_op jit(solution)/shard_map/product/pallas_call | solution.py:171
  118.6 3.9 %collective-permute-done.35 = f32[64,1024]{1,0:T(8,128)S(1)} collective-permute-done((f32[64,1024]{1,0:T(8,128)S(1)}, f32[64,1024]{1,0:T(8,128)S(1)}, u32[]{:S(2)}, u32[]{:S(2)}) %collective-permute-start.35) | collective-permute-done | bytes 262176 | tf_op jit(solution)/shard_map/ppermute | solution.py:246
  124.6 2.2 %collective-permute-start.46 = (f32[64,1024]{1,0:T(8,128)S(1)}, f32[64,1024]{1,0:T(8,128)S(1)}, u32[]{:S(2)}, u32[]{:S(2)}) collective-permute-start(f32[64,1024]{1,0:T(8,128)S(1)} %broadcast_select_fusion.1), channel_id=1, source_target_pairs={{0,1},{1,0},{2,3},{3,2},{4,5},{5,4},{6,7},{7,6},{8,9},{9,8},{10,11... | collective-permute-start | bytes 786440 | tf_op jit(solution)/shard_map/ppermute | solution.py:246
  128.9 4.0 %collective-permute-done.37.refs_5_ = f32[32,1024]{1,0:T(8,128)S(1)} collective-permute-done((f32[32,1024]{1,0:T(8,128)S(1)}, f32[32,1024]{1,0:T(8,128)S(1)}, u32[]{:S(2)}, u32[]{:S(2)}) %collective-permute-start.37) | collective-permute-done | bytes 131104 | tf_op jit(solution)/shard_map/ppermute | solution.py:246
  132.9 3.2 %collective-permute-done.46 = f32[64,1024]{1,0:T(8,128)S(1)} collective-permute-done((f32[64,1024]{1,0:T(8,128)S(1)}, f32[64,1024]{1,0:T(8,128)S(1)}, u32[]{:S(2)}, u32[]{:S(2)}) %collective-permute-start.46) | collective-permute-done | bytes 262176 | tf_op jit(solution)/shard_map/ppermute | solution.py:246
  137.0 2.3 %collective-permute-start.44 = (f32[32,1024]{1,0:T(8,128)S(1)}, f32[32,1024]{1,0:T(8,128)S(1)}, u32[]{:S(2)}, u32[]{:S(2)}) collective-permute-start(f32[32,1024]{1,0:T(8,128)S(1)} %get-tuple-element.341), channel_id=1, source_target_pairs={{0,2},{1,3},{2,0},{3,1},{4,6},{5,7},{6,4},{7,5},{8,10},{9,11},{10,... | collective-permute-start | bytes 393224 | tf_op jit(solution)/shard_map/ppermute | solution.py:246
  141.2 3.9 %collective-permute-done.45 = f32[64,1024]{1,0:T(8,128)S(1)} collective-permute-done((f32[64,1024]{1,0:T(8,128)S(1)}, f32[64,1024]{1,0:T(8,128)S(1)}, u32[]{:S(2)}, u32[]{:S(2)}) %collective-permute-start.45) | collective-permute-done | bytes 262176 | tf_op jit(solution)/shard_map/ppermute | solution.py:246
  147.1 3.2 %collective-permute-done.50 = f32[32,1024]{1,0:T(8,128)S(1)} collective-permute-done((f32[32,1024]{1,0:T(8,128)S(1)}, f32[32,1024]{1,0:T(8,128)S(1)}, u32[]{:S(2)}, u32[]{:S(2)}) %collective-permute-start.50) | collective-permute-done | bytes 131104 | tf_op jit(solution)/shard_map/ppermute | solution.py:240
  153.3 4.1 %collective-permute-done.51.refs_15_ = f32[32,1024]{1,0:T(8,128)S(1)} collective-permute-done((f32[32,1024]{1,0:T(8,128)S(1)}, f32[32,1024]{1,0:T(8,128)S(1)}, u32[]{:S(2)}, u32[]{:S(2)}) %collective-permute-start.51) | collective-permute-done | bytes 131104 | tf_op jit(solution)/shard_map/ppermute | solution.py:246
  (169 shorter events, 63.9 us)
Async XLA Ops:
  0.0 51.2 %collective-permute-start.11 = (f32[2048,1024]{1,0:T(8,128)}, f32[2048,1024]{1,0:T(8,128)}, u32[]{:S(2)}, u32[]{:S(2)}) collective-permute-start(f32[2048,1024]{1,0:T(8,128)} %whole_ref.2), channel_id=1, source_target_pairs={{0,4},{4,0},{8,12},{12,8},{16,20},{20,16},{24,28},{28,24},{1,5},{5... | collective-permute-start | bytes 25165832 | tf_op jit(solution)/shard_map/ppermute | solution.py:240
  2.4 14.4 %collective-permute-start = (f32[8,2048]{1,0:T(8,128)S(1)}, f32[8,2048]{1,0:T(8,128)S(1)}, u32[]{:S(2)}, u32[]{:S(2)}) collective-permute-start(f32[8,2048]{1,0:T(8,128)S(1)} %get-tuple-element.171), channel_id=1, source_target_pairs={{0,1},{1,0},{2,3},{3,2},{4,5},{5,4},{6,7},{7,6},{8,9},{9,8},{10,11... | collective-permute-start | bytes 196616 | tf_op jit(solution)/shard_map/ppermute | solution.py:246
  5.0 11.7 %collective-permute-start.1 = (f32[8,2048]{1,0:T(8,128)S(1)}, f32[8,2048]{1,0:T(8,128)S(1)}, u32[]{:S(2)}, u32[]{:S(2)}) collective-permute-start(f32[8,2048]{1,0:T(8,128)S(1)} %get-tuple-element.172), channel_id=1, source_target_pairs={{0,2},{1,3},{2,0},{3,1},{4,6},{5,7},{6,4},{7,5},{8,10},{9,11},{10,... | collective-permute-start | bytes 196616 | tf_op jit(solution)/shard_map/ppermute | solution.py:246
  20.7 10.0 %collective-permute-start.7 = (f32[8,2048]{1,0:T(8,128)S(1)}, f32[8,2048]{1,0:T(8,128)S(1)}, u32[]{:S(2)}, u32[]{:S(2)}) collective-permute-start(f32[8,2048]{1,0:T(8,128)S(1)} %get-tuple-element.180), channel_id=1, source_target_pairs={{0,1},{1,0},{2,3},{3,2},{4,5},{5,4},{6,7},{7,6},{8,9},{9,8},{10,11... | collective-permute-start | bytes 196616 | tf_op jit(solution)/shard_map/ppermute | solution.py:246
  26.8 12.1 %collective-permute-start.5 = (f32[16,2048]{1,0:T(8,128)S(1)}, f32[16,2048]{1,0:T(8,128)S(1)}, u32[]{:S(2)}, u32[]{:S(2)}) collective-permute-start(f32[16,2048]{1,0:T(8,128)S(1)} %slice.54), channel_id=1, source_target_pairs={{0,16},{4,20},{8,24},{12,28},{16,0},{20,4},{24,8},{28,12},{1,17},{... | collective-permute-start | bytes 393224 | tf_op jit(solution)/shard_map/ppermute | solution.py:240
  28.4 13.0 %collective-permute-start.6 = (f32[16,2048]{1,0:T(8,128)S(1)}, f32[16,2048]{1,0:T(8,128)S(1)}, u32[]{:S(2)}, u32[]{:S(2)}) collective-permute-start(f32[16,2048]{1,0:T(8,128)S(1)} %slice.55), channel_id=1, source_target_pairs={{0,8},{4,12},{8,0},{12,4},{16,24},{20,28},{24,16},{28,20},{1,9},{5... | collective-permute-start | bytes 393224 | tf_op jit(solution)/shard_map/ppermute | solution.py:240
  35.6 14.8 %collective-permute-start.12 = (f32[16,2048]{1,0:T(8,128)S(1)}, f32[16,2048]{1,0:T(8,128)S(1)}, u32[]{:S(2)}, u32[]{:S(2)}) collective-permute-start(f32[16,2048]{1,0:T(8,128)S(1)} %get-tuple-element.191), channel_id=1, source_target_pairs={{0,1},{1,0},{2,3},{3,2},{4,5},{5,4},{6,7},{7,6},{8,9},{9,8},{10,11... | collective-permute-start | bytes 393224 | tf_op jit(solution)/shard_map/ppermute | solution.py:246
  37.3 13.0 %collective-permute-start.13 = (f32[16,2048]{1,0:T(8,128)S(1)}, f32[16,2048]{1,0:T(8,128)S(1)}, u32[]{:S(2)}, u32[]{:S(2)}) collective-permute-start(f32[16,2048]{1,0:T(8,128)S(1)} %get-tuple-element.192), channel_id=1, source_target_pairs={{0,2},{1,3},{2,0},{3,1},{4,6},{5,7},{6,4},{7,5},{8,10},{9,11},{10,... | collective-permute-start | bytes 393224 | tf_op jit(solution)/shard_map/ppermute | solution.py:246
  38.9 11.5 %collective-permute-start.14 = (f32[16,2048]{1,0:T(8,128)S(1)}, f32[16,2048]{1,0:T(8,128)S(1)}, u32[]{:S(2)}, u32[]{:S(2)}) collective-permute-start(f32[16,2048]{1,0:T(8,128)S(1)} %get-tuple-element.193), channel_id=1, source_target_pairs={{0,3},{1,2},{2,1},{3,0},{4,7},{5,6},{6,5},{7,4},{8,11},{9,10},{10,... | collective-permute-start | bytes 393224 | tf_op jit(solution)/shard_map/ppermute | solution.py:246
  49.7 12.1 %collective-permute-start.10 = (f32[64,1024]{1,0:T(8,128)S(1)}, f32[64,1024]{1,0:T(8,128)}, u32[]{:S(2)}, u32[]{:S(2)}) collective-permute-start(f32[64,1024]{1,0:T(8,128)S(1)} %get-tuple-element.211), channel_id=1, source_target_pairs={{0,8},{4,12},{8,0},{12,4},{16,24},{20,28},{24,16},{28,20},{1,9},{5... | collective-permute-start | bytes 786440 | tf_op jit(solution)/shard_map/ppermute | solution.py:240
  60.4 9.2 %collective-permute-start.17 = (f32[64,1024]{1,0:T(8,128)S(1)}, f32[64,1024]{1,0:T(8,128)S(1)}, u32[]{:S(2)}, u32[]{:S(2)}) collective-permute-start(f32[64,1024]{1,0:T(8,128)S(1)} %get-tuple-element.232), channel_id=1, source_target_pairs={{0,8},{4,12},{8,0},{12,4},{16,24},{20,28},{24,16},{28,20},{1,9},{5... | collective-permute-start | bytes 786440 | tf_op jit(solution)/shard_map/ppermute | solution.py:240
  63.0 15.1 %collective-permute-start.19 = (f32[64,2048]{1,0:T(8,128)}, f32[64,2048]{1,0:T(8,128)S(1)}, u32[]{:S(2)}, u32[]{:S(2)}) collective-permute-start(f32[64,2048]{1,0:T(8,128)} %copy-done.18), channel_id=1, source_target_pairs={{0,16},{4,20},{8,24},{12,28},{16,0},{20,4},{24,8},{28,12},{1,17},{... | collective-permute-start | bytes 1572872 | tf_op jit(solution)/shard_map/ppermute | solution.py:240
  63.6 9.8 %collective-permute-start.22 = (f32[32,2048]{1,0:T(8,128)S(1)}, f32[32,2048]{1,0:T(8,128)S(1)}, u32[]{:S(2)}, u32[]{:S(2)}) collective-permute-start(f32[32,2048]{1,0:T(8,128)S(1)} %get-tuple-element.273.refs_0_), channel_id=1, source_target_pairs={{0,8},{4,12},{8,0},{12,4},{16,24},{20,28},{24,16},{28,20},{1,9},{5... | collective-permute-start | bytes 786440 | tf_op jit(solution)/shard_map/ppermute | solution.py:240
  69.7 15.8 %collective-permute-start.21 = (f32[64,1024]{1,0:T(8,128)S(1)}, f32[64,1024]{1,0:T(8,128)S(1)}, u32[]{:S(2)}, u32[]{:S(2)}) collective-permute-start(f32[64,1024]{1,0:T(8,128)S(1)} %broadcast_select_fusion.6), channel_id=1, source_target_pairs={{0,1},{1,0},{2,3},{3,2},{4,5},{5,4},{6,7},{7,6},{8,9},{9,8},{10,11... | collective-permute-start | bytes 786440 | tf_op jit(solution)/shard_map/ppermute | solution.py:246
  69.8 16.3 %collective-permute-start.20 = (f32[32,2048]{1,0:T(8,128)S(1)}, f32[32,2048]{1,0:T(8,128)S(1)}, u32[]{:S(2)}, u32[]{:S(2)}) collective-permute-start(f32[32,2048]{1,0:T(8,128)S(1)} %get-tuple-element.295.refs_0_), channel_id=1, source_target_pairs={{0,8},{4,12},{8,0},{12,4},{16,24},{20,28},{24,16},{28,20},{1,9},{5... | collective-permute-start | bytes 786440 | tf_op jit(solution)/shard_map/ppermute | solution.py:240
  71.4 18.8 %collective-permute-start.18 = (f32[32,1024]{1,0:T(8,128)S(1)}, f32[32,1024]{1,0:T(8,128)S(1)}, u32[]{:S(2)}, u32[]{:S(2)}) collective-permute-start(f32[32,1024]{1,0:T(8,128)S(1)} %get-tuple-element.361), channel_id=1, source_target_pairs={{0,16},{4,20},{8,24},{12,28},{16,0},{20,4},{24,8},{28,12},{1,17},{... | collective-permute-start | bytes 393224 | tf_op jit(solution)/shard_map/ppermute | solution.py:240
  73.4 20.6 %collective-permute-start.26 = (f32[64,2048]{1,0:T(8,128)S(1)}, f32[64,2048]{1,0:T(8,128)S(1)}, u32[]{:S(2)}, u32[]{:S(2)}) collective-permute-start(f32[64,2048]{1,0:T(8,128)S(1)} %constant_dynamic-update-slice_fusion.2), channel_id=1, source_target_pairs={{0,16},{4,20},{8,24},{12,28},{16,0},{20,4},{24,8},{28,12},{1,17},{... | collective-permute-start | bytes 1572872 | tf_op jit(solution)/shard_map/ppermute | solution.py:240
  85.5 12.6 %collective-permute-start.25 = (f32[32,1024]{1,0:T(8,128)S(1)}, f32[32,1024]{1,0:T(8,128)S(1)}, u32[]{:S(2)}, u32[]{:S(2)}) collective-permute-start(f32[32,1024]{1,0:T(8,128)S(1)} %get-tuple-element.358), channel_id=1, source_target_pairs={{0,16},{4,20},{8,24},{12,28},{16,0},{20,4},{24,8},{28,12},{1,17},{... | collective-permute-start | bytes 393224 | tf_op jit(solution)/shard_map/ppermute | solution.py:240
  86.2 23.1 %collective-permute-start.33 = (f32[64,2048]{1,0:T(8,128)S(1)}, f32[64,2048]{1,0:T(8,128)S(1)}, u32[]{:S(2)}, u32[]{:S(2)}) collective-permute-start(f32[64,2048]{1,0:T(8,128)S(1)} %constant_dynamic-update-slice_fusion.4), channel_id=1, source_target_pairs={{0,16},{4,20},{8,24},{12,28},{16,0},{20,4},{24,8},{28,12},{1,17},{... | collective-permute-start | bytes 1572872 | tf_op jit(solution)/shard_map/ppermute | solution.py:240
  90.2 9.4 %collective-permute-start.24 = (f32[64,1024]{1,0:T(8,128)S(1)}, f32[64,1024]{1,0:T(8,128)S(1)}, u32[]{:S(2)}, u32[]{:S(2)}) collective-permute-start(f32[64,1024]{1,0:T(8,128)S(1)} %get-tuple-element.256), channel_id=1, source_target_pairs={{0,8},{4,12},{8,0},{12,4},{16,24},{20,28},{24,16},{28,20},{1,9},{5... | collective-permute-start | bytes 786440 | tf_op jit(solution)/shard_map/ppermute | solution.py:240
  94.1 11.6 %collective-permute-start.30 = (f32[64,1024]{1,0:T(8,128)S(1)}, f32[64,1024]{1,0:T(8,128)S(1)}, u32[]{:S(2)}, u32[]{:S(2)}) collective-permute-start(f32[64,1024]{1,0:T(8,128)S(1)} %broadcast_select_fusion.5), channel_id=1, source_target_pairs={{0,1},{1,0},{2,3},{3,2},{4,5},{5,4},{6,7},{7,6},{8,9},{9,8},{10,11... | collective-permute-start | bytes 786440 | tf_op jit(solution)/shard_map/ppermute | solution.py:246
  98.1 9.2 %collective-permute-start.29 = (f32[64,1024]{1,0:T(8,128)S(1)}, f32[64,1024]{1,0:T(8,128)S(1)}, u32[]{:S(2)}, u32[]{:S(2)}) collective-permute-start(f32[64,1024]{1,0:T(8,128)S(1)} %get-tuple-element.266), channel_id=1, source_target_pairs={{0,8},{4,12},{8,0},{12,4},{16,24},{20,28},{24,16},{28,20},{1,9},{5... | collective-permute-start | bytes 786440 | tf_op jit(solution)/shard_map/ppermute | solution.py:240
  99.6 9.6 %collective-permute-start.28 = (f32[32,1024]{1,0:T(8,128)S(1)}, f32[32,1024]{1,0:T(8,128)S(1)}, u32[]{:S(2)}, u32[]{:S(2)}) collective-permute-start(f32[32,1024]{1,0:T(8,128)S(1)} %get-tuple-element.356), channel_id=1, source_target_pairs={{0,2},{1,3},{2,0},{3,1},{4,6},{5,7},{6,4},{7,5},{8,10},{9,11},{10,... | collective-permute-start | bytes 393224 | tf_op jit(solution)/shard_map/ppermute | solution.py:246
  102.0 12.9 %collective-permute-start.31 = (f32[64,1024]{1,0:T(8,128)S(1)}, f32[64,1024]{1,0:T(8,128)S(1)}, u32[]{:S(2)}, u32[]{:S(2)}) collective-permute-start(f32[64,1024]{1,0:T(8,128)S(1)} %broadcast_select_fusion.4), channel_id=1, source_target_pairs={{0,1},{1,0},{2,3},{3,2},{4,5},{5,4},{6,7},{7,6},{8,9},{9,8},{10,11... | collective-permute-start | bytes 786440 | tf_op jit(solution)/shard_map/ppermute | solution.py:246
  105.7 10.1 %collective-permute-start.36 = (f32[64,1024]{1,0:T(8,128)S(1)}, f32[64,1024]{1,0:T(8,128)S(1)}, u32[]{:S(2)}, u32[]{:S(2)}) collective-permute-start(f32[64,1024]{1,0:T(8,128)S(1)} %get-tuple-element.278), channel_id=1, source_target_pairs={{0,8},{4,12},{8,0},{12,4},{16,24},{20,28},{24,16},{28,20},{1,9},{5... | collective-permute-start | bytes 786440 | tf_op jit(solution)/shard_map/ppermute | solution.py:240
  109.2 13.3 %collective-permute-start.35 = (f32[64,1024]{1,0:T(8,128)S(1)}, f32[64,1024]{1,0:T(8,128)S(1)}, u32[]{:S(2)}, u32[]{:S(2)}) collective-permute-start(f32[64,1024]{1,0:T(8,128)S(1)} %broadcast_select_fusion.3), channel_id=1, source_target_pairs={{0,1},{1,0},{2,3},{3,2},{4,5},{5,4},{6,7},{7,6},{8,9},{9,8},{10,11... | collective-permute-start | bytes 786440 | tf_op jit(solution)/shard_map/ppermute | solution.py:246
  111.7 12.8 %collective-permute-start.42 = (f32[64,1024]{1,0:T(8,128)S(1)}, f32[64,1024]{1,0:T(8,128)S(1)}, u32[]{:S(2)}, u32[]{:S(2)}) collective-permute-start(f32[64,1024]{1,0:T(8,128)S(1)} %get-tuple-element.289), channel_id=1, source_target_pairs={{0,8},{4,12},{8,0},{12,4},{16,24},{20,28},{24,16},{28,20},{1,9},{5... | collective-permute-start | bytes 786440 | tf_op jit(solution)/shard_map/ppermute | solution.py:240
  113.2 11.4 %collective-permute-start.41 = (f32[32,1024]{1,0:T(8,128)S(1)}, f32[32,1024]{1,0:T(8,128)S(1)}, u32[]{:S(2)}, u32[]{:S(2)}) collective-permute-start(f32[32,1024]{1,0:T(8,128)S(1)} %get-tuple-element.346), channel_id=1, source_target_pairs={{0,2},{1,3},{2,0},{3,1},{4,6},{5,7},{6,4},{7,5},{8,10},{9,11},{10,... | collective-permute-start | bytes 393224 | tf_op jit(solution)/shard_map/ppermute | solution.py:246
  115.8 11.1 %collective-permute-start.40 = (f32[64,1024]{1,0:T(8,128)S(1)}, f32[64,1024]{1,0:T(8,128)S(1)}, u32[]{:S(2)}, u32[]{:S(2)}) collective-permute-start(f32[64,1024]{1,0:T(8,128)S(1)} %broadcast_select_fusion.2), channel_id=1, source_target_pairs={{0,1},{1,0},{2,3},{3,2},{4,5},{5,4},{6,7},{7,6},{8,9},{9,8},{10,11... | collective-permute-start | bytes 786440 | tf_op jit(solution)/shard_map/ppermute | solution.py:246
  124.6 11.4 %collective-permute-start.46 = (f32[64,1024]{1,0:T(8,128)S(1)}, f32[64,1024]{1,0:T(8,128)S(1)}, u32[]{:S(2)}, u32[]{:S(2)}) collective-permute-start(f32[64,1024]{1,0:T(8,128)S(1)} %broadcast_select_fusion.1), channel_id=1, source_target_pairs={{0,1},{1,0},{2,3},{3,2},{4,5},{5,4},{6,7},{7,6},{8,9},{9,8},{10,11... | collective-permute-start | bytes 786440 | tf_op jit(solution)/shard_map/ppermute | solution.py:246
  128.1 11.1 %collective-permute-start.48 = (f32[32,1024]{1,0:T(8,128)S(1)}, f32[32,1024]{1,0:T(8,128)S(1)}, u32[]{:S(2)}, u32[]{:S(2)}) collective-permute-start(f32[32,1024]{1,0:T(8,128)S(1)} %get-tuple-element.338), channel_id=1, source_target_pairs={{0,2},{1,3},{2,0},{3,1},{4,6},{5,7},{6,4},{7,5},{8,10},{9,11},{10,... | collective-permute-start | bytes 393224 | tf_op jit(solution)/shard_map/ppermute | solution.py:246
  137.0 10.0 %collective-permute-start.44 = (f32[32,1024]{1,0:T(8,128)S(1)}, f32[32,1024]{1,0:T(8,128)S(1)}, u32[]{:S(2)}, u32[]{:S(2)}) collective-permute-start(f32[32,1024]{1,0:T(8,128)S(1)} %get-tuple-element.341), channel_id=1, source_target_pairs={{0,2},{1,3},{2,0},{3,1},{4,6},{5,7},{6,4},{7,5},{8,10},{9,11},{10,... | collective-permute-start | bytes 393224 | tf_op jit(solution)/shard_map/ppermute | solution.py:246
  (40 other events, 380.6 us)

commit v9 on v8

--- a/solution.py
+++ b/solution.py
@@ -14,10 +14,10 @@
 UNITS = tuple((chunk, (half,)) for chunk in range(CHUNKS) for half in range(CORES))
 
 ORDER = (
-    "s0", "f0", "s1", "p0", "g00", "s2", "g01", "p1", "g10", "e0", "f1", "g11", "p2", "e1",
-    "g20", "r0", "r1", "g30", "x0", "g21", "e3", "x1", "g31", "e2", "z0", "r3", "e5", "z1",
-    "r2", "l0", "e4", "x3", "r5", "l1", "e6", "z3", "x2", "r4", "e7", "x5", "z2", "r6", "l3",
-    "x4", "z5", "r7", "l2", "z4", "x6", "l5", "z6", "x7", "l4", "z7", "l6", "l7",
+    "s0", "s1", "p0", "g00", "g01", "f0", "e0", "p1", "g10", "s2", "f1", "r0", "e1", "g11",
+    "p2", "g20", "x0", "r1", "g30", "e2", "x1", "e3", "z0", "g21", "r2", "r3", "z1", "l0",
+    "e4", "x2", "e5", "g31", "x3", "r4", "z2", "r5", "l1", "z3", "x4", "e6", "l2", "x5", "e7",
+    "r6", "z4", "l3", "r7", "z5", "x6", "l4", "x7", "z6", "l5", "z7", "l6", "l7",
 )
 
 SMEM = pl.BlockSpec(memory_space=pltpu.SMEM)
@@ -58,8 +58,7 @@
     return [outs[g * count : (g + 1) * count] for g in range(len(bounds))]
 
 
-def pack_kernel(count, part, place_ref, token_ref, *refs):
-    del token_ref
+def pack_kernel(count, part, place_ref, *refs):
     z = place_ref[2]
     for c, out in enumerate(refs[count:]):
         for m in range(count):
@@ -67,45 +66,48 @@
             out[rows, :] = refs[m][c * part : (c + 1) * part, :]
 
 
-def pack(blocks, part, place, token):
+def pack(blocks, part, place):
     count = len(blocks)
     rows, depth = blocks[0].shape
     shape = jax.ShapeDtypeStruct((count * part, depth), blocks[0].dtype)
     return pl.pallas_call(
         functools.partial(pack_kernel, count, part),
-        in_specs=[SMEM, HBM] + [VMEM] * count,
+        in_specs=[SMEM] + [VMEM] * count,
         out_specs=[VMEM] * (rows // part),
         out_shape=[shape] * (rows // part),
         cost_estimate=SMALL,
         compiler_params=pltpu.CompilerParams(vmem_limit_bytes=2**20),
         name="pack",
-    )(place, token, *blocks)
+    )(place, *blocks)
 
 
 def split_kernel(step, whole_ref, high_ref, low_ref, token_ref, buffer, sems):
     count = whole_ref.shape[0] // step
+    slots = buffer.shape[0]
 
     def copy(i):
         return pltpu.make_async_copy(
-            whole_ref.at[pl.ds(i * step, step)], buffer.at[i % 2], sems.at[i % 2]
+            whole_ref.at[pl.ds(i * step, step)], buffer.at[i % slots], sems.at[i % slots]
         )
 
-    copy(0).start()
+    for i in range(min(slots, count)):
+        copy(i).start()
     token_ref[...] = jnp.zeros_like(token_ref)
     for i in range(count):
-        if i + 1 < count:
-            copy(i + 1).start()
         copy(i).wait()
-        whole = buffer[i % 2]
+        whole = buffer[i % slots]
         high = whole.astype(jnp.bfloat16)
         here = slice(i * step, (i + 1) * step)
         high_ref[here, :] = high
         low_ref[here, :] = (whole - high.astype(jnp.float32)).astype(jnp.bfloat16)
+        if i + slots < count:
+            copy(i + slots).start()
 
 
 def split(whole):
     rows, columns = whole.shape
     step = min(256, rows)
+    slots = min(4, rows // step)
     half = jax.ShapeDtypeStruct((rows, columns), jnp.bfloat16)
     return pl.pallas_call(
         functools.partial(split_kernel, step),
@@ -113,11 +115,11 @@
         out_specs=[VMEM, VMEM, VMEM],
         out_shape=[half, half, jax.ShapeDtypeStruct((8, 128), jnp.float32)],
         scratch_shapes=[
-            pltpu.VMEM((2, step, columns), jnp.float32),
-            pltpu.SemaphoreType.DMA((2,)),
+            pltpu.VMEM((slots, step, columns), jnp.float32),
+            pltpu.SemaphoreType.DMA((slots,)),
         ],
         cost_estimate=SMALL,
-        compiler_params=pltpu.CompilerParams(vmem_limit_bytes=3 * 2**20),
+        compiler_params=pltpu.CompilerParams(vmem_limit_bytes=6 * 2**20),
         name="split",
     )(whole)
 
@@ -246,7 +248,6 @@
         return lax.ppermute(value, "narrow", [(n, n ^ mask) for n in range(narrow_count)])
 
     last = []
-    token = []
 
     def ordered(*values):
         return list(lax.optimization_barrier((*values, *last))[: len(values)])
@@ -269,7 +270,7 @@
         spread[g] = [pieces[g][0]] + [along(send, n + 1) for n, send in enumerate(sends)]
 
     def pack_step(g):
-        packed = pack(ordered(*spread[g]), part, place, token[-1])
+        packed = pack(ordered(*spread[g]), part, place)
         mark(*packed)
         mine.update(zip(GROUPS[g], packed))
 
@@ -298,7 +299,7 @@
 
     def split_step(half):
         *factors[half], done = split(*ordered(integrals if half == 0 else swapped))
-        token.append(done)
+        mark(done)
 
     def multiply(unit):
         chunk, halves = UNITS[unit]

time: 160 us -> 161 us (level)
  waiting for transfers between devices: 51.6 us -> 67.8 us
  local copies, waits for them, and re-layouts: 18.9 us -> 5.85 us
    ppermute x27, waiting for transfers between devices: 24.3 us -> 39.6 us  [across(): lax.ppermute(value, 'wide', [(w, w ^ mask) for w in range(wide_count)])]
    unnamed x43 -> x25, local copies, waits for them, and re-layouts: 18.5 us -> 5.5 us
  transfers between devices with their start and end apart: 52 -> 52, of which waited for: 21 -> 25; matrix products, arithmetic and copies ran while one was open for 1% -> 1% of each run, Pallas kernels for 19% -> 18%
where the time goes in v9:
time: 161 us
  waiting for transfers between devices  67.8 us (42%)
  starting transfers between devices  55.3 us (34%)
  Pallas kernels  30.5 us (19%)
  local copies, waits for them, and re-layouts  5.85 us (4%)
    ppermute x27, waiting for transfers between devices, across(): lax.ppermute(value, 'wide', [(w, w ^ mask) for w in range(wide_count)])  39.6 us
    ppermute x27, starting transfers between devices, across(): lax.ppermute(value, 'wide', [(w, w ^ mask) for w in range(wide_count)])  29.1 us
    ppermute x25, waiting for transfers between devices, along(): lax.ppermute(value, 'narrow', [(n, n ^ mask) for n in range(narrow_count)])  28.2 us
    ppermute x25, starting transfers between devices, along(): lax.ppermute(value, 'narrow', [(n, n ^ mask) for n in range(narrow_count)])  26.1 us
    pallas_call x8, Pallas kernels, product(): pl.pallas_call(functools.partial(product_kernel, count, rows, layout, tar...  19.9 us
    pallas_call x2, Pallas kernels, split(): pl.pallas_call(functools.partial(split_kernel, step), in_specs=[HBM], out...  6.48 us
    unnamed x25, local copies, waits for them, and re-layouts  5.5 us
  transfers between devices with their start and end apart: 52, of which 25 were waited for; matrix products, arithmetic and copies ran while one was open for 1% of the time, Pallas kernels for 18%

profile of v9, /device:TPU:0, one launch (start us, length us, event | category | flops | bytes accessed | tf_op | source)
XLA Modules:
  0.0 161.0 jit_solution(15339990843934226293)
XLA Ops:
  2.4 2.6 %collective-permute-start = (f32[8,2048]{1,0:T(8,128)S(1)}, f32[8,2048]{1,0:T(8,128)S(1)}, u32[]{:S(2)}, u32[]{:S(2)}) collective-permute-start(f32[8,2048]{1,0:T(8,128)S(1)} %get-tuple-element.170), channel_id=1, source_target_pairs={{0,1},{1,0},{2,3},{3,2},{4,5},{5,4},{6,7},{7,6},{8,9},{9,8},{10,11... | collective-permute-start | bytes 196616 | tf_op jit(solution)/shard_map/ppermute | solution.py:248
  5.0 2.6 %collective-permute-start.1 = (f32[8,2048]{1,0:T(8,128)S(1)}, f32[8,2048]{1,0:T(8,128)S(1)}, u32[]{:S(2)}, u32[]{:S(2)}) collective-permute-start(f32[8,2048]{1,0:T(8,128)S(1)} %get-tuple-element.171), channel_id=1, source_target_pairs={{0,2},{1,3},{2,0},{3,1},{4,6},{5,7},{6,4},{7,5},{8,10},{9,11},{10,... | collective-permute-start | bytes 196616 | tf_op jit(solution)/shard_map/ppermute | solution.py:248
  7.8 4.2 %collective-permute-done.1.refs_2_ = f32[8,2048]{1,0:T(8,128)S(1)} collective-permute-done((f32[8,2048]{1,0:T(8,128)S(1)}, f32[8,2048]{1,0:T(8,128)S(1)}, u32[]{:S(2)}, u32[]{:S(2)}) %collective-permute-start.1) | collective-permute-done | bytes 65568 | tf_op jit(solution)/shard_map/ppermute | solution.py:248
  17.4 4.0 %collective-permute-done.3.refs_1_ = f32[32,2048]{1,0:T(8,128)S(1)} collective-permute-done((f32[32,2048]{1,0:T(8,128)S(1)}, f32[32,2048]{1,0:T(8,128)S(1)}, u32[]{:S(2)}, u32[]{:S(2)}) %collective-permute-start.3) | collective-permute-done | bytes 262176 | tf_op jit(solution)/shard_map/ppermute | solution.py:242
  24.8 3.4 %copy-done = f32[2048,1024]{1,0:T(8,128)S(1)} copy-done((f32[2048,1024]{1,0:T(8,128)S(1)}, f32[2048,1024]{1,0:T(8,128)}, u32[]{:S(2)}) %copy-start) | copy-done | bytes 8388632
  28.2 2.2 %split.2 = (bf16[2048,1024]{1,0:T(8,128)(2,1)S(1)}, bf16[2048,1024]{1,0:T(8,128)(2,1)S(1)}, f32[8,128]{1,0:T(8,128)}) custom-call(f32[2048,1024]{1,0:T(8,128)S(1)} %copy-done), custom_call_target="tpu_custom_call" | custom-call | flops 1 | bytes 1 | tf_op jit(solution)/shard_map/split/pallas_call | solution.py:112
  30.4 2.5 %product.8 = (f32[64,1024]{1,0:T(8,128)S(1)}, f32[64,1024]{1,0:T(8,128)S(1)}) custom-call(s32[3]{0:T(128)S(1)} %pad_add_fusion.place_ref, s32[8,64]{1,0:T(8,128)S(1)} %copy-done.8, s32[8]{0:T(128)S(1)} %copy-done.9, f32[32,2048]{1,0:T(8,128)S(1)} %pack.3.refs_0_, f32[32,2048]{1,0:T(8,128)S(1)} %collective-permute-done.3.refs_1_, ...), custom_call_target="tpu_custom_call" | custom-call | flops 3221225472 | bytes 1 | tf_op jit(solution)/shard_map/product/pallas_call | solution.py:173
  35.2 2.5 %collective-permute-start.10 = (f32[8,2048]{1,0:T(8,128)S(1)}, f32[8,2048]{1,0:T(8,128)S(1)}, u32[]{:S(2)}, u32[]{:S(2)}) collective-permute-start(f32[8,2048]{1,0:T(8,128)S(1)} %get-tuple-element.177), channel_id=1, source_target_pairs={{0,2},{1,3},{2,0},{3,1},{4,6},{5,7},{6,4},{7,5},{8,10},{9,11},{10,... | collective-permute-start | bytes 196616 | tf_op jit(solution)/shard_map/ppermute | solution.py:248
  40.4 3.4 %collective-permute-done.11.refs_3_ = f32[8,2048]{1,0:T(8,128)S(1)} collective-permute-done((f32[8,2048]{1,0:T(8,128)S(1)}, f32[8,2048]{1,0:T(8,128)S(1)}, u32[]{:S(2)}, u32[]{:S(2)}) %collective-permute-start.11) | collective-permute-done | bytes 65568 | tf_op jit(solution)/shard_map/ppermute | solution.py:248
  45.8 3.7 %collective-permute-start.13 = (f32[16,2048]{1,0:T(8,128)S(1)}, f32[16,2048]{1,0:T(8,128)S(1)}, u32[]{:S(2)}, u32[]{:S(2)}) collective-permute-start(f32[16,2048]{1,0:T(8,128)S(1)} %get-tuple-element.210), channel_id=1, source_target_pairs={{0,2},{1,3},{2,0},{3,1},{4,6},{5,7},{6,4},{7,5},{8,10},{9,11},{10,... | collective-permute-start | bytes 393224 | tf_op jit(solution)/shard_map/ppermute | solution.py:248
  50.2 4.3 %split.3 = (bf16[2048,1024]{1,0:T(8,128)(2,1)S(1)}, bf16[2048,1024]{1,0:T(8,128)(2,1)S(1)}, f32[8,128]{1,0:T(8,128)}) custom-call(f32[2048,1024]{1,0:T(8,128)} %collective-permute-done.16.whole_ref), custom_call_target="tpu_custom_call" | custom-call | flops 1 | bytes 1 | tf_op jit(solution)/shard_map/split/pallas_call | solution.py:112
  54.6 2.5 %product.9 = (f32[64,1024]{1,0:T(8,128)S(1)}, f32[64,1024]{1,0:T(8,128)S(1)}) custom-call(s32[3]{0:T(128)S(1)} %pad_add_fusion.place_ref, s32[8,64]{1,0:T(8,128)S(1)} %copy-done.8, s32[8]{0:T(128)S(1)} %copy-done.9, f32[32,2048]{1,0:T(8,128)S(1)} %pack.3.refs_0_, f32[32,2048]{1,0:T(8,128)S(1)} %collective-permute-done.3.refs_1_, ...), custom_call_target="tpu_custom_call" | custom-call | flops 3221225472 | bytes 1 | tf_op jit(solution)/shard_map/product/pallas_call | solution.py:173
  65.4 2.5 %collective-permute-start.20 = (f32[64,1024]{1,0:T(8,128)S(1)}, f32[64,1024]{1,0:T(8,128)S(1)}, u32[]{:S(2)}, u32[]{:S(2)}) collective-permute-start(f32[64,1024]{1,0:T(8,128)S(1)} %broadcast_select_fusion.6), channel_id=1, source_target_pairs={{0,1},{1,0},{2,3},{3,2},{4,5},{5,4},{6,7},{7,6},{8,9},{9,8},{10,11... | collective-permute-start | bytes 786440 | tf_op jit(solution)/shard_map/ppermute | solution.py:248
  69.9 3.6 %collective-permute-done.18.refs_2_ = f32[64,2048]{1,0:T(8,128)S(1)} collective-permute-done((f32[64,2048]{1,0:T(8,128)S(1)}, f32[64,2048]{1,0:T(8,128)S(1)}, u32[]{:S(2)}, u32[]{:S(2)}) %collective-permute-start.18) | collective-permute-done | bytes 524320 | tf_op jit(solution)/shard_map/ppermute | solution.py:242
  73.4 2.5 %product.10 = (f32[64,1024]{1,0:T(8,128)S(1)}, f32[64,1024]{1,0:T(8,128)S(1)}) custom-call(s32[3]{0:T(128)S(1)} %pad_add_fusion.place_ref, s32[8,64]{1,0:T(8,128)S(1)} %copy-done.8, s32[8]{0:T(128)S(1)} %copy-done.9, f32[32,2048]{1,0:T(8,128)S(1)} %pack.4.refs_0_, f32[32,2048]{1,0:T(8,128)S(1)} %collective-permute-done.15.refs_1_, ...), custom_call_target="tpu_custom_call" | custom-call | flops 3221225472 | bytes 1 | tf_op jit(solution)/shard_map/product/pallas_call | solution.py:173
  78.0 2.5 %product.11 = (f32[64,1024]{1,0:T(8,128)S(1)}, f32[64,1024]{1,0:T(8,128)S(1)}) custom-call(s32[3]{0:T(128)S(1)} %pad_add_fusion.place_ref, s32[8,64]{1,0:T(8,128)S(1)} %copy-done.8, s32[8]{0:T(128)S(1)} %copy-done.9, f32[32,2048]{1,0:T(8,128)S(1)} %pack.4.refs_0_, f32[32,2048]{1,0:T(8,128)S(1)} %collective-permute-done.15.refs_1_, ...), custom_call_target="tpu_custom_call" | custom-call | flops 3221225472 | bytes 1 | tf_op jit(solution)/shard_map/product/pallas_call | solution.py:173
  81.5 2.9 %collective-permute-done.24 = f32[64,1024]{1,0:T(8,128)S(1)} collective-permute-done((f32[64,1024]{1,0:T(8,128)S(1)}, f32[64,1024]{1,0:T(8,128)S(1)}, u32[]{:S(2)}, u32[]{:S(2)}) %collective-permute-start.24) | collective-permute-done | bytes 262176 | tf_op jit(solution)/shard_map/ppermute | solution.py:242
  87.3 2.1 %collective-permute-start.32 = (f32[64,1024]{1,0:T(8,128)S(1)}, f32[64,1024]{1,0:T(8,128)S(1)}, u32[]{:S(2)}, u32[]{:S(2)}) collective-permute-start(f32[64,1024]{1,0:T(8,128)S(1)} %broadcast_select_fusion.4), channel_id=1, source_target_pairs={{0,1},{1,0},{2,3},{3,2},{4,5},{5,4},{6,7},{7,6},{8,9},{9,8},{10,11... | collective-permute-start | bytes 786440 | tf_op jit(solution)/shard_map/ppermute | solution.py:248
  89.5 4.1 %collective-permute-done.27.refs_2_ = f32[64,2048]{1,0:T(8,128)S(1)} collective-permute-done((f32[64,2048]{1,0:T(8,128)S(1)}, f32[64,2048]{1,0:T(8,128)S(1)}, u32[]{:S(2)}, u32[]{:S(2)}) %collective-permute-start.27) | collective-permute-done | bytes 524320 | tf_op jit(solution)/shard_map/ppermute | solution.py:242
  93.6 2.6 %product.12 = (f32[64,1024]{1,0:T(8,128)S(1)}, f32[64,1024]{1,0:T(8,128)S(1)}) custom-call(s32[3]{0:T(128)S(1)} %pad_add_fusion.place_ref, s32[8,64]{1,0:T(8,128)S(1)} %copy-done.8, s32[8]{0:T(128)S(1)} %copy-done.9, f32[32,2048]{1,0:T(8,128)S(1)} %get-tuple-element.268.refs_0_, f32[32,2048]{1,0:T(8,128)S(1)} %collective-permute-done.25.refs_1_, ...), custom_call_target="tpu_custom_call" | custom-call | flops 3221225472 | bytes 1 | tf_op jit(solution)/shard_map/product/pallas_call | solution.py:173
  98.0 2.2 %collective-permute-start.30 = (f32[32,1024]{1,0:T(8,128)S(1)}, f32[32,1024]{1,0:T(8,128)S(1)}, u32[]{:S(2)}, u32[]{:S(2)}) collective-permute-start(f32[32,1024]{1,0:T(8,128)S(1)} %get-tuple-element.350), channel_id=1, source_target_pairs={{0,16},{4,20},{8,24},{12,28},{16,0},{20,4},{24,8},{28,12},{1,17},{... | collective-permute-start | bytes 393224 | tf_op jit(solution)/shard_map/ppermute | solution.py:242
  100.2 2.5 %product.13 = (f32[64,1024]{1,0:T(8,128)S(1)}, f32[64,1024]{1,0:T(8,128)S(1)}) custom-call(s32[3]{0:T(128)S(1)} %pad_add_fusion.place_ref, s32[8,64]{1,0:T(8,128)S(1)} %copy-done.8, s32[8]{0:T(128)S(1)} %copy-done.9, f32[32,2048]{1,0:T(8,128)S(1)} %get-tuple-element.268.refs_0_, f32[32,2048]{1,0:T(8,128)S(1)} %collective-permute-done.25.refs_1_, ...), custom_call_target="tpu_custom_call" | custom-call | flops 3221225472 | bytes 1 | tf_op jit(solution)/shard_map/product/pallas_call | solution.py:173
  106.3 2.8 %collective-permute-done.29 = f32[64,1024]{1,0:T(8,128)S(1)} collective-permute-done((f32[64,1024]{1,0:T(8,128)S(1)}, f32[64,1024]{1,0:T(8,128)S(1)}, u32[]{:S(2)}, u32[]{:S(2)}) %collective-permute-start.29) | collective-permute-done | bytes 262176 | tf_op jit(solution)/shard_map/ppermute | solution.py:242
  109.2 7.9 %collective-permute-done.37 = f32[32,1024]{1,0:T(8,128)S(1)} collective-permute-done((f32[32,1024]{1,0:T(8,128)S(1)}, f32[32,1024]{1,0:T(8,128)S(1)}, u32[]{:S(2)}, u32[]{:S(2)}) %collective-permute-start.37) | collective-permute-done | bytes 131104 | tf_op jit(solution)/shard_map/ppermute | solution.py:242
  119.4 2.5 %product.14 = (f32[64,1024]{1,0:T(8,128)S(1)}, f32[64,1024]{1,0:T(8,128)S(1)}) custom-call(s32[3]{0:T(128)S(1)} %pad_add_fusion.place_ref, s32[8,64]{1,0:T(8,128)S(1)} %copy-done.8, s32[8]{0:T(128)S(1)} %copy-done.9, f32[32,2048]{1,0:T(8,128)S(1)} %get-tuple-element.297.refs_0_, f32[32,2048]{1,0:T(8,128)S(1)} %collective-permute-done.33.refs_1_, ...), custom_call_target="tpu_custom_call" | custom-call | flops 3221225472 | bytes 1 | tf_op jit(solution)/shard_map/product/pallas_call | solution.py:173
  123.2 2.5 %product.15 = (f32[64,1024]{1,0:T(8,128)S(1)}, f32[64,1024]{1,0:T(8,128)S(1)}) custom-call(s32[3]{0:T(128)S(1)} %pad_add_fusion.place_ref, s32[8,64]{1,0:T(8,128)S(1)} %copy-done.8, s32[8]{0:T(128)S(1)} %copy-done.9, f32[32,2048]{1,0:T(8,128)S(1)} %get-tuple-element.297.refs_0_, f32[32,2048]{1,0:T(8,128)S(1)} %collective-permute-done.33.refs_1_, ...), custom_call_target="tpu_custom_call" | custom-call | flops 3221225472 | bytes 1 | tf_op jit(solution)/shard_map/product/pallas_call | solution.py:173
  126.8 4.1 %collective-permute-done.40 = f32[64,1024]{1,0:T(8,128)S(1)} collective-permute-done((f32[64,1024]{1,0:T(8,128)S(1)}, f32[64,1024]{1,0:T(8,128)S(1)}, u32[]{:S(2)}, u32[]{:S(2)}) %collective-permute-start.40) | collective-permute-done | bytes 262176 | tf_op jit(solution)/shard_map/ppermute | solution.py:242
  131.0 2.7 %collective-permute-start.42 = (f32[32,1024]{1,0:T(8,128)S(1)}, f32[32,1024]{1,0:T(8,128)S(1)}, u32[]{:S(2)}, u32[]{:S(2)}) collective-permute-start(f32[32,1024]{1,0:T(8,128)S(1)} %get-tuple-element.340), channel_id=1, source_target_pairs={{0,2},{1,3},{2,0},{3,1},{4,6},{5,7},{6,4},{7,5},{8,10},{9,11},{10,... | collective-permute-start | bytes 393224 | tf_op jit(solution)/shard_map/ppermute | solution.py:248
  136.5 6.3 %collective-permute-done.43 = f32[64,1024]{1,0:T(8,128)S(1)} collective-permute-done((f32[64,1024]{1,0:T(8,128)S(1)}, f32[64,1024]{1,0:T(8,128)S(1)}, u32[]{:S(2)}, u32[]{:S(2)}) %collective-permute-start.43) | collective-permute-done | bytes 262176 | tf_op jit(solution)/shard_map/ppermute | solution.py:248
  143.1 2.9 %collective-permute-done.48 = f32[64,1024]{1,0:T(8,128)S(1)} collective-permute-done((f32[64,1024]{1,0:T(8,128)S(1)}, f32[64,1024]{1,0:T(8,128)S(1)}, u32[]{:S(2)}, u32[]{:S(2)}) %collective-permute-start.48) | collective-permute-done | bytes 262176 | tf_op jit(solution)/shard_map/ppermute | solution.py:248
  148.1 3.1 %collective-permute-done.50 = f32[32,1024]{1,0:T(8,128)S(1)} collective-permute-done((f32[32,1024]{1,0:T(8,128)S(1)}, f32[32,1024]{1,0:T(8,128)S(1)}, u32[]{:S(2)}, u32[]{:S(2)}) %collective-permute-start.50) | collective-permute-done | bytes 131104 | tf_op jit(solution)/shard_map/ppermute | solution.py:242
  152.4 5.3 %collective-permute-done.49.refs_13_ = f32[32,1024]{1,0:T(8,128)S(1)} collective-permute-done((f32[32,1024]{1,0:T(8,128)S(1)}, f32[32,1024]{1,0:T(8,128)S(1)}, u32[]{:S(2)}, u32[]{:S(2)}) %collective-permute-start.49) | collective-permute-done | bytes 131104 | tf_op jit(solution)/shard_map/ppermute | solution.py:248
  (151 shorter events, 55.0 us)
Async XLA Ops:
  0.0 50.0 %collective-permute-start.16 = (f32[2048,1024]{1,0:T(8,128)}, f32[2048,1024]{1,0:T(8,128)}, u32[]{:S(2)}, u32[]{:S(2)}) collective-permute-start(f32[2048,1024]{1,0:T(8,128)} %whole_ref.2), channel_id=1, source_target_pairs={{0,4},{4,0},{8,12},{12,8},{16,20},{20,16},{24,28},{28,24},{1,5},{5... | collective-permute-start | bytes 25165832 | tf_op jit(solution)/shard_map/ppermute | solution.py:242
  33.7 15.8 %collective-permute-start.7 = (f32[64,1024]{1,0:T(8,128)S(1)}, f32[64,1024]{1,0:T(8,128)S(1)}, u32[]{:S(2)}, u32[]{:S(2)}) collective-permute-start(f32[64,1024]{1,0:T(8,128)S(1)} %get-tuple-element.196), channel_id=1, source_target_pairs={{0,8},{4,12},{8,0},{12,4},{16,24},{20,28},{24,16},{28,20},{1,9},{5... | collective-permute-start | bytes 786440 | tf_op jit(solution)/shard_map/ppermute | solution.py:242
  45.0 12.0 %collective-permute-start.15 = (f32[32,2048]{1,0:T(8,128)S(1)}, f32[32,2048]{1,0:T(8,128)S(1)}, u32[]{:S(2)}, u32[]{:S(2)}) collective-permute-start(f32[32,2048]{1,0:T(8,128)S(1)} %pack.4.refs_0_), channel_id=1, source_target_pairs={{0,8},{4,12},{8,0},{12,4},{16,24},{20,28},{24,16},{28,20},{1,9},{5... | collective-permute-start | bytes 786440 | tf_op jit(solution)/shard_map/ppermute | solution.py:242
  45.6 14.5 %collective-permute-start.12 = (f32[16,2048]{1,0:T(8,128)S(1)}, f32[16,2048]{1,0:T(8,128)S(1)}, u32[]{:S(2)}, u32[]{:S(2)}) collective-permute-start(f32[16,2048]{1,0:T(8,128)S(1)} %get-tuple-element.209), channel_id=1, source_target_pairs={{0,1},{1,0},{2,3},{3,2},{4,5},{5,4},{6,7},{7,6},{8,9},{9,8},{10,11... | collective-permute-start | bytes 393224 | tf_op jit(solution)/shard_map/ppermute | solution.py:248
  45.8 14.3 %collective-permute-start.13 = (f32[16,2048]{1,0:T(8,128)S(1)}, f32[16,2048]{1,0:T(8,128)S(1)}, u32[]{:S(2)}, u32[]{:S(2)}) collective-permute-start(f32[16,2048]{1,0:T(8,128)S(1)} %get-tuple-element.210), channel_id=1, source_target_pairs={{0,2},{1,3},{2,0},{3,1},{4,6},{5,7},{6,4},{7,5},{8,10},{9,11},{10,... | collective-permute-start | bytes 393224 | tf_op jit(solution)/shard_map/ppermute | solution.py:248
  49.6 10.6 %collective-permute-start.14 = (f32[16,2048]{1,0:T(8,128)S(1)}, f32[16,2048]{1,0:T(8,128)S(1)}, u32[]{:S(2)}, u32[]{:S(2)}) collective-permute-start(f32[16,2048]{1,0:T(8,128)S(1)} %get-tuple-element.211), channel_id=1, source_target_pairs={{0,3},{1,2},{2,1},{3,0},{4,7},{5,6},{6,5},{7,4},{8,11},{9,10},{10,... | collective-permute-start | bytes 393224 | tf_op jit(solution)/shard_map/ppermute | solution.py:248
  50.0 9.5 %collective-permute-start.8 = (f32[64,1024]{1,0:T(8,128)S(1)}, f32[64,1024]{1,0:T(8,128)S(1)}, u32[]{:S(2)}, u32[]{:S(2)}) collective-permute-start(f32[64,1024]{1,0:T(8,128)S(1)} %broadcast_select_fusion.7), channel_id=1, source_target_pairs={{0,1},{1,0},{2,3},{3,2},{4,5},{5,4},{6,7},{7,6},{8,9},{9,8},{10,11... | collective-permute-start | bytes 786440 | tf_op jit(solution)/shard_map/ppermute | solution.py:248
  59.6 13.9 %collective-permute-start.18 = (f32[64,2048]{1,0:T(8,128)S(1)}, f32[64,2048]{1,0:T(8,128)S(1)}, u32[]{:S(2)}, u32[]{:S(2)}) collective-permute-start(f32[64,2048]{1,0:T(8,128)S(1)} %constant_dynamic-update-slice_fusion), channel_id=1, source_target_pairs={{0,16},{4,20},{8,24},{12,28},{16,0},{20,4},{24,8},{28,12},{1,17},{... | collective-permute-start | bytes 1572872 | tf_op jit(solution)/shard_map/ppermute | solution.py:242
  60.8 20.5 %collective-permute-start.25 = (f32[32,2048]{1,0:T(8,128)S(1)}, f32[32,2048]{1,0:T(8,128)S(1)}, u32[]{:S(2)}, u32[]{:S(2)}) collective-permute-start(f32[32,2048]{1,0:T(8,128)S(1)} %get-tuple-element.268.refs_0_), channel_id=1, source_target_pairs={{0,8},{4,12},{8,0},{12,4},{16,24},{20,28},{24,16},{28,20},{1,9},{5... | collective-permute-start | bytes 786440 | tf_op jit(solution)/shard_map/ppermute | solution.py:242
  62.2 18.3 %collective-permute-start.17 = (f32[32,1024]{1,0:T(8,128)S(1)}, f32[32,1024]{1,0:T(8,128)S(1)}, u32[]{:S(2)}, u32[]{:S(2)}) collective-permute-start(f32[32,1024]{1,0:T(8,128)S(1)} %get-tuple-element.357), channel_id=1, source_target_pairs={{0,16},{4,20},{8,24},{12,28},{16,0},{20,4},{24,8},{28,12},{1,17},{... | collective-permute-start | bytes 393224 | tf_op jit(solution)/shard_map/ppermute | solution.py:242
  65.4 11.9 %collective-permute-start.20 = (f32[64,1024]{1,0:T(8,128)S(1)}, f32[64,1024]{1,0:T(8,128)S(1)}, u32[]{:S(2)}, u32[]{:S(2)}) collective-permute-start(f32[64,1024]{1,0:T(8,128)S(1)} %broadcast_select_fusion.6), channel_id=1, source_target_pairs={{0,1},{1,0},{2,3},{3,2},{4,5},{5,4},{6,7},{7,6},{8,9},{9,8},{10,11... | collective-permute-start | bytes 786440 | tf_op jit(solution)/shard_map/ppermute | solution.py:248
  67.9 34.7 %collective-permute-start.33 = (f32[32,2048]{1,0:T(8,128)S(1)}, f32[32,2048]{1,0:T(8,128)S(1)}, u32[]{:S(2)}, u32[]{:S(2)}) collective-permute-start(f32[32,2048]{1,0:T(8,128)S(1)} %get-tuple-element.297.refs_0_), channel_id=1, source_target_pairs={{0,8},{4,12},{8,0},{12,4},{16,24},{20,28},{24,16},{28,20},{1,9},{5... | collective-permute-start | bytes 786440 | tf_op jit(solution)/shard_map/ppermute | solution.py:242
  75.9 8.5 %collective-permute-start.24 = (f32[64,1024]{1,0:T(8,128)S(1)}, f32[64,1024]{1,0:T(8,128)S(1)}, u32[]{:S(2)}, u32[]{:S(2)}) collective-permute-start(f32[64,1024]{1,0:T(8,128)S(1)} %get-tuple-element.241), channel_id=1, source_target_pairs={{0,8},{4,12},{8,0},{12,4},{16,24},{20,28},{24,16},{28,20},{1,9},{5... | collective-permute-start | bytes 786440 | tf_op jit(solution)/shard_map/ppermute | solution.py:242
  77.4 9.9 %collective-permute-start.22 = (f32[32,1024]{1,0:T(8,128)S(1)}, f32[32,1024]{1,0:T(8,128)S(1)}, u32[]{:S(2)}, u32[]{:S(2)}) collective-permute-start(f32[32,1024]{1,0:T(8,128)S(1)} %get-tuple-element.354), channel_id=1, source_target_pairs={{0,16},{4,20},{8,24},{12,28},{16,0},{20,4},{24,8},{28,12},{1,17},{... | collective-permute-start | bytes 393224 | tf_op jit(solution)/shard_map/ppermute | solution.py:242
  84.4 9.2 %collective-permute-start.27 = (f32[64,2048]{1,0:T(8,128)S(1)}, f32[64,2048]{1,0:T(8,128)S(1)}, u32[]{:S(2)}, u32[]{:S(2)}) collective-permute-start(f32[64,2048]{1,0:T(8,128)S(1)} %constant_dynamic-update-slice_fusion.2), channel_id=1, source_target_pairs={{0,16},{4,20},{8,24},{12,28},{16,0},{20,4},{24,8},{28,12},{1,17},{... | collective-permute-start | bytes 1572872 | tf_op jit(solution)/shard_map/ppermute | solution.py:242
  87.2 10.6 %collective-permute-start.28 = (f32[64,1024]{1,0:T(8,128)S(1)}, f32[64,1024]{1,0:T(8,128)S(1)}, u32[]{:S(2)}, u32[]{:S(2)}) collective-permute-start(f32[64,1024]{1,0:T(8,128)S(1)} %broadcast_select_fusion.5), channel_id=1, source_target_pairs={{0,1},{1,0},{2,3},{3,2},{4,5},{5,4},{6,7},{7,6},{8,9},{9,8},{10,11... | collective-permute-start | bytes 786440 | tf_op jit(solution)/shard_map/ppermute | solution.py:248
  87.3 16.6 %collective-permute-start.32 = (f32[64,1024]{1,0:T(8,128)S(1)}, f32[64,1024]{1,0:T(8,128)S(1)}, u32[]{:S(2)}, u32[]{:S(2)}) collective-permute-start(f32[64,1024]{1,0:T(8,128)S(1)} %broadcast_select_fusion.4), channel_id=1, source_target_pairs={{0,1},{1,0},{2,3},{3,2},{4,5},{5,4},{6,7},{7,6},{8,9},{9,8},{10,11... | collective-permute-start | bytes 786440 | tf_op jit(solution)/shard_map/ppermute | solution.py:248
  89.4 19.7 %collective-permute-start.26 = (f32[32,1024]{1,0:T(8,128)S(1)}, f32[32,1024]{1,0:T(8,128)S(1)}, u32[]{:S(2)}, u32[]{:S(2)}) collective-permute-start(f32[32,1024]{1,0:T(8,128)S(1)} %get-tuple-element.352), channel_id=1, source_target_pairs={{0,2},{1,3},{2,0},{3,1},{4,6},{5,7},{6,4},{7,5},{8,10},{9,11},{10,... | collective-permute-start | bytes 393224 | tf_op jit(solution)/shard_map/ppermute | solution.py:248
  103.9 15.5 %collective-permute-start.35 = (f32[64,2048]{1,0:T(8,128)S(1)}, f32[64,2048]{1,0:T(8,128)S(1)}, u32[]{:S(2)}, u32[]{:S(2)}) collective-permute-start(f32[64,2048]{1,0:T(8,128)S(1)} %constant_dynamic-update-slice_fusion.4), channel_id=1, source_target_pairs={{0,16},{4,20},{8,24},{12,28},{16,0},{20,4},{24,8},{28,12},{1,17},{... | collective-permute-start | bytes 1572872 | tf_op jit(solution)/shard_map/ppermute | solution.py:242
  104.7 12.5 %collective-permute-start.37 = (f32[32,1024]{1,0:T(8,128)S(1)}, f32[32,1024]{1,0:T(8,128)S(1)}, u32[]{:S(2)}, u32[]{:S(2)}) collective-permute-start(f32[32,1024]{1,0:T(8,128)S(1)} %get-tuple-element.346), channel_id=1, source_target_pairs={{0,16},{4,20},{8,24},{12,28},{16,0},{20,4},{24,8},{28,12},{1,17},{... | collective-permute-start | bytes 393224 | tf_op jit(solution)/shard_map/ppermute | solution.py:242
  106.2 11.1 %collective-permute-start.36 = (f32[64,1024]{1,0:T(8,128)S(1)}, f32[64,1024]{1,0:T(8,128)S(1)}, u32[]{:S(2)}, u32[]{:S(2)}) collective-permute-start(f32[64,1024]{1,0:T(8,128)S(1)} %broadcast_select_fusion.3), channel_id=1, source_target_pairs={{0,1},{1,0},{2,3},{3,2},{4,5},{5,4},{6,7},{7,6},{8,9},{9,8},{10,11... | collective-permute-start | bytes 786440 | tf_op jit(solution)/shard_map/ppermute | solution.py:248
  109.1 13.7 %collective-permute-start.34 = (f32[32,1024]{1,0:T(8,128)S(1)}, f32[32,1024]{1,0:T(8,128)S(1)}, u32[]{:S(2)}, u32[]{:S(2)}) collective-permute-start(f32[32,1024]{1,0:T(8,128)S(1)} %get-tuple-element.348), channel_id=1, source_target_pairs={{0,2},{1,3},{2,0},{3,1},{4,6},{5,7},{6,4},{7,5},{8,10},{9,11},{10,... | collective-permute-start | bytes 393224 | tf_op jit(solution)/shard_map/ppermute | solution.py:248
  109.2 13.7 %collective-permute-start.41 = (f32[64,1024]{1,0:T(8,128)S(1)}, f32[64,1024]{1,0:T(8,128)S(1)}, u32[]{:S(2)}, u32[]{:S(2)}) collective-permute-start(f32[64,1024]{1,0:T(8,128)S(1)} %broadcast_select_fusion.2), channel_id=1, source_target_pairs={{0,1},{1,0},{2,3},{3,2},{4,5},{5,4},{6,7},{7,6},{8,9},{9,8},{10,11... | collective-permute-start | bytes 786440 | tf_op jit(solution)/shard_map/ppermute | solution.py:248
  117.2 16.5 %collective-permute-start.38 = (f32[32,1024]{1,0:T(8,128)S(1)}, f32[32,1024]{1,0:T(8,128)S(1)}, u32[]{:S(2)}, u32[]{:S(2)}) collective-permute-start(f32[32,1024]{1,0:T(8,128)S(1)} %get-tuple-element.344), channel_id=1, source_target_pairs={{0,2},{1,3},{2,0},{3,1},{4,6},{5,7},{6,4},{7,5},{8,10},{9,11},{10,... | collective-permute-start | bytes 393224 | tf_op jit(solution)/shard_map/ppermute | solution.py:248
  117.4 13.6 %collective-permute-start.39 = (f32[32,1024]{1,0:T(8,128)S(1)}, f32[32,1024]{1,0:T(8,128)S(1)}, u32[]{:S(2)}, u32[]{:S(2)}) collective-permute-start(f32[32,1024]{1,0:T(8,128)S(1)} %get-tuple-element.342), channel_id=1, source_target_pairs={{0,16},{4,20},{8,24},{12,28},{16,0},{20,4},{24,8},{28,12},{1,17},{... | collective-permute-start | bytes 393224 | tf_op jit(solution)/shard_map/ppermute | solution.py:242
  121.9 9.0 %collective-permute-start.40 = (f32[64,1024]{1,0:T(8,128)S(1)}, f32[64,1024]{1,0:T(8,128)S(1)}, u32[]{:S(2)}, u32[]{:S(2)}) collective-permute-start(f32[64,1024]{1,0:T(8,128)S(1)} %get-tuple-element.293), channel_id=1, source_target_pairs={{0,8},{4,12},{8,0},{12,4},{16,24},{20,28},{24,16},{28,20},{1,9},{5... | collective-permute-start | bytes 786440 | tf_op jit(solution)/shard_map/ppermute | solution.py:242
  122.9 12.9 %collective-permute-start.44 = (f32[32,1024]{1,0:T(8,128)S(1)}, f32[32,1024]{1,0:T(8,128)S(1)}, u32[]{:S(2)}, u32[]{:S(2)}) collective-permute-start(f32[32,1024]{1,0:T(8,128)S(1)} %get-tuple-element.338), channel_id=1, source_target_pairs={{0,16},{4,20},{8,24},{12,28},{16,0},{20,4},{24,8},{28,12},{1,17},{... | collective-permute-start | bytes 393224 | tf_op jit(solution)/shard_map/ppermute | solution.py:242
  130.9 12.0 %collective-permute-start.43 = (f32[64,1024]{1,0:T(8,128)S(1)}, f32[64,1024]{1,0:T(8,128)S(1)}, u32[]{:S(2)}, u32[]{:S(2)}) collective-permute-start(f32[64,1024]{1,0:T(8,128)S(1)} %broadcast_select_fusion.1), channel_id=1, source_target_pairs={{0,1},{1,0},{2,3},{3,2},{4,5},{5,4},{6,7},{7,6},{8,9},{9,8},{10,11... | collective-permute-start | bytes 786440 | tf_op jit(solution)/shard_map/ppermute | solution.py:248
  131.0 12.1 %collective-permute-start.42 = (f32[32,1024]{1,0:T(8,128)S(1)}, f32[32,1024]{1,0:T(8,128)S(1)}, u32[]{:S(2)}, u32[]{:S(2)}) collective-permute-start(f32[32,1024]{1,0:T(8,128)S(1)} %get-tuple-element.340), channel_id=1, source_target_pairs={{0,2},{1,3},{2,0},{3,1},{4,6},{5,7},{6,4},{7,5},{8,10},{9,11},{10,... | collective-permute-start | bytes 393224 | tf_op jit(solution)/shard_map/ppermute | solution.py:248
  133.7 12.3 %collective-permute-start.48 = (f32[64,1024]{1,0:T(8,128)S(1)}, f32[64,1024]{1,0:T(8,128)S(1)}, u32[]{:S(2)}, u32[]{:S(2)}) collective-permute-start(f32[64,1024]{1,0:T(8,128)S(1)} %broadcast_select_fusion), channel_id=1, source_target_pairs={{0,1},{1,0},{2,3},{3,2},{4,5},{5,4},{6,7},{7,6},{8,9},{9,8},{10,11... | collective-permute-start | bytes 786440 | tf_op jit(solution)/shard_map/ppermute | solution.py:248
  135.8 12.2 %collective-permute-start.46 = (f32[32,1024]{1,0:T(8,128)S(1)}, f32[32,1024]{1,0:T(8,128)S(1)}, u32[]{:S(2)}, u32[]{:S(2)}) collective-permute-start(f32[32,1024]{1,0:T(8,128)S(1)} %get-tuple-element.336), channel_id=1, source_target_pairs={{0,2},{1,3},{2,0},{3,1},{4,6},{5,7},{6,4},{7,5},{8,10},{9,11},{10,... | collective-permute-start | bytes 393224 | tf_op jit(solution)/shard_map/ppermute | solution.py:248
  148.0 9.8 %collective-permute-start.49 = (f32[32,1024]{1,0:T(8,128)S(1)}, f32[32,1024]{1,0:T(8,128)S(1)}, u32[]{:S(2)}, u32[]{:S(2)}) collective-permute-start(f32[32,1024]{1,0:T(8,128)S(1)} %get-tuple-element.332), channel_id=1, source_target_pairs={{0,2},{1,3},{2,0},{3,1},{4,6},{5,7},{6,4},{7,5},{8,10},{9,11},{10,... | collective-permute-start | bytes 393224 | tf_op jit(solution)/shard_map/ppermute | solution.py:248
  (31 other events, 291.9 us)

commit v10 on v9

--- a/solution.py
+++ b/solution.py
@@ -14,10 +14,10 @@
 UNITS = tuple((chunk, (half,)) for chunk in range(CHUNKS) for half in range(CORES))
 
 ORDER = (
-    "s0", "s1", "p0", "g00", "g01", "f0", "e0", "p1", "g10", "s2", "f1", "r0", "e1", "g11",
-    "p2", "g20", "x0", "r1", "g30", "e2", "x1", "e3", "z0", "g21", "r2", "r3", "z1", "l0",
-    "e4", "x2", "e5", "g31", "x3", "r4", "z2", "r5", "l1", "z3", "x4", "e6", "l2", "x5", "e7",
-    "r6", "z4", "l3", "r7", "z5", "x6", "l4", "x7", "z6", "l5", "z7", "l6", "l7",
+    "s0", "s1", "p0", "g00", "p1", "g01", "g10", "s2", "f0", "e0", "g11", "p2", "g20", "f1",
+    "e1", "r0", "g21", "e3", "g30", "r1", "x0", "e2", "r3", "x1", "z0", "g31", "e5", "z1",
+    "x3", "r2", "l0", "e4", "r5", "e7", "z3", "x2", "l1", "r4", "e6", "x5", "z2", "r7", "x4",
+    "z5", "l3", "r6", "l2", "z4", "x7", "z7", "l5", "x6", "l4", "z6", "l7", "l6",
 )
 
 SMEM = pl.BlockSpec(memory_space=pltpu.SMEM)

time: 161 us -> 144 us (0.89)
  waiting for transfers between devices: 67.8 us -> 41.5 us
  starting transfers between devices: 55.3 us -> 65.3 us
    ppermute x27, waiting for transfers between devices: 39.6 us -> 9.31 us  [across(): lax.ppermute(value, 'wide', [(w, w ^ mask) for w in range(wide_count)])]
    ppermute x25, starting transfers between devices: 26.1 us -> 31.9 us  [along(): lax.ppermute(value, 'narrow', [(n, n ^ mask) for n in range(narrow_count)])]
    ppermute x27, starting transfers between devices: 29.1 us -> 33.4 us  [across(): lax.ppermute(value, 'wide', [(w, w ^ mask) for w in range(wide_count)])]
    ppermute x25, waiting for transfers between devices: 28.2 us -> 32.2 us  [along(): lax.ppermute(value, 'narrow', [(n, n ^ mask) for n in range(narrow_count)])]
    unnamed x25 -> x17, local copies, waits for them, and re-layouts: 5.5 us -> 4.69 us
  transfers between devices with their start and end apart: 52 -> 52, of which waited for: 25 -> 20; matrix products, arithmetic and copies ran while one was open for 1% -> 1% of each run, Pallas kernels for 18% -> 20%
where the time goes in v10:
time: 144 us
  starting transfers between devices  65.3 us (45%)
  waiting for transfers between devices  41.5 us (29%)
  Pallas kernels  30.6 us (21%)
  local copies, waits for them, and re-layouts  5.03 us (3%)
    ppermute x27, starting transfers between devices, across(): lax.ppermute(value, 'wide', [(w, w ^ mask) for w in range(wide_count)])  33.4 us
    ppermute x25, waiting for transfers between devices, along(): lax.ppermute(value, 'narrow', [(n, n ^ mask) for n in range(narrow_count)])  32.2 us
    ppermute x25, starting transfers between devices, along(): lax.ppermute(value, 'narrow', [(n, n ^ mask) for n in range(narrow_count)])  31.9 us
    pallas_call x8, Pallas kernels, product(): pl.pallas_call(functools.partial(product_kernel, count, rows, layout, tar...  20 us
    ppermute x27, waiting for transfers between devices, across(): lax.ppermute(value, 'wide', [(w, w ^ mask) for w in range(wide_count)])  9.31 us
    pallas_call x2, Pallas kernels, split(): pl.pallas_call(functools.partial(split_kernel, step), in_specs=[HBM], out...  6.48 us
    unnamed x17, local copies, waits for them, and re-layouts  4.69 us
  transfers between devices with their start and end apart: 52, of which 20 were waited for; matrix products, arithmetic and copies ran while one was open for 1% of the time, Pallas kernels for 20%

profile of v10, /device:TPU:0, one launch (start us, length us, event | category | flops | bytes accessed | tf_op | source)
XLA Modules:
  0.0 144.0 jit_solution(5663897417024937645)
XLA Ops:
  2.4 2.6 %collective-permute-start = (f32[8,2048]{1,0:T(8,128)S(1)}, f32[8,2048]{1,0:T(8,128)S(1)}, u32[]{:S(2)}, u32[]{:S(2)}) collective-permute-start(f32[8,2048]{1,0:T(8,128)S(1)} %get-tuple-element.165), channel_id=1, source_target_pairs={{0,1},{1,0},{2,3},{3,2},{4,5},{5,4},{6,7},{7,6},{8,9},{9,8},{10,11... | collective-permute-start | bytes 196616 | tf_op jit(solution)/shard_map/ppermute | solution.py:248
  5.0 2.6 %collective-permute-start.1 = (f32[8,2048]{1,0:T(8,128)S(1)}, f32[8,2048]{1,0:T(8,128)S(1)}, u32[]{:S(2)}, u32[]{:S(2)}) collective-permute-start(f32[8,2048]{1,0:T(8,128)S(1)} %get-tuple-element.166), channel_id=1, source_target_pairs={{0,2},{1,3},{2,0},{3,1},{4,6},{5,7},{6,4},{7,5},{8,10},{9,11},{10,... | collective-permute-start | bytes 196616 | tf_op jit(solution)/shard_map/ppermute | solution.py:248
  7.8 4.2 %collective-permute-done.1.refs_2_ = f32[8,2048]{1,0:T(8,128)S(1)} collective-permute-done((f32[8,2048]{1,0:T(8,128)S(1)}, f32[8,2048]{1,0:T(8,128)S(1)}, u32[]{:S(2)}, u32[]{:S(2)}) %collective-permute-start.1) | collective-permute-done | bytes 65568 | tf_op jit(solution)/shard_map/ppermute | solution.py:248
  21.7 2.9 %collective-permute-start.7 = (f32[8,2048]{1,0:T(8,128)S(1)}, f32[8,2048]{1,0:T(8,128)S(1)}, u32[]{:S(2)}, u32[]{:S(2)}) collective-permute-start(f32[8,2048]{1,0:T(8,128)S(1)} %get-tuple-element.173), channel_id=1, source_target_pairs={{0,3},{1,2},{2,1},{3,0},{4,7},{5,6},{6,5},{7,4},{8,11},{9,10},{10,... | collective-permute-start | bytes 196616 | tf_op jit(solution)/shard_map/ppermute | solution.py:248
  25.7 2.1 %collective-permute-done.7.refs_3_ = f32[8,2048]{1,0:T(8,128)S(1)} collective-permute-done((f32[8,2048]{1,0:T(8,128)S(1)}, f32[8,2048]{1,0:T(8,128)S(1)}, u32[]{:S(2)}, u32[]{:S(2)}) %collective-permute-start.7) | collective-permute-done | bytes 65568 | tf_op jit(solution)/shard_map/ppermute | solution.py:248
  31.1 3.4 %copy-done = f32[2048,1024]{1,0:T(8,128)S(1)} copy-done((f32[2048,1024]{1,0:T(8,128)S(1)}, f32[2048,1024]{1,0:T(8,128)}, u32[]{:S(2)}) %copy-start) | copy-done | bytes 8388632
  34.5 2.2 %split.2 = (bf16[2048,1024]{1,0:T(8,128)(2,1)S(1)}, bf16[2048,1024]{1,0:T(8,128)(2,1)S(1)}, f32[8,128]{1,0:T(8,128)}) custom-call(f32[2048,1024]{1,0:T(8,128)S(1)} %copy-done), custom_call_target="tpu_custom_call" | custom-call | flops 1 | bytes 1 | tf_op jit(solution)/shard_map/split/pallas_call | solution.py:112
  36.6 3.5 %collective-permute-start.13 = (f32[16,2048]{1,0:T(8,128)S(1)}, f32[16,2048]{1,0:T(8,128)S(1)}, u32[]{:S(2)}, u32[]{:S(2)}) collective-permute-start(f32[16,2048]{1,0:T(8,128)S(1)} %get-tuple-element.196), channel_id=1, source_target_pairs={{0,2},{1,3},{2,0},{3,1},{4,6},{5,7},{6,4},{7,5},{8,10},{9,11},{10,... | collective-permute-start | bytes 393224 | tf_op jit(solution)/shard_map/ppermute | solution.py:248
  41.1 2.5 %product.8 = (f32[64,1024]{1,0:T(8,128)S(1)}, f32[64,1024]{1,0:T(8,128)S(1)}) custom-call(s32[3]{0:T(128)S(1)} %pad_add_fusion.place_ref, s32[8,64]{1,0:T(8,128)S(1)} %copy-done.4, s32[8]{0:T(128)S(1)} %copy-done.5, f32[32,2048]{1,0:T(8,128)S(1)} %pack.3.refs_0_, f32[32,2048]{1,0:T(8,128)S(1)} %collective-permute-done.3.refs_1_, ...), custom_call_target="tpu_custom_call" | custom-call | flops 3221225472 | bytes 1 | tf_op jit(solution)/shard_map/product/pallas_call | solution.py:173
  48.4 4.3 %split.3 = (bf16[2048,1024]{1,0:T(8,128)(2,1)S(1)}, bf16[2048,1024]{1,0:T(8,128)(2,1)S(1)}, f32[8,128]{1,0:T(8,128)}) custom-call(f32[2048,1024]{1,0:T(8,128)} %collective-permute-done.11.whole_ref), custom_call_target="tpu_custom_call" | custom-call | flops 1 | bytes 1 | tf_op jit(solution)/shard_map/split/pallas_call | solution.py:112
  52.7 2.5 %product.9 = (f32[64,1024]{1,0:T(8,128)S(1)}, f32[64,1024]{1,0:T(8,128)S(1)}) custom-call(s32[3]{0:T(128)S(1)} %pad_add_fusion.place_ref, s32[8,64]{1,0:T(8,128)S(1)} %copy-done.4, s32[8]{0:T(128)S(1)} %copy-done.5, f32[32,2048]{1,0:T(8,128)S(1)} %pack.3.refs_0_, f32[32,2048]{1,0:T(8,128)S(1)} %collective-permute-done.3.refs_1_, ...), custom_call_target="tpu_custom_call" | custom-call | flops 3221225472 | bytes 1 | tf_op jit(solution)/shard_map/product/pallas_call | solution.py:173
  56.8 2.0 %collective-permute-start.16 = (f32[64,1024]{1,0:T(8,128)S(1)}, f32[64,1024]{1,0:T(8,128)S(1)}, u32[]{:S(2)}, u32[]{:S(2)}) collective-permute-start(f32[64,1024]{1,0:T(8,128)S(1)} %broadcast_select_fusion.7), channel_id=1, source_target_pairs={{0,1},{1,0},{2,3},{3,2},{4,5},{5,4},{6,7},{7,6},{8,9},{9,8},{10,11... | collective-permute-start | bytes 786440 | tf_op jit(solution)/shard_map/ppermute | solution.py:248
  58.9 2.5 %product.10 = (f32[64,1024]{1,0:T(8,128)S(1)}, f32[64,1024]{1,0:T(8,128)S(1)}) custom-call(s32[3]{0:T(128)S(1)} %pad_add_fusion.place_ref, s32[8,64]{1,0:T(8,128)S(1)} %copy-done.4, s32[8]{0:T(128)S(1)} %copy-done.5, f32[32,2048]{1,0:T(8,128)S(1)} %pack.4.refs_0_, f32[32,2048]{1,0:T(8,128)S(1)} %collective-permute-done.15.refs_1_, ...), custom_call_target="tpu_custom_call" | custom-call | flops 3221225472 | bytes 1 | tf_op jit(solution)/shard_map/product/pallas_call | solution.py:173
  67.1 2.5 %product.11 = (f32[64,1024]{1,0:T(8,128)S(1)}, f32[64,1024]{1,0:T(8,128)S(1)}) custom-call(s32[3]{0:T(128)S(1)} %pad_add_fusion.place_ref, s32[8,64]{1,0:T(8,128)S(1)} %copy-done.4, s32[8]{0:T(128)S(1)} %copy-done.5, f32[32,2048]{1,0:T(8,128)S(1)} %pack.4.refs_0_, f32[32,2048]{1,0:T(8,128)S(1)} %collective-permute-done.15.refs_1_, ...), custom_call_target="tpu_custom_call" | custom-call | flops 3221225472 | bytes 1 | tf_op jit(solution)/shard_map/product/pallas_call | solution.py:173
  73.7 3.2 %collective-permute-done.20 = f32[32,1024]{1,0:T(8,128)S(1)} collective-permute-done((f32[32,1024]{1,0:T(8,128)S(1)}, f32[32,1024]{1,0:T(8,128)S(1)}, u32[]{:S(2)}, u32[]{:S(2)}) %collective-permute-start.20) | collective-permute-done | bytes 131104 | tf_op jit(solution)/shard_map/ppermute | solution.py:242
  79.2 2.5 %product.12 = (f32[64,1024]{1,0:T(8,128)S(1)}, f32[64,1024]{1,0:T(8,128)S(1)}) custom-call(s32[3]{0:T(128)S(1)} %pad_add_fusion.place_ref, s32[8,64]{1,0:T(8,128)S(1)} %copy-done.4, s32[8]{0:T(128)S(1)} %copy-done.5, f32[32,2048]{1,0:T(8,128)S(1)} %get-tuple-element.260.refs_0_, f32[32,2048]{1,0:T(8,128)S(1)} %collective-permute-done.19.refs_1_, ...), custom_call_target="tpu_custom_call" | custom-call | flops 3221225472 | bytes 1 | tf_op jit(solution)/shard_map/product/pallas_call | solution.py:173
  83.4 3.0 %collective-permute-start.29 = (f32[32,1024]{1,0:T(8,128)S(1)}, f32[32,1024]{1,0:T(8,128)S(1)}, u32[]{:S(2)}, u32[]{:S(2)}) collective-permute-start(f32[32,1024]{1,0:T(8,128)S(1)} %get-tuple-element.342), channel_id=1, source_target_pairs={{0,2},{1,3},{2,0},{3,1},{4,6},{5,7},{6,4},{7,5},{8,10},{9,11},{10,... | collective-permute-start | bytes 393224 | tf_op jit(solution)/shard_map/ppermute | solution.py:248
  88.1 2.6 %product.13 = (f32[64,1024]{1,0:T(8,128)S(1)}, f32[64,1024]{1,0:T(8,128)S(1)}) custom-call(s32[3]{0:T(128)S(1)} %pad_add_fusion.place_ref, s32[8,64]{1,0:T(8,128)S(1)} %copy-done.4, s32[8]{0:T(128)S(1)} %copy-done.5, f32[32,2048]{1,0:T(8,128)S(1)} %get-tuple-element.260.refs_0_, f32[32,2048]{1,0:T(8,128)S(1)} %collective-permute-done.19.refs_1_, ...), custom_call_target="tpu_custom_call" | custom-call | flops 3221225472 | bytes 1 | tf_op jit(solution)/shard_map/product/pallas_call | solution.py:173
  91.4 3.1 %collective-permute-done.30 = f32[64,1024]{1,0:T(8,128)S(1)} collective-permute-done((f32[64,1024]{1,0:T(8,128)S(1)}, f32[64,1024]{1,0:T(8,128)S(1)}, u32[]{:S(2)}, u32[]{:S(2)}) %collective-permute-start.30) | collective-permute-done | bytes 262176 | tf_op jit(solution)/shard_map/ppermute | solution.py:248
  94.5 2.5 %product.14 = (f32[64,1024]{1,0:T(8,128)S(1)}, f32[64,1024]{1,0:T(8,128)S(1)}) custom-call(s32[3]{0:T(128)S(1)} %pad_add_fusion.place_ref, s32[8,64]{1,0:T(8,128)S(1)} %copy-done.4, s32[8]{0:T(128)S(1)} %copy-done.5, f32[32,2048]{1,0:T(8,128)S(1)} %get-tuple-element.281.refs_0_, f32[32,2048]{1,0:T(8,128)S(1)} %collective-permute-done.28.refs_1_, ...), custom_call_target="tpu_custom_call" | custom-call | flops 3221225472 | bytes 1 | tf_op jit(solution)/shard_map/product/pallas_call | solution.py:173
  97.0 2.6 %collective-permute-start.42 = (f32[64,1024]{1,0:T(8,128)S(1)}, f32[64,1024]{1,0:T(8,128)S(1)}, u32[]{:S(2)}, u32[]{:S(2)}) collective-permute-start(f32[64,1024]{1,0:T(8,128)S(1)} %get-tuple-element.273), channel_id=1, source_target_pairs={{0,8},{4,12},{8,0},{12,4},{16,24},{20,28},{24,16},{28,20},{1,9},{5... | collective-permute-start | bytes 786440 | tf_op jit(solution)/shard_map/ppermute | solution.py:242
  99.6 1.9 %collective-permute-start.39 = (f32[32,1024]{1,0:T(8,128)S(1)}, f32[32,1024]{1,0:T(8,128)S(1)}, u32[]{:S(2)}, u32[]{:S(2)}) collective-permute-start(f32[32,1024]{1,0:T(8,128)S(1)} %get-tuple-element.334), channel_id=1, source_target_pairs={{0,2},{1,3},{2,0},{3,1},{4,6},{5,7},{6,4},{7,5},{8,10},{9,11},{10,... | collective-permute-start | bytes 393224 | tf_op jit(solution)/shard_map/ppermute | solution.py:248
  103.5 2.5 %product.15 = (f32[64,1024]{1,0:T(8,128)S(1)}, f32[64,1024]{1,0:T(8,128)S(1)}) custom-call(s32[3]{0:T(128)S(1)} %pad_add_fusion.place_ref, s32[8,64]{1,0:T(8,128)S(1)} %copy-done.4, s32[8]{0:T(128)S(1)} %copy-done.5, f32[32,2048]{1,0:T(8,128)S(1)} %get-tuple-element.281.refs_0_, f32[32,2048]{1,0:T(8,128)S(1)} %collective-permute-done.28.refs_1_, ...), custom_call_target="tpu_custom_call" | custom-call | flops 3221225472 | bytes 1 | tf_op jit(solution)/shard_map/product/pallas_call | solution.py:173
  106.3 2.7 %collective-permute-start.38 = (f32[64,1024]{1,0:T(8,128)S(1)}, f32[64,1024]{1,0:T(8,128)S(1)}, u32[]{:S(2)}, u32[]{:S(2)}) collective-permute-start(f32[64,1024]{1,0:T(8,128)S(1)} %get-tuple-element.286), channel_id=1, source_target_pairs={{0,8},{4,12},{8,0},{12,4},{16,24},{20,28},{24,16},{28,20},{1,9},{5... | collective-permute-start | bytes 786440 | tf_op jit(solution)/shard_map/ppermute | solution.py:242
  110.3 4.8 %collective-permute-done.41 = f32[64,1024]{1,0:T(8,128)S(1)} collective-permute-done((f32[64,1024]{1,0:T(8,128)S(1)}, f32[64,1024]{1,0:T(8,128)S(1)}, u32[]{:S(2)}, u32[]{:S(2)}) %collective-permute-start.41) | collective-permute-done | bytes 262176 | tf_op jit(solution)/shard_map/ppermute | solution.py:248
  115.3 3.6 %collective-permute-start.46 = (f32[32,1024]{1,0:T(8,128)S(1)}, f32[32,1024]{1,0:T(8,128)S(1)}, u32[]{:S(2)}, u32[]{:S(2)}) collective-permute-start(f32[32,1024]{1,0:T(8,128)S(1)} %get-tuple-element.326), channel_id=1, source_target_pairs={{0,2},{1,3},{2,0},{3,1},{4,6},{5,7},{6,4},{7,5},{8,10},{9,11},{10,... | collective-permute-start | bytes 393224 | tf_op jit(solution)/shard_map/ppermute | solution.py:248
  119.3 1.9 %collective-permute-done.43 = f32[32,1024]{1,0:T(8,128)S(1)} collective-permute-done((f32[32,1024]{1,0:T(8,128)S(1)}, f32[32,1024]{1,0:T(8,128)S(1)}, u32[]{:S(2)}, u32[]{:S(2)}) %collective-permute-start.43) | collective-permute-done | bytes 131104 | tf_op jit(solution)/shard_map/ppermute | solution.py:242
  121.2 2.1 %collective-permute-start.44 = (f32[32,1024]{1,0:T(8,128)S(1)}, f32[32,1024]{1,0:T(8,128)S(1)}, u32[]{:S(2)}, u32[]{:S(2)}) collective-permute-start(f32[32,1024]{1,0:T(8,128)S(1)} %get-tuple-element.327), channel_id=1, source_target_pairs={{0,2},{1,3},{2,0},{3,1},{4,6},{5,7},{6,4},{7,5},{8,10},{9,11},{10,... | collective-permute-start | bytes 393224 | tf_op jit(solution)/shard_map/ppermute | solution.py:248
  125.7 4.1 %collective-permute-done.45 = f32[64,1024]{1,0:T(8,128)S(1)} collective-permute-done((f32[64,1024]{1,0:T(8,128)S(1)}, f32[64,1024]{1,0:T(8,128)S(1)}, u32[]{:S(2)}, u32[]{:S(2)}) %collective-permute-start.45) | collective-permute-done | bytes 262176 | tf_op jit(solution)/shard_map/ppermute | solution.py:248
  132.0 3.0 %collective-permute-done.49 = f32[32,1024]{1,0:T(8,128)S(1)} collective-permute-done((f32[32,1024]{1,0:T(8,128)S(1)}, f32[32,1024]{1,0:T(8,128)S(1)}, u32[]{:S(2)}, u32[]{:S(2)}) %collective-permute-start.49) | collective-permute-done | bytes 131104 | tf_op jit(solution)/shard_map/ppermute | solution.py:242
  136.0 2.2 %collective-permute-done.51.refs_15_ = f32[32,1024]{1,0:T(8,128)S(1)} collective-permute-done((f32[32,1024]{1,0:T(8,128)S(1)}, f32[32,1024]{1,0:T(8,128)S(1)}, u32[]{:S(2)}, u32[]{:S(2)}) %collective-permute-start.51) | collective-permute-done | bytes 131104 | tf_op jit(solution)/shard_map/ppermute | solution.py:248
  138.2 4.0 %collective-permute-done.50.refs_13_ = f32[32,1024]{1,0:T(8,128)S(1)} collective-permute-done((f32[32,1024]{1,0:T(8,128)S(1)}, f32[32,1024]{1,0:T(8,128)S(1)}, u32[]{:S(2)}, u32[]{:S(2)}) %collective-permute-start.50) | collective-permute-done | bytes 131104 | tf_op jit(solution)/shard_map/ppermute | solution.py:248
  (143 shorter events, 51.7 us)
Async XLA Ops:
  0.0 48.4 %collective-permute-start.11 = (f32[2048,1024]{1,0:T(8,128)}, f32[2048,1024]{1,0:T(8,128)}, u32[]{:S(2)}, u32[]{:S(2)}) collective-permute-start(f32[2048,1024]{1,0:T(8,128)} %whole_ref.2), channel_id=1, source_target_pairs={{0,4},{4,0},{8,12},{12,8},{16,20},{20,16},{24,28},{28,24},{1,5},{5... | collective-permute-start | bytes 25165832 | tf_op jit(solution)/shard_map/ppermute | solution.py:242
  14.3 14.1 %collective-permute-start.3 = (f32[32,2048]{1,0:T(8,128)S(1)}, f32[32,2048]{1,0:T(8,128)S(1)}, u32[]{:S(2)}, u32[]{:S(2)}) collective-permute-start(f32[32,2048]{1,0:T(8,128)S(1)} %pack.3.refs_0_), channel_id=1, source_target_pairs={{0,8},{4,12},{8,0},{12,4},{16,24},{20,28},{24,16},{28,20},{1,9},{5... | collective-permute-start | bytes 786440 | tf_op jit(solution)/shard_map/ppermute | solution.py:242
  15.9 12.5 %collective-permute-start.4 = (f32[32,2048]{1,0:T(8,128)S(1)}, f32[32,2048]{1,0:T(8,128)S(1)}, u32[]{:S(2)}, u32[]{:S(2)}) collective-permute-start(f32[32,2048]{1,0:T(8,128)S(1)} %pack.3.refs_0_), channel_id=1, source_target_pairs={{0,16},{4,20},{8,24},{12,28},{16,0},{20,4},{24,8},{28,12},{1,17},{... | collective-permute-start | bytes 786440 | tf_op jit(solution)/shard_map/ppermute | solution.py:242
  29.0 11.2 %collective-permute-start.9 = (f32[16,2048]{1,0:T(8,128)S(1)}, f32[16,2048]{1,0:T(8,128)S(1)}, u32[]{:S(2)}, u32[]{:S(2)}) collective-permute-start(f32[16,2048]{1,0:T(8,128)S(1)} %slice.55), channel_id=1, source_target_pairs={{0,8},{4,12},{8,0},{12,4},{16,24},{20,28},{24,16},{28,20},{1,9},{5... | collective-permute-start | bytes 393224 | tf_op jit(solution)/shard_map/ppermute | solution.py:242
  29.6 14.0 %collective-permute-start.15 = (f32[32,2048]{1,0:T(8,128)S(1)}, f32[32,2048]{1,0:T(8,128)S(1)}, u32[]{:S(2)}, u32[]{:S(2)}) collective-permute-start(f32[32,2048]{1,0:T(8,128)S(1)} %pack.4.refs_0_), channel_id=1, source_target_pairs={{0,8},{4,12},{8,0},{12,4},{16,24},{20,28},{24,16},{28,20},{1,9},{5... | collective-permute-start | bytes 786440 | tf_op jit(solution)/shard_map/ppermute | solution.py:242
  31.1 13.2 %collective-permute-start.12 = (f32[16,2048]{1,0:T(8,128)S(1)}, f32[16,2048]{1,0:T(8,128)S(1)}, u32[]{:S(2)}, u32[]{:S(2)}) collective-permute-start(f32[16,2048]{1,0:T(8,128)S(1)} %get-tuple-element.195), channel_id=1, source_target_pairs={{0,1},{1,0},{2,3},{3,2},{4,5},{5,4},{6,7},{7,6},{8,9},{9,8},{10,11... | collective-permute-start | bytes 393224 | tf_op jit(solution)/shard_map/ppermute | solution.py:248
  36.6 10.6 %collective-permute-start.13 = (f32[16,2048]{1,0:T(8,128)S(1)}, f32[16,2048]{1,0:T(8,128)S(1)}, u32[]{:S(2)}, u32[]{:S(2)}) collective-permute-start(f32[16,2048]{1,0:T(8,128)S(1)} %get-tuple-element.196), channel_id=1, source_target_pairs={{0,2},{1,3},{2,0},{3,1},{4,6},{5,7},{6,4},{7,5},{8,10},{9,11},{10,... | collective-permute-start | bytes 393224 | tf_op jit(solution)/shard_map/ppermute | solution.py:248
  43.6 13.2 %collective-permute-start.10 = (f32[64,1024]{1,0:T(8,128)S(1)}, f32[64,1024]{1,0:T(8,128)S(1)}, u32[]{:S(2)}, u32[]{:S(2)}) collective-permute-start(f32[64,1024]{1,0:T(8,128)S(1)} %get-tuple-element.203), channel_id=1, source_target_pairs={{0,8},{4,12},{8,0},{12,4},{16,24},{20,28},{24,16},{28,20},{1,9},{5... | collective-permute-start | bytes 786440 | tf_op jit(solution)/shard_map/ppermute | solution.py:242
  44.2 14.7 %collective-permute-start.18 = (f32[64,2048]{1,0:T(8,128)S(1)}, f32[64,2048]{1,0:T(8,128)S(1)}, u32[]{:S(2)}, u32[]{:S(2)}) collective-permute-start(f32[64,2048]{1,0:T(8,128)S(1)} %constant_dynamic-update-slice_fusion), channel_id=1, source_target_pairs={{0,16},{4,20},{8,24},{12,28},{16,0},{20,4},{24,8},{28,12},{1,17},{... | collective-permute-start | bytes 1572872 | tf_op jit(solution)/shard_map/ppermute | solution.py:242
  47.8 11.0 %collective-permute-start.19 = (f32[32,2048]{1,0:T(8,128)S(1)}, f32[32,2048]{1,0:T(8,128)S(1)}, u32[]{:S(2)}, u32[]{:S(2)}) collective-permute-start(f32[32,2048]{1,0:T(8,128)S(1)} %get-tuple-element.260.refs_0_), channel_id=1, source_target_pairs={{0,8},{4,12},{8,0},{12,4},{16,24},{20,28},{24,16},{28,20},{1,9},{5... | collective-permute-start | bytes 786440 | tf_op jit(solution)/shard_map/ppermute | solution.py:242
  55.2 9.8 %collective-permute-start.17 = (f32[64,1024]{1,0:T(8,128)S(1)}, f32[64,1024]{1,0:T(8,128)S(1)}, u32[]{:S(2)}, u32[]{:S(2)}) collective-permute-start(f32[64,1024]{1,0:T(8,128)S(1)} %get-tuple-element.219), channel_id=1, source_target_pairs={{0,8},{4,12},{8,0},{12,4},{16,24},{20,28},{24,16},{28,20},{1,9},{5... | collective-permute-start | bytes 786440 | tf_op jit(solution)/shard_map/ppermute | solution.py:242
  61.4 9.3 %collective-permute-start.22 = (f32[64,1024]{1,0:T(8,128)S(1)}, f32[64,1024]{1,0:T(8,128)S(1)}, u32[]{:S(2)}, u32[]{:S(2)}) collective-permute-start(f32[64,1024]{1,0:T(8,128)S(1)} %get-tuple-element.229), channel_id=1, source_target_pairs={{0,8},{4,12},{8,0},{12,4},{16,24},{20,28},{24,16},{28,20},{1,9},{5... | collective-permute-start | bytes 786440 | tf_op jit(solution)/shard_map/ppermute | solution.py:242
  62.0 16.6 %collective-permute-start.27 = (f32[64,2048]{1,0:T(8,128)S(1)}, f32[64,2048]{1,0:T(8,128)S(1)}, u32[]{:S(2)}, u32[]{:S(2)}) collective-permute-start(f32[64,2048]{1,0:T(8,128)S(1)} %constant_dynamic-update-slice_fusion.2), channel_id=1, source_target_pairs={{0,16},{4,20},{8,24},{12,28},{16,0},{20,4},{24,8},{28,12},{1,17},{... | collective-permute-start | bytes 1572872 | tf_op jit(solution)/shard_map/ppermute | solution.py:242
  63.5 14.9 %collective-permute-start.28 = (f32[32,2048]{1,0:T(8,128)S(1)}, f32[32,2048]{1,0:T(8,128)S(1)}, u32[]{:S(2)}, u32[]{:S(2)}) collective-permute-start(f32[32,2048]{1,0:T(8,128)S(1)} %get-tuple-element.281.refs_0_), channel_id=1, source_target_pairs={{0,8},{4,12},{8,0},{12,4},{16,24},{20,28},{24,16},{28,20},{1,9},{5... | collective-permute-start | bytes 786440 | tf_op jit(solution)/shard_map/ppermute | solution.py:242
  65.6 11.3 %collective-permute-start.20 = (f32[32,1024]{1,0:T(8,128)S(1)}, f32[32,1024]{1,0:T(8,128)S(1)}, u32[]{:S(2)}, u32[]{:S(2)}) collective-permute-start(f32[32,1024]{1,0:T(8,128)S(1)} %get-tuple-element.347), channel_id=1, source_target_pairs={{0,16},{4,20},{8,24},{12,28},{16,0},{20,4},{24,8},{28,12},{1,17},{... | collective-permute-start | bytes 393224 | tf_op jit(solution)/shard_map/ppermute | solution.py:242
  70.7 15.6 %collective-permute-start.24 = (f32[64,1024]{1,0:T(8,128)S(1)}, f32[64,1024]{1,0:T(8,128)S(1)}, u32[]{:S(2)}, u32[]{:S(2)}) collective-permute-start(f32[64,1024]{1,0:T(8,128)S(1)} %get-tuple-element.239), channel_id=1, source_target_pairs={{0,8},{4,12},{8,0},{12,4},{16,24},{20,28},{24,16},{28,20},{1,9},{5... | collective-permute-start | bytes 786440 | tf_op jit(solution)/shard_map/ppermute | solution.py:242
  78.5 9.5 %collective-permute-start.23 = (f32[32,1024]{1,0:T(8,128)S(1)}, f32[32,1024]{1,0:T(8,128)S(1)}, u32[]{:S(2)}, u32[]{:S(2)}) collective-permute-start(f32[32,1024]{1,0:T(8,128)S(1)} %get-tuple-element.345), channel_id=1, source_target_pairs={{0,2},{1,3},{2,0},{3,1},{4,6},{5,7},{6,4},{7,5},{8,10},{9,11},{10,... | collective-permute-start | bytes 393224 | tf_op jit(solution)/shard_map/ppermute | solution.py:248
  78.6 15.9 %collective-permute-start.32 = (f32[64,2048]{1,0:T(8,128)S(1)}, f32[64,2048]{1,0:T(8,128)S(1)}, u32[]{:S(2)}, u32[]{:S(2)}) collective-permute-start(f32[64,2048]{1,0:T(8,128)S(1)} %constant_dynamic-update-slice_fusion.4), channel_id=1, source_target_pairs={{0,16},{4,20},{8,24},{12,28},{16,0},{20,4},{24,8},{28,12},{1,17},{... | collective-permute-start | bytes 1572872 | tf_op jit(solution)/shard_map/ppermute | solution.py:242
  81.7 9.1 %collective-permute-start.33 = (f32[64,1024]{1,0:T(8,128)S(1)}, f32[64,1024]{1,0:T(8,128)S(1)}, u32[]{:S(2)}, u32[]{:S(2)}) collective-permute-start(f32[64,1024]{1,0:T(8,128)S(1)} %get-tuple-element.252), channel_id=1, source_target_pairs={{0,8},{4,12},{8,0},{12,4},{16,24},{20,28},{24,16},{28,20},{1,9},{5... | collective-permute-start | bytes 786440 | tf_op jit(solution)/shard_map/ppermute | solution.py:242
  83.4 18.2 %collective-permute-start.29 = (f32[32,1024]{1,0:T(8,128)S(1)}, f32[32,1024]{1,0:T(8,128)S(1)}, u32[]{:S(2)}, u32[]{:S(2)}) collective-permute-start(f32[32,1024]{1,0:T(8,128)S(1)} %get-tuple-element.342), channel_id=1, source_target_pairs={{0,2},{1,3},{2,0},{3,1},{4,6},{5,7},{6,4},{7,5},{8,10},{9,11},{10,... | collective-permute-start | bytes 393224 | tf_op jit(solution)/shard_map/ppermute | solution.py:248
  86.4 13.2 %collective-permute-start.31 = (f32[32,1024]{1,0:T(8,128)S(1)}, f32[32,1024]{1,0:T(8,128)S(1)}, u32[]{:S(2)}, u32[]{:S(2)}) collective-permute-start(f32[32,1024]{1,0:T(8,128)S(1)} %get-tuple-element.340), channel_id=1, source_target_pairs={{0,16},{4,20},{8,24},{12,28},{16,0},{20,4},{24,8},{28,12},{1,17},{... | collective-permute-start | bytes 393224 | tf_op jit(solution)/shard_map/ppermute | solution.py:242
  90.7 12.0 %collective-permute-start.36 = (f32[64,1024]{1,0:T(8,128)S(1)}, f32[64,1024]{1,0:T(8,128)S(1)}, u32[]{:S(2)}, u32[]{:S(2)}) collective-permute-start(f32[64,1024]{1,0:T(8,128)S(1)} %get-tuple-element.265), channel_id=1, source_target_pairs={{0,8},{4,12},{8,0},{12,4},{16,24},{20,28},{24,16},{28,20},{1,9},{5... | collective-permute-start | bytes 786440 | tf_op jit(solution)/shard_map/ppermute | solution.py:242
  94.4 11.9 %collective-permute-start.35 = (f32[64,1024]{1,0:T(8,128)S(1)}, f32[64,1024]{1,0:T(8,128)S(1)}, u32[]{:S(2)}, u32[]{:S(2)}) collective-permute-start(f32[64,1024]{1,0:T(8,128)S(1)} %broadcast_select_fusion.3), channel_id=1, source_target_pairs={{0,1},{1,0},{2,3},{3,2},{4,5},{5,4},{6,7},{7,6},{8,9},{9,8},{10,11... | collective-permute-start | bytes 786440 | tf_op jit(solution)/shard_map/ppermute | solution.py:248
  97.0 13.2 %collective-permute-start.42 = (f32[64,1024]{1,0:T(8,128)S(1)}, f32[64,1024]{1,0:T(8,128)S(1)}, u32[]{:S(2)}, u32[]{:S(2)}) collective-permute-start(f32[64,1024]{1,0:T(8,128)S(1)} %get-tuple-element.273), channel_id=1, source_target_pairs={{0,8},{4,12},{8,0},{12,4},{16,24},{20,28},{24,16},{28,20},{1,9},{5... | collective-permute-start | bytes 786440 | tf_op jit(solution)/shard_map/ppermute | solution.py:242
  99.6 15.8 %collective-permute-start.39 = (f32[32,1024]{1,0:T(8,128)S(1)}, f32[32,1024]{1,0:T(8,128)S(1)}, u32[]{:S(2)}, u32[]{:S(2)}) collective-permute-start(f32[32,1024]{1,0:T(8,128)S(1)} %get-tuple-element.334), channel_id=1, source_target_pairs={{0,2},{1,3},{2,0},{3,1},{4,6},{5,7},{6,4},{7,5},{8,10},{9,11},{10,... | collective-permute-start | bytes 393224 | tf_op jit(solution)/shard_map/ppermute | solution.py:248
  102.7 12.4 %collective-permute-start.41 = (f32[64,1024]{1,0:T(8,128)S(1)}, f32[64,1024]{1,0:T(8,128)S(1)}, u32[]{:S(2)}, u32[]{:S(2)}) collective-permute-start(f32[64,1024]{1,0:T(8,128)S(1)} %broadcast_select_fusion.2), channel_id=1, source_target_pairs={{0,1},{1,0},{2,3},{3,2},{4,5},{5,4},{6,7},{7,6},{8,9},{9,8},{10,11... | collective-permute-start | bytes 786440 | tf_op jit(solution)/shard_map/ppermute | solution.py:248
  106.3 12.6 %collective-permute-start.38 = (f32[64,1024]{1,0:T(8,128)S(1)}, f32[64,1024]{1,0:T(8,128)S(1)}, u32[]{:S(2)}, u32[]{:S(2)}) collective-permute-start(f32[64,1024]{1,0:T(8,128)S(1)} %get-tuple-element.286), channel_id=1, source_target_pairs={{0,8},{4,12},{8,0},{12,4},{16,24},{20,28},{24,16},{28,20},{1,9},{5... | collective-permute-start | bytes 786440 | tf_op jit(solution)/shard_map/ppermute | solution.py:242
  110.2 9.0 %collective-permute-start.37 = (f32[32,1024]{1,0:T(8,128)S(1)}, f32[32,1024]{1,0:T(8,128)S(1)}, u32[]{:S(2)}, u32[]{:S(2)}) collective-permute-start(f32[32,1024]{1,0:T(8,128)S(1)} %get-tuple-element.335), channel_id=1, source_target_pairs={{0,2},{1,3},{2,0},{3,1},{4,6},{5,7},{6,4},{7,5},{8,10},{9,11},{10,... | collective-permute-start | bytes 393224 | tf_op jit(solution)/shard_map/ppermute | solution.py:248
  115.1 9.1 %collective-permute-start.47 = (f32[64,1024]{1,0:T(8,128)S(1)}, f32[64,1024]{1,0:T(8,128)S(1)}, u32[]{:S(2)}, u32[]{:S(2)}) collective-permute-start(f32[64,1024]{1,0:T(8,128)S(1)} %broadcast_select_fusion.1), channel_id=1, source_target_pairs={{0,1},{1,0},{2,3},{3,2},{4,5},{5,4},{6,7},{7,6},{8,9},{9,8},{10,11... | collective-permute-start | bytes 786440 | tf_op jit(solution)/shard_map/ppermute | solution.py:248
  115.3 14.6 %collective-permute-start.46 = (f32[32,1024]{1,0:T(8,128)S(1)}, f32[32,1024]{1,0:T(8,128)S(1)}, u32[]{:S(2)}, u32[]{:S(2)}) collective-permute-start(f32[32,1024]{1,0:T(8,128)S(1)} %get-tuple-element.326), channel_id=1, source_target_pairs={{0,2},{1,3},{2,0},{3,1},{4,6},{5,7},{6,4},{7,5},{8,10},{9,11},{10,... | collective-permute-start | bytes 393224 | tf_op jit(solution)/shard_map/ppermute | solution.py:248
  119.0 10.8 %collective-permute-start.45 = (f32[64,1024]{1,0:T(8,128)S(1)}, f32[64,1024]{1,0:T(8,128)S(1)}, u32[]{:S(2)}, u32[]{:S(2)}) collective-permute-start(f32[64,1024]{1,0:T(8,128)S(1)} %broadcast_select_fusion), channel_id=1, source_target_pairs={{0,1},{1,0},{2,3},{3,2},{4,5},{5,4},{6,7},{7,6},{8,9},{9,8},{10,11... | collective-permute-start | bytes 786440 | tf_op jit(solution)/shard_map/ppermute | solution.py:248
  121.2 10.8 %collective-permute-start.44 = (f32[32,1024]{1,0:T(8,128)S(1)}, f32[32,1024]{1,0:T(8,128)S(1)}, u32[]{:S(2)}, u32[]{:S(2)}) collective-permute-start(f32[32,1024]{1,0:T(8,128)S(1)} %get-tuple-element.327), channel_id=1, source_target_pairs={{0,2},{1,3},{2,0},{3,1},{4,6},{5,7},{6,4},{7,5},{8,10},{9,11},{10,... | collective-permute-start | bytes 393224 | tf_op jit(solution)/shard_map/ppermute | solution.py:248
  (27 other events, 241.3 us)

commit v11 on v10

--- a/solution.py
+++ b/solution.py
@@ -14,10 +14,10 @@
 UNITS = tuple((chunk, (half,)) for chunk in range(CHUNKS) for half in range(CORES))
 
 ORDER = (
-    "s0", "s1", "p0", "g00", "p1", "g01", "g10", "s2", "f0", "e0", "g11", "p2", "g20", "f1",
-    "e1", "r0", "g21", "e3", "g30", "r1", "x0", "e2", "r3", "x1", "z0", "g31", "e5", "z1",
-    "x3", "r2", "l0", "e4", "r5", "e7", "z3", "x2", "l1", "r4", "e6", "x5", "z2", "r7", "x4",
-    "z5", "l3", "r6", "l2", "z4", "x7", "z7", "l5", "x6", "l4", "z6", "l7", "l6",
+    "s0", "s1", "p0", "g00", "p1", "g01", "g10", "s2", "f0", "e0", "g11", "f1", "e1", "r0",
+    "p2", "g20", "e2", "x0", "r1", "g21", "g30", "z0", "r2", "x1", "e3", "g31", "e4", "z1",
+    "x2", "r3", "l0", "e5", "r4", "l1", "e7", "z2", "x3", "r5", "e6", "z3", "r7", "x4", "l2",
+    "x5", "z4", "r6", "l3", "z5", "x7", "l4", "z7", "x6", "l5", "z6", "l7", "l6",
 )
 
 SMEM = pl.BlockSpec(memory_space=pltpu.SMEM)
@@ -104,10 +104,10 @@
             copy(i + slots).start()
 
 
-def split(whole):
+def split(whole, limit):
     rows, columns = whole.shape
-    step = min(256, rows)
-    slots = min(4, rows // step)
+    step = min(128, rows)
+    slots = min(8, rows // step)
     half = jax.ShapeDtypeStruct((rows, columns), jnp.bfloat16)
     return pl.pallas_call(
         functools.partial(split_kernel, step),
@@ -119,7 +119,7 @@
             pltpu.SemaphoreType.DMA((slots,)),
         ],
         cost_estimate=SMALL,
-        compiler_params=pltpu.CompilerParams(vmem_limit_bytes=6 * 2**20),
+        compiler_params=pltpu.CompilerParams(vmem_limit_bytes=limit * 2**20),
         name="split",
     )(whole)
 
@@ -298,7 +298,8 @@
             layouts[chunk].append([(k | bit, 0, rows) for k in range(bit)])
 
     def split_step(half):
-        *factors[half], done = split(*ordered(integrals if half == 0 else swapped))
+        source, limit = ((integrals, 42), (swapped, 6))[half]
+        *factors[half], done = split(*ordered(source), limit)
         mark(done)
 
     def multiply(unit):

time: 144 us -> 143 us (level)
  local copies, waits for them, and re-layouts: 5.03 us -> 1.65 us
  waiting for transfers between devices: 41.5 us -> 44.1 us
  starting transfers between devices: 65.3 us -> 63.2 us
    unnamed x17 -> x15, local copies, waits for them, and re-layouts: 4.69 us -> 1.31 us
    pallas_call x2, Pallas kernels: 6.48 us -> 8.53 us  [split(): pl.pallas_call(functools.partial(split_kernel, step), in_specs=[HBM], out...]
    ppermute x25, starting transfers between devices: 31.9 us -> 30.2 us  [along(): lax.ppermute(value, 'narrow', [(n, n ^ mask) for n in range(narrow_count)])]
    ppermute x25, waiting for transfers between devices: 32.2 us -> 33.8 us  [along(): lax.ppermute(value, 'narrow', [(n, n ^ mask) for n in range(narrow_count)])]
  transfers between devices with their start and end apart: 52 -> 52, of which waited for: 20 -> 24; matrix products, arithmetic and copies ran while one was open for 1% -> 1% of each run, Pallas kernels for 20% -> 21%
where the time goes in v11:
time: 143 us; the launch traced here: 142 us
  starting transfers between devices  63.2 us (44%)
  waiting for transfers between devices  44.1 us (31%)
  Pallas kernels  32 us (22%)
  local copies, waits for them, and re-layouts  1.65 us (1%)
    ppermute x25, waiting for transfers between devices, along(): lax.ppermute(value, 'narrow', [(n, n ^ mask) for n in range(narrow_count)])  33.8 us
    ppermute x27, starting transfers between devices, across(): lax.ppermute(value, 'wide', [(w, w ^ mask) for w in range(wide_count)])  33 us
    ppermute x25, starting transfers between devices, along(): lax.ppermute(value, 'narrow', [(n, n ^ mask) for n in range(narrow_count)])  30.2 us
    pallas_call x8, Pallas kernels, product(): pl.pallas_call(functools.partial(product_kernel, count, rows, layout, tar...  19.4 us
    ppermute x27, waiting for transfers between devices, across(): lax.ppermute(value, 'wide', [(w, w ^ mask) for w in range(wide_count)])  10.3 us
    pallas_call x2, Pallas kernels, split(): pl.pallas_call(functools.partial(split_kernel, step), in_specs=[HBM], out...  8.53 us
  transfers between devices with their start and end apart: 52, of which 24 were waited for; matrix products, arithmetic and copies ran while one was open for 1% of the time, Pallas kernels for 21%

profile of v11, /device:TPU:0, one launch (start us, length us, event | category | flops | bytes accessed | tf_op | source)
XLA Modules:
  0.0 142.5 jit_solution(13893532876237151632)
XLA Ops:
  2.4 2.6 %collective-permute-start = (f32[8,2048]{1,0:T(8,128)S(1)}, f32[8,2048]{1,0:T(8,128)S(1)}, u32[]{:S(2)}, u32[]{:S(2)}) collective-permute-start(f32[8,2048]{1,0:T(8,128)S(1)} %get-tuple-element.165), channel_id=1, source_target_pairs={{0,1},{1,0},{2,3},{3,2},{4,5},{5,4},{6,7},{7,6},{8,9},{9,8},{10,11... | collective-permute-start | bytes 196616 | tf_op jit(solution)/shard_map/ppermute | solution.py:248
  5.0 2.6 %collective-permute-start.1 = (f32[8,2048]{1,0:T(8,128)S(1)}, f32[8,2048]{1,0:T(8,128)S(1)}, u32[]{:S(2)}, u32[]{:S(2)}) collective-permute-start(f32[8,2048]{1,0:T(8,128)S(1)} %get-tuple-element.166), channel_id=1, source_target_pairs={{0,2},{1,3},{2,0},{3,1},{4,6},{5,7},{6,4},{7,5},{8,10},{9,11},{10,... | collective-permute-start | bytes 196616 | tf_op jit(solution)/shard_map/ppermute | solution.py:248
  7.8 4.2 %collective-permute-done.1.refs_2_ = f32[8,2048]{1,0:T(8,128)S(1)} collective-permute-done((f32[8,2048]{1,0:T(8,128)S(1)}, f32[8,2048]{1,0:T(8,128)S(1)}, u32[]{:S(2)}, u32[]{:S(2)}) %collective-permute-start.1) | collective-permute-done | bytes 65568 | tf_op jit(solution)/shard_map/ppermute | solution.py:248
  12.0 1.8 %collective-permute-done.2.refs_3_ = f32[8,2048]{1,0:T(8,128)S(1)} collective-permute-done((f32[8,2048]{1,0:T(8,128)S(1)}, f32[8,2048]{1,0:T(8,128)S(1)}, u32[]{:S(2)}, u32[]{:S(2)}) %collective-permute-start.2) | collective-permute-done | bytes 65568 | tf_op jit(solution)/shard_map/ppermute | solution.py:248
  18.6 1.7 %collective-permute-start.6 = (f32[8,2048]{1,0:T(8,128)S(1)}, f32[8,2048]{1,0:T(8,128)S(1)}, u32[]{:S(2)}, u32[]{:S(2)}) collective-permute-start(f32[8,2048]{1,0:T(8,128)S(1)} %get-tuple-element.172), channel_id=1, source_target_pairs={{0,2},{1,3},{2,0},{3,1},{4,6},{5,7},{6,4},{7,5},{8,10},{9,11},{10,... | collective-permute-start | bytes 196616 | tf_op jit(solution)/shard_map/ppermute | solution.py:248
  21.7 2.9 %collective-permute-start.7 = (f32[8,2048]{1,0:T(8,128)S(1)}, f32[8,2048]{1,0:T(8,128)S(1)}, u32[]{:S(2)}, u32[]{:S(2)}) collective-permute-start(f32[8,2048]{1,0:T(8,128)S(1)} %get-tuple-element.173), channel_id=1, source_target_pairs={{0,3},{1,2},{2,1},{3,0},{4,7},{5,6},{6,5},{7,4},{8,11},{9,10},{10,... | collective-permute-start | bytes 196616 | tf_op jit(solution)/shard_map/ppermute | solution.py:248
  25.7 2.1 %collective-permute-done.7.refs_3_ = f32[8,2048]{1,0:T(8,128)S(1)} collective-permute-done((f32[8,2048]{1,0:T(8,128)S(1)}, f32[8,2048]{1,0:T(8,128)S(1)}, u32[]{:S(2)}, u32[]{:S(2)}) %collective-permute-start.7) | collective-permute-done | bytes 65568 | tf_op jit(solution)/shard_map/ppermute | solution.py:248
  31.1 4.3 %split.2 = (bf16[2048,1024]{1,0:T(8,128)(2,1)S(1)}, bf16[2048,1024]{1,0:T(8,128)(2,1)S(1)}, f32[8,128]{1,0:T(8,128)}) custom-call(f32[2048,1024]{1,0:T(8,128)} %whole_ref.2), custom_call_target="tpu_custom_call" | custom-call | flops 1 | bytes 1 | tf_op jit(solution)/shard_map/split/pallas_call | solution.py:112
  35.4 3.5 %collective-permute-start.16 = (f32[16,2048]{1,0:T(8,128)S(1)}, f32[16,2048]{1,0:T(8,128)S(1)}, u32[]{:S(2)}, u32[]{:S(2)}) collective-permute-start(f32[16,2048]{1,0:T(8,128)S(1)} %get-tuple-element.196), channel_id=1, source_target_pairs={{0,2},{1,3},{2,0},{3,1},{4,6},{5,7},{6,4},{7,5},{8,10},{9,11},{10,... | collective-permute-start | bytes 393224 | tf_op jit(solution)/shard_map/ppermute | solution.py:248
  39.8 2.4 %product.8 = (f32[64,1024]{1,0:T(8,128)S(1)}, f32[64,1024]{1,0:T(8,128)S(1)}) custom-call(s32[3]{0:T(128)S(1)} %pad_add_fusion.place_ref, s32[8,64]{1,0:T(8,128)S(1)} %copy-done.3, s32[8]{0:T(128)S(1)} %copy-done.4, f32[32,2048]{1,0:T(8,128)S(1)} %pack.3.refs_0_, f32[32,2048]{1,0:T(8,128)S(1)} %collective-permute-done.3.refs_1_, ...), custom_call_target="tpu_custom_call" | custom-call | flops 3221225472 | bytes 1 | tf_op jit(solution)/shard_map/product/pallas_call | solution.py:173
  44.5 4.3 %split.3 = (bf16[2048,1024]{1,0:T(8,128)(2,1)S(1)}, bf16[2048,1024]{1,0:T(8,128)(2,1)S(1)}, f32[8,128]{1,0:T(8,128)}) custom-call(f32[2048,1024]{1,0:T(8,128)} %collective-permute-done.11.whole_ref), custom_call_target="tpu_custom_call" | custom-call | flops 1 | bytes 1 | tf_op jit(solution)/shard_map/split/pallas_call | solution.py:112
  48.7 2.4 %product.9 = (f32[64,1024]{1,0:T(8,128)S(1)}, f32[64,1024]{1,0:T(8,128)S(1)}) custom-call(s32[3]{0:T(128)S(1)} %pad_add_fusion.place_ref, s32[8,64]{1,0:T(8,128)S(1)} %copy-done.3, s32[8]{0:T(128)S(1)} %copy-done.4, f32[32,2048]{1,0:T(8,128)S(1)} %pack.3.refs_0_, f32[32,2048]{1,0:T(8,128)S(1)} %collective-permute-done.3.refs_1_, ...), custom_call_target="tpu_custom_call" | custom-call | flops 3221225472 | bytes 1 | tf_op jit(solution)/shard_map/product/pallas_call | solution.py:173
  54.1 2.4 %product.10 = (f32[64,1024]{1,0:T(8,128)S(1)}, f32[64,1024]{1,0:T(8,128)S(1)}) custom-call(s32[3]{0:T(128)S(1)} %pad_add_fusion.place_ref, s32[8,64]{1,0:T(8,128)S(1)} %copy-done.3, s32[8]{0:T(128)S(1)} %copy-done.4, f32[32,2048]{1,0:T(8,128)S(1)} %pack.4.refs_0_, f32[32,2048]{1,0:T(8,128)S(1)} %collective-permute-done.12.refs_1_, ...), custom_call_target="tpu_custom_call" | custom-call | flops 3221225472 | bytes 1 | tf_op jit(solution)/shard_map/product/pallas_call | solution.py:173
  58.0 5.3 %collective-permute-done.13 = f32[64,1024]{1,0:T(8,128)S(1)} collective-permute-done((f32[64,1024]{1,0:T(8,128)S(1)}, f32[64,1024]{1,0:T(8,128)S(1)}, u32[]{:S(2)}, u32[]{:S(2)}) %collective-permute-start.13) | collective-permute-done | bytes 262176 | tf_op jit(solution)/shard_map/ppermute | solution.py:248
  68.6 2.7 %collective-permute-start.25 = (f32[64,1024]{1,0:T(8,128)S(1)}, f32[64,1024]{1,0:T(8,128)S(1)}, u32[]{:S(2)}, u32[]{:S(2)}) collective-permute-start(f32[64,1024]{1,0:T(8,128)S(1)} %broadcast_select_fusion.5), channel_id=1, source_target_pairs={{0,1},{1,0},{2,3},{3,2},{4,5},{5,4},{6,7},{7,6},{8,9},{9,8},{10,11... | collective-permute-start | bytes 786440 | tf_op jit(solution)/shard_map/ppermute | solution.py:248
  73.0 2.4 %product.11 = (f32[64,1024]{1,0:T(8,128)S(1)}, f32[64,1024]{1,0:T(8,128)S(1)}) custom-call(s32[3]{0:T(128)S(1)} %pad_add_fusion.place_ref, s32[8,64]{1,0:T(8,128)S(1)} %copy-done.3, s32[8]{0:T(128)S(1)} %copy-done.4, f32[32,2048]{1,0:T(8,128)S(1)} %pack.4.refs_0_, f32[32,2048]{1,0:T(8,128)S(1)} %collective-permute-done.12.refs_1_, ...), custom_call_target="tpu_custom_call" | custom-call | flops 3221225472 | bytes 1 | tf_op jit(solution)/shard_map/product/pallas_call | solution.py:173
  76.4 2.8 %collective-permute-done.25 = f32[64,1024]{1,0:T(8,128)S(1)} collective-permute-done((f32[64,1024]{1,0:T(8,128)S(1)}, f32[64,1024]{1,0:T(8,128)S(1)}, u32[]{:S(2)}, u32[]{:S(2)}) %collective-permute-start.25) | collective-permute-done | bytes 262176 | tf_op jit(solution)/shard_map/ppermute | solution.py:248
  80.9 2.4 %product.12 = (f32[64,1024]{1,0:T(8,128)S(1)}, f32[64,1024]{1,0:T(8,128)S(1)}) custom-call(s32[3]{0:T(128)S(1)} %pad_add_fusion.place_ref, s32[8,64]{1,0:T(8,128)S(1)} %copy-done.3, s32[8]{0:T(128)S(1)} %copy-done.4, f32[32,2048]{1,0:T(8,128)S(1)} %get-tuple-element.260.refs_0_, f32[32,2048]{1,0:T(8,128)S(1)} %collective-permute-done.19.refs_1_, ...), custom_call_target="tpu_custom_call" | custom-call | flops 3221225472 | bytes 1 | tf_op jit(solution)/shard_map/product/pallas_call | solution.py:173
  86.2 2.4 %collective-permute-start.36 = (f32[64,1024]{1,0:T(8,128)S(1)}, f32[64,1024]{1,0:T(8,128)S(1)}, u32[]{:S(2)}, u32[]{:S(2)}) collective-permute-start(f32[64,1024]{1,0:T(8,128)S(1)} %broadcast_select_fusion.4), channel_id=1, source_target_pairs={{0,1},{1,0},{2,3},{3,2},{4,5},{5,4},{6,7},{7,6},{8,9},{9,8},{10,11... | collective-permute-start | bytes 786440 | tf_op jit(solution)/shard_map/ppermute | solution.py:248
  88.6 2.5 %product.13 = (f32[64,1024]{1,0:T(8,128)S(1)}, f32[64,1024]{1,0:T(8,128)S(1)}) custom-call(s32[3]{0:T(128)S(1)} %pad_add_fusion.place_ref, s32[8,64]{1,0:T(8,128)S(1)} %copy-done.3, s32[8]{0:T(128)S(1)} %copy-done.4, f32[32,2048]{1,0:T(8,128)S(1)} %get-tuple-element.260.refs_0_, f32[32,2048]{1,0:T(8,128)S(1)} %collective-permute-done.19.refs_1_, ...), custom_call_target="tpu_custom_call" | custom-call | flops 3221225472 | bytes 1 | tf_op jit(solution)/shard_map/product/pallas_call | solution.py:173
  93.7 2.4 %product.14 = (f32[64,1024]{1,0:T(8,128)S(1)}, f32[64,1024]{1,0:T(8,128)S(1)}) custom-call(s32[3]{0:T(128)S(1)} %pad_add_fusion.place_ref, s32[8,64]{1,0:T(8,128)S(1)} %copy-done.3, s32[8]{0:T(128)S(1)} %copy-done.4, f32[32,2048]{1,0:T(8,128)S(1)} %get-tuple-element.281.refs_0_, f32[32,2048]{1,0:T(8,128)S(1)} %collective-permute-done.28.refs_1_, ...), custom_call_target="tpu_custom_call" | custom-call | flops 3221225472 | bytes 1 | tf_op jit(solution)/shard_map/product/pallas_call | solution.py:173
  97.0 2.8 %collective-permute-start.33 = (f32[32,1024]{1,0:T(8,128)S(1)}, f32[32,1024]{1,0:T(8,128)S(1)}, u32[]{:S(2)}, u32[]{:S(2)}) collective-permute-start(f32[32,1024]{1,0:T(8,128)S(1)} %get-tuple-element.337), channel_id=1, source_target_pairs={{0,2},{1,3},{2,0},{3,1},{4,6},{5,7},{6,4},{7,5},{8,10},{9,11},{10,... | collective-permute-start | bytes 393224 | tf_op jit(solution)/shard_map/ppermute | solution.py:248
  101.0 2.4 %product.15 = (f32[64,1024]{1,0:T(8,128)S(1)}, f32[64,1024]{1,0:T(8,128)S(1)}) custom-call(s32[3]{0:T(128)S(1)} %pad_add_fusion.place_ref, s32[8,64]{1,0:T(8,128)S(1)} %copy-done.3, s32[8]{0:T(128)S(1)} %copy-done.4, f32[32,2048]{1,0:T(8,128)S(1)} %get-tuple-element.281.refs_0_, f32[32,2048]{1,0:T(8,128)S(1)} %collective-permute-done.28.refs_1_, ...), custom_call_target="tpu_custom_call" | custom-call | flops 3221225472 | bytes 1 | tf_op jit(solution)/shard_map/product/pallas_call | solution.py:173
  110.1 2.9 %collective-permute-start.45 = (f32[32,1024]{1,0:T(8,128)S(1)}, f32[32,1024]{1,0:T(8,128)S(1)}, u32[]{:S(2)}, u32[]{:S(2)}) collective-permute-start(f32[32,1024]{1,0:T(8,128)S(1)} %get-tuple-element.328), channel_id=1, source_target_pairs={{0,16},{4,20},{8,24},{12,28},{16,0},{20,4},{24,8},{28,12},{1,17},{... | collective-permute-start | bytes 393224 | tf_op jit(solution)/shard_map/ppermute | solution.py:242
  116.0 2.6 %collective-permute-done.44 = f32[64,1024]{1,0:T(8,128)S(1)} collective-permute-done((f32[64,1024]{1,0:T(8,128)S(1)}, f32[64,1024]{1,0:T(8,128)S(1)}, u32[]{:S(2)}, u32[]{:S(2)}) %collective-permute-start.44) | collective-permute-done | bytes 262176 | tf_op jit(solution)/shard_map/ppermute | solution.py:248
  121.9 1.8 %collective-permute-done.48 = f32[32,1024]{1,0:T(8,128)S(1)} collective-permute-done((f32[32,1024]{1,0:T(8,128)S(1)}, f32[32,1024]{1,0:T(8,128)S(1)}, u32[]{:S(2)}, u32[]{:S(2)}) %collective-permute-start.48) | collective-permute-done | bytes 131104 | tf_op jit(solution)/shard_map/ppermute | solution.py:242
  123.8 4.4 %collective-permute-done.47 = f32[64,1024]{1,0:T(8,128)S(1)} collective-permute-done((f32[64,1024]{1,0:T(8,128)S(1)}, f32[64,1024]{1,0:T(8,128)S(1)}, u32[]{:S(2)}, u32[]{:S(2)}) %collective-permute-start.47) | collective-permute-done | bytes 262176 | tf_op jit(solution)/shard_map/ppermute | solution.py:248
  128.3 2.1 %collective-permute-start.49 = (f32[32,1024]{1,0:T(8,128)S(1)}, f32[32,1024]{1,0:T(8,128)S(1)}, u32[]{:S(2)}, u32[]{:S(2)}) collective-permute-start(f32[32,1024]{1,0:T(8,128)S(1)} %get-tuple-element.322), channel_id=1, source_target_pairs={{0,16},{4,20},{8,24},{12,28},{16,0},{20,4},{24,8},{28,12},{1,17},{... | collective-permute-start | bytes 393224 | tf_op jit(solution)/shard_map/ppermute | solution.py:242
  130.4 2.9 %collective-permute-done.49 = f32[32,1024]{1,0:T(8,128)S(1)} collective-permute-done((f32[32,1024]{1,0:T(8,128)S(1)}, f32[32,1024]{1,0:T(8,128)S(1)}, u32[]{:S(2)}, u32[]{:S(2)}) %collective-permute-start.49) | collective-permute-done | bytes 131104 | tf_op jit(solution)/shard_map/ppermute | solution.py:242
  134.6 2.0 %collective-permute-done.51.refs_15_ = f32[32,1024]{1,0:T(8,128)S(1)} collective-permute-done((f32[32,1024]{1,0:T(8,128)S(1)}, f32[32,1024]{1,0:T(8,128)S(1)}, u32[]{:S(2)}, u32[]{:S(2)}) %collective-permute-start.51) | collective-permute-done | bytes 131104 | tf_op jit(solution)/shard_map/ppermute | solution.py:248
  136.6 4.1 %collective-permute-done.50.refs_13_ = f32[32,1024]{1,0:T(8,128)S(1)} collective-permute-done((f32[32,1024]{1,0:T(8,128)S(1)}, f32[32,1024]{1,0:T(8,128)S(1)}, u32[]{:S(2)}, u32[]{:S(2)}) %collective-permute-start.50) | collective-permute-done | bytes 131104 | tf_op jit(solution)/shard_map/ppermute | solution.py:248
  140.7 1.8 %finish.1 = f32[128,2048]{1,0:T(8,128)} custom-call(s32[3]{0:T(128)S(1)} %pad_add_fusion.place_ref, f32[128,2048]{1,0:T(8,128)S(1)} %copy-done, f32[128,1]{1,0:T(8,128)S(1)} %copy.8.occ_ref, f32[1,2048]{1,0:T(1,128)S(1)} %bitcast.5, f32[32,1024]{1,0:T(8,128)S(1)} %get-tuple-element.258.refs_0_, f32[32,1024]{1,0:T(8,128)S(1)} %collective-permute-done.21.refs_1_, ...), custom_call_target="tpu_custom_call" | custom-call | flops 1 | bytes 1 | tf_op jit(solution)/shard_map/finish/pallas_call | solution.py:209
  (141 shorter events, 52.2 us)
Async XLA Ops:
  0.0 42.9 %collective-permute-start.11 = (f32[2048,1024]{1,0:T(8,128)}, f32[2048,1024]{1,0:T(8,128)}, u32[]{:S(2)}, u32[]{:S(2)}) collective-permute-start(f32[2048,1024]{1,0:T(8,128)} %whole_ref.2), channel_id=1, source_target_pairs={{0,4},{4,0},{8,12},{12,8},{16,20},{20,16},{24,28},{28,24},{1,5},{5... | collective-permute-start | bytes 25165832 | tf_op jit(solution)/shard_map/ppermute | solution.py:242
  14.3 14.1 %collective-permute-start.3 = (f32[32,2048]{1,0:T(8,128)S(1)}, f32[32,2048]{1,0:T(8,128)S(1)}, u32[]{:S(2)}, u32[]{:S(2)}) collective-permute-start(f32[32,2048]{1,0:T(8,128)S(1)} %pack.3.refs_0_), channel_id=1, source_target_pairs={{0,8},{4,12},{8,0},{12,4},{16,24},{20,28},{24,16},{28,20},{1,9},{5... | collective-permute-start | bytes 786440 | tf_op jit(solution)/shard_map/ppermute | solution.py:242
  15.9 12.5 %collective-permute-start.4 = (f32[32,2048]{1,0:T(8,128)S(1)}, f32[32,2048]{1,0:T(8,128)S(1)}, u32[]{:S(2)}, u32[]{:S(2)}) collective-permute-start(f32[32,2048]{1,0:T(8,128)S(1)} %pack.3.refs_0_), channel_id=1, source_target_pairs={{0,16},{4,20},{8,24},{12,28},{16,0},{20,4},{24,8},{28,12},{1,17},{... | collective-permute-start | bytes 786440 | tf_op jit(solution)/shard_map/ppermute | solution.py:242
  29.0 9.9 %collective-permute-start.9 = (f32[16,2048]{1,0:T(8,128)S(1)}, f32[16,2048]{1,0:T(8,128)S(1)}, u32[]{:S(2)}, u32[]{:S(2)}) collective-permute-start(f32[16,2048]{1,0:T(8,128)S(1)} %slice.55), channel_id=1, source_target_pairs={{0,8},{4,12},{8,0},{12,4},{16,24},{20,28},{24,16},{28,20},{1,9},{5... | collective-permute-start | bytes 393224 | tf_op jit(solution)/shard_map/ppermute | solution.py:242
  29.6 12.6 %collective-permute-start.12 = (f32[32,2048]{1,0:T(8,128)S(1)}, f32[32,2048]{1,0:T(8,128)S(1)}, u32[]{:S(2)}, u32[]{:S(2)}) collective-permute-start(f32[32,2048]{1,0:T(8,128)S(1)} %pack.4.refs_0_), channel_id=1, source_target_pairs={{0,8},{4,12},{8,0},{12,4},{16,24},{20,28},{24,16},{28,20},{1,9},{5... | collective-permute-start | bytes 786440 | tf_op jit(solution)/shard_map/ppermute | solution.py:242
  31.1 21.7 %collective-permute-start.15 = (f32[16,2048]{1,0:T(8,128)S(1)}, f32[16,2048]{1,0:T(8,128)S(1)}, u32[]{:S(2)}, u32[]{:S(2)}) collective-permute-start(f32[16,2048]{1,0:T(8,128)S(1)} %get-tuple-element.195), channel_id=1, source_target_pairs={{0,1},{1,0},{2,3},{3,2},{4,5},{5,4},{6,7},{7,6},{8,9},{9,8},{10,11... | collective-permute-start | bytes 393224 | tf_op jit(solution)/shard_map/ppermute | solution.py:248
  35.4 17.5 %collective-permute-start.16 = (f32[16,2048]{1,0:T(8,128)S(1)}, f32[16,2048]{1,0:T(8,128)S(1)}, u32[]{:S(2)}, u32[]{:S(2)}) collective-permute-start(f32[16,2048]{1,0:T(8,128)S(1)} %get-tuple-element.196), channel_id=1, source_target_pairs={{0,2},{1,3},{2,0},{3,1},{4,6},{5,7},{6,4},{7,5},{8,10},{9,11},{10,... | collective-permute-start | bytes 393224 | tf_op jit(solution)/shard_map/ppermute | solution.py:248
  38.8 14.0 %collective-permute-start.17 = (f32[16,2048]{1,0:T(8,128)S(1)}, f32[16,2048]{1,0:T(8,128)S(1)}, u32[]{:S(2)}, u32[]{:S(2)}) collective-permute-start(f32[16,2048]{1,0:T(8,128)S(1)} %get-tuple-element.197), channel_id=1, source_target_pairs={{0,3},{1,2},{2,1},{3,0},{4,7},{5,6},{6,5},{7,4},{8,11},{9,10},{10,... | collective-permute-start | bytes 393224 | tf_op jit(solution)/shard_map/ppermute | solution.py:248
  42.2 8.9 %collective-permute-start.10 = (f32[64,1024]{1,0:T(8,128)S(1)}, f32[64,1024]{1,0:T(8,128)S(1)}, u32[]{:S(2)}, u32[]{:S(2)}) collective-permute-start(f32[64,1024]{1,0:T(8,128)S(1)} %get-tuple-element.203), channel_id=1, source_target_pairs={{0,8},{4,12},{8,0},{12,4},{16,24},{20,28},{24,16},{28,20},{1,9},{5... | collective-permute-start | bytes 786440 | tf_op jit(solution)/shard_map/ppermute | solution.py:242
  42.9 11.2 %collective-permute-start.14 = (f32[64,2048]{1,0:T(8,128)S(1)}, f32[64,2048]{1,0:T(8,128)S(1)}, u32[]{:S(2)}, u32[]{:S(2)}) collective-permute-start(f32[64,2048]{1,0:T(8,128)S(1)} %constant_dynamic-update-slice_fusion), channel_id=1, source_target_pairs={{0,16},{4,20},{8,24},{12,28},{16,0},{20,4},{24,8},{28,12},{1,17},{... | collective-permute-start | bytes 1572872 | tf_op jit(solution)/shard_map/ppermute | solution.py:242
  51.2 12.8 %collective-permute-start.20 = (f32[64,1024]{1,0:T(8,128)S(1)}, f32[64,1024]{1,0:T(8,128)S(1)}, u32[]{:S(2)}, u32[]{:S(2)}) collective-permute-start(f32[64,1024]{1,0:T(8,128)S(1)} %get-tuple-element.211), channel_id=1, source_target_pairs={{0,8},{4,12},{8,0},{12,4},{16,24},{20,28},{24,16},{28,20},{1,9},{5... | collective-permute-start | bytes 786440 | tf_op jit(solution)/shard_map/ppermute | solution.py:242
  52.8 10.6 %collective-permute-start.13 = (f32[64,1024]{1,0:T(8,128)S(1)}, f32[64,1024]{1,0:T(8,128)S(1)}, u32[]{:S(2)}, u32[]{:S(2)}) collective-permute-start(f32[64,1024]{1,0:T(8,128)S(1)} %broadcast_select_fusion.7), channel_id=1, source_target_pairs={{0,1},{1,0},{2,3},{3,2},{4,5},{5,4},{6,7},{7,6},{8,9},{9,8},{10,11... | collective-permute-start | bytes 786440 | tf_op jit(solution)/shard_map/ppermute | solution.py:248
  53.5 12.1 %collective-permute-start.19 = (f32[32,2048]{1,0:T(8,128)S(1)}, f32[32,2048]{1,0:T(8,128)S(1)}, u32[]{:S(2)}, u32[]{:S(2)}) collective-permute-start(f32[32,2048]{1,0:T(8,128)S(1)} %get-tuple-element.260.refs_0_), channel_id=1, source_target_pairs={{0,8},{4,12},{8,0},{12,4},{16,24},{20,28},{24,16},{28,20},{1,9},{5... | collective-permute-start | bytes 786440 | tf_op jit(solution)/shard_map/ppermute | solution.py:242
  56.5 12.1 %collective-permute-start.23 = (f32[64,1024]{1,0:T(8,128)S(1)}, f32[64,1024]{1,0:T(8,128)S(1)}, u32[]{:S(2)}, u32[]{:S(2)}) collective-permute-start(f32[64,1024]{1,0:T(8,128)S(1)} %get-tuple-element.227), channel_id=1, source_target_pairs={{0,8},{4,12},{8,0},{12,4},{16,24},{20,28},{24,16},{28,20},{1,9},{5... | collective-permute-start | bytes 786440 | tf_op jit(solution)/shard_map/ppermute | solution.py:242
  65.6 15.3 %collective-permute-start.27 = (f32[64,2048]{1,0:T(8,128)S(1)}, f32[64,2048]{1,0:T(8,128)S(1)}, u32[]{:S(2)}, u32[]{:S(2)}) collective-permute-start(f32[64,2048]{1,0:T(8,128)S(1)} %constant_dynamic-update-slice_fusion.2), channel_id=1, source_target_pairs={{0,16},{4,20},{8,24},{12,28},{16,0},{20,4},{24,8},{28,12},{1,17},{... | collective-permute-start | bytes 1572872 | tf_op jit(solution)/shard_map/ppermute | solution.py:242
  66.7 9.2 %collective-permute-start.28 = (f32[32,2048]{1,0:T(8,128)S(1)}, f32[32,2048]{1,0:T(8,128)S(1)}, u32[]{:S(2)}, u32[]{:S(2)}) collective-permute-start(f32[32,2048]{1,0:T(8,128)S(1)} %get-tuple-element.281.refs_0_), channel_id=1, source_target_pairs={{0,8},{4,12},{8,0},{12,4},{16,24},{20,28},{24,16},{28,20},{1,9},{5... | collective-permute-start | bytes 786440 | tf_op jit(solution)/shard_map/ppermute | solution.py:242
  68.5 17.6 %collective-permute-start.21 = (f32[32,1024]{1,0:T(8,128)S(1)}, f32[32,1024]{1,0:T(8,128)S(1)}, u32[]{:S(2)}, u32[]{:S(2)}) collective-permute-start(f32[32,1024]{1,0:T(8,128)S(1)} %get-tuple-element.345), channel_id=1, source_target_pairs={{0,2},{1,3},{2,0},{3,1},{4,6},{5,7},{6,4},{7,5},{8,10},{9,11},{10,... | collective-permute-start | bytes 393224 | tf_op jit(solution)/shard_map/ppermute | solution.py:248
  68.6 10.5 %collective-permute-start.25 = (f32[64,1024]{1,0:T(8,128)S(1)}, f32[64,1024]{1,0:T(8,128)S(1)}, u32[]{:S(2)}, u32[]{:S(2)}) collective-permute-start(f32[64,1024]{1,0:T(8,128)S(1)} %broadcast_select_fusion.5), channel_id=1, source_target_pairs={{0,1},{1,0},{2,3},{3,2},{4,5},{5,4},{6,7},{7,6},{8,9},{9,8},{10,11... | collective-permute-start | bytes 786440 | tf_op jit(solution)/shard_map/ppermute | solution.py:248
  71.4 13.6 %collective-permute-start.26 = (f32[32,1024]{1,0:T(8,128)S(1)}, f32[32,1024]{1,0:T(8,128)S(1)}, u32[]{:S(2)}, u32[]{:S(2)}) collective-permute-start(f32[32,1024]{1,0:T(8,128)S(1)} %get-tuple-element.344), channel_id=1, source_target_pairs={{0,16},{4,20},{8,24},{12,28},{16,0},{20,4},{24,8},{28,12},{1,17},{... | collective-permute-start | bytes 393224 | tf_op jit(solution)/shard_map/ppermute | solution.py:242
  75.9 9.2 %collective-permute-start.24 = (f32[64,1024]{1,0:T(8,128)S(1)}, f32[64,1024]{1,0:T(8,128)S(1)}, u32[]{:S(2)}, u32[]{:S(2)}) collective-permute-start(f32[64,1024]{1,0:T(8,128)S(1)} %get-tuple-element.244), channel_id=1, source_target_pairs={{0,8},{4,12},{8,0},{12,4},{16,24},{20,28},{24,16},{28,20},{1,9},{5... | collective-permute-start | bytes 786440 | tf_op jit(solution)/shard_map/ppermute | solution.py:242
  79.1 14.6 %collective-permute-start.32 = (f32[64,2048]{1,0:T(8,128)S(1)}, f32[64,2048]{1,0:T(8,128)S(1)}, u32[]{:S(2)}, u32[]{:S(2)}) collective-permute-start(f32[64,2048]{1,0:T(8,128)S(1)} %constant_dynamic-update-slice_fusion.4), channel_id=1, source_target_pairs={{0,16},{4,20},{8,24},{12,28},{16,0},{20,4},{24,8},{28,12},{1,17},{... | collective-permute-start | bytes 1572872 | tf_op jit(solution)/shard_map/ppermute | solution.py:242
  85.1 11.8 %collective-permute-start.31 = (f32[32,1024]{1,0:T(8,128)S(1)}, f32[32,1024]{1,0:T(8,128)S(1)}, u32[]{:S(2)}, u32[]{:S(2)}) collective-permute-start(f32[32,1024]{1,0:T(8,128)S(1)} %get-tuple-element.340), channel_id=1, source_target_pairs={{0,16},{4,20},{8,24},{12,28},{16,0},{20,4},{24,8},{28,12},{1,17},{... | collective-permute-start | bytes 393224 | tf_op jit(solution)/shard_map/ppermute | solution.py:242
  86.2 13.7 %collective-permute-start.36 = (f32[64,1024]{1,0:T(8,128)S(1)}, f32[64,1024]{1,0:T(8,128)S(1)}, u32[]{:S(2)}, u32[]{:S(2)}) collective-permute-start(f32[64,1024]{1,0:T(8,128)S(1)} %broadcast_select_fusion.4), channel_id=1, source_target_pairs={{0,1},{1,0},{2,3},{3,2},{4,5},{5,4},{6,7},{7,6},{8,9},{9,8},{10,11... | collective-permute-start | bytes 786440 | tf_op jit(solution)/shard_map/ppermute | solution.py:248
  91.6 9.3 %collective-permute-start.38 = (f32[64,1024]{1,0:T(8,128)S(1)}, f32[64,1024]{1,0:T(8,128)S(1)}, u32[]{:S(2)}, u32[]{:S(2)}) collective-permute-start(f32[64,1024]{1,0:T(8,128)S(1)} %get-tuple-element.265), channel_id=1, source_target_pairs={{0,8},{4,12},{8,0},{12,4},{16,24},{20,28},{24,16},{28,20},{1,9},{5... | collective-permute-start | bytes 786440 | tf_op jit(solution)/shard_map/ppermute | solution.py:242
  93.7 13.4 %collective-permute-start.34 = (f32[64,1024]{1,0:T(8,128)S(1)}, f32[64,1024]{1,0:T(8,128)S(1)}, u32[]{:S(2)}, u32[]{:S(2)}) collective-permute-start(f32[64,1024]{1,0:T(8,128)S(1)} %broadcast_select_fusion.3), channel_id=1, source_target_pairs={{0,1},{1,0},{2,3},{3,2},{4,5},{5,4},{6,7},{7,6},{8,9},{9,8},{10,11... | collective-permute-start | bytes 786440 | tf_op jit(solution)/shard_map/ppermute | solution.py:248
  96.2 9.9 %collective-permute-start.35 = (f32[64,1024]{1,0:T(8,128)S(1)}, f32[64,1024]{1,0:T(8,128)S(1)}, u32[]{:S(2)}, u32[]{:S(2)}) collective-permute-start(f32[64,1024]{1,0:T(8,128)S(1)} %get-tuple-element.275), channel_id=1, source_target_pairs={{0,8},{4,12},{8,0},{12,4},{16,24},{20,28},{24,16},{28,20},{1,9},{5... | collective-permute-start | bytes 786440 | tf_op jit(solution)/shard_map/ppermute | solution.py:242
  97.0 11.8 %collective-permute-start.33 = (f32[32,1024]{1,0:T(8,128)S(1)}, f32[32,1024]{1,0:T(8,128)S(1)}, u32[]{:S(2)}, u32[]{:S(2)}) collective-permute-start(f32[32,1024]{1,0:T(8,128)S(1)} %get-tuple-element.337), channel_id=1, source_target_pairs={{0,2},{1,3},{2,0},{3,1},{4,6},{5,7},{6,4},{7,5},{8,10},{9,11},{10,... | collective-permute-start | bytes 393224 | tf_op jit(solution)/shard_map/ppermute | solution.py:248
  100.9 9.1 %collective-permute-start.42 = (f32[64,1024]{1,0:T(8,128)S(1)}, f32[64,1024]{1,0:T(8,128)S(1)}, u32[]{:S(2)}, u32[]{:S(2)}) collective-permute-start(f32[64,1024]{1,0:T(8,128)S(1)} %broadcast_select_fusion.2), channel_id=1, source_target_pairs={{0,1},{1,0},{2,3},{3,2},{4,5},{5,4},{6,7},{7,6},{8,9},{9,8},{10,11... | collective-permute-start | bytes 786440 | tf_op jit(solution)/shard_map/ppermute | solution.py:248
  104.9 10.1 %collective-permute-start.40 = (f32[64,1024]{1,0:T(8,128)S(1)}, f32[64,1024]{1,0:T(8,128)S(1)}, u32[]{:S(2)}, u32[]{:S(2)}) collective-permute-start(f32[64,1024]{1,0:T(8,128)S(1)} %get-tuple-element.286), channel_id=1, source_target_pairs={{0,8},{4,12},{8,0},{12,4},{16,24},{20,28},{24,16},{28,20},{1,9},{5... | collective-permute-start | bytes 786440 | tf_op jit(solution)/shard_map/ppermute | solution.py:242
  106.1 9.9 %collective-permute-start.39 = (f32[32,1024]{1,0:T(8,128)S(1)}, f32[32,1024]{1,0:T(8,128)S(1)}, u32[]{:S(2)}, u32[]{:S(2)}) collective-permute-start(f32[32,1024]{1,0:T(8,128)S(1)} %get-tuple-element.334), channel_id=1, source_target_pairs={{0,2},{1,3},{2,0},{3,1},{4,6},{5,7},{6,4},{7,5},{8,10},{9,11},{10,... | collective-permute-start | bytes 393224 | tf_op jit(solution)/shard_map/ppermute | solution.py:248
  107.1 11.5 %collective-permute-start.44 = (f32[64,1024]{1,0:T(8,128)S(1)}, f32[64,1024]{1,0:T(8,128)S(1)}, u32[]{:S(2)}, u32[]{:S(2)}) collective-permute-start(f32[64,1024]{1,0:T(8,128)S(1)} %broadcast_select_fusion.1), channel_id=1, source_target_pairs={{0,1},{1,0},{2,3},{3,2},{4,5},{5,4},{6,7},{7,6},{8,9},{9,8},{10,11... | collective-permute-start | bytes 786440 | tf_op jit(solution)/shard_map/ppermute | solution.py:248
  120.3 10.1 %collective-permute-start.46 = (f32[32,1024]{1,0:T(8,128)S(1)}, f32[32,1024]{1,0:T(8,128)S(1)}, u32[]{:S(2)}, u32[]{:S(2)}) collective-permute-start(f32[32,1024]{1,0:T(8,128)S(1)} %get-tuple-element.326), channel_id=1, source_target_pairs={{0,2},{1,3},{2,0},{3,1},{4,6},{5,7},{6,4},{7,5},{8,10},{9,11},{10,... | collective-permute-start | bytes 393224 | tf_op jit(solution)/shard_map/ppermute | solution.py:248
  (26 other events, 236.2 us)

commit v12 on v11

--- a/solution.py
+++ b/solution.py
@@ -10,14 +10,15 @@
 TILE = 128
 CHUNKS = 4
 CORES = 2
+DIRECT = (0,)
 GROUPS = ((0,), (1,), (2, 3))
 UNITS = tuple((chunk, (half,)) for chunk in range(CHUNKS) for half in range(CORES))
 
 ORDER = (
-    "s0", "s1", "p0", "g00", "p1", "g01", "g10", "s2", "f0", "e0", "g11", "f1", "e1", "r0",
-    "p2", "g20", "e2", "x0", "r1", "g21", "g30", "z0", "r2", "x1", "e3", "g31", "e4", "z1",
-    "x2", "r3", "l0", "e5", "r4", "l1", "e7", "z2", "x3", "r5", "e6", "z3", "r7", "x4", "l2",
-    "x5", "z4", "r6", "l3", "z5", "x7", "l4", "z7", "x6", "l5", "z6", "l7", "l6",
+    "s0", "s1", "p0", "g00", "p1", "g10", "s2", "f0", "e0", "f1", "e1", "g11", "r0", "p2",
+    "g20", "g30", "r1", "x0", "g21", "e3", "z0", "x1", "e2", "g31", "r3", "l0", "e4", "z1",
+    "r2", "e5", "x3", "r4", "l1", "e7", "z3", "x2", "r5", "e6", "z2", "x4", "l3", "r7", "x5",
+    "z4", "r6", "z5", "x7", "l4", "l2", "x6", "z7", "l5", "z6", "l7", "l6",
 )
 
 SMEM = pl.BlockSpec(memory_space=pltpu.SMEM)
@@ -278,18 +279,11 @@
         if number == 0:
             held[chunk] = [mine[chunk]]
             layouts[chunk] = [[(0, 0, rows)]]
-        direct = chunk == 0 and chips == 4
-        if direct and number == 0:
+        if chunk in DIRECT and chips == 4:
             (send,) = ordered(mine[chunk])
             mark(send)
-            held[chunk] += [across_chips(send, 1), across_chips(send, 2)]
-            layouts[chunk] += [[(1, 0, rows)], [(2, 0, rows)]]
-        elif direct:
-            near, far = ordered(held[chunk][1], held[chunk][2])
-            near, far = near[: rows // 2], far[rows // 2 :]
-            mark(near, far)
-            held[chunk] += [across_chips(near, 2), across_chips(far, 1)]
-            layouts[chunk] += [[(3, 0, rows // 2)], [(3, rows // 2, rows // 2)]]
+            held[chunk] += [across_chips(send, k) for k in (3, 1, 2)]
+            layouts[chunk] += [[(k, 0, rows)] for k in (3, 1, 2)]
         else:
             bit = chip_bits[number]
             send = jnp.concatenate(ordered(*held[chunk]), axis=0)

time: 143 us -> 152 us (1.063)
  local copies, waits for them, and re-layouts: 1.65 us -> 7.66 us
  starting transfers between devices: 63.2 us -> 66.9 us
    ppermute x25, starting transfers between devices: 30.2 us -> 37.5 us  [along(): lax.ppermute(value, 'narrow', [(n, n ^ mask) for n in range(narrow_count)])]
    ppermute x25, waiting for transfers between devices: 33.8 us -> 27.4 us  [along(): lax.ppermute(value, 'narrow', [(n, n ^ mask) for n in range(narrow_count)])]
    unnamed x15 -> x37, local copies, waits for them, and re-layouts: 1.31 us -> 7.34 us
    ppermute x27 -> x26, waiting for transfers between devices: 10.3 us -> 15.9 us  [across(): lax.ppermute(value, 'wide', [(w, w ^ mask) for w in range(wide_count)])]
    ppermute x27 -> x26, starting transfers between devices: 33 us -> 29.4 us  [across(): lax.ppermute(value, 'wide', [(w, w ^ mask) for w in range(wide_count)])]
  transfers between devices with their start and end apart: 52 -> 51, of which waited for: 24 -> 16; matrix products, arithmetic and copies ran while one was open for 1% -> 1% of each run, Pallas kernels for 21% -> 20%
where the time goes in v12:
time: 152 us
  starting transfers between devices  66.9 us (44%)
  waiting for transfers between devices  43.3 us (28%)
  Pallas kernels  32.7 us (22%)
  local copies, waits for them, and re-layouts  7.66 us (5%)
    ppermute x25, starting transfers between devices, along(): lax.ppermute(value, 'narrow', [(n, n ^ mask) for n in range(narrow_count)])  37.5 us
    ppermute x26, starting transfers between devices, across(): lax.ppermute(value, 'wide', [(w, w ^ mask) for w in range(wide_count)])  29.4 us
    ppermute x25, waiting for transfers between devices, along(): lax.ppermute(value, 'narrow', [(n, n ^ mask) for n in range(narrow_count)])  27.4 us
    pallas_call x8, Pallas kernels, product(): pl.pallas_call(functools.partial(product_kernel, count, rows, layout, tar...  19.4 us
    ppermute x26, waiting for transfers between devices, across(): lax.ppermute(value, 'wide', [(w, w ^ mask) for w in range(wide_count)])  15.9 us
    pallas_call x2, Pallas kernels, split(): pl.pallas_call(functools.partial(split_kernel, step), in_specs=[HBM], out...  8.53 us
    unnamed x37, local copies, waits for them, and re-layouts  7.34 us
  transfers between devices with their start and end apart: 51, of which 16 were waited for; matrix products, arithmetic and copies ran while one was open for 1% of the time, Pallas kernels for 20%

profile of v12, /device:TPU:0, one launch (start us, length us, event | category | flops | bytes accessed | tf_op | source)
XLA Modules:
  0.0 152.0 jit_solution(1212088037934072446)
XLA Ops:
  3.0 2.6 %collective-permute-start = (f32[8,2048]{1,0:T(8,128)S(1)}, f32[8,2048]{1,0:T(8,128)S(1)}, u32[]{:S(2)}, u32[]{:S(2)}) collective-permute-start(f32[8,2048]{1,0:T(8,128)S(1)} %get-tuple-element.162), channel_id=1, source_target_pairs={{0,1},{1,0},{2,3},{3,2},{4,5},{5,4},{6,7},{7,6},{8,9},{9,8},{10,11... | collective-permute-start | bytes 196616 | tf_op jit(solution)/shard_map/ppermute | solution.py:249
  5.6 2.6 %collective-permute-start.1 = (f32[8,2048]{1,0:T(8,128)S(1)}, f32[8,2048]{1,0:T(8,128)S(1)}, u32[]{:S(2)}, u32[]{:S(2)}) collective-permute-start(f32[8,2048]{1,0:T(8,128)S(1)} %get-tuple-element.163), channel_id=1, source_target_pairs={{0,2},{1,3},{2,0},{3,1},{4,6},{5,7},{6,4},{7,5},{8,10},{9,11},{10,... | collective-permute-start | bytes 196616 | tf_op jit(solution)/shard_map/ppermute | solution.py:249
  8.3 4.2 %collective-permute-done.1.refs_2_ = f32[8,2048]{1,0:T(8,128)S(1)} collective-permute-done((f32[8,2048]{1,0:T(8,128)S(1)}, f32[8,2048]{1,0:T(8,128)S(1)}, u32[]{:S(2)}, u32[]{:S(2)}) %collective-permute-start.1) | collective-permute-done | bytes 65568 | tf_op jit(solution)/shard_map/ppermute | solution.py:249
  14.9 2.5 %collective-permute-start.3 = (f32[32,2048]{1,0:T(8,128)S(1)}, f32[32,2048]{1,0:T(8,128)S(1)}, u32[]{:S(2)}, u32[]{:S(2)}) collective-permute-start(f32[32,2048]{1,0:T(8,128)S(1)} %pack.3.refs_0_), channel_id=1, source_target_pairs={{0,24},{4,28},{8,16},{12,20},{16,8},{20,12},{24,0},{28,4},{1,25},{... | collective-permute-start | bytes 786440 | tf_op jit(solution)/shard_map/ppermute | solution.py:243
  19.7 3.0 %collective-permute-done.6.refs_1_ = f32[8,2048]{1,0:T(8,128)S(1)} collective-permute-done((f32[8,2048]{1,0:T(8,128)S(1)}, f32[8,2048]{1,0:T(8,128)S(1)}, u32[]{:S(2)}, u32[]{:S(2)}) %collective-permute-start.6) | collective-permute-done | bytes 65568 | tf_op jit(solution)/shard_map/ppermute | solution.py:249
  22.7 2.2 %collective-permute-start.7 = (f32[8,2048]{1,0:T(8,128)S(1)}, f32[8,2048]{1,0:T(8,128)S(1)}, u32[]{:S(2)}, u32[]{:S(2)}) collective-permute-start(f32[8,2048]{1,0:T(8,128)S(1)} %get-tuple-element.169), channel_id=1, source_target_pairs={{0,2},{1,3},{2,0},{3,1},{4,6},{5,7},{6,4},{7,5},{8,10},{9,11},{10,... | collective-permute-start | bytes 196616 | tf_op jit(solution)/shard_map/ppermute | solution.py:249
  24.9 3.0 %collective-permute-done.7.refs_2_ = f32[8,2048]{1,0:T(8,128)S(1)} collective-permute-done((f32[8,2048]{1,0:T(8,128)S(1)}, f32[8,2048]{1,0:T(8,128)S(1)}, u32[]{:S(2)}, u32[]{:S(2)}) %collective-permute-start.7) | collective-permute-done | bytes 65568 | tf_op jit(solution)/shard_map/ppermute | solution.py:249
  27.9 4.0 %collective-permute-start.8 = (f32[8,2048]{1,0:T(8,128)S(1)}, f32[8,2048]{1,0:T(8,128)S(1)}, u32[]{:S(2)}, u32[]{:S(2)}) collective-permute-start(f32[8,2048]{1,0:T(8,128)S(1)} %get-tuple-element.170), channel_id=1, source_target_pairs={{0,3},{1,2},{2,1},{3,0},{4,7},{5,6},{6,5},{7,4},{8,11},{9,10},{10,... | collective-permute-start | bytes 196616 | tf_op jit(solution)/shard_map/ppermute | solution.py:249
  31.9 2.2 %collective-permute-done.8.refs_3_ = f32[8,2048]{1,0:T(8,128)S(1)} collective-permute-done((f32[8,2048]{1,0:T(8,128)S(1)}, f32[8,2048]{1,0:T(8,128)S(1)}, u32[]{:S(2)}, u32[]{:S(2)}) %collective-permute-start.8) | collective-permute-done | bytes 65568 | tf_op jit(solution)/shard_map/ppermute | solution.py:249
  36.2 4.3 %split.2 = (bf16[2048,1024]{1,0:T(8,128)(2,1)S(1)}, bf16[2048,1024]{1,0:T(8,128)(2,1)S(1)}, f32[8,128]{1,0:T(8,128)}) custom-call(f32[2048,1024]{1,0:T(8,128)} %whole_ref.2), custom_call_target="tpu_custom_call" | custom-call | flops 1 | bytes 1 | tf_op jit(solution)/shard_map/split/pallas_call | solution.py:113
  40.7 4.4 %collective-permute-start.15 = (f32[16,2048]{1,0:T(8,128)S(1)}, f32[16,2048]{1,0:T(8,128)S(1)}, u32[]{:S(2)}, u32[]{:S(2)}) collective-permute-start(f32[16,2048]{1,0:T(8,128)S(1)} %get-tuple-element.190), channel_id=1, source_target_pairs={{0,2},{1,3},{2,0},{3,1},{4,6},{5,7},{6,4},{7,5},{8,10},{9,11},{10,... | collective-permute-start | bytes 393224 | tf_op jit(solution)/shard_map/ppermute | solution.py:249
  45.0 2.5 %product.8 = (f32[64,1024]{1,0:T(8,128)S(1)}, f32[64,1024]{1,0:T(8,128)S(1)}) custom-call(s32[3]{0:T(128)S(1)} %pad_add_fusion.place_ref, s32[8,64]{1,0:T(8,128)S(1)} %copy-done.13, s32[8]{0:T(128)S(1)} %copy-done.14, f32[32,2048]{1,0:T(8,128)S(1)} %pack.3.refs_0_, f32[32,2048]{1,0:T(8,128)S(1)} %collective-permute-done.3.refs_1_, ...), custom_call_target="tpu_custom_call" | custom-call | flops 3221225472 | bytes 1 | tf_op jit(solution)/shard_map/product/pallas_call | solution.py:174
  48.1 4.3 %split.3 = (bf16[2048,1024]{1,0:T(8,128)(2,1)S(1)}, bf16[2048,1024]{1,0:T(8,128)(2,1)S(1)}, f32[8,128]{1,0:T(8,128)}) custom-call(f32[2048,1024]{1,0:T(8,128)} %collective-permute-done.11.whole_ref), custom_call_target="tpu_custom_call" | custom-call | flops 1 | bytes 1 | tf_op jit(solution)/shard_map/split/pallas_call | solution.py:113
  52.4 2.4 %product.9 = (f32[64,1024]{1,0:T(8,128)S(1)}, f32[64,1024]{1,0:T(8,128)S(1)}) custom-call(s32[3]{0:T(128)S(1)} %pad_add_fusion.place_ref, s32[8,64]{1,0:T(8,128)S(1)} %copy-done.13, s32[8]{0:T(128)S(1)} %copy-done.14, f32[32,2048]{1,0:T(8,128)S(1)} %pack.3.refs_0_, f32[32,2048]{1,0:T(8,128)S(1)} %collective-permute-done.3.refs_1_, ...), custom_call_target="tpu_custom_call" | custom-call | flops 3221225472 | bytes 1 | tf_op jit(solution)/shard_map/product/pallas_call | solution.py:174
  69.7 4.3 %collective-permute-done.18.refs_2_ = f32[64,2048]{1,0:T(8,128)S(1)} collective-permute-done((f32[64,2048]{1,0:T(8,128)}, f32[64,2048]{1,0:T(8,128)S(1)}, u32[]{:S(2)}, u32[]{:S(2)}) %collective-permute-start.18) | collective-permute-done | bytes 524320 | tf_op jit(solution)/shard_map/ppermute | solution.py:243
  73.9 2.2 %copy-done.8 = bf16[2048,1024]{1,0:T(8,128)(2,1)S(1)} copy-done((bf16[2048,1024]{1,0:T(8,128)(2,1)S(1)}, bf16[2048,1024]{1,0:T(8,128)(2,1)}, u32[]{:S(2)}) %copy-start.8) | copy-done | bytes 4194328
  76.1 2.2 %copy-done.11 = bf16[2048,1024]{1,0:T(8,128)(2,1)S(1)} copy-done((bf16[2048,1024]{1,0:T(8,128)(2,1)S(1)}, bf16[2048,1024]{1,0:T(8,128)(2,1)}, u32[]{:S(2)}) %copy-start.11) | copy-done | bytes 4194328
  78.3 2.5 %product.10 = (f32[64,1024]{1,0:T(8,128)S(1)}, f32[64,1024]{1,0:T(8,128)S(1)}) custom-call(s32[3]{0:T(128)S(1)} %pad_add_fusion.place_ref, s32[8,64]{1,0:T(8,128)S(1)} %copy-done.13, s32[8]{0:T(128)S(1)} %copy-done.14, f32[32,2048]{1,0:T(8,128)S(1)} %pack.4.refs_0_, f32[32,2048]{1,0:T(8,128)S(1)} %collective-permute-done.10.refs_1_, ...), custom_call_target="tpu_custom_call" | custom-call | flops 3221225472 | bytes 1 | tf_op jit(solution)/shard_map/product/pallas_call | solution.py:174
  82.5 3.6 %collective-permute-start.20 = (f32[32,1024]{1,0:T(8,128)S(1)}, f32[32,1024]{1,0:T(8,128)S(1)}, u32[]{:S(2)}, u32[]{:S(2)}) collective-permute-start(f32[32,1024]{1,0:T(8,128)S(1)} %get-tuple-element.339), channel_id=1, source_target_pairs={{0,2},{1,3},{2,0},{3,1},{4,6},{5,7},{6,4},{7,5},{8,10},{9,11},{10,... | collective-permute-start | bytes 393224 | tf_op jit(solution)/shard_map/ppermute | solution.py:249
  87.8 2.4 %product.11 = (f32[64,1024]{1,0:T(8,128)S(1)}, f32[64,1024]{1,0:T(8,128)S(1)}) custom-call(s32[3]{0:T(128)S(1)} %pad_add_fusion.place_ref, s32[8,64]{1,0:T(8,128)S(1)} %copy-done.13, s32[8]{0:T(128)S(1)} %copy-done.14, f32[32,2048]{1,0:T(8,128)S(1)} %pack.4.refs_0_, f32[32,2048]{1,0:T(8,128)S(1)} %collective-permute-done.10.refs_1_, ...), custom_call_target="tpu_custom_call" | custom-call | flops 3221225472 | bytes 1 | tf_op jit(solution)/shard_map/product/pallas_call | solution.py:174
  92.0 2.4 %product.12 = (f32[64,1024]{1,0:T(8,128)S(1)}, f32[64,1024]{1,0:T(8,128)S(1)}) custom-call(s32[3]{0:T(128)S(1)} %pad_add_fusion.place_ref, s32[8,64]{1,0:T(8,128)S(1)} %copy-done.13, s32[8]{0:T(128)S(1)} %copy-done.14, f32[32,2048]{1,0:T(8,128)S(1)} %get-tuple-element.253.refs_0_, f32[32,2048]{1,0:T(8,128)S(1)} %collective-permute-done.19.refs_1_, ...), custom_call_target="tpu_custom_call" | custom-call | flops 3221225472 | bytes 1 | tf_op jit(solution)/shard_map/product/pallas_call | solution.py:174
  94.4 2.5 %collective-permute-start.27 = (f32[64,1024]{1,0:T(8,128)S(1)}, f32[64,1024]{1,0:T(8,128)S(1)}, u32[]{:S(2)}, u32[]{:S(2)}) collective-permute-start(f32[64,1024]{1,0:T(8,128)S(1)} %get-tuple-element.248), channel_id=1, source_target_pairs={{0,8},{4,12},{8,0},{12,4},{16,24},{20,28},{24,16},{28,20},{1,9},{5... | collective-permute-start | bytes 786440 | tf_op jit(solution)/shard_map/ppermute | solution.py:243
  98.8 2.1 %collective-permute-start.30 = (f32[64,1024]{1,0:T(8,128)S(1)}, f32[64,1024]{1,0:T(8,128)S(1)}, u32[]{:S(2)}, u32[]{:S(2)}) collective-permute-start(f32[64,1024]{1,0:T(8,128)S(1)} %broadcast_select_fusion.4), channel_id=1, source_target_pairs={{0,1},{1,0},{2,3},{3,2},{4,5},{5,4},{6,7},{7,6},{8,9},{9,8},{10,11... | collective-permute-start | bytes 786440 | tf_op jit(solution)/shard_map/ppermute | solution.py:249
  100.9 2.4 %product.13 = (f32[64,1024]{1,0:T(8,128)S(1)}, f32[64,1024]{1,0:T(8,128)S(1)}) custom-call(s32[3]{0:T(128)S(1)} %pad_add_fusion.place_ref, s32[8,64]{1,0:T(8,128)S(1)} %copy-done.13, s32[8]{0:T(128)S(1)} %copy-done.14, f32[32,2048]{1,0:T(8,128)S(1)} %get-tuple-element.253.refs_0_, f32[32,2048]{1,0:T(8,128)S(1)} %collective-permute-done.19.refs_1_, ...), custom_call_target="tpu_custom_call" | custom-call | flops 3221225472 | bytes 1 | tf_op jit(solution)/shard_map/product/pallas_call | solution.py:174
  107.1 2.4 %product.14 = (f32[64,1024]{1,0:T(8,128)S(1)}, f32[64,1024]{1,0:T(8,128)S(1)}) custom-call(s32[3]{0:T(128)S(1)} %pad_add_fusion.place_ref, s32[8,64]{1,0:T(8,128)S(1)} %copy-done.13, s32[8]{0:T(128)S(1)} %copy-done.14, f32[32,2048]{1,0:T(8,128)S(1)} %get-tuple-element.275.refs_0_, f32[32,2048]{1,0:T(8,128)S(1)} %collective-permute-done.22.refs_1_, ...), custom_call_target="tpu_custom_call" | custom-call | flops 3221225472 | bytes 1 | tf_op jit(solution)/shard_map/product/pallas_call | solution.py:174
  109.7 3.5 %collective-permute-start.40 = (f32[32,1024]{1,0:T(8,128)S(1)}, f32[32,1024]{1,0:T(8,128)S(1)}, u32[]{:S(2)}, u32[]{:S(2)}) collective-permute-start(f32[32,1024]{1,0:T(8,128)S(1)} %get-tuple-element.326), channel_id=1, source_target_pairs={{0,2},{1,3},{2,0},{3,1},{4,6},{5,7},{6,4},{7,5},{8,10},{9,11},{10,... | collective-permute-start | bytes 393224 | tf_op jit(solution)/shard_map/ppermute | solution.py:249
  113.7 2.4 %product.15 = (f32[64,1024]{1,0:T(8,128)S(1)}, f32[64,1024]{1,0:T(8,128)S(1)}) custom-call(s32[3]{0:T(128)S(1)} %pad_add_fusion.place_ref, s32[8,64]{1,0:T(8,128)S(1)} %copy-done.13, s32[8]{0:T(128)S(1)} %copy-done.14, f32[32,2048]{1,0:T(8,128)S(1)} %get-tuple-element.275.refs_0_, f32[32,2048]{1,0:T(8,128)S(1)} %collective-permute-done.22.refs_1_, ...), custom_call_target="tpu_custom_call" | custom-call | flops 3221225472 | bytes 1 | tf_op jit(solution)/shard_map/product/pallas_call | solution.py:174
  116.1 2.3 %collective-permute-done.33 = f32[32,1024]{1,0:T(8,128)S(1)} collective-permute-done((f32[32,1024]{1,0:T(8,128)S(1)}, f32[32,1024]{1,0:T(8,128)S(1)}, u32[]{:S(2)}, u32[]{:S(2)}) %collective-permute-start.33) | collective-permute-done | bytes 131104 | tf_op jit(solution)/shard_map/ppermute | solution.py:243
  131.9 4.2 %collective-permute-done.41.refs_9_ = f32[32,1024]{1,0:T(8,128)S(1)} collective-permute-done((f32[32,1024]{1,0:T(8,128)S(1)}, f32[32,1024]{1,0:T(8,128)S(1)}, u32[]{:S(2)}, u32[]{:S(2)}) %collective-permute-start.41) | collective-permute-done | bytes 131104 | tf_op jit(solution)/shard_map/ppermute | solution.py:249
  136.0 3.1 %collective-permute-done.47 = f32[64,1024]{1,0:T(8,128)S(1)} collective-permute-done((f32[64,1024]{1,0:T(8,128)S(1)}, f32[64,1024]{1,0:T(8,128)S(1)}, u32[]{:S(2)}, u32[]{:S(2)}) %collective-permute-start.47) | collective-permute-done | bytes 262176 | tf_op jit(solution)/shard_map/ppermute | solution.py:249
  139.4 4.8 %collective-permute-done.48 = f32[32,1024]{1,0:T(8,128)S(1)} collective-permute-done((f32[32,1024]{1,0:T(8,128)S(1)}, f32[32,1024]{1,0:T(8,128)S(1)}, u32[]{:S(2)}, u32[]{:S(2)}) %collective-permute-start.48) | collective-permute-done | bytes 131104 | tf_op jit(solution)/shard_map/ppermute | solution.py:243
  145.3 4.9 %collective-permute-done.49.refs_13_ = f32[32,1024]{1,0:T(8,128)S(1)} collective-permute-done((f32[32,1024]{1,0:T(8,128)S(1)}, f32[32,1024]{1,0:T(8,128)S(1)}, u32[]{:S(2)}, u32[]{:S(2)}) %collective-permute-start.49) | collective-permute-done | bytes 131104 | tf_op jit(solution)/shard_map/ppermute | solution.py:249
  (159 shorter events, 53.1 us)
Async XLA Ops:
  0.0 47.5 %collective-permute-start.11 = (f32[2048,1024]{1,0:T(8,128)}, f32[2048,1024]{1,0:T(8,128)}, u32[]{:S(2)}, u32[]{:S(2)}) collective-permute-start(f32[2048,1024]{1,0:T(8,128)} %whole_ref.2), channel_id=1, source_target_pairs={{0,4},{4,0},{8,12},{12,8},{16,20},{20,16},{24,28},{28,24},{1,5},{5... | collective-permute-start | bytes 25165832 | tf_op jit(solution)/shard_map/ppermute | solution.py:243
  14.9 25.7 %collective-permute-start.3 = (f32[32,2048]{1,0:T(8,128)S(1)}, f32[32,2048]{1,0:T(8,128)S(1)}, u32[]{:S(2)}, u32[]{:S(2)}) collective-permute-start(f32[32,2048]{1,0:T(8,128)S(1)} %pack.3.refs_0_), channel_id=1, source_target_pairs={{0,24},{4,28},{8,16},{12,20},{16,8},{20,12},{24,0},{28,4},{1,25},{... | collective-permute-start | bytes 786440 | tf_op jit(solution)/shard_map/ppermute | solution.py:243
  17.4 23.3 %collective-permute-start.4 = (f32[32,2048]{1,0:T(8,128)S(1)}, f32[32,2048]{1,0:T(8,128)S(1)}, u32[]{:S(2)}, u32[]{:S(2)}) collective-permute-start(f32[32,2048]{1,0:T(8,128)S(1)} %pack.3.refs_0_), channel_id=1, source_target_pairs={{0,8},{4,12},{8,0},{12,4},{16,24},{20,28},{24,16},{28,20},{1,9},{5... | collective-permute-start | bytes 786440 | tf_op jit(solution)/shard_map/ppermute | solution.py:243
  17.9 27.1 %collective-permute-start.5 = (f32[32,2048]{1,0:T(8,128)S(1)}, f32[32,2048]{1,0:T(8,128)S(1)}, u32[]{:S(2)}, u32[]{:S(2)}) collective-permute-start(f32[32,2048]{1,0:T(8,128)S(1)} %pack.3.refs_0_), channel_id=1, source_target_pairs={{0,16},{4,20},{8,24},{12,28},{16,0},{20,4},{24,8},{28,12},{1,17},{... | collective-permute-start | bytes 786440 | tf_op jit(solution)/shard_map/ppermute | solution.py:243
  34.7 21.1 %collective-permute-start.10 = (f32[32,2048]{1,0:T(8,128)S(1)}, f32[32,2048]{1,0:T(8,128)S(1)}, u32[]{:S(2)}, u32[]{:S(2)}) collective-permute-start(f32[32,2048]{1,0:T(8,128)S(1)} %pack.4.refs_0_), channel_id=1, source_target_pairs={{0,8},{4,12},{8,0},{12,4},{16,24},{20,28},{24,16},{28,20},{1,9},{5... | collective-permute-start | bytes 786440 | tf_op jit(solution)/shard_map/ppermute | solution.py:243
  40.6 18.2 %collective-permute-start.14 = (f32[16,2048]{1,0:T(8,128)}, f32[16,2048]{1,0:T(8,128)S(1)}, u32[]{:S(2)}, u32[]{:S(2)}) collective-permute-start(f32[16,2048]{1,0:T(8,128)} %get-tuple-element.189), channel_id=1, source_target_pairs={{0,1},{1,0},{2,3},{3,2},{4,5},{5,4},{6,7},{7,6},{8,9},{9,8},{10,11... | collective-permute-start | bytes 393224 | tf_op jit(solution)/shard_map/ppermute | solution.py:249
  40.7 18.2 %collective-permute-start.15 = (f32[16,2048]{1,0:T(8,128)S(1)}, f32[16,2048]{1,0:T(8,128)S(1)}, u32[]{:S(2)}, u32[]{:S(2)}) collective-permute-start(f32[16,2048]{1,0:T(8,128)S(1)} %get-tuple-element.190), channel_id=1, source_target_pairs={{0,2},{1,3},{2,0},{3,1},{4,6},{5,7},{6,4},{7,5},{8,10},{9,11},{10,... | collective-permute-start | bytes 393224 | tf_op jit(solution)/shard_map/ppermute | solution.py:249
  45.0 13.8 %collective-permute-start.16 = (f32[16,2048]{1,0:T(8,128)S(1)}, f32[16,2048]{1,0:T(8,128)S(1)}, u32[]{:S(2)}, u32[]{:S(2)}) collective-permute-start(f32[16,2048]{1,0:T(8,128)S(1)} %get-tuple-element.191), channel_id=1, source_target_pairs={{0,3},{1,2},{2,1},{3,0},{4,7},{5,6},{6,5},{7,4},{8,11},{9,10},{10,... | collective-permute-start | bytes 393224 | tf_op jit(solution)/shard_map/ppermute | solution.py:249
  47.5 9.8 %collective-permute-start.9 = (f32[64,1024]{1,0:T(8,128)S(1)}, f32[64,1024]{1,0:T(8,128)S(1)}, u32[]{:S(2)}, u32[]{:S(2)}) collective-permute-start(f32[64,1024]{1,0:T(8,128)S(1)} %get-tuple-element.197), channel_id=1, source_target_pairs={{0,8},{4,12},{8,0},{12,4},{16,24},{20,28},{24,16},{28,20},{1,9},{5... | collective-permute-start | bytes 786440 | tf_op jit(solution)/shard_map/ppermute | solution.py:243
  55.8 9.2 %collective-permute-start.13 = (f32[64,1024]{1,0:T(8,128)S(1)}, f32[64,1024]{1,0:T(8,128)S(1)}, u32[]{:S(2)}, u32[]{:S(2)}) collective-permute-start(f32[64,1024]{1,0:T(8,128)S(1)} %get-tuple-element.203), channel_id=1, source_target_pairs={{0,8},{4,12},{8,0},{12,4},{16,24},{20,28},{24,16},{28,20},{1,9},{5... | collective-permute-start | bytes 786440 | tf_op jit(solution)/shard_map/ppermute | solution.py:243
  60.0 13.9 %collective-permute-start.18 = (f32[64,2048]{1,0:T(8,128)}, f32[64,2048]{1,0:T(8,128)S(1)}, u32[]{:S(2)}, u32[]{:S(2)}) collective-permute-start(f32[64,2048]{1,0:T(8,128)} %copy-done.15), channel_id=1, source_target_pairs={{0,16},{4,20},{8,24},{12,28},{16,0},{20,4},{24,8},{28,12},{1,17},{... | collective-permute-start | bytes 1572872 | tf_op jit(solution)/shard_map/ppermute | solution.py:243
  61.5 28.7 %collective-permute-start.22 = (f32[32,2048]{1,0:T(8,128)S(1)}, f32[32,2048]{1,0:T(8,128)S(1)}, u32[]{:S(2)}, u32[]{:S(2)}) collective-permute-start(f32[32,2048]{1,0:T(8,128)S(1)} %get-tuple-element.275.refs_0_), channel_id=1, source_target_pairs={{0,8},{4,12},{8,0},{12,4},{16,24},{20,28},{24,16},{28,20},{1,9},{5... | collective-permute-start | bytes 786440 | tf_op jit(solution)/shard_map/ppermute | solution.py:243
  65.0 21.1 %collective-permute-start.23 = (f32[64,1024]{1,0:T(8,128)S(1)}, f32[64,1024]{1,0:T(8,128)S(1)}, u32[]{:S(2)}, u32[]{:S(2)}) collective-permute-start(f32[64,1024]{1,0:T(8,128)S(1)} %broadcast_select_fusion.6), channel_id=1, source_target_pairs={{0,1},{1,0},{2,3},{3,2},{4,5},{5,4},{6,7},{7,6},{8,9},{9,8},{10,11... | collective-permute-start | bytes 786440 | tf_op jit(solution)/shard_map/ppermute | solution.py:249
  65.8 16.7 %collective-permute-start.17 = (f32[32,1024]{1,0:T(8,128)S(1)}, f32[32,1024]{1,0:T(8,128)S(1)}, u32[]{:S(2)}, u32[]{:S(2)}) collective-permute-start(f32[32,1024]{1,0:T(8,128)S(1)} %get-tuple-element.341), channel_id=1, source_target_pairs={{0,16},{4,20},{8,24},{12,28},{16,0},{20,4},{24,8},{28,12},{1,17},{... | collective-permute-start | bytes 393224 | tf_op jit(solution)/shard_map/ppermute | solution.py:243
  68.1 23.9 %collective-permute-start.25 = (f32[64,2048]{1,0:T(8,128)S(1)}, f32[64,2048]{1,0:T(8,128)S(1)}, u32[]{:S(2)}, u32[]{:S(2)}) collective-permute-start(f32[64,2048]{1,0:T(8,128)S(1)} %constant_dynamic-update-slice_fusion.2), channel_id=1, source_target_pairs={{0,16},{4,20},{8,24},{12,28},{16,0},{20,4},{24,8},{28,12},{1,17},{... | collective-permute-start | bytes 1572872 | tf_op jit(solution)/shard_map/ppermute | solution.py:243
  80.8 9.9 %collective-permute-start.21 = (f32[64,1024]{1,0:T(8,128)S(1)}, f32[64,1024]{1,0:T(8,128)S(1)}, u32[]{:S(2)}, u32[]{:S(2)}) collective-permute-start(f32[64,1024]{1,0:T(8,128)S(1)} %get-tuple-element.227), channel_id=1, source_target_pairs={{0,8},{4,12},{8,0},{12,4},{16,24},{20,28},{24,16},{28,20},{1,9},{5... | collective-permute-start | bytes 786440 | tf_op jit(solution)/shard_map/ppermute | solution.py:243
  86.2 10.8 %collective-permute-start.24 = (f32[32,1024]{1,0:T(8,128)S(1)}, f32[32,1024]{1,0:T(8,128)S(1)}, u32[]{:S(2)}, u32[]{:S(2)}) collective-permute-start(f32[32,1024]{1,0:T(8,128)S(1)} %get-tuple-element.338), channel_id=1, source_target_pairs={{0,16},{4,20},{8,24},{12,28},{16,0},{20,4},{24,8},{28,12},{1,17},{... | collective-permute-start | bytes 393224 | tf_op jit(solution)/shard_map/ppermute | solution.py:243
  90.6 16.5 %collective-permute-start.32 = (f32[64,2048]{1,0:T(8,128)S(1)}, f32[64,2048]{1,0:T(8,128)S(1)}, u32[]{:S(2)}, u32[]{:S(2)}) collective-permute-start(f32[64,2048]{1,0:T(8,128)S(1)} %constant_dynamic-update-slice_fusion.4), channel_id=1, source_target_pairs={{0,16},{4,20},{8,24},{12,28},{16,0},{20,4},{24,8},{28,12},{1,17},{... | collective-permute-start | bytes 1572872 | tf_op jit(solution)/shard_map/ppermute | solution.py:243
  91.4 11.9 %collective-permute-start.28 = (f32[64,1024]{1,0:T(8,128)S(1)}, f32[64,1024]{1,0:T(8,128)S(1)}, u32[]{:S(2)}, u32[]{:S(2)}) collective-permute-start(f32[64,1024]{1,0:T(8,128)S(1)} %broadcast_select_fusion.5), channel_id=1, source_target_pairs={{0,1},{1,0},{2,3},{3,2},{4,5},{5,4},{6,7},{7,6},{8,9},{9,8},{10,11... | collective-permute-start | bytes 786440 | tf_op jit(solution)/shard_map/ppermute | solution.py:249
  94.4 9.1 %collective-permute-start.27 = (f32[64,1024]{1,0:T(8,128)S(1)}, f32[64,1024]{1,0:T(8,128)S(1)}, u32[]{:S(2)}, u32[]{:S(2)}) collective-permute-start(f32[64,1024]{1,0:T(8,128)S(1)} %get-tuple-element.248), channel_id=1, source_target_pairs={{0,8},{4,12},{8,0},{12,4},{16,24},{20,28},{24,16},{28,20},{1,9},{5... | collective-permute-start | bytes 786440 | tf_op jit(solution)/shard_map/ppermute | solution.py:243
  98.8 10.8 %collective-permute-start.30 = (f32[64,1024]{1,0:T(8,128)S(1)}, f32[64,1024]{1,0:T(8,128)S(1)}, u32[]{:S(2)}, u32[]{:S(2)}) collective-permute-start(f32[64,1024]{1,0:T(8,128)S(1)} %broadcast_select_fusion.4), channel_id=1, source_target_pairs={{0,1},{1,0},{2,3},{3,2},{4,5},{5,4},{6,7},{7,6},{8,9},{9,8},{10,11... | collective-permute-start | bytes 786440 | tf_op jit(solution)/shard_map/ppermute | solution.py:249
  103.3 10.1 %collective-permute-start.34 = (f32[64,1024]{1,0:T(8,128)S(1)}, f32[64,1024]{1,0:T(8,128)S(1)}, u32[]{:S(2)}, u32[]{:S(2)}) collective-permute-start(f32[64,1024]{1,0:T(8,128)S(1)} %get-tuple-element.258), channel_id=1, source_target_pairs={{0,8},{4,12},{8,0},{12,4},{16,24},{20,28},{24,16},{28,20},{1,9},{5... | collective-permute-start | bytes 786440 | tf_op jit(solution)/shard_map/ppermute | solution.py:243
  105.6 14.7 %collective-permute-start.36 = (f32[64,1024]{1,0:T(8,128)S(1)}, f32[64,1024]{1,0:T(8,128)S(1)}, u32[]{:S(2)}, u32[]{:S(2)}) collective-permute-start(f32[64,1024]{1,0:T(8,128)S(1)} %broadcast_select_fusion.3), channel_id=1, source_target_pairs={{0,1},{1,0},{2,3},{3,2},{4,5},{5,4},{6,7},{7,6},{8,9},{9,8},{10,11... | collective-permute-start | bytes 786440 | tf_op jit(solution)/shard_map/ppermute | solution.py:249
  109.6 12.4 %collective-permute-start.39 = (f32[64,1024]{1,0:T(8,128)S(1)}, f32[64,1024]{1,0:T(8,128)S(1)}, u32[]{:S(2)}, u32[]{:S(2)}) collective-permute-start(f32[64,1024]{1,0:T(8,128)S(1)} %get-tuple-element.269), channel_id=1, source_target_pairs={{0,8},{4,12},{8,0},{12,4},{16,24},{20,28},{24,16},{28,20},{1,9},{5... | collective-permute-start | bytes 786440 | tf_op jit(solution)/shard_map/ppermute | solution.py:243
  109.7 11.0 %collective-permute-start.40 = (f32[32,1024]{1,0:T(8,128)S(1)}, f32[32,1024]{1,0:T(8,128)S(1)}, u32[]{:S(2)}, u32[]{:S(2)}) collective-permute-start(f32[32,1024]{1,0:T(8,128)S(1)} %get-tuple-element.326), channel_id=1, source_target_pairs={{0,2},{1,3},{2,0},{3,1},{4,6},{5,7},{6,4},{7,5},{8,10},{9,11},{10,... | collective-permute-start | bytes 393224 | tf_op jit(solution)/shard_map/ppermute | solution.py:249
  113.4 9.8 %collective-permute-start.38 = (f32[64,1024]{1,0:T(8,128)S(1)}, f32[64,1024]{1,0:T(8,128)S(1)}, u32[]{:S(2)}, u32[]{:S(2)}) collective-permute-start(f32[64,1024]{1,0:T(8,128)S(1)} %broadcast_select_fusion.2), channel_id=1, source_target_pairs={{0,1},{1,0},{2,3},{3,2},{4,5},{5,4},{6,7},{7,6},{8,9},{9,8},{10,11... | collective-permute-start | bytes 786440 | tf_op jit(solution)/shard_map/ppermute | solution.py:249
  118.5 10.1 %collective-permute-start.44 = (f32[64,1024]{1,0:T(8,128)S(1)}, f32[64,1024]{1,0:T(8,128)S(1)}, u32[]{:S(2)}, u32[]{:S(2)}) collective-permute-start(f32[64,1024]{1,0:T(8,128)S(1)} %get-tuple-element.280), channel_id=1, source_target_pairs={{0,8},{4,12},{8,0},{12,4},{16,24},{20,28},{24,16},{28,20},{1,9},{5... | collective-permute-start | bytes 786440 | tf_op jit(solution)/shard_map/ppermute | solution.py:243
  120.3 15.7 %collective-permute-start.35 = (f32[32,1024]{1,0:T(8,128)S(1)}, f32[32,1024]{1,0:T(8,128)S(1)}, u32[]{:S(2)}, u32[]{:S(2)}) collective-permute-start(f32[32,1024]{1,0:T(8,128)S(1)} %get-tuple-element.329), channel_id=1, source_target_pairs={{0,2},{1,3},{2,0},{3,1},{4,6},{5,7},{6,4},{7,5},{8,10},{9,11},{10,... | collective-permute-start | bytes 393224 | tf_op jit(solution)/shard_map/ppermute | solution.py:249
  122.0 9.0 %collective-permute-start.42 = (f32[64,1024]{1,0:T(8,128)S(1)}, f32[64,1024]{1,0:T(8,128)S(1)}, u32[]{:S(2)}, u32[]{:S(2)}) collective-permute-start(f32[64,1024]{1,0:T(8,128)S(1)} %broadcast_select_fusion.1), channel_id=1, source_target_pairs={{0,1},{1,0},{2,3},{3,2},{4,5},{5,4},{6,7},{7,6},{8,9},{9,8},{10,11... | collective-permute-start | bytes 786440 | tf_op jit(solution)/shard_map/ppermute | solution.py:249
  126.9 9.1 %collective-permute-start.41 = (f32[32,1024]{1,0:T(8,128)S(1)}, f32[32,1024]{1,0:T(8,128)S(1)}, u32[]{:S(2)}, u32[]{:S(2)}) collective-permute-start(f32[32,1024]{1,0:T(8,128)S(1)} %get-tuple-element.323), channel_id=1, source_target_pairs={{0,2},{1,3},{2,0},{3,1},{4,6},{5,7},{6,4},{7,5},{8,10},{9,11},{10,... | collective-permute-start | bytes 393224 | tf_op jit(solution)/shard_map/ppermute | solution.py:249
  128.6 10.6 %collective-permute-start.47 = (f32[64,1024]{1,0:T(8,128)S(1)}, f32[64,1024]{1,0:T(8,128)S(1)}, u32[]{:S(2)}, u32[]{:S(2)}) collective-permute-start(f32[64,1024]{1,0:T(8,128)S(1)} %broadcast_select_fusion), channel_id=1, source_target_pairs={{0,1},{1,0},{2,3},{3,2},{4,5},{5,4},{6,7},{7,6},{8,9},{9,8},{10,11... | collective-permute-start | bytes 786440 | tf_op jit(solution)/shard_map/ppermute | solution.py:249
  129.4 10.0 %collective-permute-start.45 = (f32[32,1024]{1,0:T(8,128)S(1)}, f32[32,1024]{1,0:T(8,128)S(1)}, u32[]{:S(2)}, u32[]{:S(2)}) collective-permute-start(f32[32,1024]{1,0:T(8,128)S(1)} %get-tuple-element.320), channel_id=1, source_target_pairs={{0,2},{1,3},{2,0},{3,1},{4,6},{5,7},{6,4},{7,5},{8,10},{9,11},{10,... | collective-permute-start | bytes 393224 | tf_op jit(solution)/shard_map/ppermute | solution.py:249
  (36 other events, 304.9 us)

commit v13 on v12

--- a/solution.py
+++ b/solution.py
@@ -15,10 +15,11 @@
 UNITS = tuple((chunk, (half,)) for chunk in range(CHUNKS) for half in range(CORES))
 
 ORDER = (
-    "s0", "s1", "p0", "g00", "p1", "g10", "s2", "f0", "e0", "f1", "e1", "g11", "r0", "p2",
-    "g20", "g30", "r1", "x0", "g21", "e3", "z0", "x1", "e2", "g31", "r3", "l0", "e4", "z1",
-    "r2", "e5", "x3", "r4", "l1", "e7", "z3", "x2", "r5", "e6", "z2", "x4", "l3", "r7", "x5",
-    "z4", "r6", "z5", "x7", "l4", "l2", "x6", "z7", "l5", "z6", "l7", "l6",
+    "s00", "s10", "s01", "s20", "s11", "p0", "g00", "s21", "p1", "g10", "f1", "e1", "p2",
+    "g20", "g11", "f0", "e0", "g30", "g21", "r1", "r0", "e3", "x1", "e2", "x0", "z1", "r3",
+    "g31", "e5", "r2", "z0", "e4", "x3", "l1", "r5", "e6", "z3", "x2", "r4", "l0", "e7", "z2",
+    "x5", "l3", "r6", "z5", "x4", "l2", "r7", "x6", "z4", "x7", "z6", "l5", "z7", "l4", "l7",
+    "l6",
 )
 
 SMEM = pl.BlockSpec(memory_space=pltpu.SMEM)
@@ -35,17 +36,19 @@
     z = place_ref[2]
     depth = outs[0].shape[1]
     for g, (low, high) in enumerate(bounds):
+        size = high - low
         for m in range(count):
             start = pl.multiple_of((z ^ m) * depth, depth)
-            outs[g * count + m][...] = whole_ref[low:high, pl.ds(start, depth)]
+            here = slice(m // 2 * size, (m // 2 + 1) * size)
+            outs[2 * g + m % 2][here, :] = whole_ref[low:high, pl.ds(start, depth)]
 
 
 def cut(whole, count, depth, part, place):
     bounds = [(group[0] * part, (group[-1] + 1) * part) for group in GROUPS]
     shapes = [
-        jax.ShapeDtypeStruct((high - low, depth), whole.dtype)
+        jax.ShapeDtypeStruct((count // 2 * (high - low), depth), whole.dtype)
         for low, high in bounds
-        for _ in range(count)
+        for _ in range(2)
     ]
     outs = pl.pallas_call(
         functools.partial(cut_kernel, count, bounds),
@@ -56,26 +59,27 @@
         compiler_params=pltpu.CompilerParams(vmem_limit_bytes=2**20),
         name="cut",
     )(place, whole)
-    return [outs[g * count : (g + 1) * count] for g in range(len(bounds))]
-
-
-def pack_kernel(count, part, place_ref, *refs):
+    return [outs[2 * g : 2 * g + 2] for g in range(len(bounds))]
+
+
+def pack_kernel(part, starts, place_ref, *refs):
     z = place_ref[2]
+    count = len(starts)
     for c, out in enumerate(refs[count:]):
         for m in range(count):
             rows = pl.ds(pl.multiple_of((z ^ m) * part, part), part)
-            out[rows, :] = refs[m][c * part : (c + 1) * part, :]
-
-
-def pack(blocks, part, place):
+            first = starts[m] + c * part
+            out[rows, :] = refs[m][first : first + part, :]
+
+
+def pack(blocks, starts, chunks, part, place):
     count = len(blocks)
-    rows, depth = blocks[0].shape
-    shape = jax.ShapeDtypeStruct((count * part, depth), blocks[0].dtype)
+    shape = jax.ShapeDtypeStruct((count * part, blocks[0].shape[1]), blocks[0].dtype)
     return pl.pallas_call(
-        functools.partial(pack_kernel, count, part),
+        functools.partial(pack_kernel, part, starts),
         in_specs=[SMEM] + [VMEM] * count,
-        out_specs=[VMEM] * (rows // part),
-        out_shape=[shape] * (rows // part),
+        out_specs=[VMEM] * chunks,
+        out_shape=[shape] * chunks,
         cost_estimate=SMALL,
         compiler_params=pltpu.CompilerParams(vmem_limit_bytes=2**20),
         name="pack",
@@ -265,13 +269,36 @@
     factors = {}
     state = {}
 
-    def spread_step(g):
-        sends = ordered(*pieces[g][1:])
-        mark(*sends)
-        spread[g] = [pieces[g][0]] + [along(send, n + 1) for n, send in enumerate(sends)]
+    def spread_step(g, number):
+        size = len(GROUPS[g]) * part
+        bit = narrow_bits[number]
+        if number == 0:
+            kept, send = pieces[g]
+            (send,) = ordered(send)
+            names = [(m, 0) for m in range(1, narrow_count, 2)]
+            held_now = {(m, 0): (kept, m // 2 * size) for m in range(0, narrow_count, 2)}
+        else:
+            held_now = spread[g]
+            names = [name for name in held_now if name[0] & bit]
+            taken = ordered(*[held_now[name][0] for name in names])
+            send = jnp.concatenate(
+                [
+                    value[held_now[name][1] : held_now[name][1] + size]
+                    for name, value in zip(names, taken)
+                ],
+                axis=0,
+            )
+        mark(send)
+        arrived = along(send, bit)
+        spread[g] = {name: value for name, value in held_now.items() if not name[0] & bit}
+        for n, (m, s) in enumerate(names):
+            spread[g][m ^ bit, s | bit] = (arrived, n * size)
 
     def pack_step(g):
-        packed = pack(ordered(*spread[g]), part, place)
+        blocks = [spread[g][0, s] for s in range(narrow_count)]
+        values = ordered(*[value for value, _ in blocks])
+        starts = [start for _, start in blocks]
+        packed = pack(values, starts, len(GROUPS[g]), part, place)
         mark(*packed)
         mine.update(zip(GROUPS[g], packed))
 
@@ -371,7 +398,8 @@
         for half in range(CORES):
             split_step(half)
         for g in range(len(GROUPS)):
-            spread_step(g)
+            for number in range(len(narrow_bits)):
+                spread_step(g, number)
             pack_step(g)
         for chunk in range(CHUNKS):
             for number in range(len(chip_bits)):

time: 152 us -> 152 us (level)
  local copies, waits for them, and re-layouts: 7.66 us -> 1.67 us
  waiting for transfers between devices: 43.3 us -> 48.1 us
    ppermute x25 -> x22, waiting for transfers between devices: 27.4 us -> 34.6 us  [along(): lax.ppermute(value, 'narrow', [(n, n ^ mask) for n in range(narrow_count)])]
    unnamed x37 -> x15, local copies, waits for them, and re-layouts: 7.34 us -> 1.3 us
    ppermute x25 -> x22, starting transfers between devices: 37.5 us -> 42.4 us  [along(): lax.ppermute(value, 'narrow', [(n, n ^ mask) for n in range(narrow_count)])]
    ppermute x26, starting transfers between devices: 29.4 us -> 25.2 us  [across(): lax.ppermute(value, 'wide', [(w, w ^ mask) for w in range(wide_count)])]
    ppermute x26, waiting for transfers between devices: 15.9 us -> 13.4 us  [across(): lax.ppermute(value, 'wide', [(w, w ^ mask) for w in range(wide_count)])]
  transfers between devices with their start and end apart: 51 -> 48, of which waited for: 16 -> 16; matrix products, arithmetic and copies ran while one was open for 1% -> 1% of each run, Pallas kernels for 20% -> 20%
where the time goes in v13:
time: 152 us
  starting transfers between devices  67.6 us (44%)
  waiting for transfers between devices  48.1 us (32%)
  Pallas kernels  32.4 us (21%)
  other arithmetic  1.69 us (1%)
  local copies, waits for them, and re-layouts  1.67 us (1%)
    ppermute x22, starting transfers between devices, along(): lax.ppermute(value, 'narrow', [(n, n ^ mask) for n in range(narrow_count)])  42.4 us
    ppermute x22, waiting for transfers between devices, along(): lax.ppermute(value, 'narrow', [(n, n ^ mask) for n in range(narrow_count)])  34.6 us
    ppermute x26, starting transfers between devices, across(): lax.ppermute(value, 'wide', [(w, w ^ mask) for w in range(wide_count)])  25.2 us
    pallas_call x8, Pallas kernels, product(): pl.pallas_call(functools.partial(product_kernel, count, rows, layout, tar...  19.8 us
    ppermute x26, waiting for transfers between devices, across(): lax.ppermute(value, 'wide', [(w, w ^ mask) for w in range(wide_count)])  13.4 us
    pallas_call x2, Pallas kernels, split(): pl.pallas_call(functools.partial(split_kernel, step), in_specs=[HBM], out...  8.51 us
  transfers between devices with their start and end apart: 48, of which 16 were waited for; matrix products, arithmetic and copies ran while one was open for 1% of the time, Pallas kernels for 20%

profile of v13, /device:TPU:0, one launch (start us, length us, event | category | flops | bytes accessed | tf_op | source)
XLA Modules:
  0.0 151.9 jit_solution(14221234302205220688)
XLA Ops:
  2.4 2.6 %collective-permute-start = (f32[16,2048]{1,0:T(8,128)S(1)}, f32[16,2048]{1,0:T(8,128)S(1)}, u32[]{:S(2)}, u32[]{:S(2)}) collective-permute-start(f32[16,2048]{1,0:T(8,128)S(1)} %get-tuple-element.152), channel_id=1, source_target_pairs={{0,1},{1,0},{2,3},{3,2},{4,5},{5,4},{6,7},{7,6},{8,9},{9,8},{10,11... | collective-permute-start | bytes 393224 | tf_op jit(solution)/shard_map/ppermute | solution.py:253
  5.1 4.3 %collective-permute-done.refs_1_ = f32[16,2048]{1,0:T(8,128)S(1)} collective-permute-done((f32[16,2048]{1,0:T(8,128)S(1)}, f32[16,2048]{1,0:T(8,128)S(1)}, u32[]{:S(2)}, u32[]{:S(2)}) %collective-permute-start) | collective-permute-done | bytes 131104 | tf_op jit(solution)/shard_map/ppermute | solution.py:253
  11.4 2.6 %collective-permute-start.1 = (f32[16,2048]{1,0:T(8,128)S(1)}, f32[16,2048]{1,0:T(8,128)S(1)}, u32[]{:S(2)}, u32[]{:S(2)}) collective-permute-start(f32[16,2048]{1,0:T(8,128)S(1)} %pad_maximum_fusion.1), channel_id=1, source_target_pairs={{0,2},{1,3},{2,0},{3,1},{4,6},{5,7},{6,4},{7,5},{8,10},{9,11},{10,... | collective-permute-start | bytes 393224 | tf_op jit(solution)/shard_map/ppermute | solution.py:253
  14.0 5.7 %collective-permute-done.1.refs_2_.refs_3_ = f32[16,2048]{1,0:T(8,128)S(1)} collective-permute-done((f32[16,2048]{1,0:T(8,128)S(1)}, f32[16,2048]{1,0:T(8,128)S(1)}, u32[]{:S(2)}, u32[]{:S(2)}) %collective-permute-start.1) | collective-permute-done | bytes 131104 | tf_op jit(solution)/shard_map/ppermute | solution.py:253
  20.3 2.5 %collective-permute-start.3 = (f32[32,2048]{1,0:T(8,128)S(1)}, f32[32,2048]{1,0:T(8,128)S(1)}, u32[]{:S(2)}, u32[]{:S(2)}) collective-permute-start(f32[32,2048]{1,0:T(8,128)S(1)} %pack.3.refs_0_), channel_id=1, source_target_pairs={{0,24},{4,28},{8,16},{12,20},{16,8},{20,12},{24,0},{28,4},{1,25},{... | collective-permute-start | bytes 786440 | tf_op jit(solution)/shard_map/ppermute | solution.py:247
  23.8 3.4 %collective-permute-start.6 = (f32[16,2048]{1,0:T(8,128)S(1)}, f32[16,2048]{1,0:T(8,128)S(1)}, u32[]{:S(2)}, u32[]{:S(2)}) collective-permute-start(f32[16,2048]{1,0:T(8,128)S(1)} %pad_maximum_fusion.2), channel_id=1, source_target_pairs={{0,2},{1,3},{2,0},{3,1},{4,6},{5,7},{6,4},{7,5},{8,10},{9,11},{10,... | collective-permute-start | bytes 393224 | tf_op jit(solution)/shard_map/ppermute | solution.py:253
  27.3 3.7 %collective-permute-done.6.refs_2_.refs_3_ = f32[16,2048]{1,0:T(8,128)S(1)} collective-permute-done((f32[16,2048]{1,0:T(8,128)S(1)}, f32[16,2048]{1,0:T(8,128)S(1)}, u32[]{:S(2)}, u32[]{:S(2)}) %collective-permute-start.6) | collective-permute-done | bytes 131104 | tf_op jit(solution)/shard_map/ppermute | solution.py:253
  31.0 2.2 %collective-permute-start.9 = (f32[32,2048]{1,0:T(8,128)S(1)}, f32[32,2048]{1,0:T(8,128)S(1)}, u32[]{:S(2)}, u32[]{:S(2)}) collective-permute-start(f32[32,2048]{1,0:T(8,128)S(1)} %pad_maximum_fusion), channel_id=1, source_target_pairs={{0,2},{1,3},{2,0},{3,1},{4,6},{5,7},{6,4},{7,5},{8,10},{9,11},{10,... | collective-permute-start | bytes 786440 | tf_op jit(solution)/shard_map/ppermute | solution.py:253
  35.3 4.3 %split.2 = (bf16[2048,1024]{1,0:T(8,128)(2,1)S(1)}, bf16[2048,1024]{1,0:T(8,128)(2,1)S(1)}, f32[8,128]{1,0:T(8,128)}) custom-call(f32[2048,1024]{1,0:T(8,128)} %collective-permute-done.10.whole_ref), custom_call_target="tpu_custom_call" | custom-call | flops 1 | bytes 1 | tf_op jit(solution)/shard_map/split/pallas_call | solution.py:117
  39.6 2.5 %product.8 = (f32[64,1024]{1,0:T(8,128)S(1)}, f32[64,1024]{1,0:T(8,128)S(1)}) custom-call(s32[3]{0:T(128)S(1)} %pad_add_fusion.place_ref, s32[8,64]{1,0:T(8,128)S(1)} %copy-done.3, s32[8]{0:T(128)S(1)} %copy-done.4, f32[32,2048]{1,0:T(8,128)S(1)} %pack.3.refs_0_, f32[32,2048]{1,0:T(8,128)S(1)} %collective-permute-done.3.refs_1_, ...), custom_call_target="tpu_custom_call" | custom-call | flops 3221225472 | bytes 1 | tf_op jit(solution)/shard_map/product/pallas_call | solution.py:178
  45.9 4.3 %split.3 = (bf16[2048,1024]{1,0:T(8,128)(2,1)S(1)}, bf16[2048,1024]{1,0:T(8,128)(2,1)S(1)}, f32[8,128]{1,0:T(8,128)}) custom-call(f32[2048,1024]{1,0:T(8,128)} %whole_ref.2), custom_call_target="tpu_custom_call" | custom-call | flops 1 | bytes 1 | tf_op jit(solution)/shard_map/split/pallas_call | solution.py:117
  50.2 2.4 %product.9 = (f32[64,1024]{1,0:T(8,128)S(1)}, f32[64,1024]{1,0:T(8,128)S(1)}) custom-call(s32[3]{0:T(128)S(1)} %pad_add_fusion.place_ref, s32[8,64]{1,0:T(8,128)S(1)} %copy-done.3, s32[8]{0:T(128)S(1)} %copy-done.4, f32[32,2048]{1,0:T(8,128)S(1)} %pack.3.refs_0_, f32[32,2048]{1,0:T(8,128)S(1)} %collective-permute-done.3.refs_1_, ...), custom_call_target="tpu_custom_call" | custom-call | flops 3221225472 | bytes 1 | tf_op jit(solution)/shard_map/product/pallas_call | solution.py:178
  56.9 4.4 %collective-permute-start.16 = (f32[64,1024]{1,0:T(8,128)S(1)}, f32[64,1024]{1,0:T(8,128)S(1)}, u32[]{:S(2)}, u32[]{:S(2)}) collective-permute-start(f32[64,1024]{1,0:T(8,128)S(1)} %broadcast_select_fusion.7), channel_id=1, source_target_pairs={{0,1},{1,0},{2,3},{3,2},{4,5},{5,4},{6,7},{7,6},{8,9},{9,8},{10,11... | collective-permute-start | bytes 786440 | tf_op jit(solution)/shard_map/ppermute | solution.py:253
  61.9 3.7 %collective-permute-start.14 = (f32[64,1024]{1,0:T(8,128)S(1)}, f32[64,1024]{1,0:T(8,128)S(1)}, u32[]{:S(2)}, u32[]{:S(2)}) collective-permute-start(f32[64,1024]{1,0:T(8,128)S(1)} %broadcast_select_fusion.6), channel_id=1, source_target_pairs={{0,1},{1,0},{2,3},{3,2},{4,5},{5,4},{6,7},{7,6},{8,9},{9,8},{10,11... | collective-permute-start | bytes 786440 | tf_op jit(solution)/shard_map/ppermute | solution.py:253
  65.6 2.5 %collective-permute-done.15.refs_2_ = f32[64,2048]{1,0:T(8,128)S(1)} collective-permute-done((f32[64,2048]{1,0:T(8,128)S(1)}, f32[64,2048]{1,0:T(8,128)S(1)}, u32[]{:S(2)}, u32[]{:S(2)}) %collective-permute-start.15) | collective-permute-done | bytes 524320 | tf_op jit(solution)/shard_map/ppermute | solution.py:247
  68.1 2.5 %product.10 = (f32[64,1024]{1,0:T(8,128)S(1)}, f32[64,1024]{1,0:T(8,128)S(1)}) custom-call(s32[3]{0:T(128)S(1)} %pad_add_fusion.place_ref, s32[8,64]{1,0:T(8,128)S(1)} %copy-done.3, s32[8]{0:T(128)S(1)} %copy-done.4, f32[32,2048]{1,0:T(8,128)S(1)} %pack.4.refs_0_, f32[32,2048]{1,0:T(8,128)S(1)} %collective-permute-done.8.refs_1_, ...), custom_call_target="tpu_custom_call" | custom-call | flops 3221225472 | bytes 1 | tf_op jit(solution)/shard_map/product/pallas_call | solution.py:178
  73.8 2.4 %product.11 = (f32[64,1024]{1,0:T(8,128)S(1)}, f32[64,1024]{1,0:T(8,128)S(1)}) custom-call(s32[3]{0:T(128)S(1)} %pad_add_fusion.place_ref, s32[8,64]{1,0:T(8,128)S(1)} %copy-done.3, s32[8]{0:T(128)S(1)} %copy-done.4, f32[32,2048]{1,0:T(8,128)S(1)} %pack.4.refs_0_, f32[32,2048]{1,0:T(8,128)S(1)} %collective-permute-done.8.refs_1_, ...), custom_call_target="tpu_custom_call" | custom-call | flops 3221225472 | bytes 1 | tf_op jit(solution)/shard_map/product/pallas_call | solution.py:178
  76.9 2.9 %collective-permute-done.22 = f32[32,1024]{1,0:T(8,128)S(1)} collective-permute-done((f32[32,1024]{1,0:T(8,128)S(1)}, f32[32,1024]{1,0:T(8,128)S(1)}, u32[]{:S(2)}, u32[]{:S(2)}) %collective-permute-start.22) | collective-permute-done | bytes 131104 | tf_op jit(solution)/shard_map/ppermute | solution.py:247
  81.3 2.8 %collective-permute-start.30 = (f32[32,1024]{1,0:T(8,128)S(1)}, f32[32,1024]{1,0:T(8,128)S(1)}, u32[]{:S(2)}, u32[]{:S(2)}) collective-permute-start(f32[32,1024]{1,0:T(8,128)S(1)} %get-tuple-element.320), channel_id=1, source_target_pairs={{0,2},{1,3},{2,0},{3,1},{4,6},{5,7},{6,4},{7,5},{8,10},{9,11},{10,... | collective-permute-start | bytes 393224 | tf_op jit(solution)/shard_map/ppermute | solution.py:253
  84.7 2.7 %product.12 = (f32[64,1024]{1,0:T(8,128)S(1)}, f32[64,1024]{1,0:T(8,128)S(1)}) custom-call(s32[3]{0:T(128)S(1)} %pad_add_fusion.place_ref, s32[8,64]{1,0:T(8,128)S(1)} %copy-done.3, s32[8]{0:T(128)S(1)} %copy-done.4, f32[32,2048]{1,0:T(8,128)S(1)} %get-tuple-element.237.refs_0_, f32[32,2048]{1,0:T(8,128)S(1)} %collective-permute-done.13.refs_1_, ...), custom_call_target="tpu_custom_call" | custom-call | flops 3221225472 | bytes 1 | tf_op jit(solution)/shard_map/product/pallas_call | solution.py:178
  90.1 2.4 %product.13 = (f32[64,1024]{1,0:T(8,128)S(1)}, f32[64,1024]{1,0:T(8,128)S(1)}) custom-call(s32[3]{0:T(128)S(1)} %pad_add_fusion.place_ref, s32[8,64]{1,0:T(8,128)S(1)} %copy-done.3, s32[8]{0:T(128)S(1)} %copy-done.4, f32[32,2048]{1,0:T(8,128)S(1)} %get-tuple-element.237.refs_0_, f32[32,2048]{1,0:T(8,128)S(1)} %collective-permute-done.13.refs_1_, ...), custom_call_target="tpu_custom_call" | custom-call | flops 3221225472 | bytes 1 | tf_op jit(solution)/shard_map/product/pallas_call | solution.py:178
  92.5 2.4 %collective-permute-done.26 = f32[64,1024]{1,0:T(8,128)S(1)} collective-permute-done((f32[64,1024]{1,0:T(8,128)S(1)}, f32[64,1024]{1,0:T(8,128)S(1)}, u32[]{:S(2)}, u32[]{:S(2)}) %collective-permute-start.26) | collective-permute-done | bytes 262176 | tf_op jit(solution)/shard_map/ppermute | solution.py:253
  97.7 2.1 %collective-permute-start.34 = (f32[64,1024]{1,0:T(8,128)S(1)}, f32[64,1024]{1,0:T(8,128)S(1)}, u32[]{:S(2)}, u32[]{:S(2)}) collective-permute-start(f32[64,1024]{1,0:T(8,128)S(1)} %broadcast_select_fusion.3), channel_id=1, source_target_pairs={{0,1},{1,0},{2,3},{3,2},{4,5},{5,4},{6,7},{7,6},{8,9},{9,8},{10,11... | collective-permute-start | bytes 786440 | tf_op jit(solution)/shard_map/ppermute | solution.py:253
  99.9 2.4 %product.14 = (f32[64,1024]{1,0:T(8,128)S(1)}, f32[64,1024]{1,0:T(8,128)S(1)}) custom-call(s32[3]{0:T(128)S(1)} %pad_add_fusion.place_ref, s32[8,64]{1,0:T(8,128)S(1)} %copy-done.3, s32[8]{0:T(128)S(1)} %copy-done.4, f32[32,2048]{1,0:T(8,128)S(1)} %get-tuple-element.261.refs_0_, f32[32,2048]{1,0:T(8,128)S(1)} %collective-permute-done.20.refs_1_, ...), custom_call_target="tpu_custom_call" | custom-call | flops 3221225472 | bytes 1 | tf_op jit(solution)/shard_map/product/pallas_call | solution.py:178
  102.5 2.4 %collective-permute-start.37 = (f32[32,1024]{1,0:T(8,128)S(1)}, f32[32,1024]{1,0:T(8,128)S(1)}, u32[]{:S(2)}, u32[]{:S(2)}) collective-permute-start(f32[32,1024]{1,0:T(8,128)S(1)} %get-tuple-element.312), channel_id=1, source_target_pairs={{0,2},{1,3},{2,0},{3,1},{4,6},{5,7},{6,4},{7,5},{8,10},{9,11},{10,... | collective-permute-start | bytes 393224 | tf_op jit(solution)/shard_map/ppermute | solution.py:253
  107.0 2.5 %product.15 = (f32[64,1024]{1,0:T(8,128)S(1)}, f32[64,1024]{1,0:T(8,128)S(1)}) custom-call(s32[3]{0:T(128)S(1)} %pad_add_fusion.place_ref, s32[8,64]{1,0:T(8,128)S(1)} %copy-done.3, s32[8]{0:T(128)S(1)} %copy-done.4, f32[32,2048]{1,0:T(8,128)S(1)} %get-tuple-element.261.refs_0_, f32[32,2048]{1,0:T(8,128)S(1)} %collective-permute-done.20.refs_1_, ...), custom_call_target="tpu_custom_call" | custom-call | flops 3221225472 | bytes 1 | tf_op jit(solution)/shard_map/product/pallas_call | solution.py:178
  112.6 2.8 %collective-permute-start.39 = (f32[64,1024]{1,0:T(8,128)S(1)}, f32[64,1024]{1,0:T(8,128)S(1)}, u32[]{:S(2)}, u32[]{:S(2)}) collective-permute-start(f32[64,1024]{1,0:T(8,128)S(1)} %broadcast_select_fusion.1), channel_id=1, source_target_pairs={{0,1},{1,0},{2,3},{3,2},{4,5},{5,4},{6,7},{7,6},{8,9},{9,8},{10,11... | collective-permute-start | bytes 786440 | tf_op jit(solution)/shard_map/ppermute | solution.py:253
  115.4 2.8 %collective-permute-done.35 = f32[32,1024]{1,0:T(8,128)S(1)} collective-permute-done((f32[32,1024]{1,0:T(8,128)S(1)}, f32[32,1024]{1,0:T(8,128)S(1)}, u32[]{:S(2)}, u32[]{:S(2)}) %collective-permute-start.35) | collective-permute-done | bytes 131104 | tf_op jit(solution)/shard_map/ppermute | solution.py:247
  122.5 5.4 %collective-permute-done.39 = f32[64,1024]{1,0:T(8,128)S(1)} collective-permute-done((f32[64,1024]{1,0:T(8,128)S(1)}, f32[64,1024]{1,0:T(8,128)S(1)}, u32[]{:S(2)}, u32[]{:S(2)}) %collective-permute-start.39) | collective-permute-done | bytes 262176 | tf_op jit(solution)/shard_map/ppermute | solution.py:253
  129.1 2.7 %collective-permute-done.42 = f32[64,1024]{1,0:T(8,128)S(1)} collective-permute-done((f32[64,1024]{1,0:T(8,128)S(1)}, f32[64,1024]{1,0:T(8,128)S(1)}, u32[]{:S(2)}, u32[]{:S(2)}) %collective-permute-start.42) | collective-permute-done | bytes 262176 | tf_op jit(solution)/shard_map/ppermute | solution.py:253
  133.1 3.9 %collective-permute-done.43 = f32[32,1024]{1,0:T(8,128)S(1)} collective-permute-done((f32[32,1024]{1,0:T(8,128)S(1)}, f32[32,1024]{1,0:T(8,128)S(1)}, u32[]{:S(2)}, u32[]{:S(2)}) %collective-permute-start.43) | collective-permute-done | bytes 131104 | tf_op jit(solution)/shard_map/ppermute | solution.py:247
  140.7 8.0 %collective-permute-done.47.refs_15_ = f32[32,1024]{1,0:T(8,128)S(1)} collective-permute-done((f32[32,1024]{1,0:T(8,128)}, f32[32,1024]{1,0:T(8,128)S(1)}, u32[]{:S(2)}, u32[]{:S(2)}) %collective-permute-start.47) | collective-permute-done | bytes 131104 | tf_op jit(solution)/shard_map/ppermute | solution.py:253
  (140 shorter events, 47.5 us)
Async XLA Ops:
  0.0 35.3 %collective-permute-start.10 = (f32[2048,1024]{1,0:T(8,128)}, f32[2048,1024]{1,0:T(8,128)}, u32[]{:S(2)}, u32[]{:S(2)}) collective-permute-start(f32[2048,1024]{1,0:T(8,128)} %whole_ref.2), channel_id=1, source_target_pairs={{0,4},{4,0},{8,12},{12,8},{16,20},{20,16},{24,28},{28,24},{1,5},{5... | collective-permute-start | bytes 25165832 | tf_op jit(solution)/shard_map/ppermute | solution.py:247
  9.4 14.4 %collective-permute-start.7 = (f32[32,2048]{1,0:T(8,128)S(1)}, f32[32,2048]{1,0:T(8,128)S(1)}, u32[]{:S(2)}, u32[]{:S(2)}) collective-permute-start(f32[32,2048]{1,0:T(8,128)S(1)} %get-tuple-element.159), channel_id=1, source_target_pairs={{0,1},{1,0},{2,3},{3,2},{4,5},{5,4},{6,7},{7,6},{8,9},{9,8},{10,11... | collective-permute-start | bytes 786440 | tf_op jit(solution)/shard_map/ppermute | solution.py:253
  20.3 13.5 %collective-permute-start.3 = (f32[32,2048]{1,0:T(8,128)S(1)}, f32[32,2048]{1,0:T(8,128)S(1)}, u32[]{:S(2)}, u32[]{:S(2)}) collective-permute-start(f32[32,2048]{1,0:T(8,128)S(1)} %pack.3.refs_0_), channel_id=1, source_target_pairs={{0,24},{4,28},{8,16},{12,20},{16,8},{20,12},{24,0},{28,4},{1,25},{... | collective-permute-start | bytes 786440 | tf_op jit(solution)/shard_map/ppermute | solution.py:247
  22.8 12.6 %collective-permute-start.4 = (f32[32,2048]{1,0:T(8,128)S(1)}, f32[32,2048]{1,0:T(8,128)S(1)}, u32[]{:S(2)}, u32[]{:S(2)}) collective-permute-start(f32[32,2048]{1,0:T(8,128)S(1)} %pack.3.refs_0_), channel_id=1, source_target_pairs={{0,8},{4,12},{8,0},{12,4},{16,24},{20,28},{24,16},{28,20},{1,9},{5... | collective-permute-start | bytes 786440 | tf_op jit(solution)/shard_map/ppermute | solution.py:247
  23.3 12.0 %collective-permute-start.5 = (f32[32,2048]{1,0:T(8,128)S(1)}, f32[32,2048]{1,0:T(8,128)S(1)}, u32[]{:S(2)}, u32[]{:S(2)}) collective-permute-start(f32[32,2048]{1,0:T(8,128)S(1)} %pack.3.refs_0_), channel_id=1, source_target_pairs={{0,16},{4,20},{8,24},{12,28},{16,0},{20,4},{24,8},{28,12},{1,17},{... | collective-permute-start | bytes 786440 | tf_op jit(solution)/shard_map/ppermute | solution.py:247
  31.0 12.7 %collective-permute-start.9 = (f32[32,2048]{1,0:T(8,128)S(1)}, f32[32,2048]{1,0:T(8,128)S(1)}, u32[]{:S(2)}, u32[]{:S(2)}) collective-permute-start(f32[32,2048]{1,0:T(8,128)S(1)} %pad_maximum_fusion), channel_id=1, source_target_pairs={{0,2},{1,3},{2,0},{3,1},{4,6},{5,7},{6,4},{7,5},{8,10},{9,11},{10,... | collective-permute-start | bytes 786440 | tf_op jit(solution)/shard_map/ppermute | solution.py:253
  33.8 12.1 %collective-permute-start.8 = (f32[32,2048]{1,0:T(8,128)S(1)}, f32[32,2048]{1,0:T(8,128)S(1)}, u32[]{:S(2)}, u32[]{:S(2)}) collective-permute-start(f32[32,2048]{1,0:T(8,128)S(1)} %pack.4.refs_0_), channel_id=1, source_target_pairs={{0,8},{4,12},{8,0},{12,4},{16,24},{20,28},{24,16},{28,20},{1,9},{5... | collective-permute-start | bytes 786440 | tf_op jit(solution)/shard_map/ppermute | solution.py:247
  42.1 14.7 %collective-permute-start.12 = (f32[64,1024]{1,0:T(8,128)S(1)}, f32[64,1024]{1,0:T(8,128)S(1)}, u32[]{:S(2)}, u32[]{:S(2)}) collective-permute-start(f32[64,1024]{1,0:T(8,128)S(1)} %get-tuple-element.184), channel_id=1, source_target_pairs={{0,8},{4,12},{8,0},{12,4},{16,24},{20,28},{24,16},{28,20},{1,9},{5... | collective-permute-start | bytes 786440 | tf_op jit(solution)/shard_map/ppermute | solution.py:247
  44.3 11.9 %collective-permute-start.13 = (f32[32,2048]{1,0:T(8,128)S(1)}, f32[32,2048]{1,0:T(8,128)S(1)}, u32[]{:S(2)}, u32[]{:S(2)}) collective-permute-start(f32[32,2048]{1,0:T(8,128)S(1)} %get-tuple-element.237.refs_0_), channel_id=1, source_target_pairs={{0,8},{4,12},{8,0},{12,4},{16,24},{20,28},{24,16},{28,20},{1,9},{5... | collective-permute-start | bytes 786440 | tf_op jit(solution)/shard_map/ppermute | solution.py:247
  53.2 14.9 %collective-permute-start.15 = (f32[64,2048]{1,0:T(8,128)S(1)}, f32[64,2048]{1,0:T(8,128)S(1)}, u32[]{:S(2)}, u32[]{:S(2)}) collective-permute-start(f32[64,2048]{1,0:T(8,128)S(1)} %constant_dynamic-update-slice_fusion), channel_id=1, source_target_pairs={{0,16},{4,20},{8,24},{12,28},{16,0},{20,4},{24,8},{28,12},{1,17},{... | collective-permute-start | bytes 1572872 | tf_op jit(solution)/shard_map/ppermute | solution.py:247
  54.7 29.4 %collective-permute-start.20 = (f32[32,2048]{1,0:T(8,128)S(1)}, f32[32,2048]{1,0:T(8,128)S(1)}, u32[]{:S(2)}, u32[]{:S(2)}) collective-permute-start(f32[32,2048]{1,0:T(8,128)S(1)} %get-tuple-element.261.refs_0_), channel_id=1, source_target_pairs={{0,8},{4,12},{8,0},{12,4},{16,24},{20,28},{24,16},{28,20},{1,9},{5... | collective-permute-start | bytes 786440 | tf_op jit(solution)/shard_map/ppermute | solution.py:247
  56.3 28.0 %collective-permute-start.19 = (f32[64,2048]{1,0:T(8,128)S(1)}, f32[64,2048]{1,0:T(8,128)S(1)}, u32[]{:S(2)}, u32[]{:S(2)}) collective-permute-start(f32[64,2048]{1,0:T(8,128)S(1)} %constant_dynamic-update-slice_fusion.2), channel_id=1, source_target_pairs={{0,16},{4,20},{8,24},{12,28},{16,0},{20,4},{24,8},{28,12},{1,17},{... | collective-permute-start | bytes 1572872 | tf_op jit(solution)/shard_map/ppermute | solution.py:247
  56.9 15.2 %collective-permute-start.16 = (f32[64,1024]{1,0:T(8,128)S(1)}, f32[64,1024]{1,0:T(8,128)S(1)}, u32[]{:S(2)}, u32[]{:S(2)}) collective-permute-start(f32[64,1024]{1,0:T(8,128)S(1)} %broadcast_select_fusion.7), channel_id=1, source_target_pairs={{0,1},{1,0},{2,3},{3,2},{4,5},{5,4},{6,7},{7,6},{8,9},{9,8},{10,11... | collective-permute-start | bytes 786440 | tf_op jit(solution)/shard_map/ppermute | solution.py:253
  61.9 14.3 %collective-permute-start.14 = (f32[64,1024]{1,0:T(8,128)S(1)}, f32[64,1024]{1,0:T(8,128)S(1)}, u32[]{:S(2)}, u32[]{:S(2)}) collective-permute-start(f32[64,1024]{1,0:T(8,128)S(1)} %broadcast_select_fusion.6), channel_id=1, source_target_pairs={{0,1},{1,0},{2,3},{3,2},{4,5},{5,4},{6,7},{7,6},{8,9},{9,8},{10,11... | collective-permute-start | bytes 786440 | tf_op jit(solution)/shard_map/ppermute | solution.py:253
  70.6 10.7 %collective-permute-start.21 = (f32[64,1024]{1,0:T(8,128)S(1)}, f32[64,1024]{1,0:T(8,128)S(1)}, u32[]{:S(2)}, u32[]{:S(2)}) collective-permute-start(f32[64,1024]{1,0:T(8,128)S(1)} %get-tuple-element.212), channel_id=1, source_target_pairs={{0,8},{4,12},{8,0},{12,4},{16,24},{20,28},{24,16},{28,20},{1,9},{5... | collective-permute-start | bytes 786440 | tf_op jit(solution)/shard_map/ppermute | solution.py:247
  76.2 11.1 %collective-permute-start.18 = (f32[64,1024]{1,0:T(8,128)S(1)}, f32[64,1024]{1,0:T(8,128)S(1)}, u32[]{:S(2)}, u32[]{:S(2)}) collective-permute-start(f32[64,1024]{1,0:T(8,128)S(1)} %get-tuple-element.219), channel_id=1, source_target_pairs={{0,8},{4,12},{8,0},{12,4},{16,24},{20,28},{24,16},{28,20},{1,9},{5... | collective-permute-start | bytes 786440 | tf_op jit(solution)/shard_map/ppermute | solution.py:247
  81.3 14.7 %collective-permute-start.30 = (f32[32,1024]{1,0:T(8,128)S(1)}, f32[32,1024]{1,0:T(8,128)S(1)}, u32[]{:S(2)}, u32[]{:S(2)}) collective-permute-start(f32[32,1024]{1,0:T(8,128)S(1)} %get-tuple-element.320), channel_id=1, source_target_pairs={{0,2},{1,3},{2,0},{3,1},{4,6},{5,7},{6,4},{7,5},{8,10},{9,11},{10,... | collective-permute-start | bytes 393224 | tf_op jit(solution)/shard_map/ppermute | solution.py:253
  84.2 10.7 %collective-permute-start.26 = (f32[64,1024]{1,0:T(8,128)S(1)}, f32[64,1024]{1,0:T(8,128)S(1)}, u32[]{:S(2)}, u32[]{:S(2)}) collective-permute-start(f32[64,1024]{1,0:T(8,128)S(1)} %broadcast_select_fusion.5), channel_id=1, source_target_pairs={{0,1},{1,0},{2,3},{3,2},{4,5},{5,4},{6,7},{7,6},{8,9},{9,8},{10,11... | collective-permute-start | bytes 786440 | tf_op jit(solution)/shard_map/ppermute | solution.py:253
  84.3 15.6 %collective-permute-start.28 = (f32[64,2048]{1,0:T(8,128)S(1)}, f32[64,2048]{1,0:T(8,128)S(1)}, u32[]{:S(2)}, u32[]{:S(2)}) collective-permute-start(f32[64,2048]{1,0:T(8,128)S(1)} %constant_dynamic-update-slice_fusion.4), channel_id=1, source_target_pairs={{0,16},{4,20},{8,24},{12,28},{16,0},{20,4},{24,8},{28,12},{1,17},{... | collective-permute-start | bytes 1572872 | tf_op jit(solution)/shard_map/ppermute | solution.py:247
  94.9 10.0 %collective-permute-start.24 = (f32[64,1024]{1,0:T(8,128)S(1)}, f32[64,1024]{1,0:T(8,128)S(1)}, u32[]{:S(2)}, u32[]{:S(2)}) collective-permute-start(f32[64,1024]{1,0:T(8,128)S(1)} %get-tuple-element.242), channel_id=1, source_target_pairs={{0,8},{4,12},{8,0},{12,4},{16,24},{20,28},{24,16},{28,20},{1,9},{5... | collective-permute-start | bytes 786440 | tf_op jit(solution)/shard_map/ppermute | solution.py:247
  96.0 10.1 %collective-permute-start.23 = (f32[32,1024]{1,0:T(8,128)S(1)}, f32[32,1024]{1,0:T(8,128)S(1)}, u32[]{:S(2)}, u32[]{:S(2)}) collective-permute-start(f32[32,1024]{1,0:T(8,128)S(1)} %get-tuple-element.323), channel_id=1, source_target_pairs={{0,2},{1,3},{2,0},{3,1},{4,6},{5,7},{6,4},{7,5},{8,10},{9,11},{10,... | collective-permute-start | bytes 393224 | tf_op jit(solution)/shard_map/ppermute | solution.py:253
  97.7 11.8 %collective-permute-start.34 = (f32[64,1024]{1,0:T(8,128)S(1)}, f32[64,1024]{1,0:T(8,128)S(1)}, u32[]{:S(2)}, u32[]{:S(2)}) collective-permute-start(f32[64,1024]{1,0:T(8,128)S(1)} %broadcast_select_fusion.3), channel_id=1, source_target_pairs={{0,1},{1,0},{2,3},{3,2},{4,5},{5,4},{6,7},{7,6},{8,9},{9,8},{10,11... | collective-permute-start | bytes 786440 | tf_op jit(solution)/shard_map/ppermute | solution.py:253
  102.3 10.2 %collective-permute-start.36 = (f32[64,1024]{1,0:T(8,128)S(1)}, f32[64,1024]{1,0:T(8,128)S(1)}, u32[]{:S(2)}, u32[]{:S(2)}) collective-permute-start(f32[64,1024]{1,0:T(8,128)S(1)} %get-tuple-element.252), channel_id=1, source_target_pairs={{0,8},{4,12},{8,0},{12,4},{16,24},{20,28},{24,16},{28,20},{1,9},{5... | collective-permute-start | bytes 786440 | tf_op jit(solution)/shard_map/ppermute | solution.py:247
  106.0 13.8 %collective-permute-start.33 = (f32[64,1024]{1,0:T(8,128)S(1)}, f32[64,1024]{1,0:T(8,128)S(1)}, u32[]{:S(2)}, u32[]{:S(2)}) collective-permute-start(f32[64,1024]{1,0:T(8,128)S(1)} %broadcast_select_fusion.2), channel_id=1, source_target_pairs={{0,1},{1,0},{2,3},{3,2},{4,5},{5,4},{6,7},{7,6},{8,9},{9,8},{10,11... | collective-permute-start | bytes 786440 | tf_op jit(solution)/shard_map/ppermute | solution.py:253
  109.5 11.5 %collective-permute-start.40 = (f32[64,1024]{1,0:T(8,128)S(1)}, f32[64,1024]{1,0:T(8,128)S(1)}, u32[]{:S(2)}, u32[]{:S(2)}) collective-permute-start(f32[64,1024]{1,0:T(8,128)S(1)} %get-tuple-element.266), channel_id=1, source_target_pairs={{0,8},{4,12},{8,0},{12,4},{16,24},{20,28},{24,16},{28,20},{1,9},{5... | collective-permute-start | bytes 786440 | tf_op jit(solution)/shard_map/ppermute | solution.py:247
  110.8 10.3 %collective-permute-start.32 = (f32[32,1024]{1,0:T(8,128)S(1)}, f32[32,1024]{1,0:T(8,128)S(1)}, u32[]{:S(2)}, u32[]{:S(2)}) collective-permute-start(f32[32,1024]{1,0:T(8,128)S(1)} %get-tuple-element.315), channel_id=1, source_target_pairs={{0,2},{1,3},{2,0},{3,1},{4,6},{5,7},{6,4},{7,5},{8,10},{9,11},{10,... | collective-permute-start | bytes 393224 | tf_op jit(solution)/shard_map/ppermute | solution.py:253
  112.6 15.3 %collective-permute-start.39 = (f32[64,1024]{1,0:T(8,128)S(1)}, f32[64,1024]{1,0:T(8,128)S(1)}, u32[]{:S(2)}, u32[]{:S(2)}) collective-permute-start(f32[64,1024]{1,0:T(8,128)S(1)} %broadcast_select_fusion.1), channel_id=1, source_target_pairs={{0,1},{1,0},{2,3},{3,2},{4,5},{5,4},{6,7},{7,6},{8,9},{9,8},{10,11... | collective-permute-start | bytes 786440 | tf_op jit(solution)/shard_map/ppermute | solution.py:253
  118.3 14.8 %collective-permute-start.44 = (f32[32,1024]{1,0:T(8,128)S(1)}, f32[32,1024]{1,0:T(8,128)S(1)}, u32[]{:S(2)}, u32[]{:S(2)}) collective-permute-start(f32[32,1024]{1,0:T(8,128)S(1)} %get-tuple-element.304), channel_id=1, source_target_pairs={{0,2},{1,3},{2,0},{3,1},{4,6},{5,7},{6,4},{7,5},{8,10},{9,11},{10,... | collective-permute-start | bytes 393224 | tf_op jit(solution)/shard_map/ppermute | solution.py:253
  121.1 10.8 %collective-permute-start.42 = (f32[64,1024]{1,0:T(8,128)S(1)}, f32[64,1024]{1,0:T(8,128)S(1)}, u32[]{:S(2)}, u32[]{:S(2)}) collective-permute-start(f32[64,1024]{1,0:T(8,128)S(1)} %broadcast_select_fusion), channel_id=1, source_target_pairs={{0,1},{1,0},{2,3},{3,2},{4,5},{5,4},{6,7},{7,6},{8,9},{9,8},{10,11... | collective-permute-start | bytes 786440 | tf_op jit(solution)/shard_map/ppermute | solution.py:253
  128.1 12.6 %collective-permute-start.41 = (f32[32,1024]{1,0:T(8,128)S(1)}, f32[32,1024]{1,0:T(8,128)S(1)}, u32[]{:S(2)}, u32[]{:S(2)}) collective-permute-start(f32[32,1024]{1,0:T(8,128)S(1)} %get-tuple-element.307), channel_id=1, source_target_pairs={{0,2},{1,3},{2,0},{3,1},{4,6},{5,7},{6,4},{7,5},{8,10},{9,11},{10,... | collective-permute-start | bytes 393224 | tf_op jit(solution)/shard_map/ppermute | solution.py:253
  137.6 11.0 %collective-permute-start.47 = (f32[32,1024]{1,0:T(8,128)}, f32[32,1024]{1,0:T(8,128)S(1)}, u32[]{:S(2)}, u32[]{:S(2)}) collective-permute-start(f32[32,1024]{1,0:T(8,128)} %get-tuple-element.298), channel_id=1, source_target_pairs={{0,2},{1,3},{2,0},{3,1},{4,6},{5,7},{6,4},{7,5},{8,10},{9,11},{10,... | collective-permute-start | bytes 393224 | tf_op jit(solution)/shard_map/ppermute | solution.py:253
  139.5 10.7 %collective-permute-start.46 = (f32[32,1024]{1,0:T(8,128)S(1)}, f32[32,1024]{1,0:T(8,128)S(1)}, u32[]{:S(2)}, u32[]{:S(2)}) collective-permute-start(f32[32,1024]{1,0:T(8,128)S(1)} %get-tuple-element.300), channel_id=1, source_target_pairs={{0,2},{1,3},{2,0},{3,1},{4,6},{5,7},{6,4},{7,5},{8,10},{9,11},{10,... | collective-permute-start | bytes 393224 | tf_op jit(solution)/shard_map/ppermute | solution.py:253
  (22 other events, 237.4 us)

commit v14 on v13

--- a/solution.py
+++ b/solution.py
@@ -15,11 +15,11 @@
 UNITS = tuple((chunk, (half,)) for chunk in range(CHUNKS) for half in range(CORES))
 
 ORDER = (
-    "s00", "s10", "s01", "s20", "s11", "p0", "g00", "s21", "p1", "g10", "f1", "e1", "p2",
-    "g20", "g11", "f0", "e0", "g30", "g21", "r1", "r0", "e3", "x1", "e2", "x0", "z1", "r3",
-    "g31", "e5", "r2", "z0", "e4", "x3", "l1", "r5", "e6", "z3", "x2", "r4", "l0", "e7", "z2",
-    "x5", "l3", "r6", "z5", "x4", "l2", "r7", "x6", "z4", "x7", "z6", "l5", "z7", "l4", "l7",
-    "l6",
+    "s00", "s10", "s01", "s11", "p0", "s20", "g00", "p1", "g10", "s21", "f1", "e1", "p2",
+    "g20", "g11", "f0", "e0", "g30", "g21", "r1", "e3", "r0", "x1", "g31", "e2", "z1", "r3",
+    "x0", "e5", "r2", "l1", "e4", "z0", "x3", "r5", "e6", "z3", "x2", "l0", "r4", "e7", "z2",
+    "x5", "l3", "r6", "x4", "z5", "l2", "r7", "z4", "x6", "l5", "z6", "x7", "l4", "z7", "l6",
+    "l7",
 )
 
 SMEM = pl.BlockSpec(memory_space=pltpu.SMEM)

time: 152 us -> 147 us (0.967)
  waiting for transfers between devices: 48.1 us -> 44.8 us
  starting transfers between devices: 67.6 us -> 66 us
    ppermute x22, waiting for transfers between devices: 34.6 us -> 23.6 us  [along(): lax.ppermute(value, 'narrow', [(n, n ^ mask) for n in range(narrow_count)])]
    ppermute x26, waiting for transfers between devices: 13.4 us -> 21.2 us  [across(): lax.ppermute(value, 'wide', [(w, w ^ mask) for w in range(wide_count)])]
    ppermute x22, starting transfers between devices: 42.4 us -> 40.1 us  [along(): lax.ppermute(value, 'narrow', [(n, n ^ mask) for n in range(narrow_count)])]
  transfers between devices with their start and end apart: 48 -> 48, of which waited for: 16 -> 17; matrix products, arithmetic and copies ran while one was open for 1% -> 1% of each run, Pallas kernels for 20% -> 21%
where the time goes in v14:
time: 147 us; the launch traced here: 146 us
  starting transfers between devices  66 us (45%)
  waiting for transfers between devices  44.8 us (30%)
  Pallas kernels  32.3 us (22%)
  local copies, waits for them, and re-layouts  1.67 us (1%)
    ppermute x22, starting transfers between devices, along(): lax.ppermute(value, 'narrow', [(n, n ^ mask) for n in range(narrow_count)])  40.1 us
    ppermute x26, starting transfers between devices, across(): lax.ppermute(value, 'wide', [(w, w ^ mask) for w in range(wide_count)])  25.9 us
    ppermute x22, waiting for transfers between devices, along(): lax.ppermute(value, 'narrow', [(n, n ^ mask) for n in range(narrow_count)])  23.6 us
    ppermute x26, waiting for transfers between devices, across(): lax.ppermute(value, 'wide', [(w, w ^ mask) for w in range(wide_count)])  21.2 us
    pallas_call x8, Pallas kernels, product(): pl.pallas_call(functools.partial(product_kernel, count, rows, layout, tar...  19.7 us
    pallas_call x2, Pallas kernels, split(): pl.pallas_call(functools.partial(split_kernel, step), in_specs=[HBM], out...  8.51 us
  transfers between devices with their start and end apart: 48, of which 17 were waited for; matrix products, arithmetic and copies ran while one was open for 1% of the time, Pallas kernels for 21%

profile of v14, /device:TPU:0, one launch (start us, length us, event | category | flops | bytes accessed | tf_op | source)
XLA Modules:
  0.0 146.3 jit_solution(15810885047530087636)
XLA Ops:
  2.4 2.6 %collective-permute-start = (f32[16,2048]{1,0:T(8,128)S(1)}, f32[16,2048]{1,0:T(8,128)S(1)}, u32[]{:S(2)}, u32[]{:S(2)}) collective-permute-start(f32[16,2048]{1,0:T(8,128)S(1)} %get-tuple-element.152), channel_id=1, source_target_pairs={{0,1},{1,0},{2,3},{3,2},{4,5},{5,4},{6,7},{7,6},{8,9},{9,8},{10,11... | collective-permute-start | bytes 393224 | tf_op jit(solution)/shard_map/ppermute | solution.py:253
  5.1 4.3 %collective-permute-done.refs_1_ = f32[16,2048]{1,0:T(8,128)S(1)} collective-permute-done((f32[16,2048]{1,0:T(8,128)S(1)}, f32[16,2048]{1,0:T(8,128)S(1)}, u32[]{:S(2)}, u32[]{:S(2)}) %collective-permute-start) | collective-permute-done | bytes 131104 | tf_op jit(solution)/shard_map/ppermute | solution.py:253
  9.4 3.0 %collective-permute-start.1 = (f32[16,2048]{1,0:T(8,128)S(1)}, f32[16,2048]{1,0:T(8,128)S(1)}, u32[]{:S(2)}, u32[]{:S(2)}) collective-permute-start(f32[16,2048]{1,0:T(8,128)S(1)} %pad_maximum_fusion.1), channel_id=1, source_target_pairs={{0,2},{1,3},{2,0},{3,1},{4,6},{5,7},{6,4},{7,5},{8,10},{9,11},{10,... | collective-permute-start | bytes 393224 | tf_op jit(solution)/shard_map/ppermute | solution.py:253
  12.5 2.8 %collective-permute-start.6 = (f32[16,2048]{1,0:T(8,128)S(1)}, f32[16,2048]{1,0:T(8,128)S(1)}, u32[]{:S(2)}, u32[]{:S(2)}) collective-permute-start(f32[16,2048]{1,0:T(8,128)S(1)} %pad_maximum_fusion.2), channel_id=1, source_target_pairs={{0,2},{1,3},{2,0},{3,1},{4,6},{5,7},{6,4},{7,5},{8,10},{9,11},{10,... | collective-permute-start | bytes 393224 | tf_op jit(solution)/shard_map/ppermute | solution.py:253
  15.2 7.1 %collective-permute-done.1.refs_2_.refs_3_ = f32[16,2048]{1,0:T(8,128)S(1)} collective-permute-done((f32[16,2048]{1,0:T(8,128)S(1)}, f32[16,2048]{1,0:T(8,128)S(1)}, u32[]{:S(2)}, u32[]{:S(2)}) %collective-permute-start.1) | collective-permute-done | bytes 131104 | tf_op jit(solution)/shard_map/ppermute | solution.py:253
  27.0 5.1 %collective-permute-done.5.refs_3_ = f32[32,2048]{1,0:T(8,128)S(1)} collective-permute-done((f32[32,2048]{1,0:T(8,128)S(1)}, f32[32,2048]{1,0:T(8,128)S(1)}, u32[]{:S(2)}, u32[]{:S(2)}) %collective-permute-start.5) | collective-permute-done | bytes 262176 | tf_op jit(solution)/shard_map/ppermute | solution.py:247
  33.7 4.8 %collective-permute-done.3.refs_1_ = f32[32,2048]{1,0:T(8,128)S(1)} collective-permute-done((f32[32,2048]{1,0:T(8,128)S(1)}, f32[32,2048]{1,0:T(8,128)S(1)}, u32[]{:S(2)}, u32[]{:S(2)}) %collective-permute-start.3) | collective-permute-done | bytes 262176 | tf_op jit(solution)/shard_map/ppermute | solution.py:247
  38.7 4.3 %split.2 = (bf16[2048,1024]{1,0:T(8,128)(2,1)S(1)}, bf16[2048,1024]{1,0:T(8,128)(2,1)S(1)}, f32[8,128]{1,0:T(8,128)}) custom-call(f32[2048,1024]{1,0:T(8,128)} %collective-permute-done.10.whole_ref), custom_call_target="tpu_custom_call" | custom-call | flops 1 | bytes 1 | tf_op jit(solution)/shard_map/split/pallas_call | solution.py:117
  43.0 2.5 %product.8 = (f32[64,1024]{1,0:T(8,128)S(1)}, f32[64,1024]{1,0:T(8,128)S(1)}) custom-call(s32[3]{0:T(128)S(1)} %pad_add_fusion.place_ref, s32[8,64]{1,0:T(8,128)S(1)} %copy-done.3, s32[8]{0:T(128)S(1)} %copy-done.4, f32[32,2048]{1,0:T(8,128)S(1)} %pack.3.refs_0_, f32[32,2048]{1,0:T(8,128)S(1)} %collective-permute-done.3.refs_1_, ...), custom_call_target="tpu_custom_call" | custom-call | flops 3221225472 | bytes 1 | tf_op jit(solution)/shard_map/product/pallas_call | solution.py:178
  45.8 2.9 %collective-permute-done.9.refs_2_.refs_3_ = f32[32,2048]{1,0:T(8,128)S(1)} collective-permute-done((f32[32,2048]{1,0:T(8,128)S(1)}, f32[32,2048]{1,0:T(8,128)S(1)}, u32[]{:S(2)}, u32[]{:S(2)}) %collective-permute-start.9) | collective-permute-done | bytes 262176 | tf_op jit(solution)/shard_map/ppermute | solution.py:253
  51.8 4.3 %split.3 = (bf16[2048,1024]{1,0:T(8,128)(2,1)S(1)}, bf16[2048,1024]{1,0:T(8,128)(2,1)S(1)}, f32[8,128]{1,0:T(8,128)}) custom-call(f32[2048,1024]{1,0:T(8,128)} %whole_ref.2), custom_call_target="tpu_custom_call" | custom-call | flops 1 | bytes 1 | tf_op jit(solution)/shard_map/split/pallas_call | solution.py:117
  56.1 2.4 %product.9 = (f32[64,1024]{1,0:T(8,128)S(1)}, f32[64,1024]{1,0:T(8,128)S(1)}) custom-call(s32[3]{0:T(128)S(1)} %pad_add_fusion.place_ref, s32[8,64]{1,0:T(8,128)S(1)} %copy-done.3, s32[8]{0:T(128)S(1)} %copy-done.4, f32[32,2048]{1,0:T(8,128)S(1)} %pack.3.refs_0_, f32[32,2048]{1,0:T(8,128)S(1)} %collective-permute-done.3.refs_1_, ...), custom_call_target="tpu_custom_call" | custom-call | flops 3221225472 | bytes 1 | tf_op jit(solution)/shard_map/product/pallas_call | solution.py:178
  64.8 2.5 %product.10 = (f32[64,1024]{1,0:T(8,128)S(1)}, f32[64,1024]{1,0:T(8,128)S(1)}) custom-call(s32[3]{0:T(128)S(1)} %pad_add_fusion.place_ref, s32[8,64]{1,0:T(8,128)S(1)} %copy-done.3, s32[8]{0:T(128)S(1)} %copy-done.4, f32[32,2048]{1,0:T(8,128)S(1)} %pack.4.refs_0_, f32[32,2048]{1,0:T(8,128)S(1)} %collective-permute-done.7.refs_1_, ...), custom_call_target="tpu_custom_call" | custom-call | flops 3221225472 | bytes 1 | tf_op jit(solution)/shard_map/product/pallas_call | solution.py:178
  72.1 2.4 %product.11 = (f32[64,1024]{1,0:T(8,128)S(1)}, f32[64,1024]{1,0:T(8,128)S(1)}) custom-call(s32[3]{0:T(128)S(1)} %pad_add_fusion.place_ref, s32[8,64]{1,0:T(8,128)S(1)} %copy-done.3, s32[8]{0:T(128)S(1)} %copy-done.4, f32[32,2048]{1,0:T(8,128)S(1)} %pack.4.refs_0_, f32[32,2048]{1,0:T(8,128)S(1)} %collective-permute-done.7.refs_1_, ...), custom_call_target="tpu_custom_call" | custom-call | flops 3221225472 | bytes 1 | tf_op jit(solution)/shard_map/product/pallas_call | solution.py:178
  74.5 4.4 %collective-permute-done.18 = f32[32,1024]{1,0:T(8,128)S(1)} collective-permute-done((f32[32,1024]{1,0:T(8,128)S(1)}, f32[32,1024]{1,0:T(8,128)S(1)}, u32[]{:S(2)}, u32[]{:S(2)}) %collective-permute-start.18) | collective-permute-done | bytes 131104 | tf_op jit(solution)/shard_map/ppermute | solution.py:247
  80.1 2.4 %collective-permute-start.26 = (f32[64,1024]{1,0:T(8,128)S(1)}, f32[64,1024]{1,0:T(8,128)S(1)}, u32[]{:S(2)}, u32[]{:S(2)}) collective-permute-start(f32[64,1024]{1,0:T(8,128)S(1)} %broadcast_select_fusion.5), channel_id=1, source_target_pairs={{0,1},{1,0},{2,3},{3,2},{4,5},{5,4},{6,7},{7,6},{8,9},{9,8},{10,11... | collective-permute-start | bytes 786440 | tf_op jit(solution)/shard_map/ppermute | solution.py:253
  82.6 2.2 %collective-permute-start.20 = (f32[32,1024]{1,0:T(8,128)S(1)}, f32[32,1024]{1,0:T(8,128)S(1)}, u32[]{:S(2)}, u32[]{:S(2)}) collective-permute-start(f32[32,1024]{1,0:T(8,128)S(1)} %get-tuple-element.325), channel_id=1, source_target_pairs={{0,16},{4,20},{8,24},{12,28},{16,0},{20,4},{24,8},{28,12},{1,17},{... | collective-permute-start | bytes 393224 | tf_op jit(solution)/shard_map/ppermute | solution.py:247
  84.8 2.6 %product.12 = (f32[64,1024]{1,0:T(8,128)S(1)}, f32[64,1024]{1,0:T(8,128)S(1)}) custom-call(s32[3]{0:T(128)S(1)} %pad_add_fusion.place_ref, s32[8,64]{1,0:T(8,128)S(1)} %copy-done.3, s32[8]{0:T(128)S(1)} %copy-done.4, f32[32,2048]{1,0:T(8,128)S(1)} %get-tuple-element.236.refs_0_, f32[32,2048]{1,0:T(8,128)S(1)} %collective-permute-done.14.refs_1_, ...), custom_call_target="tpu_custom_call" | custom-call | flops 3221225472 | bytes 1 | tf_op jit(solution)/shard_map/product/pallas_call | solution.py:178
  87.6 3.0 %collective-permute-start.25 = (f32[64,1024]{1,0:T(8,128)S(1)}, f32[64,1024]{1,0:T(8,128)S(1)}, u32[]{:S(2)}, u32[]{:S(2)}) collective-permute-start(f32[64,1024]{1,0:T(8,128)S(1)} %broadcast_select_fusion.4), channel_id=1, source_target_pairs={{0,1},{1,0},{2,3},{3,2},{4,5},{5,4},{6,7},{7,6},{8,9},{9,8},{10,11... | collective-permute-start | bytes 786440 | tf_op jit(solution)/shard_map/ppermute | solution.py:253
  90.6 2.4 %product.13 = (f32[64,1024]{1,0:T(8,128)S(1)}, f32[64,1024]{1,0:T(8,128)S(1)}) custom-call(s32[3]{0:T(128)S(1)} %pad_add_fusion.place_ref, s32[8,64]{1,0:T(8,128)S(1)} %copy-done.3, s32[8]{0:T(128)S(1)} %copy-done.4, f32[32,2048]{1,0:T(8,128)S(1)} %get-tuple-element.236.refs_0_, f32[32,2048]{1,0:T(8,128)S(1)} %collective-permute-done.14.refs_1_, ...), custom_call_target="tpu_custom_call" | custom-call | flops 3221225472 | bytes 1 | tf_op jit(solution)/shard_map/product/pallas_call | solution.py:178
  93.7 2.2 %collective-permute-start.24 = (f32[32,1024]{1,0:T(8,128)S(1)}, f32[32,1024]{1,0:T(8,128)S(1)}, u32[]{:S(2)}, u32[]{:S(2)}) collective-permute-start(f32[32,1024]{1,0:T(8,128)S(1)} %get-tuple-element.321), channel_id=1, source_target_pairs={{0,2},{1,3},{2,0},{3,1},{4,6},{5,7},{6,4},{7,5},{8,10},{9,11},{10,... | collective-permute-start | bytes 393224 | tf_op jit(solution)/shard_map/ppermute | solution.py:253
  96.8 2.4 %product.14 = (f32[64,1024]{1,0:T(8,128)S(1)}, f32[64,1024]{1,0:T(8,128)S(1)}) custom-call(s32[3]{0:T(128)S(1)} %pad_add_fusion.place_ref, s32[8,64]{1,0:T(8,128)S(1)} %copy-done.3, s32[8]{0:T(128)S(1)} %copy-done.4, f32[32,2048]{1,0:T(8,128)S(1)} %get-tuple-element.261.refs_0_, f32[32,2048]{1,0:T(8,128)S(1)} %collective-permute-done.19.refs_1_, ...), custom_call_target="tpu_custom_call" | custom-call | flops 3221225472 | bytes 1 | tf_op jit(solution)/shard_map/product/pallas_call | solution.py:178
  102.1 2.9 %collective-permute-start.37 = (f32[32,1024]{1,0:T(8,128)S(1)}, f32[32,1024]{1,0:T(8,128)S(1)}, u32[]{:S(2)}, u32[]{:S(2)}) collective-permute-start(f32[32,1024]{1,0:T(8,128)S(1)} %get-tuple-element.312), channel_id=1, source_target_pairs={{0,2},{1,3},{2,0},{3,1},{4,6},{5,7},{6,4},{7,5},{8,10},{9,11},{10,... | collective-permute-start | bytes 393224 | tf_op jit(solution)/shard_map/ppermute | solution.py:253
  107.0 2.5 %product.15 = (f32[64,1024]{1,0:T(8,128)S(1)}, f32[64,1024]{1,0:T(8,128)S(1)}) custom-call(s32[3]{0:T(128)S(1)} %pad_add_fusion.place_ref, s32[8,64]{1,0:T(8,128)S(1)} %copy-done.3, s32[8]{0:T(128)S(1)} %copy-done.4, f32[32,2048]{1,0:T(8,128)S(1)} %get-tuple-element.261.refs_0_, f32[32,2048]{1,0:T(8,128)S(1)} %collective-permute-done.19.refs_1_, ...), custom_call_target="tpu_custom_call" | custom-call | flops 3221225472 | bytes 1 | tf_op jit(solution)/shard_map/product/pallas_call | solution.py:178
  114.2 3.2 %collective-permute-done.35 = f32[64,1024]{1,0:T(8,128)S(1)} collective-permute-done((f32[64,1024]{1,0:T(8,128)S(1)}, f32[64,1024]{1,0:T(8,128)S(1)}, u32[]{:S(2)}, u32[]{:S(2)}) %collective-permute-start.35) | collective-permute-done | bytes 262176 | tf_op jit(solution)/shard_map/ppermute | solution.py:253
  118.7 2.3 %collective-permute-start.44 = (f32[32,1024]{1,0:T(8,128)S(1)}, f32[32,1024]{1,0:T(8,128)S(1)}, u32[]{:S(2)}, u32[]{:S(2)}) collective-permute-start(f32[32,1024]{1,0:T(8,128)S(1)} %get-tuple-element.304), channel_id=1, source_target_pairs={{0,2},{1,3},{2,0},{3,1},{4,6},{5,7},{6,4},{7,5},{8,10},{9,11},{10,... | collective-permute-start | bytes 393224 | tf_op jit(solution)/shard_map/ppermute | solution.py:253
  121.1 2.0 %collective-permute-done.38 = f32[32,1024]{1,0:T(8,128)S(1)} collective-permute-done((f32[32,1024]{1,0:T(8,128)S(1)}, f32[32,1024]{1,0:T(8,128)S(1)}, u32[]{:S(2)}, u32[]{:S(2)}) %collective-permute-start.38) | collective-permute-done | bytes 131104 | tf_op jit(solution)/shard_map/ppermute | solution.py:247
  124.1 5.2 %collective-permute-start.40 = (f32[32,1024]{1,0:T(8,128)S(1)}, f32[32,1024]{1,0:T(8,128)S(1)}, u32[]{:S(2)}, u32[]{:S(2)}) collective-permute-start(f32[32,1024]{1,0:T(8,128)S(1)} %get-tuple-element.307), channel_id=1, source_target_pairs={{0,2},{1,3},{2,0},{3,1},{4,6},{5,7},{6,4},{7,5},{8,10},{9,11},{10,... | collective-permute-start | bytes 393224 | tf_op jit(solution)/shard_map/ppermute | solution.py:253
  131.1 2.0 %collective-permute-start.46 = (f32[32,1024]{1,0:T(8,128)S(1)}, f32[32,1024]{1,0:T(8,128)S(1)}, u32[]{:S(2)}, u32[]{:S(2)}) collective-permute-start(f32[32,1024]{1,0:T(8,128)S(1)} %get-tuple-element.300), channel_id=1, source_target_pairs={{0,16},{4,20},{8,24},{12,28},{16,0},{20,4},{24,8},{28,12},{1,17},{... | collective-permute-start | bytes 393224 | tf_op jit(solution)/shard_map/ppermute | solution.py:247
  133.1 2.3 %collective-permute-start.45 = (f32[32,1024]{1,0:T(8,128)S(1)}, f32[32,1024]{1,0:T(8,128)S(1)}, u32[]{:S(2)}, u32[]{:S(2)}) collective-permute-start(f32[32,1024]{1,0:T(8,128)S(1)} %get-tuple-element.302), channel_id=1, source_target_pairs={{0,2},{1,3},{2,0},{3,1},{4,6},{5,7},{6,4},{7,5},{8,10},{9,11},{10,... | collective-permute-start | bytes 393224 | tf_op jit(solution)/shard_map/ppermute | solution.py:253
  136.2 4.1 %collective-permute-start.47 = (f32[32,1024]{1,0:T(8,128)S(1)}, f32[32,1024]{1,0:T(8,128)S(1)}, u32[]{:S(2)}, u32[]{:S(2)}) collective-permute-start(f32[32,1024]{1,0:T(8,128)S(1)} %get-tuple-element.298), channel_id=1, source_target_pairs={{0,2},{1,3},{2,0},{3,1},{4,6},{5,7},{6,4},{7,5},{8,10},{9,11},{10,... | collective-permute-start | bytes 393224 | tf_op jit(solution)/shard_map/ppermute | solution.py:253
  141.4 3.2 %collective-permute-done.47.refs_15_ = f32[32,1024]{1,0:T(8,128)S(1)} collective-permute-done((f32[32,1024]{1,0:T(8,128)S(1)}, f32[32,1024]{1,0:T(8,128)S(1)}, u32[]{:S(2)}, u32[]{:S(2)}) %collective-permute-start.47) | collective-permute-done | bytes 131104 | tf_op jit(solution)/shard_map/ppermute | solution.py:253
  (140 shorter events, 43.6 us)
Async XLA Ops:
  0.0 38.7 %collective-permute-start.10 = (f32[2048,1024]{1,0:T(8,128)}, f32[2048,1024]{1,0:T(8,128)}, u32[]{:S(2)}, u32[]{:S(2)}) collective-permute-start(f32[2048,1024]{1,0:T(8,128)} %whole_ref.2), channel_id=1, source_target_pairs={{0,4},{4,0},{8,12},{12,8},{16,20},{20,16},{24,28},{28,24},{1,5},{5... | collective-permute-start | bytes 25165832 | tf_op jit(solution)/shard_map/ppermute | solution.py:247
  9.4 12.9 %collective-permute-start.1 = (f32[16,2048]{1,0:T(8,128)S(1)}, f32[16,2048]{1,0:T(8,128)S(1)}, u32[]{:S(2)}, u32[]{:S(2)}) collective-permute-start(f32[16,2048]{1,0:T(8,128)S(1)} %pad_maximum_fusion.1), channel_id=1, source_target_pairs={{0,2},{1,3},{2,0},{3,1},{4,6},{5,7},{6,4},{7,5},{8,10},{9,11},{10,... | collective-permute-start | bytes 393224 | tf_op jit(solution)/shard_map/ppermute | solution.py:253
  12.5 14.0 %collective-permute-start.6 = (f32[16,2048]{1,0:T(8,128)S(1)}, f32[16,2048]{1,0:T(8,128)S(1)}, u32[]{:S(2)}, u32[]{:S(2)}) collective-permute-start(f32[16,2048]{1,0:T(8,128)S(1)} %pad_maximum_fusion.2), channel_id=1, source_target_pairs={{0,2},{1,3},{2,0},{3,1},{4,6},{5,7},{6,4},{7,5},{8,10},{9,11},{10,... | collective-permute-start | bytes 393224 | tf_op jit(solution)/shard_map/ppermute | solution.py:253
  22.9 9.2 %collective-permute-start.5 = (f32[32,2048]{1,0:T(8,128)S(1)}, f32[32,2048]{1,0:T(8,128)S(1)}, u32[]{:S(2)}, u32[]{:S(2)}) collective-permute-start(f32[32,2048]{1,0:T(8,128)S(1)} %pack.3.refs_0_), channel_id=1, source_target_pairs={{0,16},{4,20},{8,24},{12,28},{16,0},{20,4},{24,8},{28,12},{1,17},{... | collective-permute-start | bytes 786440 | tf_op jit(solution)/shard_map/ppermute | solution.py:247
  24.4 9.2 %collective-permute-start.4 = (f32[32,2048]{1,0:T(8,128)S(1)}, f32[32,2048]{1,0:T(8,128)S(1)}, u32[]{:S(2)}, u32[]{:S(2)}) collective-permute-start(f32[32,2048]{1,0:T(8,128)S(1)} %pack.3.refs_0_), channel_id=1, source_target_pairs={{0,8},{4,12},{8,0},{12,4},{16,24},{20,28},{24,16},{28,20},{1,9},{5... | collective-permute-start | bytes 786440 | tf_op jit(solution)/shard_map/ppermute | solution.py:247
  25.9 12.6 %collective-permute-start.3 = (f32[32,2048]{1,0:T(8,128)S(1)}, f32[32,2048]{1,0:T(8,128)S(1)}, u32[]{:S(2)}, u32[]{:S(2)}) collective-permute-start(f32[32,2048]{1,0:T(8,128)S(1)} %pack.3.refs_0_), channel_id=1, source_target_pairs={{0,24},{4,28},{8,16},{12,20},{16,8},{20,12},{24,0},{28,4},{1,25},{... | collective-permute-start | bytes 786440 | tf_op jit(solution)/shard_map/ppermute | solution.py:247
  26.5 12.0 %collective-permute-start.8 = (f32[32,2048]{1,0:T(8,128)S(1)}, f32[32,2048]{1,0:T(8,128)S(1)}, u32[]{:S(2)}, u32[]{:S(2)}) collective-permute-start(f32[32,2048]{1,0:T(8,128)S(1)} %get-tuple-element.165), channel_id=1, source_target_pairs={{0,1},{1,0},{2,3},{3,2},{4,5},{5,4},{6,7},{7,6},{8,9},{9,8},{10,11... | collective-permute-start | bytes 786440 | tf_op jit(solution)/shard_map/ppermute | solution.py:253
  32.2 18.0 %collective-permute-start.7 = (f32[32,2048]{1,0:T(8,128)S(1)}, f32[32,2048]{1,0:T(8,128)S(1)}, u32[]{:S(2)}, u32[]{:S(2)}) collective-permute-start(f32[32,2048]{1,0:T(8,128)S(1)} %pack.4.refs_0_), channel_id=1, source_target_pairs={{0,8},{4,12},{8,0},{12,4},{16,24},{20,28},{24,16},{28,20},{1,9},{5... | collective-permute-start | bytes 786440 | tf_op jit(solution)/shard_map/ppermute | solution.py:247
  38.6 10.1 %collective-permute-start.9 = (f32[32,2048]{1,0:T(8,128)S(1)}, f32[32,2048]{1,0:T(8,128)S(1)}, u32[]{:S(2)}, u32[]{:S(2)}) collective-permute-start(f32[32,2048]{1,0:T(8,128)S(1)} %pad_maximum_fusion), channel_id=1, source_target_pairs={{0,2},{1,3},{2,0},{3,1},{4,6},{5,7},{6,4},{7,5},{8,10},{9,11},{10,... | collective-permute-start | bytes 786440 | tf_op jit(solution)/shard_map/ppermute | solution.py:253
  45.4 15.8 %collective-permute-start.13 = (f32[64,1024]{1,0:T(8,128)S(1)}, f32[64,1024]{1,0:T(8,128)S(1)}, u32[]{:S(2)}, u32[]{:S(2)}) collective-permute-start(f32[64,1024]{1,0:T(8,128)S(1)} %get-tuple-element.184), channel_id=1, source_target_pairs={{0,8},{4,12},{8,0},{12,4},{16,24},{20,28},{24,16},{28,20},{1,9},{5... | collective-permute-start | bytes 786440 | tf_op jit(solution)/shard_map/ppermute | solution.py:247
  49.3 11.3 %collective-permute-start.14 = (f32[32,2048]{1,0:T(8,128)S(1)}, f32[32,2048]{1,0:T(8,128)S(1)}, u32[]{:S(2)}, u32[]{:S(2)}) collective-permute-start(f32[32,2048]{1,0:T(8,128)S(1)} %get-tuple-element.236.refs_0_), channel_id=1, source_target_pairs={{0,8},{4,12},{8,0},{12,4},{16,24},{20,28},{24,16},{28,20},{1,9},{5... | collective-permute-start | bytes 786440 | tf_op jit(solution)/shard_map/ppermute | solution.py:247
  50.2 14.6 %collective-permute-start.12 = (f32[64,2048]{1,0:T(8,128)S(1)}, f32[64,2048]{1,0:T(8,128)S(1)}, u32[]{:S(2)}, u32[]{:S(2)}) collective-permute-start(f32[64,2048]{1,0:T(8,128)S(1)} %constant_dynamic-update-slice_fusion), channel_id=1, source_target_pairs={{0,16},{4,20},{8,24},{12,28},{16,0},{20,4},{24,8},{28,12},{1,17},{... | collective-permute-start | bytes 1572872 | tf_op jit(solution)/shard_map/ppermute | solution.py:247
  58.5 10.0 %collective-permute-start.11 = (f32[64,1024]{1,0:T(8,128)S(1)}, f32[64,1024]{1,0:T(8,128)S(1)}, u32[]{:S(2)}, u32[]{:S(2)}) collective-permute-start(f32[64,1024]{1,0:T(8,128)S(1)} %get-tuple-element.199), channel_id=1, source_target_pairs={{0,8},{4,12},{8,0},{12,4},{16,24},{20,28},{24,16},{28,20},{1,9},{5... | collective-permute-start | bytes 786440 | tf_op jit(solution)/shard_map/ppermute | solution.py:247
  59.1 12.4 %collective-permute-start.19 = (f32[32,2048]{1,0:T(8,128)S(1)}, f32[32,2048]{1,0:T(8,128)S(1)}, u32[]{:S(2)}, u32[]{:S(2)}) collective-permute-start(f32[32,2048]{1,0:T(8,128)S(1)} %get-tuple-element.261.refs_0_), channel_id=1, source_target_pairs={{0,8},{4,12},{8,0},{12,4},{16,24},{20,28},{24,16},{28,20},{1,9},{5... | collective-permute-start | bytes 786440 | tf_op jit(solution)/shard_map/ppermute | solution.py:247
  60.6 22.0 %collective-permute-start.21 = (f32[64,2048]{1,0:T(8,128)S(1)}, f32[64,2048]{1,0:T(8,128)S(1)}, u32[]{:S(2)}, u32[]{:S(2)}) collective-permute-start(f32[64,2048]{1,0:T(8,128)S(1)} %constant_dynamic-update-slice_fusion.2), channel_id=1, source_target_pairs={{0,16},{4,20},{8,24},{12,28},{16,0},{20,4},{24,8},{28,12},{1,17},{... | collective-permute-start | bytes 1572872 | tf_op jit(solution)/shard_map/ppermute | solution.py:247
  67.3 12.6 %collective-permute-start.16 = (f32[64,1024]{1,0:T(8,128)S(1)}, f32[64,1024]{1,0:T(8,128)S(1)}, u32[]{:S(2)}, u32[]{:S(2)}) collective-permute-start(f32[64,1024]{1,0:T(8,128)S(1)} %get-tuple-element.210), channel_id=1, source_target_pairs={{0,8},{4,12},{8,0},{12,4},{16,24},{20,28},{24,16},{28,20},{1,9},{5... | collective-permute-start | bytes 786440 | tf_op jit(solution)/shard_map/ppermute | solution.py:247
  68.5 11.6 %collective-permute-start.15 = (f32[64,1024]{1,0:T(8,128)S(1)}, f32[64,1024]{1,0:T(8,128)S(1)}, u32[]{:S(2)}, u32[]{:S(2)}) collective-permute-start(f32[64,1024]{1,0:T(8,128)S(1)} %broadcast_select_fusion.6), channel_id=1, source_target_pairs={{0,1},{1,0},{2,3},{3,2},{4,5},{5,4},{6,7},{7,6},{8,9},{9,8},{10,11... | collective-permute-start | bytes 786440 | tf_op jit(solution)/shard_map/ppermute | solution.py:253
  71.5 24.6 %collective-permute-start.28 = (f32[64,2048]{1,0:T(8,128)S(1)}, f32[64,2048]{1,0:T(8,128)S(1)}, u32[]{:S(2)}, u32[]{:S(2)}) collective-permute-start(f32[64,2048]{1,0:T(8,128)S(1)} %constant_dynamic-update-slice_fusion.4), channel_id=1, source_target_pairs={{0,16},{4,20},{8,24},{12,28},{16,0},{20,4},{24,8},{28,12},{1,17},{... | collective-permute-start | bytes 1572872 | tf_op jit(solution)/shard_map/ppermute | solution.py:247
  80.1 13.5 %collective-permute-start.26 = (f32[64,1024]{1,0:T(8,128)S(1)}, f32[64,1024]{1,0:T(8,128)S(1)}, u32[]{:S(2)}, u32[]{:S(2)}) collective-permute-start(f32[64,1024]{1,0:T(8,128)S(1)} %broadcast_select_fusion.5), channel_id=1, source_target_pairs={{0,1},{1,0},{2,3},{3,2},{4,5},{5,4},{6,7},{7,6},{8,9},{9,8},{10,11... | collective-permute-start | bytes 786440 | tf_op jit(solution)/shard_map/ppermute | solution.py:253
  82.6 10.4 %collective-permute-start.20 = (f32[32,1024]{1,0:T(8,128)S(1)}, f32[32,1024]{1,0:T(8,128)S(1)}, u32[]{:S(2)}, u32[]{:S(2)}) collective-permute-start(f32[32,1024]{1,0:T(8,128)S(1)} %get-tuple-element.325), channel_id=1, source_target_pairs={{0,16},{4,20},{8,24},{12,28},{16,0},{20,4},{24,8},{28,12},{1,17},{... | collective-permute-start | bytes 393224 | tf_op jit(solution)/shard_map/ppermute | solution.py:247
  87.6 11.6 %collective-permute-start.25 = (f32[64,1024]{1,0:T(8,128)S(1)}, f32[64,1024]{1,0:T(8,128)S(1)}, u32[]{:S(2)}, u32[]{:S(2)}) collective-permute-start(f32[64,1024]{1,0:T(8,128)S(1)} %broadcast_select_fusion.4), channel_id=1, source_target_pairs={{0,1},{1,0},{2,3},{3,2},{4,5},{5,4},{6,7},{7,6},{8,9},{9,8},{10,11... | collective-permute-start | bytes 786440 | tf_op jit(solution)/shard_map/ppermute | solution.py:253
  93.0 12.2 %collective-permute-start.31 = (f32[64,1024]{1,0:T(8,128)S(1)}, f32[64,1024]{1,0:T(8,128)S(1)}, u32[]{:S(2)}, u32[]{:S(2)}) collective-permute-start(f32[64,1024]{1,0:T(8,128)S(1)} %get-tuple-element.241), channel_id=1, source_target_pairs={{0,8},{4,12},{8,0},{12,4},{16,24},{20,28},{24,16},{28,20},{1,9},{5... | collective-permute-start | bytes 786440 | tf_op jit(solution)/shard_map/ppermute | solution.py:247
  93.7 11.4 %collective-permute-start.24 = (f32[32,1024]{1,0:T(8,128)S(1)}, f32[32,1024]{1,0:T(8,128)S(1)}, u32[]{:S(2)}, u32[]{:S(2)}) collective-permute-start(f32[32,1024]{1,0:T(8,128)S(1)} %get-tuple-element.321), channel_id=1, source_target_pairs={{0,2},{1,3},{2,0},{3,1},{4,6},{5,7},{6,4},{7,5},{8,10},{9,11},{10,... | collective-permute-start | bytes 393224 | tf_op jit(solution)/shard_map/ppermute | solution.py:253
  96.1 15.4 %collective-permute-start.33 = (f32[64,1024]{1,0:T(8,128)S(1)}, f32[64,1024]{1,0:T(8,128)S(1)}, u32[]{:S(2)}, u32[]{:S(2)}) collective-permute-start(f32[64,1024]{1,0:T(8,128)S(1)} %broadcast_select_fusion.3), channel_id=1, source_target_pairs={{0,1},{1,0},{2,3},{3,2},{4,5},{5,4},{6,7},{7,6},{8,9},{9,8},{10,11... | collective-permute-start | bytes 786440 | tf_op jit(solution)/shard_map/ppermute | solution.py:253
  99.2 13.6 %collective-permute-start.36 = (f32[64,1024]{1,0:T(8,128)S(1)}, f32[64,1024]{1,0:T(8,128)S(1)}, u32[]{:S(2)}, u32[]{:S(2)}) collective-permute-start(f32[64,1024]{1,0:T(8,128)S(1)} %get-tuple-element.252), channel_id=1, source_target_pairs={{0,8},{4,12},{8,0},{12,4},{16,24},{20,28},{24,16},{28,20},{1,9},{5... | collective-permute-start | bytes 786440 | tf_op jit(solution)/shard_map/ppermute | solution.py:247
  102.1 9.7 %collective-permute-start.37 = (f32[32,1024]{1,0:T(8,128)S(1)}, f32[32,1024]{1,0:T(8,128)S(1)}, u32[]{:S(2)}, u32[]{:S(2)}) collective-permute-start(f32[32,1024]{1,0:T(8,128)S(1)} %get-tuple-element.312), channel_id=1, source_target_pairs={{0,2},{1,3},{2,0},{3,1},{4,6},{5,7},{6,4},{7,5},{8,10},{9,11},{10,... | collective-permute-start | bytes 393224 | tf_op jit(solution)/shard_map/ppermute | solution.py:253
  105.3 12.1 %collective-permute-start.35 = (f32[64,1024]{1,0:T(8,128)S(1)}, f32[64,1024]{1,0:T(8,128)S(1)}, u32[]{:S(2)}, u32[]{:S(2)}) collective-permute-start(f32[64,1024]{1,0:T(8,128)S(1)} %broadcast_select_fusion.2), channel_id=1, source_target_pairs={{0,1},{1,0},{2,3},{3,2},{4,5},{5,4},{6,7},{7,6},{8,9},{9,8},{10,11... | collective-permute-start | bytes 786440 | tf_op jit(solution)/shard_map/ppermute | solution.py:253
  110.1 11.0 %collective-permute-start.39 = (f32[64,1024]{1,0:T(8,128)S(1)}, f32[64,1024]{1,0:T(8,128)S(1)}, u32[]{:S(2)}, u32[]{:S(2)}) collective-permute-start(f32[64,1024]{1,0:T(8,128)S(1)} %get-tuple-element.266), channel_id=1, source_target_pairs={{0,8},{4,12},{8,0},{12,4},{16,24},{20,28},{24,16},{28,20},{1,9},{5... | collective-permute-start | bytes 786440 | tf_op jit(solution)/shard_map/ppermute | solution.py:247
  111.5 9.5 %collective-permute-start.32 = (f32[32,1024]{1,0:T(8,128)S(1)}, f32[32,1024]{1,0:T(8,128)S(1)}, u32[]{:S(2)}, u32[]{:S(2)}) collective-permute-start(f32[32,1024]{1,0:T(8,128)S(1)} %get-tuple-element.315), channel_id=1, source_target_pairs={{0,2},{1,3},{2,0},{3,1},{4,6},{5,7},{6,4},{7,5},{8,10},{9,11},{10,... | collective-permute-start | bytes 393224 | tf_op jit(solution)/shard_map/ppermute | solution.py:253
  112.9 10.2 %collective-permute-start.42 = (f32[64,1024]{1,0:T(8,128)S(1)}, f32[64,1024]{1,0:T(8,128)S(1)}, u32[]{:S(2)}, u32[]{:S(2)}) collective-permute-start(f32[64,1024]{1,0:T(8,128)S(1)} %broadcast_select_fusion.1), channel_id=1, source_target_pairs={{0,1},{1,0},{2,3},{3,2},{4,5},{5,4},{6,7},{7,6},{8,9},{9,8},{10,11... | collective-permute-start | bytes 786440 | tf_op jit(solution)/shard_map/ppermute | solution.py:253
  118.7 10.5 %collective-permute-start.44 = (f32[32,1024]{1,0:T(8,128)S(1)}, f32[32,1024]{1,0:T(8,128)S(1)}, u32[]{:S(2)}, u32[]{:S(2)}) collective-permute-start(f32[32,1024]{1,0:T(8,128)S(1)} %get-tuple-element.304), channel_id=1, source_target_pairs={{0,2},{1,3},{2,0},{3,1},{4,6},{5,7},{6,4},{7,5},{8,10},{9,11},{10,... | collective-permute-start | bytes 393224 | tf_op jit(solution)/shard_map/ppermute | solution.py:253
  124.1 11.4 %collective-permute-start.40 = (f32[32,1024]{1,0:T(8,128)S(1)}, f32[32,1024]{1,0:T(8,128)S(1)}, u32[]{:S(2)}, u32[]{:S(2)}) collective-permute-start(f32[32,1024]{1,0:T(8,128)S(1)} %get-tuple-element.307), channel_id=1, source_target_pairs={{0,2},{1,3},{2,0},{3,1},{4,6},{5,7},{6,4},{7,5},{8,10},{9,11},{10,... | collective-permute-start | bytes 393224 | tf_op jit(solution)/shard_map/ppermute | solution.py:253
  (22 other events, 215.8 us)

commit v15 on v14

--- a/solution.py
+++ b/solution.py
@@ -10,16 +10,17 @@
 TILE = 128
 CHUNKS = 4
 CORES = 2
-DIRECT = (0,)
+DIRECT = ()
+FORWARD = (0,)
 GROUPS = ((0,), (1,), (2, 3))
 UNITS = tuple((chunk, (half,)) for chunk in range(CHUNKS) for half in range(CORES))
 
 ORDER = (
-    "s00", "s10", "s01", "s11", "p0", "s20", "g00", "p1", "g10", "s21", "f1", "e1", "p2",
-    "g20", "g11", "f0", "e0", "g30", "g21", "r1", "e3", "r0", "x1", "g31", "e2", "z1", "r3",
-    "x0", "e5", "r2", "l1", "e4", "z0", "x3", "r5", "e6", "z3", "x2", "l0", "r4", "e7", "z2",
-    "x5", "l3", "r6", "x4", "z5", "l2", "r7", "z4", "x6", "l5", "z6", "x7", "l4", "z7", "l6",
-    "l7",
+    "s00", "p0", "s10", "g00", "s11", "s20", "g01", "p1", "g10", "s21", "f0", "e0", "g11",
+    "p2", "g30", "f1", "e1", "g20", "g31", "r0", "e3", "r1", "x0", "g21", "e6", "z0", "r3",
+    "x1", "e2", "r6", "l0", "e4", "z1", "x3", "r2", "e7", "z3", "l1", "x6", "r4", "e5", "z6",
+    "l3", "x2", "r7", "x4", "z2", "r5", "x7", "z4", "l2", "z7", "l6", "x5", "z5", "l4", "l7",
+    "l5",
 )
 
 SMEM = pl.BlockSpec(memory_space=pltpu.SMEM)
@@ -35,22 +36,27 @@
 def cut_kernel(count, bounds, place_ref, whole_ref, *outs):
     z = place_ref[2]
     depth = outs[0].shape[1]
-    for g, (low, high) in enumerate(bounds):
+    outs = list(outs)
+    for low, high, stacks in bounds:
         size = high - low
         for m in range(count):
             start = pl.multiple_of((z ^ m) * depth, depth)
-            here = slice(m // 2 * size, (m // 2 + 1) * size)
-            outs[2 * g + m % 2][here, :] = whole_ref[low:high, pl.ds(start, depth)]
+            here = slice(m // stacks * size, (m // stacks + 1) * size)
+            outs[m % stacks][here, :] = whole_ref[low:high, pl.ds(start, depth)]
+        del outs[:stacks]
 
 
 def cut(whole, count, depth, part, place):
-    bounds = [(group[0] * part, (group[-1] + 1) * part) for group in GROUPS]
+    bounds = [
+        (group[0] * part, (group[-1] + 1) * part, 2 if g else count)
+        for g, group in enumerate(GROUPS)
+    ]
     shapes = [
-        jax.ShapeDtypeStruct((count // 2 * (high - low), depth), whole.dtype)
-        for low, high in bounds
-        for _ in range(2)
+        jax.ShapeDtypeStruct((count // stacks * (high - low), depth), whole.dtype)
+        for low, high, stacks in bounds
+        for _ in range(stacks)
     ]
-    outs = pl.pallas_call(
+    outs = list(pl.pallas_call(
         functools.partial(cut_kernel, count, bounds),
         in_specs=[SMEM, VMEM],
         out_specs=[VMEM] * len(shapes),
@@ -58,8 +64,8 @@
         cost_estimate=SMALL,
         compiler_params=pltpu.CompilerParams(vmem_limit_bytes=2**20),
         name="cut",
-    )(place, whole)
-    return [outs[2 * g : 2 * g + 2] for g in range(len(bounds))]
+    )(place, whole))
+    return [[outs.pop(0) for _ in range(stacks)] for _, _, stacks in bounds]
 
 
 def pack_kernel(part, starts, place_ref, *refs):
@@ -272,6 +278,14 @@
     def spread_step(g, number):
         size = len(GROUPS[g]) * part
         bit = narrow_bits[number]
+        if g == 0:
+            if number == 0:
+                sends = ordered(*pieces[g][1:])
+                mark(*sends)
+                spread[g] = {(0, 0): (pieces[g][0], 0)}
+                for n, send in enumerate(sends):
+                    spread[g][0, n + 1] = (along(send, n + 1), 0)
+            return
         if number == 0:
             kept, send = pieces[g]
             (send,) = ordered(send)
@@ -306,7 +320,19 @@
         if number == 0:
             held[chunk] = [mine[chunk]]
             layouts[chunk] = [[(0, 0, rows)]]
-        if chunk in DIRECT and chips == 4:
+        if chunk in FORWARD and chips == 4:
+            if number == 0:
+                (send,) = ordered(mine[chunk])
+                mark(send)
+                held[chunk] += [across_chips(send, 1), across_chips(send, 2)]
+                layouts[chunk] += [[(1, 0, rows)], [(2, 0, rows)]]
+            else:
+                near, far = ordered(held[chunk][1], held[chunk][2])
+                near, far = near[: rows // 2], far[rows // 2 :]
+                mark(near, far)
+                held[chunk] += [across_chips(near, 2), across_chips(far, 1)]
+                layouts[chunk] += [[(3, 0, rows // 2)], [(3, rows // 2, rows // 2)]]
+        elif chunk in DIRECT and chips == 4:
             (send,) = ordered(mine[chunk])
             mark(send)
             held[chunk] += [across_chips(send, k) for k in (3, 1, 2)]

time: 147 us -> 140 us (0.952)
  starting transfers between devices: 66 us -> 56.1 us
  waiting for transfers between devices: 44.8 us -> 47.3 us
    ppermute x22 -> x23, starting transfers between devices: 40.1 us -> 22.9 us  [along(): lax.ppermute(value, 'narrow', [(n, n ^ mask) for n in range(narrow_count)])]
    ppermute x26 -> x27, starting transfers between devices: 25.9 us -> 33.2 us  [across(): lax.ppermute(value, 'wide', [(w, w ^ mask) for w in range(wide_count)])]
    ppermute x22 -> x23, waiting for transfers between devices: 23.6 us -> 29.2 us  [along(): lax.ppermute(value, 'narrow', [(n, n ^ mask) for n in range(narrow_count)])]
    ppermute x26 -> x27, waiting for transfers between devices: 21.2 us -> 18.1 us  [across(): lax.ppermute(value, 'wide', [(w, w ^ mask) for w in range(wide_count)])]
  transfers between devices with their start and end apart: 48 -> 50, of which waited for: 17 -> 24; matrix products, arithmetic and copies ran while one was open for 1% -> 2% of each run, Pallas kernels for 21% -> 22%
where the time goes in v15:
time: 140 us
  starting transfers between devices  56.1 us (40%)
  waiting for transfers between devices  47.3 us (34%)
  Pallas kernels  32.2 us (23%)
  other arithmetic  1.81 us (1%)
  local copies, waits for them, and re-layouts  1.69 us (1%)
    ppermute x27, starting transfers between devices, across(): lax.ppermute(value, 'wide', [(w, w ^ mask) for w in range(wide_count)])  33.2 us
    ppermute x23, waiting for transfers between devices, along(): lax.ppermute(value, 'narrow', [(n, n ^ mask) for n in range(narrow_count)])  29.2 us
    ppermute x23, starting transfers between devices, along(): lax.ppermute(value, 'narrow', [(n, n ^ mask) for n in range(narrow_count)])  22.9 us
    pallas_call x8, Pallas kernels, product(): pl.pallas_call(functools.partial(product_kernel, count, rows, layout, tar...  19.6 us
    ppermute x27, waiting for transfers between devices, across(): lax.ppermute(value, 'wide', [(w, w ^ mask) for w in range(wide_count)])  18.1 us
    pallas_call x2, Pallas kernels, split(): pl.pallas_call(functools.partial(split_kernel, step), in_specs=[HBM], out...  8.51 us
  transfers between devices with their start and end apart: 50, of which 24 were waited for; matrix products, arithmetic and copies ran while one was open for 2% of the time, Pallas kernels for 22%

profile of v15, /device:TPU:0, one launch (start us, length us, event | category | flops | bytes accessed | tf_op | source)
XLA Modules:
  0.0 139.6 jit_solution(15070580823447542137)
XLA Ops:
  2.4 2.6 %collective-permute-start = (f32[8,2048]{1,0:T(8,128)S(1)}, f32[8,2048]{1,0:T(8,128)S(1)}, u32[]{:S(2)}, u32[]{:S(2)}) collective-permute-start(f32[8,2048]{1,0:T(8,128)S(1)} %get-tuple-element.161), channel_id=1, source_target_pairs={{0,1},{1,0},{2,3},{3,2},{4,5},{5,4},{6,7},{7,6},{8,9},{9,8},{10,11... | collective-permute-start | bytes 196616 | tf_op jit(solution)/shard_map/ppermute | solution.py:259
  5.0 2.6 %collective-permute-start.1 = (f32[8,2048]{1,0:T(8,128)S(1)}, f32[8,2048]{1,0:T(8,128)S(1)}, u32[]{:S(2)}, u32[]{:S(2)}) collective-permute-start(f32[8,2048]{1,0:T(8,128)S(1)} %get-tuple-element.162), channel_id=1, source_target_pairs={{0,2},{1,3},{2,0},{3,1},{4,6},{5,7},{6,4},{7,5},{8,10},{9,11},{10,... | collective-permute-start | bytes 196616 | tf_op jit(solution)/shard_map/ppermute | solution.py:259
  7.8 4.2 %collective-permute-done.1.refs_2_ = f32[8,2048]{1,0:T(8,128)S(1)} collective-permute-done((f32[8,2048]{1,0:T(8,128)S(1)}, f32[8,2048]{1,0:T(8,128)S(1)}, u32[]{:S(2)}, u32[]{:S(2)}) %collective-permute-start.1) | collective-permute-done | bytes 65568 | tf_op jit(solution)/shard_map/ppermute | solution.py:259
  12.0 1.8 %collective-permute-done.2.refs_3_ = f32[8,2048]{1,0:T(8,128)S(1)} collective-permute-done((f32[8,2048]{1,0:T(8,128)S(1)}, f32[8,2048]{1,0:T(8,128)S(1)}, u32[]{:S(2)}, u32[]{:S(2)}) %collective-permute-start.2) | collective-permute-done | bytes 65568 | tf_op jit(solution)/shard_map/ppermute | solution.py:259
  30.4 3.5 %collective-permute-start.11 = (f32[32,2048]{1,0:T(8,128)S(1)}, f32[32,2048]{1,0:T(8,128)S(1)}, u32[]{:S(2)}, u32[]{:S(2)}) collective-permute-start(f32[32,2048]{1,0:T(8,128)S(1)} %pad_maximum_fusion), channel_id=1, source_target_pairs={{0,2},{1,3},{2,0},{3,1},{4,6},{5,7},{6,4},{7,5},{8,10},{9,11},{10,... | collective-permute-start | bytes 786440 | tf_op jit(solution)/shard_map/ppermute | solution.py:259
  34.0 4.3 %split.2 = (bf16[2048,1024]{1,0:T(8,128)(2,1)S(1)}, bf16[2048,1024]{1,0:T(8,128)(2,1)S(1)}, f32[8,128]{1,0:T(8,128)}) custom-call(f32[2048,1024]{1,0:T(8,128)} %whole_ref.2), custom_call_target="tpu_custom_call" | custom-call | flops 1 | bytes 1 | tf_op jit(solution)/shard_map/split/pallas_call | solution.py:123
  38.3 2.4 %product.8 = (f32[64,1024]{1,0:T(8,128)S(1)}, f32[64,1024]{1,0:T(8,128)S(1)}) custom-call(s32[3]{0:T(128)S(1)} %pad_add_fusion.place_ref, s32[8,64]{1,0:T(8,128)S(1)} %copy-done.3, s32[8]{0:T(128)S(1)} %copy-done.4, f32[32,2048]{1,0:T(8,128)S(1)} %pack.3.refs_0_, f32[32,2048]{1,0:T(8,128)S(1)} %collective-permute-done.3.refs_1_, ...), custom_call_target="tpu_custom_call" | custom-call | flops 3221225472 | bytes 1 | tf_op jit(solution)/shard_map/product/pallas_call | solution.py:184
  45.1 4.3 %split.3 = (bf16[2048,1024]{1,0:T(8,128)(2,1)S(1)}, bf16[2048,1024]{1,0:T(8,128)(2,1)S(1)}, f32[8,128]{1,0:T(8,128)}) custom-call(f32[2048,1024]{1,0:T(8,128)} %collective-permute-done.14.whole_ref), custom_call_target="tpu_custom_call" | custom-call | flops 1 | bytes 1 | tf_op jit(solution)/shard_map/split/pallas_call | solution.py:123
  49.3 2.5 %product.9 = (f32[64,1024]{1,0:T(8,128)S(1)}, f32[64,1024]{1,0:T(8,128)S(1)}) custom-call(s32[3]{0:T(128)S(1)} %pad_add_fusion.place_ref, s32[8,64]{1,0:T(8,128)S(1)} %copy-done.3, s32[8]{0:T(128)S(1)} %copy-done.4, f32[32,2048]{1,0:T(8,128)S(1)} %pack.3.refs_0_, f32[32,2048]{1,0:T(8,128)S(1)} %collective-permute-done.3.refs_1_, ...), custom_call_target="tpu_custom_call" | custom-call | flops 3221225472 | bytes 1 | tf_op jit(solution)/shard_map/product/pallas_call | solution.py:184
  55.1 2.5 %product.10 = (f32[64,1024]{1,0:T(8,128)S(1)}, f32[64,1024]{1,0:T(8,128)S(1)}) custom-call(s32[3]{0:T(128)S(1)} %pad_add_fusion.place_ref, s32[8,64]{1,0:T(8,128)S(1)} %copy-done.3, s32[8]{0:T(128)S(1)} %copy-done.4, f32[32,2048]{1,0:T(8,128)S(1)} %pack.4.refs_0_, f32[32,2048]{1,0:T(8,128)S(1)} %collective-permute-done.12.refs_1_, ...), custom_call_target="tpu_custom_call" | custom-call | flops 3221225472 | bytes 1 | tf_op jit(solution)/shard_map/product/pallas_call | solution.py:184
  59.1 2.0 %collective-permute-done.16 = f32[64,1024]{1,0:T(8,128)S(1)} collective-permute-done((f32[64,1024]{1,0:T(8,128)S(1)}, f32[64,1024]{1,0:T(8,128)S(1)}, u32[]{:S(2)}, u32[]{:S(2)}) %collective-permute-start.16) | collective-permute-done | bytes 262176 | tf_op jit(solution)/shard_map/ppermute | solution.py:253
  61.3 2.2 %collective-permute-done.15 = f32[64,1024]{1,0:T(8,128)S(1)} collective-permute-done((f32[64,1024]{1,0:T(8,128)S(1)}, f32[64,1024]{1,0:T(8,128)S(1)}, u32[]{:S(2)}, u32[]{:S(2)}) %collective-permute-start.15) | collective-permute-done | bytes 262176 | tf_op jit(solution)/shard_map/ppermute | solution.py:259
  63.9 2.9 %collective-permute-done.20.refs_1_ = f32[32,2048]{1,0:T(8,128)S(1)} collective-permute-done((f32[32,2048]{1,0:T(8,128)S(1)}, f32[32,2048]{1,0:T(8,128)S(1)}, u32[]{:S(2)}, u32[]{:S(2)}) %collective-permute-start.20) | collective-permute-done | bytes 262176 | tf_op jit(solution)/shard_map/ppermute | solution.py:253
  68.9 2.4 %product.11 = (f32[64,1024]{1,0:T(8,128)S(1)}, f32[64,1024]{1,0:T(8,128)S(1)}) custom-call(s32[3]{0:T(128)S(1)} %pad_add_fusion.place_ref, s32[8,64]{1,0:T(8,128)S(1)} %copy-done.3, s32[8]{0:T(128)S(1)} %copy-done.4, f32[32,2048]{1,0:T(8,128)S(1)} %get-tuple-element.260.refs_0_, f32[32,2048]{1,0:T(8,128)S(1)} %collective-permute-done.13.refs_1_, ...), custom_call_target="tpu_custom_call" | custom-call | flops 3221225472 | bytes 1 | tf_op jit(solution)/shard_map/product/pallas_call | solution.py:184
  75.1 2.4 %product.12 = (f32[64,1024]{1,0:T(8,128)S(1)}, f32[64,1024]{1,0:T(8,128)S(1)}) custom-call(s32[3]{0:T(128)S(1)} %pad_add_fusion.place_ref, s32[8,64]{1,0:T(8,128)S(1)} %copy-done.3, s32[8]{0:T(128)S(1)} %copy-done.4, f32[32,2048]{1,0:T(8,128)S(1)} %pack.4.refs_0_, f32[32,2048]{1,0:T(8,128)S(1)} %collective-permute-done.12.refs_1_, ...), custom_call_target="tpu_custom_call" | custom-call | flops 3221225472 | bytes 1 | tf_op jit(solution)/shard_map/product/pallas_call | solution.py:184
  77.6 2.5 %collective-permute-done.22 = f32[64,1024]{1,0:T(8,128)S(1)} collective-permute-done((f32[64,1024]{1,0:T(8,128)S(1)}, f32[64,1024]{1,0:T(8,128)S(1)}, u32[]{:S(2)}, u32[]{:S(2)}) %collective-permute-start.22) | collective-permute-done | bytes 262176 | tf_op jit(solution)/shard_map/ppermute | solution.py:253
  81.4 2.4 %product.13 = (f32[64,1024]{1,0:T(8,128)S(1)}, f32[64,1024]{1,0:T(8,128)S(1)}) custom-call(s32[3]{0:T(128)S(1)} %pad_add_fusion.place_ref, s32[8,64]{1,0:T(8,128)S(1)} %copy-done.3, s32[8]{0:T(128)S(1)} %copy-done.4, f32[32,2048]{1,0:T(8,128)S(1)} %get-tuple-element.273.refs_0_, f32[32,2048]{1,0:T(8,128)S(1)} %collective-permute-done.20.refs_1_, ...), custom_call_target="tpu_custom_call" | custom-call | flops 3221225472 | bytes 1 | tf_op jit(solution)/shard_map/product/pallas_call | solution.py:184
  88.1 2.5 %product.14 = (f32[64,1024]{1,0:T(8,128)S(1)}, f32[64,1024]{1,0:T(8,128)S(1)}) custom-call(s32[3]{0:T(128)S(1)} %pad_add_fusion.place_ref, s32[8,64]{1,0:T(8,128)S(1)} %copy-done.3, s32[8]{0:T(128)S(1)} %copy-done.4, f32[32,2048]{1,0:T(8,128)S(1)} %get-tuple-element.260.refs_0_, f32[32,2048]{1,0:T(8,128)S(1)} %collective-permute-done.13.refs_1_, ...), custom_call_target="tpu_custom_call" | custom-call | flops 3221225472 | bytes 1 | tf_op jit(solution)/shard_map/product/pallas_call | solution.py:184
  92.2 3.2 %collective-permute-done.27.refs_3_ = f32[32,1024]{1,0:T(8,128)S(1)} collective-permute-done((f32[32,1024]{1,0:T(8,128)S(1)}, f32[32,1024]{1,0:T(8,128)S(1)}, u32[]{:S(2)}, u32[]{:S(2)}) %collective-permute-start.27) | collective-permute-done | bytes 131104 | tf_op jit(solution)/shard_map/ppermute | solution.py:259
  98.1 2.5 %product.15 = (f32[64,1024]{1,0:T(8,128)S(1)}, f32[64,1024]{1,0:T(8,128)S(1)}) custom-call(s32[3]{0:T(128)S(1)} %pad_add_fusion.place_ref, s32[8,64]{1,0:T(8,128)S(1)} %copy-done.3, s32[8]{0:T(128)S(1)} %copy-done.4, f32[32,2048]{1,0:T(8,128)S(1)} %get-tuple-element.273.refs_0_, f32[32,2048]{1,0:T(8,128)S(1)} %collective-permute-done.20.refs_1_, ...), custom_call_target="tpu_custom_call" | custom-call | flops 3221225472 | bytes 1 | tf_op jit(solution)/shard_map/product/pallas_call | solution.py:184
  101.7 1.9 %collective-permute-start.45 = (f32[32,1024]{1,0:T(8,128)S(1)}, f32[32,1024]{1,0:T(8,128)S(1)}, u32[]{:S(2)}, u32[]{:S(2)}) collective-permute-start(f32[32,1024]{1,0:T(8,128)S(1)} %get-tuple-element.318), channel_id=1, source_target_pairs={{0,2},{1,3},{2,0},{3,1},{4,6},{5,7},{6,4},{7,5},{8,10},{9,11},{10,... | collective-permute-start | bytes 393224 | tf_op jit(solution)/shard_map/ppermute | solution.py:259
  103.7 2.5 %collective-permute-start.36 = (f32[32,1024]{1,0:T(8,128)S(1)}, f32[32,1024]{1,0:T(8,128)S(1)}, u32[]{:S(2)}, u32[]{:S(2)}) collective-permute-start(f32[32,1024]{1,0:T(8,128)S(1)} %get-tuple-element.325), channel_id=1, source_target_pairs={{0,16},{4,20},{8,24},{12,28},{16,0},{20,4},{24,8},{28,12},{1,17},{... | collective-permute-start | bytes 393224 | tf_op jit(solution)/shard_map/ppermute | solution.py:253
  106.3 3.9 %collective-permute-done.37 = f32[64,1024]{1,0:T(8,128)S(1)} collective-permute-done((f32[64,1024]{1,0:T(8,128)S(1)}, f32[64,1024]{1,0:T(8,128)S(1)}, u32[]{:S(2)}, u32[]{:S(2)}) %collective-permute-start.37) | collective-permute-done | bytes 262176 | tf_op jit(solution)/shard_map/ppermute | solution.py:259
  110.2 1.8 %collective-permute-start.40 = (f32[32,1024]{1,0:T(8,128)S(1)}, f32[32,1024]{1,0:T(8,128)S(1)}, u32[]{:S(2)}, u32[]{:S(2)}) collective-permute-start(f32[32,1024]{1,0:T(8,128)S(1)} %get-tuple-element.322), channel_id=1, source_target_pairs={{0,16},{4,20},{8,24},{12,28},{16,0},{20,4},{24,8},{28,12},{1,17},{... | collective-permute-start | bytes 393224 | tf_op jit(solution)/shard_map/ppermute | solution.py:253
  113.6 2.5 %collective-permute-done.41 = f32[64,1024]{1,0:T(8,128)S(1)} collective-permute-done((f32[64,1024]{1,0:T(8,128)S(1)}, f32[64,1024]{1,0:T(8,128)S(1)}, u32[]{:S(2)}, u32[]{:S(2)}) %collective-permute-start.41) | collective-permute-done | bytes 262176 | tf_op jit(solution)/shard_map/ppermute | solution.py:259
  116.2 3.3 %collective-permute-start.46 = (f32[32,1024]{1,0:T(8,128)S(1)}, f32[32,1024]{1,0:T(8,128)S(1)}, u32[]{:S(2)}, u32[]{:S(2)}) collective-permute-start(f32[32,1024]{1,0:T(8,128)S(1)} %get-tuple-element.316), channel_id=1, source_target_pairs={{0,16},{4,20},{8,24},{12,28},{16,0},{20,4},{24,8},{28,12},{1,17},{... | collective-permute-start | bytes 393224 | tf_op jit(solution)/shard_map/ppermute | solution.py:253
  119.5 4.0 %collective-permute-done.46 = f32[32,1024]{1,0:T(8,128)S(1)} collective-permute-done((f32[32,1024]{1,0:T(8,128)S(1)}, f32[32,1024]{1,0:T(8,128)S(1)}, u32[]{:S(2)}, u32[]{:S(2)}) %collective-permute-start.46) | collective-permute-done | bytes 131104 | tf_op jit(solution)/shard_map/ppermute | solution.py:253
  123.6 1.8 %collective-permute-start.47 = (f32[32,1024]{1,0:T(8,128)S(1)}, f32[32,1024]{1,0:T(8,128)S(1)}, u32[]{:S(2)}, u32[]{:S(2)}) collective-permute-start(f32[32,1024]{1,0:T(8,128)S(1)} %get-tuple-element.313), channel_id=1, source_target_pairs={{0,16},{4,20},{8,24},{12,28},{16,0},{20,4},{24,8},{28,12},{1,17},{... | collective-permute-start | bytes 393224 | tf_op jit(solution)/shard_map/ppermute | solution.py:253
  125.5 2.9 %collective-permute-start.49 = (f32[32,1024]{1,0:T(8,128)S(1)}, f32[32,1024]{1,0:T(8,128)S(1)}, u32[]{:S(2)}, u32[]{:S(2)}) collective-permute-start(f32[32,1024]{1,0:T(8,128)S(1)} %get-tuple-element.310), channel_id=1, source_target_pairs={{0,2},{1,3},{2,0},{3,1},{4,6},{5,7},{6,4},{7,5},{8,10},{9,11},{10,... | collective-permute-start | bytes 393224 | tf_op jit(solution)/shard_map/ppermute | solution.py:259
  129.5 5.4 %collective-permute-done.43.refs_9_ = f32[32,1024]{1,0:T(8,128)S(1)} collective-permute-done((f32[32,1024]{1,0:T(8,128)S(1)}, f32[32,1024]{1,0:T(8,128)S(1)}, u32[]{:S(2)}, u32[]{:S(2)}) %collective-permute-start.43) | collective-permute-done | bytes 131104 | tf_op jit(solution)/shard_map/ppermute | solution.py:259
  134.9 1.6 %collective-permute-done.49.refs_15_ = f32[32,1024]{1,0:T(8,128)S(1)} collective-permute-done((f32[32,1024]{1,0:T(8,128)S(1)}, f32[32,1024]{1,0:T(8,128)S(1)}, u32[]{:S(2)}, u32[]{:S(2)}) %collective-permute-start.49) | collective-permute-done | bytes 131104 | tf_op jit(solution)/shard_map/ppermute | solution.py:259
  137.9 1.8 %finish.1 = f32[128,2048]{1,0:T(8,128)} custom-call(s32[3]{0:T(128)S(1)} %pad_add_fusion.place_ref, f32[128,2048]{1,0:T(8,128)S(1)} %copy-done, f32[128,1]{1,0:T(8,128)S(1)} %copy.8.occ_ref, f32[1,2048]{1,0:T(1,128)S(1)} %bitcast.5, f32[32,1024]{1,0:T(8,128)S(1)} %get-tuple-element.247.refs_0_, f32[32,1024]{1,0:T(8,128)S(1)} %collective-permute-done.21.refs_1_, ...), custom_call_target="tpu_custom_call" | custom-call | flops 1 | bytes 1 | tf_op jit(solution)/shard_map/finish/pallas_call | solution.py:220
  (143 shorter events, 50.1 us)
Async XLA Ops:
  0.0 45.1 %collective-permute-start.14 = (f32[2048,1024]{1,0:T(8,128)}, f32[2048,1024]{1,0:T(8,128)}, u32[]{:S(2)}, u32[]{:S(2)}) collective-permute-start(f32[2048,1024]{1,0:T(8,128)} %whole_ref.2), channel_id=1, source_target_pairs={{0,4},{4,0},{8,12},{12,8},{16,20},{20,16},{24,28},{28,24},{1,5},{5... | collective-permute-start | bytes 25165832 | tf_op jit(solution)/shard_map/ppermute | solution.py:253
  19.4 11.0 %collective-permute-start.8 = (f32[32,2048]{1,0:T(8,128)S(1)}, f32[32,2048]{1,0:T(8,128)S(1)}, u32[]{:S(2)}, u32[]{:S(2)}) collective-permute-start(f32[32,2048]{1,0:T(8,128)S(1)} %get-tuple-element.175), channel_id=1, source_target_pairs={{0,1},{1,0},{2,3},{3,2},{4,5},{5,4},{6,7},{7,6},{8,9},{9,8},{10,11... | collective-permute-start | bytes 786440 | tf_op jit(solution)/shard_map/ppermute | solution.py:259
  24.5 13.7 %collective-permute-start.6 = (f32[16,2048]{1,0:T(8,128)S(1)}, f32[16,2048]{1,0:T(8,128)S(1)}, u32[]{:S(2)}, u32[]{:S(2)}) collective-permute-start(f32[16,2048]{1,0:T(8,128)S(1)} %slice.68), channel_id=1, source_target_pairs={{0,16},{4,20},{8,24},{12,28},{16,0},{20,4},{24,8},{28,12},{1,17},{... | collective-permute-start | bytes 393224 | tf_op jit(solution)/shard_map/ppermute | solution.py:253
  26.1 12.2 %collective-permute-start.7 = (f32[16,2048]{1,0:T(8,128)S(1)}, f32[16,2048]{1,0:T(8,128)S(1)}, u32[]{:S(2)}, u32[]{:S(2)}) collective-permute-start(f32[16,2048]{1,0:T(8,128)S(1)} %slice.69), channel_id=1, source_target_pairs={{0,8},{4,12},{8,0},{12,4},{16,24},{20,28},{24,16},{28,20},{1,9},{5... | collective-permute-start | bytes 393224 | tf_op jit(solution)/shard_map/ppermute | solution.py:253
  28.8 12.4 %collective-permute-start.12 = (f32[32,2048]{1,0:T(8,128)S(1)}, f32[32,2048]{1,0:T(8,128)S(1)}, u32[]{:S(2)}, u32[]{:S(2)}) collective-permute-start(f32[32,2048]{1,0:T(8,128)S(1)} %pack.4.refs_0_), channel_id=1, source_target_pairs={{0,8},{4,12},{8,0},{12,4},{16,24},{20,28},{24,16},{28,20},{1,9},{5... | collective-permute-start | bytes 786440 | tf_op jit(solution)/shard_map/ppermute | solution.py:253
  30.4 12.9 %collective-permute-start.11 = (f32[32,2048]{1,0:T(8,128)S(1)}, f32[32,2048]{1,0:T(8,128)S(1)}, u32[]{:S(2)}, u32[]{:S(2)}) collective-permute-start(f32[32,2048]{1,0:T(8,128)S(1)} %pad_maximum_fusion), channel_id=1, source_target_pairs={{0,2},{1,3},{2,0},{3,1},{4,6},{5,7},{6,4},{7,5},{8,10},{9,11},{10,... | collective-permute-start | bytes 786440 | tf_op jit(solution)/shard_map/ppermute | solution.py:259
  40.7 14.3 %collective-permute-start.10 = (f32[64,1024]{1,0:T(8,128)S(1)}, f32[64,1024]{1,0:T(8,128)S(1)}, u32[]{:S(2)}, u32[]{:S(2)}) collective-permute-start(f32[64,1024]{1,0:T(8,128)S(1)} %get-tuple-element.196), channel_id=1, source_target_pairs={{0,8},{4,12},{8,0},{12,4},{16,24},{20,28},{24,16},{28,20},{1,9},{5... | collective-permute-start | bytes 786440 | tf_op jit(solution)/shard_map/ppermute | solution.py:253
  41.3 13.8 %collective-permute-start.17 = (f32[64,2048]{1,0:T(8,128)S(1)}, f32[64,2048]{1,0:T(8,128)S(1)}, u32[]{:S(2)}, u32[]{:S(2)}) collective-permute-start(f32[64,2048]{1,0:T(8,128)S(1)} %constant_dynamic-update-slice_fusion), channel_id=1, source_target_pairs={{0,16},{4,20},{8,24},{12,28},{16,0},{20,4},{24,8},{28,12},{1,17},{... | collective-permute-start | bytes 1572872 | tf_op jit(solution)/shard_map/ppermute | solution.py:253
  43.9 10.0 %collective-permute-start.13 = (f32[32,2048]{1,0:T(8,128)S(1)}, f32[32,2048]{1,0:T(8,128)S(1)}, u32[]{:S(2)}, u32[]{:S(2)}) collective-permute-start(f32[32,2048]{1,0:T(8,128)S(1)} %get-tuple-element.260.refs_0_), channel_id=1, source_target_pairs={{0,8},{4,12},{8,0},{12,4},{16,24},{20,28},{24,16},{28,20},{1,9},{5... | collective-permute-start | bytes 786440 | tf_op jit(solution)/shard_map/ppermute | solution.py:253
  51.8 9.3 %collective-permute-start.16 = (f32[64,1024]{1,0:T(8,128)S(1)}, f32[64,1024]{1,0:T(8,128)S(1)}, u32[]{:S(2)}, u32[]{:S(2)}) collective-permute-start(f32[64,1024]{1,0:T(8,128)S(1)} %get-tuple-element.211), channel_id=1, source_target_pairs={{0,8},{4,12},{8,0},{12,4},{16,24},{20,28},{24,16},{28,20},{1,9},{5... | collective-permute-start | bytes 786440 | tf_op jit(solution)/shard_map/ppermute | solution.py:253
  52.8 13.9 %collective-permute-start.20 = (f32[32,2048]{1,0:T(8,128)S(1)}, f32[32,2048]{1,0:T(8,128)S(1)}, u32[]{:S(2)}, u32[]{:S(2)}) collective-permute-start(f32[32,2048]{1,0:T(8,128)S(1)} %get-tuple-element.273.refs_0_), channel_id=1, source_target_pairs={{0,8},{4,12},{8,0},{12,4},{16,24},{20,28},{24,16},{28,20},{1,9},{5... | collective-permute-start | bytes 786440 | tf_op jit(solution)/shard_map/ppermute | solution.py:253
  54.0 14.9 %collective-permute-start.19 = (f32[64,2048]{1,0:T(8,128)S(1)}, f32[64,2048]{1,0:T(8,128)S(1)}, u32[]{:S(2)}, u32[]{:S(2)}) collective-permute-start(f32[64,2048]{1,0:T(8,128)S(1)} %constant_dynamic-update-slice_fusion.2), channel_id=1, source_target_pairs={{0,16},{4,20},{8,24},{12,28},{16,0},{20,4},{24,8},{28,12},{1,17},{... | collective-permute-start | bytes 1572872 | tf_op jit(solution)/shard_map/ppermute | solution.py:253
  57.6 14.8 %collective-permute-start.24 = (f32[64,1024]{1,0:T(8,128)S(1)}, f32[64,1024]{1,0:T(8,128)S(1)}, u32[]{:S(2)}, u32[]{:S(2)}) collective-permute-start(f32[64,1024]{1,0:T(8,128)S(1)} %get-tuple-element.222), channel_id=1, source_target_pairs={{0,8},{4,12},{8,0},{12,4},{16,24},{20,28},{24,16},{28,20},{1,9},{5... | collective-permute-start | bytes 786440 | tf_op jit(solution)/shard_map/ppermute | solution.py:253
  61.2 12.1 %collective-permute-start.23 = (f32[64,1024]{1,0:T(8,128)S(1)}, f32[64,1024]{1,0:T(8,128)S(1)}, u32[]{:S(2)}, u32[]{:S(2)}) collective-permute-start(f32[64,1024]{1,0:T(8,128)S(1)} %broadcast_select_fusion.6), channel_id=1, source_target_pairs={{0,1},{1,0},{2,3},{3,2},{4,5},{5,4},{6,7},{7,6},{8,9},{9,8},{10,11... | collective-permute-start | bytes 786440 | tf_op jit(solution)/shard_map/ppermute | solution.py:259
  63.6 8.7 %collective-permute-start.18 = (f32[32,1024]{1,0:T(8,128)S(1)}, f32[32,1024]{1,0:T(8,128)S(1)}, u32[]{:S(2)}, u32[]{:S(2)}) collective-permute-start(f32[32,1024]{1,0:T(8,128)S(1)} %get-tuple-element.339), channel_id=1, source_target_pairs={{0,16},{4,20},{8,24},{12,28},{16,0},{20,4},{24,8},{28,12},{1,17},{... | collective-permute-start | bytes 393224 | tf_op jit(solution)/shard_map/ppermute | solution.py:253
  66.8 14.6 %collective-permute-start.26 = (f32[64,2048]{1,0:T(8,128)S(1)}, f32[64,2048]{1,0:T(8,128)S(1)}, u32[]{:S(2)}, u32[]{:S(2)}) collective-permute-start(f32[64,2048]{1,0:T(8,128)S(1)} %constant_dynamic-update-slice_fusion.4), channel_id=1, source_target_pairs={{0,16},{4,20},{8,24},{12,28},{16,0},{20,4},{24,8},{28,12},{1,17},{... | collective-permute-start | bytes 1572872 | tf_op jit(solution)/shard_map/ppermute | solution.py:253
  71.3 8.7 %collective-permute-start.22 = (f32[64,1024]{1,0:T(8,128)S(1)}, f32[64,1024]{1,0:T(8,128)S(1)}, u32[]{:S(2)}, u32[]{:S(2)}) collective-permute-start(f32[64,1024]{1,0:T(8,128)S(1)} %get-tuple-element.233), channel_id=1, source_target_pairs={{0,8},{4,12},{8,0},{12,4},{16,24},{20,28},{24,16},{28,20},{1,9},{5... | collective-permute-start | bytes 786440 | tf_op jit(solution)/shard_map/ppermute | solution.py:253
  72.5 14.1 %collective-permute-start.28 = (f32[64,1024]{1,0:T(8,128)S(1)}, f32[64,1024]{1,0:T(8,128)S(1)}, u32[]{:S(2)}, u32[]{:S(2)}) collective-permute-start(f32[64,1024]{1,0:T(8,128)S(1)} %broadcast_select_fusion.5), channel_id=1, source_target_pairs={{0,1},{1,0},{2,3},{3,2},{4,5},{5,4},{6,7},{7,6},{8,9},{9,8},{10,11... | collective-permute-start | bytes 786440 | tf_op jit(solution)/shard_map/ppermute | solution.py:259
  73.6 11.7 %collective-permute-start.25 = (f32[32,1024]{1,0:T(8,128)S(1)}, f32[32,1024]{1,0:T(8,128)S(1)}, u32[]{:S(2)}, u32[]{:S(2)}) collective-permute-start(f32[32,1024]{1,0:T(8,128)S(1)} %get-tuple-element.336), channel_id=1, source_target_pairs={{0,16},{4,20},{8,24},{12,28},{16,0},{20,4},{24,8},{28,12},{1,17},{... | collective-permute-start | bytes 393224 | tf_op jit(solution)/shard_map/ppermute | solution.py:253
  80.5 14.9 %collective-permute-start.33 = (f32[64,1024]{1,0:T(8,128)S(1)}, f32[64,1024]{1,0:T(8,128)S(1)}, u32[]{:S(2)}, u32[]{:S(2)}) collective-permute-start(f32[64,1024]{1,0:T(8,128)S(1)} %broadcast_select_fusion.4), channel_id=1, source_target_pairs={{0,1},{1,0},{2,3},{3,2},{4,5},{5,4},{6,7},{7,6},{8,9},{9,8},{10,11... | collective-permute-start | bytes 786440 | tf_op jit(solution)/shard_map/ppermute | solution.py:259
  83.9 13.2 %collective-permute-start.35 = (f32[64,1024]{1,0:T(8,128)S(1)}, f32[64,1024]{1,0:T(8,128)S(1)}, u32[]{:S(2)}, u32[]{:S(2)}) collective-permute-start(f32[64,1024]{1,0:T(8,128)S(1)} %get-tuple-element.254), channel_id=1, source_target_pairs={{0,8},{4,12},{8,0},{12,4},{16,24},{20,28},{24,16},{28,20},{1,9},{5... | collective-permute-start | bytes 786440 | tf_op jit(solution)/shard_map/ppermute | solution.py:253
  85.3 10.1 %collective-permute-start.27 = (f32[32,1024]{1,0:T(8,128)S(1)}, f32[32,1024]{1,0:T(8,128)S(1)}, u32[]{:S(2)}, u32[]{:S(2)}) collective-permute-start(f32[32,1024]{1,0:T(8,128)S(1)} %get-tuple-element.333), channel_id=1, source_target_pairs={{0,2},{1,3},{2,0},{3,1},{4,6},{5,7},{6,4},{7,5},{8,10},{9,11},{10,... | collective-permute-start | bytes 393224 | tf_op jit(solution)/shard_map/ppermute | solution.py:259
  88.1 12.5 %collective-permute-start.31 = (f32[64,1024]{1,0:T(8,128)S(1)}, f32[64,1024]{1,0:T(8,128)S(1)}, u32[]{:S(2)}, u32[]{:S(2)}) collective-permute-start(f32[64,1024]{1,0:T(8,128)S(1)} %broadcast_select_fusion.3), channel_id=1, source_target_pairs={{0,1},{1,0},{2,3},{3,2},{4,5},{5,4},{6,7},{7,6},{8,9},{9,8},{10,11... | collective-permute-start | bytes 786440 | tf_op jit(solution)/shard_map/ppermute | solution.py:259
  92.2 14.0 %collective-permute-start.38 = (f32[64,1024]{1,0:T(8,128)S(1)}, f32[64,1024]{1,0:T(8,128)S(1)}, u32[]{:S(2)}, u32[]{:S(2)}) collective-permute-start(f32[64,1024]{1,0:T(8,128)S(1)} %get-tuple-element.265), channel_id=1, source_target_pairs={{0,8},{4,12},{8,0},{12,4},{16,24},{20,28},{24,16},{28,20},{1,9},{5... | collective-permute-start | bytes 786440 | tf_op jit(solution)/shard_map/ppermute | solution.py:253
  97.0 13.1 %collective-permute-start.37 = (f32[64,1024]{1,0:T(8,128)S(1)}, f32[64,1024]{1,0:T(8,128)S(1)}, u32[]{:S(2)}, u32[]{:S(2)}) collective-permute-start(f32[64,1024]{1,0:T(8,128)S(1)} %broadcast_select_fusion.2), channel_id=1, source_target_pairs={{0,1},{1,0},{2,3},{3,2},{4,5},{5,4},{6,7},{7,6},{8,9},{9,8},{10,11... | collective-permute-start | bytes 786440 | tf_op jit(solution)/shard_map/ppermute | solution.py:259
  100.6 11.6 %collective-permute-start.42 = (f32[64,1024]{1,0:T(8,128)S(1)}, f32[64,1024]{1,0:T(8,128)S(1)}, u32[]{:S(2)}, u32[]{:S(2)}) collective-permute-start(f32[64,1024]{1,0:T(8,128)S(1)} %get-tuple-element.278), channel_id=1, source_target_pairs={{0,8},{4,12},{8,0},{12,4},{16,24},{20,28},{24,16},{28,20},{1,9},{5... | collective-permute-start | bytes 786440 | tf_op jit(solution)/shard_map/ppermute | solution.py:253
  101.7 21.8 %collective-permute-start.45 = (f32[32,1024]{1,0:T(8,128)S(1)}, f32[32,1024]{1,0:T(8,128)S(1)}, u32[]{:S(2)}, u32[]{:S(2)}) collective-permute-start(f32[32,1024]{1,0:T(8,128)S(1)} %get-tuple-element.318), channel_id=1, source_target_pairs={{0,2},{1,3},{2,0},{3,1},{4,6},{5,7},{6,4},{7,5},{8,10},{9,11},{10,... | collective-permute-start | bytes 393224 | tf_op jit(solution)/shard_map/ppermute | solution.py:259
  106.2 9.9 %collective-permute-start.41 = (f32[64,1024]{1,0:T(8,128)S(1)}, f32[64,1024]{1,0:T(8,128)S(1)}, u32[]{:S(2)}, u32[]{:S(2)}) collective-permute-start(f32[64,1024]{1,0:T(8,128)S(1)} %broadcast_select_fusion.1), channel_id=1, source_target_pairs={{0,1},{1,0},{2,3},{3,2},{4,5},{5,4},{6,7},{7,6},{8,9},{9,8},{10,11... | collective-permute-start | bytes 786440 | tf_op jit(solution)/shard_map/ppermute | solution.py:259
  110.2 9.3 %collective-permute-start.40 = (f32[32,1024]{1,0:T(8,128)S(1)}, f32[32,1024]{1,0:T(8,128)S(1)}, u32[]{:S(2)}, u32[]{:S(2)}) collective-permute-start(f32[32,1024]{1,0:T(8,128)S(1)} %get-tuple-element.322), channel_id=1, source_target_pairs={{0,16},{4,20},{8,24},{12,28},{16,0},{20,4},{24,8},{28,12},{1,17},{... | collective-permute-start | bytes 393224 | tf_op jit(solution)/shard_map/ppermute | solution.py:253
  112.2 11.3 %collective-permute-start.44 = (f32[64,1024]{1,0:T(8,128)S(1)}, f32[64,1024]{1,0:T(8,128)S(1)}, u32[]{:S(2)}, u32[]{:S(2)}) collective-permute-start(f32[64,1024]{1,0:T(8,128)S(1)} %broadcast_select_fusion), channel_id=1, source_target_pairs={{0,1},{1,0},{2,3},{3,2},{4,5},{5,4},{6,7},{7,6},{8,9},{9,8},{10,11... | collective-permute-start | bytes 786440 | tf_op jit(solution)/shard_map/ppermute | solution.py:259
  125.4 9.4 %collective-permute-start.43 = (f32[32,1024]{1,0:T(8,128)S(1)}, f32[32,1024]{1,0:T(8,128)S(1)}, u32[]{:S(2)}, u32[]{:S(2)}) collective-permute-start(f32[32,1024]{1,0:T(8,128)S(1)} %get-tuple-element.320), channel_id=1, source_target_pairs={{0,2},{1,3},{2,0},{3,1},{4,6},{5,7},{6,4},{7,5},{8,10},{9,11},{10,... | collective-permute-start | bytes 393224 | tf_op jit(solution)/shard_map/ppermute | solution.py:259
  125.5 11.0 %collective-permute-start.49 = (f32[32,1024]{1,0:T(8,128)S(1)}, f32[32,1024]{1,0:T(8,128)S(1)}, u32[]{:S(2)}, u32[]{:S(2)}) collective-permute-start(f32[32,1024]{1,0:T(8,128)S(1)} %get-tuple-element.310), channel_id=1, source_target_pairs={{0,2},{1,3},{2,0},{3,1},{4,6},{5,7},{6,4},{7,5},{8,10},{9,11},{10,... | collective-permute-start | bytes 393224 | tf_op jit(solution)/shard_map/ppermute | solution.py:259
  (24 other events, 238.1 us)

commit v16 on v15

--- a/solution.py
+++ b/solution.py
@@ -16,7 +16,7 @@
 UNITS = tuple((chunk, (half,)) for chunk in range(CHUNKS) for half in range(CORES))
 
 ORDER = (
-    "s00", "p0", "s10", "g00", "s11", "s20", "g01", "p1", "g10", "s21", "f0", "e0", "g11",
+    "s00", "p0", "s10", "g00", "s11", "s20", "g01", "f0", "p1", "g10", "s21", "e0", "g11",
     "p2", "g30", "f1", "e1", "g20", "g31", "r0", "e3", "r1", "x0", "g21", "e6", "z0", "r3",
     "x1", "e2", "r6", "l0", "e4", "z1", "x3", "r2", "e7", "z3", "l1", "x6", "r4", "e5", "z6",
     "l3", "x2", "r7", "x4", "z2", "r5", "x7", "z4", "l2", "z7", "l6", "x5", "z5", "l4", "l7",

time: 140 us -> 140 us (level)
  waiting for transfers between devices: 47.3 us -> 50.5 us
  starting transfers between devices: 56.1 us -> 53.2 us
    ppermute x27, starting transfers between devices: 33.2 us -> 26.8 us  [across(): lax.ppermute(value, 'wide', [(w, w ^ mask) for w in range(wide_count)])]
    ppermute x23, starting transfers between devices: 22.9 us -> 26.5 us  [along(): lax.ppermute(value, 'narrow', [(n, n ^ mask) for n in range(narrow_count)])]
    ppermute x23, waiting for transfers between devices: 29.2 us -> 31.2 us  [along(): lax.ppermute(value, 'narrow', [(n, n ^ mask) for n in range(narrow_count)])]
  transfers between devices with their start and end apart: 50 -> 50, of which waited for: 24 -> 25; matrix products, arithmetic and copies ran while one was open for 2% -> 2% of each run, Pallas kernels for 22% -> 22%
where the time goes in v16:
time: 140 us
  starting transfers between devices  53.2 us (38%)
  waiting for transfers between devices  50.5 us (36%)
  Pallas kernels  32.2 us (23%)
  other arithmetic  1.78 us (1%)
  local copies, waits for them, and re-layouts  1.69 us (1%)
    ppermute x23, waiting for transfers between devices, along(): lax.ppermute(value, 'narrow', [(n, n ^ mask) for n in range(narrow_count)])  31.2 us
    ppermute x27, starting transfers between devices, across(): lax.ppermute(value, 'wide', [(w, w ^ mask) for w in range(wide_count)])  26.8 us
    ppermute x23, starting transfers between devices, along(): lax.ppermute(value, 'narrow', [(n, n ^ mask) for n in range(narrow_count)])  26.5 us
    pallas_call x8, Pallas kernels, product(): pl.pallas_call(functools.partial(product_kernel, count, rows, layout, tar...  19.6 us
    ppermute x27, waiting for transfers between devices, across(): lax.ppermute(value, 'wide', [(w, w ^ mask) for w in range(wide_count)])  19.3 us
    pallas_call x2, Pallas kernels, split(): pl.pallas_call(functools.partial(split_kernel, step), in_specs=[HBM], out...  8.51 us
  transfers between devices with their start and end apart: 50, of which 25 were waited for; matrix products, arithmetic and copies ran while one was open for 2% of the time, Pallas kernels for 22%

profile of v16, /device:TPU:0, one launch (start us, length us, event | category | flops | bytes accessed | tf_op | source)
XLA Modules:
  0.0 139.9 jit_solution(9448518902462291616)
XLA Ops:
  2.4 2.6 %collective-permute-start = (f32[8,2048]{1,0:T(8,128)S(1)}, f32[8,2048]{1,0:T(8,128)S(1)}, u32[]{:S(2)}, u32[]{:S(2)}) collective-permute-start(f32[8,2048]{1,0:T(8,128)S(1)} %get-tuple-element.166), channel_id=1, source_target_pairs={{0,1},{1,0},{2,3},{3,2},{4,5},{5,4},{6,7},{7,6},{8,9},{9,8},{10,11... | collective-permute-start | bytes 196616 | tf_op jit(solution)/shard_map/ppermute | solution.py:259
  5.0 2.6 %collective-permute-start.1 = (f32[8,2048]{1,0:T(8,128)S(1)}, f32[8,2048]{1,0:T(8,128)S(1)}, u32[]{:S(2)}, u32[]{:S(2)}) collective-permute-start(f32[8,2048]{1,0:T(8,128)S(1)} %get-tuple-element.167), channel_id=1, source_target_pairs={{0,2},{1,3},{2,0},{3,1},{4,6},{5,7},{6,4},{7,5},{8,10},{9,11},{10,... | collective-permute-start | bytes 196616 | tf_op jit(solution)/shard_map/ppermute | solution.py:259
  7.8 4.2 %collective-permute-done.1.refs_2_ = f32[8,2048]{1,0:T(8,128)S(1)} collective-permute-done((f32[8,2048]{1,0:T(8,128)S(1)}, f32[8,2048]{1,0:T(8,128)S(1)}, u32[]{:S(2)}, u32[]{:S(2)}) %collective-permute-start.1) | collective-permute-done | bytes 65568 | tf_op jit(solution)/shard_map/ppermute | solution.py:259
  12.0 1.8 %collective-permute-done.2.refs_3_ = f32[8,2048]{1,0:T(8,128)S(1)} collective-permute-done((f32[8,2048]{1,0:T(8,128)S(1)}, f32[8,2048]{1,0:T(8,128)S(1)}, u32[]{:S(2)}, u32[]{:S(2)}) %collective-permute-start.2) | collective-permute-done | bytes 65568 | tf_op jit(solution)/shard_map/ppermute | solution.py:259
  26.7 4.3 %split.2 = (bf16[2048,1024]{1,0:T(8,128)(2,1)S(1)}, bf16[2048,1024]{1,0:T(8,128)(2,1)S(1)}, f32[8,128]{1,0:T(8,128)}) custom-call(f32[2048,1024]{1,0:T(8,128)} %whole_ref.2), custom_call_target="tpu_custom_call" | custom-call | flops 1 | bytes 1 | tf_op jit(solution)/shard_map/split/pallas_call | solution.py:123
  33.9 2.4 %product.8 = (f32[64,1024]{1,0:T(8,128)S(1)}, f32[64,1024]{1,0:T(8,128)S(1)}) custom-call(s32[3]{0:T(128)S(1)} %pad_add_fusion.place_ref, s32[8,64]{1,0:T(8,128)S(1)} %copy-done.3, s32[8]{0:T(128)S(1)} %copy-done.4, f32[32,2048]{1,0:T(8,128)S(1)} %pack.3.refs_0_, f32[32,2048]{1,0:T(8,128)S(1)} %collective-permute-done.3.refs_1_, ...), custom_call_target="tpu_custom_call" | custom-call | flops 3221225472 | bytes 1 | tf_op jit(solution)/shard_map/product/pallas_call | solution.py:184
  36.9 2.9 %collective-permute-done.12.refs_1_ = f32[32,2048]{1,0:T(8,128)S(1)} collective-permute-done((f32[32,2048]{1,0:T(8,128)S(1)}, f32[32,2048]{1,0:T(8,128)S(1)}, u32[]{:S(2)}, u32[]{:S(2)}) %collective-permute-start.12) | collective-permute-done | bytes 262176 | tf_op jit(solution)/shard_map/ppermute | solution.py:253
  40.0 4.7 %collective-permute-done.11.refs_2_.refs_3_ = f32[32,2048]{1,0:T(8,128)S(1)} collective-permute-done((f32[32,2048]{1,0:T(8,128)S(1)}, f32[32,2048]{1,0:T(8,128)S(1)}, u32[]{:S(2)}, u32[]{:S(2)}) %collective-permute-start.11) | collective-permute-done | bytes 262176 | tf_op jit(solution)/shard_map/ppermute | solution.py:259
  45.9 4.3 %split.3 = (bf16[2048,1024]{1,0:T(8,128)(2,1)S(1)}, bf16[2048,1024]{1,0:T(8,128)(2,1)S(1)}, f32[8,128]{1,0:T(8,128)}) custom-call(f32[2048,1024]{1,0:T(8,128)} %collective-permute-done.14.whole_ref), custom_call_target="tpu_custom_call" | custom-call | flops 1 | bytes 1 | tf_op jit(solution)/shard_map/split/pallas_call | solution.py:123
  50.2 2.5 %product.9 = (f32[64,1024]{1,0:T(8,128)S(1)}, f32[64,1024]{1,0:T(8,128)S(1)}) custom-call(s32[3]{0:T(128)S(1)} %pad_add_fusion.place_ref, s32[8,64]{1,0:T(8,128)S(1)} %copy-done.3, s32[8]{0:T(128)S(1)} %copy-done.4, f32[32,2048]{1,0:T(8,128)S(1)} %pack.3.refs_0_, f32[32,2048]{1,0:T(8,128)S(1)} %collective-permute-done.3.refs_1_, ...), custom_call_target="tpu_custom_call" | custom-call | flops 3221225472 | bytes 1 | tf_op jit(solution)/shard_map/product/pallas_call | solution.py:184
  55.5 2.5 %product.10 = (f32[64,1024]{1,0:T(8,128)S(1)}, f32[64,1024]{1,0:T(8,128)S(1)}) custom-call(s32[3]{0:T(128)S(1)} %pad_add_fusion.place_ref, s32[8,64]{1,0:T(8,128)S(1)} %copy-done.3, s32[8]{0:T(128)S(1)} %copy-done.4, f32[32,2048]{1,0:T(8,128)S(1)} %pack.4.refs_0_, f32[32,2048]{1,0:T(8,128)S(1)} %collective-permute-done.12.refs_1_, ...), custom_call_target="tpu_custom_call" | custom-call | flops 3221225472 | bytes 1 | tf_op jit(solution)/shard_map/product/pallas_call | solution.py:184
  59.5 2.5 %collective-permute-done.16 = f32[64,1024]{1,0:T(8,128)S(1)} collective-permute-done((f32[64,1024]{1,0:T(8,128)S(1)}, f32[64,1024]{1,0:T(8,128)S(1)}, u32[]{:S(2)}, u32[]{:S(2)}) %collective-permute-start.16) | collective-permute-done | bytes 262176 | tf_op jit(solution)/shard_map/ppermute | solution.py:253
  62.1 1.9 %collective-permute-done.15 = f32[64,1024]{1,0:T(8,128)S(1)} collective-permute-done((f32[64,1024]{1,0:T(8,128)S(1)}, f32[64,1024]{1,0:T(8,128)S(1)}, u32[]{:S(2)}, u32[]{:S(2)}) %collective-permute-start.15) | collective-permute-done | bytes 262176 | tf_op jit(solution)/shard_map/ppermute | solution.py:259
  64.1 1.8 %collective-permute-start.18 = (f32[32,1024]{1,0:T(8,128)S(1)}, f32[32,1024]{1,0:T(8,128)S(1)}, u32[]{:S(2)}, u32[]{:S(2)}) collective-permute-start(f32[32,1024]{1,0:T(8,128)S(1)} %get-tuple-element.349), channel_id=1, source_target_pairs={{0,16},{4,20},{8,24},{12,28},{16,0},{20,4},{24,8},{28,12},{1,17},{... | collective-permute-start | bytes 393224 | tf_op jit(solution)/shard_map/ppermute | solution.py:253
  65.8 1.7 %collective-permute-done.20.refs_1_ = f32[32,2048]{1,0:T(8,128)S(1)} collective-permute-done((f32[32,2048]{1,0:T(8,128)S(1)}, f32[32,2048]{1,0:T(8,128)S(1)}, u32[]{:S(2)}, u32[]{:S(2)}) %collective-permute-start.20) | collective-permute-done | bytes 262176 | tf_op jit(solution)/shard_map/ppermute | solution.py:253
  69.7 2.4 %product.11 = (f32[64,1024]{1,0:T(8,128)S(1)}, f32[64,1024]{1,0:T(8,128)S(1)}) custom-call(s32[3]{0:T(128)S(1)} %pad_add_fusion.place_ref, s32[8,64]{1,0:T(8,128)S(1)} %copy-done.3, s32[8]{0:T(128)S(1)} %copy-done.4, f32[32,2048]{1,0:T(8,128)S(1)} %get-tuple-element.270.refs_0_, f32[32,2048]{1,0:T(8,128)S(1)} %collective-permute-done.13.refs_1_, ...), custom_call_target="tpu_custom_call" | custom-call | flops 3221225472 | bytes 1 | tf_op jit(solution)/shard_map/product/pallas_call | solution.py:184
  73.8 2.4 %collective-permute-start.28 = (f32[64,1024]{1,0:T(8,128)S(1)}, f32[64,1024]{1,0:T(8,128)S(1)}, u32[]{:S(2)}, u32[]{:S(2)}) collective-permute-start(f32[64,1024]{1,0:T(8,128)S(1)} %broadcast_select_fusion.5), channel_id=1, source_target_pairs={{0,1},{1,0},{2,3},{3,2},{4,5},{5,4},{6,7},{7,6},{8,9},{9,8},{10,11... | collective-permute-start | bytes 786440 | tf_op jit(solution)/shard_map/ppermute | solution.py:259
  77.1 2.4 %product.12 = (f32[64,1024]{1,0:T(8,128)S(1)}, f32[64,1024]{1,0:T(8,128)S(1)}) custom-call(s32[3]{0:T(128)S(1)} %pad_add_fusion.place_ref, s32[8,64]{1,0:T(8,128)S(1)} %copy-done.3, s32[8]{0:T(128)S(1)} %copy-done.4, f32[32,2048]{1,0:T(8,128)S(1)} %pack.4.refs_0_, f32[32,2048]{1,0:T(8,128)S(1)} %collective-permute-done.12.refs_1_, ...), custom_call_target="tpu_custom_call" | custom-call | flops 3221225472 | bytes 1 | tf_op jit(solution)/shard_map/product/pallas_call | solution.py:184
  82.7 2.4 %product.13 = (f32[64,1024]{1,0:T(8,128)S(1)}, f32[64,1024]{1,0:T(8,128)S(1)}) custom-call(s32[3]{0:T(128)S(1)} %pad_add_fusion.place_ref, s32[8,64]{1,0:T(8,128)S(1)} %copy-done.3, s32[8]{0:T(128)S(1)} %copy-done.4, f32[32,2048]{1,0:T(8,128)S(1)} %get-tuple-element.283.refs_0_, f32[32,2048]{1,0:T(8,128)S(1)} %collective-permute-done.20.refs_1_, ...), custom_call_target="tpu_custom_call" | custom-call | flops 3221225472 | bytes 1 | tf_op jit(solution)/shard_map/product/pallas_call | solution.py:184
  86.0 2.1 %collective-permute-start.27 = (f32[32,1024]{1,0:T(8,128)S(1)}, f32[32,1024]{1,0:T(8,128)S(1)}, u32[]{:S(2)}, u32[]{:S(2)}) collective-permute-start(f32[32,1024]{1,0:T(8,128)S(1)} %get-tuple-element.343), channel_id=1, source_target_pairs={{0,2},{1,3},{2,0},{3,1},{4,6},{5,7},{6,4},{7,5},{8,10},{9,11},{10,... | collective-permute-start | bytes 393224 | tf_op jit(solution)/shard_map/ppermute | solution.py:259
  89.1 2.5 %product.14 = (f32[64,1024]{1,0:T(8,128)S(1)}, f32[64,1024]{1,0:T(8,128)S(1)}) custom-call(s32[3]{0:T(128)S(1)} %pad_add_fusion.place_ref, s32[8,64]{1,0:T(8,128)S(1)} %copy-done.3, s32[8]{0:T(128)S(1)} %copy-done.4, f32[32,2048]{1,0:T(8,128)S(1)} %get-tuple-element.270.refs_0_, f32[32,2048]{1,0:T(8,128)S(1)} %collective-permute-done.13.refs_1_, ...), custom_call_target="tpu_custom_call" | custom-call | flops 3221225472 | bytes 1 | tf_op jit(solution)/shard_map/product/pallas_call | solution.py:184
  91.6 2.5 %collective-permute-done.29 = f32[32,1024]{1,0:T(8,128)S(1)} collective-permute-done((f32[32,1024]{1,0:T(8,128)S(1)}, f32[32,1024]{1,0:T(8,128)S(1)}, u32[]{:S(2)}, u32[]{:S(2)}) %collective-permute-start.29) | collective-permute-done | bytes 131104 | tf_op jit(solution)/shard_map/ppermute | solution.py:253
  99.0 2.5 %product.15 = (f32[64,1024]{1,0:T(8,128)S(1)}, f32[64,1024]{1,0:T(8,128)S(1)}) custom-call(s32[3]{0:T(128)S(1)} %pad_add_fusion.place_ref, s32[8,64]{1,0:T(8,128)S(1)} %copy-done.3, s32[8]{0:T(128)S(1)} %copy-done.4, f32[32,2048]{1,0:T(8,128)S(1)} %get-tuple-element.283.refs_0_, f32[32,2048]{1,0:T(8,128)S(1)} %collective-permute-done.20.refs_1_, ...), custom_call_target="tpu_custom_call" | custom-call | flops 3221225472 | bytes 1 | tf_op jit(solution)/shard_map/product/pallas_call | solution.py:184
  106.1 2.6 %collective-permute-start.41 = (f32[64,1024]{1,0:T(8,128)S(1)}, f32[64,1024]{1,0:T(8,128)S(1)}, u32[]{:S(2)}, u32[]{:S(2)}) collective-permute-start(f32[64,1024]{1,0:T(8,128)S(1)} %broadcast_select_fusion.1), channel_id=1, source_target_pairs={{0,1},{1,0},{2,3},{3,2},{4,5},{5,4},{6,7},{7,6},{8,9},{9,8},{10,11... | collective-permute-start | bytes 786440 | tf_op jit(solution)/shard_map/ppermute | solution.py:259
  108.8 2.6 %collective-permute-done.37 = f32[64,1024]{1,0:T(8,128)S(1)} collective-permute-done((f32[64,1024]{1,0:T(8,128)S(1)}, f32[64,1024]{1,0:T(8,128)S(1)}, u32[]{:S(2)}, u32[]{:S(2)}) %collective-permute-start.37) | collective-permute-done | bytes 262176 | tf_op jit(solution)/shard_map/ppermute | solution.py:259
  112.1 2.6 %collective-permute-start.44 = (f32[64,1024]{1,0:T(8,128)S(1)}, f32[64,1024]{1,0:T(8,128)S(1)}, u32[]{:S(2)}, u32[]{:S(2)}) collective-permute-start(f32[64,1024]{1,0:T(8,128)S(1)} %broadcast_select_fusion), channel_id=1, source_target_pairs={{0,1},{1,0},{2,3},{3,2},{4,5},{5,4},{6,7},{7,6},{8,9},{9,8},{10,11... | collective-permute-start | bytes 786440 | tf_op jit(solution)/shard_map/ppermute | solution.py:259
  114.6 3.2 %collective-permute-done.41 = f32[64,1024]{1,0:T(8,128)S(1)} collective-permute-done((f32[64,1024]{1,0:T(8,128)S(1)}, f32[64,1024]{1,0:T(8,128)S(1)}, u32[]{:S(2)}, u32[]{:S(2)}) %collective-permute-start.41) | collective-permute-done | bytes 262176 | tf_op jit(solution)/shard_map/ppermute | solution.py:259
  119.2 3.7 %collective-permute-done.46 = f32[32,1024]{1,0:T(8,128)S(1)} collective-permute-done((f32[32,1024]{1,0:T(8,128)S(1)}, f32[32,1024]{1,0:T(8,128)S(1)}, u32[]{:S(2)}, u32[]{:S(2)}) %collective-permute-start.46) | collective-permute-done | bytes 131104 | tf_op jit(solution)/shard_map/ppermute | solution.py:253
  124.2 2.9 %collective-permute-start.49 = (f32[32,1024]{1,0:T(8,128)S(1)}, f32[32,1024]{1,0:T(8,128)S(1)}, u32[]{:S(2)}, u32[]{:S(2)}) collective-permute-start(f32[32,1024]{1,0:T(8,128)S(1)} %get-tuple-element.320), channel_id=1, source_target_pairs={{0,2},{1,3},{2,0},{3,1},{4,6},{5,7},{6,4},{7,5},{8,10},{9,11},{10,... | collective-permute-start | bytes 393224 | tf_op jit(solution)/shard_map/ppermute | solution.py:259
  128.9 6.1 %collective-permute-done.43.refs_9_ = f32[32,1024]{1,0:T(8,128)S(1)} collective-permute-done((f32[32,1024]{1,0:T(8,128)S(1)}, f32[32,1024]{1,0:T(8,128)S(1)}, u32[]{:S(2)}, u32[]{:S(2)}) %collective-permute-start.43) | collective-permute-done | bytes 131104 | tf_op jit(solution)/shard_map/ppermute | solution.py:259
  135.0 1.8 %collective-permute-done.49.refs_15_ = f32[32,1024]{1,0:T(8,128)S(1)} collective-permute-done((f32[32,1024]{1,0:T(8,128)S(1)}, f32[32,1024]{1,0:T(8,128)S(1)}, u32[]{:S(2)}, u32[]{:S(2)}) %collective-permute-start.49) | collective-permute-done | bytes 131104 | tf_op jit(solution)/shard_map/ppermute | solution.py:259
  138.2 1.8 %finish.1 = f32[128,2048]{1,0:T(8,128)} custom-call(s32[3]{0:T(128)S(1)} %pad_add_fusion.place_ref, f32[128,2048]{1,0:T(8,128)S(1)} %copy-done, f32[128,1]{1,0:T(8,128)S(1)} %copy.8.occ_ref, f32[1,2048]{1,0:T(1,128)S(1)} %bitcast.5, f32[32,1024]{1,0:T(8,128)S(1)} %get-tuple-element.257.refs_0_, f32[32,1024]{1,0:T(8,128)S(1)} %collective-permute-done.21.refs_1_, ...), custom_call_target="tpu_custom_call" | custom-call | flops 1 | bytes 1 | tf_op jit(solution)/shard_map/finish/pallas_call | solution.py:220
  (143 shorter events, 50.4 us)
Async XLA Ops:
  0.0 45.9 %collective-permute-start.14 = (f32[2048,1024]{1,0:T(8,128)}, f32[2048,1024]{1,0:T(8,128)}, u32[]{:S(2)}, u32[]{:S(2)}) collective-permute-start(f32[2048,1024]{1,0:T(8,128)} %whole_ref.2), channel_id=1, source_target_pairs={{0,4},{4,0},{8,12},{12,8},{16,20},{20,16},{24,28},{28,24},{1,5},{5... | collective-permute-start | bytes 25165832 | tf_op jit(solution)/shard_map/ppermute | solution.py:253
  19.4 13.7 %collective-permute-start.8 = (f32[32,2048]{1,0:T(8,128)S(1)}, f32[32,2048]{1,0:T(8,128)S(1)}, u32[]{:S(2)}, u32[]{:S(2)}) collective-permute-start(f32[32,2048]{1,0:T(8,128)S(1)} %get-tuple-element.180), channel_id=1, source_target_pairs={{0,1},{1,0},{2,3},{3,2},{4,5},{5,4},{6,7},{7,6},{8,9},{9,8},{10,11... | collective-permute-start | bytes 786440 | tf_op jit(solution)/shard_map/ppermute | solution.py:259
  20.8 10.1 %collective-permute-start.9 = (f32[16,2048]{1,0:T(8,128)S(1)}, f32[16,2048]{1,0:T(8,128)S(1)}, u32[]{:S(2)}, u32[]{:S(2)}) collective-permute-start(f32[16,2048]{1,0:T(8,128)S(1)} %pad_maximum_fusion.1), channel_id=1, source_target_pairs={{0,2},{1,3},{2,0},{3,1},{4,6},{5,7},{6,4},{7,5},{8,10},{9,11},{10,... | collective-permute-start | bytes 393224 | tf_op jit(solution)/shard_map/ppermute | solution.py:259
  24.5 9.4 %collective-permute-start.6 = (f32[16,2048]{1,0:T(8,128)S(1)}, f32[16,2048]{1,0:T(8,128)S(1)}, u32[]{:S(2)}, u32[]{:S(2)}) collective-permute-start(f32[16,2048]{1,0:T(8,128)S(1)} %slice.68), channel_id=1, source_target_pairs={{0,16},{4,20},{8,24},{12,28},{16,0},{20,4},{24,8},{28,12},{1,17},{... | collective-permute-start | bytes 393224 | tf_op jit(solution)/shard_map/ppermute | solution.py:253
  33.1 11.6 %collective-permute-start.11 = (f32[32,2048]{1,0:T(8,128)S(1)}, f32[32,2048]{1,0:T(8,128)S(1)}, u32[]{:S(2)}, u32[]{:S(2)}) collective-permute-start(f32[32,2048]{1,0:T(8,128)S(1)} %pad_maximum_fusion), channel_id=1, source_target_pairs={{0,2},{1,3},{2,0},{3,1},{4,6},{5,7},{6,4},{7,5},{8,10},{9,11},{10,... | collective-permute-start | bytes 786440 | tf_op jit(solution)/shard_map/ppermute | solution.py:259
  36.3 19.0 %collective-permute-start.10 = (f32[64,1024]{1,0:T(8,128)S(1)}, f32[64,1024]{1,0:T(8,128)S(1)}, u32[]{:S(2)}, u32[]{:S(2)}) collective-permute-start(f32[64,1024]{1,0:T(8,128)S(1)} %get-tuple-element.201), channel_id=1, source_target_pairs={{0,8},{4,12},{8,0},{12,4},{16,24},{20,28},{24,16},{28,20},{1,9},{5... | collective-permute-start | bytes 786440 | tf_op jit(solution)/shard_map/ppermute | solution.py:253
  39.9 15.6 %collective-permute-start.17 = (f32[64,2048]{1,0:T(8,128)S(1)}, f32[64,2048]{1,0:T(8,128)S(1)}, u32[]{:S(2)}, u32[]{:S(2)}) collective-permute-start(f32[64,2048]{1,0:T(8,128)S(1)} %constant_dynamic-update-slice_fusion), channel_id=1, source_target_pairs={{0,16},{4,20},{8,24},{12,28},{16,0},{20,4},{24,8},{28,12},{1,17},{... | collective-permute-start | bytes 1572872 | tf_op jit(solution)/shard_map/ppermute | solution.py:253
  45.3 9.5 %collective-permute-start.13 = (f32[32,2048]{1,0:T(8,128)S(1)}, f32[32,2048]{1,0:T(8,128)S(1)}, u32[]{:S(2)}, u32[]{:S(2)}) collective-permute-start(f32[32,2048]{1,0:T(8,128)S(1)} %get-tuple-element.270.refs_0_), channel_id=1, source_target_pairs={{0,8},{4,12},{8,0},{12,4},{16,24},{20,28},{24,16},{28,20},{1,9},{5... | collective-permute-start | bytes 786440 | tf_op jit(solution)/shard_map/ppermute | solution.py:253
  52.6 9.3 %collective-permute-start.16 = (f32[64,1024]{1,0:T(8,128)S(1)}, f32[64,1024]{1,0:T(8,128)S(1)}, u32[]{:S(2)}, u32[]{:S(2)}) collective-permute-start(f32[64,1024]{1,0:T(8,128)S(1)} %get-tuple-element.221), channel_id=1, source_target_pairs={{0,8},{4,12},{8,0},{12,4},{16,24},{20,28},{24,16},{28,20},{1,9},{5... | collective-permute-start | bytes 786440 | tf_op jit(solution)/shard_map/ppermute | solution.py:253
  54.2 13.4 %collective-permute-start.20 = (f32[32,2048]{1,0:T(8,128)S(1)}, f32[32,2048]{1,0:T(8,128)S(1)}, u32[]{:S(2)}, u32[]{:S(2)}) collective-permute-start(f32[32,2048]{1,0:T(8,128)S(1)} %get-tuple-element.283.refs_0_), channel_id=1, source_target_pairs={{0,8},{4,12},{8,0},{12,4},{16,24},{20,28},{24,16},{28,20},{1,9},{5... | collective-permute-start | bytes 786440 | tf_op jit(solution)/shard_map/ppermute | solution.py:253
  54.8 14.9 %collective-permute-start.19 = (f32[64,2048]{1,0:T(8,128)S(1)}, f32[64,2048]{1,0:T(8,128)S(1)}, u32[]{:S(2)}, u32[]{:S(2)}) collective-permute-start(f32[64,2048]{1,0:T(8,128)S(1)} %constant_dynamic-update-slice_fusion.2), channel_id=1, source_target_pairs={{0,16},{4,20},{8,24},{12,28},{16,0},{20,4},{24,8},{28,12},{1,17},{... | collective-permute-start | bytes 1572872 | tf_op jit(solution)/shard_map/ppermute | solution.py:253
  58.0 15.8 %collective-permute-start.24 = (f32[64,1024]{1,0:T(8,128)S(1)}, f32[64,1024]{1,0:T(8,128)S(1)}, u32[]{:S(2)}, u32[]{:S(2)}) collective-permute-start(f32[64,1024]{1,0:T(8,128)S(1)} %get-tuple-element.232), channel_id=1, source_target_pairs={{0,8},{4,12},{8,0},{12,4},{16,24},{20,28},{24,16},{28,20},{1,9},{5... | collective-permute-start | bytes 786440 | tf_op jit(solution)/shard_map/ppermute | solution.py:253
  62.0 14.3 %collective-permute-start.23 = (f32[64,1024]{1,0:T(8,128)S(1)}, f32[64,1024]{1,0:T(8,128)S(1)}, u32[]{:S(2)}, u32[]{:S(2)}) collective-permute-start(f32[64,1024]{1,0:T(8,128)S(1)} %broadcast_select_fusion.6), channel_id=1, source_target_pairs={{0,1},{1,0},{2,3},{3,2},{4,5},{5,4},{6,7},{7,6},{8,9},{9,8},{10,11... | collective-permute-start | bytes 786440 | tf_op jit(solution)/shard_map/ppermute | solution.py:259
  64.1 9.6 %collective-permute-start.18 = (f32[32,1024]{1,0:T(8,128)S(1)}, f32[32,1024]{1,0:T(8,128)S(1)}, u32[]{:S(2)}, u32[]{:S(2)}) collective-permute-start(f32[32,1024]{1,0:T(8,128)S(1)} %get-tuple-element.349), channel_id=1, source_target_pairs={{0,16},{4,20},{8,24},{12,28},{16,0},{20,4},{24,8},{28,12},{1,17},{... | collective-permute-start | bytes 393224 | tf_op jit(solution)/shard_map/ppermute | solution.py:253
  67.6 15.1 %collective-permute-start.26 = (f32[64,2048]{1,0:T(8,128)S(1)}, f32[64,2048]{1,0:T(8,128)S(1)}, u32[]{:S(2)}, u32[]{:S(2)}) collective-permute-start(f32[64,2048]{1,0:T(8,128)S(1)} %constant_dynamic-update-slice_fusion.4), channel_id=1, source_target_pairs={{0,16},{4,20},{8,24},{12,28},{16,0},{20,4},{24,8},{28,12},{1,17},{... | collective-permute-start | bytes 1572872 | tf_op jit(solution)/shard_map/ppermute | solution.py:253
  72.1 8.9 %collective-permute-start.22 = (f32[64,1024]{1,0:T(8,128)S(1)}, f32[64,1024]{1,0:T(8,128)S(1)}, u32[]{:S(2)}, u32[]{:S(2)}) collective-permute-start(f32[64,1024]{1,0:T(8,128)S(1)} %get-tuple-element.243), channel_id=1, source_target_pairs={{0,8},{4,12},{8,0},{12,4},{16,24},{20,28},{24,16},{28,20},{1,9},{5... | collective-permute-start | bytes 786440 | tf_op jit(solution)/shard_map/ppermute | solution.py:253
  73.7 8.9 %collective-permute-start.21 = (f32[32,1024]{1,0:T(8,128)S(1)}, f32[32,1024]{1,0:T(8,128)S(1)}, u32[]{:S(2)}, u32[]{:S(2)}) collective-permute-start(f32[32,1024]{1,0:T(8,128)S(1)} %get-tuple-element.347), channel_id=1, source_target_pairs={{0,2},{1,3},{2,0},{3,1},{4,6},{5,7},{6,4},{7,5},{8,10},{9,11},{10,... | collective-permute-start | bytes 393224 | tf_op jit(solution)/shard_map/ppermute | solution.py:259
  73.8 14.3 %collective-permute-start.28 = (f32[64,1024]{1,0:T(8,128)S(1)}, f32[64,1024]{1,0:T(8,128)S(1)}, u32[]{:S(2)}, u32[]{:S(2)}) collective-permute-start(f32[64,1024]{1,0:T(8,128)S(1)} %broadcast_select_fusion.5), channel_id=1, source_target_pairs={{0,1},{1,0},{2,3},{3,2},{4,5},{5,4},{6,7},{7,6},{8,9},{9,8},{10,11... | collective-permute-start | bytes 786440 | tf_op jit(solution)/shard_map/ppermute | solution.py:259
  76.5 9.5 %collective-permute-start.25 = (f32[32,1024]{1,0:T(8,128)S(1)}, f32[32,1024]{1,0:T(8,128)S(1)}, u32[]{:S(2)}, u32[]{:S(2)}) collective-permute-start(f32[32,1024]{1,0:T(8,128)S(1)} %get-tuple-element.346), channel_id=1, source_target_pairs={{0,16},{4,20},{8,24},{12,28},{16,0},{20,4},{24,8},{28,12},{1,17},{... | collective-permute-start | bytes 393224 | tf_op jit(solution)/shard_map/ppermute | solution.py:253
  82.6 13.6 %collective-permute-start.33 = (f32[64,1024]{1,0:T(8,128)S(1)}, f32[64,1024]{1,0:T(8,128)S(1)}, u32[]{:S(2)}, u32[]{:S(2)}) collective-permute-start(f32[64,1024]{1,0:T(8,128)S(1)} %broadcast_select_fusion.4), channel_id=1, source_target_pairs={{0,1},{1,0},{2,3},{3,2},{4,5},{5,4},{6,7},{7,6},{8,9},{9,8},{10,11... | collective-permute-start | bytes 786440 | tf_op jit(solution)/shard_map/ppermute | solution.py:259
  85.1 12.2 %collective-permute-start.35 = (f32[64,1024]{1,0:T(8,128)S(1)}, f32[64,1024]{1,0:T(8,128)S(1)}, u32[]{:S(2)}, u32[]{:S(2)}) collective-permute-start(f32[64,1024]{1,0:T(8,128)S(1)} %get-tuple-element.264), channel_id=1, source_target_pairs={{0,8},{4,12},{8,0},{12,4},{16,24},{20,28},{24,16},{28,20},{1,9},{5... | collective-permute-start | bytes 786440 | tf_op jit(solution)/shard_map/ppermute | solution.py:253
  86.0 10.1 %collective-permute-start.27 = (f32[32,1024]{1,0:T(8,128)S(1)}, f32[32,1024]{1,0:T(8,128)S(1)}, u32[]{:S(2)}, u32[]{:S(2)}) collective-permute-start(f32[32,1024]{1,0:T(8,128)S(1)} %get-tuple-element.343), channel_id=1, source_target_pairs={{0,2},{1,3},{2,0},{3,1},{4,6},{5,7},{6,4},{7,5},{8,10},{9,11},{10,... | collective-permute-start | bytes 393224 | tf_op jit(solution)/shard_map/ppermute | solution.py:259
  88.9 13.8 %collective-permute-start.31 = (f32[64,1024]{1,0:T(8,128)S(1)}, f32[64,1024]{1,0:T(8,128)S(1)}, u32[]{:S(2)}, u32[]{:S(2)}) collective-permute-start(f32[64,1024]{1,0:T(8,128)S(1)} %broadcast_select_fusion.3), channel_id=1, source_target_pairs={{0,1},{1,0},{2,3},{3,2},{4,5},{5,4},{6,7},{7,6},{8,9},{9,8},{10,11... | collective-permute-start | bytes 786440 | tf_op jit(solution)/shard_map/ppermute | solution.py:259
  94.1 12.0 %collective-permute-start.38 = (f32[64,1024]{1,0:T(8,128)S(1)}, f32[64,1024]{1,0:T(8,128)S(1)}, u32[]{:S(2)}, u32[]{:S(2)}) collective-permute-start(f32[64,1024]{1,0:T(8,128)S(1)} %get-tuple-element.275), channel_id=1, source_target_pairs={{0,8},{4,12},{8,0},{12,4},{16,24},{20,28},{24,16},{28,20},{1,9},{5... | collective-permute-start | bytes 786440 | tf_op jit(solution)/shard_map/ppermute | solution.py:253
  97.4 14.0 %collective-permute-start.37 = (f32[64,1024]{1,0:T(8,128)S(1)}, f32[64,1024]{1,0:T(8,128)S(1)}, u32[]{:S(2)}, u32[]{:S(2)}) collective-permute-start(f32[64,1024]{1,0:T(8,128)S(1)} %broadcast_select_fusion.2), channel_id=1, source_target_pairs={{0,1},{1,0},{2,3},{3,2},{4,5},{5,4},{6,7},{7,6},{8,9},{9,8},{10,11... | collective-permute-start | bytes 786440 | tf_op jit(solution)/shard_map/ppermute | solution.py:259
  102.7 9.4 %collective-permute-start.42 = (f32[64,1024]{1,0:T(8,128)S(1)}, f32[64,1024]{1,0:T(8,128)S(1)}, u32[]{:S(2)}, u32[]{:S(2)}) collective-permute-start(f32[64,1024]{1,0:T(8,128)S(1)} %get-tuple-element.288), channel_id=1, source_target_pairs={{0,8},{4,12},{8,0},{12,4},{16,24},{20,28},{24,16},{28,20},{1,9},{5... | collective-permute-start | bytes 786440 | tf_op jit(solution)/shard_map/ppermute | solution.py:253
  103.3 19.7 %collective-permute-start.45 = (f32[32,1024]{1,0:T(8,128)S(1)}, f32[32,1024]{1,0:T(8,128)S(1)}, u32[]{:S(2)}, u32[]{:S(2)}) collective-permute-start(f32[32,1024]{1,0:T(8,128)S(1)} %get-tuple-element.328), channel_id=1, source_target_pairs={{0,2},{1,3},{2,0},{3,1},{4,6},{5,7},{6,4},{7,5},{8,10},{9,11},{10,... | collective-permute-start | bytes 393224 | tf_op jit(solution)/shard_map/ppermute | solution.py:259
  106.1 11.6 %collective-permute-start.41 = (f32[64,1024]{1,0:T(8,128)S(1)}, f32[64,1024]{1,0:T(8,128)S(1)}, u32[]{:S(2)}, u32[]{:S(2)}) collective-permute-start(f32[64,1024]{1,0:T(8,128)S(1)} %broadcast_select_fusion.1), channel_id=1, source_target_pairs={{0,1},{1,0},{2,3},{3,2},{4,5},{5,4},{6,7},{7,6},{8,9},{9,8},{10,11... | collective-permute-start | bytes 786440 | tf_op jit(solution)/shard_map/ppermute | solution.py:259
  112.1 10.9 %collective-permute-start.44 = (f32[64,1024]{1,0:T(8,128)S(1)}, f32[64,1024]{1,0:T(8,128)S(1)}, u32[]{:S(2)}, u32[]{:S(2)}) collective-permute-start(f32[64,1024]{1,0:T(8,128)S(1)} %broadcast_select_fusion), channel_id=1, source_target_pairs={{0,1},{1,0},{2,3},{3,2},{4,5},{5,4},{6,7},{7,6},{8,9},{9,8},{10,11... | collective-permute-start | bytes 786440 | tf_op jit(solution)/shard_map/ppermute | solution.py:259
  124.2 10.7 %collective-permute-start.43 = (f32[32,1024]{1,0:T(8,128)S(1)}, f32[32,1024]{1,0:T(8,128)S(1)}, u32[]{:S(2)}, u32[]{:S(2)}) collective-permute-start(f32[32,1024]{1,0:T(8,128)S(1)} %get-tuple-element.330), channel_id=1, source_target_pairs={{0,2},{1,3},{2,0},{3,1},{4,6},{5,7},{6,4},{7,5},{8,10},{9,11},{10,... | collective-permute-start | bytes 393224 | tf_op jit(solution)/shard_map/ppermute | solution.py:259
  124.2 12.5 %collective-permute-start.49 = (f32[32,1024]{1,0:T(8,128)S(1)}, f32[32,1024]{1,0:T(8,128)S(1)}, u32[]{:S(2)}, u32[]{:S(2)}) collective-permute-start(f32[32,1024]{1,0:T(8,128)S(1)} %get-tuple-element.320), channel_id=1, source_target_pairs={{0,2},{1,3},{2,0},{3,1},{4,6},{5,7},{6,4},{7,5},{8,10},{9,11},{10,... | collective-permute-start | bytes 393224 | tf_op jit(solution)/shard_map/ppermute | solution.py:259
  128.8 9.4 %collective-permute-start.48 = (f32[32,1024]{1,0:T(8,128)}, f32[32,1024]{1,0:T(8,128)S(1)}, u32[]{:S(2)}, u32[]{:S(2)}) collective-permute-start(f32[32,1024]{1,0:T(8,128)} %get-tuple-element.322), channel_id=1, source_target_pairs={{0,2},{1,3},{2,0},{3,1},{4,6},{5,7},{6,4},{7,5},{8,10},{9,11},{10,... | collective-permute-start | bytes 393224 | tf_op jit(solution)/shard_map/ppermute | solution.py:259
  (24 other events, 235.8 us)

commit v17 on v16

--- a/solution.py
+++ b/solution.py
@@ -16,11 +16,10 @@
 UNITS = tuple((chunk, (half,)) for chunk in range(CHUNKS) for half in range(CORES))
 
 ORDER = (
-    "s00", "p0", "s10", "g00", "s11", "s20", "g01", "f0", "p1", "g10", "s21", "e0", "g11",
-    "p2", "g30", "f1", "e1", "g20", "g31", "r0", "e3", "r1", "x0", "g21", "e6", "z0", "r3",
-    "x1", "e2", "r6", "l0", "e4", "z1", "x3", "r2", "e7", "z3", "l1", "x6", "r4", "e5", "z6",
-    "l3", "x2", "r7", "x4", "z2", "r5", "x7", "z4", "l2", "z7", "l6", "x5", "z5", "l4", "l7",
-    "l5",
+    "s00", "p0", "s10", "g00", "s11", "s20", "g01", "f0", "p1", "g10", "s21", "e0", "f1", "e1",
+    "g11", "r0", "p2", "g20", "r1", "g30", "x0", "g21", "e3", "z0", "e2", "x1", "g31", "r3",
+    "l0", "e4", "z1", "r2", "e5", "x3", "r4", "l1", "e7", "z3", "x2", "r5", "e6", "z2", "x4",
+    "r7", "l3", "x5", "z4", "l2", "r6", "z5", "x7", "l4", "x6", "z7", "l5", "z6", "l7", "l6",
 )
 
 SMEM = pl.BlockSpec(memory_space=pltpu.SMEM)

time: 140 us -> 140 us (level)
  local copies, waits for them, and re-layouts: 1.69 us -> 5.05 us
  waiting for transfers between devices: 50.5 us -> 48.3 us
  starting transfers between devices: 53.2 us -> 51.4 us
    ppermute x27, waiting for transfers between devices: 19.3 us -> 15.6 us  [across(): lax.ppermute(value, 'wide', [(w, w ^ mask) for w in range(wide_count)])]
    unnamed x15 -> x33, local copies, waits for them, and re-layouts: 1.31 us -> 4.49 us
    ppermute x27, starting transfers between devices: 26.8 us -> 25 us  [across(): lax.ppermute(value, 'wide', [(w, w ^ mask) for w in range(wide_count)])]
    ppermute x23, waiting for transfers between devices: 31.2 us -> 32.7 us  [along(): lax.ppermute(value, 'narrow', [(n, n ^ mask) for n in range(narrow_count)])]
  transfers between devices with their start and end apart: 50 -> 50, of which waited for: 25 -> 23; matrix products, arithmetic and copies ran while one was open for 2% -> 2% of each run, Pallas kernels for 22% -> 22%
where the time goes in v17:
time: 140 us
  starting transfers between devices  51.4 us (37%)
  waiting for transfers between devices  48.3 us (34%)
  Pallas kernels  32.1 us (23%)
  local copies, waits for them, and re-layouts  5.05 us (4%)
  other arithmetic  2.74 us (2%)
    ppermute x23, waiting for transfers between devices, along(): lax.ppermute(value, 'narrow', [(n, n ^ mask) for n in range(narrow_count)])  32.7 us
    ppermute x23, starting transfers between devices, along(): lax.ppermute(value, 'narrow', [(n, n ^ mask) for n in range(narrow_count)])  26.4 us
    ppermute x27, starting transfers between devices, across(): lax.ppermute(value, 'wide', [(w, w ^ mask) for w in range(wide_count)])  25 us
    pallas_call x8, Pallas kernels, product(): pl.pallas_call(functools.partial(product_kernel, count, rows, layout, tar...  19.5 us
    ppermute x27, waiting for transfers between devices, across(): lax.ppermute(value, 'wide', [(w, w ^ mask) for w in range(wide_count)])  15.6 us
    pallas_call x2, Pallas kernels, split(): pl.pallas_call(functools.partial(split_kernel, step), in_specs=[HBM], out...  8.51 us
    unnamed x33, local copies, waits for them, and re-layouts  4.49 us
  transfers between devices with their start and end apart: 50, of which 23 were waited for; matrix products, arithmetic and copies ran while one was open for 2% of the time, Pallas kernels for 22%

profile of v17, /device:TPU:0, one launch (start us, length us, event | category | flops | bytes accessed | tf_op | source)
XLA Modules:
  0.0 140.3 jit_solution(9461691152050352803)
XLA Ops:
  2.4 2.6 %collective-permute-start = (f32[8,2048]{1,0:T(8,128)S(1)}, f32[8,2048]{1,0:T(8,128)S(1)}, u32[]{:S(2)}, u32[]{:S(2)}) collective-permute-start(f32[8,2048]{1,0:T(8,128)S(1)} %get-tuple-element.166), channel_id=1, source_target_pairs={{0,1},{1,0},{2,3},{3,2},{4,5},{5,4},{6,7},{7,6},{8,9},{9,8},{10,11... | collective-permute-start | bytes 196616 | tf_op jit(solution)/shard_map/ppermute | solution.py:258
  5.0 2.6 %collective-permute-start.1 = (f32[8,2048]{1,0:T(8,128)S(1)}, f32[8,2048]{1,0:T(8,128)S(1)}, u32[]{:S(2)}, u32[]{:S(2)}) collective-permute-start(f32[8,2048]{1,0:T(8,128)S(1)} %get-tuple-element.167), channel_id=1, source_target_pairs={{0,2},{1,3},{2,0},{3,1},{4,6},{5,7},{6,4},{7,5},{8,10},{9,11},{10,... | collective-permute-start | bytes 196616 | tf_op jit(solution)/shard_map/ppermute | solution.py:258
  7.8 4.2 %collective-permute-done.1.refs_2_ = f32[8,2048]{1,0:T(8,128)S(1)} collective-permute-done((f32[8,2048]{1,0:T(8,128)S(1)}, f32[8,2048]{1,0:T(8,128)S(1)}, u32[]{:S(2)}, u32[]{:S(2)}) %collective-permute-start.1) | collective-permute-done | bytes 65568 | tf_op jit(solution)/shard_map/ppermute | solution.py:258
  12.0 1.8 %collective-permute-done.2.refs_3_ = f32[8,2048]{1,0:T(8,128)S(1)} collective-permute-done((f32[8,2048]{1,0:T(8,128)S(1)}, f32[8,2048]{1,0:T(8,128)S(1)}, u32[]{:S(2)}, u32[]{:S(2)}) %collective-permute-start.2) | collective-permute-done | bytes 65568 | tf_op jit(solution)/shard_map/ppermute | solution.py:258
  26.7 4.3 %split.2 = (bf16[2048,1024]{1,0:T(8,128)(2,1)S(1)}, bf16[2048,1024]{1,0:T(8,128)(2,1)S(1)}, f32[8,128]{1,0:T(8,128)}) custom-call(f32[2048,1024]{1,0:T(8,128)} %whole_ref.2), custom_call_target="tpu_custom_call" | custom-call | flops 1 | bytes 1 | tf_op jit(solution)/shard_map/split/pallas_call | solution.py:122
  35.0 2.5 %product.8 = (f32[64,1024]{1,0:T(8,128)S(1)}, f32[64,1024]{1,0:T(8,128)S(1)}) custom-call(s32[3]{0:T(128)S(1)} %pad_add_fusion.place_ref, s32[8,64]{1,0:T(8,128)S(1)} %copy-done.12, s32[8]{0:T(128)S(1)} %copy-done.13, f32[32,2048]{1,0:T(8,128)S(1)} %pack.3.refs_0_, f32[32,2048]{1,0:T(8,128)S(1)} %collective-permute-done.3.refs_1_, ...), custom_call_target="tpu_custom_call" | custom-call | flops 3221225472 | bytes 1 | tf_op jit(solution)/shard_map/product/pallas_call | solution.py:183
  38.3 4.3 %split.3 = (bf16[2048,1024]{1,0:T(8,128)(2,1)S(1)}, bf16[2048,1024]{1,0:T(8,128)(2,1)S(1)}, f32[8,128]{1,0:T(8,128)}) custom-call(f32[2048,1024]{1,0:T(8,128)} %collective-permute-done.12.whole_ref), custom_call_target="tpu_custom_call" | custom-call | flops 1 | bytes 1 | tf_op jit(solution)/shard_map/split/pallas_call | solution.py:122
  42.6 2.5 %product.9 = (f32[64,1024]{1,0:T(8,128)S(1)}, f32[64,1024]{1,0:T(8,128)S(1)}) custom-call(s32[3]{0:T(128)S(1)} %pad_add_fusion.place_ref, s32[8,64]{1,0:T(8,128)S(1)} %copy-done.12, s32[8]{0:T(128)S(1)} %copy-done.13, f32[32,2048]{1,0:T(8,128)S(1)} %pack.3.refs_0_, f32[32,2048]{1,0:T(8,128)S(1)} %collective-permute-done.3.refs_1_, ...), custom_call_target="tpu_custom_call" | custom-call | flops 3221225472 | bytes 1 | tf_op jit(solution)/shard_map/product/pallas_call | solution.py:183
  48.2 1.7 %collective-permute-start.13 = (f32[64,1024]{1,0:T(8,128)}, f32[64,1024]{1,0:T(8,128)S(1)}, u32[]{:S(2)}, u32[]{:S(2)}) collective-permute-start(f32[64,1024]{1,0:T(8,128)} %broadcast_select_fusion.7), channel_id=1, source_target_pairs={{0,1},{1,0},{2,3},{3,2},{4,5},{5,4},{6,7},{7,6},{8,9},{9,8},{10,11... | collective-permute-start | bytes 786440 | tf_op jit(solution)/shard_map/ppermute | solution.py:258
  51.7 3.5 %collective-permute-done.15 = f32[64,1024]{1,0:T(8,128)S(1)} collective-permute-done((f32[64,1024]{1,0:T(8,128)S(1)}, f32[64,1024]{1,0:T(8,128)S(1)}, u32[]{:S(2)}, u32[]{:S(2)}) %collective-permute-start.15) | collective-permute-done | bytes 262176 | tf_op jit(solution)/shard_map/ppermute | solution.py:252
  55.2 1.8 %collective-permute-start.22 = (f32[64,1024]{1,0:T(8,128)S(1)}, f32[64,1024]{1,0:T(8,128)S(1)}, u32[]{:S(2)}, u32[]{:S(2)}) collective-permute-start(f32[64,1024]{1,0:T(8,128)S(1)} %broadcast_select_fusion.6), channel_id=1, source_target_pairs={{0,1},{1,0},{2,3},{3,2},{4,5},{5,4},{6,7},{7,6},{8,9},{9,8},{10,11... | collective-permute-start | bytes 786440 | tf_op jit(solution)/shard_map/ppermute | solution.py:258
  62.0 2.5 %collective-permute-done.17.refs_2_ = f32[64,2048]{1,0:T(8,128)S(1)} collective-permute-done((f32[64,2048]{1,0:T(8,128)S(1)}, f32[64,2048]{1,0:T(8,128)S(1)}, u32[]{:S(2)}, u32[]{:S(2)}) %collective-permute-start.17) | collective-permute-done | bytes 524320 | tf_op jit(solution)/shard_map/ppermute | solution.py:252
  64.5 2.2 %copy-done.10 = bf16[2048,1024]{1,0:T(8,128)(2,1)S(1)} copy-done((bf16[2048,1024]{1,0:T(8,128)(2,1)S(1)}, bf16[2048,1024]{1,0:T(8,128)(2,1)}, u32[]{:S(2)}) %copy-start.10) | copy-done | bytes 4194328
  66.7 2.4 %product.10 = (f32[64,1024]{1,0:T(8,128)S(1)}, f32[64,1024]{1,0:T(8,128)S(1)}) custom-call(s32[3]{0:T(128)S(1)} %pad_add_fusion.place_ref, s32[8,64]{1,0:T(8,128)S(1)} %copy-done.12, s32[8]{0:T(128)S(1)} %copy-done.13, f32[32,2048]{1,0:T(8,128)S(1)} %pack.4.refs_0_, f32[32,2048]{1,0:T(8,128)S(1)} %collective-permute-done.11.refs_1_, ...), custom_call_target="tpu_custom_call" | custom-call | flops 3221225472 | bytes 1 | tf_op jit(solution)/shard_map/product/pallas_call | solution.py:183
  71.1 2.4 %product.11 = (f32[64,1024]{1,0:T(8,128)S(1)}, f32[64,1024]{1,0:T(8,128)S(1)}) custom-call(s32[3]{0:T(128)S(1)} %pad_add_fusion.place_ref, s32[8,64]{1,0:T(8,128)S(1)} %copy-done.12, s32[8]{0:T(128)S(1)} %copy-done.13, f32[32,2048]{1,0:T(8,128)S(1)} %pack.4.refs_0_, f32[32,2048]{1,0:T(8,128)S(1)} %collective-permute-done.11.refs_1_, ...), custom_call_target="tpu_custom_call" | custom-call | flops 3221225472 | bytes 1 | tf_op jit(solution)/shard_map/product/pallas_call | solution.py:183
  77.4 2.3 %collective-permute-done.19.refs_1_ = f32[32,1024]{1,0:T(8,128)S(1)} collective-permute-done((f32[32,1024]{1,0:T(8,128)S(1)}, f32[32,1024]{1,0:T(8,128)S(1)}, u32[]{:S(2)}, u32[]{:S(2)}) %collective-permute-start.19) | collective-permute-done | bytes 131104 | tf_op jit(solution)/shard_map/ppermute | solution.py:258
  79.8 2.4 %product.12 = (f32[64,1024]{1,0:T(8,128)S(1)}, f32[64,1024]{1,0:T(8,128)S(1)}) custom-call(s32[3]{0:T(128)S(1)} %pad_add_fusion.place_ref, s32[8,64]{1,0:T(8,128)S(1)} %copy-done.12, s32[8]{0:T(128)S(1)} %copy-done.13, f32[32,2048]{1,0:T(8,128)S(1)} %get-tuple-element.261.refs_0_, f32[32,2048]{1,0:T(8,128)S(1)} %collective-permute-done.18.refs_1_, ...), custom_call_target="tpu_custom_call" | custom-call | flops 3221225472 | bytes 1 | tf_op jit(solution)/shard_map/product/pallas_call | solution.py:183
  82.2 1.7 %collective-permute-start.26 = (f32[64,1024]{1,0:T(8,128)S(1)}, f32[64,1024]{1,0:T(8,128)S(1)}, u32[]{:S(2)}, u32[]{:S(2)}) collective-permute-start(f32[64,1024]{1,0:T(8,128)S(1)} %get-tuple-element.256), channel_id=1, source_target_pairs={{0,8},{4,12},{8,0},{12,4},{16,24},{20,28},{24,16},{28,20},{1,9},{5... | collective-permute-start | bytes 786440 | tf_op jit(solution)/shard_map/ppermute | solution.py:252
  83.9 2.4 %collective-permute-start.25 = (f32[32,1024]{1,0:T(8,128)S(1)}, f32[32,1024]{1,0:T(8,128)S(1)}, u32[]{:S(2)}, u32[]{:S(2)}) collective-permute-start(f32[32,1024]{1,0:T(8,128)S(1)} %get-tuple-element.343), channel_id=1, source_target_pairs={{0,2},{1,3},{2,0},{3,1},{4,6},{5,7},{6,4},{7,5},{8,10},{9,11},{10,... | collective-permute-start | bytes 393224 | tf_op jit(solution)/shard_map/ppermute | solution.py:258
  86.5 2.4 %product.13 = (f32[64,1024]{1,0:T(8,128)S(1)}, f32[64,1024]{1,0:T(8,128)S(1)}) custom-call(s32[3]{0:T(128)S(1)} %pad_add_fusion.place_ref, s32[8,64]{1,0:T(8,128)S(1)} %copy-done.12, s32[8]{0:T(128)S(1)} %copy-done.13, f32[32,2048]{1,0:T(8,128)S(1)} %get-tuple-element.261.refs_0_, f32[32,2048]{1,0:T(8,128)S(1)} %collective-permute-done.18.refs_1_, ...), custom_call_target="tpu_custom_call" | custom-call | flops 3221225472 | bytes 1 | tf_op jit(solution)/shard_map/product/pallas_call | solution.py:183
  88.9 2.2 %collective-permute-start.33 = (f32[64,1024]{1,0:T(8,128)S(1)}, f32[64,1024]{1,0:T(8,128)S(1)}, u32[]{:S(2)}, u32[]{:S(2)}) collective-permute-start(f32[64,1024]{1,0:T(8,128)S(1)} %get-tuple-element.266), channel_id=1, source_target_pairs={{0,8},{4,12},{8,0},{12,4},{16,24},{20,28},{24,16},{28,20},{1,9},{5... | collective-permute-start | bytes 786440 | tf_op jit(solution)/shard_map/ppermute | solution.py:252
  91.4 2.5 %collective-permute-done.25.refs_3_ = f32[32,1024]{1,0:T(8,128)S(1)} collective-permute-done((f32[32,1024]{1,0:T(8,128)S(1)}, f32[32,1024]{1,0:T(8,128)S(1)}, u32[]{:S(2)}, u32[]{:S(2)}) %collective-permute-start.25) | collective-permute-done | bytes 131104 | tf_op jit(solution)/shard_map/ppermute | solution.py:258
  93.9 2.4 %product.14 = (f32[64,1024]{1,0:T(8,128)S(1)}, f32[64,1024]{1,0:T(8,128)S(1)}) custom-call(s32[3]{0:T(128)S(1)} %pad_add_fusion.place_ref, s32[8,64]{1,0:T(8,128)S(1)} %copy-done.12, s32[8]{0:T(128)S(1)} %copy-done.13, f32[32,2048]{1,0:T(8,128)S(1)} %get-tuple-element.283.refs_0_, f32[32,2048]{1,0:T(8,128)S(1)} %collective-permute-done.21.refs_1_, ...), custom_call_target="tpu_custom_call" | custom-call | flops 3221225472 | bytes 1 | tf_op jit(solution)/shard_map/product/pallas_call | solution.py:183
  96.5 2.1 %collective-permute-done.29 = f32[64,1024]{1,0:T(8,128)S(1)} collective-permute-done((f32[64,1024]{1,0:T(8,128)S(1)}, f32[64,1024]{1,0:T(8,128)S(1)}, u32[]{:S(2)}, u32[]{:S(2)}) %collective-permute-start.29) | collective-permute-done | bytes 262176 | tf_op jit(solution)/shard_map/ppermute | solution.py:258
  102.0 2.4 %product.15 = (f32[64,1024]{1,0:T(8,128)S(1)}, f32[64,1024]{1,0:T(8,128)S(1)}) custom-call(s32[3]{0:T(128)S(1)} %pad_add_fusion.place_ref, s32[8,64]{1,0:T(8,128)S(1)} %copy-done.12, s32[8]{0:T(128)S(1)} %copy-done.13, f32[32,2048]{1,0:T(8,128)S(1)} %get-tuple-element.283.refs_0_, f32[32,2048]{1,0:T(8,128)S(1)} %collective-permute-done.21.refs_1_, ...), custom_call_target="tpu_custom_call" | custom-call | flops 3221225472 | bytes 1 | tf_op jit(solution)/shard_map/product/pallas_call | solution.py:183
  109.6 5.9 %collective-permute-done.37 = f32[64,1024]{1,0:T(8,128)S(1)} collective-permute-done((f32[64,1024]{1,0:T(8,128)S(1)}, f32[64,1024]{1,0:T(8,128)S(1)}, u32[]{:S(2)}, u32[]{:S(2)}) %collective-permute-start.37) | collective-permute-done | bytes 262176 | tf_op jit(solution)/shard_map/ppermute | solution.py:258
  116.1 2.5 %collective-permute-start.46 = (f32[64,1024]{1,0:T(8,128)S(1)}, f32[64,1024]{1,0:T(8,128)S(1)}, u32[]{:S(2)}, u32[]{:S(2)}) collective-permute-start(f32[64,1024]{1,0:T(8,128)S(1)} %broadcast_select_fusion), channel_id=1, source_target_pairs={{0,1},{1,0},{2,3},{3,2},{4,5},{5,4},{6,7},{7,6},{8,9},{9,8},{10,11... | collective-permute-start | bytes 786440 | tf_op jit(solution)/shard_map/ppermute | solution.py:258
  118.6 2.8 %collective-permute-done.42 = f32[32,1024]{1,0:T(8,128)S(1)} collective-permute-done((f32[32,1024]{1,0:T(8,128)S(1)}, f32[32,1024]{1,0:T(8,128)S(1)}, u32[]{:S(2)}, u32[]{:S(2)}) %collective-permute-start.42) | collective-permute-done | bytes 131104 | tf_op jit(solution)/shard_map/ppermute | solution.py:252
  121.7 4.8 %collective-permute-done.40.refs_9_ = f32[32,1024]{1,0:T(8,128)S(1)} collective-permute-done((f32[32,1024]{1,0:T(8,128)S(1)}, f32[32,1024]{1,0:T(8,128)S(1)}, u32[]{:S(2)}, u32[]{:S(2)}) %collective-permute-start.40) | collective-permute-done | bytes 131104 | tf_op jit(solution)/shard_map/ppermute | solution.py:258
  126.6 1.9 %collective-permute-start.47 = (f32[32,1024]{1,0:T(8,128)S(1)}, f32[32,1024]{1,0:T(8,128)S(1)}, u32[]{:S(2)}, u32[]{:S(2)}) collective-permute-start(f32[32,1024]{1,0:T(8,128)S(1)} %get-tuple-element.324), channel_id=1, source_target_pairs={{0,16},{4,20},{8,24},{12,28},{16,0},{20,4},{24,8},{28,12},{1,17},{... | collective-permute-start | bytes 393224 | tf_op jit(solution)/shard_map/ppermute | solution.py:252
  132.4 4.6 %collective-permute-done.49.refs_15_ = f32[32,1024]{1,0:T(8,128)S(1)} collective-permute-done((f32[32,1024]{1,0:T(8,128)S(1)}, f32[32,1024]{1,0:T(8,128)S(1)}, u32[]{:S(2)}, u32[]{:S(2)}) %collective-permute-start.49) | collective-permute-done | bytes 131104 | tf_op jit(solution)/shard_map/ppermute | solution.py:258
  138.5 1.8 %finish.1 = f32[128,2048]{1,0:T(8,128)} custom-call(s32[3]{0:T(128)S(1)} %pad_add_fusion.place_ref, f32[128,2048]{1,0:T(8,128)S(1)} %copy-done, f32[128,1]{1,0:T(8,128)S(1)} %copy.8.occ_ref, f32[1,2048]{1,0:T(1,128)S(1)} %bitcast.5, f32[32,1024]{1,0:T(8,128)S(1)} %get-tuple-element.249.refs_0_, f32[32,1024]{1,0:T(8,128)S(1)} %collective-permute-done.19.refs_1_, ...), custom_call_target="tpu_custom_call" | custom-call | flops 1 | bytes 1 | tf_op jit(solution)/shard_map/finish/pallas_call | solution.py:219
  (161 shorter events, 51.2 us)
Async XLA Ops:
  0.0 38.3 %collective-permute-start.12 = (f32[2048,1024]{1,0:T(8,128)}, f32[2048,1024]{1,0:T(8,128)}, u32[]{:S(2)}, u32[]{:S(2)}) collective-permute-start(f32[2048,1024]{1,0:T(8,128)} %whole_ref.2), channel_id=1, source_target_pairs={{0,4},{4,0},{8,12},{12,8},{16,20},{20,16},{24,28},{28,24},{1,5},{5... | collective-permute-start | bytes 25165832 | tf_op jit(solution)/shard_map/ppermute | solution.py:252
  19.4 13.7 %collective-permute-start.8 = (f32[32,2048]{1,0:T(8,128)S(1)}, f32[32,2048]{1,0:T(8,128)S(1)}, u32[]{:S(2)}, u32[]{:S(2)}) collective-permute-start(f32[32,2048]{1,0:T(8,128)S(1)} %get-tuple-element.180), channel_id=1, source_target_pairs={{0,1},{1,0},{2,3},{3,2},{4,5},{5,4},{6,7},{7,6},{8,9},{9,8},{10,11... | collective-permute-start | bytes 786440 | tf_op jit(solution)/shard_map/ppermute | solution.py:258
  20.8 10.1 %collective-permute-start.9 = (f32[16,2048]{1,0:T(8,128)S(1)}, f32[16,2048]{1,0:T(8,128)S(1)}, u32[]{:S(2)}, u32[]{:S(2)}) collective-permute-start(f32[16,2048]{1,0:T(8,128)S(1)} %pad_maximum_fusion.1), channel_id=1, source_target_pairs={{0,2},{1,3},{2,0},{3,1},{4,6},{5,7},{6,4},{7,5},{8,10},{9,11},{10,... | collective-permute-start | bytes 393224 | tf_op jit(solution)/shard_map/ppermute | solution.py:258
  24.5 10.5 %collective-permute-start.6 = (f32[16,2048]{1,0:T(8,128)S(1)}, f32[16,2048]{1,0:T(8,128)S(1)}, u32[]{:S(2)}, u32[]{:S(2)}) collective-permute-start(f32[16,2048]{1,0:T(8,128)S(1)} %slice.68), channel_id=1, source_target_pairs={{0,16},{4,20},{8,24},{12,28},{16,0},{20,4},{24,8},{28,12},{1,17},{... | collective-permute-start | bytes 393224 | tf_op jit(solution)/shard_map/ppermute | solution.py:252
  31.5 15.9 %collective-permute-start.11 = (f32[32,2048]{1,0:T(8,128)S(1)}, f32[32,2048]{1,0:T(8,128)S(1)}, u32[]{:S(2)}, u32[]{:S(2)}) collective-permute-start(f32[32,2048]{1,0:T(8,128)S(1)} %pack.4.refs_0_), channel_id=1, source_target_pairs={{0,8},{4,12},{8,0},{12,4},{16,24},{20,28},{24,16},{28,20},{1,9},{5... | collective-permute-start | bytes 786440 | tf_op jit(solution)/shard_map/ppermute | solution.py:252
  34.3 16.0 %collective-permute-start.14 = (f32[32,2048]{1,0:T(8,128)}, f32[32,2048]{1,0:T(8,128)S(1)}, u32[]{:S(2)}, u32[]{:S(2)}) collective-permute-start(f32[32,2048]{1,0:T(8,128)} %pad_maximum_fusion), channel_id=1, source_target_pairs={{0,2},{1,3},{2,0},{3,1},{4,6},{5,7},{6,4},{7,5},{8,10},{9,11},{10,... | collective-permute-start | bytes 786440 | tf_op jit(solution)/shard_map/ppermute | solution.py:258
  37.5 9.9 %collective-permute-start.10 = (f32[64,1024]{1,0:T(8,128)S(1)}, f32[64,1024]{1,0:T(8,128)S(1)}, u32[]{:S(2)}, u32[]{:S(2)}) collective-permute-start(f32[64,1024]{1,0:T(8,128)S(1)} %get-tuple-element.201), channel_id=1, source_target_pairs={{0,8},{4,12},{8,0},{12,4},{16,24},{20,28},{24,16},{28,20},{1,9},{5... | collective-permute-start | bytes 786440 | tf_op jit(solution)/shard_map/ppermute | solution.py:252
  46.0 9.1 %collective-permute-start.15 = (f32[64,1024]{1,0:T(8,128)S(1)}, f32[64,1024]{1,0:T(8,128)S(1)}, u32[]{:S(2)}, u32[]{:S(2)}) collective-permute-start(f32[64,1024]{1,0:T(8,128)S(1)} %get-tuple-element.212), channel_id=1, source_target_pairs={{0,8},{4,12},{8,0},{12,4},{16,24},{20,28},{24,16},{28,20},{1,9},{5... | collective-permute-start | bytes 786440 | tf_op jit(solution)/shard_map/ppermute | solution.py:252
  48.2 10.2 %collective-permute-start.13 = (f32[64,1024]{1,0:T(8,128)}, f32[64,1024]{1,0:T(8,128)S(1)}, u32[]{:S(2)}, u32[]{:S(2)}) collective-permute-start(f32[64,1024]{1,0:T(8,128)} %broadcast_select_fusion.7), channel_id=1, source_target_pairs={{0,1},{1,0},{2,3},{3,2},{4,5},{5,4},{6,7},{7,6},{8,9},{9,8},{10,11... | collective-permute-start | bytes 786440 | tf_op jit(solution)/shard_map/ppermute | solution.py:258
  49.8 14.7 %collective-permute-start.17 = (f32[64,2048]{1,0:T(8,128)S(1)}, f32[64,2048]{1,0:T(8,128)S(1)}, u32[]{:S(2)}, u32[]{:S(2)}) collective-permute-start(f32[64,2048]{1,0:T(8,128)S(1)} %constant_dynamic-update-slice_fusion), channel_id=1, source_target_pairs={{0,16},{4,20},{8,24},{12,28},{16,0},{20,4},{24,8},{28,12},{1,17},{... | collective-permute-start | bytes 1572872 | tf_op jit(solution)/shard_map/ppermute | solution.py:252
  50.9 9.4 %collective-permute-start.18 = (f32[32,2048]{1,0:T(8,128)S(1)}, f32[32,2048]{1,0:T(8,128)S(1)}, u32[]{:S(2)}, u32[]{:S(2)}) collective-permute-start(f32[32,2048]{1,0:T(8,128)S(1)} %get-tuple-element.261.refs_0_), channel_id=1, source_target_pairs={{0,8},{4,12},{8,0},{12,4},{16,24},{20,28},{24,16},{28,20},{1,9},{5... | collective-permute-start | bytes 786440 | tf_op jit(solution)/shard_map/ppermute | solution.py:252
  55.2 18.4 %collective-permute-start.22 = (f32[64,1024]{1,0:T(8,128)S(1)}, f32[64,1024]{1,0:T(8,128)S(1)}, u32[]{:S(2)}, u32[]{:S(2)}) collective-permute-start(f32[64,1024]{1,0:T(8,128)S(1)} %broadcast_select_fusion.6), channel_id=1, source_target_pairs={{0,1},{1,0},{2,3},{3,2},{4,5},{5,4},{6,7},{7,6},{8,9},{9,8},{10,11... | collective-permute-start | bytes 786440 | tf_op jit(solution)/shard_map/ppermute | solution.py:258
  56.9 18.1 %collective-permute-start.21 = (f32[32,2048]{1,0:T(8,128)S(1)}, f32[32,2048]{1,0:T(8,128)S(1)}, u32[]{:S(2)}, u32[]{:S(2)}) collective-permute-start(f32[32,2048]{1,0:T(8,128)S(1)} %get-tuple-element.283.refs_0_), channel_id=1, source_target_pairs={{0,8},{4,12},{8,0},{12,4},{16,24},{20,28},{24,16},{28,20},{1,9},{5... | collective-permute-start | bytes 786440 | tf_op jit(solution)/shard_map/ppermute | solution.py:252
  58.4 11.6 %collective-permute-start.16 = (f32[32,1024]{1,0:T(8,128)S(1)}, f32[32,1024]{1,0:T(8,128)S(1)}, u32[]{:S(2)}, u32[]{:S(2)}) collective-permute-start(f32[32,1024]{1,0:T(8,128)S(1)} %get-tuple-element.349), channel_id=1, source_target_pairs={{0,16},{4,20},{8,24},{12,28},{16,0},{20,4},{24,8},{28,12},{1,17},{... | collective-permute-start | bytes 393224 | tf_op jit(solution)/shard_map/ppermute | solution.py:252
  60.4 19.4 %collective-permute-start.24 = (f32[64,2048]{1,0:T(8,128)S(1)}, f32[64,2048]{1,0:T(8,128)S(1)}, u32[]{:S(2)}, u32[]{:S(2)}) collective-permute-start(f32[64,2048]{1,0:T(8,128)S(1)} %constant_dynamic-update-slice_fusion.2), channel_id=1, source_target_pairs={{0,16},{4,20},{8,24},{12,28},{16,0},{20,4},{24,8},{28,12},{1,17},{... | collective-permute-start | bytes 1572872 | tf_op jit(solution)/shard_map/ppermute | solution.py:252
  70.1 9.7 %collective-permute-start.19 = (f32[32,1024]{1,0:T(8,128)S(1)}, f32[32,1024]{1,0:T(8,128)S(1)}, u32[]{:S(2)}, u32[]{:S(2)}) collective-permute-start(f32[32,1024]{1,0:T(8,128)S(1)} %get-tuple-element.347), channel_id=1, source_target_pairs={{0,2},{1,3},{2,0},{3,1},{4,6},{5,7},{6,4},{7,5},{8,10},{9,11},{10,... | collective-permute-start | bytes 393224 | tf_op jit(solution)/shard_map/ppermute | solution.py:258
  73.5 12.8 %collective-permute-start.28 = (f32[64,1024]{1,0:T(8,128)S(1)}, f32[64,1024]{1,0:T(8,128)S(1)}, u32[]{:S(2)}, u32[]{:S(2)}) collective-permute-start(f32[64,1024]{1,0:T(8,128)S(1)} %get-tuple-element.243), channel_id=1, source_target_pairs={{0,8},{4,12},{8,0},{12,4},{16,24},{20,28},{24,16},{28,20},{1,9},{5... | collective-permute-start | bytes 786440 | tf_op jit(solution)/shard_map/ppermute | solution.py:252
  77.0 16.9 %collective-permute-start.31 = (f32[64,2048]{1,0:T(8,128)S(1)}, f32[64,2048]{1,0:T(8,128)S(1)}, u32[]{:S(2)}, u32[]{:S(2)}) collective-permute-start(f32[64,2048]{1,0:T(8,128)S(1)} %constant_dynamic-update-slice_fusion.4), channel_id=1, source_target_pairs={{0,16},{4,20},{8,24},{12,28},{16,0},{20,4},{24,8},{28,12},{1,17},{... | collective-permute-start | bytes 1572872 | tf_op jit(solution)/shard_map/ppermute | solution.py:252
  79.8 9.2 %collective-permute-start.27 = (f32[64,1024]{1,0:T(8,128)S(1)}, f32[64,1024]{1,0:T(8,128)S(1)}, u32[]{:S(2)}, u32[]{:S(2)}) collective-permute-start(f32[64,1024]{1,0:T(8,128)S(1)} %broadcast_select_fusion.5), channel_id=1, source_target_pairs={{0,1},{1,0},{2,3},{3,2},{4,5},{5,4},{6,7},{7,6},{8,9},{9,8},{10,11... | collective-permute-start | bytes 786440 | tf_op jit(solution)/shard_map/ppermute | solution.py:258
  83.9 9.9 %collective-permute-start.25 = (f32[32,1024]{1,0:T(8,128)S(1)}, f32[32,1024]{1,0:T(8,128)S(1)}, u32[]{:S(2)}, u32[]{:S(2)}) collective-permute-start(f32[32,1024]{1,0:T(8,128)S(1)} %get-tuple-element.343), channel_id=1, source_target_pairs={{0,2},{1,3},{2,0},{3,1},{4,6},{5,7},{6,4},{7,5},{8,10},{9,11},{10,... | collective-permute-start | bytes 393224 | tf_op jit(solution)/shard_map/ppermute | solution.py:258
  86.4 12.2 %collective-permute-start.29 = (f32[64,1024]{1,0:T(8,128)S(1)}, f32[64,1024]{1,0:T(8,128)S(1)}, u32[]{:S(2)}, u32[]{:S(2)}) collective-permute-start(f32[64,1024]{1,0:T(8,128)S(1)} %broadcast_select_fusion.4), channel_id=1, source_target_pairs={{0,1},{1,0},{2,3},{3,2},{4,5},{5,4},{6,7},{7,6},{8,9},{9,8},{10,11... | collective-permute-start | bytes 786440 | tf_op jit(solution)/shard_map/ppermute | solution.py:258
  88.9 11.5 %collective-permute-start.33 = (f32[64,1024]{1,0:T(8,128)S(1)}, f32[64,1024]{1,0:T(8,128)S(1)}, u32[]{:S(2)}, u32[]{:S(2)}) collective-permute-start(f32[64,1024]{1,0:T(8,128)S(1)} %get-tuple-element.266), channel_id=1, source_target_pairs={{0,8},{4,12},{8,0},{12,4},{16,24},{20,28},{24,16},{28,20},{1,9},{5... | collective-permute-start | bytes 786440 | tf_op jit(solution)/shard_map/ppermute | solution.py:252
  93.9 12.6 %collective-permute-start.35 = (f32[64,1024]{1,0:T(8,128)S(1)}, f32[64,1024]{1,0:T(8,128)S(1)}, u32[]{:S(2)}, u32[]{:S(2)}) collective-permute-start(f32[64,1024]{1,0:T(8,128)S(1)} %broadcast_select_fusion.3), channel_id=1, source_target_pairs={{0,1},{1,0},{2,3},{3,2},{4,5},{5,4},{6,7},{7,6},{8,9},{9,8},{10,11... | collective-permute-start | bytes 786440 | tf_op jit(solution)/shard_map/ppermute | solution.py:258
  96.3 11.0 %collective-permute-start.39 = (f32[64,1024]{1,0:T(8,128)S(1)}, f32[64,1024]{1,0:T(8,128)S(1)}, u32[]{:S(2)}, u32[]{:S(2)}) collective-permute-start(f32[64,1024]{1,0:T(8,128)S(1)} %get-tuple-element.277), channel_id=1, source_target_pairs={{0,8},{4,12},{8,0},{12,4},{16,24},{20,28},{24,16},{28,20},{1,9},{5... | collective-permute-start | bytes 786440 | tf_op jit(solution)/shard_map/ppermute | solution.py:252
  98.7 10.2 %collective-permute-start.38 = (f32[32,1024]{1,0:T(8,128)S(1)}, f32[32,1024]{1,0:T(8,128)S(1)}, u32[]{:S(2)}, u32[]{:S(2)}) collective-permute-start(f32[32,1024]{1,0:T(8,128)S(1)} %get-tuple-element.334), channel_id=1, source_target_pairs={{0,2},{1,3},{2,0},{3,1},{4,6},{5,7},{6,4},{7,5},{8,10},{9,11},{10,... | collective-permute-start | bytes 393224 | tf_op jit(solution)/shard_map/ppermute | solution.py:258
  100.5 15.0 %collective-permute-start.37 = (f32[64,1024]{1,0:T(8,128)S(1)}, f32[64,1024]{1,0:T(8,128)S(1)}, u32[]{:S(2)}, u32[]{:S(2)}) collective-permute-start(f32[64,1024]{1,0:T(8,128)S(1)} %broadcast_select_fusion.2), channel_id=1, source_target_pairs={{0,1},{1,0},{2,3},{3,2},{4,5},{5,4},{6,7},{7,6},{8,9},{9,8},{10,11... | collective-permute-start | bytes 786440 | tf_op jit(solution)/shard_map/ppermute | solution.py:258
  105.4 10.6 %collective-permute-start.43 = (f32[64,1024]{1,0:T(8,128)S(1)}, f32[64,1024]{1,0:T(8,128)S(1)}, u32[]{:S(2)}, u32[]{:S(2)}) collective-permute-start(f32[64,1024]{1,0:T(8,128)S(1)} %get-tuple-element.288), channel_id=1, source_target_pairs={{0,8},{4,12},{8,0},{12,4},{16,24},{20,28},{24,16},{28,20},{1,9},{5... | collective-permute-start | bytes 786440 | tf_op jit(solution)/shard_map/ppermute | solution.py:252
  106.5 9.5 %collective-permute-start.34 = (f32[32,1024]{1,0:T(8,128)S(1)}, f32[32,1024]{1,0:T(8,128)S(1)}, u32[]{:S(2)}, u32[]{:S(2)}) collective-permute-start(f32[32,1024]{1,0:T(8,128)S(1)} %get-tuple-element.337), channel_id=1, source_target_pairs={{0,2},{1,3},{2,0},{3,1},{4,6},{5,7},{6,4},{7,5},{8,10},{9,11},{10,... | collective-permute-start | bytes 393224 | tf_op jit(solution)/shard_map/ppermute | solution.py:258
  108.9 12.6 %collective-permute-start.41 = (f32[64,1024]{1,0:T(8,128)S(1)}, f32[64,1024]{1,0:T(8,128)S(1)}, u32[]{:S(2)}, u32[]{:S(2)}) collective-permute-start(f32[64,1024]{1,0:T(8,128)S(1)} %broadcast_select_fusion.1), channel_id=1, source_target_pairs={{0,1},{1,0},{2,3},{3,2},{4,5},{5,4},{6,7},{7,6},{8,9},{9,8},{10,11... | collective-permute-start | bytes 786440 | tf_op jit(solution)/shard_map/ppermute | solution.py:258
  115.7 10.8 %collective-permute-start.40 = (f32[32,1024]{1,0:T(8,128)S(1)}, f32[32,1024]{1,0:T(8,128)S(1)}, u32[]{:S(2)}, u32[]{:S(2)}) collective-permute-start(f32[32,1024]{1,0:T(8,128)S(1)} %get-tuple-element.332), channel_id=1, source_target_pairs={{0,2},{1,3},{2,0},{3,1},{4,6},{5,7},{6,4},{7,5},{8,10},{9,11},{10,... | collective-permute-start | bytes 393224 | tf_op jit(solution)/shard_map/ppermute | solution.py:258
  116.1 10.4 %collective-permute-start.46 = (f32[64,1024]{1,0:T(8,128)S(1)}, f32[64,1024]{1,0:T(8,128)S(1)}, u32[]{:S(2)}, u32[]{:S(2)}) collective-permute-start(f32[64,1024]{1,0:T(8,128)S(1)} %broadcast_select_fusion), channel_id=1, source_target_pairs={{0,1},{1,0},{2,3},{3,2},{4,5},{5,4},{6,7},{7,6},{8,9},{9,8},{10,11... | collective-permute-start | bytes 786440 | tf_op jit(solution)/shard_map/ppermute | solution.py:258
  121.5 9.3 %collective-permute-start.44 = (f32[32,1024]{1,0:T(8,128)S(1)}, f32[32,1024]{1,0:T(8,128)S(1)}, u32[]{:S(2)}, u32[]{:S(2)}) collective-permute-start(f32[32,1024]{1,0:T(8,128)S(1)} %get-tuple-element.328), channel_id=1, source_target_pairs={{0,2},{1,3},{2,0},{3,1},{4,6},{5,7},{6,4},{7,5},{8,10},{9,11},{10,... | collective-permute-start | bytes 393224 | tf_op jit(solution)/shard_map/ppermute | solution.py:258
  (33 other events, 300.9 us)

commit v18 on v17

--- a/solution.py
+++ b/solution.py
@@ -17,9 +17,9 @@
 
 ORDER = (
     "s00", "p0", "s10", "g00", "s11", "s20", "g01", "f0", "p1", "g10", "s21", "e0", "f1", "e1",
-    "g11", "r0", "p2", "g20", "r1", "g30", "x0", "g21", "e3", "z0", "e2", "x1", "g31", "r3",
-    "l0", "e4", "z1", "r2", "e5", "x3", "r4", "l1", "e7", "z3", "x2", "r5", "e6", "z2", "x4",
-    "r7", "l3", "x5", "z4", "l2", "r6", "z5", "x7", "l4", "x6", "z7", "l5", "z6", "l7", "l6",
+    "g11", "r0", "p2", "g30", "r1", "g20", "e3", "g31", "x0", "g21", "e6", "z0", "r3", "x1",
+    "e2", "r6", "l0", "e4", "z1", "x3", "r2", "e7", "z3", "l1", "x6", "r4", "e5", "z6", "l3",
+    "x2", "r7", "x4", "z2", "r5", "x7", "z4", "l2", "z7", "l6", "x5", "z5", "l4", "l7", "l5",
 )
 
 SMEM = pl.BlockSpec(memory_space=pltpu.SMEM)

time: 140 us -> 152 us (1.086)
  starting transfers between devices: 51.4 us -> 60.6 us
  local copies, waits for them, and re-layouts: 5.05 us -> 8.32 us
  waiting for transfers between devices: 48.3 us -> 46.7 us
    ppermute x27, starting transfers between devices: 25 us -> 32.6 us  [across(): lax.ppermute(value, 'wide', [(w, w ^ mask) for w in range(wide_count)])]
    ppermute x23, waiting for transfers between devices: 32.7 us -> 28.4 us  [along(): lax.ppermute(value, 'narrow', [(n, n ^ mask) for n in range(narrow_count)])]
    ppermute x27, waiting for transfers between devices: 15.6 us -> 18.3 us  [across(): lax.ppermute(value, 'wide', [(w, w ^ mask) for w in range(wide_count)])]
    unnamed x33 -> x35, local copies, waits for them, and re-layouts: 4.49 us -> 7.25 us
  transfers between devices with their start and end apart: 50 -> 50, of which waited for: 23 -> 22; matrix products, arithmetic and copies ran while one was open for 2% -> 3% of each run, Pallas kernels for 22% -> 20%
where the time goes in v18:
time: 152 us
  starting transfers between devices  60.6 us (40%)
  waiting for transfers between devices  46.7 us (31%)
  Pallas kernels  32.1 us (21%)
  local copies, waits for them, and re-layouts  8.32 us (5%)
  other arithmetic  3.22 us (2%)
    ppermute x27, starting transfers between devices, across(): lax.ppermute(value, 'wide', [(w, w ^ mask) for w in range(wide_count)])  32.6 us
    ppermute x23, waiting for transfers between devices, along(): lax.ppermute(value, 'narrow', [(n, n ^ mask) for n in range(narrow_count)])  28.4 us
    ppermute x23, starting transfers between devices, along(): lax.ppermute(value, 'narrow', [(n, n ^ mask) for n in range(narrow_count)])  28 us
    pallas_call x8, Pallas kernels, product(): pl.pallas_call(functools.partial(product_kernel, count, rows, layout, tar...  19.5 us
    ppermute x27, waiting for transfers between devices, across(): lax.ppermute(value, 'wide', [(w, w ^ mask) for w in range(wide_count)])  18.3 us
    pallas_call x2, Pallas kernels, split(): pl.pallas_call(functools.partial(split_kernel, step), in_specs=[HBM], out...  8.51 us
    unnamed x35, local copies, waits for them, and re-layouts  7.25 us
  transfers between devices with their start and end apart: 50, of which 22 were waited for; matrix products, arithmetic and copies ran while one was open for 3% of the time, Pallas kernels for 20%

profile of v18, /device:TPU:0, one launch (start us, length us, event | category | flops | bytes accessed | tf_op | source)
XLA Modules:
  0.0 151.5 jit_solution(5527459411251965222)
XLA Ops:
  2.4 2.6 %collective-permute-start = (f32[8,2048]{1,0:T(8,128)S(1)}, f32[8,2048]{1,0:T(8,128)S(1)}, u32[]{:S(2)}, u32[]{:S(2)}) collective-permute-start(f32[8,2048]{1,0:T(8,128)S(1)} %get-tuple-element.166), channel_id=1, source_target_pairs={{0,1},{1,0},{2,3},{3,2},{4,5},{5,4},{6,7},{7,6},{8,9},{9,8},{10,11... | collective-permute-start | bytes 196616 | tf_op jit(solution)/shard_map/ppermute | solution.py:258
  5.0 2.6 %collective-permute-start.1 = (f32[8,2048]{1,0:T(8,128)S(1)}, f32[8,2048]{1,0:T(8,128)S(1)}, u32[]{:S(2)}, u32[]{:S(2)}) collective-permute-start(f32[8,2048]{1,0:T(8,128)S(1)} %get-tuple-element.167), channel_id=1, source_target_pairs={{0,2},{1,3},{2,0},{3,1},{4,6},{5,7},{6,4},{7,5},{8,10},{9,11},{10,... | collective-permute-start | bytes 196616 | tf_op jit(solution)/shard_map/ppermute | solution.py:258
  7.8 4.2 %collective-permute-done.1.refs_2_ = f32[8,2048]{1,0:T(8,128)S(1)} collective-permute-done((f32[8,2048]{1,0:T(8,128)S(1)}, f32[8,2048]{1,0:T(8,128)S(1)}, u32[]{:S(2)}, u32[]{:S(2)}) %collective-permute-start.1) | collective-permute-done | bytes 65568 | tf_op jit(solution)/shard_map/ppermute | solution.py:258
  12.0 1.8 %collective-permute-done.2.refs_3_ = f32[8,2048]{1,0:T(8,128)S(1)} collective-permute-done((f32[8,2048]{1,0:T(8,128)S(1)}, f32[8,2048]{1,0:T(8,128)S(1)}, u32[]{:S(2)}, u32[]{:S(2)}) %collective-permute-start.2) | collective-permute-done | bytes 65568 | tf_op jit(solution)/shard_map/ppermute | solution.py:258
  24.5 1.6 %collective-permute-start.6 = (f32[16,2048]{1,0:T(8,128)S(1)}, f32[16,2048]{1,0:T(8,128)S(1)}, u32[]{:S(2)}, u32[]{:S(2)}) collective-permute-start(f32[16,2048]{1,0:T(8,128)S(1)} %slice.68), channel_id=1, source_target_pairs={{0,16},{4,20},{8,24},{12,28},{16,0},{20,4},{24,8},{28,12},{1,17},{... | collective-permute-start | bytes 393224 | tf_op jit(solution)/shard_map/ppermute | solution.py:252
  26.7 4.3 %split.2 = (bf16[2048,1024]{1,0:T(8,128)(2,1)S(1)}, bf16[2048,1024]{1,0:T(8,128)(2,1)S(1)}, f32[8,128]{1,0:T(8,128)}) custom-call(f32[2048,1024]{1,0:T(8,128)} %whole_ref.2), custom_call_target="tpu_custom_call" | custom-call | flops 1 | bytes 1 | tf_op jit(solution)/shard_map/split/pallas_call | solution.py:122
  33.9 2.5 %product.8 = (f32[64,1024]{1,0:T(8,128)S(1)}, f32[64,1024]{1,0:T(8,128)S(1)}) custom-call(s32[3]{0:T(128)S(1)} %pad_add_fusion.place_ref, s32[8,64]{1,0:T(8,128)S(1)} %copy-done.13, s32[8]{0:T(128)S(1)} %copy-done.14, f32[32,2048]{1,0:T(8,128)S(1)} %pack.3.refs_0_, f32[32,2048]{1,0:T(8,128)S(1)} %collective-permute-done.3.refs_1_, ...), custom_call_target="tpu_custom_call" | custom-call | flops 3221225472 | bytes 1 | tf_op jit(solution)/shard_map/product/pallas_call | solution.py:183
  37.0 4.3 %split.3 = (bf16[2048,1024]{1,0:T(8,128)(2,1)S(1)}, bf16[2048,1024]{1,0:T(8,128)(2,1)S(1)}, f32[8,128]{1,0:T(8,128)}) custom-call(f32[2048,1024]{1,0:T(8,128)} %collective-permute-done.12.whole_ref), custom_call_target="tpu_custom_call" | custom-call | flops 1 | bytes 1 | tf_op jit(solution)/shard_map/split/pallas_call | solution.py:122
  41.3 2.5 %product.9 = (f32[64,1024]{1,0:T(8,128)S(1)}, f32[64,1024]{1,0:T(8,128)S(1)}) custom-call(s32[3]{0:T(128)S(1)} %pad_add_fusion.place_ref, s32[8,64]{1,0:T(8,128)S(1)} %copy-done.13, s32[8]{0:T(128)S(1)} %copy-done.14, f32[32,2048]{1,0:T(8,128)S(1)} %pack.3.refs_0_, f32[32,2048]{1,0:T(8,128)S(1)} %collective-permute-done.3.refs_1_, ...), custom_call_target="tpu_custom_call" | custom-call | flops 3221225472 | bytes 1 | tf_op jit(solution)/shard_map/product/pallas_call | solution.py:183
  52.8 1.6 %collective-permute-start.23 = (f32[64,1024]{1,0:T(8,128)S(1)}, f32[64,1024]{1,0:T(8,128)S(1)}, u32[]{:S(2)}, u32[]{:S(2)}) collective-permute-start(f32[64,1024]{1,0:T(8,128)S(1)} %broadcast_select_fusion.6), channel_id=1, source_target_pairs={{0,1},{1,0},{2,3},{3,2},{4,5},{5,4},{6,7},{7,6},{8,9},{9,8},{10,11... | collective-permute-start | bytes 786440 | tf_op jit(solution)/shard_map/ppermute | solution.py:258
  54.4 2.5 %collective-permute-start.20 = (f32[32,2048]{1,0:T(8,128)S(1)}, f32[32,2048]{1,0:T(8,128)S(1)}, u32[]{:S(2)}, u32[]{:S(2)}) collective-permute-start(f32[32,2048]{1,0:T(8,128)S(1)} %get-tuple-element.283.refs_0_), channel_id=1, source_target_pairs={{0,8},{4,12},{8,0},{12,4},{16,24},{20,28},{24,16},{28,20},{1,9},{5... | collective-permute-start | bytes 786440 | tf_op jit(solution)/shard_map/ppermute | solution.py:252
  58.4 2.2 %copy-done.4 = bf16[2048,1024]{1,0:T(8,128)(2,1)S(1)} copy-done((bf16[2048,1024]{1,0:T(8,128)(2,1)S(1)}, bf16[2048,1024]{1,0:T(8,128)(2,1)}, u32[]{:S(2)}) %copy-start.4) | copy-done | bytes 4194328
  60.6 2.2 %copy-done.7 = bf16[2048,1024]{1,0:T(8,128)(2,1)S(1)} copy-done((bf16[2048,1024]{1,0:T(8,128)(2,1)S(1)}, bf16[2048,1024]{1,0:T(8,128)(2,1)}, u32[]{:S(2)}) %copy-start.7) | copy-done | bytes 4194328
  62.8 2.4 %product.10 = (f32[64,1024]{1,0:T(8,128)S(1)}, f32[64,1024]{1,0:T(8,128)S(1)}) custom-call(s32[3]{0:T(128)S(1)} %pad_add_fusion.place_ref, s32[8,64]{1,0:T(8,128)S(1)} %copy-done.13, s32[8]{0:T(128)S(1)} %copy-done.14, f32[32,2048]{1,0:T(8,128)S(1)} %pack.4.refs_0_, f32[32,2048]{1,0:T(8,128)S(1)} %collective-permute-done.11.refs_1_, ...), custom_call_target="tpu_custom_call" | custom-call | flops 3221225472 | bytes 1 | tf_op jit(solution)/shard_map/product/pallas_call | solution.py:183
  69.5 11.3 %collective-permute-done.19.refs_2_ = f32[64,2048]{1,0:T(8,128)S(1)} collective-permute-done((f32[64,2048]{1,0:T(8,128)S(1)}, f32[64,2048]{1,0:T(8,128)S(1)}, u32[]{:S(2)}, u32[]{:S(2)}) %collective-permute-start.19) | collective-permute-done | bytes 524320 | tf_op jit(solution)/shard_map/ppermute | solution.py:252
  80.8 2.4 %product.11 = (f32[64,1024]{1,0:T(8,128)S(1)}, f32[64,1024]{1,0:T(8,128)S(1)}) custom-call(s32[3]{0:T(128)S(1)} %pad_add_fusion.place_ref, s32[8,64]{1,0:T(8,128)S(1)} %copy-done.13, s32[8]{0:T(128)S(1)} %copy-done.14, f32[32,2048]{1,0:T(8,128)S(1)} %get-tuple-element.270.refs_0_, f32[32,2048]{1,0:T(8,128)S(1)} %collective-permute-done.15.refs_1_, ...), custom_call_target="tpu_custom_call" | custom-call | flops 3221225472 | bytes 1 | tf_op jit(solution)/shard_map/product/pallas_call | solution.py:183
  83.2 1.6 %collective-permute-start.22 = (f32[64,1024]{1,0:T(8,128)S(1)}, f32[64,1024]{1,0:T(8,128)S(1)}, u32[]{:S(2)}, u32[]{:S(2)}) collective-permute-start(f32[64,1024]{1,0:T(8,128)S(1)} %get-tuple-element.243), channel_id=1, source_target_pairs={{0,8},{4,12},{8,0},{12,4},{16,24},{20,28},{24,16},{28,20},{1,9},{5... | collective-permute-start | bytes 786440 | tf_op jit(solution)/shard_map/ppermute | solution.py:252
  84.8 2.1 %collective-permute-start.21 = (f32[32,1024]{1,0:T(8,128)S(1)}, f32[32,1024]{1,0:T(8,128)S(1)}, u32[]{:S(2)}, u32[]{:S(2)}) collective-permute-start(f32[32,1024]{1,0:T(8,128)S(1)} %get-tuple-element.347), channel_id=1, source_target_pairs={{0,2},{1,3},{2,0},{3,1},{4,6},{5,7},{6,4},{7,5},{8,10},{9,11},{10,... | collective-permute-start | bytes 393224 | tf_op jit(solution)/shard_map/ppermute | solution.py:258
  88.2 2.4 %product.12 = (f32[64,1024]{1,0:T(8,128)S(1)}, f32[64,1024]{1,0:T(8,128)S(1)}) custom-call(s32[3]{0:T(128)S(1)} %pad_add_fusion.place_ref, s32[8,64]{1,0:T(8,128)S(1)} %copy-done.13, s32[8]{0:T(128)S(1)} %copy-done.14, f32[32,2048]{1,0:T(8,128)S(1)} %pack.4.refs_0_, f32[32,2048]{1,0:T(8,128)S(1)} %collective-permute-done.11.refs_1_, ...), custom_call_target="tpu_custom_call" | custom-call | flops 3221225472 | bytes 1 | tf_op jit(solution)/shard_map/product/pallas_call | solution.py:183
  93.0 1.6 %collective-permute-done.21.refs_1_ = f32[32,1024]{1,0:T(8,128)S(1)} collective-permute-done((f32[32,1024]{1,0:T(8,128)S(1)}, f32[32,1024]{1,0:T(8,128)S(1)}, u32[]{:S(2)}, u32[]{:S(2)}) %collective-permute-start.21) | collective-permute-done | bytes 131104 | tf_op jit(solution)/shard_map/ppermute | solution.py:258
  94.7 2.4 %product.13 = (f32[64,1024]{1,0:T(8,128)S(1)}, f32[64,1024]{1,0:T(8,128)S(1)}) custom-call(s32[3]{0:T(128)S(1)} %pad_add_fusion.place_ref, s32[8,64]{1,0:T(8,128)S(1)} %copy-done.13, s32[8]{0:T(128)S(1)} %copy-done.14, f32[32,2048]{1,0:T(8,128)S(1)} %get-tuple-element.283.refs_0_, f32[32,2048]{1,0:T(8,128)S(1)} %collective-permute-done.20.refs_1_, ...), custom_call_target="tpu_custom_call" | custom-call | flops 3221225472 | bytes 1 | tf_op jit(solution)/shard_map/product/pallas_call | solution.py:183
  97.7 1.7 %collective-permute-start.27 = (f32[32,1024]{1,0:T(8,128)S(1)}, f32[32,1024]{1,0:T(8,128)S(1)}, u32[]{:S(2)}, u32[]{:S(2)}) collective-permute-start(f32[32,1024]{1,0:T(8,128)S(1)} %get-tuple-element.343), channel_id=1, source_target_pairs={{0,2},{1,3},{2,0},{3,1},{4,6},{5,7},{6,4},{7,5},{8,10},{9,11},{10,... | collective-permute-start | bytes 393224 | tf_op jit(solution)/shard_map/ppermute | solution.py:258
  99.9 1.9 %collective-permute-start.31 = (f32[64,1024]{1,0:T(8,128)S(1)}, f32[64,1024]{1,0:T(8,128)S(1)}, u32[]{:S(2)}, u32[]{:S(2)}) collective-permute-start(f32[64,1024]{1,0:T(8,128)S(1)} %broadcast_select_fusion.3), channel_id=1, source_target_pairs={{0,1},{1,0},{2,3},{3,2},{4,5},{5,4},{6,7},{7,6},{8,9},{9,8},{10,11... | collective-permute-start | bytes 786440 | tf_op jit(solution)/shard_map/ppermute | solution.py:258
  101.9 2.4 %product.14 = (f32[64,1024]{1,0:T(8,128)S(1)}, f32[64,1024]{1,0:T(8,128)S(1)}) custom-call(s32[3]{0:T(128)S(1)} %pad_add_fusion.place_ref, s32[8,64]{1,0:T(8,128)S(1)} %copy-done.13, s32[8]{0:T(128)S(1)} %copy-done.14, f32[32,2048]{1,0:T(8,128)S(1)} %get-tuple-element.270.refs_0_, f32[32,2048]{1,0:T(8,128)S(1)} %collective-permute-done.15.refs_1_, ...), custom_call_target="tpu_custom_call" | custom-call | flops 3221225472 | bytes 1 | tf_op jit(solution)/shard_map/product/pallas_call | solution.py:183
  104.5 3.2 %collective-permute-start.38 = (f32[64,1024]{1,0:T(8,128)S(1)}, f32[64,1024]{1,0:T(8,128)S(1)}, u32[]{:S(2)}, u32[]{:S(2)}) collective-permute-start(f32[64,1024]{1,0:T(8,128)S(1)} %get-tuple-element.275), channel_id=1, source_target_pairs={{0,8},{4,12},{8,0},{12,4},{16,24},{20,28},{24,16},{28,20},{1,9},{5... | collective-permute-start | bytes 786440 | tf_op jit(solution)/shard_map/ppermute | solution.py:252
  109.4 2.8 %collective-permute-start.37 = (f32[64,1024]{1,0:T(8,128)S(1)}, f32[64,1024]{1,0:T(8,128)S(1)}, u32[]{:S(2)}, u32[]{:S(2)}) collective-permute-start(f32[64,1024]{1,0:T(8,128)S(1)} %broadcast_select_fusion.2), channel_id=1, source_target_pairs={{0,1},{1,0},{2,3},{3,2},{4,5},{5,4},{6,7},{7,6},{8,9},{9,8},{10,11... | collective-permute-start | bytes 786440 | tf_op jit(solution)/shard_map/ppermute | solution.py:258
  112.2 2.4 %product.15 = (f32[64,1024]{1,0:T(8,128)S(1)}, f32[64,1024]{1,0:T(8,128)S(1)}) custom-call(s32[3]{0:T(128)S(1)} %pad_add_fusion.place_ref, s32[8,64]{1,0:T(8,128)S(1)} %copy-done.13, s32[8]{0:T(128)S(1)} %copy-done.14, f32[32,2048]{1,0:T(8,128)S(1)} %get-tuple-element.283.refs_0_, f32[32,2048]{1,0:T(8,128)S(1)} %collective-permute-done.20.refs_1_, ...), custom_call_target="tpu_custom_call" | custom-call | flops 3221225472 | bytes 1 | tf_op jit(solution)/shard_map/product/pallas_call | solution.py:183
  118.6 4.6 %collective-permute-done.37 = f32[64,1024]{1,0:T(8,128)S(1)} collective-permute-done((f32[64,1024]{1,0:T(8,128)S(1)}, f32[64,1024]{1,0:T(8,128)S(1)}, u32[]{:S(2)}, u32[]{:S(2)}) %collective-permute-start.37) | collective-permute-done | bytes 262176 | tf_op jit(solution)/shard_map/ppermute | solution.py:258
  129.4 7.0 %collective-permute-done.39.refs_5_ = f32[32,1024]{1,0:T(8,128)S(1)} collective-permute-done((f32[32,1024]{1,0:T(8,128)S(1)}, f32[32,1024]{1,0:T(8,128)S(1)}, u32[]{:S(2)}, u32[]{:S(2)}) %collective-permute-start.39) | collective-permute-done | bytes 131104 | tf_op jit(solution)/shard_map/ppermute | solution.py:258
  137.9 2.4 %collective-permute-start.49 = (f32[32,1024]{1,0:T(8,128)S(1)}, f32[32,1024]{1,0:T(8,128)S(1)}, u32[]{:S(2)}, u32[]{:S(2)}) collective-permute-start(f32[32,1024]{1,0:T(8,128)S(1)} %get-tuple-element.320), channel_id=1, source_target_pairs={{0,2},{1,3},{2,0},{3,1},{4,6},{5,7},{6,4},{7,5},{8,10},{9,11},{10,... | collective-permute-start | bytes 393224 | tf_op jit(solution)/shard_map/ppermute | solution.py:258
  144.1 4.2 %collective-permute-done.49.refs_15_ = f32[32,1024]{1,0:T(8,128)S(1)} collective-permute-done((f32[32,1024]{1,0:T(8,128)S(1)}, f32[32,1024]{1,0:T(8,128)S(1)}, u32[]{:S(2)}, u32[]{:S(2)}) %collective-permute-start.49) | collective-permute-done | bytes 131104 | tf_op jit(solution)/shard_map/ppermute | solution.py:258
  149.7 1.8 %finish.1 = f32[128,2048]{1,0:T(8,128)} custom-call(s32[3]{0:T(128)S(1)} %pad_add_fusion.place_ref, f32[128,2048]{1,0:T(8,128)S(1)} %copy-done, f32[128,1]{1,0:T(8,128)S(1)} %copy.8.occ_ref, f32[1,2048]{1,0:T(1,128)S(1)} %bitcast.5, f32[32,1024]{1,0:T(8,128)S(1)} %get-tuple-element.257.refs_0_, f32[32,1024]{1,0:T(8,128)S(1)} %collective-permute-done.21.refs_1_, ...), custom_call_target="tpu_custom_call" | custom-call | flops 1 | bytes 1 | tf_op jit(solution)/shard_map/finish/pallas_call | solution.py:219
  (163 shorter events, 55.5 us)
Async XLA Ops:
  0.0 37.0 %collective-permute-start.12 = (f32[2048,1024]{1,0:T(8,128)}, f32[2048,1024]{1,0:T(8,128)}, u32[]{:S(2)}, u32[]{:S(2)}) collective-permute-start(f32[2048,1024]{1,0:T(8,128)} %whole_ref.2), channel_id=1, source_target_pairs={{0,4},{4,0},{8,12},{12,8},{16,20},{20,16},{24,28},{28,24},{1,5},{5... | collective-permute-start | bytes 25165832 | tf_op jit(solution)/shard_map/ppermute | solution.py:252
  19.4 13.7 %collective-permute-start.8 = (f32[32,2048]{1,0:T(8,128)S(1)}, f32[32,2048]{1,0:T(8,128)S(1)}, u32[]{:S(2)}, u32[]{:S(2)}) collective-permute-start(f32[32,2048]{1,0:T(8,128)S(1)} %get-tuple-element.180), channel_id=1, source_target_pairs={{0,1},{1,0},{2,3},{3,2},{4,5},{5,4},{6,7},{7,6},{8,9},{9,8},{10,11... | collective-permute-start | bytes 786440 | tf_op jit(solution)/shard_map/ppermute | solution.py:258
  20.8 10.1 %collective-permute-start.9 = (f32[16,2048]{1,0:T(8,128)S(1)}, f32[16,2048]{1,0:T(8,128)S(1)}, u32[]{:S(2)}, u32[]{:S(2)}) collective-permute-start(f32[16,2048]{1,0:T(8,128)S(1)} %pad_maximum_fusion.1), channel_id=1, source_target_pairs={{0,2},{1,3},{2,0},{3,1},{4,6},{5,7},{6,4},{7,5},{8,10},{9,11},{10,... | collective-permute-start | bytes 393224 | tf_op jit(solution)/shard_map/ppermute | solution.py:258
  24.5 9.4 %collective-permute-start.6 = (f32[16,2048]{1,0:T(8,128)S(1)}, f32[16,2048]{1,0:T(8,128)S(1)}, u32[]{:S(2)}, u32[]{:S(2)}) collective-permute-start(f32[16,2048]{1,0:T(8,128)S(1)} %slice.68), channel_id=1, source_target_pairs={{0,16},{4,20},{8,24},{12,28},{16,0},{20,4},{24,8},{28,12},{1,17},{... | collective-permute-start | bytes 393224 | tf_op jit(solution)/shard_map/ppermute | solution.py:252
  31.5 14.6 %collective-permute-start.11 = (f32[32,2048]{1,0:T(8,128)S(1)}, f32[32,2048]{1,0:T(8,128)S(1)}, u32[]{:S(2)}, u32[]{:S(2)}) collective-permute-start(f32[32,2048]{1,0:T(8,128)S(1)} %pack.4.refs_0_), channel_id=1, source_target_pairs={{0,8},{4,12},{8,0},{12,4},{16,24},{20,28},{24,16},{28,20},{1,9},{5... | collective-permute-start | bytes 786440 | tf_op jit(solution)/shard_map/ppermute | solution.py:252
  33.1 17.4 %collective-permute-start.14 = (f32[32,2048]{1,0:T(8,128)S(1)}, f32[32,2048]{1,0:T(8,128)S(1)}, u32[]{:S(2)}, u32[]{:S(2)}) collective-permute-start(f32[32,2048]{1,0:T(8,128)S(1)} %pad_maximum_fusion), channel_id=1, source_target_pairs={{0,2},{1,3},{2,0},{3,1},{4,6},{5,7},{6,4},{7,5},{8,10},{9,11},{10,... | collective-permute-start | bytes 786440 | tf_op jit(solution)/shard_map/ppermute | solution.py:258
  36.4 12.6 %collective-permute-start.10 = (f32[64,1024]{1,0:T(8,128)S(1)}, f32[64,1024]{1,0:T(8,128)S(1)}, u32[]{:S(2)}, u32[]{:S(2)}) collective-permute-start(f32[64,1024]{1,0:T(8,128)S(1)} %get-tuple-element.201), channel_id=1, source_target_pairs={{0,8},{4,12},{8,0},{12,4},{16,24},{20,28},{24,16},{28,20},{1,9},{5... | collective-permute-start | bytes 786440 | tf_op jit(solution)/shard_map/ppermute | solution.py:252
  47.6 10.8 %collective-permute-start.16 = (f32[64,2048]{1,0:T(8,128)}, f32[64,2048]{1,0:T(8,128)S(1)}, u32[]{:S(2)}, u32[]{:S(2)}) collective-permute-start(f32[64,2048]{1,0:T(8,128)} %constant_dynamic-update-slice_fusion), channel_id=1, source_target_pairs={{0,16},{4,20},{8,24},{12,28},{16,0},{20,4},{24,8},{28,12},{1,17},{... | collective-permute-start | bytes 1572872 | tf_op jit(solution)/shard_map/ppermute | solution.py:252
  51.1 14.7 %collective-permute-start.15 = (f32[32,2048]{1,0:T(8,128)S(1)}, f32[32,2048]{1,0:T(8,128)S(1)}, u32[]{:S(2)}, u32[]{:S(2)}) collective-permute-start(f32[32,2048]{1,0:T(8,128)S(1)} %get-tuple-element.270.refs_0_), channel_id=1, source_target_pairs={{0,8},{4,12},{8,0},{12,4},{16,24},{20,28},{24,16},{28,20},{1,9},{5... | collective-permute-start | bytes 786440 | tf_op jit(solution)/shard_map/ppermute | solution.py:252
  52.8 16.6 %collective-permute-start.23 = (f32[64,1024]{1,0:T(8,128)S(1)}, f32[64,1024]{1,0:T(8,128)S(1)}, u32[]{:S(2)}, u32[]{:S(2)}) collective-permute-start(f32[64,1024]{1,0:T(8,128)S(1)} %broadcast_select_fusion.6), channel_id=1, source_target_pairs={{0,1},{1,0},{2,3},{3,2},{4,5},{5,4},{6,7},{7,6},{8,9},{9,8},{10,11... | collective-permute-start | bytes 786440 | tf_op jit(solution)/shard_map/ppermute | solution.py:258
  54.4 13.6 %collective-permute-start.20 = (f32[32,2048]{1,0:T(8,128)S(1)}, f32[32,2048]{1,0:T(8,128)S(1)}, u32[]{:S(2)}, u32[]{:S(2)}) collective-permute-start(f32[32,2048]{1,0:T(8,128)S(1)} %get-tuple-element.283.refs_0_), channel_id=1, source_target_pairs={{0,8},{4,12},{8,0},{12,4},{16,24},{20,28},{24,16},{28,20},{1,9},{5... | collective-permute-start | bytes 786440 | tf_op jit(solution)/shard_map/ppermute | solution.py:252
  65.2 21.7 %collective-permute-start.24 = (f32[64,1024]{1,0:T(8,128)S(1)}, f32[64,1024]{1,0:T(8,128)S(1)}, u32[]{:S(2)}, u32[]{:S(2)}) collective-permute-start(f32[64,1024]{1,0:T(8,128)S(1)} %get-tuple-element.232), channel_id=1, source_target_pairs={{0,8},{4,12},{8,0},{12,4},{16,24},{20,28},{24,16},{28,20},{1,9},{5... | collective-permute-start | bytes 786440 | tf_op jit(solution)/shard_map/ppermute | solution.py:252
  65.9 14.9 %collective-permute-start.19 = (f32[64,2048]{1,0:T(8,128)S(1)}, f32[64,2048]{1,0:T(8,128)S(1)}, u32[]{:S(2)}, u32[]{:S(2)}) collective-permute-start(f32[64,2048]{1,0:T(8,128)S(1)} %constant_dynamic-update-slice_fusion.2), channel_id=1, source_target_pairs={{0,16},{4,20},{8,24},{12,28},{16,0},{20,4},{24,8},{28,12},{1,17},{... | collective-permute-start | bytes 1572872 | tf_op jit(solution)/shard_map/ppermute | solution.py:252
  67.2 17.6 %collective-permute-start.18 = (f32[32,1024]{1,0:T(8,128)S(1)}, f32[32,1024]{1,0:T(8,128)S(1)}, u32[]{:S(2)}, u32[]{:S(2)}) collective-permute-start(f32[32,1024]{1,0:T(8,128)S(1)} %get-tuple-element.349), channel_id=1, source_target_pairs={{0,16},{4,20},{8,24},{12,28},{16,0},{20,4},{24,8},{28,12},{1,17},{... | collective-permute-start | bytes 393224 | tf_op jit(solution)/shard_map/ppermute | solution.py:252
  68.1 26.6 %collective-permute-start.26 = (f32[64,2048]{1,0:T(8,128)S(1)}, f32[64,2048]{1,0:T(8,128)S(1)}, u32[]{:S(2)}, u32[]{:S(2)}) collective-permute-start(f32[64,2048]{1,0:T(8,128)S(1)} %constant_dynamic-update-slice_fusion.4), channel_id=1, source_target_pairs={{0,16},{4,20},{8,24},{12,28},{16,0},{20,4},{24,8},{28,12},{1,17},{... | collective-permute-start | bytes 1572872 | tf_op jit(solution)/shard_map/ppermute | solution.py:252
  84.8 9.8 %collective-permute-start.21 = (f32[32,1024]{1,0:T(8,128)S(1)}, f32[32,1024]{1,0:T(8,128)S(1)}, u32[]{:S(2)}, u32[]{:S(2)}) collective-permute-start(f32[32,1024]{1,0:T(8,128)S(1)} %get-tuple-element.347), channel_id=1, source_target_pairs={{0,2},{1,3},{2,0},{3,1},{4,6},{5,7},{6,4},{7,5},{8,10},{9,11},{10,... | collective-permute-start | bytes 393224 | tf_op jit(solution)/shard_map/ppermute | solution.py:258
  87.0 12.4 %collective-permute-start.28 = (f32[64,1024]{1,0:T(8,128)S(1)}, f32[64,1024]{1,0:T(8,128)S(1)}, u32[]{:S(2)}, u32[]{:S(2)}) collective-permute-start(f32[64,1024]{1,0:T(8,128)S(1)} %broadcast_select_fusion.5), channel_id=1, source_target_pairs={{0,1},{1,0},{2,3},{3,2},{4,5},{5,4},{6,7},{7,6},{8,9},{9,8},{10,11... | collective-permute-start | bytes 786440 | tf_op jit(solution)/shard_map/ppermute | solution.py:258
  87.3 10.4 %collective-permute-start.25 = (f32[32,1024]{1,0:T(8,128)S(1)}, f32[32,1024]{1,0:T(8,128)S(1)}, u32[]{:S(2)}, u32[]{:S(2)}) collective-permute-start(f32[32,1024]{1,0:T(8,128)S(1)} %get-tuple-element.346), channel_id=1, source_target_pairs={{0,16},{4,20},{8,24},{12,28},{16,0},{20,4},{24,8},{28,12},{1,17},{... | collective-permute-start | bytes 393224 | tf_op jit(solution)/shard_map/ppermute | solution.py:252
  94.7 13.5 %collective-permute-start.33 = (f32[64,1024]{1,0:T(8,128)S(1)}, f32[64,1024]{1,0:T(8,128)S(1)}, u32[]{:S(2)}, u32[]{:S(2)}) collective-permute-start(f32[64,1024]{1,0:T(8,128)S(1)} %broadcast_select_fusion.4), channel_id=1, source_target_pairs={{0,1},{1,0},{2,3},{3,2},{4,5},{5,4},{6,7},{7,6},{8,9},{9,8},{10,11... | collective-permute-start | bytes 786440 | tf_op jit(solution)/shard_map/ppermute | solution.py:258
  97.1 12.2 %collective-permute-start.35 = (f32[64,1024]{1,0:T(8,128)S(1)}, f32[64,1024]{1,0:T(8,128)S(1)}, u32[]{:S(2)}, u32[]{:S(2)}) collective-permute-start(f32[64,1024]{1,0:T(8,128)S(1)} %get-tuple-element.264), channel_id=1, source_target_pairs={{0,8},{4,12},{8,0},{12,4},{16,24},{20,28},{24,16},{28,20},{1,9},{5... | collective-permute-start | bytes 786440 | tf_op jit(solution)/shard_map/ppermute | solution.py:252
  97.7 10.0 %collective-permute-start.27 = (f32[32,1024]{1,0:T(8,128)S(1)}, f32[32,1024]{1,0:T(8,128)S(1)}, u32[]{:S(2)}, u32[]{:S(2)}) collective-permute-start(f32[32,1024]{1,0:T(8,128)S(1)} %get-tuple-element.343), channel_id=1, source_target_pairs={{0,2},{1,3},{2,0},{3,1},{4,6},{5,7},{6,4},{7,5},{8,10},{9,11},{10,... | collective-permute-start | bytes 393224 | tf_op jit(solution)/shard_map/ppermute | solution.py:258
  99.9 15.0 %collective-permute-start.31 = (f32[64,1024]{1,0:T(8,128)S(1)}, f32[64,1024]{1,0:T(8,128)S(1)}, u32[]{:S(2)}, u32[]{:S(2)}) collective-permute-start(f32[64,1024]{1,0:T(8,128)S(1)} %broadcast_select_fusion.3), channel_id=1, source_target_pairs={{0,1},{1,0},{2,3},{3,2},{4,5},{5,4},{6,7},{7,6},{8,9},{9,8},{10,11... | collective-permute-start | bytes 786440 | tf_op jit(solution)/shard_map/ppermute | solution.py:258
  104.5 12.9 %collective-permute-start.38 = (f32[64,1024]{1,0:T(8,128)S(1)}, f32[64,1024]{1,0:T(8,128)S(1)}, u32[]{:S(2)}, u32[]{:S(2)}) collective-permute-start(f32[64,1024]{1,0:T(8,128)S(1)} %get-tuple-element.275), channel_id=1, source_target_pairs={{0,8},{4,12},{8,0},{12,4},{16,24},{20,28},{24,16},{28,20},{1,9},{5... | collective-permute-start | bytes 786440 | tf_op jit(solution)/shard_map/ppermute | solution.py:252
  107.7 8.8 %collective-permute-start.32 = (f32[32,1024]{1,0:T(8,128)S(1)}, f32[32,1024]{1,0:T(8,128)S(1)}, u32[]{:S(2)}, u32[]{:S(2)}) collective-permute-start(f32[32,1024]{1,0:T(8,128)S(1)} %get-tuple-element.340), channel_id=1, source_target_pairs={{0,2},{1,3},{2,0},{3,1},{4,6},{5,7},{6,4},{7,5},{8,10},{9,11},{10,... | collective-permute-start | bytes 393224 | tf_op jit(solution)/shard_map/ppermute | solution.py:258
  109.4 13.8 %collective-permute-start.37 = (f32[64,1024]{1,0:T(8,128)S(1)}, f32[64,1024]{1,0:T(8,128)S(1)}, u32[]{:S(2)}, u32[]{:S(2)}) collective-permute-start(f32[64,1024]{1,0:T(8,128)S(1)} %broadcast_select_fusion.2), channel_id=1, source_target_pairs={{0,1},{1,0},{2,3},{3,2},{4,5},{5,4},{6,7},{7,6},{8,9},{9,8},{10,11... | collective-permute-start | bytes 786440 | tf_op jit(solution)/shard_map/ppermute | solution.py:258
  114.9 10.0 %collective-permute-start.42 = (f32[64,1024]{1,0:T(8,128)S(1)}, f32[64,1024]{1,0:T(8,128)S(1)}, u32[]{:S(2)}, u32[]{:S(2)}) collective-permute-start(f32[64,1024]{1,0:T(8,128)S(1)} %get-tuple-element.288), channel_id=1, source_target_pairs={{0,8},{4,12},{8,0},{12,4},{16,24},{20,28},{24,16},{28,20},{1,9},{5... | collective-permute-start | bytes 786440 | tf_op jit(solution)/shard_map/ppermute | solution.py:252
  116.3 20.2 %collective-permute-start.45 = (f32[32,1024]{1,0:T(8,128)S(1)}, f32[32,1024]{1,0:T(8,128)S(1)}, u32[]{:S(2)}, u32[]{:S(2)}) collective-permute-start(f32[32,1024]{1,0:T(8,128)S(1)} %get-tuple-element.328), channel_id=1, source_target_pairs={{0,2},{1,3},{2,0},{3,1},{4,6},{5,7},{6,4},{7,5},{8,10},{9,11},{10,... | collective-permute-start | bytes 393224 | tf_op jit(solution)/shard_map/ppermute | solution.py:258
  117.4 9.3 %collective-permute-start.41 = (f32[64,1024]{1,0:T(8,128)S(1)}, f32[64,1024]{1,0:T(8,128)S(1)}, u32[]{:S(2)}, u32[]{:S(2)}) collective-permute-start(f32[64,1024]{1,0:T(8,128)S(1)} %broadcast_select_fusion.1), channel_id=1, source_target_pairs={{0,1},{1,0},{2,3},{3,2},{4,5},{5,4},{6,7},{7,6},{8,9},{9,8},{10,11... | collective-permute-start | bytes 786440 | tf_op jit(solution)/shard_map/ppermute | solution.py:258
  124.8 11.6 %collective-permute-start.39 = (f32[32,1024]{1,0:T(8,128)S(1)}, f32[32,1024]{1,0:T(8,128)S(1)}, u32[]{:S(2)}, u32[]{:S(2)}) collective-permute-start(f32[32,1024]{1,0:T(8,128)S(1)} %get-tuple-element.333), channel_id=1, source_target_pairs={{0,2},{1,3},{2,0},{3,1},{4,6},{5,7},{6,4},{7,5},{8,10},{9,11},{10,... | collective-permute-start | bytes 393224 | tf_op jit(solution)/shard_map/ppermute | solution.py:258
  125.0 11.5 %collective-permute-start.44 = (f32[64,1024]{1,0:T(8,128)S(1)}, f32[64,1024]{1,0:T(8,128)S(1)}, u32[]{:S(2)}, u32[]{:S(2)}) collective-permute-start(f32[64,1024]{1,0:T(8,128)S(1)} %broadcast_select_fusion), channel_id=1, source_target_pairs={{0,1},{1,0},{2,3},{3,2},{4,5},{5,4},{6,7},{7,6},{8,9},{9,8},{10,11... | collective-permute-start | bytes 786440 | tf_op jit(solution)/shard_map/ppermute | solution.py:258
  126.8 9.7 %collective-permute-start.46 = (f32[32,1024]{1,0:T(8,128)S(1)}, f32[32,1024]{1,0:T(8,128)S(1)}, u32[]{:S(2)}, u32[]{:S(2)}) collective-permute-start(f32[32,1024]{1,0:T(8,128)S(1)} %get-tuple-element.326), channel_id=1, source_target_pairs={{0,16},{4,20},{8,24},{12,28},{16,0},{20,4},{24,8},{28,12},{1,17},{... | collective-permute-start | bytes 393224 | tf_op jit(solution)/shard_map/ppermute | solution.py:252
  137.9 10.4 %collective-permute-start.49 = (f32[32,1024]{1,0:T(8,128)S(1)}, f32[32,1024]{1,0:T(8,128)S(1)}, u32[]{:S(2)}, u32[]{:S(2)}) collective-permute-start(f32[32,1024]{1,0:T(8,128)S(1)} %get-tuple-element.320), channel_id=1, source_target_pairs={{0,2},{1,3},{2,0},{3,1},{4,6},{5,7},{6,4},{7,5},{8,10},{9,11},{10,... | collective-permute-start | bytes 393224 | tf_op jit(solution)/shard_map/ppermute | solution.py:258
  (34 other events, 309.7 us)

commit v19 on v18

--- a/solution.py
+++ b/solution.py
@@ -17,9 +17,9 @@
 
 ORDER = (
     "s00", "p0", "s10", "g00", "s11", "s20", "g01", "f0", "p1", "g10", "s21", "e0", "f1", "e1",
-    "g11", "r0", "p2", "g30", "r1", "g20", "e3", "g31", "x0", "g21", "e6", "z0", "r3", "x1",
-    "e2", "r6", "l0", "e4", "z1", "x3", "r2", "e7", "z3", "l1", "x6", "r4", "e5", "z6", "l3",
-    "x2", "r7", "x4", "z2", "r5", "x7", "z4", "l2", "z7", "l6", "x5", "z5", "l4", "l7", "l5",
+    "g11", "r0", "p2", "g20", "r1", "x0", "g30", "g21", "e2", "z0", "e3", "x1", "g31", "r2",
+    "l0", "e5", "z1", "r3", "e4", "x2", "r5", "l1", "e6", "z2", "x3", "r4", "e7", "z3", "x5",
+    "l2", "r6", "x4", "z5", "r7", "l3", "z4", "x6", "l5", "z6", "x7", "l4", "z7", "l6", "l7",
 )
 
 SMEM = pl.BlockSpec(memory_space=pltpu.SMEM)

time: 152 us -> 144 us (0.947)
  starting transfers between devices: 60.6 us -> 52.2 us
  waiting for transfers between devices: 46.7 us -> 51 us
  local copies, waits for them, and re-layouts: 8.32 us -> 5.69 us
    ppermute x27, starting transfers between devices: 32.6 us -> 26.4 us  [across(): lax.ppermute(value, 'wide', [(w, w ^ mask) for w in range(wide_count)])]
    ppermute x23, waiting for transfers between devices: 28.4 us -> 32.1 us  [along(): lax.ppermute(value, 'narrow', [(n, n ^ mask) for n in range(narrow_count)])]
    ppermute x23, starting transfers between devices: 28 us -> 25.8 us  [along(): lax.ppermute(value, 'narrow', [(n, n ^ mask) for n in range(narrow_count)])]
    unnamed x35, local copies, waits for them, and re-layouts: 7.25 us -> 5.14 us
  transfers between devices with their start and end apart: 50 -> 50, of which waited for: 22 -> 27; matrix products, arithmetic and copies ran while one was open for 3% -> 2% of each run, Pallas kernels for 20% -> 21%
where the time goes in v19:
time: 144 us
  starting transfers between devices  52.2 us (36%)
  waiting for transfers between devices  51 us (35%)
  Pallas kernels  32.1 us (22%)
  local copies, waits for them, and re-layouts  5.69 us (4%)
  other arithmetic  2.13 us (1%)
    ppermute x23, waiting for transfers between devices, along(): lax.ppermute(value, 'narrow', [(n, n ^ mask) for n in range(narrow_count)])  32.1 us
    ppermute x27, starting transfers between devices, across(): lax.ppermute(value, 'wide', [(w, w ^ mask) for w in range(wide_count)])  26.4 us
    ppermute x23, starting transfers between devices, along(): lax.ppermute(value, 'narrow', [(n, n ^ mask) for n in range(narrow_count)])  25.8 us
    pallas_call x8, Pallas kernels, product(): pl.pallas_call(functools.partial(product_kernel, count, rows, layout, tar...  19.4 us
    ppermute x27, waiting for transfers between devices, across(): lax.ppermute(value, 'wide', [(w, w ^ mask) for w in range(wide_count)])  18.9 us
    pallas_call x2, Pallas kernels, split(): pl.pallas_call(functools.partial(split_kernel, step), in_specs=[HBM], out...  8.51 us
    unnamed x35, local copies, waits for them, and re-layouts  5.14 us
  transfers between devices with their start and end apart: 50, of which 27 were waited for; matrix products, arithmetic and copies ran while one was open for 2% of the time, Pallas kernels for 21%

profile of v19, /device:TPU:0, one launch (start us, length us, event | category | flops | bytes accessed | tf_op | source)
XLA Modules:
  0.0 143.7 jit_solution(8147074118068229019)
XLA Ops:
  2.4 2.6 %collective-permute-start = (f32[8,2048]{1,0:T(8,128)S(1)}, f32[8,2048]{1,0:T(8,128)S(1)}, u32[]{:S(2)}, u32[]{:S(2)}) collective-permute-start(f32[8,2048]{1,0:T(8,128)S(1)} %get-tuple-element.166), channel_id=1, source_target_pairs={{0,1},{1,0},{2,3},{3,2},{4,5},{5,4},{6,7},{7,6},{8,9},{9,8},{10,11... | collective-permute-start | bytes 196616 | tf_op jit(solution)/shard_map/ppermute | solution.py:258
  5.0 2.6 %collective-permute-start.1 = (f32[8,2048]{1,0:T(8,128)S(1)}, f32[8,2048]{1,0:T(8,128)S(1)}, u32[]{:S(2)}, u32[]{:S(2)}) collective-permute-start(f32[8,2048]{1,0:T(8,128)S(1)} %get-tuple-element.167), channel_id=1, source_target_pairs={{0,2},{1,3},{2,0},{3,1},{4,6},{5,7},{6,4},{7,5},{8,10},{9,11},{10,... | collective-permute-start | bytes 196616 | tf_op jit(solution)/shard_map/ppermute | solution.py:258
  7.8 4.2 %collective-permute-done.1.refs_2_ = f32[8,2048]{1,0:T(8,128)S(1)} collective-permute-done((f32[8,2048]{1,0:T(8,128)S(1)}, f32[8,2048]{1,0:T(8,128)S(1)}, u32[]{:S(2)}, u32[]{:S(2)}) %collective-permute-start.1) | collective-permute-done | bytes 65568 | tf_op jit(solution)/shard_map/ppermute | solution.py:258
  12.0 1.8 %collective-permute-done.2.refs_3_ = f32[8,2048]{1,0:T(8,128)S(1)} collective-permute-done((f32[8,2048]{1,0:T(8,128)S(1)}, f32[8,2048]{1,0:T(8,128)S(1)}, u32[]{:S(2)}, u32[]{:S(2)}) %collective-permute-start.2) | collective-permute-done | bytes 65568 | tf_op jit(solution)/shard_map/ppermute | solution.py:258
  26.7 4.3 %split.2 = (bf16[2048,1024]{1,0:T(8,128)(2,1)S(1)}, bf16[2048,1024]{1,0:T(8,128)(2,1)S(1)}, f32[8,128]{1,0:T(8,128)}) custom-call(f32[2048,1024]{1,0:T(8,128)} %whole_ref.2), custom_call_target="tpu_custom_call" | custom-call | flops 1 | bytes 1 | tf_op jit(solution)/shard_map/split/pallas_call | solution.py:122
  35.1 2.5 %product.8 = (f32[64,1024]{1,0:T(8,128)S(1)}, f32[64,1024]{1,0:T(8,128)S(1)}) custom-call(s32[3]{0:T(128)S(1)} %pad_add_fusion.place_ref, s32[8,64]{1,0:T(8,128)S(1)} %copy-done.12, s32[8]{0:T(128)S(1)} %copy-done.13, f32[32,2048]{1,0:T(8,128)S(1)} %pack.3.refs_0_, f32[32,2048]{1,0:T(8,128)S(1)} %collective-permute-done.3.refs_1_, ...), custom_call_target="tpu_custom_call" | custom-call | flops 3221225472 | bytes 1 | tf_op jit(solution)/shard_map/product/pallas_call | solution.py:183
  38.2 4.3 %split.3 = (bf16[2048,1024]{1,0:T(8,128)(2,1)S(1)}, bf16[2048,1024]{1,0:T(8,128)(2,1)S(1)}, f32[8,128]{1,0:T(8,128)}) custom-call(f32[2048,1024]{1,0:T(8,128)} %collective-permute-done.12.whole_ref), custom_call_target="tpu_custom_call" | custom-call | flops 1 | bytes 1 | tf_op jit(solution)/shard_map/split/pallas_call | solution.py:122
  42.5 2.5 %product.9 = (f32[64,1024]{1,0:T(8,128)S(1)}, f32[64,1024]{1,0:T(8,128)S(1)}) custom-call(s32[3]{0:T(128)S(1)} %pad_add_fusion.place_ref, s32[8,64]{1,0:T(8,128)S(1)} %copy-done.12, s32[8]{0:T(128)S(1)} %copy-done.13, f32[32,2048]{1,0:T(8,128)S(1)} %pack.3.refs_0_, f32[32,2048]{1,0:T(8,128)S(1)} %collective-permute-done.3.refs_1_, ...), custom_call_target="tpu_custom_call" | custom-call | flops 3221225472 | bytes 1 | tf_op jit(solution)/shard_map/product/pallas_call | solution.py:183
  48.2 1.7 %collective-permute-start.13 = (f32[64,1024]{1,0:T(8,128)S(1)}, f32[64,1024]{1,0:T(8,128)S(1)}, u32[]{:S(2)}, u32[]{:S(2)}) collective-permute-start(f32[64,1024]{1,0:T(8,128)S(1)} %broadcast_select_fusion.7), channel_id=1, source_target_pairs={{0,1},{1,0},{2,3},{3,2},{4,5},{5,4},{6,7},{7,6},{8,9},{9,8},{10,11... | collective-permute-start | bytes 786440 | tf_op jit(solution)/shard_map/ppermute | solution.py:258
  51.6 3.4 %collective-permute-done.14 = f32[64,1024]{1,0:T(8,128)S(1)} collective-permute-done((f32[64,1024]{1,0:T(8,128)S(1)}, f32[64,1024]{1,0:T(8,128)S(1)}, u32[]{:S(2)}, u32[]{:S(2)}) %collective-permute-start.14) | collective-permute-done | bytes 262176 | tf_op jit(solution)/shard_map/ppermute | solution.py:252
  62.1 2.7 %collective-permute-done.17.refs_2_ = f32[64,2048]{1,0:T(8,128)S(1)} collective-permute-done((f32[64,2048]{1,0:T(8,128)}, f32[64,2048]{1,0:T(8,128)S(1)}, u32[]{:S(2)}, u32[]{:S(2)}) %collective-permute-start.17) | collective-permute-done | bytes 524320 | tf_op jit(solution)/shard_map/ppermute | solution.py:252
  64.8 2.2 %copy-done.6 = bf16[2048,1024]{1,0:T(8,128)(2,1)S(1)} copy-done((bf16[2048,1024]{1,0:T(8,128)(2,1)S(1)}, bf16[2048,1024]{1,0:T(8,128)(2,1)}, u32[]{:S(2)}) %copy-start.6) | copy-done | bytes 4194328
  67.0 2.4 %product.10 = (f32[64,1024]{1,0:T(8,128)S(1)}, f32[64,1024]{1,0:T(8,128)S(1)}) custom-call(s32[3]{0:T(128)S(1)} %pad_add_fusion.place_ref, s32[8,64]{1,0:T(8,128)S(1)} %copy-done.12, s32[8]{0:T(128)S(1)} %copy-done.13, f32[32,2048]{1,0:T(8,128)S(1)} %pack.4.refs_0_, f32[32,2048]{1,0:T(8,128)S(1)} %collective-permute-done.11.refs_1_, ...), custom_call_target="tpu_custom_call" | custom-call | flops 3221225472 | bytes 1 | tf_op jit(solution)/shard_map/product/pallas_call | solution.py:183
  71.2 2.4 %product.11 = (f32[64,1024]{1,0:T(8,128)S(1)}, f32[64,1024]{1,0:T(8,128)S(1)}) custom-call(s32[3]{0:T(128)S(1)} %pad_add_fusion.place_ref, s32[8,64]{1,0:T(8,128)S(1)} %copy-done.12, s32[8]{0:T(128)S(1)} %copy-done.13, f32[32,2048]{1,0:T(8,128)S(1)} %pack.4.refs_0_, f32[32,2048]{1,0:T(8,128)S(1)} %collective-permute-done.11.refs_1_, ...), custom_call_target="tpu_custom_call" | custom-call | flops 3221225472 | bytes 1 | tf_op jit(solution)/shard_map/product/pallas_call | solution.py:183
  77.8 2.4 %collective-permute-done.19.refs_1_ = f32[32,1024]{1,0:T(8,128)S(1)} collective-permute-done((f32[32,1024]{1,0:T(8,128)S(1)}, f32[32,1024]{1,0:T(8,128)S(1)}, u32[]{:S(2)}, u32[]{:S(2)}) %collective-permute-start.19) | collective-permute-done | bytes 131104 | tf_op jit(solution)/shard_map/ppermute | solution.py:258
  80.2 2.4 %product.12 = (f32[64,1024]{1,0:T(8,128)S(1)}, f32[64,1024]{1,0:T(8,128)S(1)}) custom-call(s32[3]{0:T(128)S(1)} %pad_add_fusion.place_ref, s32[8,64]{1,0:T(8,128)S(1)} %copy-done.12, s32[8]{0:T(128)S(1)} %copy-done.13, f32[32,2048]{1,0:T(8,128)S(1)} %get-tuple-element.261.refs_0_, f32[32,2048]{1,0:T(8,128)S(1)} %collective-permute-done.18.refs_1_, ...), custom_call_target="tpu_custom_call" | custom-call | flops 3221225472 | bytes 1 | tf_op jit(solution)/shard_map/product/pallas_call | solution.py:183
  84.2 2.5 %collective-permute-start.25 = (f32[32,1024]{1,0:T(8,128)S(1)}, f32[32,1024]{1,0:T(8,128)S(1)}, u32[]{:S(2)}, u32[]{:S(2)}) collective-permute-start(f32[32,1024]{1,0:T(8,128)S(1)} %get-tuple-element.343), channel_id=1, source_target_pairs={{0,2},{1,3},{2,0},{3,1},{4,6},{5,7},{6,4},{7,5},{8,10},{9,11},{10,... | collective-permute-start | bytes 393224 | tf_op jit(solution)/shard_map/ppermute | solution.py:258
  86.9 2.4 %product.13 = (f32[64,1024]{1,0:T(8,128)S(1)}, f32[64,1024]{1,0:T(8,128)S(1)}) custom-call(s32[3]{0:T(128)S(1)} %pad_add_fusion.place_ref, s32[8,64]{1,0:T(8,128)S(1)} %copy-done.12, s32[8]{0:T(128)S(1)} %copy-done.13, f32[32,2048]{1,0:T(8,128)S(1)} %get-tuple-element.261.refs_0_, f32[32,2048]{1,0:T(8,128)S(1)} %collective-permute-done.18.refs_1_, ...), custom_call_target="tpu_custom_call" | custom-call | flops 3221225472 | bytes 1 | tf_op jit(solution)/shard_map/product/pallas_call | solution.py:183
  89.3 2.2 %collective-permute-start.35 = (f32[64,1024]{1,0:T(8,128)S(1)}, f32[64,1024]{1,0:T(8,128)S(1)}, u32[]{:S(2)}, u32[]{:S(2)}) collective-permute-start(f32[64,1024]{1,0:T(8,128)S(1)} %get-tuple-element.266), channel_id=1, source_target_pairs={{0,8},{4,12},{8,0},{12,4},{16,24},{20,28},{24,16},{28,20},{1,9},{5... | collective-permute-start | bytes 786440 | tf_op jit(solution)/shard_map/ppermute | solution.py:252
  91.7 2.3 %collective-permute-done.25.refs_3_ = f32[32,1024]{1,0:T(8,128)S(1)} collective-permute-done((f32[32,1024]{1,0:T(8,128)S(1)}, f32[32,1024]{1,0:T(8,128)S(1)}, u32[]{:S(2)}, u32[]{:S(2)}) %collective-permute-start.25) | collective-permute-done | bytes 131104 | tf_op jit(solution)/shard_map/ppermute | solution.py:258
  94.0 2.4 %product.14 = (f32[64,1024]{1,0:T(8,128)S(1)}, f32[64,1024]{1,0:T(8,128)S(1)}) custom-call(s32[3]{0:T(128)S(1)} %pad_add_fusion.place_ref, s32[8,64]{1,0:T(8,128)S(1)} %copy-done.12, s32[8]{0:T(128)S(1)} %copy-done.13, f32[32,2048]{1,0:T(8,128)S(1)} %get-tuple-element.283.refs_0_, f32[32,2048]{1,0:T(8,128)S(1)} %collective-permute-done.21.refs_1_, ...), custom_call_target="tpu_custom_call" | custom-call | flops 3221225472 | bytes 1 | tf_op jit(solution)/shard_map/product/pallas_call | solution.py:183
  96.8 2.2 %collective-permute-done.33 = f32[64,1024]{1,0:T(8,128)S(1)} collective-permute-done((f32[64,1024]{1,0:T(8,128)S(1)}, f32[64,1024]{1,0:T(8,128)S(1)}, u32[]{:S(2)}, u32[]{:S(2)}) %collective-permute-start.33) | collective-permute-done | bytes 262176 | tf_op jit(solution)/shard_map/ppermute | solution.py:258
  100.1 2.1 %collective-permute-start.39 = (f32[64,1024]{1,0:T(8,128)S(1)}, f32[64,1024]{1,0:T(8,128)S(1)}, u32[]{:S(2)}, u32[]{:S(2)}) collective-permute-start(f32[64,1024]{1,0:T(8,128)S(1)} %broadcast_select_fusion.2), channel_id=1, source_target_pairs={{0,1},{1,0},{2,3},{3,2},{4,5},{5,4},{6,7},{7,6},{8,9},{9,8},{10,11... | collective-permute-start | bytes 786440 | tf_op jit(solution)/shard_map/ppermute | solution.py:258
  102.1 2.4 %product.15 = (f32[64,1024]{1,0:T(8,128)S(1)}, f32[64,1024]{1,0:T(8,128)S(1)}) custom-call(s32[3]{0:T(128)S(1)} %pad_add_fusion.place_ref, s32[8,64]{1,0:T(8,128)S(1)} %copy-done.12, s32[8]{0:T(128)S(1)} %copy-done.13, f32[32,2048]{1,0:T(8,128)S(1)} %get-tuple-element.283.refs_0_, f32[32,2048]{1,0:T(8,128)S(1)} %collective-permute-done.21.refs_1_, ...), custom_call_target="tpu_custom_call" | custom-call | flops 3221225472 | bytes 1 | tf_op jit(solution)/shard_map/product/pallas_call | solution.py:183
  113.2 1.9 %collective-permute-start.46 = (f32[32,1024]{1,0:T(8,128)S(1)}, f32[32,1024]{1,0:T(8,128)S(1)}, u32[]{:S(2)}, u32[]{:S(2)}) collective-permute-start(f32[32,1024]{1,0:T(8,128)S(1)} %get-tuple-element.326), channel_id=1, source_target_pairs={{0,2},{1,3},{2,0},{3,1},{4,6},{5,7},{6,4},{7,5},{8,10},{9,11},{10,... | collective-permute-start | bytes 393224 | tf_op jit(solution)/shard_map/ppermute | solution.py:258
  115.6 4.6 %collective-permute-done.44 = f32[64,1024]{1,0:T(8,128)S(1)} collective-permute-done((f32[64,1024]{1,0:T(8,128)S(1)}, f32[64,1024]{1,0:T(8,128)S(1)}, u32[]{:S(2)}, u32[]{:S(2)}) %collective-permute-start.44) | collective-permute-done | bytes 262176 | tf_op jit(solution)/shard_map/ppermute | solution.py:258
  121.4 2.1 %collective-permute-start.42 = (f32[32,1024]{1,0:T(8,128)S(1)}, f32[32,1024]{1,0:T(8,128)S(1)}, u32[]{:S(2)}, u32[]{:S(2)}) collective-permute-start(f32[32,1024]{1,0:T(8,128)S(1)} %get-tuple-element.329), channel_id=1, source_target_pairs={{0,2},{1,3},{2,0},{3,1},{4,6},{5,7},{6,4},{7,5},{8,10},{9,11},{10,... | collective-permute-start | bytes 393224 | tf_op jit(solution)/shard_map/ppermute | solution.py:258
  123.5 1.7 %collective-permute-done.45 = f32[32,1024]{1,0:T(8,128)S(1)} collective-permute-done((f32[32,1024]{1,0:T(8,128)S(1)}, f32[32,1024]{1,0:T(8,128)S(1)}, u32[]{:S(2)}, u32[]{:S(2)}) %collective-permute-start.45) | collective-permute-done | bytes 131104 | tf_op jit(solution)/shard_map/ppermute | solution.py:252
  125.3 5.0 %collective-permute-done.43 = f32[64,1024]{1,0:T(8,128)S(1)} collective-permute-done((f32[64,1024]{1,0:T(8,128)S(1)}, f32[64,1024]{1,0:T(8,128)S(1)}, u32[]{:S(2)}, u32[]{:S(2)}) %collective-permute-start.43) | collective-permute-done | bytes 262176 | tf_op jit(solution)/shard_map/ppermute | solution.py:258
  130.9 4.5 %collective-permute-done.48 = f32[32,1024]{1,0:T(8,128)S(1)} collective-permute-done((f32[32,1024]{1,0:T(8,128)S(1)}, f32[32,1024]{1,0:T(8,128)S(1)}, u32[]{:S(2)}, u32[]{:S(2)}) %collective-permute-start.48) | collective-permute-done | bytes 131104 | tf_op jit(solution)/shard_map/ppermute | solution.py:252
  137.2 4.7 %collective-permute-done.49.refs_15_ = f32[32,1024]{1,0:T(8,128)S(1)} collective-permute-done((f32[32,1024]{1,0:T(8,128)S(1)}, f32[32,1024]{1,0:T(8,128)S(1)}, u32[]{:S(2)}, u32[]{:S(2)}) %collective-permute-start.49) | collective-permute-done | bytes 131104 | tf_op jit(solution)/shard_map/ppermute | solution.py:258
  141.9 1.8 %finish.1 = f32[128,2048]{1,0:T(8,128)} custom-call(s32[3]{0:T(128)S(1)} %pad_add_fusion.place_ref, f32[128,2048]{1,0:T(8,128)S(1)} %copy-done, f32[128,1]{1,0:T(8,128)S(1)} %copy.8.occ_ref, f32[1,2048]{1,0:T(1,128)S(1)} %bitcast.5, f32[32,1024]{1,0:T(8,128)S(1)} %get-tuple-element.249.refs_0_, f32[32,1024]{1,0:T(8,128)S(1)} %collective-permute-done.19.refs_1_, ...), custom_call_target="tpu_custom_call" | custom-call | flops 1 | bytes 1 | tf_op jit(solution)/shard_map/finish/pallas_call | solution.py:219
  (163 shorter events, 54.0 us)
Async XLA Ops:
  0.0 38.2 %collective-permute-start.12 = (f32[2048,1024]{1,0:T(8,128)}, f32[2048,1024]{1,0:T(8,128)}, u32[]{:S(2)}, u32[]{:S(2)}) collective-permute-start(f32[2048,1024]{1,0:T(8,128)} %whole_ref.2), channel_id=1, source_target_pairs={{0,4},{4,0},{8,12},{12,8},{16,20},{20,16},{24,28},{28,24},{1,5},{5... | collective-permute-start | bytes 25165832 | tf_op jit(solution)/shard_map/ppermute | solution.py:252
  19.4 13.7 %collective-permute-start.8 = (f32[32,2048]{1,0:T(8,128)S(1)}, f32[32,2048]{1,0:T(8,128)S(1)}, u32[]{:S(2)}, u32[]{:S(2)}) collective-permute-start(f32[32,2048]{1,0:T(8,128)S(1)} %get-tuple-element.180), channel_id=1, source_target_pairs={{0,1},{1,0},{2,3},{3,2},{4,5},{5,4},{6,7},{7,6},{8,9},{9,8},{10,11... | collective-permute-start | bytes 786440 | tf_op jit(solution)/shard_map/ppermute | solution.py:258
  20.8 10.1 %collective-permute-start.9 = (f32[16,2048]{1,0:T(8,128)S(1)}, f32[16,2048]{1,0:T(8,128)S(1)}, u32[]{:S(2)}, u32[]{:S(2)}) collective-permute-start(f32[16,2048]{1,0:T(8,128)S(1)} %pad_maximum_fusion.1), channel_id=1, source_target_pairs={{0,2},{1,3},{2,0},{3,1},{4,6},{5,7},{6,4},{7,5},{8,10},{9,11},{10,... | collective-permute-start | bytes 393224 | tf_op jit(solution)/shard_map/ppermute | solution.py:258
  24.5 10.6 %collective-permute-start.6 = (f32[16,2048]{1,0:T(8,128)S(1)}, f32[16,2048]{1,0:T(8,128)S(1)}, u32[]{:S(2)}, u32[]{:S(2)}) collective-permute-start(f32[16,2048]{1,0:T(8,128)S(1)} %slice.68), channel_id=1, source_target_pairs={{0,16},{4,20},{8,24},{12,28},{16,0},{20,4},{24,8},{28,12},{1,17},{... | collective-permute-start | bytes 393224 | tf_op jit(solution)/shard_map/ppermute | solution.py:252
  26.1 9.0 %collective-permute-start.7 = (f32[16,2048]{1,0:T(8,128)S(1)}, f32[16,2048]{1,0:T(8,128)S(1)}, u32[]{:S(2)}, u32[]{:S(2)}) collective-permute-start(f32[16,2048]{1,0:T(8,128)S(1)} %slice.69), channel_id=1, source_target_pairs={{0,8},{4,12},{8,0},{12,4},{16,24},{20,28},{24,16},{28,20},{1,9},{5... | collective-permute-start | bytes 393224 | tf_op jit(solution)/shard_map/ppermute | solution.py:252
  31.5 15.8 %collective-permute-start.11 = (f32[32,2048]{1,0:T(8,128)S(1)}, f32[32,2048]{1,0:T(8,128)S(1)}, u32[]{:S(2)}, u32[]{:S(2)}) collective-permute-start(f32[32,2048]{1,0:T(8,128)S(1)} %pack.4.refs_0_), channel_id=1, source_target_pairs={{0,8},{4,12},{8,0},{12,4},{16,24},{20,28},{24,16},{28,20},{1,9},{5... | collective-permute-start | bytes 786440 | tf_op jit(solution)/shard_map/ppermute | solution.py:252
  34.4 16.1 %collective-permute-start.15 = (f32[32,2048]{1,0:T(8,128)}, f32[32,2048]{1,0:T(8,128)S(1)}, u32[]{:S(2)}, u32[]{:S(2)}) collective-permute-start(f32[32,2048]{1,0:T(8,128)} %pad_maximum_fusion), channel_id=1, source_target_pairs={{0,2},{1,3},{2,0},{3,1},{4,6},{5,7},{6,4},{7,5},{8,10},{9,11},{10,... | collective-permute-start | bytes 786440 | tf_op jit(solution)/shard_map/ppermute | solution.py:258
  37.6 9.8 %collective-permute-start.10 = (f32[64,1024]{1,0:T(8,128)S(1)}, f32[64,1024]{1,0:T(8,128)S(1)}, u32[]{:S(2)}, u32[]{:S(2)}) collective-permute-start(f32[64,1024]{1,0:T(8,128)S(1)} %get-tuple-element.201), channel_id=1, source_target_pairs={{0,8},{4,12},{8,0},{12,4},{16,24},{20,28},{24,16},{28,20},{1,9},{5... | collective-permute-start | bytes 786440 | tf_op jit(solution)/shard_map/ppermute | solution.py:252
  45.8 9.2 %collective-permute-start.14 = (f32[64,1024]{1,0:T(8,128)S(1)}, f32[64,1024]{1,0:T(8,128)S(1)}, u32[]{:S(2)}, u32[]{:S(2)}) collective-permute-start(f32[64,1024]{1,0:T(8,128)S(1)} %get-tuple-element.212), channel_id=1, source_target_pairs={{0,8},{4,12},{8,0},{12,4},{16,24},{20,28},{24,16},{28,20},{1,9},{5... | collective-permute-start | bytes 786440 | tf_op jit(solution)/shard_map/ppermute | solution.py:252
  49.9 14.9 %collective-permute-start.17 = (f32[64,2048]{1,0:T(8,128)}, f32[64,2048]{1,0:T(8,128)S(1)}, u32[]{:S(2)}, u32[]{:S(2)}) collective-permute-start(f32[64,2048]{1,0:T(8,128)} %copy-done.14), channel_id=1, source_target_pairs={{0,16},{4,20},{8,24},{12,28},{16,0},{20,4},{24,8},{28,12},{1,17},{... | collective-permute-start | bytes 1572872 | tf_op jit(solution)/shard_map/ppermute | solution.py:252
  51.0 9.4 %collective-permute-start.18 = (f32[32,2048]{1,0:T(8,128)S(1)}, f32[32,2048]{1,0:T(8,128)S(1)}, u32[]{:S(2)}, u32[]{:S(2)}) collective-permute-start(f32[32,2048]{1,0:T(8,128)S(1)} %get-tuple-element.261.refs_0_), channel_id=1, source_target_pairs={{0,8},{4,12},{8,0},{12,4},{16,24},{20,28},{24,16},{28,20},{1,9},{5... | collective-permute-start | bytes 786440 | tf_op jit(solution)/shard_map/ppermute | solution.py:252
  55.7 14.6 %collective-permute-start.16 = (f32[32,1024]{1,0:T(8,128)S(1)}, f32[32,1024]{1,0:T(8,128)S(1)}, u32[]{:S(2)}, u32[]{:S(2)}) collective-permute-start(f32[32,1024]{1,0:T(8,128)S(1)} %get-tuple-element.349), channel_id=1, source_target_pairs={{0,16},{4,20},{8,24},{12,28},{16,0},{20,4},{24,8},{28,12},{1,17},{... | collective-permute-start | bytes 393224 | tf_op jit(solution)/shard_map/ppermute | solution.py:252
  56.7 17.0 %collective-permute-start.22 = (f32[64,1024]{1,0:T(8,128)S(1)}, f32[64,1024]{1,0:T(8,128)S(1)}, u32[]{:S(2)}, u32[]{:S(2)}) collective-permute-start(f32[64,1024]{1,0:T(8,128)S(1)} %broadcast_select_fusion.6), channel_id=1, source_target_pairs={{0,1},{1,0},{2,3},{3,2},{4,5},{5,4},{6,7},{7,6},{8,9},{9,8},{10,11... | collective-permute-start | bytes 786440 | tf_op jit(solution)/shard_map/ppermute | solution.py:258
  58.3 17.1 %collective-permute-start.21 = (f32[32,2048]{1,0:T(8,128)S(1)}, f32[32,2048]{1,0:T(8,128)S(1)}, u32[]{:S(2)}, u32[]{:S(2)}) collective-permute-start(f32[32,2048]{1,0:T(8,128)S(1)} %get-tuple-element.283.refs_0_), channel_id=1, source_target_pairs={{0,8},{4,12},{8,0},{12,4},{16,24},{20,28},{24,16},{28,20},{1,9},{5... | collective-permute-start | bytes 786440 | tf_op jit(solution)/shard_map/ppermute | solution.py:252
  60.5 19.7 %collective-permute-start.24 = (f32[64,2048]{1,0:T(8,128)S(1)}, f32[64,2048]{1,0:T(8,128)S(1)}, u32[]{:S(2)}, u32[]{:S(2)}) collective-permute-start(f32[64,2048]{1,0:T(8,128)S(1)} %constant_dynamic-update-slice_fusion.2), channel_id=1, source_target_pairs={{0,16},{4,20},{8,24},{12,28},{16,0},{20,4},{24,8},{28,12},{1,17},{... | collective-permute-start | bytes 1572872 | tf_op jit(solution)/shard_map/ppermute | solution.py:252
  70.3 10.0 %collective-permute-start.19 = (f32[32,1024]{1,0:T(8,128)S(1)}, f32[32,1024]{1,0:T(8,128)S(1)}, u32[]{:S(2)}, u32[]{:S(2)}) collective-permute-start(f32[32,1024]{1,0:T(8,128)S(1)} %get-tuple-element.347), channel_id=1, source_target_pairs={{0,2},{1,3},{2,0},{3,1},{4,6},{5,7},{6,4},{7,5},{8,10},{9,11},{10,... | collective-permute-start | bytes 393224 | tf_op jit(solution)/shard_map/ppermute | solution.py:258
  73.7 13.1 %collective-permute-start.28 = (f32[64,1024]{1,0:T(8,128)S(1)}, f32[64,1024]{1,0:T(8,128)S(1)}, u32[]{:S(2)}, u32[]{:S(2)}) collective-permute-start(f32[64,1024]{1,0:T(8,128)S(1)} %get-tuple-element.243), channel_id=1, source_target_pairs={{0,8},{4,12},{8,0},{12,4},{16,24},{20,28},{24,16},{28,20},{1,9},{5... | collective-permute-start | bytes 786440 | tf_op jit(solution)/shard_map/ppermute | solution.py:252
  77.3 16.8 %collective-permute-start.30 = (f32[64,2048]{1,0:T(8,128)S(1)}, f32[64,2048]{1,0:T(8,128)S(1)}, u32[]{:S(2)}, u32[]{:S(2)}) collective-permute-start(f32[64,2048]{1,0:T(8,128)S(1)} %constant_dynamic-update-slice_fusion.4), channel_id=1, source_target_pairs={{0,16},{4,20},{8,24},{12,28},{16,0},{20,4},{24,8},{28,12},{1,17},{... | collective-permute-start | bytes 1572872 | tf_op jit(solution)/shard_map/ppermute | solution.py:252
  80.2 9.1 %collective-permute-start.27 = (f32[64,1024]{1,0:T(8,128)S(1)}, f32[64,1024]{1,0:T(8,128)S(1)}, u32[]{:S(2)}, u32[]{:S(2)}) collective-permute-start(f32[64,1024]{1,0:T(8,128)S(1)} %broadcast_select_fusion.5), channel_id=1, source_target_pairs={{0,1},{1,0},{2,3},{3,2},{4,5},{5,4},{6,7},{7,6},{8,9},{9,8},{10,11... | collective-permute-start | bytes 786440 | tf_op jit(solution)/shard_map/ppermute | solution.py:258
  82.7 8.9 %collective-permute-start.26 = (f32[64,1024]{1,0:T(8,128)S(1)}, f32[64,1024]{1,0:T(8,128)S(1)}, u32[]{:S(2)}, u32[]{:S(2)}) collective-permute-start(f32[64,1024]{1,0:T(8,128)S(1)} %get-tuple-element.256), channel_id=1, source_target_pairs={{0,8},{4,12},{8,0},{12,4},{16,24},{20,28},{24,16},{28,20},{1,9},{5... | collective-permute-start | bytes 786440 | tf_op jit(solution)/shard_map/ppermute | solution.py:252
  84.2 9.8 %collective-permute-start.25 = (f32[32,1024]{1,0:T(8,128)S(1)}, f32[32,1024]{1,0:T(8,128)S(1)}, u32[]{:S(2)}, u32[]{:S(2)}) collective-permute-start(f32[32,1024]{1,0:T(8,128)S(1)} %get-tuple-element.343), channel_id=1, source_target_pairs={{0,2},{1,3},{2,0},{3,1},{4,6},{5,7},{6,4},{7,5},{8,10},{9,11},{10,... | collective-permute-start | bytes 393224 | tf_op jit(solution)/shard_map/ppermute | solution.py:258
  86.8 12.2 %collective-permute-start.33 = (f32[64,1024]{1,0:T(8,128)S(1)}, f32[64,1024]{1,0:T(8,128)S(1)}, u32[]{:S(2)}, u32[]{:S(2)}) collective-permute-start(f32[64,1024]{1,0:T(8,128)S(1)} %broadcast_select_fusion.4), channel_id=1, source_target_pairs={{0,1},{1,0},{2,3},{3,2},{4,5},{5,4},{6,7},{7,6},{8,9},{9,8},{10,11... | collective-permute-start | bytes 786440 | tf_op jit(solution)/shard_map/ppermute | solution.py:258
  89.3 10.7 %collective-permute-start.35 = (f32[64,1024]{1,0:T(8,128)S(1)}, f32[64,1024]{1,0:T(8,128)S(1)}, u32[]{:S(2)}, u32[]{:S(2)}) collective-permute-start(f32[64,1024]{1,0:T(8,128)S(1)} %get-tuple-element.266), channel_id=1, source_target_pairs={{0,8},{4,12},{8,0},{12,4},{16,24},{20,28},{24,16},{28,20},{1,9},{5... | collective-permute-start | bytes 786440 | tf_op jit(solution)/shard_map/ppermute | solution.py:252
  94.0 12.9 %collective-permute-start.32 = (f32[64,1024]{1,0:T(8,128)S(1)}, f32[64,1024]{1,0:T(8,128)S(1)}, u32[]{:S(2)}, u32[]{:S(2)}) collective-permute-start(f32[64,1024]{1,0:T(8,128)S(1)} %broadcast_select_fusion.3), channel_id=1, source_target_pairs={{0,1},{1,0},{2,3},{3,2},{4,5},{5,4},{6,7},{7,6},{8,9},{9,8},{10,11... | collective-permute-start | bytes 786440 | tf_op jit(solution)/shard_map/ppermute | solution.py:258
  96.4 12.2 %collective-permute-start.40 = (f32[64,1024]{1,0:T(8,128)S(1)}, f32[64,1024]{1,0:T(8,128)S(1)}, u32[]{:S(2)}, u32[]{:S(2)}) collective-permute-start(f32[64,1024]{1,0:T(8,128)S(1)} %get-tuple-element.277), channel_id=1, source_target_pairs={{0,8},{4,12},{8,0},{12,4},{16,24},{20,28},{24,16},{28,20},{1,9},{5... | collective-permute-start | bytes 786440 | tf_op jit(solution)/shard_map/ppermute | solution.py:252
  99.1 9.1 %collective-permute-start.31 = (f32[32,1024]{1,0:T(8,128)S(1)}, f32[32,1024]{1,0:T(8,128)S(1)}, u32[]{:S(2)}, u32[]{:S(2)}) collective-permute-start(f32[32,1024]{1,0:T(8,128)S(1)} %get-tuple-element.339), channel_id=1, source_target_pairs={{0,2},{1,3},{2,0},{3,1},{4,6},{5,7},{6,4},{7,5},{8,10},{9,11},{10,... | collective-permute-start | bytes 393224 | tf_op jit(solution)/shard_map/ppermute | solution.py:258
  100.1 10.4 %collective-permute-start.39 = (f32[64,1024]{1,0:T(8,128)S(1)}, f32[64,1024]{1,0:T(8,128)S(1)}, u32[]{:S(2)}, u32[]{:S(2)}) collective-permute-start(f32[64,1024]{1,0:T(8,128)S(1)} %broadcast_select_fusion.2), channel_id=1, source_target_pairs={{0,1},{1,0},{2,3},{3,2},{4,5},{5,4},{6,7},{7,6},{8,9},{9,8},{10,11... | collective-permute-start | bytes 786440 | tf_op jit(solution)/shard_map/ppermute | solution.py:258
  104.8 10.2 %collective-permute-start.37 = (f32[64,1024]{1,0:T(8,128)S(1)}, f32[64,1024]{1,0:T(8,128)S(1)}, u32[]{:S(2)}, u32[]{:S(2)}) collective-permute-start(f32[64,1024]{1,0:T(8,128)S(1)} %get-tuple-element.288), channel_id=1, source_target_pairs={{0,8},{4,12},{8,0},{12,4},{16,24},{20,28},{24,16},{28,20},{1,9},{5... | collective-permute-start | bytes 786440 | tf_op jit(solution)/shard_map/ppermute | solution.py:252
  108.6 11.5 %collective-permute-start.44 = (f32[64,1024]{1,0:T(8,128)S(1)}, f32[64,1024]{1,0:T(8,128)S(1)}, u32[]{:S(2)}, u32[]{:S(2)}) collective-permute-start(f32[64,1024]{1,0:T(8,128)S(1)} %broadcast_select_fusion.1), channel_id=1, source_target_pairs={{0,1},{1,0},{2,3},{3,2},{4,5},{5,4},{6,7},{7,6},{8,9},{9,8},{10,11... | collective-permute-start | bytes 786440 | tf_op jit(solution)/shard_map/ppermute | solution.py:258
  113.2 10.3 %collective-permute-start.46 = (f32[32,1024]{1,0:T(8,128)S(1)}, f32[32,1024]{1,0:T(8,128)S(1)}, u32[]{:S(2)}, u32[]{:S(2)}) collective-permute-start(f32[32,1024]{1,0:T(8,128)S(1)} %get-tuple-element.326), channel_id=1, source_target_pairs={{0,2},{1,3},{2,0},{3,1},{4,6},{5,7},{6,4},{7,5},{8,10},{9,11},{10,... | collective-permute-start | bytes 393224 | tf_op jit(solution)/shard_map/ppermute | solution.py:258
  121.4 8.9 %collective-permute-start.43 = (f32[64,1024]{1,0:T(8,128)S(1)}, f32[64,1024]{1,0:T(8,128)S(1)}, u32[]{:S(2)}, u32[]{:S(2)}) collective-permute-start(f32[64,1024]{1,0:T(8,128)S(1)} %broadcast_select_fusion), channel_id=1, source_target_pairs={{0,1},{1,0},{2,3},{3,2},{4,5},{5,4},{6,7},{7,6},{8,9},{9,8},{10,11... | collective-permute-start | bytes 786440 | tf_op jit(solution)/shard_map/ppermute | solution.py:258
  121.4 9.5 %collective-permute-start.42 = (f32[32,1024]{1,0:T(8,128)S(1)}, f32[32,1024]{1,0:T(8,128)S(1)}, u32[]{:S(2)}, u32[]{:S(2)}) collective-permute-start(f32[32,1024]{1,0:T(8,128)S(1)} %get-tuple-element.329), channel_id=1, source_target_pairs={{0,2},{1,3},{2,0},{3,1},{4,6},{5,7},{6,4},{7,5},{8,10},{9,11},{10,... | collective-permute-start | bytes 393224 | tf_op jit(solution)/shard_map/ppermute | solution.py:258
  (34 other events, 284.8 us)
